TPU v7x, 32 devices: a whole 2x2x4 slice. The times are simulated.
32 devices in a mesh: groups: 2 (over x), grid: 8 (over z, y), depth: 2 (over core).
Axes of the slice: x: 2, y: 2, z: 4, core: 2. Of those that a mesh axis runs over, the one named last changes fastest.
Arguments:
- x_band: bfloat16 [8192, 4096], P(('groups', 'grid')), parts along dimension 0, may hold values from -6 to 6
- w_band: bfloat16 [8192, 4096], P(('groups', 'grid')), parts along dimension 0, may hold values from -0.09375 to 0.09375
- a_mask: int32 [128, 64], P(('groups', 'grid')), parts along dimension 0, may hold values from 0 to 1, as said below
- keep_mask: int32 [128, 64], P(('groups', 'grid', 'depth')), parts along dimension 0, may hold values 0 or 1
Outputs:
- new_iterate: bfloat16 [8192, 4096], P(('groups', 'grid', 'depth')), parts along dimension 0
There are 2 independent parts, one for each index of `groups`. A program takes and returns all parts, laid end to end along the dimension named above; each array names one. Nothing has to cross between parts.
Inputs may be any that keep to these rules, and one draw needn't show every extreme that they name: `a_mask`: 0 or 1 per block; the share of ones differs from block row to block row.
All inputs are finite; a program needn't handle non-finite values. No bound on the sum of `keep_mask` on one device may be relied on, other than what follows from the above.
Results may differ from a plain program's by a relative error of at most 0.0046.
Values may be sent and summed in bfloat16 or wider, within the bound.
No kernel may reach another device: no remote copies, remote signals or barrier semaphores. Data moves between devices by JAX's collectives and lax.ppermute only.
A program may use at most 128 MiB of HBM per device.

v0:
```python
import jax
import jax.numpy as jnp
from jax import lax
from jax.sharding import PartitionSpec as P


def shifted(shard, axis, by):
    count = lax.axis_size(axis)
    return lax.ppermute(shard, axis, [(i, (i + by) % count) for i in range(count)])


def expand_blocks(mask, block):
    rows, cols = mask.shape
    wide = jnp.broadcast_to(mask[:, None, :, None], (rows, block, cols, block))
    return wide.reshape(rows * block, cols * block)


def local(x_band, w_band, a_mask, keep_mask):
    panel = x_band.shape[0]
    block = panel // a_mask.shape[0]
    band_cols = x_band.shape[1]
    xm = x_band * expand_blocks(a_mask, block).astype(jnp.bfloat16)
    rows = lax.broadcasted_iota(jnp.int32, x_band.shape, 0)
    cols = lax.broadcasted_iota(jnp.int32, x_band.shape, 1)
    identity = jnp.where(cols == rows + 4 * panel, 1.0, 0.0).astype(jnp.float32)
    b_panel = (1.5 * identity - 0.5 * w_band.astype(jnp.float32)).astype(jnp.bfloat16)
    layer = lax.axis_index("depth")
    current = shifted(b_panel, ("grid", "depth"), -5)
    wide = jnp.zeros((panel, 2 * band_cols), jnp.float32)
    for step in range(4):
        offset = 6 + layer - 2 * step
        ablock = lax.dynamic_slice_in_dim(xm, offset * panel, panel, 1)
        term = jnp.dot(ablock, current, preferred_element_type=jnp.float32)
        region = lax.dynamic_slice_in_dim(wide, offset * panel, band_cols, 1)
        wide = lax.dynamic_update_slice_in_dim(wide, region + term, offset * panel, 1)
        if step < 3:
            current = shifted(current, "grid", 2)
    partial_band = wide[:, 4 * panel : 12 * panel]
    mine = lax.psum_scatter(partial_band, "depth", scatter_dimension=0, tiled=True)
    keep = expand_blocks(keep_mask, block).astype(jnp.float32)
    return (mine * keep).astype(jnp.bfloat16)


def solution(mesh):
    placed = (
        P(("groups", "grid"), None),
        P(("groups", "grid"), None),
        P(("groups", "grid"), None),
        P(("groups", "grid", "depth"), None),
    )
    return jax.shard_map(
        local,
        mesh=mesh,
        in_specs=placed,
        out_specs=P(("groups", "grid", "depth"), None),
        check_vma=False,
    )
```

profile of v0, /device:TPU:0, one launch (start us, length us, event | category | flops | bytes accessed | tf_op | source)
XLA Modules:
  0.0 554.1 jit_solution(8245120790010569868)
XLA Ops:
  6.5 0.0 reduce-scatter.2.cloned.1.call-start
  6.5 0.0 copy-start.3
  6.5 4.1 subtract_convert_fusion
  10.7 4.5 collective-permute-start
  15.2 91.0 %collective-permute-done = bf16[512,4096]{1,0:T(8,128)(2,1)S(1)} collective-permute-done((bf16[512,4096]{1,0:T(8,128)(2,1)S(1)}, bf16[512,4096]{1,0:T(8,128)(2,1)S(1)}, u32[]{:S(2)}, u32[]{:S(2)}) %collective-permute-start) | collective-permute-done | bytes 4194336 | tf_op jit(solution)/shard_map/ppermute | solution.py:9
  106.1 0.0 copy-start
  106.1 2.0 copy-done
  108.1 134.5 %collective-permute-start.1 = (bf16[512,4096]{1,0:T(8,128)(2,1)S(1)}, bf16[512,4096]{1,0:T(8,128)(2,1)S(1)}, u32[]{:S(2)}, u32[]{:S(2)}) collective-permute-start(bf16[512,4096]{1,0:T(8,128)(2,1)S(1)} %collective-permute-done), channel_id=1, source_target_pairs={{0,4},{2,6},{4,8},{6,10},{8,12},{10,14},{12,0},{14,2},{1,5},{3,7},... | collective-permute-start | bytes 12582920 | tf_op jit(solution)/shard_map/ppermute | solution.py:9
  242.6 46.0 %collective-permute-done.1 = bf16[512,4096]{1,0:T(8,128)(2,1)S(1)} collective-permute-done((bf16[512,4096]{1,0:T(8,128)(2,1)S(1)}, bf16[512,4096]{1,0:T(8,128)(2,1)S(1)}, u32[]{:S(2)}, u32[]{:S(2)}) %collective-permute-start.1) | collective-permute-done | bytes 4194336 | tf_op jit(solution)/shard_map/ppermute | solution.py:9
  288.6 0.0 copy-start.1
  288.6 1.9 copy-done.1
  290.5 43.6 %collective-permute-start.2 = (bf16[512,4096]{1,0:T(8,128)(2,1)S(1)}, bf16[512,4096]{1,0:T(8,128)(2,1)}, u32[]{:S(2)}, u32[]{:S(2)}) collective-permute-start(bf16[512,4096]{1,0:T(8,128)(2,1)S(1)} %collective-permute-done.1), channel_id=1, source_target_pairs={{0,4},{2,6},{4,8},{6,10},{8,12},{10,14},{12,0},{14,2},{1,5},{3,7},... | collective-permute-start | bytes 12582920 | tf_op jit(solution)/shard_map/ppermute | solution.py:9
  334.2 91.1 %collective-permute-done.2 = bf16[512,4096]{1,0:T(8,128)(2,1)} collective-permute-done((bf16[512,4096]{1,0:T(8,128)(2,1)S(1)}, bf16[512,4096]{1,0:T(8,128)(2,1)}, u32[]{:S(2)}, u32[]{:S(2)}) %collective-permute-start.2) | collective-permute-done | bytes 4194336 | tf_op jit(solution)/shard_map/ppermute | solution.py:9
  425.3 0.0 collective-permute-start.3
  425.3 0.0 copy-done.3
  425.3 5.4 broadcast_in_dim.24
  430.7 12.1 %convert_element_type.24 = bf16[512,4096]{1,0:T(8,128)(2,1)} reshape(bf16[8,64,64,64]{3,2,1,0:T(8,128)(2,1)} %broadcast_in_dim.24) | data formatting | bytes 8388608 | tf_op jit(solution)/shard_map/convert_element_type | solution.py:22
  442.8 5.0 mul.37
  447.8 2.0 broadcast_in_dim.23
  449.8 0.0 copy-start.2
  449.8 4.7 convolution_dynamic-update-slice_fusion
  454.5 0.0 copy-done.2
  454.5 3.2 add_dynamic-update-slice_fusion.2
  457.8 5.3 add_dynamic-update-slice_fusion.1
  463.0 54.8 %collective-permute-done.3 = bf16[512,4096]{1,0:T(8,128)(2,1)} collective-permute-done((bf16[512,4096]{1,0:T(8,128)(2,1)}, bf16[512,4096]{1,0:T(8,128)(2,1)}, u32[]{:S(2)}, u32[]{:S(2)}) %collective-permute-start.3) | collective-permute-done | bytes 4194336 | tf_op jit(solution)/shard_map/ppermute | solution.py:9
  517.9 5.3 add_dynamic-update-slice_fusion
  523.1 4.0 slice.4
  527.1 0.0 reduce-scatter.2.cloned.1.call-update
  527.2 0.7 copy-done.4
  527.8 5.0 broadcast_in_dim.27
  532.8 9.2 %convert_element_type.28 = f32[256,4096]{1,0:T(8,128)} reshape(f32[4,64,64,64]{3,2,1,0:T(8,128)} %broadcast_in_dim.27) | data formatting | bytes 8388608 | tf_op jit(solution)/shard_map/convert_element_type | solution.py:40
  542.0 5.3 multiply_convert_fusion
  (5 shorter events, 0.0 us)
Async XLA Ops:
  6.5 535.4 %reduce-scatter.2.cloned.1.call-start = ((), (), s32[]{:S(2)}) async-start(), calls=%async_computation.1 | async-start | bytes 12582912 | tf_op jit(solution)/shard_map/reduce_scatter | solution.py:39
  6.5 418.8 %copy-start.3 = (s32[8,64]{1,0:T(8,128)S(1)}, s32[8,64]{1,0:T(8,128)}, u32[]{:S(2)}) copy-start(s32[8,64]{1,0:T(8,128)} %param.6) | copy-start | bytes 6148
  10.7 95.4 %collective-permute-start = (bf16[512,4096]{1,0:T(8,128)(2,1)S(1)}, bf16[512,4096]{1,0:T(8,128)(2,1)S(1)}, u32[]{:S(2)}, u32[]{:S(2)}) collective-permute-start(bf16[512,4096]{1,0:T(8,128)(2,1)S(1)} %subtract_convert_fusion), channel_id=1, source_target_pairs={{0,11},{1,12},{2,13},{3,14},{4,15},{5,0},{6,1},{7,2},{8,3},{9,4},{... | collective-permute-start | bytes 12582920 | tf_op jit(solution)/shard_map/ppermute | solution.py:9
  106.1 2.0 copy-start
  108.1 180.5 %collective-permute-start.1 = (bf16[512,4096]{1,0:T(8,128)(2,1)S(1)}, bf16[512,4096]{1,0:T(8,128)(2,1)S(1)}, u32[]{:S(2)}, u32[]{:S(2)}) collective-permute-start(bf16[512,4096]{1,0:T(8,128)(2,1)S(1)} %collective-permute-done), channel_id=1, source_target_pairs={{0,4},{2,6},{4,8},{6,10},{8,12},{10,14},{12,0},{14,2},{1,5},{3,7},... | collective-permute-start | bytes 12582920 | tf_op jit(solution)/shard_map/ppermute | solution.py:9
  288.6 1.9 copy-start.1
  290.5 134.8 %collective-permute-start.2 = (bf16[512,4096]{1,0:T(8,128)(2,1)S(1)}, bf16[512,4096]{1,0:T(8,128)(2,1)}, u32[]{:S(2)}, u32[]{:S(2)}) collective-permute-start(bf16[512,4096]{1,0:T(8,128)(2,1)S(1)} %collective-permute-done.1), channel_id=1, source_target_pairs={{0,4},{2,6},{4,8},{6,10},{8,12},{10,14},{12,0},{14,2},{1,5},{3,7},... | collective-permute-start | bytes 12582920 | tf_op jit(solution)/shard_map/ppermute | solution.py:9
  425.3 92.6 %collective-permute-start.3 = (bf16[512,4096]{1,0:T(8,128)(2,1)}, bf16[512,4096]{1,0:T(8,128)(2,1)}, u32[]{:S(2)}, u32[]{:S(2)}) collective-permute-start(bf16[512,4096]{1,0:T(8,128)(2,1)} %collective-permute-done.2), channel_id=1, source_target_pairs={{0,4},{2,6},{4,8},{6,10},{8,12},{10,14},{12,0},{14,2},{1,5},{3,7},... | collective-permute-start | bytes 12582920 | tf_op jit(solution)/shard_map/ppermute | solution.py:9
  449.8 4.7 copy-start.2
  527.1 0.7 copy-start.4
Sparse Core Ops, SparseCore 0:
  527.3 14.0 reduce-scatter.1
where the time goes:
time: 555 us; the launch traced here: 554 us
  waiting for transfers between devices  283 us (51%)
  starting transfers between devices  183 us (33%)
  local copies, waits for them, and re-layouts  42.2 us (8%)
  matrix products  18.4 us (3%)
  other arithmetic  14.4 us (3%)
  between operations  13.5 us (2%)
    ppermute x4, waiting for transfers between devices, shifted(): lax.ppermute(shard, axis, [(i, (i + by) % count) for i in range(count)])  283 us
    ppermute x4, starting transfers between devices, shifted(): lax.ppermute(shard, axis, [(i, (i + by) % count) for i in range(count)])  183 us
    dot_general x4, matrix products, local(): term = jnp.dot(ablock, current, preferred_element_type=jnp.float32)  18.4 us
    convert_element_type x1, local copies, waits for them, and re-layouts, local(): xm = x_band * expand_blocks(a_mask, block).astype(jnp.bfloat16)  12.1 us
  transfers between devices with their start and end apart: 5, of which 4 were waited for; matrix products, arithmetic and copies ran while one was open for 9% of the time, Pallas kernels for 0%

commit v1 on v0

--- a/solution.py
+++ b/solution.py
@@ -1,7 +1,14 @@
+import functools
+
 import jax
 import jax.numpy as jnp
 from jax import lax
+from jax.experimental import pallas as pl
+from jax.experimental.pallas import tpu as pltpu
 from jax.sharding import PartitionSpec as P
+
+LANES = 128
+MIB = 1 << 20
 
 
 def shifted(shard, axis, by):
@@ -15,7 +22,7 @@
     return wide.reshape(rows * block, cols * block)
 
 
-def local(x_band, w_band, a_mask, keep_mask):
+def ring(x_band, w_band, a_mask, keep_mask):
     panel = x_band.shape[0]
     block = panel // a_mask.shape[0]
     band_cols = x_band.shape[1]
@@ -41,6 +48,311 @@
     return (mine * keep).astype(jnp.bfloat16)
 
 
+def strips_kernel(quarter_ref, w_ref, b_ref, held, sems):
+    panel = held.shape[0]
+    quarter = quarter_ref[0]
+    band = held.shape[1] // LANES
+    copies = []
+    for j in range(band):
+        at = pl.multiple_of(j * panel + quarter * LANES, LANES)
+        copies.append(
+            pltpu.make_async_copy(
+                w_ref.at[:, pl.ds(at, LANES)],
+                held.at[:, j * LANES : (j + 1) * LANES],
+                sems.at[j],
+            )
+        )
+        copies[-1].start()
+    for j in range(band):
+        copies[j].wait()
+        value = -0.5 * held[:, j * LANES : (j + 1) * LANES].astype(jnp.float32)
+        if j == band // 2:
+            rows = lax.broadcasted_iota(jnp.int32, value.shape, 0)
+            cols = lax.broadcasted_iota(jnp.int32, value.shape, 1)
+            value = value + jnp.where(rows == cols + quarter * LANES, 1.5, 0.0)
+        b_ref[:, j * LANES : (j + 1) * LANES] = value.astype(jnp.bfloat16)
+
+
+def b_strips(w_band, quarter):
+    panel = w_band.shape[0]
+    band = w_band.shape[1] // panel
+    shape = (panel, band * LANES)
+    return pl.pallas_call(
+        strips_kernel,
+        out_shape=jax.ShapeDtypeStruct(shape, jnp.bfloat16),
+        in_specs=[
+            pl.BlockSpec(memory_space=pltpu.SMEM),
+            pl.BlockSpec(memory_space=pl.ANY),
+        ],
+        out_specs=pl.BlockSpec(memory_space=pltpu.VMEM),
+        scratch_shapes=[pltpu.VMEM(shape, jnp.bfloat16), pltpu.SemaphoreType.DMA((band,))],
+        compiler_params=pltpu.CompilerParams(vmem_limit_bytes=16 * MIB),
+        cost_estimate=pl.CostEstimate(flops=1000, bytes_accessed=4 * shape[0] * shape[1], transcendentals=0),
+        name="b_strips",
+    )(quarter.reshape(1), w_band)
+
+
+def mask_kernel(half_ref, mask_ref, x_ref, out_ref):
+    out_ref[...] = (x_ref[...].astype(jnp.float32) * mask_ref[0]).astype(jnp.bfloat16)
+
+
+def masked_half(x_band, mask_wide, half):
+    block = x_band.shape[0] // mask_wide.shape[0]
+    per_half = mask_wide.shape[0] // 2
+    cols = x_band.shape[1]
+    return pl.pallas_call(
+        mask_kernel,
+        grid_spec=pltpu.PrefetchScalarGridSpec(
+            num_scalar_prefetch=1,
+            grid=(per_half,),
+            in_specs=[
+                pl.BlockSpec((1, 1, cols), lambda i, h: (h[0] * per_half + i, 0, 0)),
+                pl.BlockSpec((block, cols), lambda i, h: (h[0] * per_half + i, 0)),
+            ],
+            out_specs=pl.BlockSpec((block, cols), lambda i, h: (i, 0)),
+        ),
+        out_shape=jax.ShapeDtypeStruct((x_band.shape[0] // 2, cols), jnp.bfloat16),
+        compiler_params=pltpu.CompilerParams(vmem_limit_bytes=16 * MIB),
+        cost_estimate=pl.CostEstimate(flops=1000, bytes_accessed=2 * x_band.shape[0] * cols, transcendentals=0),
+        name="masked_half",
+    )(half.reshape(1), mask_wide, x_band)
+
+
+def product_kernel(widths, has_prev, final, meta_ref, *refs):
+    n_b = len(widths)
+    x_refs, refs = refs[:4], refs[4:]
+    middle_refs, refs = refs[:n_b], refs[n_b:]
+    end_refs, refs = refs[:n_b], refs[n_b:]
+    prev_ref, refs = (refs[0], refs[1:]) if has_prev else (None, refs)
+    n_out = 4 if final else 1
+    out_refs, refs = refs[:n_out], refs[n_out:]
+    xv, bv, acc, x_sems, b_sems, prev_sem = refs
+    panel = bv.shape[1]
+    quarter = bv.shape[2]
+    band = quarter // LANES
+    low = band // 2 * LANES
+    is_end = meta_ref[0]
+
+    def window(p):
+        return pl.ds(pl.multiple_of(meta_ref[1 + 3 * p] * LANES, LANES), widths[p] * LANES)
+
+    def b_copies(p):
+        return (
+            pltpu.make_async_copy(middle_refs[p], bv.at[p], b_sems.at[p]),
+            pltpu.make_async_copy(end_refs[p], bv.at[p, :, window(p)], b_sems.at[p]),
+        )
+
+    def x_copy(p, r):
+        at = pl.multiple_of(meta_ref[1 + 3 * p + 1 + r // 2] * panel, panel)
+        return pltpu.make_async_copy(
+            x_refs[r].at[:, pl.ds(at, panel)], xv.at[p, r], x_sems.at[p, r]
+        )
+
+    if has_prev:
+        prev_copy = pltpu.make_async_copy(prev_ref, acc.at[:, :, low : low + quarter], prev_sem)
+        prev_copy.start()
+    for p in range(n_b):
+        middle, end = b_copies(p)
+
+        @pl.when(is_end == 0)
+        def _():
+            middle.start()
+
+        @pl.when(is_end != 0)
+        def _():
+            end.start()
+
+        for r in range(4):
+            x_copy(p, r).start()
+    if has_prev:
+        prev_copy.wait()
+    else:
+        acc[...] = jnp.zeros_like(acc)
+    for p in range(n_b):
+        middle, end = b_copies(p)
+
+        @pl.when(is_end == 0)
+        def _():
+            middle.wait()
+
+        @pl.when(is_end != 0)
+        def _():
+            end.wait()
+
+        for r in range(4):
+            x_copy(p, r).wait()
+
+        def step(r, carry):
+            offset = meta_ref[1 + 3 * p + 1 + r // 2]
+            cols = pl.ds(pl.multiple_of(offset * LANES, LANES), quarter)
+            acc[r, :, cols] += jnp.dot(xv[p, r], bv[p], preferred_element_type=jnp.float32)
+            return carry
+
+        lax.fori_loop(0, 4, step, 0)
+    if final:
+        for r in range(4):
+            out_refs[r][...] = acc[r, :, low : low + quarter].astype(jnp.bfloat16)
+    else:
+        out_refs[0][...] = acc[:, :, low : low + quarter]
+
+
+def products(meta, xs, middle, end, prev, final, name):
+    rows = xs[0].shape[0]
+    panel, quarter = middle[0].shape
+    n_b = len(middle)
+    widths = tuple(e.shape[1] // LANES for e in end)
+    any_spec = pl.BlockSpec(memory_space=pl.ANY)
+    vmem_spec = pl.BlockSpec(memory_space=pltpu.VMEM)
+    operands = [meta, *xs, *middle, *end] + ([] if prev is None else [prev])
+    if final:
+        out_shape = [jax.ShapeDtypeStruct((rows, quarter), jnp.bfloat16)] * 4
+        out_specs = [vmem_spec] * 4
+    else:
+        out_shape = jax.ShapeDtypeStruct((4, rows, quarter), jnp.float32)
+        out_specs = vmem_spec
+    return pl.pallas_call(
+        functools.partial(product_kernel, widths, prev is not None, final),
+        out_shape=out_shape,
+        in_specs=[pl.BlockSpec(memory_space=pltpu.SMEM)] + [any_spec] * (len(operands) - 1),
+        out_specs=out_specs,
+        scratch_shapes=[
+            pltpu.VMEM((n_b, 4, rows, panel), jnp.bfloat16),
+            pltpu.VMEM((n_b, panel, quarter), jnp.bfloat16),
+            pltpu.VMEM((4, rows, 2 * quarter), jnp.float32),
+            pltpu.SemaphoreType.DMA((n_b, 4)),
+            pltpu.SemaphoreType.DMA((n_b,)),
+            pltpu.SemaphoreType.DMA,
+        ],
+        compiler_params=pltpu.CompilerParams(vmem_limit_bytes=40 * MIB),
+        cost_estimate=pl.CostEstimate(
+            flops=2 * n_b * 4 * rows * panel * quarter,
+            bytes_accessed=n_b * 2 * (4 * rows * panel + panel * quarter),
+            transcendentals=0,
+        ),
+        name=name,
+    )(*operands)
+
+
+def assemble_kernel(quarter_ref, mask_ref, *refs):
+    *pieces, out_ref = refs
+    n = len(pieces)
+    band = pieces[0].shape[1] // LANES
+    panel = n * LANES
+    for mine in range(n):
+
+        @pl.when(quarter_ref[0] == mine)
+        def _():
+            for t in range(n):
+                for j in range(band):
+                    cols = slice(j * panel + t * LANES, j * panel + (t + 1) * LANES)
+                    value = pieces[t ^ mine][:, j * LANES : (j + 1) * LANES].astype(jnp.float32)
+                    out_ref[:, cols] = (value * mask_ref[0, :, cols]).astype(jnp.bfloat16)
+
+
+def assembled(quarter, keep_wide, pieces):
+    rows, width = pieces[0].shape
+    steps = keep_wide.shape[0]
+    block = rows // steps
+    cols = width * len(pieces)
+    return pl.pallas_call(
+        assemble_kernel,
+        grid_spec=pltpu.PrefetchScalarGridSpec(
+            num_scalar_prefetch=1,
+            grid=(steps,),
+            in_specs=[pl.BlockSpec((1, 1, cols), lambda i, q: (i, 0, 0))]
+            + [pl.BlockSpec((block, width), lambda i, q: (i, 0))] * len(pieces),
+            out_specs=pl.BlockSpec((block, cols), lambda i, q: (i, 0)),
+        ),
+        out_shape=jax.ShapeDtypeStruct((rows, cols), jnp.bfloat16),
+        compiler_params=pltpu.CompilerParams(vmem_limit_bytes=16 * MIB),
+        cost_estimate=pl.CostEstimate(flops=1000, bytes_accessed=4 * rows * cols, transcendentals=0),
+        name="assembled",
+    )(quarter.reshape(1), keep_wide, *pieces)
+
+
+def widen(mask, block):
+    rows, cols = mask.shape
+    wide = jnp.broadcast_to(mask.astype(jnp.float32)[:, :, None], (rows, cols, block))
+    return wide.reshape(rows, 1, cols * block)
+
+
+def pairs_in_line(x_band, w_band, a_mask, keep_mask):
+    panel = x_band.shape[0]
+    block = panel // a_mask.shape[0]
+    g, c = lax.axis_index("grid"), lax.axis_index("depth")
+    z, y = g // 2, g % 2
+    left = z < 2
+    is_end = ((z == 0) | (z == 3)).astype(jnp.int32)
+    toward = jnp.where(left, 1, -1)
+    q = 2 * y + c
+
+    inward = [(0, 2), (1, 3), (6, 4), (7, 5)]
+    outward = [(2, 0), (3, 1), (4, 6), (5, 7)]
+    cross = [(2, 4), (3, 5), (4, 2), (5, 3)]
+    across = [(i, i ^ 1) for i in range(8)]
+    layers = [(0, 1), (1, 0)]
+    opposite = [(i, i ^ 3) for i in range(16)]
+    line = lambda value, pairs: lax.ppermute(value, "grid", pairs)
+    seven = 7 * LANES
+    start_near = jnp.where(left, 0, 1)
+    start_far = jnp.where(left, 1, 0)
+    near = lambda value: lax.dynamic_slice_in_dim(value, start_near * LANES, seven, 1)
+    far = lambda value: lax.dynamic_slice_in_dim(value, start_far * LANES, seven, 1)
+
+    own_a = b_strips(w_band, q)
+    cross_a = line(own_a, cross)
+    in_a = line(own_a, inward)
+    near_a = line(near(own_a), outward)
+    own_b = line(b_strips(w_band, q ^ 2), across)
+    cross_b = line(own_b, cross)
+    in_b = line(own_b, inward)
+    near_b = line(near(own_b), outward)
+
+    mask_wide = widen(a_mask, block)
+    x_mine = masked_half(x_band, mask_wide, c)
+    x_rest = masked_half(x_band, mask_wide, 1 - c)
+    x_across = line(x_mine, across)
+    x_opposite = lax.ppermute(x_across, "depth", layers)
+    xs = [x_mine, x_rest, x_across, x_opposite]
+
+    mid_a = line(cross_a, outward)
+    fwd_a = line(in_a, cross)
+    mid_b = line(cross_b, outward)
+    fwd_b = line(in_b, cross)
+    far_a = line(far(fwd_a), outward)
+    far_b = line(far(fwd_b), outward)
+
+    def offsets(delta, start):
+        tilt = 2 * y - 1
+        a = [start, (2 * delta + 4) % 8, (2 * delta + tilt + 4) % 8]
+        b = [start, (2 * delta - tilt + 4) % 8, (2 * delta + 4) % 8]
+        return a + b
+
+    zero = jnp.zeros_like(z)
+    third = jnp.where(is_end == 1, 2, -toward)
+    fourth = jnp.where(is_end == 1, -toward, 2)
+    meta = [is_end] + offsets(zero, zero) + offsets(toward, start_near) + offsets(third, zero)
+    meta = jnp.stack(meta).astype(jnp.int32)
+    meta_last = jnp.stack([is_end] + offsets(fourth, start_far)).astype(jnp.int32)
+    total = products(
+        meta,
+        xs,
+        [own_a, own_b, cross_a, cross_b, in_a, in_b],
+        [own_a, own_b, near_a, near_b, mid_a, mid_b],
+        None,
+        False,
+        "first_products",
+    )
+    pieces = products(meta_last, xs, [fwd_a, fwd_b], [far_a, far_b], total, True, "last_products")
+    pieces = [
+        pieces[0],
+        lax.ppermute(pieces[1], "depth", layers),
+        line(pieces[2], across),
+        lax.ppermute(pieces[3], ("grid", "depth"), opposite),
+    ]
+    return assembled(q, widen(keep_mask, block), pieces)
+
+
 def solution(mesh):
     placed = (
         P(("groups", "grid"), None),
@@ -48,6 +360,13 @@
         P(("groups", "grid"), None),
         P(("groups", "grid", "depth"), None),
     )
+
+    def local(x_band, w_band, a_mask, keep_mask):
+        panel, cols = x_band.shape
+        pairs = mesh.shape["grid"] == 8 and mesh.shape["depth"] == 2
+        pairs = pairs and cols == 8 * panel and panel == 4 * LANES
+        return (pairs_in_line if pairs else ring)(x_band, w_band, a_mask, keep_mask)
+
     return jax.shard_map(
         local,
         mesh=mesh,

time: 555 us -> 243 us (0.44)
  starting transfers between devices: 183 us -> 29 us
  waiting for transfers between devices: 283 us -> 166 us
  Pallas kernels: 0 us -> 28 us
  local copies, waits for them, and re-layouts: 42.2 us -> 19.4 us
  matrix products: 18.4 us -> 0 us
  other arithmetic: 14.4 us -> 0.01 us
  between operations: 13.5 us -> 0.23 us
    ppermute x4 -> x18, starting transfers between devices: 183 us -> 29 us  [the longest x15 28.9 us: pairs_in_line(): line = lambda value, pairs: lax.ppermute(value, 'grid', pairs)]
    ppermute x4 -> x18, waiting for transfers between devices: 283 us -> 166 us  [the longest x15 156 us: pairs_in_line(): line = lambda value, pairs: lax.ppermute(value, 'grid', pairs)]
    pallas_call x0 -> x7, Pallas kernels: none -> 28 us  [the longest x2 22.7 us: products(): pl.pallas_call(functools.partial(product_kernel, widths, prev is not None...]
    convert_element_type x2 -> x0, local copies, waits for them, and re-layouts: 21.2 us -> none  [the longest x1 12.1 us: local(): xm = x_band * expand_blocks(a_mask, block).astype(jnp.bfloat16)]
    dot_general x4 -> x0, matrix products: 18.4 us -> none  [local(): term = jnp.dot(ablock, current, preferred_element_type=jnp.float32)]
    broadcast_in_dim x3 -> x2, local copies, waits for them, and re-layouts: 12.4 us -> 0.21 us  [widen(): jnp.broadcast_to(mask.astype(jnp.float32)[:, :, None], (rows, cols, block))]
    convert_element_type x4 -> x2, other arithmetic: 9.43 us -> 0.01 us  [widen(): mask.astype(jnp.float32)[:, :, None]]
    dynamic_slice x0 -> x4, local copies, waits for them, and re-layouts: none -> 7.59 us  [the longest x2 4.41 us: pairs_in_line(): lax.dynamic_slice_in_dim(value, start_far * LANES, seven, 1)]
  transfers between devices with their start and end apart: 5 -> 18, of which waited for: 4 -> 11; matrix products, arithmetic and copies ran while one was open for 9% -> 3% of each run, Pallas kernels for 0% -> 7%
where the time goes in v1:
time: 243 us
  waiting for transfers between devices  166 us (68%)
  starting transfers between devices  29 us (12%)
  Pallas kernels  28 us (12%)
  local copies, waits for them, and re-layouts  19.4 us (8%)
    ppermute x15, waiting for transfers between devices, pairs_in_line(): line = lambda value, pairs: lax.ppermute(value, 'grid', pairs)  156 us
    ppermute x15, starting transfers between devices, pairs_in_line(): line = lambda value, pairs: lax.ppermute(value, 'grid', pairs)  28.9 us
    pallas_call x2, Pallas kernels, products(): pl.pallas_call(functools.partial(product_kernel, widths, prev is not None...  22.7 us
    unnamed x16, local copies, waits for them, and re-layouts  11.1 us
    ppermute x1, waiting for transfers between devices, pairs_in_line(): lax.ppermute(pieces[3], ('grid', 'depth'), opposite)  10.3 us
  transfers between devices with their start and end apart: 18, of which 11 were waited for; matrix products, arithmetic and copies ran while one was open for 3% of the time, Pallas kernels for 7%

profile of v1, /device:TPU:0, one launch (start us, length us, event | category | flops | bytes accessed | tf_op | source)
XLA Modules:
  0.0 242.7 jit_solution(11651637322391940453)
XLA Ops:
  0.0 2.2 copy-done.2
  2.2 1.7 b_strips.3
  3.9 3.0 %collective-permute-start.4 = (bf16[512,1024]{1,0:T(8,128)(2,1)}, bf16[512,1024]{1,0:T(8,128)(2,1)}, u32[]{:S(2)}, u32[]{:S(2)}) collective-permute-start(bf16[512,1024]{1,0:T(8,128)(2,1)} %b_strips.3), channel_id=1, source_target_pairs={{0,2},{2,0},{4,6},{6,4},{8,10},{10,8},{12,14},{14,12},{1,3},{3,1},... | collective-permute-start | bytes 3145736 | tf_op jit(solution)/shard_map/ppermute | solution.py:295
  7.2 2.2 copy-done.4
  9.9 1.7 copy-done.3
  12.3 4.5 %collective-permute-start.2 = (bf16[512,1024]{1,0:T(8,128)(2,1)S(1)}, bf16[512,1024]{1,0:T(8,128)(2,1)}, u32[]{:S(2)}, u32[]{:S(2)}) collective-permute-start(bf16[512,1024]{1,0:T(8,128)(2,1)S(1)} %b_strips.2.refs_4_.refs_10_), channel_id=1, source_target_pairs={{0,4},{2,6},{12,8},{14,10},{1,5},{3,7},{13,9},{15,11},{16,20},{18,... | collective-permute-start | bytes 3145736 | tf_op jit(solution)/shard_map/ppermute | solution.py:295
  16.8 14.4 %collective-permute-done.4.refs_5_.refs_11_ = bf16[512,1024]{1,0:T(8,128)(2,1)} collective-permute-done((bf16[512,1024]{1,0:T(8,128)(2,1)}, bf16[512,1024]{1,0:T(8,128)(2,1)}, u32[]{:S(2)}, u32[]{:S(2)}) %collective-permute-start.4) | collective-permute-done | bytes 1048608 | tf_op jit(solution)/shard_map/ppermute | solution.py:295
  31.2 5.0 %collective-permute-start.5 = (bf16[512,1024]{1,0:T(8,128)(2,1)}, bf16[512,1024]{1,0:T(8,128)(2,1)}, u32[]{:S(2)}, u32[]{:S(2)}) collective-permute-start(bf16[512,1024]{1,0:T(8,128)(2,1)} %collective-permute-done.4.refs_5_.refs_11_), channel_id=1, source_target_pairs={{0,4},{2,6},{12,8},{14,10},{1,5},{3,7},{13,9},{15,11},{16,20},{18,... | collective-permute-start | bytes 3145736 | tf_op jit(solution)/shard_map/ppermute | solution.py:295
  36.3 1.6 collective-permute-start.9
  37.9 1.7 collective-permute-start.10
  39.6 1.7 collective-permute-start.3
  41.3 19.2 %collective-permute-done.5.refs_9_ = bf16[512,1024]{1,0:T(8,128)(2,1)} collective-permute-done((bf16[512,1024]{1,0:T(8,128)(2,1)}, bf16[512,1024]{1,0:T(8,128)(2,1)}, u32[]{:S(2)}, u32[]{:S(2)}) %collective-permute-start.5) | collective-permute-done | bytes 1048608 | tf_op jit(solution)/shard_map/ppermute | solution.py:295
  60.5 1.7 collective-permute-start.6
  62.2 13.2 %collective-permute-done.refs_2_ = bf16[256,4096]{1,0:T(8,128)(2,1)} collective-permute-done((bf16[256,4096]{1,0:T(8,128)(2,1)S(1)}, bf16[256,4096]{1,0:T(8,128)(2,1)}, u32[]{:S(2)}, u32[]{:S(2)}) %collective-permute-start) | collective-permute-done | bytes 2097184 | tf_op jit(solution)/shard_map/ppermute | solution.py:295
  76.3 2.2 constant_dynamic-slice_fusion
  83.7 2.2 constant_dynamic-slice_fusion.3
  85.9 2.2 constant_dynamic-slice_fusion.2
  88.1 15.7 %collective-permute-done.11.refs_12_ = bf16[512,896]{1,0:T(8,128)(2,1)} collective-permute-done((bf16[512,896]{1,0:T(8,128)(2,1)}, bf16[512,896]{1,0:T(8,128)(2,1)}, u32[]{:S(2)}, u32[]{:S(2)}) %collective-permute-start.11) | collective-permute-done | bytes 917536 | tf_op jit(solution)/shard_map/ppermute | solution.py:295
  105.1 18.4 %collective-permute-done.12.refs_13_ = bf16[512,896]{1,0:T(8,128)(2,1)} collective-permute-done((bf16[512,896]{1,0:T(8,128)(2,1)}, bf16[512,896]{1,0:T(8,128)(2,1)}, u32[]{:S(2)}, u32[]{:S(2)}) %collective-permute-start.12) | collective-permute-done | bytes 917536 | tf_op jit(solution)/shard_map/ppermute | solution.py:295
  124.8 2.2 copy-done.5
  127.4 1.3 copy-done
  128.9 17.1 %collective-permute-done.13.refs_14_ = bf16[512,1024]{1,0:T(8,128)(2,1)} collective-permute-done((bf16[512,1024]{1,0:T(8,128)(2,1)}, bf16[512,1024]{1,0:T(8,128)(2,1)}, u32[]{:S(2)}, u32[]{:S(2)}) %collective-permute-start.13) | collective-permute-done | bytes 1048608 | tf_op jit(solution)/shard_map/ppermute | solution.py:295
  146.0 22.5 %collective-permute-done.14.refs_15_ = bf16[512,1024]{1,0:T(8,128)(2,1)} collective-permute-done((bf16[512,1024]{1,0:T(8,128)(2,1)}, bf16[512,1024]{1,0:T(8,128)(2,1)}, u32[]{:S(2)}, u32[]{:S(2)}) %collective-permute-start.14) | collective-permute-done | bytes 1048608 | tf_op jit(solution)/shard_map/ppermute | solution.py:295
  168.5 1.6 copy-done.1
  170.1 14.9 %first_products.1.refs_8_ = f32[4,256,1024]{2,1,0:T(8,128)} custom-call(s32[19]{0:T(128)S(1)} %stack.71.meta_ref, bf16[256,4096]{1,0:T(8,128)(2,1)S(1)} %masked_half.2.refs_0_, bf16[256,4096]{1,0:T(8,128)(2,1)S(1)} %copy-done.1, bf16[256,4096]{1,0:T(8,128)(2,1)} %collective-permute-done.refs_2_, bf16[256,4096]{1,0:T(8,128)(2,1)} %collective-permute-done.1.refs_3_, ...), custom_call_target="tpu_custom_call" | custom-call | flops 6442450944 | bytes 12582912 | tf_op jit(solution)/shard_map/first_products/pallas_call | solution.py:213
  185.0 3.1 %collective-permute-done.7.refs_6_ = bf16[512,896]{1,0:T(8,128)(2,1)} collective-permute-done((bf16[512,896]{1,0:T(8,128)(2,1)}, bf16[512,896]{1,0:T(8,128)(2,1)}, u32[]{:S(2)}, u32[]{:S(2)}) %collective-permute-start.7) | collective-permute-done | bytes 917536 | tf_op jit(solution)/shard_map/ppermute | solution.py:295
  188.1 19.3 %collective-permute-done.8.refs_7_ = bf16[512,896]{1,0:T(8,128)(2,1)} collective-permute-done((bf16[512,896]{1,0:T(8,128)(2,1)}, bf16[512,896]{1,0:T(8,128)(2,1)}, u32[]{:S(2)}, u32[]{:S(2)}) %collective-permute-start.8) | collective-permute-done | bytes 917536 | tf_op jit(solution)/shard_map/ppermute | solution.py:295
  207.4 7.8 %last_products.1 = (bf16[256,1024]{1,0:T(8,128)(2,1)S(1)}, bf16[256,1024]{1,0:T(8,128)(2,1)}, bf16[256,1024]{1,0:T(8,128)(2,1)}, bf16[256,1024]{1,0:T(8,128)(2,1)S(1)}) custom-call(s32[7]{0:T(128)S(1)} %stack.61.meta_ref, bf16[256,4096]{1,0:T(8,128)(2,1)S(1)} %masked_half.2.refs_0_, bf16[256,4096]{1,0:T(8,128)(2,1)S(1)} %copy-done.1, ...), custom_call_target="tpu_custom_call" | custom-call | flops 2147483648 | bytes 4194304 | tf_op jit(solution)/shard_map/last_products/pallas_call | solution.py:213
  215.3 1.8 collective-permute-start.16
  217.4 12.9 %collective-permute-done.16.refs_2_ = bf16[256,1024]{1,0:T(8,128)(2,1)S(1)} collective-permute-done((bf16[256,1024]{1,0:T(8,128)(2,1)}, bf16[256,1024]{1,0:T(8,128)(2,1)S(1)}, u32[]{:S(2)}, u32[]{:S(2)}) %collective-permute-start.16) | collective-permute-done | bytes 524320 | tf_op jit(solution)/shard_map/ppermute | solution.py:295
  230.3 10.3 %collective-permute-done.17.refs_3_ = bf16[256,1024]{1,0:T(8,128)(2,1)S(1)} collective-permute-done((bf16[256,1024]{1,0:T(8,128)(2,1)S(1)}, bf16[256,1024]{1,0:T(8,128)(2,1)S(1)}, u32[]{:S(2)}, u32[]{:S(2)}) %collective-permute-start.17) | collective-permute-done | bytes 524320 | tf_op jit(solution)/shard_map/ppermute | solution.py:351
  240.6 2.0 assembled.1
  (39 shorter events, 11.2 us)
Async XLA Ops:
  0.0 2.2 copy-start.2
  2.2 4.7 %copy-start.6 = (s32[8,64]{1,0:T(8,128)S(1)}, s32[8,64]{1,0:T(8,128)}, u32[]{:S(2)}) copy-start(s32[8,64]{1,0:T(8,128)} %param.6) | copy-start | bytes 6148
  3.9 27.3 %collective-permute-start.4 = (bf16[512,1024]{1,0:T(8,128)(2,1)}, bf16[512,1024]{1,0:T(8,128)(2,1)}, u32[]{:S(2)}, u32[]{:S(2)}) collective-permute-start(bf16[512,1024]{1,0:T(8,128)(2,1)} %b_strips.3), channel_id=1, source_target_pairs={{0,2},{2,0},{4,6},{6,4},{8,10},{10,8},{12,14},{14,12},{1,3},{3,1},... | collective-permute-start | bytes 3145736 | tf_op jit(solution)/shard_map/ppermute | solution.py:295
  7.2 2.2 copy-start.4
  9.4 2.2 copy-start.3
  9.9 65.5 %collective-permute-start = (bf16[256,4096]{1,0:T(8,128)(2,1)S(1)}, bf16[256,4096]{1,0:T(8,128)(2,1)}, u32[]{:S(2)}, u32[]{:S(2)}) collective-permute-start(bf16[256,4096]{1,0:T(8,128)(2,1)S(1)} %masked_half.2.refs_0_), channel_id=1, source_target_pairs={{0,2},{2,0},{4,6},{6,4},{8,10},{10,8},{12,14},{14,12},{1,3},{3,1},... | collective-permute-start | bytes 6291464 | tf_op jit(solution)/shard_map/ppermute | solution.py:295
  12.3 27.2 %collective-permute-start.2 = (bf16[512,1024]{1,0:T(8,128)(2,1)S(1)}, bf16[512,1024]{1,0:T(8,128)(2,1)}, u32[]{:S(2)}, u32[]{:S(2)}) collective-permute-start(bf16[512,1024]{1,0:T(8,128)(2,1)S(1)} %b_strips.2.refs_4_.refs_10_), channel_id=1, source_target_pairs={{0,4},{2,6},{12,8},{14,10},{1,5},{3,7},{13,9},{15,11},{16,20},{18,... | collective-permute-start | bytes 3145736 | tf_op jit(solution)/shard_map/ppermute | solution.py:295
  31.2 29.3 %collective-permute-start.5 = (bf16[512,1024]{1,0:T(8,128)(2,1)}, bf16[512,1024]{1,0:T(8,128)(2,1)}, u32[]{:S(2)}, u32[]{:S(2)}) collective-permute-start(bf16[512,1024]{1,0:T(8,128)(2,1)} %collective-permute-done.4.refs_5_.refs_11_), channel_id=1, source_target_pairs={{0,4},{2,6},{12,8},{14,10},{1,5},{3,7},{13,9},{15,11},{16,20},{18,... | collective-permute-start | bytes 3145736 | tf_op jit(solution)/shard_map/ppermute | solution.py:295
  36.3 42.3 %collective-permute-start.9 = (bf16[512,1024]{1,0:T(8,128)(2,1)S(1)}, bf16[512,1024]{1,0:T(8,128)(2,1)}, u32[]{:S(2)}, u32[]{:S(2)}) collective-permute-start(bf16[512,1024]{1,0:T(8,128)(2,1)S(1)} %b_strips.2.refs_4_.refs_10_), channel_id=1, source_target_pairs={{4,8},{6,10},{8,4},{10,6},{5,9},{7,11},{9,5},{11,7},{20,24},{22,26... | collective-permute-start | bytes 3145736 | tf_op jit(solution)/shard_map/ppermute | solution.py:295
  37.9 41.9 %collective-permute-start.10 = (bf16[512,1024]{1,0:T(8,128)(2,1)}, bf16[512,1024]{1,0:T(8,128)(2,1)}, u32[]{:S(2)}, u32[]{:S(2)}) collective-permute-start(bf16[512,1024]{1,0:T(8,128)(2,1)} %collective-permute-done.4.refs_5_.refs_11_), channel_id=1, source_target_pairs={{4,8},{6,10},{8,4},{10,6},{5,9},{7,11},{9,5},{11,7},{20,24},{22,26... | collective-permute-start | bytes 3145736 | tf_op jit(solution)/shard_map/ppermute | solution.py:295
  39.6 41.5 %collective-permute-start.3 = (bf16[512,1024]{1,0:T(8,128)(2,1)}, bf16[512,1024]{1,0:T(8,128)(2,1)}, u32[]{:S(2)}, u32[]{:S(2)}) collective-permute-start(bf16[512,1024]{1,0:T(8,128)(2,1)} %collective-permute-done.2.refs_8_), channel_id=1, source_target_pairs={{4,8},{6,10},{8,4},{10,6},{5,9},{7,11},{9,5},{11,7},{20,24},{22,26... | collective-permute-start | bytes 3145736 | tf_op jit(solution)/shard_map/ppermute | solution.py:295
  60.5 21.9 %collective-permute-start.6 = (bf16[512,1024]{1,0:T(8,128)(2,1)}, bf16[512,1024]{1,0:T(8,128)(2,1)}, u32[]{:S(2)}, u32[]{:S(2)}) collective-permute-start(bf16[512,1024]{1,0:T(8,128)(2,1)} %collective-permute-done.5.refs_9_), channel_id=1, source_target_pairs={{4,8},{6,10},{8,4},{10,6},{5,9},{7,11},{9,5},{11,7},{20,24},{22,26... | collective-permute-start | bytes 3145736 | tf_op jit(solution)/shard_map/ppermute | solution.py:295
  75.3 93.1 %collective-permute-start.1 = (bf16[256,4096]{1,0:T(8,128)(2,1)}, bf16[256,4096]{1,0:T(8,128)(2,1)}, u32[]{:S(2)}, u32[]{:S(2)}) collective-permute-start(bf16[256,4096]{1,0:T(8,128)(2,1)} %collective-permute-done.refs_2_), channel_id=1, source_target_pairs={{0,1},{1,0},{2,3},{3,2},{4,5},{5,4},{6,7},{7,6},{8,9},{9,8},{10,11... | collective-permute-start | bytes 6291464 | tf_op jit(solution)/shard_map/ppermute | solution.py:315
  78.5 25.3 %collective-permute-start.11 = (bf16[512,896]{1,0:T(8,128)(2,1)}, bf16[512,896]{1,0:T(8,128)(2,1)}, u32[]{:S(2)}, u32[]{:S(2)}) collective-permute-start(bf16[512,896]{1,0:T(8,128)(2,1)} %constant_dynamic-slice_fusion.1), channel_id=1, source_target_pairs={{4,0},{6,2},{8,12},{10,14},{5,1},{7,3},{9,13},{11,15},{20,16},{22,... | collective-permute-start | bytes 2752520 | tf_op jit(solution)/shard_map/ppermute | solution.py:295
  79.8 43.7 %collective-permute-start.12 = (bf16[512,896]{1,0:T(8,128)(2,1)}, bf16[512,896]{1,0:T(8,128)(2,1)}, u32[]{:S(2)}, u32[]{:S(2)}) collective-permute-start(bf16[512,896]{1,0:T(8,128)(2,1)} %constant_dynamic-slice_fusion), channel_id=1, source_target_pairs={{4,0},{6,2},{8,12},{10,14},{5,1},{7,3},{9,13},{11,15},{20,16},{22,... | collective-permute-start | bytes 2752520 | tf_op jit(solution)/shard_map/ppermute | solution.py:295
  81.1 64.9 %collective-permute-start.13 = (bf16[512,1024]{1,0:T(8,128)(2,1)}, bf16[512,1024]{1,0:T(8,128)(2,1)}, u32[]{:S(2)}, u32[]{:S(2)}) collective-permute-start(bf16[512,1024]{1,0:T(8,128)(2,1)} %collective-permute-done.9.refs_6_), channel_id=1, source_target_pairs={{4,0},{6,2},{8,12},{10,14},{5,1},{7,3},{9,13},{11,15},{20,16},{22,... | collective-permute-start | bytes 3145736 | tf_op jit(solution)/shard_map/ppermute | solution.py:295
  82.4 86.0 %collective-permute-start.14 = (bf16[512,1024]{1,0:T(8,128)(2,1)}, bf16[512,1024]{1,0:T(8,128)(2,1)}, u32[]{:S(2)}, u32[]{:S(2)}) collective-permute-start(bf16[512,1024]{1,0:T(8,128)(2,1)} %collective-permute-done.10.refs_7_), channel_id=1, source_target_pairs={{4,0},{6,2},{8,12},{10,14},{5,1},{7,3},{9,13},{11,15},{20,16},{22,... | collective-permute-start | bytes 3145736 | tf_op jit(solution)/shard_map/ppermute | solution.py:295
  103.9 84.3 %collective-permute-start.7 = (bf16[512,896]{1,0:T(8,128)(2,1)}, bf16[512,896]{1,0:T(8,128)(2,1)}, u32[]{:S(2)}, u32[]{:S(2)}) collective-permute-start(bf16[512,896]{1,0:T(8,128)(2,1)} %constant_dynamic-slice_fusion.3), channel_id=1, source_target_pairs={{4,0},{6,2},{8,12},{10,14},{5,1},{7,3},{9,13},{11,15},{20,16},{22,... | collective-permute-start | bytes 2752520 | tf_op jit(solution)/shard_map/ppermute | solution.py:295
  123.5 83.9 %collective-permute-start.8 = (bf16[512,896]{1,0:T(8,128)(2,1)}, bf16[512,896]{1,0:T(8,128)(2,1)}, u32[]{:S(2)}, u32[]{:S(2)}) collective-permute-start(bf16[512,896]{1,0:T(8,128)(2,1)} %constant_dynamic-slice_fusion.2), channel_id=1, source_target_pairs={{4,0},{6,2},{8,12},{10,14},{5,1},{7,3},{9,13},{11,15},{20,16},{22,... | collective-permute-start | bytes 2752520 | tf_op jit(solution)/shard_map/ppermute | solution.py:295
  124.8 2.2 copy-start.5
  127.4 1.3 copy-start
  168.5 1.6 copy-start.1
  185.0 32.2 %copy-start.7 = (s32[4,64]{1,0:T(4,128)S(1)}, s32[4,64]{1,0:T(4,128)}, u32[]{:S(2)}) copy-start(s32[4,64]{1,0:T(4,128)} %param.7) | copy-start | bytes 3076
  215.2 2.2 collective-permute-start.15
  215.3 15.0 %collective-permute-start.16 = (bf16[256,1024]{1,0:T(8,128)(2,1)}, bf16[256,1024]{1,0:T(8,128)(2,1)S(1)}, u32[]{:S(2)}, u32[]{:S(2)}) collective-permute-start(bf16[256,1024]{1,0:T(8,128)(2,1)} %get-tuple-element.11), channel_id=1, source_target_pairs={{0,2},{2,0},{4,6},{6,4},{8,10},{10,8},{12,14},{14,12},{1,3},{3,1},... | collective-permute-start | bytes 1572872 | tf_op jit(solution)/shard_map/ppermute | solution.py:295
  217.1 23.5 %collective-permute-start.17 = (bf16[256,1024]{1,0:T(8,128)(2,1)S(1)}, bf16[256,1024]{1,0:T(8,128)(2,1)S(1)}, u32[]{:S(2)}, u32[]{:S(2)}) collective-permute-start(bf16[256,1024]{1,0:T(8,128)(2,1)S(1)} %get-tuple-element.12), channel_id=1, source_target_pairs={{0,3},{1,2},{2,1},{3,0},{4,7},{5,6},{6,5},{7,4},{8,11},{9,10},{10,... | collective-permute-start | bytes 1572872 | tf_op jit(solution)/shard_map/ppermute | solution.py:351

commit v2 on v1

v2 whole, which is shorter than its diff:
```python
import functools

import jax
import jax.numpy as jnp
from jax import lax
from jax.experimental import pallas as pl
from jax.experimental.pallas import tpu as pltpu
from jax.sharding import PartitionSpec as P

LANES = 128
MIB = 1 << 20


def shifted(shard, axis, by):
    count = lax.axis_size(axis)
    return lax.ppermute(shard, axis, [(i, (i + by) % count) for i in range(count)])


def expand_blocks(mask, block):
    rows, cols = mask.shape
    wide = jnp.broadcast_to(mask[:, None, :, None], (rows, block, cols, block))
    return wide.reshape(rows * block, cols * block)


def ring(x_band, w_band, a_mask, keep_mask):
    panel = x_band.shape[0]
    block = panel // a_mask.shape[0]
    band_cols = x_band.shape[1]
    xm = x_band * expand_blocks(a_mask, block).astype(jnp.bfloat16)
    rows = lax.broadcasted_iota(jnp.int32, x_band.shape, 0)
    cols = lax.broadcasted_iota(jnp.int32, x_band.shape, 1)
    identity = jnp.where(cols == rows + 4 * panel, 1.0, 0.0).astype(jnp.float32)
    b_panel = (1.5 * identity - 0.5 * w_band.astype(jnp.float32)).astype(jnp.bfloat16)
    layer = lax.axis_index("depth")
    current = shifted(b_panel, ("grid", "depth"), -5)
    wide = jnp.zeros((panel, 2 * band_cols), jnp.float32)
    for step in range(4):
        offset = 6 + layer - 2 * step
        ablock = lax.dynamic_slice_in_dim(xm, offset * panel, panel, 1)
        term = jnp.dot(ablock, current, preferred_element_type=jnp.float32)
        region = lax.dynamic_slice_in_dim(wide, offset * panel, band_cols, 1)
        wide = lax.dynamic_update_slice_in_dim(wide, region + term, offset * panel, 1)
        if step < 3:
            current = shifted(current, "grid", 2)
    partial_band = wide[:, 4 * panel : 12 * panel]
    mine = lax.psum_scatter(partial_band, "depth", scatter_dimension=0, tiled=True)
    keep = expand_blocks(keep_mask, block).astype(jnp.float32)
    return (mine * keep).astype(jnp.bfloat16)


def strips_kernel(quarter_ref, w_ref, b_ref, held, sems):
    panel = held.shape[0]
    quarter = quarter_ref[0]
    band = held.shape[1] // LANES
    copies = []
    for j in range(band):
        at = pl.multiple_of(j * panel + quarter * LANES, LANES)
        copies.append(
            pltpu.make_async_copy(
                w_ref.at[:, pl.ds(at, LANES)],
                held.at[:, j * LANES : (j + 1) * LANES],
                sems.at[j],
            )
        )
        copies[-1].start()
    for j in range(band):
        copies[j].wait()
        value = -0.5 * held[:, j * LANES : (j + 1) * LANES].astype(jnp.float32)
        if j == band // 2:
            rows = lax.broadcasted_iota(jnp.int32, value.shape, 0)
            cols = lax.broadcasted_iota(jnp.int32, value.shape, 1)
            value = value + jnp.where(rows == cols + quarter * LANES, 1.5, 0.0)
        b_ref[:, j * LANES : (j + 1) * LANES] = value.astype(jnp.bfloat16)


def b_strips(w_band, quarter):
    panel = w_band.shape[0]
    band = w_band.shape[1] // panel
    shape = (panel, band * LANES)
    return pl.pallas_call(
        strips_kernel,
        out_shape=jax.ShapeDtypeStruct(shape, jnp.bfloat16),
        in_specs=[
            pl.BlockSpec(memory_space=pltpu.SMEM),
            pl.BlockSpec(memory_space=pl.ANY),
        ],
        out_specs=pl.BlockSpec(memory_space=pltpu.VMEM),
        scratch_shapes=[pltpu.VMEM(shape, jnp.bfloat16), pltpu.SemaphoreType.DMA((band,))],
        compiler_params=pltpu.CompilerParams(vmem_limit_bytes=16 * MIB),
        cost_estimate=pl.CostEstimate(flops=1000, bytes_accessed=4 * shape[0] * shape[1], transcendentals=0),
        name="b_strips",
    )(quarter.reshape(1), w_band)


def mask_kernel(half_ref, mask_ref, x_ref, out_ref):
    out_ref[...] = (x_ref[...].astype(jnp.float32) * mask_ref[0]).astype(jnp.bfloat16)


def masked_half(x_band, mask_wide, half):
    block = x_band.shape[0] // mask_wide.shape[0]
    per_half = mask_wide.shape[0] // 2
    cols = x_band.shape[1]
    return pl.pallas_call(
        mask_kernel,
        grid_spec=pltpu.PrefetchScalarGridSpec(
            num_scalar_prefetch=1,
            grid=(per_half,),
            in_specs=[
                pl.BlockSpec((1, 1, cols), lambda i, h: (h[0] * per_half + i, 0, 0)),
                pl.BlockSpec((block, cols), lambda i, h: (h[0] * per_half + i, 0)),
            ],
            out_specs=pl.BlockSpec((block, cols), lambda i, h: (i, 0)),
        ),
        out_shape=jax.ShapeDtypeStruct((x_band.shape[0] // 2, cols), jnp.bfloat16),
        compiler_params=pltpu.CompilerParams(vmem_limit_bytes=16 * MIB),
        cost_estimate=pl.CostEstimate(flops=1000, bytes_accessed=2 * x_band.shape[0] * cols, transcendentals=0),
        name="masked_half",
    )(half.reshape(1), mask_wide, x_band)


def x_copies(x_refs, xv, sems, offset_of):
    n_b, _, rows, panel = xv.shape
    half = rows // 2
    copies = {}
    for p in range(n_b):
        for r in range(4):
            at = pl.multiple_of(offset_of(p, r // 2) * panel, panel)
            copies[p, r] = pltpu.make_async_copy(
                x_refs[r].at[:, pl.ds(at, panel)],
                xv.at[p, r // 2, (r % 2) * half : (r % 2 + 1) * half],
                sems.at[p, r],
            )
    return copies


def add_products(acc, xv, p, strips, offset_of, start):
    def step(g, carry):
        at = (offset_of(p, g) + start) * LANES
        cols = pl.ds(pl.multiple_of(at, LANES), strips.shape[1])
        acc[g, :, cols] += jnp.dot(xv[p, g], strips[...], preferred_element_type=jnp.float32)
        return carry

    lax.fori_loop(0, 2, step, 0)


def first_kernel(windows, meta_ref, *refs):
    n_b = len(windows)
    x_refs, middle_refs, end_refs = refs[:4], refs[4 : 4 + n_b], refs[4 + n_b : 4 + 2 * n_b]
    out_ref, xv, bv, acc, x_sems, b_sems, out_sem = refs[4 + 2 * n_b :]
    quarter = bv.shape[2]
    low = quarter // 2
    is_end = meta_ref[0]

    def offset_of(p, g):
        return meta_ref[1 + 2 * p + g]

    def b_copies(p):
        start, width = windows[p]
        target = bv.at[p, :, start * LANES : (start + width) * LANES]
        return (
            pltpu.make_async_copy(middle_refs[p], bv.at[p], b_sems.at[p]),
            pltpu.make_async_copy(end_refs[p], target, b_sems.at[p]),
        )

    copies = x_copies(x_refs, xv, x_sems, offset_of)
    for p in range(n_b):
        middle, end = b_copies(p)
        pl.when(is_end == 0)(middle.start)
        pl.when(is_end != 0)(end.start)
        for r in range(4):
            copies[p, r].start()
    acc[...] = jnp.zeros_like(acc)
    for p in range(n_b):
        middle, end = b_copies(p)
        pl.when(is_end == 0)(middle.wait)
        pl.when(is_end != 0)(end.wait)
        for r in range(4):
            copies[p, r].wait()
        add_products(acc, xv, p, bv.at[p], offset_of, 0)
    out = pltpu.make_async_copy(acc.at[:, :, low : low + quarter], out_ref, out_sem)
    out.start()
    out.wait()


def first_products(meta, xs, middle, end, windows):
    rows = xs[0].shape[0]
    panel, quarter = middle[0].shape
    n_b = len(middle)
    any_spec = pl.BlockSpec(memory_space=pl.ANY)
    operands = [meta, *xs, *middle, *end]
    return pl.pallas_call(
        functools.partial(first_kernel, windows),
        out_shape=jax.ShapeDtypeStruct((2, 2 * rows, quarter), jnp.float32),
        in_specs=[pl.BlockSpec(memory_space=pltpu.SMEM)] + [any_spec] * (len(operands) - 1),
        out_specs=any_spec,
        scratch_shapes=[
            pltpu.VMEM((n_b, 2, 2 * rows, panel), jnp.bfloat16),
            pltpu.VMEM((n_b, panel, quarter), jnp.bfloat16),
            pltpu.VMEM((2, 2 * rows, 2 * quarter), jnp.float32),
            pltpu.SemaphoreType.DMA((n_b, 4)),
            pltpu.SemaphoreType.DMA((n_b,)),
            pltpu.SemaphoreType.DMA,
        ],
        compiler_params=pltpu.CompilerParams(vmem_limit_bytes=32 * MIB),
        cost_estimate=pl.CostEstimate(
            flops=2 * n_b * 4 * rows * panel * quarter,
            bytes_accessed=n_b * 2 * (4 * rows * panel + panel * quarter),
            transcendentals=0,
        ),
        name="first_products",
    )(*operands)


def give_pieces(out_refs, acc, at):
    half, width = out_refs[0].shape
    cols = pl.ds(pl.multiple_of(at * LANES, LANES), width)
    for r in range(4):
        rows = slice((r % 2) * half, (r % 2 + 1) * half)
        out_refs[r][...] = acc[r // 2, rows, cols].astype(jnp.bfloat16)


def half_kernel(meta_ref, *refs):
    x_refs, prev_ref, middle_ref, end_ref, second_ref = refs[:4], *refs[4:8]
    out_refs, rest_ref, xv, bv, acc, x_sems, b_sems, prev_sem, rest_sem = refs[8:12], *refs[12:]
    quarter = bv.shape[2]
    half = quarter // 2
    low = quarter // 2
    band = quarter // LANES
    is_end = meta_ref[0]

    def offset_of(p, g):
        return meta_ref[5 + 2 * p + g]

    copies = x_copies(x_refs, xv, x_sems, offset_of)
    middle = pltpu.make_async_copy(middle_ref, bv.at[0], b_sems.at[0])
    end = pltpu.make_async_copy(end_ref, bv.at[0], b_sems.at[0])
    second = pltpu.make_async_copy(second_ref, bv.at[1], b_sems.at[1])
    prev = pltpu.make_async_copy(prev_ref, acc.at[:, :, low : low + quarter], prev_sem)
    prev.start()
    for copy in copies.values():
        copy.start()

    @pl.when(is_end == 0)
    def _():
        middle.start()
        second.start()

    pl.when(is_end != 0)(end.start)
    prev.wait()
    for copy in copies.values():
        copy.wait()
    pl.when(is_end == 0)(middle.wait)
    pl.when(is_end != 0)(end.wait)
    for p in range(2):
        add_products(acc, xv, p, bv.at[0, :, p * half : (p + 1) * half], offset_of, meta_ref[1])

    @pl.when(is_end == 0)
    def _():
        second.wait()
        for p in range(2):
            add_products(acc, xv, p, bv.at[1, :, p * half : (p + 1) * half], offset_of, meta_ref[2])

    at = pl.multiple_of((meta_ref[4] + band // 2) * LANES, LANES)
    rest = pltpu.make_async_copy(acc.at[:, :, pl.ds(at, rest_ref.shape[2])], rest_ref, rest_sem)
    rest.start()
    give_pieces(out_refs, acc, meta_ref[3] + band // 2)
    rest.wait()


def half_products(meta, xs, prev, middle, end, second, n_done):
    rows = xs[0].shape[0]
    panel, quarter = middle.shape
    any_spec = pl.BlockSpec(memory_space=pl.ANY)
    n_rest = quarter // LANES - n_done
    return pl.pallas_call(
        half_kernel,
        out_shape=[jax.ShapeDtypeStruct((rows, n_done * LANES), jnp.bfloat16)] * 4
        + [jax.ShapeDtypeStruct((2, 2 * rows, n_rest * LANES), jnp.float32)],
        in_specs=[pl.BlockSpec(memory_space=pltpu.SMEM)] + [any_spec] * 8,
        out_specs=[pl.BlockSpec(memory_space=pltpu.VMEM)] * 4 + [any_spec],
        scratch_shapes=[
            pltpu.VMEM((2, 2, 2 * rows, panel), jnp.bfloat16),
            pltpu.VMEM((2, panel, quarter), jnp.bfloat16),
            pltpu.VMEM((2, 2 * rows, 2 * quarter), jnp.float32),
            pltpu.SemaphoreType.DMA((2, 4)),
            pltpu.SemaphoreType.DMA((2,)),
            pltpu.SemaphoreType.DMA,
            pltpu.SemaphoreType.DMA,
        ],
        compiler_params=pltpu.CompilerParams(vmem_limit_bytes=24 * MIB),
        cost_estimate=pl.CostEstimate(
            flops=2 * 2 * 4 * rows * panel * quarter, bytes_accessed=10 * MIB, transcendentals=0
        ),
        name="half_products",
    )(meta, *xs, prev, middle, end, second)


def rest_kernel(meta_ref, *refs):
    x_refs, rest_ref, b_ref = refs[:4], *refs[4:6]
    out_refs, xv, bv, acc, x_sems, b_sem, rest_sem = refs[6:10], *refs[10:]
    band = acc.shape[2] // (2 * LANES)
    half = bv.shape[1] // 2
    is_end = meta_ref[0]

    def offset_of(p, g):
        return meta_ref[3 + 2 * p + g]

    at = pl.multiple_of((meta_ref[2] + band // 2) * LANES, LANES)
    rest = pltpu.make_async_copy(rest_ref, acc.at[:, :, pl.ds(at, rest_ref.shape[2])], rest_sem)
    rest.start()
    copies = x_copies(x_refs, xv, x_sems, offset_of)
    b_copy = pltpu.make_async_copy(b_ref, bv, b_sem)

    @pl.when(is_end != 0)
    def _():
        b_copy.start()
        for copy in copies.values():
            copy.start()

    rest.wait()

    @pl.when(is_end != 0)
    def _():
        b_copy.wait()
        for copy in copies.values():
            copy.wait()
        for p in range(2):
            add_products(acc, xv, p, bv.at[:, p * half : (p + 1) * half], offset_of, meta_ref[1])

    give_pieces(out_refs, acc, meta_ref[2] + band // 2)


def rest_products(meta, xs, rest, b, quarter):
    rows = xs[0].shape[0]
    panel = b.shape[0]
    width = rest.shape[2]
    any_spec = pl.BlockSpec(memory_space=pl.ANY)
    return pl.pallas_call(
        rest_kernel,
        out_shape=[jax.ShapeDtypeStruct((rows, width), jnp.bfloat16)] * 4,
        in_specs=[pl.BlockSpec(memory_space=pltpu.SMEM)] + [any_spec] * 6,
        out_specs=[pl.BlockSpec(memory_space=pltpu.VMEM)] * 4,
        scratch_shapes=[
            pltpu.VMEM((2, 2, 2 * rows, panel), jnp.bfloat16),
            pltpu.VMEM(b.shape, jnp.bfloat16),
            pltpu.VMEM((2, 2 * rows, 2 * quarter), jnp.float32),
            pltpu.SemaphoreType.DMA((2, 4)),
            pltpu.SemaphoreType.DMA,
            pltpu.SemaphoreType.DMA,
        ],
        compiler_params=pltpu.CompilerParams(vmem_limit_bytes=24 * MIB),
        cost_estimate=pl.CostEstimate(
            flops=2 * 4 * rows * panel * b.shape[1], bytes_accessed=5 * MIB, transcendentals=0
        ),
        name="rest_products",
    )(meta, *xs, rest, b)


def assemble_kernel(place_ref, mask_ref, *refs):
    *pieces, out_ref = refs
    n = len(pieces) // 2
    done, rest = pieces[:n], pieces[n:]
    n_done, n_rest = done[0].shape[1] // LANES, rest[0].shape[1] // LANES
    panel = n * LANES
    for left in range(2):
        for mine in range(n):

            @pl.when((place_ref[0] == mine) & (place_ref[1] == left))
            def _():
                for j in range(n_done + n_rest):
                    if left:
                        source, at = (rest, j) if j < n_rest else (done, j - n_rest)
                    else:
                        source, at = (done, j) if j < n_done else (rest, j - n_done)
                    for t in range(n):
                        cols = slice(j * panel + t * LANES, j * panel + (t + 1) * LANES)
                        value = source[t ^ mine][:, at * LANES : (at + 1) * LANES].astype(jnp.float32)
                        out_ref[:, cols] = (value * mask_ref[0, :, cols]).astype(jnp.bfloat16)


def assembled(place, keep_wide, done, rest):
    rows = done[0].shape[0]
    steps = keep_wide.shape[0]
    block = rows // steps
    cols = keep_wide.shape[2]
    return pl.pallas_call(
        assemble_kernel,
        grid_spec=pltpu.PrefetchScalarGridSpec(
            num_scalar_prefetch=1,
            grid=(steps,),
            in_specs=[pl.BlockSpec((1, 1, cols), lambda i, q: (i, 0, 0))]
            + [pl.BlockSpec((block, piece.shape[1]), lambda i, q: (i, 0)) for piece in done + rest],
            out_specs=pl.BlockSpec((block, cols), lambda i, q: (i, 0)),
        ),
        out_shape=jax.ShapeDtypeStruct((rows, cols), jnp.bfloat16),
        compiler_params=pltpu.CompilerParams(vmem_limit_bytes=16 * MIB),
        cost_estimate=pl.CostEstimate(flops=1000, bytes_accessed=4 * rows * cols, transcendentals=0),
        name="assembled",
    )(place, keep_wide, *done, *rest)


def widen(mask, block):
    rows, cols = mask.shape
    wide = jnp.broadcast_to(mask.astype(jnp.float32)[:, :, None], (rows, cols, block))
    return wide.reshape(rows, 1, cols * block)


def together(*values):
    return lax.optimization_barrier(values)


def pairs_in_line(x_band, w_band, a_mask, keep_mask):
    panel = x_band.shape[0]
    block = panel // a_mask.shape[0]
    g, c = lax.axis_index("grid"), lax.axis_index("depth")
    z, y = g // 2, g % 2
    left = z < 2
    is_end = ((z == 0) | (z == 3)).astype(jnp.int32)
    toward = jnp.where(left, 1, -1)
    q = 2 * y + c

    swap = [(0, 2), (1, 3), (2, 0), (3, 1), (4, 6), (5, 7), (6, 4), (7, 5)]
    outward = [(2, 0), (3, 1), (4, 6), (5, 7)]
    cross = [(2, 4), (3, 5), (4, 2), (5, 3)]
    across = [(i, i ^ 1) for i in range(8)]
    layers = [(0, 1), (1, 0)]
    opposite = [(i, i ^ 3) for i in range(16)]

    def line(value, pairs):
        return lax.ppermute(value, "grid", pairs)

    def strips(value, start, count):
        return lax.dynamic_slice_in_dim(value, start * LANES, count * LANES, 1)

    first_out, second_out = jnp.where(left, 0, 4), jnp.where(left, 4, 0)
    first_in, second_in = second_out, first_out
    last_in = jnp.where(left, 1, 4)

    own_a = b_strips(w_band, q)
    swap_a = line(own_a, swap)
    cross_a = line(own_a, cross)
    own_b = line(b_strips(w_band, q ^ 2), across)
    mask_wide = widen(a_mask, block)
    x_mine = masked_half(x_band, mask_wide, c)
    own_b, x_mine = together(own_b, x_mine)
    swap_b = line(own_b, swap)
    cross_b = line(own_b, cross)
    x_across = line(x_mine, across)
    x_rest = masked_half(x_band, mask_wide, 1 - c)

    swap_a, cross_a, swap_b, cross_b = together(swap_a, cross_a, swap_b, cross_b)
    even = jnp.where(y == 0, cross_a, cross_b)
    odd = jnp.where(y == 0, cross_b[:, 3 * LANES :], cross_a[:, 3 * LANES :])
    mid = line(jnp.concatenate([even, odd], 1), outward)
    fwd_first = line(jnp.concatenate([strips(v, first_out, 4) for v in (swap_a, swap_b)], 1), cross)
    fwd_second_out = jnp.concatenate([strips(v, second_out, 4) for v in (swap_a, swap_b)], 1)
    fwd_first, fwd_second_out, x_across, mid = together(fwd_first, fwd_second_out, x_across, mid)
    fwd_second = line(fwd_second_out, cross)
    x_opposite = lax.ppermute(x_across, "depth", layers)
    xs = [x_mine, x_rest, x_across, x_opposite]
    far_first = line(fwd_first, outward)

    def offsets(delta):
        tilt = 2 * y - 1
        return [(2 * delta + 4) % 8, (2 * delta + tilt + 4) % 8, (2 * delta - tilt + 4) % 8, (2 * delta + 4) % 8]

    zero = jnp.zeros_like(z)
    third = [
        jnp.where(is_end == 1, ours, theirs)
        for ours, theirs in zip([8 - y, 7 + y, 9 - y, 8 + y], offsets(-toward))
    ]
    third = [v % 8 for v in third]
    fourth = offsets(jnp.where(is_end == 1, -toward, 2))
    meta = jnp.stack([is_end, *offsets(zero), *offsets(toward), *third]).astype(jnp.int32)
    whole = (0, 8)
    total = first_products(
        meta,
        xs,
        [own_a, own_b, cross_a, cross_b, swap_a, swap_b],
        [own_a, own_b, swap_a, swap_b, mid[:, : 8 * LANES], mid[:, 8 * LANES :]],
        [whole, whole, whole, whole, whole, (3, 5)],
    )
    fwd_second, far_first, total = together(fwd_second, far_first, total)
    last = jnp.concatenate([strips(fwd_second, jnp.where(left, 1, 0), 3), strips(fwd_second, jnp.where(left, 5, 4), 3)], 1)
    far_second = line(last, outward)

    def exchanged(pieces):
        return [
            pieces[0],
            lax.ppermute(pieces[1], "depth", layers),
            line(pieces[2], across),
            lax.ppermute(pieces[3], ("grid", "depth"), opposite),
        ]

    done_at, rest_at = jnp.where(left, 3, 0), jnp.where(left, 0, 5)
    meta = jnp.stack([is_end, first_in, second_in, done_at, rest_at, *fourth]).astype(jnp.int32)
    *done, rest = half_products(meta, xs, total, fwd_first, far_first, fwd_second, 5)
    far_second, *done = together(far_second, *exchanged(done))
    meta = jnp.stack([is_end, last_in, rest_at, *fourth]).astype(jnp.int32)
    rest = exchanged(rest_products(meta, xs, rest, far_second, own_a.shape[1]))
    place = jnp.stack([q, left.astype(jnp.int32)]).astype(jnp.int32)
    return assembled(place, widen(keep_mask, block), done, rest)


def solution(mesh):
    placed = (
        P(("groups", "grid"), None),
        P(("groups", "grid"), None),
        P(("groups", "grid"), None),
        P(("groups", "grid", "depth"), None),
    )

    def local(x_band, w_band, a_mask, keep_mask):
        panel, cols = x_band.shape
        pairs = mesh.shape["grid"] == 8 and mesh.shape["depth"] == 2
        pairs = pairs and cols == 8 * panel and panel == 4 * LANES
        return (pairs_in_line if pairs else ring)(x_band, w_band, a_mask, keep_mask)

    return jax.shard_map(
        local,
        mesh=mesh,
        in_specs=placed,
        out_specs=P(("groups", "grid", "depth"), None),
        check_vma=False,
    )
```

time: 243 us -> 189 us (0.78)
  waiting for transfers between devices: 166 us -> 104 us
  starting transfers between devices: 29 us -> 22.1 us
  other arithmetic: 0.01 us -> 6.36 us
  local copies, waits for them, and re-layouts: 19.4 us -> 25.4 us
  Pallas kernels: 28 us -> 30.8 us
    ppermute x17, waiting for transfers between devices: 166 us -> 104 us  [the longest x13 94.4 us: line(): return lax.ppermute(value, 'grid', pairs)]
    unnamed x16 -> x32, local copies, waits for them, and re-layouts: 11.1 us -> 19.4 us
    ppermute x17, starting transfers between devices: 29 us -> 22.1 us  [the longest x13 20.4 us: line(): return lax.ppermute(value, 'grid', pairs)]
    dynamic_slice x4 -> x2, local copies, waits for them, and re-layouts: 7.59 us -> 2.6 us  [strips(): return lax.dynamic_slice_in_dim(value, start * LANES, count * LANES, 1)]
    concatenate x0 -> x4, other arithmetic: none -> 3.58 us  [the longest x1 1.31 us: pairs_in_line(): mid = line(jnp.concatenate([even, odd], 1), outward)]
    select_n x0 -> x2, other arithmetic: none -> 2.7 us  [the longest x1 1.36 us: pairs_in_line(): odd = jnp.where(y == 0, cross_b[:, 3 * LANES:], cross_a[:, 3 * LANES:])]
    slice x0 -> x2, local copies, waits for them, and re-layouts: none -> 2.59 us  [the longest x1 1.44 us: pairs_in_line(): mid[:, :8 * LANES]]
    pallas_call x2 -> x3, Pallas kernels: 22.7 us -> 22.2 us  [the longest x1 11.5 us: first_products(): pl.pallas_call(functools.partial(first_kernel, windows), out_shape=jax.Sh...]
  transfers between devices with their start and end apart: 18 -> 18, of which waited for: 11 -> 9; matrix products, arithmetic and copies ran while one was open for 3% -> 5% of each run, Pallas kernels for 7% -> 11%
where the time goes in v2:
time: 189 us
  waiting for transfers between devices  104 us (55%)
  Pallas kernels  30.8 us (16%)
  local copies, waits for them, and re-layouts  25.4 us (13%)
  starting transfers between devices  22.1 us (12%)
  other arithmetic  6.36 us (3%)
    ppermute x13, waiting for transfers between devices, line(): return lax.ppermute(value, 'grid', pairs)  94.4 us
    ppermute x13, starting transfers between devices, line(): return lax.ppermute(value, 'grid', pairs)  20.4 us
    unnamed x32, local copies, waits for them, and re-layouts  19.4 us
    pallas_call x1, Pallas kernels, first_products(): pl.pallas_call(functools.partial(first_kernel, windows), out_shape=jax.Sh...  11.5 us
    ppermute x2, waiting for transfers between devices, exchanged(): lax.ppermute(pieces[3], ('grid', 'depth'), opposite)  9.22 us
    pallas_call x1, Pallas kernels, half_products(): pl.pallas_call(half_kernel, out_shape=[jax.ShapeDtypeStruct((rows, n_done...  5.99 us
    pallas_call x1, Pallas kernels, rest_products(): pl.pallas_call(rest_kernel, out_shape=[jax.ShapeDtypeStruct((rows, width)...  4.78 us
    pallas_call x1, Pallas kernels, assembled(): pl.pallas_call(assemble_kernel, grid_spec=pltpu.PrefetchScalarGridSpec(nu...  4.29 us
  transfers between devices with their start and end apart: 18, of which 9 were waited for; matrix products, arithmetic and copies ran while one was open for 5% of the time, Pallas kernels for 11%

profile of v2, /device:TPU:0, one launch (start us, length us, event | category | flops | bytes accessed | tf_op | source)
XLA Modules:
  0.0 188.6 jit_solution(4655872596160592327)
XLA Ops:
  0.0 2.2 %copy-done.4 = bf16[512,4096]{1,0:T(8,128)(2,1)S(1)} copy-done((bf16[512,4096]{1,0:T(8,128)(2,1)S(1)}, bf16[512,4096]{1,0:T(8,128)(2,1)}, u32[]{:S(2)}) %copy-start.4) | copy-done | bytes 4194328
  2.2 1.7 b_strips.3
  3.9 3.0 %collective-permute-start.2 = (bf16[512,1024]{1,0:T(8,128)(2,1)}, bf16[512,1024]{1,0:T(8,128)(2,1)}, u32[]{:S(2)}, u32[]{:S(2)}) collective-permute-start(bf16[512,1024]{1,0:T(8,128)(2,1)} %b_strips.3), channel_id=1, source_target_pairs={{0,2},{2,0},{4,6},{6,4},{8,10},{10,8},{12,14},{14,12},{1,3},{3,1},... | collective-permute-start | bytes 3145736 | tf_op jit(solution)/shard_map/ppermute | solution.py:430
  6.9 1.8 b_strips.2.refs_4_.refs_10_
  8.7 1.6 collective-permute-start
  10.3 1.6 collective-permute-start.1
  12.3 2.2 %copy-done.6 = bf16[512,4096]{1,0:T(8,128)(2,1)S(1)} copy-done((bf16[512,4096]{1,0:T(8,128)(2,1)S(1)}, bf16[512,4096]{1,0:T(8,128)(2,1)}, u32[]{:S(2)}) %copy-start.6) | copy-done | bytes 4194328
  14.9 15.4 %collective-permute-done.2.refs_5_.refs_11_ = bf16[512,1024]{1,0:T(8,128)(2,1)} collective-permute-done((bf16[512,1024]{1,0:T(8,128)(2,1)}, bf16[512,1024]{1,0:T(8,128)(2,1)}, u32[]{:S(2)}, u32[]{:S(2)}) %collective-permute-start.2) | collective-permute-done | bytes 1048608 | tf_op jit(solution)/shard_map/ppermute | solution.py:430
  30.4 1.8 collective-permute-start.3
  32.2 1.6 collective-permute-start.4
  33.8 1.5 collective-permute-start.6
  35.3 20.9 %collective-permute-done.3.refs_9_.refs_13_ = bf16[512,1024]{1,0:T(8,128)(2,1)} collective-permute-done((bf16[512,1024]{1,0:T(8,128)(2,1)}, bf16[512,1024]{1,0:T(8,128)(2,1)}, u32[]{:S(2)}, u32[]{:S(2)}) %collective-permute-start.3) | collective-permute-done | bytes 1048608 | tf_op jit(solution)/shard_map/ppermute | solution.py:430
  63.1 1.7 collective-permute-start.5
  65.8 14.3 %collective-permute-done.6.refs_2_ = bf16[256,4096]{1,0:T(8,128)(2,1)} collective-permute-done((bf16[256,4096]{1,0:T(8,128)(2,1)S(1)}, bf16[256,4096]{1,0:T(8,128)(2,1)}, u32[]{:S(2)}, u32[]{:S(2)}) %collective-permute-start.6) | collective-permute-done | bytes 2097184 | tf_op jit(solution)/shard_map/ppermute | solution.py:430
  80.1 22.6 %collective-permute-done.7 = bf16[512,1664]{1,0:T(8,128)(2,1)} collective-permute-done((bf16[512,1664]{1,0:T(8,128)(2,1)}, bf16[512,1664]{1,0:T(8,128)(2,1)}, u32[]{:S(2)}, u32[]{:S(2)}) %collective-permute-start.7) | collective-permute-done | bytes 1703968 | tf_op jit(solution)/shard_map/ppermute | solution.py:430
  102.7 1.6 collective-permute-start.8
  105.6 2.2 %copy-done.7 = bf16[512,4096]{1,0:T(8,128)(2,1)S(1)} copy-done((bf16[512,4096]{1,0:T(8,128)(2,1)S(1)}, bf16[512,4096]{1,0:T(8,128)(2,1)}, u32[]{:S(2)}) %copy-start.7) | copy-done | bytes 4194328
  109.6 1.4 slice.14.refs_14_
  112.2 11.5 %first_products.1.refs_4_ = f32[2,512,1024]{2,1,0:T(8,128)S(1)} custom-call(s32[13]{0:T(128)S(1)} %stack.100.meta_ref, bf16[256,4096]{1,0:T(8,128)(2,1)S(1)} %masked_half.2.refs_0_, bf16[256,4096]{1,0:T(8,128)(2,1)S(1)} %copy-done.1, bf16[256,4096]{1,0:T(8,128)(2,1)} %collective-permute-done.6.refs_2_, bf16[256,4096]{1,0:T(8,128)(2,1)} %collective-permute-done.10.refs_3_, ...), custom_call_target="tpu_custom_call" | custom-call | flops 6442450944 | bytes 12582912 | tf_op jit(solution)/shard_map/first_products/pallas_call | solution.py:191
  123.7 2.0 %copy-done.8 = f32[2,512,1024]{2,1,0:T(8,128)} copy-done((f32[2,512,1024]{2,1,0:T(8,128)}, f32[2,512,1024]{2,1,0:T(8,128)S(1)}, u32[]{:S(2)}) %copy-start.8) | copy-done | bytes 4194328
  125.7 6.4 %collective-permute-done.9.refs_6_ = bf16[512,1024]{1,0:T(8,128)(2,1)} collective-permute-done((bf16[512,1024]{1,0:T(8,128)(2,1)}, bf16[512,1024]{1,0:T(8,128)(2,1)}, u32[]{:S(2)}, u32[]{:S(2)}) %collective-permute-start.9) | collective-permute-done | bytes 1048608 | tf_op jit(solution)/shard_map/ppermute | solution.py:430
  135.8 1.6 copy-done.2
  137.4 2.2 %copy-done.9 = f32[2,512,1024]{2,1,0:T(8,128)S(1)} copy-done((f32[2,512,1024]{2,1,0:T(8,128)S(1)}, f32[2,512,1024]{2,1,0:T(8,128)}, u32[]{:S(2)}) %copy-start.9) | copy-done | bytes 4194328
  139.5 6.0 %half_products.1 = (bf16[256,640]{1,0:T(8,128)(2,1)S(1)}, bf16[256,640]{1,0:T(8,128)(2,1)}, bf16[256,640]{1,0:T(8,128)(2,1)}, bf16[256,640]{1,0:T(8,128)(2,1)}, f32[2,512,384]{2,1,0:T(8,128)S(1)}) custom-call(s32[9]{0:T(128)S(1)} %stack.108.meta_ref, bf16[256,4096]{1,0:T(8,128)(2,1)S(1)} %masked_half.2.refs_0_, bf16[256,4096]{1,0:T(8,128)(2,1)S(1)} %copy-done.2, ...), custom_call_target="tpu_custom_call" | custom-call | flops 2147483648 | bytes 10485760 | tf_op jit(solution)/shard_map/half_products/pallas_call | solution.py:275
  148.7 8.9 %collective-permute-done.13.refs_2_ = bf16[256,640]{1,0:T(8,128)(2,1)} collective-permute-done((bf16[256,640]{1,0:T(8,128)(2,1)}, bf16[256,640]{1,0:T(8,128)(2,1)}, u32[]{:S(2)}, u32[]{:S(2)}) %collective-permute-start.13) | collective-permute-done | bytes 327712 | tf_op jit(solution)/shard_map/ppermute | solution.py:430
  157.5 6.2 %collective-permute-done.14.refs_3_ = bf16[256,640]{1,0:T(8,128)(2,1)} collective-permute-done((bf16[256,640]{1,0:T(8,128)(2,1)}, bf16[256,640]{1,0:T(8,128)(2,1)}, u32[]{:S(2)}, u32[]{:S(2)}) %collective-permute-start.14) | collective-permute-done | bytes 327712 | tf_op jit(solution)/shard_map/ppermute | solution.py:492
  163.8 1.6 copy-done.3
  165.4 1.4 copy-done.11
  166.8 4.8 %rest_products.1 = (bf16[256,384]{1,0:T(8,128)(2,1)S(1)}, bf16[256,384]{1,0:T(8,128)(2,1)}, bf16[256,384]{1,0:T(8,128)(2,1)}, bf16[256,384]{1,0:T(8,128)(2,1)}) custom-call(s32[7]{0:T(128)S(1)} %stack.110.meta_ref, bf16[256,4096]{1,0:T(8,128)(2,1)S(1)} %masked_half.2.refs_0_, bf16[256,4096]{1,0:T(8,128)(2,1)S(1)} %copy-done.3, ...), custom_call_target="tpu_custom_call" | custom-call | flops 805306368 | bytes 5242880 | tf_op jit(solution)/shard_map/rest_products/pallas_call | solution.py:338
  174.4 6.0 %collective-permute-done.16.refs_6_ = bf16[256,384]{1,0:T(8,128)(2,1)S(1)} collective-permute-done((bf16[256,384]{1,0:T(8,128)(2,1)}, bf16[256,384]{1,0:T(8,128)(2,1)S(1)}, u32[]{:S(2)}, u32[]{:S(2)}) %collective-permute-start.16) | collective-permute-done | bytes 196640 | tf_op jit(solution)/shard_map/ppermute | solution.py:430
  180.4 3.0 %collective-permute-done.17.refs_7_ = bf16[256,384]{1,0:T(8,128)(2,1)S(1)} collective-permute-done((bf16[256,384]{1,0:T(8,128)(2,1)}, bf16[256,384]{1,0:T(8,128)(2,1)S(1)}, u32[]{:S(2)}, u32[]{:S(2)}) %collective-permute-start.17) | collective-permute-done | bytes 196640 | tf_op jit(solution)/shard_map/ppermute | solution.py:492
  184.3 4.3 %assembled.1 = bf16[256,4096]{1,0:T(8,128)(2,1)} custom-call(s32[2]{0:T(128)S(1)} %pad_add_fusion.place_ref, f32[4,1,4096]{2,1,0:T(1,128)S(1)} %reshape.18.mask_ref, bf16[256,640]{1,0:T(8,128)(2,1)S(1)} %get-tuple-element.49.refs_0_, bf16[256,640]{1,0:T(8,128)(2,1)S(1)} %collective-permute-done.12.refs_1_, bf16[256,640]{1,0:T(8,128)(2,1)} %collective-permute-done.13.refs_2_, ...), custom_call_target="tpu_custom_call" | custom-call | flops 1000 | bytes 4194304 | tf_op jit(solution)/shard_map/assembled/pallas_call | solution.py:386
  (64 shorter events, 23.4 us)
Async XLA Ops:
  0.0 2.2 %copy-start.4 = (bf16[512,4096]{1,0:T(8,128)(2,1)S(1)}, bf16[512,4096]{1,0:T(8,128)(2,1)}, u32[]{:S(2)}) copy-start(bf16[512,4096]{1,0:T(8,128)(2,1)} %w_ref.3) | copy-start | bytes 12582916
  2.2 4.7 %copy-start.5 = (bf16[512,4096]{1,0:T(8,128)(2,1)S(1)}, bf16[512,4096]{1,0:T(8,128)(2,1)}, u32[]{:S(2)}) copy-start(bf16[512,4096]{1,0:T(8,128)(2,1)} %w_ref.3) | copy-start | bytes 12582916
  3.9 26.5 %collective-permute-start.2 = (bf16[512,1024]{1,0:T(8,128)(2,1)}, bf16[512,1024]{1,0:T(8,128)(2,1)}, u32[]{:S(2)}, u32[]{:S(2)}) collective-permute-start(bf16[512,1024]{1,0:T(8,128)(2,1)} %b_strips.3), channel_id=1, source_target_pairs={{0,2},{2,0},{4,6},{6,4},{8,10},{10,8},{12,14},{14,12},{1,3},{3,1},... | collective-permute-start | bytes 3145736 | tf_op jit(solution)/shard_map/ppermute | solution.py:430
  6.9 5.1 %copy-start.14 = (s32[8,64]{1,0:T(8,128)S(1)}, s32[8,64]{1,0:T(8,128)}, u32[]{:S(2)}) copy-start(s32[8,64]{1,0:T(8,128)} %param.6) | copy-start | bytes 6148
  8.7 26.6 %collective-permute-start = (bf16[512,1024]{1,0:T(8,128)(2,1)}, bf16[512,1024]{1,0:T(8,128)(2,1)S(1)}, u32[]{:S(2)}, u32[]{:S(2)}) collective-permute-start(bf16[512,1024]{1,0:T(8,128)(2,1)} %b_strips.2.refs_4_.refs_10_), channel_id=1, source_target_pairs={{0,4},{2,6},{4,0},{6,2},{8,12},{10,14},{12,8},{14,10},{1,5},{3,7},... | collective-permute-start | bytes 3145736 | tf_op jit(solution)/shard_map/ppermute | solution.py:430
  10.3 25.0 %collective-permute-start.1 = (bf16[512,1024]{1,0:T(8,128)(2,1)}, bf16[512,1024]{1,0:T(8,128)(2,1)}, u32[]{:S(2)}, u32[]{:S(2)}) collective-permute-start(bf16[512,1024]{1,0:T(8,128)(2,1)} %b_strips.2.refs_4_.refs_10_), channel_id=1, source_target_pairs={{4,8},{6,10},{8,4},{10,6},{5,9},{7,11},{9,5},{11,7},{20,24},{22,26... | collective-permute-start | bytes 3145736 | tf_op jit(solution)/shard_map/ppermute | solution.py:430
  12.3 2.2 %copy-start.6 = (bf16[512,4096]{1,0:T(8,128)(2,1)S(1)}, bf16[512,4096]{1,0:T(8,128)(2,1)}, u32[]{:S(2)}) copy-start(bf16[512,4096]{1,0:T(8,128)(2,1)} %x_ref.3) | copy-start | bytes 12582916
  30.4 25.8 %collective-permute-start.3 = (bf16[512,1024]{1,0:T(8,128)(2,1)}, bf16[512,1024]{1,0:T(8,128)(2,1)}, u32[]{:S(2)}, u32[]{:S(2)}) collective-permute-start(bf16[512,1024]{1,0:T(8,128)(2,1)} %collective-permute-done.2.refs_5_.refs_11_), channel_id=1, source_target_pairs={{0,4},{2,6},{4,0},{6,2},{8,12},{10,14},{12,8},{14,10},{1,5},{3,7},... | collective-permute-start | bytes 3145736 | tf_op jit(solution)/shard_map/ppermute | solution.py:430
  32.2 24.0 %collective-permute-start.4 = (bf16[512,1024]{1,0:T(8,128)(2,1)}, bf16[512,1024]{1,0:T(8,128)(2,1)}, u32[]{:S(2)}, u32[]{:S(2)}) collective-permute-start(bf16[512,1024]{1,0:T(8,128)(2,1)} %collective-permute-done.2.refs_5_.refs_11_), channel_id=1, source_target_pairs={{4,8},{6,10},{8,4},{10,6},{5,9},{7,11},{9,5},{11,7},{20,24},{22,26... | collective-permute-start | bytes 3145736 | tf_op jit(solution)/shard_map/ppermute | solution.py:430
  33.8 46.3 %collective-permute-start.6 = (bf16[256,4096]{1,0:T(8,128)(2,1)S(1)}, bf16[256,4096]{1,0:T(8,128)(2,1)}, u32[]{:S(2)}, u32[]{:S(2)}) collective-permute-start(bf16[256,4096]{1,0:T(8,128)(2,1)S(1)} %masked_half.2.refs_0_), channel_id=1, source_target_pairs={{0,2},{2,0},{4,6},{6,4},{8,10},{10,8},{12,14},{14,12},{1,3},{3,1},... | collective-permute-start | bytes 6291464 | tf_op jit(solution)/shard_map/ppermute | solution.py:430
  60.2 42.5 %collective-permute-start.7 = (bf16[512,1664]{1,0:T(8,128)(2,1)}, bf16[512,1664]{1,0:T(8,128)(2,1)}, u32[]{:S(2)}, u32[]{:S(2)}) collective-permute-start(bf16[512,1664]{1,0:T(8,128)(2,1)} %pad_maximum_fusion), channel_id=1, source_target_pairs={{4,0},{6,2},{8,12},{10,14},{5,1},{7,3},{9,13},{11,15},{20,16},{22,... | collective-permute-start | bytes 5111816 | tf_op jit(solution)/shard_map/ppermute | solution.py:430
  63.1 2.8 %collective-permute-start.5 = (bf16[512,1024]{1,0:T(8,128)(2,1)S(1)}, bf16[512,1024]{1,0:T(8,128)(2,1)}, u32[]{:S(2)}, u32[]{:S(2)}) collective-permute-start(bf16[512,1024]{1,0:T(8,128)(2,1)S(1)} %pad_maximum_fusion.1), channel_id=1, source_target_pairs={{4,8},{6,10},{8,4},{10,6},{5,9},{7,11},{9,5},{11,7},{20,24},{22,26... | collective-permute-start | bytes 3145736 | tf_op jit(solution)/shard_map/ppermute | solution.py:430
  102.7 9.5 %collective-permute-start.10 = (bf16[256,4096]{1,0:T(8,128)(2,1)}, bf16[256,4096]{1,0:T(8,128)(2,1)}, u32[]{:S(2)}, u32[]{:S(2)}) collective-permute-start(bf16[256,4096]{1,0:T(8,128)(2,1)} %collective-permute-done.6.refs_2_), channel_id=1, source_target_pairs={{0,1},{1,0},{2,3},{3,2},{4,5},{5,4},{6,7},{7,6},{8,9},{9,8},{10,11... | collective-permute-start | bytes 6291464 | tf_op jit(solution)/shard_map/ppermute | solution.py:459
  102.7 23.0 %collective-permute-start.8 = (bf16[512,1024]{1,0:T(8,128)(2,1)}, bf16[512,1024]{1,0:T(8,128)(2,1)}, u32[]{:S(2)}, u32[]{:S(2)}) collective-permute-start(bf16[512,1024]{1,0:T(8,128)(2,1)} %pad_maximum_fusion.2), channel_id=1, source_target_pairs={{4,8},{6,10},{8,4},{10,6},{5,9},{7,11},{9,5},{11,7},{20,24},{22,26... | collective-permute-start | bytes 3145736 | tf_op jit(solution)/shard_map/ppermute | solution.py:430
  104.3 27.8 %collective-permute-start.9 = (bf16[512,1024]{1,0:T(8,128)(2,1)}, bf16[512,1024]{1,0:T(8,128)(2,1)}, u32[]{:S(2)}, u32[]{:S(2)}) collective-permute-start(bf16[512,1024]{1,0:T(8,128)(2,1)} %collective-permute-done.5.refs_5_), channel_id=1, source_target_pairs={{4,0},{6,2},{8,12},{10,14},{5,1},{7,3},{9,13},{11,15},{20,16},{22,... | collective-permute-start | bytes 3145736 | tf_op jit(solution)/shard_map/ppermute | solution.py:430
  105.6 2.2 %copy-start.7 = (bf16[512,4096]{1,0:T(8,128)(2,1)S(1)}, bf16[512,4096]{1,0:T(8,128)(2,1)}, u32[]{:S(2)}) copy-start(bf16[512,4096]{1,0:T(8,128)(2,1)} %x_ref.3) | copy-start | bytes 12582916
  108.2 1.3 copy-start
  109.6 2.6 %copy-start.1 = (bf16[256,4096]{1,0:T(8,128)(2,1)S(1)}, bf16[256,4096]{1,0:T(8,128)(2,1)}, u32[]{:S(2)}) copy-start(bf16[256,4096]{1,0:T(8,128)(2,1)} %copy-done) | copy-start | bytes 6291460
  123.7 2.0 %copy-start.8 = (f32[2,512,1024]{2,1,0:T(8,128)}, f32[2,512,1024]{2,1,0:T(8,128)S(1)}, u32[]{:S(2)}) copy-start(f32[2,512,1024]{2,1,0:T(8,128)S(1)} %first_products.1.refs_4_) | copy-start | bytes 12582916
  134.3 29.5 %collective-permute-start.11 = (bf16[512,768]{1,0:T(8,128)(2,1)}, bf16[512,768]{1,0:T(8,128)(2,1)S(1)}, u32[]{:S(2)}, u32[]{:S(2)}) collective-permute-start(bf16[512,768]{1,0:T(8,128)(2,1)} %pad_maximum_fusion.3), channel_id=1, source_target_pairs={{4,0},{6,2},{8,12},{10,14},{5,1},{7,3},{9,13},{11,15},{20,16},{22,... | collective-permute-start | bytes 2359304 | tf_op jit(solution)/shard_map/ppermute | solution.py:430
  135.8 1.6 copy-start.2
  137.4 2.2 %copy-start.9 = (f32[2,512,1024]{2,1,0:T(8,128)S(1)}, f32[2,512,1024]{2,1,0:T(8,128)}, u32[]{:S(2)}) copy-start(f32[2,512,1024]{2,1,0:T(8,128)} %copy-done.8) | copy-start | bytes 12582916
  145.5 1.2 copy-start.10
  146.7 1.9 %collective-permute-start.12 = (bf16[256,640]{1,0:T(8,128)(2,1)}, bf16[256,640]{1,0:T(8,128)(2,1)S(1)}, u32[]{:S(2)}, u32[]{:S(2)}) collective-permute-start(bf16[256,640]{1,0:T(8,128)(2,1)} %get-tuple-element.46), channel_id=1, source_target_pairs={{0,1},{1,0},{2,3},{3,2},{4,5},{5,4},{6,7},{7,6},{8,9},{9,8},{10,11... | collective-permute-start | bytes 983048 | tf_op jit(solution)/shard_map/ppermute | solution.py:490
  146.7 10.8 %collective-permute-start.13 = (bf16[256,640]{1,0:T(8,128)(2,1)}, bf16[256,640]{1,0:T(8,128)(2,1)}, u32[]{:S(2)}, u32[]{:S(2)}) collective-permute-start(bf16[256,640]{1,0:T(8,128)(2,1)} %get-tuple-element.47), channel_id=1, source_target_pairs={{0,2},{2,0},{4,6},{6,4},{8,10},{10,8},{12,14},{14,12},{1,3},{3,1},... | collective-permute-start | bytes 983048 | tf_op jit(solution)/shard_map/ppermute | solution.py:430
  147.7 16.1 %collective-permute-start.14 = (bf16[256,640]{1,0:T(8,128)(2,1)}, bf16[256,640]{1,0:T(8,128)(2,1)}, u32[]{:S(2)}, u32[]{:S(2)}) collective-permute-start(bf16[256,640]{1,0:T(8,128)(2,1)} %get-tuple-element.48), channel_id=1, source_target_pairs={{0,3},{1,2},{2,1},{3,0},{4,7},{5,6},{6,5},{7,4},{8,11},{9,10},{10,... | collective-permute-start | bytes 983048 | tf_op jit(solution)/shard_map/ppermute | solution.py:492
  163.8 1.6 copy-start.3
  165.4 1.4 copy-start.11
  166.8 7.3 %copy-start.15 = (s32[4,64]{1,0:T(4,128)S(1)}, s32[4,64]{1,0:T(4,128)}, u32[]{:S(2)}) copy-start(s32[4,64]{1,0:T(4,128)} %param.7) | copy-start | bytes 3076
  172.3 2.2 %collective-permute-start.15 = (bf16[256,384]{1,0:T(8,128)(2,1)}, bf16[256,384]{1,0:T(8,128)(2,1)S(1)}, u32[]{:S(2)}, u32[]{:S(2)}) collective-permute-start(bf16[256,384]{1,0:T(8,128)(2,1)} %get-tuple-element.56), channel_id=1, source_target_pairs={{0,1},{1,0},{2,3},{3,2},{4,5},{5,4},{6,7},{7,6},{8,9},{9,8},{10,11... | collective-permute-start | bytes 589832 | tf_op jit(solution)/shard_map/ppermute | solution.py:490
  172.5 7.9 %collective-permute-start.16 = (bf16[256,384]{1,0:T(8,128)(2,1)}, bf16[256,384]{1,0:T(8,128)(2,1)S(1)}, u32[]{:S(2)}, u32[]{:S(2)}) collective-permute-start(bf16[256,384]{1,0:T(8,128)(2,1)} %get-tuple-element.57), channel_id=1, source_target_pairs={{0,2},{2,0},{4,6},{6,4},{8,10},{10,8},{12,14},{14,12},{1,3},{3,1},... | collective-permute-start | bytes 589832 | tf_op jit(solution)/shard_map/ppermute | solution.py:430
  173.5 9.9 %collective-permute-start.17 = (bf16[256,384]{1,0:T(8,128)(2,1)}, bf16[256,384]{1,0:T(8,128)(2,1)S(1)}, u32[]{:S(2)}, u32[]{:S(2)}) collective-permute-start(bf16[256,384]{1,0:T(8,128)(2,1)} %get-tuple-element.58), channel_id=1, source_target_pairs={{0,3},{1,2},{2,1},{3,0},{4,7},{5,6},{6,5},{7,4},{8,11},{9,10},{10,... | collective-permute-start | bytes 589832 | tf_op jit(solution)/shard_map/ppermute | solution.py:492
  (2 other events, 1.6 us)

commit v3 on v2

--- a/solution.py
+++ b/solution.py
@@ -82,11 +82,11 @@
         out_shape=jax.ShapeDtypeStruct(shape, jnp.bfloat16),
         in_specs=[
             pl.BlockSpec(memory_space=pltpu.SMEM),
-            pl.BlockSpec(memory_space=pl.ANY),
+            pl.BlockSpec(memory_space=pltpu.HBM),
         ],
         out_specs=pl.BlockSpec(memory_space=pltpu.VMEM),
         scratch_shapes=[pltpu.VMEM(shape, jnp.bfloat16), pltpu.SemaphoreType.DMA((band,))],
-        compiler_params=pltpu.CompilerParams(vmem_limit_bytes=16 * MIB),
+        compiler_params=pltpu.CompilerParams(vmem_limit_bytes=60 * MIB),
         cost_estimate=pl.CostEstimate(flops=1000, bytes_accessed=4 * shape[0] * shape[1], transcendentals=0),
         name="b_strips",
     )(quarter.reshape(1), w_band)
@@ -143,63 +143,91 @@
     lax.fori_loop(0, 2, step, 0)
 
 
-def first_kernel(windows, meta_ref, *refs):
-    n_b = len(windows)
-    x_refs, middle_refs, end_refs = refs[:4], refs[4 : 4 + n_b], refs[4 + n_b : 4 + 2 * n_b]
-    out_ref, xv, bv, acc, x_sems, b_sems, out_sem = refs[4 + 2 * n_b :]
+def first_kernel(meta_ref, *refs):
+    x_refs, middle_refs, near_refs, (mid_a_ref, mid_b_ref), refs = refs[:4], refs[4:10], refs[10:12], refs[12:14], refs[14:]
+    out_ref, xv, bv, acc, x_sems, b_sems, out_sems = refs
+    n_b = len(middle_refs)
     quarter = bv.shape[2]
     low = quarter // 2
+    split = quarter - mid_a_ref.shape[1]
     is_end = meta_ref[0]
 
     def offset_of(p, g):
-        return meta_ref[1 + 2 * p + g]
-
-    def b_copies(p):
-        start, width = windows[p]
-        target = bv.at[p, :, start * LANES : (start + width) * LANES]
-        return (
-            pltpu.make_async_copy(middle_refs[p], bv.at[p], b_sems.at[p]),
-            pltpu.make_async_copy(end_refs[p], target, b_sems.at[p]),
-        )
+        return meta_ref[2 + 2 * p + g]
+
+    def b_middle(p):
+        return [pltpu.make_async_copy(middle_refs[p], bv.at[p], b_sems.at[p])]
+
+    def b_end(p):
+        if p < 2:
+            return b_middle(p)
+        if p < 4:
+            return [pltpu.make_async_copy(near_refs[p - 2], bv.at[p], b_sems.at[p])]
+        if p == 4:
+            return [
+                pltpu.make_async_copy(mid_a_ref, bv.at[4, :, split:], b_sems.at[4]),
+                pltpu.make_async_copy(mid_b_ref.at[:, :split], bv.at[4 + meta_ref[1], :, :split], b_sems.at[6]),
+            ]
+        return [pltpu.make_async_copy(mid_b_ref.at[:, split:], bv.at[5, :, split:], b_sems.at[5])]
 
     copies = x_copies(x_refs, xv, x_sems, offset_of)
     for p in range(n_b):
-        middle, end = b_copies(p)
-        pl.when(is_end == 0)(middle.start)
-        pl.when(is_end != 0)(end.start)
+
+        @pl.when(is_end == 0)
+        def _():
+            for copy in b_middle(p):
+                copy.start()
+
+        @pl.when(is_end != 0)
+        def _():
+            for copy in b_end(p):
+                copy.start()
+
         for r in range(4):
             copies[p, r].start()
     acc[...] = jnp.zeros_like(acc)
     for p in range(n_b):
-        middle, end = b_copies(p)
-        pl.when(is_end == 0)(middle.wait)
-        pl.when(is_end != 0)(end.wait)
+
+        @pl.when(is_end == 0)
+        def _():
+            for copy in b_middle(p):
+                copy.wait()
+
+        @pl.when(is_end != 0)
+        def _():
+            for copy in b_end(p):
+                copy.wait()
+
         for r in range(4):
             copies[p, r].wait()
         add_products(acc, xv, p, bv.at[p], offset_of, 0)
-    out = pltpu.make_async_copy(acc.at[:, :, low : low + quarter], out_ref, out_sem)
-    out.start()
-    out.wait()
-
-
-def first_products(meta, xs, middle, end, windows):
+    outs = [
+        pltpu.make_async_copy(acc.at[g, :, low : low + quarter], out_ref.at[g], out_sems.at[g]) for g in range(2)
+    ]
+    for out in outs:
+        out.start()
+    for out in outs:
+        out.wait()
+
+
+def first_products(meta, xs, middle, near, mid):
     rows = xs[0].shape[0]
     panel, quarter = middle[0].shape
     n_b = len(middle)
     any_spec = pl.BlockSpec(memory_space=pl.ANY)
-    operands = [meta, *xs, *middle, *end]
+    x_spec = pl.BlockSpec(memory_space=pltpu.HBM)
     return pl.pallas_call(
-        functools.partial(first_kernel, windows),
+        first_kernel,
         out_shape=jax.ShapeDtypeStruct((2, 2 * rows, quarter), jnp.float32),
-        in_specs=[pl.BlockSpec(memory_space=pltpu.SMEM)] + [any_spec] * (len(operands) - 1),
+        in_specs=[pl.BlockSpec(memory_space=pltpu.SMEM)] + [x_spec] * 4 + [any_spec] * (n_b + 4),
         out_specs=any_spec,
         scratch_shapes=[
             pltpu.VMEM((n_b, 2, 2 * rows, panel), jnp.bfloat16),
             pltpu.VMEM((n_b, panel, quarter), jnp.bfloat16),
             pltpu.VMEM((2, 2 * rows, 2 * quarter), jnp.float32),
             pltpu.SemaphoreType.DMA((n_b, 4)),
-            pltpu.SemaphoreType.DMA((n_b,)),
-            pltpu.SemaphoreType.DMA,
+            pltpu.SemaphoreType.DMA((n_b + 1,)),
+            pltpu.SemaphoreType.DMA((2,)),
         ],
         compiler_params=pltpu.CompilerParams(vmem_limit_bytes=32 * MIB),
         cost_estimate=pl.CostEstimate(
@@ -208,7 +236,7 @@
             transcendentals=0,
         ),
         name="first_products",
-    )(*operands)
+    )(meta, *xs, *middle, *near, *mid)
 
 
 def give_pieces(out_refs, acc, at):
@@ -220,10 +248,10 @@
 
 
 def half_kernel(meta_ref, *refs):
-    x_refs, prev_ref, middle_ref, end_ref, second_ref = refs[:4], *refs[4:8]
-    out_refs, rest_ref, xv, bv, acc, x_sems, b_sems, prev_sem, rest_sem = refs[8:12], *refs[12:]
-    quarter = bv.shape[2]
-    half = quarter // 2
+    x_refs, prev_ref, middle_refs, end_refs, second_ref, refs = refs[:4], refs[4], refs[5:7], refs[7:9], refs[9], refs[10:]
+    out_refs, rest_ref, xv, bv, acc, x_sems, b_sems, prev_sem, rest_sem = refs[:4], *refs[4:]
+    half = bv.shape[2]
+    quarter = 2 * half
     low = quarter // 2
     band = quarter // LANES
     is_end = meta_ref[0]
@@ -232,33 +260,48 @@
         return meta_ref[5 + 2 * p + g]
 
     copies = x_copies(x_refs, xv, x_sems, offset_of)
-    middle = pltpu.make_async_copy(middle_ref, bv.at[0], b_sems.at[0])
-    end = pltpu.make_async_copy(end_ref, bv.at[0], b_sems.at[0])
-    second = pltpu.make_async_copy(second_ref, bv.at[1], b_sems.at[1])
+    middle = [pltpu.make_async_copy(middle_refs[p], bv.at[p], b_sems.at[p]) for p in range(2)]
+    middle += [
+        pltpu.make_async_copy(second_ref.at[:, p * half : (p + 1) * half], bv.at[2 + p], b_sems.at[2 + p])
+        for p in range(2)
+    ]
+    end = [pltpu.make_async_copy(end_refs[p], bv.at[p], b_sems.at[p]) for p in range(2)]
     prev = pltpu.make_async_copy(prev_ref, acc.at[:, :, low : low + quarter], prev_sem)
     prev.start()
+
+    @pl.when(is_end == 0)
+    def _():
+        for copy in middle:
+            copy.start()
+
+    @pl.when(is_end != 0)
+    def _():
+        for copy in end:
+            copy.start()
+
     for copy in copies.values():
         copy.start()
 
     @pl.when(is_end == 0)
     def _():
-        middle.start()
-        second.start()
-
-    pl.when(is_end != 0)(end.start)
-    prev.wait()
+        for copy in middle:
+            copy.wait()
+
+    @pl.when(is_end != 0)
+    def _():
+        for copy in end:
+            copy.wait()
+
     for copy in copies.values():
         copy.wait()
-    pl.when(is_end == 0)(middle.wait)
-    pl.when(is_end != 0)(end.wait)
+    prev.wait()
     for p in range(2):
-        add_products(acc, xv, p, bv.at[0, :, p * half : (p + 1) * half], offset_of, meta_ref[1])
+        add_products(acc, xv, p, bv.at[p], offset_of, meta_ref[1])
 
     @pl.when(is_end == 0)
     def _():
-        second.wait()
         for p in range(2):
-            add_products(acc, xv, p, bv.at[1, :, p * half : (p + 1) * half], offset_of, meta_ref[2])
+            add_products(acc, xv, p, bv.at[2 + p], offset_of, meta_ref[2])
 
     at = pl.multiple_of((meta_ref[4] + band // 2) * LANES, LANES)
     rest = pltpu.make_async_copy(acc.at[:, :, pl.ds(at, rest_ref.shape[2])], rest_ref, rest_sem)
@@ -269,21 +312,22 @@
 
 def half_products(meta, xs, prev, middle, end, second, n_done):
     rows = xs[0].shape[0]
-    panel, quarter = middle.shape
+    panel, quarter = second.shape
     any_spec = pl.BlockSpec(memory_space=pl.ANY)
+    x_spec = pl.BlockSpec(memory_space=pltpu.HBM)
     n_rest = quarter // LANES - n_done
     return pl.pallas_call(
         half_kernel,
         out_shape=[jax.ShapeDtypeStruct((rows, n_done * LANES), jnp.bfloat16)] * 4
         + [jax.ShapeDtypeStruct((2, 2 * rows, n_rest * LANES), jnp.float32)],
-        in_specs=[pl.BlockSpec(memory_space=pltpu.SMEM)] + [any_spec] * 8,
+        in_specs=[pl.BlockSpec(memory_space=pltpu.SMEM)] + [x_spec] * 4 + [any_spec] * 6,
         out_specs=[pl.BlockSpec(memory_space=pltpu.VMEM)] * 4 + [any_spec],
         scratch_shapes=[
             pltpu.VMEM((2, 2, 2 * rows, panel), jnp.bfloat16),
-            pltpu.VMEM((2, panel, quarter), jnp.bfloat16),
+            pltpu.VMEM((4, panel, quarter // 2), jnp.bfloat16),
             pltpu.VMEM((2, 2 * rows, 2 * quarter), jnp.float32),
             pltpu.SemaphoreType.DMA((2, 4)),
-            pltpu.SemaphoreType.DMA((2,)),
+            pltpu.SemaphoreType.DMA((4,)),
             pltpu.SemaphoreType.DMA,
             pltpu.SemaphoreType.DMA,
         ],
@@ -292,7 +336,7 @@
             flops=2 * 2 * 4 * rows * panel * quarter, bytes_accessed=10 * MIB, transcendentals=0
         ),
         name="half_products",
-    )(meta, *xs, prev, middle, end, second)
+    )(meta, *xs, prev, *middle, *end, second)
 
 
 def rest_kernel(meta_ref, *refs):
@@ -335,10 +379,11 @@
     panel = b.shape[0]
     width = rest.shape[2]
     any_spec = pl.BlockSpec(memory_space=pl.ANY)
+    x_spec = pl.BlockSpec(memory_space=pltpu.HBM)
     return pl.pallas_call(
         rest_kernel,
         out_shape=[jax.ShapeDtypeStruct((rows, width), jnp.bfloat16)] * 4,
-        in_specs=[pl.BlockSpec(memory_space=pltpu.SMEM)] + [any_spec] * 6,
+        in_specs=[pl.BlockSpec(memory_space=pltpu.SMEM)] + [x_spec] * 4 + [any_spec] * 2,
         out_specs=[pl.BlockSpec(memory_space=pltpu.VMEM)] * 4,
         scratch_shapes=[
             pltpu.VMEM((2, 2, 2 * rows, panel), jnp.bfloat16),
@@ -357,46 +402,42 @@
 
 
 def assemble_kernel(place_ref, mask_ref, *refs):
-    *pieces, out_ref = refs
-    n = len(pieces) // 2
-    done, rest = pieces[:n], pieces[n:]
-    n_done, n_rest = done[0].shape[1] // LANES, rest[0].shape[1] // LANES
+    n = 4
+    pieces, (out_ref, made, sem) = refs[:n], refs[-3:]
+    steps = mask_ref.shape[0]
+    rows = made.shape[0] // steps
     panel = n * LANES
-    for left in range(2):
-        for mine in range(n):
-
-            @pl.when((place_ref[0] == mine) & (place_ref[1] == left))
-            def _():
-                for j in range(n_done + n_rest):
-                    if left:
-                        source, at = (rest, j) if j < n_rest else (done, j - n_rest)
-                    else:
-                        source, at = (done, j) if j < n_done else (rest, j - n_done)
-                    for t in range(n):
-                        cols = slice(j * panel + t * LANES, j * panel + (t + 1) * LANES)
-                        value = source[t ^ mine][:, at * LANES : (at + 1) * LANES].astype(jnp.float32)
-                        out_ref[:, cols] = (value * mask_ref[0, :, cols]).astype(jnp.bfloat16)
-
-
-def assembled(place, keep_wide, done, rest):
-    rows = done[0].shape[0]
-    steps = keep_wide.shape[0]
-    block = rows // steps
+    first = pl.multiple_of(place_ref[1] * panel, panel)
+    for r in range(n):
+        t = jnp.bitwise_xor(place_ref[0], r)
+        for j in range(made.shape[1] // panel):
+            to = pl.multiple_of(j * panel + t * LANES, LANES)
+            for i in range(steps):
+                keep = mask_ref[i, :, pl.ds(pl.multiple_of(first + to, LANES), LANES)]
+                value = pieces[r][i * rows : (i + 1) * rows, j * LANES : (j + 1) * LANES].astype(jnp.float32)
+                made[i * rows : (i + 1) * rows, pl.ds(to, LANES)] = (value * keep).astype(jnp.bfloat16)
+    copy = pltpu.make_async_copy(made, out_ref.at[:, pl.ds(first, made.shape[1])], sem)
+    copy.start()
+    copy.wait()
+
+
+def assembled(place, keep_wide, pieces, out=None):
+    rows, width = pieces[0].shape
     cols = keep_wide.shape[2]
+    vmem_spec = pl.BlockSpec(memory_space=pltpu.VMEM)
+    any_spec = pl.BlockSpec(memory_space=pltpu.HBM)
+    operands = [place, keep_wide, *pieces] + ([] if out is None else [out])
     return pl.pallas_call(
         assemble_kernel,
-        grid_spec=pltpu.PrefetchScalarGridSpec(
-            num_scalar_prefetch=1,
-            grid=(steps,),
-            in_specs=[pl.BlockSpec((1, 1, cols), lambda i, q: (i, 0, 0))]
-            + [pl.BlockSpec((block, piece.shape[1]), lambda i, q: (i, 0)) for piece in done + rest],
-            out_specs=pl.BlockSpec((block, cols), lambda i, q: (i, 0)),
-        ),
         out_shape=jax.ShapeDtypeStruct((rows, cols), jnp.bfloat16),
+        in_specs=[pl.BlockSpec(memory_space=pltpu.SMEM)] + [vmem_spec] * 5 + [any_spec] * (len(operands) - 6),
+        out_specs=any_spec,
+        scratch_shapes=[pltpu.VMEM((rows, width * len(pieces)), jnp.bfloat16), pltpu.SemaphoreType.DMA],
+        input_output_aliases={} if out is None else {6: 0},
         compiler_params=pltpu.CompilerParams(vmem_limit_bytes=16 * MIB),
-        cost_estimate=pl.CostEstimate(flops=1000, bytes_accessed=4 * rows * cols, transcendentals=0),
+        cost_estimate=pl.CostEstimate(flops=1000, bytes_accessed=4 * rows * width, transcendentals=0),
         name="assembled",
-    )(place, keep_wide, *done, *rest)
+    )(*operands)
 
 
 def widen(mask, block):
@@ -442,46 +483,42 @@
     own_b = line(b_strips(w_band, q ^ 2), across)
     mask_wide = widen(a_mask, block)
     x_mine = masked_half(x_band, mask_wide, c)
-    own_b, x_mine = together(own_b, x_mine)
+    own_b, x_mine, swap_a, cross_a = together(own_b, x_mine, swap_a, cross_a)
     swap_b = line(own_b, swap)
     cross_b = line(own_b, cross)
     x_across = line(x_mine, across)
     x_rest = masked_half(x_band, mask_wide, 1 - c)
 
-    swap_a, cross_a, swap_b, cross_b = together(swap_a, cross_a, swap_b, cross_b)
-    even = jnp.where(y == 0, cross_a, cross_b)
-    odd = jnp.where(y == 0, cross_b[:, 3 * LANES :], cross_a[:, 3 * LANES :])
-    mid = line(jnp.concatenate([even, odd], 1), outward)
-    fwd_first = line(jnp.concatenate([strips(v, first_out, 4) for v in (swap_a, swap_b)], 1), cross)
-    fwd_second_out = jnp.concatenate([strips(v, second_out, 4) for v in (swap_a, swap_b)], 1)
-    fwd_first, fwd_second_out, x_across, mid = together(fwd_first, fwd_second_out, x_across, mid)
-    fwd_second = line(fwd_second_out, cross)
+    mid_a = line(cross_a[:, 3 * LANES :], outward)
+    fwd_a = line(strips(swap_a, first_out, 4), cross)
+    mid_b = line(
+        jnp.concatenate([jnp.where(y == 0, cross_a[:, : 3 * LANES], cross_b[:, : 3 * LANES]), cross_b[:, 3 * LANES :]], 1),
+        outward,
+    )
+    swap_b, mid_a, fwd_a = together(swap_b, mid_a, fwd_a)
+    fwd_b = line(strips(swap_b, first_out, 4), cross)
+    fwd_second = line(jnp.concatenate([strips(v, second_out, 4) for v in (swap_a, swap_b)], 1), cross)
+    far_a = line(fwd_a, outward)
+    mid_b, fwd_b, x_across = together(mid_b, fwd_b, x_across)
+    far_b = line(fwd_b, outward)
     x_opposite = lax.ppermute(x_across, "depth", layers)
     xs = [x_mine, x_rest, x_across, x_opposite]
-    far_first = line(fwd_first, outward)
 
     def offsets(delta):
         tilt = 2 * y - 1
         return [(2 * delta + 4) % 8, (2 * delta + tilt + 4) % 8, (2 * delta - tilt + 4) % 8, (2 * delta + 4) % 8]
 
     zero = jnp.zeros_like(z)
-    third = [
-        jnp.where(is_end == 1, ours, theirs)
-        for ours, theirs in zip([8 - y, 7 + y, 9 - y, 8 + y], offsets(-toward))
-    ]
-    third = [v % 8 for v in third]
+    third = offsets(jnp.where(is_end == 1, 2, -toward))
     fourth = offsets(jnp.where(is_end == 1, -toward, 2))
-    meta = jnp.stack([is_end, *offsets(zero), *offsets(toward), *third]).astype(jnp.int32)
-    whole = (0, 8)
+    meta = jnp.stack([is_end, y, *offsets(zero), *offsets(toward), *third]).astype(jnp.int32)
     total = first_products(
-        meta,
-        xs,
-        [own_a, own_b, cross_a, cross_b, swap_a, swap_b],
-        [own_a, own_b, swap_a, swap_b, mid[:, : 8 * LANES], mid[:, 8 * LANES :]],
-        [whole, whole, whole, whole, whole, (3, 5)],
+        meta, xs, [own_a, own_b, cross_a, cross_b, swap_a, swap_b], [swap_a, swap_b], [mid_a, mid_b]
     )
-    fwd_second, far_first, total = together(fwd_second, far_first, total)
-    last = jnp.concatenate([strips(fwd_second, jnp.where(left, 1, 0), 3), strips(fwd_second, jnp.where(left, 5, 4), 3)], 1)
+    fwd_second, total, far_a = together(fwd_second, total, far_a)
+    last = jnp.concatenate(
+        [strips(fwd_second, jnp.where(left, 1, 0), 3), strips(fwd_second, jnp.where(left, 5, 4), 3)], 1
+    )
     far_second = line(last, outward)
 
     def exchanged(pieces):
@@ -494,12 +531,13 @@
 
     done_at, rest_at = jnp.where(left, 3, 0), jnp.where(left, 0, 5)
     meta = jnp.stack([is_end, first_in, second_in, done_at, rest_at, *fourth]).astype(jnp.int32)
-    *done, rest = half_products(meta, xs, total, fwd_first, far_first, fwd_second, 5)
+    *done, rest = half_products(meta, xs, total, [fwd_a, fwd_b], [far_a, far_b], fwd_second, 5)
     far_second, *done = together(far_second, *exchanged(done))
+    keep_wide = widen(keep_mask, block)
+    out = assembled(jnp.stack([q, done_at]).astype(jnp.int32), keep_wide, done)
     meta = jnp.stack([is_end, last_in, rest_at, *fourth]).astype(jnp.int32)
     rest = exchanged(rest_products(meta, xs, rest, far_second, own_a.shape[1]))
-    place = jnp.stack([q, left.astype(jnp.int32)]).astype(jnp.int32)
-    return assembled(place, widen(keep_mask, block), done, rest)
+    return assembled(jnp.stack([q, rest_at]).astype(jnp.int32), keep_wide, rest, out)
 
 
 def solution(mesh):

time: 189 us -> 188 us (level)
  waiting for transfers between devices: 104 us -> 89.1 us
  local copies, waits for them, and re-layouts: 25.4 us -> 36.9 us
  starting transfers between devices: 22.1 us -> 25.6 us
  other arithmetic: 6.36 us -> 3.33 us
    ppermute x13 -> x16, waiting for transfers between devices: 94.4 us -> 80.6 us  [line(): return lax.ppermute(value, 'grid', pairs)]
    unnamed x32 -> x62, local copies, waits for them, and re-layouts: 19.4 us -> 32.1 us
    ppermute x13 -> x16, starting transfers between devices: 20.4 us -> 22.8 us  [line(): return lax.ppermute(value, 'grid', pairs)]
    pallas_call x2 -> x3, Pallas kernels: 15.8 us -> 14.9 us  [the longest x1 11.3 us: first_products(): pl.pallas_call(first_kernel, out_shape=jax.ShapeDtypeStruct((2, 2 * rows,...]
  transfers between devices with their start and end apart: 18 -> 21, of which waited for: 9 -> 9; matrix products, arithmetic and copies ran while one was open for 5% -> 4% of each run, Pallas kernels for 11% -> 12%
where the time goes in v3:
time: 188 us; the launch traced here: 187 us
  waiting for transfers between devices  89.1 us (47%)
  local copies, waits for them, and re-layouts  36.9 us (20%)
  Pallas kernels  31.2 us (17%)
  starting transfers between devices  25.6 us (14%)
  other arithmetic  3.33 us (2%)
    ppermute x16, waiting for transfers between devices, line(): return lax.ppermute(value, 'grid', pairs)  80.6 us
    unnamed x62, local copies, waits for them, and re-layouts  32.1 us
    ppermute x16, starting transfers between devices, line(): return lax.ppermute(value, 'grid', pairs)  22.8 us
    pallas_call x1, Pallas kernels, first_products(): pl.pallas_call(first_kernel, out_shape=jax.ShapeDtypeStruct((2, 2 * rows,...  11.3 us
    ppermute x2, waiting for transfers between devices, exchanged(): lax.ppermute(pieces[3], ('grid', 'depth'), opposite)  8.47 us
    pallas_call x1, Pallas kernels, half_products(): pl.pallas_call(half_kernel, out_shape=[jax.ShapeDtypeStruct((rows, n_done...  5.7 us
    pallas_call x1, Pallas kernels, rest_products(): pl.pallas_call(rest_kernel, out_shape=[jax.ShapeDtypeStruct((rows, width)...  4.96 us
    pallas_call x2, Pallas kernels, b_strips(): pl.pallas_call(strips_kernel, out_shape=jax.ShapeDtypeStruct(shape, jnp.b...  4.8 us
  transfers between devices with their start and end apart: 21, of which 9 were waited for; matrix products, arithmetic and copies ran while one was open for 4% of the time, Pallas kernels for 12%

profile of v3, /device:TPU:0, one launch (start us, length us, event | category | flops | bytes accessed | tf_op | source)
XLA Modules:
  0.0 186.6 jit_solution(4848085343472642857)
XLA Ops:
  0.0 2.4 %b_strips.3.refs_4_ = bf16[512,1024]{1,0:T(8,128)(2,1)} custom-call(s32[1]{0:T(128)} %bitcast.quarter_ref, bf16[512,4096]{1,0:T(8,128)(2,1)} %w_ref.3), custom_call_target="tpu_custom_call" | custom-call | flops 1000 | bytes 2097152 | tf_op jit(solution)/shard_map/b_strips/pallas_call | solution.py:80
  2.4 3.1 %collective-permute-start.1 = (bf16[512,1024]{1,0:T(8,128)(2,1)}, bf16[512,1024]{1,0:T(8,128)(2,1)}, u32[]{:S(2)}, u32[]{:S(2)}) collective-permute-start(bf16[512,1024]{1,0:T(8,128)(2,1)} %b_strips.3.refs_4_), channel_id=1, source_target_pairs={{0,4},{2,6},{4,0},{6,2},{8,12},{10,14},{12,8},{14,10},{1,5},{3,7},... | collective-permute-start | bytes 3145736 | tf_op jit(solution)/shard_map/ppermute | solution.py:471
  6.2 2.4 %b_strips.2 = bf16[512,1024]{1,0:T(8,128)(2,1)} custom-call(s32[1]{0:T(128)} %bitcast.7.quarter_ref, bf16[512,4096]{1,0:T(8,128)(2,1)} %w_ref.3), custom_call_target="tpu_custom_call" | custom-call | flops 1000 | bytes 2097152 | tf_op jit(solution)/shard_map/b_strips/pallas_call | solution.py:80
  8.6 1.6 collective-permute-start
  10.6 2.2 %copy-done.4 = bf16[512,4096]{1,0:T(8,128)(2,1)S(1)} copy-done((bf16[512,4096]{1,0:T(8,128)(2,1)S(1)}, bf16[512,4096]{1,0:T(8,128)(2,1)}, u32[]{:S(2)}) %copy-start.4) | copy-done | bytes 4194328
  13.2 15.8 %collective-permute-done.1.refs_8_.refs_10_ = bf16[512,1024]{1,0:T(8,128)(2,1)} collective-permute-done((bf16[512,1024]{1,0:T(8,128)(2,1)}, bf16[512,1024]{1,0:T(8,128)(2,1)}, u32[]{:S(2)}, u32[]{:S(2)}) %collective-permute-start.1) | collective-permute-done | bytes 1048608 | tf_op jit(solution)/shard_map/ppermute | solution.py:471
  29.0 4.7 %collective-permute-done.refs_5_ = bf16[512,1024]{1,0:T(8,128)(2,1)} collective-permute-done((bf16[512,1024]{1,0:T(8,128)(2,1)}, bf16[512,1024]{1,0:T(8,128)(2,1)}, u32[]{:S(2)}, u32[]{:S(2)}) %collective-permute-start) | collective-permute-done | bytes 1048608 | tf_op jit(solution)/shard_map/ppermute | solution.py:471
  33.6 1.6 collective-permute-start.3
  35.3 1.5 collective-permute-start.9
  36.8 4.7 %collective-permute-start.5 = (bf16[512,1024]{1,0:T(8,128)(2,1)}, bf16[512,1024]{1,0:T(8,128)(2,1)}, u32[]{:S(2)}, u32[]{:S(2)}) collective-permute-start(bf16[512,1024]{1,0:T(8,128)(2,1)} %collective-permute-done.refs_5_), channel_id=1, source_target_pairs={{0,4},{2,6},{4,0},{6,2},{8,12},{10,14},{12,8},{14,10},{1,5},{3,7},... | collective-permute-start | bytes 3145736 | tf_op jit(solution)/shard_map/ppermute | solution.py:471
  48.5 31.3 %collective-permute-done.6.refs_12_ = bf16[512,640]{1,0:T(8,128)(2,1)S(1)} collective-permute-done((bf16[512,640]{1,0:T(8,128)(2,1)S(1)}, bf16[512,640]{1,0:T(8,128)(2,1)S(1)}, u32[]{:S(2)}, u32[]{:S(2)}) %collective-permute-start.6) | collective-permute-done | bytes 655392 | tf_op jit(solution)/shard_map/ppermute | solution.py:471
  79.8 1.5 constant_dynamic-slice_fusion.2
  82.0 17.6 %collective-permute-done.4.refs_13_ = bf16[512,1024]{1,0:T(8,128)(2,1)S(1)} collective-permute-done((bf16[512,1024]{1,0:T(8,128)(2,1)S(1)}, bf16[512,1024]{1,0:T(8,128)(2,1)S(1)}, u32[]{:S(2)}, u32[]{:S(2)}) %collective-permute-start.4) | collective-permute-done | bytes 1048608 | tf_op jit(solution)/shard_map/ppermute | solution.py:471
  102.5 2.2 %copy-done.5 = bf16[512,4096]{1,0:T(8,128)(2,1)S(1)} copy-done((bf16[512,4096]{1,0:T(8,128)(2,1)S(1)}, bf16[512,4096]{1,0:T(8,128)(2,1)}, u32[]{:S(2)}) %copy-start.5) | copy-done | bytes 4194328
  105.1 1.3 copy-done
  106.5 1.3 collective-permute-start.12
  109.1 1.6 copy-done.1
  115.5 11.3 %first_products.1.refs_4_ = f32[2,512,1024]{2,1,0:T(8,128)S(1)} custom-call(s32[14]{0:T(128)S(1)} %stack.109.meta_ref, bf16[256,4096]{1,0:T(8,128)(2,1)S(1)} %masked_half.2.refs_0_, bf16[256,4096]{1,0:T(8,128)(2,1)S(1)} %copy-done.1, bf16[256,4096]{1,0:T(8,128)(2,1)} %collective-permute-done.9.refs_2_, bf16[256,4096]{1,0:T(8,128)(2,1)} %collective-permute-done.10.refs_3_, ...), custom_call_target="tpu_custom_call" | custom-call | flops 6442450944 | bytes 12582912 | tf_op jit(solution)/shard_map/first_products/pallas_call | solution.py:219
  126.8 2.0 %copy-done.6 = f32[2,512,1024]{2,1,0:T(8,128)} copy-done((f32[2,512,1024]{2,1,0:T(8,128)}, f32[2,512,1024]{2,1,0:T(8,128)S(1)}, u32[]{:S(2)}) %copy-start.6) | copy-done | bytes 4194328
  132.1 2.2 %collective-permute-done.13.refs_8_ = bf16[512,512]{1,0:T(8,128)(2,1)} collective-permute-done((bf16[512,512]{1,0:T(8,128)(2,1)}, bf16[512,512]{1,0:T(8,128)(2,1)}, u32[]{:S(2)}, u32[]{:S(2)}) %collective-permute-start.13) | collective-permute-done | bytes 524320 | tf_op jit(solution)/shard_map/ppermute | solution.py:471
  134.3 1.6 copy-done.2
  135.9 2.2 %copy-done.7 = f32[2,512,1024]{2,1,0:T(8,128)S(1)} copy-done((f32[2,512,1024]{2,1,0:T(8,128)S(1)}, f32[2,512,1024]{2,1,0:T(8,128)}, u32[]{:S(2)}) %copy-start.7) | copy-done | bytes 4194328
  141.2 5.7 %half_products.1 = (bf16[256,640]{1,0:T(8,128)(2,1)S(1)}, bf16[256,640]{1,0:T(8,128)(2,1)}, bf16[256,640]{1,0:T(8,128)(2,1)}, bf16[256,640]{1,0:T(8,128)(2,1)}, f32[2,512,384]{2,1,0:T(8,128)S(1)}) custom-call(s32[9]{0:T(128)S(1)} %stack.99.meta_ref, bf16[256,4096]{1,0:T(8,128)(2,1)S(1)} %masked_half.2.refs_0_, bf16[256,4096]{1,0:T(8,128)(2,1)S(1)} %copy-done.2, ...), custom_call_target="tpu_custom_call" | custom-call | flops 2147483648 | bytes 10485760 | tf_op jit(solution)/shard_map/half_products/pallas_call | solution.py:319
  148.6 1.3 collective-permute-start.17
  150.8 8.1 %collective-permute-done.16.refs_2_ = bf16[256,640]{1,0:T(8,128)(2,1)S(1)} collective-permute-done((bf16[256,640]{1,0:T(8,128)(2,1)}, bf16[256,640]{1,0:T(8,128)(2,1)S(1)}, u32[]{:S(2)}, u32[]{:S(2)}) %collective-permute-start.16) | collective-permute-done | bytes 327712 | tf_op jit(solution)/shard_map/ppermute | solution.py:471
  159.6 5.5 %collective-permute-done.17.refs_3_ = bf16[256,640]{1,0:T(8,128)(2,1)S(1)} collective-permute-done((bf16[256,640]{1,0:T(8,128)(2,1)}, bf16[256,640]{1,0:T(8,128)(2,1)S(1)}, u32[]{:S(2)}, u32[]{:S(2)}) %collective-permute-start.17) | collective-permute-done | bytes 327712 | tf_op jit(solution)/shard_map/ppermute | solution.py:529
  165.8 1.6 copy-done.3
  167.4 1.4 copy-done.9
  168.8 5.0 %rest_products.1 = (bf16[256,384]{1,0:T(8,128)(2,1)S(1)}, bf16[256,384]{1,0:T(8,128)(2,1)}, bf16[256,384]{1,0:T(8,128)(2,1)}, bf16[256,384]{1,0:T(8,128)(2,1)}) custom-call(s32[7]{0:T(128)S(1)} %stack.95.meta_ref, bf16[256,4096]{1,0:T(8,128)(2,1)S(1)} %masked_half.2.refs_0_, bf16[256,4096]{1,0:T(8,128)(2,1)S(1)} %copy-done.3, ...), custom_call_target="tpu_custom_call" | custom-call | flops 805306368 | bytes 5242880 | tf_op jit(solution)/shard_map/rest_products/pallas_call | solution.py:383
  178.9 2.0 %assembled.2.refs_4_ = bf16[256,4096]{1,0:T(8,128)(2,1)} custom-call(s32[2]{0:T(128)S(1)} %get-tuple-element.66.place_ref, f32[4,1,4096]{2,1,0:T(1,128)S(1)} %reshape.18.mask_ref, bf16[256,640]{1,0:T(8,128)(2,1)S(1)} %get-tuple-element.55.refs_0_, bf16[256,640]{1,0:T(8,128)(2,1)S(1)} %copy-done.20, bf16[256,640]{1,0:T(8,128)(2,1)S(1)} %copy-done.22, ...), custom_call_target="tpu_custom_call" | custom-call | flops 1000 | bytes 655360 | tf_op jit(solution)/shard_map/assembled/pallas_call | solution.py:430
  182.0 3.0 %collective-permute-done.20.refs_3_ = bf16[256,384]{1,0:T(8,128)(2,1)S(1)} collective-permute-done((bf16[256,384]{1,0:T(8,128)(2,1)}, bf16[256,384]{1,0:T(8,128)(2,1)S(1)}, u32[]{:S(2)}, u32[]{:S(2)}) %collective-permute-start.20) | collective-permute-done | bytes 196640 | tf_op jit(solution)/shard_map/ppermute | solution.py:529
  184.9 1.6 assembled.3
  (100 shorter events, 35.1 us)
Async XLA Ops:
  2.4 26.6 %collective-permute-start.1 = (bf16[512,1024]{1,0:T(8,128)(2,1)}, bf16[512,1024]{1,0:T(8,128)(2,1)}, u32[]{:S(2)}, u32[]{:S(2)}) collective-permute-start(bf16[512,1024]{1,0:T(8,128)(2,1)} %b_strips.3.refs_4_), channel_id=1, source_target_pairs={{0,4},{2,6},{4,0},{6,2},{8,12},{10,14},{12,8},{14,10},{1,5},{3,7},... | collective-permute-start | bytes 3145736 | tf_op jit(solution)/shard_map/ppermute | solution.py:471
  5.5 23.5 %collective-permute-start.2 = (bf16[512,1024]{1,0:T(8,128)(2,1)}, bf16[512,1024]{1,0:T(8,128)(2,1)S(1)}, u32[]{:S(2)}, u32[]{:S(2)}) collective-permute-start(bf16[512,1024]{1,0:T(8,128)(2,1)} %b_strips.3.refs_4_), channel_id=1, source_target_pairs={{4,8},{6,10},{8,4},{10,6},{5,9},{7,11},{9,5},{11,7},{20,24},{22,26... | collective-permute-start | bytes 3145736 | tf_op jit(solution)/shard_map/ppermute | solution.py:471
  6.2 4.0 %copy-start.29 = (s32[8,64]{1,0:T(8,128)S(1)}, s32[8,64]{1,0:T(8,128)}, u32[]{:S(2)}) copy-start(s32[8,64]{1,0:T(8,128)} %param.6) | copy-start | bytes 6148
  8.6 25.0 %collective-permute-start = (bf16[512,1024]{1,0:T(8,128)(2,1)}, bf16[512,1024]{1,0:T(8,128)(2,1)}, u32[]{:S(2)}, u32[]{:S(2)}) collective-permute-start(bf16[512,1024]{1,0:T(8,128)(2,1)} %b_strips.2), channel_id=1, source_target_pairs={{0,2},{2,0},{4,6},{6,4},{8,10},{10,8},{12,14},{14,12},{1,3},{3,1},... | collective-permute-start | bytes 3145736 | tf_op jit(solution)/shard_map/ppermute | solution.py:471
  10.6 2.2 %copy-start.4 = (bf16[512,4096]{1,0:T(8,128)(2,1)S(1)}, bf16[512,4096]{1,0:T(8,128)(2,1)}, u32[]{:S(2)}) copy-start(bf16[512,4096]{1,0:T(8,128)(2,1)} %x_ref.3) | copy-start | bytes 12582916
  29.0 16.9 %copy-start.10 = (bf16[512,1024]{1,0:T(8,128)(2,1)}, bf16[512,1024]{1,0:T(8,128)(2,1)S(1)}, u32[]{:S(2)}) copy-start(bf16[512,1024]{1,0:T(8,128)(2,1)S(1)} %collective-permute-done.2.refs_6_) | copy-start | bytes 3145732
  33.6 11.2 %collective-permute-start.3 = (bf16[512,1024]{1,0:T(8,128)(2,1)}, bf16[512,1024]{1,0:T(8,128)(2,1)}, u32[]{:S(2)}, u32[]{:S(2)}) collective-permute-start(bf16[512,1024]{1,0:T(8,128)(2,1)} %collective-permute-done.refs_5_), channel_id=1, source_target_pairs={{4,8},{6,10},{8,4},{10,6},{5,9},{7,11},{9,5},{11,7},{20,24},{22,26... | collective-permute-start | bytes 3145736 | tf_op jit(solution)/shard_map/ppermute | solution.py:471
  35.3 65.4 %collective-permute-start.9 = (bf16[256,4096]{1,0:T(8,128)(2,1)S(1)}, bf16[256,4096]{1,0:T(8,128)(2,1)}, u32[]{:S(2)}, u32[]{:S(2)}) collective-permute-start(bf16[256,4096]{1,0:T(8,128)(2,1)S(1)} %masked_half.2.refs_0_), channel_id=1, source_target_pairs={{0,2},{2,0},{4,6},{6,4},{8,10},{10,8},{12,14},{14,12},{1,3},{3,1},... | collective-permute-start | bytes 6291464 | tf_op jit(solution)/shard_map/ppermute | solution.py:471
  36.8 43.0 %collective-permute-start.5 = (bf16[512,1024]{1,0:T(8,128)(2,1)}, bf16[512,1024]{1,0:T(8,128)(2,1)}, u32[]{:S(2)}, u32[]{:S(2)}) collective-permute-start(bf16[512,1024]{1,0:T(8,128)(2,1)} %collective-permute-done.refs_5_), channel_id=1, source_target_pairs={{0,4},{2,6},{4,0},{6,2},{8,12},{10,14},{12,8},{14,10},{1,5},{3,7},... | collective-permute-start | bytes 3145736 | tf_op jit(solution)/shard_map/ppermute | solution.py:471
  42.8 5.8 %collective-permute-start.7 = (bf16[512,512]{1,0:T(8,128)(2,1)S(1)}, bf16[512,512]{1,0:T(8,128)(2,1)S(1)}, u32[]{:S(2)}, u32[]{:S(2)}) collective-permute-start(bf16[512,512]{1,0:T(8,128)(2,1)S(1)} %get-tuple-element.62), channel_id=1, source_target_pairs={{4,8},{6,10},{8,4},{10,6},{5,9},{7,11},{9,5},{11,7},{20,24},{22,26... | collective-permute-start | bytes 1572872 | tf_op jit(solution)/shard_map/ppermute | solution.py:471
  43.5 36.3 %collective-permute-start.6 = (bf16[512,640]{1,0:T(8,128)(2,1)S(1)}, bf16[512,640]{1,0:T(8,128)(2,1)S(1)}, u32[]{:S(2)}, u32[]{:S(2)}) collective-permute-start(bf16[512,640]{1,0:T(8,128)(2,1)S(1)} %slice.15), channel_id=1, source_target_pairs={{4,0},{6,2},{8,12},{10,14},{5,1},{7,3},{9,13},{11,15},{20,16},{22,... | collective-permute-start | bytes 1966088 | tf_op jit(solution)/shard_map/ppermute | solution.py:471
  47.2 52.4 %collective-permute-start.4 = (bf16[512,1024]{1,0:T(8,128)(2,1)S(1)}, bf16[512,1024]{1,0:T(8,128)(2,1)S(1)}, u32[]{:S(2)}, u32[]{:S(2)}) collective-permute-start(bf16[512,1024]{1,0:T(8,128)(2,1)S(1)} %pad_maximum_fusion), channel_id=1, source_target_pairs={{4,0},{6,2},{8,12},{10,14},{5,1},{7,3},{9,13},{11,15},{20,16},{22,... | collective-permute-start | bytes 3145736 | tf_op jit(solution)/shard_map/ppermute | solution.py:471
  48.5 53.2 %copy-start.13 = (bf16[512,512]{1,0:T(8,128)(2,1)}, bf16[512,512]{1,0:T(8,128)(2,1)S(1)}, u32[]{:S(2)}) copy-start(bf16[512,512]{1,0:T(8,128)(2,1)S(1)} %collective-permute-done.7.refs_5_) | copy-start | bytes 1572868
  79.8 22.0 %copy-start.27 = (bf16[512,640]{1,0:T(8,128)(2,1)}, bf16[512,640]{1,0:T(8,128)(2,1)S(1)}, u32[]{:S(2)}) copy-start(bf16[512,640]{1,0:T(8,128)(2,1)S(1)} %collective-permute-done.6.refs_12_) | copy-start | bytes 1966084
  81.3 0.7 collective-permute-start.8
  82.0 18.6 %copy-start.15 = (bf16[512,512]{1,0:T(8,128)(2,1)}, bf16[512,512]{1,0:T(8,128)(2,1)S(1)}, u32[]{:S(2)}) copy-start(bf16[512,512]{1,0:T(8,128)(2,1)S(1)} %collective-permute-done.8.refs_6_) | copy-start | bytes 1572868
  100.7 8.5 %collective-permute-start.10 = (bf16[256,4096]{1,0:T(8,128)(2,1)}, bf16[256,4096]{1,0:T(8,128)(2,1)}, u32[]{:S(2)}, u32[]{:S(2)}) collective-permute-start(bf16[256,4096]{1,0:T(8,128)(2,1)} %collective-permute-done.9.refs_2_), channel_id=1, source_target_pairs={{0,1},{1,0},{2,3},{3,2},{4,5},{5,4},{6,7},{7,6},{8,9},{9,8},{10,11... | collective-permute-start | bytes 6291464 | tf_op jit(solution)/shard_map/ppermute | solution.py:504
  101.8 27.8 %collective-permute-start.11 = (bf16[512,1024]{1,0:T(8,128)(2,1)}, bf16[512,1024]{1,0:T(8,128)(2,1)S(1)}, u32[]{:S(2)}, u32[]{:S(2)}) collective-permute-start(bf16[512,1024]{1,0:T(8,128)(2,1)} %pad_maximum_fusion.1), channel_id=1, source_target_pairs={{4,8},{6,10},{8,4},{10,6},{5,9},{7,11},{9,5},{11,7},{20,24},{22,26... | collective-permute-start | bytes 3145736 | tf_op jit(solution)/shard_map/ppermute | solution.py:471
  102.5 2.2 %copy-start.5 = (bf16[512,4096]{1,0:T(8,128)(2,1)S(1)}, bf16[512,4096]{1,0:T(8,128)(2,1)}, u32[]{:S(2)}) copy-start(bf16[512,4096]{1,0:T(8,128)(2,1)} %x_ref.3) | copy-start | bytes 12582916
  106.5 22.3 %collective-permute-start.12 = (bf16[512,512]{1,0:T(8,128)(2,1)}, bf16[512,512]{1,0:T(8,128)(2,1)S(1)}, u32[]{:S(2)}, u32[]{:S(2)}) collective-permute-start(bf16[512,512]{1,0:T(8,128)(2,1)} %copy-done.13), channel_id=1, source_target_pairs={{4,0},{6,2},{8,12},{10,14},{5,1},{7,3},{9,13},{11,15},{20,16},{22,... | collective-permute-start | bytes 1572872 | tf_op jit(solution)/shard_map/ppermute | solution.py:471
  107.8 26.5 %collective-permute-start.13 = (bf16[512,512]{1,0:T(8,128)(2,1)}, bf16[512,512]{1,0:T(8,128)(2,1)}, u32[]{:S(2)}, u32[]{:S(2)}) collective-permute-start(bf16[512,512]{1,0:T(8,128)(2,1)} %copy-done.15), channel_id=1, source_target_pairs={{4,0},{6,2},{8,12},{10,14},{5,1},{7,3},{9,13},{11,15},{20,16},{22,... | collective-permute-start | bytes 1572872 | tf_op jit(solution)/shard_map/ppermute | solution.py:471
  109.1 1.6 copy-start.1
  126.8 2.0 %copy-start.6 = (f32[2,512,1024]{2,1,0:T(8,128)}, f32[2,512,1024]{2,1,0:T(8,128)S(1)}, u32[]{:S(2)}) copy-start(f32[2,512,1024]{2,1,0:T(8,128)S(1)} %first_products.1.refs_4_) | copy-start | bytes 12582916
  130.7 35.1 %collective-permute-start.14 = (bf16[512,768]{1,0:T(8,128)(2,1)}, bf16[512,768]{1,0:T(8,128)(2,1)}, u32[]{:S(2)}, u32[]{:S(2)}) collective-permute-start(bf16[512,768]{1,0:T(8,128)(2,1)} %pad_maximum_fusion.2), channel_id=1, source_target_pairs={{4,0},{6,2},{8,12},{10,14},{5,1},{7,3},{9,13},{11,15},{20,16},{22,... | collective-permute-start | bytes 2359304 | tf_op jit(solution)/shard_map/ppermute | solution.py:471
  135.9 2.2 %copy-start.7 = (f32[2,512,1024]{2,1,0:T(8,128)S(1)}, f32[2,512,1024]{2,1,0:T(8,128)}, u32[]{:S(2)}) copy-start(f32[2,512,1024]{2,1,0:T(8,128)} %copy-done.6) | copy-start | bytes 12582916
  148.1 1.9 %collective-permute-start.15 = (bf16[256,640]{1,0:T(8,128)(2,1)}, bf16[256,640]{1,0:T(8,128)(2,1)S(1)}, u32[]{:S(2)}, u32[]{:S(2)}) collective-permute-start(bf16[256,640]{1,0:T(8,128)(2,1)} %get-tuple-element.47), channel_id=1, source_target_pairs={{0,1},{1,0},{2,3},{3,2},{4,5},{5,4},{6,7},{7,6},{8,9},{9,8},{10,11... | collective-permute-start | bytes 983048 | tf_op jit(solution)/shard_map/ppermute | solution.py:527
  148.1 10.7 %collective-permute-start.16 = (bf16[256,640]{1,0:T(8,128)(2,1)}, bf16[256,640]{1,0:T(8,128)(2,1)S(1)}, u32[]{:S(2)}, u32[]{:S(2)}) collective-permute-start(bf16[256,640]{1,0:T(8,128)(2,1)} %get-tuple-element.48), channel_id=1, source_target_pairs={{0,2},{2,0},{4,6},{6,4},{8,10},{10,8},{12,14},{14,12},{1,3},{3,1},... | collective-permute-start | bytes 983048 | tf_op jit(solution)/shard_map/ppermute | solution.py:471
  148.6 16.4 %collective-permute-start.17 = (bf16[256,640]{1,0:T(8,128)(2,1)}, bf16[256,640]{1,0:T(8,128)(2,1)S(1)}, u32[]{:S(2)}, u32[]{:S(2)}) collective-permute-start(bf16[256,640]{1,0:T(8,128)(2,1)} %get-tuple-element.49), channel_id=1, source_target_pairs={{0,3},{1,2},{2,1},{3,0},{4,7},{5,6},{6,5},{7,4},{8,11},{9,10},{10,... | collective-permute-start | bytes 983048 | tf_op jit(solution)/shard_map/ppermute | solution.py:529
  168.8 6.9 %copy-start.30 = (s32[4,64]{1,0:T(4,128)S(1)}, s32[4,64]{1,0:T(4,128)}, u32[]{:S(2)}) copy-start(s32[4,64]{1,0:T(4,128)} %param.7) | copy-start | bytes 3076
  173.8 7.2 %collective-permute-start.18 = (bf16[256,384]{1,0:T(8,128)(2,1)}, bf16[256,384]{1,0:T(8,128)(2,1)S(1)}, u32[]{:S(2)}, u32[]{:S(2)}) collective-permute-start(bf16[256,384]{1,0:T(8,128)(2,1)} %get-tuple-element.52), channel_id=1, source_target_pairs={{0,1},{1,0},{2,3},{3,2},{4,5},{5,4},{6,7},{7,6},{8,9},{9,8},{10,11... | collective-permute-start | bytes 589832 | tf_op jit(solution)/shard_map/ppermute | solution.py:527
  174.0 7.9 %collective-permute-start.19 = (bf16[256,384]{1,0:T(8,128)(2,1)}, bf16[256,384]{1,0:T(8,128)(2,1)S(1)}, u32[]{:S(2)}, u32[]{:S(2)}) collective-permute-start(bf16[256,384]{1,0:T(8,128)(2,1)} %get-tuple-element.53), channel_id=1, source_target_pairs={{0,2},{2,0},{4,6},{6,4},{8,10},{10,8},{12,14},{14,12},{1,3},{3,1},... | collective-permute-start | bytes 589832 | tf_op jit(solution)/shard_map/ppermute | solution.py:471
  174.6 10.4 %collective-permute-start.20 = (bf16[256,384]{1,0:T(8,128)(2,1)}, bf16[256,384]{1,0:T(8,128)(2,1)S(1)}, u32[]{:S(2)}, u32[]{:S(2)}) collective-permute-start(bf16[256,384]{1,0:T(8,128)(2,1)} %get-tuple-element.54), channel_id=1, source_target_pairs={{0,3},{1,2},{2,1},{3,0},{4,7},{5,6},{6,5},{7,4},{8,11},{9,10},{10,... | collective-permute-start | bytes 589832 | tf_op jit(solution)/shard_map/ppermute | solution.py:529
  (20 other events, 21.9 us)

commit v4 on v3

--- a/solution.py
+++ b/solution.py
@@ -48,48 +48,50 @@
     return (mine * keep).astype(jnp.bfloat16)
 
 
-def strips_kernel(quarter_ref, w_ref, b_ref, held, sems):
-    panel = held.shape[0]
-    quarter = quarter_ref[0]
-    band = held.shape[1] // LANES
-    copies = []
-    for j in range(band):
-        at = pl.multiple_of(j * panel + quarter * LANES, LANES)
-        copies.append(
-            pltpu.make_async_copy(
-                w_ref.at[:, pl.ds(at, LANES)],
-                held.at[:, j * LANES : (j + 1) * LANES],
-                sems.at[j],
-            )
-        )
-        copies[-1].start()
-    for j in range(band):
-        copies[j].wait()
-        value = -0.5 * held[:, j * LANES : (j + 1) * LANES].astype(jnp.float32)
-        if j == band // 2:
-            rows = lax.broadcasted_iota(jnp.int32, value.shape, 0)
-            cols = lax.broadcasted_iota(jnp.int32, value.shape, 1)
-            value = value + jnp.where(rows == cols + quarter * LANES, 1.5, 0.0)
-        b_ref[:, j * LANES : (j + 1) * LANES] = value.astype(jnp.bfloat16)
-
-
-def b_strips(w_band, quarter):
+def strips_kernel(quarters_ref, w_ref, *refs):
+    *b_refs, held, sems = refs
+    _, panel, width = held.shape
+    band = width // LANES
+
+    def copy(k, j):
+        at = pl.multiple_of(j * panel + quarters_ref[k] * LANES, LANES)
+        to = held.at[k, :, j * LANES : (j + 1) * LANES]
+        return pltpu.make_async_copy(w_ref.at[:, pl.ds(at, LANES)], to, sems.at[k, j])
+
+    for k in range(len(b_refs)):
+        for j in range(band):
+            copy(k, j).start()
+    for k, b_ref in enumerate(b_refs):
+        for j in range(band):
+            copy(k, j).wait()
+            value = -0.5 * held[k, :, j * LANES : (j + 1) * LANES].astype(jnp.float32)
+            if j == band // 2:
+                rows = lax.broadcasted_iota(jnp.int32, value.shape, 0)
+                cols = lax.broadcasted_iota(jnp.int32, value.shape, 1)
+                value = value + jnp.where(rows == cols + quarters_ref[k] * LANES, 1.5, 0.0)
+            b_ref[:, j * LANES : (j + 1) * LANES] = value.astype(jnp.bfloat16)
+
+
+def b_strips(w_band, quarters):
     panel = w_band.shape[0]
     band = w_band.shape[1] // panel
+    n = len(quarters)
     shape = (panel, band * LANES)
     return pl.pallas_call(
         strips_kernel,
-        out_shape=jax.ShapeDtypeStruct(shape, jnp.bfloat16),
+        out_shape=[jax.ShapeDtypeStruct(shape, jnp.bfloat16)] * n,
         in_specs=[
             pl.BlockSpec(memory_space=pltpu.SMEM),
             pl.BlockSpec(memory_space=pltpu.HBM),
         ],
-        out_specs=pl.BlockSpec(memory_space=pltpu.VMEM),
-        scratch_shapes=[pltpu.VMEM(shape, jnp.bfloat16), pltpu.SemaphoreType.DMA((band,))],
-        compiler_params=pltpu.CompilerParams(vmem_limit_bytes=60 * MIB),
-        cost_estimate=pl.CostEstimate(flops=1000, bytes_accessed=4 * shape[0] * shape[1], transcendentals=0),
+        out_specs=[pl.BlockSpec(memory_space=pltpu.VMEM)] * n,
+        scratch_shapes=[pltpu.VMEM((n, *shape), jnp.bfloat16), pltpu.SemaphoreType.DMA((n, band))],
+        compiler_params=pltpu.CompilerParams(vmem_limit_bytes=56 * MIB),
+        cost_estimate=pl.CostEstimate(
+            flops=1000, bytes_accessed=4 * n * shape[0] * shape[1], transcendentals=0
+        ),
         name="b_strips",
-    )(quarter.reshape(1), w_band)
+    )(jnp.stack(quarters), w_band)
 
 
 def mask_kernel(half_ref, mask_ref, x_ref, out_ref):
@@ -112,7 +114,7 @@
             out_specs=pl.BlockSpec((block, cols), lambda i, h: (i, 0)),
         ),
         out_shape=jax.ShapeDtypeStruct((x_band.shape[0] // 2, cols), jnp.bfloat16),
-        compiler_params=pltpu.CompilerParams(vmem_limit_bytes=16 * MIB),
+        compiler_params=pltpu.CompilerParams(vmem_limit_bytes=58 * MIB),
         cost_estimate=pl.CostEstimate(flops=1000, bytes_accessed=2 * x_band.shape[0] * cols, transcendentals=0),
         name="masked_half",
     )(half.reshape(1), mask_wide, x_band)
@@ -144,16 +146,17 @@
 
 
 def first_kernel(meta_ref, *refs):
-    x_refs, middle_refs, near_refs, (mid_a_ref, mid_b_ref), refs = refs[:4], refs[4:10], refs[10:12], refs[12:14], refs[14:]
+    x_refs, middle_refs, (near_a_ref, near_b_ref, mid_b_ref), refs = refs[:4], refs[4:10], refs[10:13], refs[13:]
     out_ref, xv, bv, acc, x_sems, b_sems, out_sems = refs
     n_b = len(middle_refs)
     quarter = bv.shape[2]
     low = quarter // 2
-    split = quarter - mid_a_ref.shape[1]
+    near = quarter - LANES
+    split = quarter - (near_b_ref.shape[1] - near)
     is_end = meta_ref[0]
 
     def offset_of(p, g):
-        return meta_ref[2 + 2 * p + g]
+        return meta_ref[3 + 2 * p + g]
 
     def b_middle(p):
         return [pltpu.make_async_copy(middle_refs[p], bv.at[p], b_sems.at[p])]
@@ -161,11 +164,14 @@
     def b_end(p):
         if p < 2:
             return b_middle(p)
-        if p < 4:
-            return [pltpu.make_async_copy(near_refs[p - 2], bv.at[p], b_sems.at[p])]
+        if p == 2:
+            return [pltpu.make_async_copy(near_a_ref, bv.at[2], b_sems.at[2])]
+        if p == 3:
+            at = pl.multiple_of(meta_ref[2] * LANES, LANES)
+            return [pltpu.make_async_copy(near_b_ref.at[:, :near], bv.at[3, :, pl.ds(at, near)], b_sems.at[3])]
         if p == 4:
             return [
-                pltpu.make_async_copy(mid_a_ref, bv.at[4, :, split:], b_sems.at[4]),
+                pltpu.make_async_copy(near_b_ref.at[:, near:], bv.at[4, :, split:], b_sems.at[4]),
                 pltpu.make_async_copy(mid_b_ref.at[:, :split], bv.at[4 + meta_ref[1], :, :split], b_sems.at[6]),
             ]
         return [pltpu.make_async_copy(mid_b_ref.at[:, split:], bv.at[5, :, split:], b_sems.at[5])]
@@ -210,7 +216,7 @@
         out.wait()
 
 
-def first_products(meta, xs, middle, near, mid):
+def first_products(meta, xs, middle, end):
     rows = xs[0].shape[0]
     panel, quarter = middle[0].shape
     n_b = len(middle)
@@ -219,7 +225,7 @@
     return pl.pallas_call(
         first_kernel,
         out_shape=jax.ShapeDtypeStruct((2, 2 * rows, quarter), jnp.float32),
-        in_specs=[pl.BlockSpec(memory_space=pltpu.SMEM)] + [x_spec] * 4 + [any_spec] * (n_b + 4),
+        in_specs=[pl.BlockSpec(memory_space=pltpu.SMEM)] + [x_spec] * 4 + [any_spec] * (n_b + 3),
         out_specs=any_spec,
         scratch_shapes=[
             pltpu.VMEM((n_b, 2, 2 * rows, panel), jnp.bfloat16),
@@ -229,14 +235,14 @@
             pltpu.SemaphoreType.DMA((n_b + 1,)),
             pltpu.SemaphoreType.DMA((2,)),
         ],
-        compiler_params=pltpu.CompilerParams(vmem_limit_bytes=32 * MIB),
+        compiler_params=pltpu.CompilerParams(vmem_limit_bytes=59 * MIB),
         cost_estimate=pl.CostEstimate(
             flops=2 * n_b * 4 * rows * panel * quarter,
             bytes_accessed=n_b * 2 * (4 * rows * panel + panel * quarter),
             transcendentals=0,
         ),
         name="first_products",
-    )(meta, *xs, *middle, *near, *mid)
+    )(meta, *xs, *middle, *end)
 
 
 def give_pieces(out_refs, acc, at):
@@ -331,7 +337,7 @@
             pltpu.SemaphoreType.DMA,
             pltpu.SemaphoreType.DMA,
         ],
-        compiler_params=pltpu.CompilerParams(vmem_limit_bytes=24 * MIB),
+        compiler_params=pltpu.CompilerParams(vmem_limit_bytes=59 * MIB),
         cost_estimate=pl.CostEstimate(
             flops=2 * 2 * 4 * rows * panel * quarter, bytes_accessed=10 * MIB, transcendentals=0
         ),
@@ -393,7 +399,7 @@
             pltpu.SemaphoreType.DMA,
             pltpu.SemaphoreType.DMA,
         ],
-        compiler_params=pltpu.CompilerParams(vmem_limit_bytes=24 * MIB),
+        compiler_params=pltpu.CompilerParams(vmem_limit_bytes=59 * MIB),
         cost_estimate=pl.CostEstimate(
             flops=2 * 4 * rows * panel * b.shape[1], bytes_accessed=5 * MIB, transcendentals=0
         ),
@@ -461,6 +467,7 @@
     q = 2 * y + c
 
     swap = [(0, 2), (1, 3), (2, 0), (3, 1), (4, 6), (5, 7), (6, 4), (7, 5)]
+    inward = [(0, 2), (1, 3), (6, 4), (7, 5)]
     outward = [(2, 0), (3, 1), (4, 6), (5, 7)]
     cross = [(2, 4), (3, 5), (4, 2), (5, 3)]
     across = [(i, i ^ 1) for i in range(8)]
@@ -473,33 +480,35 @@
     def strips(value, start, count):
         return lax.dynamic_slice_in_dim(value, start * LANES, count * LANES, 1)
 
+    start_near = jnp.where(left, 0, 1)
     first_out, second_out = jnp.where(left, 0, 4), jnp.where(left, 4, 0)
     first_in, second_in = second_out, first_out
     last_in = jnp.where(left, 1, 4)
 
-    own_a = b_strips(w_band, q)
+    sent_b, own_a = b_strips(w_band, [q ^ 2, q])
+    own_b = line(sent_b, across)
     swap_a = line(own_a, swap)
     cross_a = line(own_a, cross)
-    own_b = line(b_strips(w_band, q ^ 2), across)
     mask_wide = widen(a_mask, block)
     x_mine = masked_half(x_band, mask_wide, c)
     own_b, x_mine, swap_a, cross_a = together(own_b, x_mine, swap_a, cross_a)
-    swap_b = line(own_b, swap)
+    near_b = line(jnp.concatenate([strips(own_b, start_near, 7), cross_a[:, 3 * LANES :]], 1), outward)
+    in_b = line(own_b, inward)
     cross_b = line(own_b, cross)
     x_across = line(x_mine, across)
     x_rest = masked_half(x_band, mask_wide, 1 - c)
 
-    mid_a = line(cross_a[:, 3 * LANES :], outward)
     fwd_a = line(strips(swap_a, first_out, 4), cross)
+    in_b, cross_b = together(in_b, cross_b)
     mid_b = line(
         jnp.concatenate([jnp.where(y == 0, cross_a[:, : 3 * LANES], cross_b[:, : 3 * LANES]), cross_b[:, 3 * LANES :]], 1),
         outward,
     )
-    swap_b, mid_a, fwd_a = together(swap_b, mid_a, fwd_a)
-    fwd_b = line(strips(swap_b, first_out, 4), cross)
-    fwd_second = line(jnp.concatenate([strips(v, second_out, 4) for v in (swap_a, swap_b)], 1), cross)
+    in_b, near_b, fwd_a = together(in_b, near_b, fwd_a)
+    fwd_b = line(strips(in_b, first_out, 4), cross)
+    fwd_second = line(jnp.concatenate([strips(v, second_out, 4) for v in (swap_a, in_b)], 1), cross)
     far_a = line(fwd_a, outward)
-    mid_b, fwd_b, x_across = together(mid_b, fwd_b, x_across)
+    x_across, mid_b, fwd_b = together(x_across, mid_b, fwd_b)
     far_b = line(fwd_b, outward)
     x_opposite = lax.ppermute(x_across, "depth", layers)
     xs = [x_mine, x_rest, x_across, x_opposite]
@@ -511,14 +520,14 @@
     zero = jnp.zeros_like(z)
     third = offsets(jnp.where(is_end == 1, 2, -toward))
     fourth = offsets(jnp.where(is_end == 1, -toward, 2))
-    meta = jnp.stack([is_end, y, *offsets(zero), *offsets(toward), *third]).astype(jnp.int32)
+    meta = jnp.stack([is_end, y, start_near, *offsets(zero), *offsets(toward), *third]).astype(jnp.int32)
     total = first_products(
-        meta, xs, [own_a, own_b, cross_a, cross_b, swap_a, swap_b], [swap_a, swap_b], [mid_a, mid_b]
+        meta, xs, [own_a, own_b, cross_a, cross_b, swap_a, in_b], [swap_a, near_b, mid_b]
     )
-    fwd_second, total, far_a = together(fwd_second, total, far_a)
     last = jnp.concatenate(
         [strips(fwd_second, jnp.where(left, 1, 0), 3), strips(fwd_second, jnp.where(left, 5, 4), 3)], 1
     )
+    last, total, far_a = together(last, total, far_a)
     far_second = line(last, outward)
 
     def exchanged(pieces):
@@ -532,7 +541,8 @@
     done_at, rest_at = jnp.where(left, 3, 0), jnp.where(left, 0, 5)
     meta = jnp.stack([is_end, first_in, second_in, done_at, rest_at, *fourth]).astype(jnp.int32)
     *done, rest = half_products(meta, xs, total, [fwd_a, fwd_b], [far_a, far_b], fwd_second, 5)
-    far_second, *done = together(far_second, *exchanged(done))
+    done = exchanged(done)
+    far_second, done[1] = together(far_second, done[1])
     keep_wide = widen(keep_mask, block)
     out = assembled(jnp.stack([q, done_at]).astype(jnp.int32), keep_wide, done)
     meta = jnp.stack([is_end, last_in, rest_at, *fourth]).astype(jnp.int32)

time: 188 us -> 190 us (1.011)
  local copies, waits for them, and re-layouts: 36.9 us -> 12.2 us
  Pallas kernels: 31.2 us -> 43.1 us
  waiting for transfers between devices: 89.1 us -> 99 us
  starting transfers between devices: 25.6 us -> 28.8 us
  other arithmetic: 3.33 us -> 5.49 us
    unnamed x62 -> x26, local copies, waits for them, and re-layouts: 32.1 us -> 4.09 us
    ppermute x16, waiting for transfers between devices: 80.6 us -> 95.7 us  [line(): return lax.ppermute(value, 'grid', pairs)]
    pallas_call x2, Pallas kernels: 0.81 us -> 7.9 us  [masked_half(): pl.pallas_call(mask_kernel, grid_spec=pltpu.PrefetchScalarGridSpec(num_sc...]
    ppermute x16, starting transfers between devices: 22.8 us -> 28.1 us  [line(): return lax.ppermute(value, 'grid', pairs)]
    ppermute x2, waiting for transfers between devices: 8.47 us -> 3.31 us  [exchanged(): lax.ppermute(pieces[3], ('grid', 'depth'), opposite)]
    pallas_call x1, Pallas kernels: 11.3 us -> 13.9 us  [first_products(): pl.pallas_call(first_kernel, out_shape=jax.ShapeDtypeStruct((2, 2 * rows,...]
    pallas_call x1, Pallas kernels: 5.7 us -> 7.81 us  [half_products(): pl.pallas_call(half_kernel, out_shape=[jax.ShapeDtypeStruct((rows, n_done...]
    ppermute x2, starting transfers between devices: 2.47 us -> 0.56 us  [exchanged(): lax.ppermute(pieces[3], ('grid', 'depth'), opposite)]
  transfers between devices with their start and end apart: 21 -> 21, of which waited for: 9 -> 9; matrix products, arithmetic and copies ran while one was open for 4% -> 7% of each run, Pallas kernels for 12% -> 20%
where the time goes in v4:
time: 190 us; the launch traced here: 189 us
  waiting for transfers between devices  99 us (52%)
  Pallas kernels  43.1 us (23%)
  starting transfers between devices  28.8 us (15%)
  local copies, waits for them, and re-layouts  12.2 us (6%)
  other arithmetic  5.49 us (3%)
    ppermute x16, waiting for transfers between devices, line(): return lax.ppermute(value, 'grid', pairs)  95.7 us
    ppermute x16, starting transfers between devices, line(): return lax.ppermute(value, 'grid', pairs)  28.1 us
    pallas_call x1, Pallas kernels, first_products(): pl.pallas_call(first_kernel, out_shape=jax.ShapeDtypeStruct((2, 2 * rows,...  13.9 us
    pallas_call x2, Pallas kernels, masked_half(): pl.pallas_call(mask_kernel, grid_spec=pltpu.PrefetchScalarGridSpec(num_sc...  7.9 us
    pallas_call x1, Pallas kernels, half_products(): pl.pallas_call(half_kernel, out_shape=[jax.ShapeDtypeStruct((rows, n_done...  7.81 us
    pallas_call x1, Pallas kernels, rest_products(): pl.pallas_call(rest_kernel, out_shape=[jax.ShapeDtypeStruct((rows, width)...  5.88 us
    unnamed x26, local copies, waits for them, and re-layouts  4.09 us
    pallas_call x1, Pallas kernels, b_strips(): pl.pallas_call(strips_kernel, out_shape=[jax.ShapeDtypeStruct(shape, jnp....  3.98 us
  transfers between devices with their start and end apart: 21, of which 9 were waited for; matrix products, arithmetic and copies ran while one was open for 7% of the time, Pallas kernels for 20%

profile of v4, /device:TPU:0, one launch (start us, length us, event | category | flops | bytes accessed | tf_op | source)
XLA Modules:
  0.0 188.9 jit_solution(570978378626609195)
XLA Ops:
  0.7 4.0 %b_strips.1 = (bf16[512,1024]{1,0:T(8,128)(2,1)}, bf16[512,1024]{1,0:T(8,128)(2,1)}) custom-call(s32[2]{0:T(128)} %pad_add_fusion.1.quarters_ref, bf16[512,4096]{1,0:T(8,128)(2,1)} %w_ref.1), custom_call_target="tpu_custom_call" | custom-call | flops 1000 | bytes 4194304 | tf_op jit(solution)/shard_map/b_strips/pallas_call | solution.py:80
  4.6 3.1 %collective-permute-start.1 = (bf16[512,1024]{1,0:T(8,128)(2,1)}, bf16[512,1024]{1,0:T(8,128)(2,1)S(1)}, u32[]{:S(2)}, u32[]{:S(2)}) collective-permute-start(bf16[512,1024]{1,0:T(8,128)(2,1)} %get-tuple-element.34.refs_4_), channel_id=1, source_target_pairs={{0,4},{2,6},{4,0},{6,2},{8,12},{10,14},{12,8},{14,10},{1,5},{3,7},... | collective-permute-start | bytes 3145736 | tf_op jit(solution)/shard_map/ppermute | solution.py:478
  8.4 1.6 collective-permute-start
  11.0 3.9 %masked_half.2.refs_0_ = bf16[256,4096]{1,0:T(8,128)(2,1)} custom-call(s32[1]{0:T(128)} %bitcast.8.half_ref, f32[8,1,4096]{2,1,0:T(1,128)} %reshape.16.mask_ref, bf16[512,4096]{1,0:T(8,128)(2,1)} %x_ref.3), custom_call_target="tpu_custom_call" | custom-call | flops 1000 | bytes 4194304 | tf_op jit(solution)/shard_map/masked_half/pallas_call | solution.py:105
  14.9 16.2 %collective-permute-done.1.refs_8_.refs_10_ = bf16[512,1024]{1,0:T(8,128)(2,1)S(1)} collective-permute-done((bf16[512,1024]{1,0:T(8,128)(2,1)}, bf16[512,1024]{1,0:T(8,128)(2,1)S(1)}, u32[]{:S(2)}, u32[]{:S(2)}) %collective-permute-start.1) | collective-permute-done | bytes 1048608 | tf_op jit(solution)/shard_map/ppermute | solution.py:478
  31.1 2.3 %collective-permute-done.refs_5_ = bf16[512,1024]{1,0:T(8,128)(2,1)} collective-permute-done((bf16[512,1024]{1,0:T(8,128)(2,1)}, bf16[512,1024]{1,0:T(8,128)(2,1)}, u32[]{:S(2)}, u32[]{:S(2)}) %collective-permute-start) | collective-permute-done | bytes 1048608 | tf_op jit(solution)/shard_map/ppermute | solution.py:478
  33.5 7.0 %collective-permute-start.4 = (bf16[512,1024]{1,0:T(8,128)(2,1)}, bf16[512,1024]{1,0:T(8,128)(2,1)}, u32[]{:S(2)}, u32[]{:S(2)}) collective-permute-start(bf16[512,1024]{1,0:T(8,128)(2,1)} %collective-permute-done.refs_5_), channel_id=1, source_target_pairs={{0,4},{2,6},{12,8},{14,10},{1,5},{3,7},{13,9},{15,11},{16,20},{18,... | collective-permute-start | bytes 3145736 | tf_op jit(solution)/shard_map/ppermute | solution.py:478
  40.4 1.6 collective-permute-start.5
  43.4 1.3 pad_maximum_fusion
  44.7 1.3 collective-permute-start.7
  46.0 1.6 collective-permute-start.3
  49.6 11.1 %collective-permute-done.4.refs_9_ = bf16[512,1024]{1,0:T(8,128)(2,1)} collective-permute-done((bf16[512,1024]{1,0:T(8,128)(2,1)}, bf16[512,1024]{1,0:T(8,128)(2,1)}, u32[]{:S(2)}, u32[]{:S(2)}) %collective-permute-start.4) | collective-permute-done | bytes 1048608 | tf_op jit(solution)/shard_map/ppermute | solution.py:478
  63.0 1.3 collective-permute-start.6
  64.3 19.9 %collective-permute-done.7.refs_11_ = bf16[512,1536]{1,0:T(8,128)(2,1)} collective-permute-done((bf16[512,1536]{1,0:T(8,128)(2,1)}, bf16[512,1536]{1,0:T(8,128)(2,1)}, u32[]{:S(2)}, u32[]{:S(2)}) %collective-permute-start.7) | collective-permute-done | bytes 1572896 | tf_op jit(solution)/shard_map/ppermute | solution.py:478
  85.5 1.5 collective-permute-start.9
  87.0 16.7 %collective-permute-done.6.refs_12_ = bf16[512,1024]{1,0:T(8,128)(2,1)S(1)} collective-permute-done((bf16[512,1024]{1,0:T(8,128)(2,1)S(1)}, bf16[512,1024]{1,0:T(8,128)(2,1)S(1)}, u32[]{:S(2)}, u32[]{:S(2)}) %collective-permute-start.6) | collective-permute-done | bytes 1048608 | tf_op jit(solution)/shard_map/ppermute | solution.py:478
  106.5 4.0 %masked_half.3.refs_1_ = bf16[256,4096]{1,0:T(8,128)(2,1)} custom-call(s32[1]{0:T(128)} %bitcast.9.half_ref, f32[8,1,4096]{2,1,0:T(1,128)} %reshape.16.mask_ref, bf16[512,4096]{1,0:T(8,128)(2,1)} %x_ref.3), custom_call_target="tpu_custom_call" | custom-call | flops 1000 | bytes 4194304 | tf_op jit(solution)/shard_map/masked_half/pallas_call | solution.py:105
  111.1 1.3 collective-permute-start.12
  112.4 1.3 collective-permute-start.13
  115.0 1.4 copy-done.3
  116.3 13.9 %first_products.1.refs_4_ = f32[2,512,1024]{2,1,0:T(8,128)} custom-call(s32[15]{0:T(128)} %stack.122.meta_ref, bf16[256,4096]{1,0:T(8,128)(2,1)} %masked_half.2.refs_0_, bf16[256,4096]{1,0:T(8,128)(2,1)} %masked_half.3.refs_1_, bf16[256,4096]{1,0:T(8,128)(2,1)} %collective-permute-done.3.refs_2_, bf16[256,4096]{1,0:T(8,128)(2,1)} %copy-done.3, ...), custom_call_target="tpu_custom_call" | custom-call | flops 6442450944 | bytes 12582912 | tf_op jit(solution)/shard_map/first_products/pallas_call | solution.py:225
  131.1 1.3 collective-permute-start.14
  133.0 5.9 %collective-permute-done.13.refs_8_ = bf16[512,512]{1,0:T(8,128)(2,1)} collective-permute-done((bf16[512,512]{1,0:T(8,128)(2,1)}, bf16[512,512]{1,0:T(8,128)(2,1)}, u32[]{:S(2)}, u32[]{:S(2)}) %collective-permute-start.13) | collective-permute-done | bytes 524320 | tf_op jit(solution)/shard_map/ppermute | solution.py:478
  138.9 7.8 %half_products.1 = (bf16[256,640]{1,0:T(8,128)(2,1)}, bf16[256,640]{1,0:T(8,128)(2,1)}, bf16[256,640]{1,0:T(8,128)(2,1)}, bf16[256,640]{1,0:T(8,128)(2,1)}, f32[2,512,384]{2,1,0:T(8,128)}) custom-call(s32[9]{0:T(128)} %stack.111.meta_ref, bf16[256,4096]{1,0:T(8,128)(2,1)} %masked_half.2.refs_0_, bf16[256,4096]{1,0:T(8,128)(2,1)} %masked_half.3.refs_1_, ...), custom_call_target="tpu_custom_call" | custom-call | flops 2147483648 | bytes 10485760 | tf_op jit(solution)/shard_map/half_products/pallas_call | solution.py:325
  146.8 1.6 collective-permute-start.19
  149.2 19.9 %collective-permute-done.14.refs_5_ = bf16[512,768]{1,0:T(8,128)(2,1)S(1)} collective-permute-done((bf16[512,768]{1,0:T(8,128)(2,1)}, bf16[512,768]{1,0:T(8,128)(2,1)S(1)}, u32[]{:S(2)}, u32[]{:S(2)}) %collective-permute-start.14) | collective-permute-done | bytes 786464 | tf_op jit(solution)/shard_map/ppermute | solution.py:478
  170.0 5.9 %rest_products.1 = (bf16[256,384]{1,0:T(8,128)(2,1)}, bf16[256,384]{1,0:T(8,128)(2,1)}, bf16[256,384]{1,0:T(8,128)(2,1)}, bf16[256,384]{1,0:T(8,128)(2,1)}) custom-call(s32[7]{0:T(128)} %stack.105.meta_ref, bf16[256,4096]{1,0:T(8,128)(2,1)} %masked_half.2.refs_0_, bf16[256,4096]{1,0:T(8,128)(2,1)} %masked_half.3.refs_1_, ...), custom_call_target="tpu_custom_call" | custom-call | flops 805306368 | bytes 5242880 | tf_op jit(solution)/shard_map/rest_products/pallas_call | solution.py:389
  176.0 1.6 collective-permute-start.17
  178.2 2.0 %assembled.2.refs_4_ = bf16[256,4096]{1,0:T(8,128)(2,1)} custom-call(s32[2]{0:T(128)S(1)} %get-tuple-element.68.place_ref, f32[4,1,4096]{2,1,0:T(1,128)S(1)} %reshape.14.mask_ref, bf16[256,640]{1,0:T(8,128)(2,1)S(1)} %copy-done, bf16[256,640]{1,0:T(8,128)(2,1)S(1)} %collective-permute-done.15.refs_1_, bf16[256,640]{1,0:T(8,128)(2,1)S(1)} %collective-permute-done.19.refs_2_, ...), custom_call_target="tpu_custom_call" | custom-call | flops 1000 | bytes 655360 | tf_op jit(solution)/shard_map/assembled/pallas_call | solution.py:436
  180.2 3.8 %collective-permute-done.17.refs_2_ = bf16[256,384]{1,0:T(8,128)(2,1)S(1)} collective-permute-done((bf16[256,384]{1,0:T(8,128)(2,1)}, bf16[256,384]{1,0:T(8,128)(2,1)S(1)}, u32[]{:S(2)}, u32[]{:S(2)}) %collective-permute-start.17) | collective-permute-done | bytes 196640 | tf_op jit(solution)/shard_map/ppermute | solution.py:478
  184.0 3.3 %collective-permute-done.18.refs_3_ = bf16[256,384]{1,0:T(8,128)(2,1)S(1)} collective-permute-done((bf16[256,384]{1,0:T(8,128)(2,1)}, bf16[256,384]{1,0:T(8,128)(2,1)S(1)}, u32[]{:S(2)}, u32[]{:S(2)}) %collective-permute-start.18) | collective-permute-done | bytes 196640 | tf_op jit(solution)/shard_map/ppermute | solution.py:538
  187.3 1.6 assembled.3
  (66 shorter events, 17.9 us)
Async XLA Ops:
  0.6 9.4 %copy-start.10 = (s32[8,64]{1,0:T(8,128)S(1)}, s32[8,64]{1,0:T(8,128)}, u32[]{:S(2)}) copy-start(s32[8,64]{1,0:T(8,128)} %param.6) | copy-start | bytes 6148
  4.6 26.5 %collective-permute-start.1 = (bf16[512,1024]{1,0:T(8,128)(2,1)}, bf16[512,1024]{1,0:T(8,128)(2,1)S(1)}, u32[]{:S(2)}, u32[]{:S(2)}) collective-permute-start(bf16[512,1024]{1,0:T(8,128)(2,1)} %get-tuple-element.34.refs_4_), channel_id=1, source_target_pairs={{0,4},{2,6},{4,0},{6,2},{8,12},{10,14},{12,8},{14,10},{1,5},{3,7},... | collective-permute-start | bytes 3145736 | tf_op jit(solution)/shard_map/ppermute | solution.py:478
  7.7 23.4 %collective-permute-start.2 = (bf16[512,1024]{1,0:T(8,128)(2,1)}, bf16[512,1024]{1,0:T(8,128)(2,1)S(1)}, u32[]{:S(2)}, u32[]{:S(2)}) collective-permute-start(bf16[512,1024]{1,0:T(8,128)(2,1)} %get-tuple-element.34.refs_4_), channel_id=1, source_target_pairs={{4,8},{6,10},{8,4},{10,6},{5,9},{7,11},{9,5},{11,7},{20,24},{22,26... | collective-permute-start | bytes 3145736 | tf_op jit(solution)/shard_map/ppermute | solution.py:478
  8.4 25.0 %collective-permute-start = (bf16[512,1024]{1,0:T(8,128)(2,1)}, bf16[512,1024]{1,0:T(8,128)(2,1)}, u32[]{:S(2)}, u32[]{:S(2)}) collective-permute-start(bf16[512,1024]{1,0:T(8,128)(2,1)} %get-tuple-element.33), channel_id=1, source_target_pairs={{0,2},{2,0},{4,6},{6,4},{8,10},{10,8},{12,14},{14,12},{1,3},{3,1},... | collective-permute-start | bytes 3145736 | tf_op jit(solution)/shard_map/ppermute | solution.py:478
  31.1 11.0 %copy-start.6 = (bf16[512,1024]{1,0:T(8,128)(2,1)}, bf16[512,1024]{1,0:T(8,128)(2,1)S(1)}, u32[]{:S(2)}) copy-start(bf16[512,1024]{1,0:T(8,128)(2,1)S(1)} %collective-permute-done.1.refs_8_.refs_10_) | copy-start | bytes 3145732
  31.1 29.5 %copy-start.5 = (bf16[512,1024]{1,0:T(8,128)(2,1)}, bf16[512,1024]{1,0:T(8,128)(2,1)S(1)}, u32[]{:S(2)}) copy-start(bf16[512,1024]{1,0:T(8,128)(2,1)S(1)} %collective-permute-done.2.refs_6_) | copy-start | bytes 3145732
  33.5 27.2 %collective-permute-start.4 = (bf16[512,1024]{1,0:T(8,128)(2,1)}, bf16[512,1024]{1,0:T(8,128)(2,1)}, u32[]{:S(2)}, u32[]{:S(2)}) collective-permute-start(bf16[512,1024]{1,0:T(8,128)(2,1)} %collective-permute-done.refs_5_), channel_id=1, source_target_pairs={{0,4},{2,6},{12,8},{14,10},{1,5},{3,7},{13,9},{15,11},{16,20},{18,... | collective-permute-start | bytes 3145736 | tf_op jit(solution)/shard_map/ppermute | solution.py:478
  40.4 20.2 %collective-permute-start.5 = (bf16[512,1024]{1,0:T(8,128)(2,1)}, bf16[512,1024]{1,0:T(8,128)(2,1)}, u32[]{:S(2)}, u32[]{:S(2)}) collective-permute-start(bf16[512,1024]{1,0:T(8,128)(2,1)} %collective-permute-done.refs_5_), channel_id=1, source_target_pairs={{4,8},{6,10},{8,4},{10,6},{5,9},{7,11},{9,5},{11,7},{20,24},{22,26... | collective-permute-start | bytes 3145736 | tf_op jit(solution)/shard_map/ppermute | solution.py:478
  43.3 2.7 %copy-start.2 = (bf16[256,4096]{1,0:T(8,128)(2,1)S(1)}, bf16[256,4096]{1,0:T(8,128)(2,1)}, u32[]{:S(2)}) copy-start(bf16[256,4096]{1,0:T(8,128)(2,1)} %masked_half.2.refs_0_) | copy-start | bytes 6291460
  44.7 39.5 %collective-permute-start.7 = (bf16[512,1536]{1,0:T(8,128)(2,1)}, bf16[512,1536]{1,0:T(8,128)(2,1)}, u32[]{:S(2)}, u32[]{:S(2)}) collective-permute-start(bf16[512,1536]{1,0:T(8,128)(2,1)} %pad_maximum_fusion), channel_id=1, source_target_pairs={{4,0},{6,2},{8,12},{10,14},{5,1},{7,3},{9,13},{11,15},{20,16},{22,... | collective-permute-start | bytes 4718600 | tf_op jit(solution)/shard_map/ppermute | solution.py:478
  46.0 57.6 %collective-permute-start.3 = (bf16[256,4096]{1,0:T(8,128)(2,1)S(1)}, bf16[256,4096]{1,0:T(8,128)(2,1)}, u32[]{:S(2)}, u32[]{:S(2)}) collective-permute-start(bf16[256,4096]{1,0:T(8,128)(2,1)S(1)} %copy-done.2), channel_id=1, source_target_pairs={{0,2},{2,0},{4,6},{6,4},{8,10},{10,8},{12,14},{14,12},{1,3},{3,1},... | collective-permute-start | bytes 6291464 | tf_op jit(solution)/shard_map/ppermute | solution.py:478
  48.9 15.4 %collective-permute-start.8 = (bf16[512,512]{1,0:T(8,128)(2,1)S(1)}, bf16[512,512]{1,0:T(8,128)(2,1)S(1)}, u32[]{:S(2)}, u32[]{:S(2)}) collective-permute-start(bf16[512,512]{1,0:T(8,128)(2,1)S(1)} %get-tuple-element.64), channel_id=1, source_target_pairs={{4,8},{6,10},{8,4},{10,6},{5,9},{7,11},{9,5},{11,7},{20,24},{22,26... | collective-permute-start | bytes 1572872 | tf_op jit(solution)/shard_map/ppermute | solution.py:478
  63.0 40.7 %collective-permute-start.6 = (bf16[512,1024]{1,0:T(8,128)(2,1)S(1)}, bf16[512,1024]{1,0:T(8,128)(2,1)S(1)}, u32[]{:S(2)}, u32[]{:S(2)}) collective-permute-start(bf16[512,1024]{1,0:T(8,128)(2,1)S(1)} %pad_maximum_fusion.1), channel_id=1, source_target_pairs={{4,0},{6,2},{8,12},{10,14},{5,1},{7,3},{9,13},{11,15},{20,16},{22,... | collective-permute-start | bytes 3145736 | tf_op jit(solution)/shard_map/ppermute | solution.py:478
  64.3 41.5 %copy-start.8 = (bf16[512,512]{1,0:T(8,128)(2,1)}, bf16[512,512]{1,0:T(8,128)(2,1)S(1)}, u32[]{:S(2)}) copy-start(bf16[512,512]{1,0:T(8,128)(2,1)S(1)} %collective-permute-done.8.refs_5_) | copy-start | bytes 1572868
  85.5 18.1 %collective-permute-start.9 = (bf16[512,512]{1,0:T(8,128)(2,1)S(1)}, bf16[512,512]{1,0:T(8,128)(2,1)}, u32[]{:S(2)}, u32[]{:S(2)}) collective-permute-start(bf16[512,512]{1,0:T(8,128)(2,1)S(1)} %get-tuple-element.66), channel_id=1, source_target_pairs={{4,8},{6,10},{8,4},{10,6},{5,9},{7,11},{9,5},{11,7},{20,24},{22,26... | collective-permute-start | bytes 1572872 | tf_op jit(solution)/shard_map/ppermute | solution.py:478
  103.7 1.0 copy-start.12
  104.6 10.3 %collective-permute-start.10 = (bf16[256,4096]{1,0:T(8,128)(2,1)}, bf16[256,4096]{1,0:T(8,128)(2,1)S(1)}, u32[]{:S(2)}, u32[]{:S(2)}) collective-permute-start(bf16[256,4096]{1,0:T(8,128)(2,1)} %collective-permute-done.3.refs_2_), channel_id=1, source_target_pairs={{0,1},{1,0},{2,3},{3,2},{4,5},{5,4},{6,7},{7,6},{8,9},{9,8},{10,11... | collective-permute-start | bytes 6291464 | tf_op jit(solution)/shard_map/ppermute | solution.py:513
  105.8 7.9 %collective-permute-start.11 = (bf16[512,1024]{1,0:T(8,128)(2,1)}, bf16[512,1024]{1,0:T(8,128)(2,1)S(1)}, u32[]{:S(2)}, u32[]{:S(2)}) collective-permute-start(bf16[512,1024]{1,0:T(8,128)(2,1)} %pad_maximum_fusion.2), channel_id=1, source_target_pairs={{4,8},{6,10},{8,4},{10,6},{5,9},{7,11},{9,5},{11,7},{20,24},{22,26... | collective-permute-start | bytes 3145736 | tf_op jit(solution)/shard_map/ppermute | solution.py:478
  111.1 19.1 %collective-permute-start.12 = (bf16[512,512]{1,0:T(8,128)(2,1)}, bf16[512,512]{1,0:T(8,128)(2,1)S(1)}, u32[]{:S(2)}, u32[]{:S(2)}) collective-permute-start(bf16[512,512]{1,0:T(8,128)(2,1)} %copy-done.8), channel_id=1, source_target_pairs={{4,0},{6,2},{8,12},{10,14},{5,1},{7,3},{9,13},{11,15},{20,16},{22,... | collective-permute-start | bytes 1572872 | tf_op jit(solution)/shard_map/ppermute | solution.py:478
  112.4 26.5 %collective-permute-start.13 = (bf16[512,512]{1,0:T(8,128)(2,1)}, bf16[512,512]{1,0:T(8,128)(2,1)}, u32[]{:S(2)}, u32[]{:S(2)}) collective-permute-start(bf16[512,512]{1,0:T(8,128)(2,1)} %collective-permute-done.9.refs_6_), channel_id=1, source_target_pairs={{4,0},{6,2},{8,12},{10,14},{5,1},{7,3},{9,13},{11,15},{20,16},{22,... | collective-permute-start | bytes 1572872 | tf_op jit(solution)/shard_map/ppermute | solution.py:478
  113.7 16.5 %copy-start.4 = (bf16[512,1024]{1,0:T(8,128)(2,1)}, bf16[512,1024]{1,0:T(8,128)(2,1)S(1)}, u32[]{:S(2)}) copy-start(bf16[512,1024]{1,0:T(8,128)(2,1)S(1)} %collective-permute-done.11.refs_9_) | copy-start | bytes 3145732
  115.0 1.4 copy-start.3
  131.1 38.1 %collective-permute-start.14 = (bf16[512,768]{1,0:T(8,128)(2,1)}, bf16[512,768]{1,0:T(8,128)(2,1)S(1)}, u32[]{:S(2)}, u32[]{:S(2)}) collective-permute-start(bf16[512,768]{1,0:T(8,128)(2,1)} %pad_maximum_fusion.3), channel_id=1, source_target_pairs={{4,0},{6,2},{8,12},{10,14},{5,1},{7,3},{9,13},{11,15},{20,16},{22,... | collective-permute-start | bytes 2359304 | tf_op jit(solution)/shard_map/ppermute | solution.py:478
  146.7 2.5 %collective-permute-start.15 = (bf16[256,640]{1,0:T(8,128)(2,1)}, bf16[256,640]{1,0:T(8,128)(2,1)S(1)}, u32[]{:S(2)}, u32[]{:S(2)}) collective-permute-start(bf16[256,640]{1,0:T(8,128)(2,1)} %get-tuple-element.51), channel_id=1, source_target_pairs={{0,1},{1,0},{2,3},{3,2},{4,5},{5,4},{6,7},{7,6},{8,9},{9,8},{10,11... | collective-permute-start | bytes 983048 | tf_op jit(solution)/shard_map/ppermute | solution.py:536
  146.8 31.4 %collective-permute-start.19 = (bf16[256,640]{1,0:T(8,128)(2,1)}, bf16[256,640]{1,0:T(8,128)(2,1)S(1)}, u32[]{:S(2)}, u32[]{:S(2)}) collective-permute-start(bf16[256,640]{1,0:T(8,128)(2,1)} %get-tuple-element.59), channel_id=1, source_target_pairs={{0,2},{2,0},{4,6},{6,4},{8,10},{10,8},{12,14},{14,12},{1,3},{3,1},... | collective-permute-start | bytes 983048 | tf_op jit(solution)/shard_map/ppermute | solution.py:478
  148.4 29.8 %collective-permute-start.20 = (bf16[256,640]{1,0:T(8,128)(2,1)}, bf16[256,640]{1,0:T(8,128)(2,1)S(1)}, u32[]{:S(2)}, u32[]{:S(2)}) collective-permute-start(bf16[256,640]{1,0:T(8,128)(2,1)} %get-tuple-element.60), channel_id=1, source_target_pairs={{0,3},{1,2},{2,1},{3,0},{4,7},{5,6},{6,5},{7,4},{8,11},{9,10},{10,... | collective-permute-start | bytes 983048 | tf_op jit(solution)/shard_map/ppermute | solution.py:538
  170.0 7.8 %copy-start.11 = (s32[4,64]{1,0:T(4,128)S(1)}, s32[4,64]{1,0:T(4,128)}, u32[]{:S(2)}) copy-start(s32[4,64]{1,0:T(4,128)} %param.7) | copy-start | bytes 3076
  170.0 8.2 %copy-start = (bf16[256,640]{1,0:T(8,128)(2,1)S(1)}, bf16[256,640]{1,0:T(8,128)(2,1)}, u32[]{:S(2)}) copy-start(bf16[256,640]{1,0:T(8,128)(2,1)} %get-tuple-element.57.refs_0_) | copy-start | bytes 983044
  175.9 11.4 %copy-start.1 = (bf16[256,384]{1,0:T(8,128)(2,1)S(1)}, bf16[256,384]{1,0:T(8,128)(2,1)}, u32[]{:S(2)}) copy-start(bf16[256,384]{1,0:T(8,128)(2,1)} %get-tuple-element.53.refs_0_) | copy-start | bytes 589828
  175.9 4.3 %collective-permute-start.16 = (bf16[256,384]{1,0:T(8,128)(2,1)}, bf16[256,384]{1,0:T(8,128)(2,1)S(1)}, u32[]{:S(2)}, u32[]{:S(2)}) collective-permute-start(bf16[256,384]{1,0:T(8,128)(2,1)} %get-tuple-element.54), channel_id=1, source_target_pairs={{0,1},{1,0},{2,3},{3,2},{4,5},{5,4},{6,7},{7,6},{8,9},{9,8},{10,11... | collective-permute-start | bytes 589832 | tf_op jit(solution)/shard_map/ppermute | solution.py:536
  176.0 8.0 %collective-permute-start.17 = (bf16[256,384]{1,0:T(8,128)(2,1)}, bf16[256,384]{1,0:T(8,128)(2,1)S(1)}, u32[]{:S(2)}, u32[]{:S(2)}) collective-permute-start(bf16[256,384]{1,0:T(8,128)(2,1)} %get-tuple-element.55), channel_id=1, source_target_pairs={{0,2},{2,0},{4,6},{6,4},{8,10},{10,8},{12,14},{14,12},{1,3},{3,1},... | collective-permute-start | bytes 589832 | tf_op jit(solution)/shard_map/ppermute | solution.py:478
  177.6 9.7 %collective-permute-start.18 = (bf16[256,384]{1,0:T(8,128)(2,1)}, bf16[256,384]{1,0:T(8,128)(2,1)S(1)}, u32[]{:S(2)}, u32[]{:S(2)}) collective-permute-start(bf16[256,384]{1,0:T(8,128)(2,1)} %get-tuple-element.56), channel_id=1, source_target_pairs={{0,3},{1,2},{2,1},{3,0},{4,7},{5,6},{6,5},{7,4},{8,11},{9,10},{10,... | collective-permute-start | bytes 589832 | tf_op jit(solution)/shard_map/ppermute | solution.py:538
  (2 other events, 1.7 us)

commit v5 on v4

--- a/solution.py
+++ b/solution.py
@@ -9,6 +9,7 @@
 
 LANES = 128
 MIB = 1 << 20
+SMALL = pl.CostEstimate(flops=1000, bytes_accessed=1000, transcendentals=0)
 
 
 def shifted(shard, axis, by):
@@ -87,9 +88,7 @@
         out_specs=[pl.BlockSpec(memory_space=pltpu.VMEM)] * n,
         scratch_shapes=[pltpu.VMEM((n, *shape), jnp.bfloat16), pltpu.SemaphoreType.DMA((n, band))],
         compiler_params=pltpu.CompilerParams(vmem_limit_bytes=56 * MIB),
-        cost_estimate=pl.CostEstimate(
-            flops=1000, bytes_accessed=4 * n * shape[0] * shape[1], transcendentals=0
-        ),
+        cost_estimate=SMALL,
         name="b_strips",
     )(jnp.stack(quarters), w_band)
 
@@ -115,7 +114,7 @@
         ),
         out_shape=jax.ShapeDtypeStruct((x_band.shape[0] // 2, cols), jnp.bfloat16),
         compiler_params=pltpu.CompilerParams(vmem_limit_bytes=58 * MIB),
-        cost_estimate=pl.CostEstimate(flops=1000, bytes_accessed=2 * x_band.shape[0] * cols, transcendentals=0),
+        cost_estimate=SMALL,
         name="masked_half",
     )(half.reshape(1), mask_wide, x_band)
 
@@ -145,65 +144,64 @@
     lax.fori_loop(0, 2, step, 0)
 
 
-def first_kernel(meta_ref, *refs):
-    x_refs, middle_refs, (near_a_ref, near_b_ref, mid_b_ref), refs = refs[:4], refs[4:10], refs[10:13], refs[13:]
-    out_ref, xv, bv, acc, x_sems, b_sems, out_sems = refs
-    n_b = len(middle_refs)
+def whole_kernel(plan, has_prev, meta_ref, *refs):
+    n_b = len(plan)
+    x_refs, refs = refs[:4], refs[4:]
+    prev_ref, refs = (refs[0], refs[1:]) if has_prev else (None, refs)
+    b_refs, (out_ref, xv, bv, acc, x_sems, b_sems, out_sems) = refs[:-7], refs[-7:]
     quarter = bv.shape[2]
     low = quarter // 2
-    near = quarter - LANES
-    split = quarter - (near_b_ref.shape[1] - near)
     is_end = meta_ref[0]
 
     def offset_of(p, g):
         return meta_ref[3 + 2 * p + g]
 
     def b_middle(p):
-        return [pltpu.make_async_copy(middle_refs[p], bv.at[p], b_sems.at[p])]
+        return [pltpu.make_async_copy(b_refs[plan[p][0]], bv.at[p], b_sems.at[p, 0])]
 
     def b_end(p):
-        if p < 2:
-            return b_middle(p)
-        if p == 2:
-            return [pltpu.make_async_copy(near_a_ref, bv.at[2], b_sems.at[2])]
-        if p == 3:
-            at = pl.multiple_of(meta_ref[2] * LANES, LANES)
-            return [pltpu.make_async_copy(near_b_ref.at[:, :near], bv.at[3, :, pl.ds(at, near)], b_sems.at[3])]
-        if p == 4:
-            return [
-                pltpu.make_async_copy(near_b_ref.at[:, near:], bv.at[4, :, split:], b_sems.at[4]),
-                pltpu.make_async_copy(mid_b_ref.at[:, :split], bv.at[4 + meta_ref[1], :, :split], b_sems.at[6]),
-            ]
-        return [pltpu.make_async_copy(mid_b_ref.at[:, split:], bv.at[5, :, split:], b_sems.at[5])]
-
-    copies = x_copies(x_refs, xv, x_sems, offset_of)
-    for p in range(n_b):
-
+        copies = []
+        for k, (operand, first, count, at, to) in enumerate(plan[p][1]):
+            at = pl.multiple_of(meta_ref[2] * LANES, LANES) if at is None else at * LANES
+            to = meta_ref[1] if to is None else to
+            source = b_refs[operand].at[:, first * LANES : (first + count) * LANES]
+            copies.append(pltpu.make_async_copy(source, bv.at[to, :, pl.ds(at, count * LANES)], b_sems.at[p, k]))
+        return copies
+
+    def on_each(p, do):
         @pl.when(is_end == 0)
         def _():
             for copy in b_middle(p):
-                copy.start()
+                do(copy)
 
         @pl.when(is_end != 0)
         def _():
             for copy in b_end(p):
-                copy.start()
-
+                do(copy)
+
+    prev_copies = [
+        pltpu.make_async_copy(prev_ref.at[g], acc.at[g, :, low : low + quarter], out_sems.at[g])
+        for g in range(2)
+        if has_prev
+    ]
+    copies = x_copies(x_refs, xv, x_sems, offset_of)
+    for p in range(n_b):
+        on_each(p, lambda copy: copy.start())
         for r in range(4):
             copies[p, r].start()
-    acc[...] = jnp.zeros_like(acc)
+        if p == 0:
+            for copy in prev_copies:
+                copy.start()
+    if has_prev:
+        for copy in prev_copies:
+            copy.wait()
+        for p in range(n_b):
+            on_each(p, lambda copy: copy.wait())
+    else:
+        acc[...] = jnp.zeros_like(acc)
     for p in range(n_b):
-
-        @pl.when(is_end == 0)
-        def _():
-            for copy in b_middle(p):
-                copy.wait()
-
-        @pl.when(is_end != 0)
-        def _():
-            for copy in b_end(p):
-                copy.wait()
-
+        if not has_prev:
+            on_each(p, lambda copy: copy.wait())
         for r in range(4):
             copies[p, r].wait()
         add_products(acc, xv, p, bv.at[p], offset_of, 0)
@@ -216,33 +214,30 @@
         out.wait()
 
 
-def first_products(meta, xs, middle, end):
+def whole_products(meta, xs, prev, operands, plan, name):
     rows = xs[0].shape[0]
-    panel, quarter = middle[0].shape
-    n_b = len(middle)
+    panel, quarter = operands[plan[0][0]].shape
+    n_b = len(plan)
     any_spec = pl.BlockSpec(memory_space=pl.ANY)
     x_spec = pl.BlockSpec(memory_space=pltpu.HBM)
+    operands = ([] if prev is None else [prev]) + operands
     return pl.pallas_call(
-        first_kernel,
+        functools.partial(whole_kernel, plan, prev is not None),
         out_shape=jax.ShapeDtypeStruct((2, 2 * rows, quarter), jnp.float32),
-        in_specs=[pl.BlockSpec(memory_space=pltpu.SMEM)] + [x_spec] * 4 + [any_spec] * (n_b + 3),
+        in_specs=[pl.BlockSpec(memory_space=pltpu.SMEM)] + [x_spec] * 4 + [any_spec] * len(operands),
         out_specs=any_spec,
         scratch_shapes=[
             pltpu.VMEM((n_b, 2, 2 * rows, panel), jnp.bfloat16),
             pltpu.VMEM((n_b, panel, quarter), jnp.bfloat16),
             pltpu.VMEM((2, 2 * rows, 2 * quarter), jnp.float32),
             pltpu.SemaphoreType.DMA((n_b, 4)),
-            pltpu.SemaphoreType.DMA((n_b + 1,)),
+            pltpu.SemaphoreType.DMA((n_b, 2)),
             pltpu.SemaphoreType.DMA((2,)),
         ],
         compiler_params=pltpu.CompilerParams(vmem_limit_bytes=59 * MIB),
-        cost_estimate=pl.CostEstimate(
-            flops=2 * n_b * 4 * rows * panel * quarter,
-            bytes_accessed=n_b * 2 * (4 * rows * panel + panel * quarter),
-            transcendentals=0,
-        ),
-        name="first_products",
-    )(meta, *xs, *middle, *end)
+        cost_estimate=SMALL,
+        name=name,
+    )(meta, *xs, *operands)
 
 
 def give_pieces(out_refs, acc, at):
@@ -338,9 +333,7 @@
             pltpu.SemaphoreType.DMA,
         ],
         compiler_params=pltpu.CompilerParams(vmem_limit_bytes=59 * MIB),
-        cost_estimate=pl.CostEstimate(
-            flops=2 * 2 * 4 * rows * panel * quarter, bytes_accessed=10 * MIB, transcendentals=0
-        ),
+        cost_estimate=SMALL,
         name="half_products",
     )(meta, *xs, prev, *middle, *end, second)
 
@@ -400,9 +393,7 @@
             pltpu.SemaphoreType.DMA,
         ],
         compiler_params=pltpu.CompilerParams(vmem_limit_bytes=59 * MIB),
-        cost_estimate=pl.CostEstimate(
-            flops=2 * 4 * rows * panel * b.shape[1], bytes_accessed=5 * MIB, transcendentals=0
-        ),
+        cost_estimate=SMALL,
         name="rest_products",
     )(meta, *xs, rest, b)
 
@@ -441,7 +432,7 @@
         scratch_shapes=[pltpu.VMEM((rows, width * len(pieces)), jnp.bfloat16), pltpu.SemaphoreType.DMA],
         input_output_aliases={} if out is None else {6: 0},
         compiler_params=pltpu.CompilerParams(vmem_limit_bytes=16 * MIB),
-        cost_estimate=pl.CostEstimate(flops=1000, bytes_accessed=4 * rows * width, transcendentals=0),
+        cost_estimate=SMALL,
         name="assembled",
     )(*operands)
 
@@ -500,18 +491,18 @@
 
     fwd_a = line(strips(swap_a, first_out, 4), cross)
     in_b, cross_b = together(in_b, cross_b)
-    mid_b = line(
-        jnp.concatenate([jnp.where(y == 0, cross_a[:, : 3 * LANES], cross_b[:, : 3 * LANES]), cross_b[:, 3 * LANES :]], 1),
-        outward,
+    mid_b = jnp.concatenate(
+        [jnp.where(y == 0, cross_a[:, : 3 * LANES], cross_b[:, : 3 * LANES]), cross_b[:, 3 * LANES :]], 1
     )
-    in_b, near_b, fwd_a = together(in_b, near_b, fwd_a)
-    fwd_b = line(strips(in_b, first_out, 4), cross)
-    fwd_second = line(jnp.concatenate([strips(v, second_out, 4) for v in (swap_a, in_b)], 1), cross)
-    far_a = line(fwd_a, outward)
-    x_across, mid_b, fwd_b = together(x_across, mid_b, fwd_b)
-    far_b = line(fwd_b, outward)
+    fwd_b = strips(in_b, first_out, 4)
+    fwd_second = jnp.concatenate([strips(v, second_out, 4) for v in (swap_a, in_b)], 1)
+    near_b, fwd_a, x_across, mid_b, fwd_b, fwd_second = together(near_b, fwd_a, x_across, mid_b, fwd_b, fwd_second)
+    mid_b = line(mid_b, outward)
     x_opposite = lax.ppermute(x_across, "depth", layers)
     xs = [x_mine, x_rest, x_across, x_opposite]
+    fwd_b = line(fwd_b, cross)
+    fwd_second = line(fwd_second, cross)
+    far_a = line(fwd_a, outward)
 
     def offsets(delta):
         tilt = 2 * y - 1
@@ -520,14 +511,21 @@
     zero = jnp.zeros_like(z)
     third = offsets(jnp.where(is_end == 1, 2, -toward))
     fourth = offsets(jnp.where(is_end == 1, -toward, 2))
-    meta = jnp.stack([is_end, y, start_near, *offsets(zero), *offsets(toward), *third]).astype(jnp.int32)
-    total = first_products(
-        meta, xs, [own_a, own_b, cross_a, cross_b, swap_a, in_b], [swap_a, near_b, mid_b]
+    zero = zero.astype(jnp.int32)
+    meta = jnp.stack([is_end, zero, start_near, *offsets(zero), *offsets(toward)]).astype(jnp.int32)
+    whole = lambda operand, p: (operand, [(operand, 0, 8, 0, p)])
+    plan = [whole(0, 0), whole(1, 1), (2, [(4, 0, 8, 0, 2)]), (3, [(5, 0, 7, None, 3)])]
+    total = whole_products(meta, xs, None, [own_a, own_b, cross_a, cross_b, swap_a, near_b], plan, "first_products")
+    last_at = jnp.where(left, 1, 0)
+    mid_b, fwd_b, total, last_at = together(mid_b, fwd_b, total, last_at)
+    far_b = line(fwd_b, outward)
+    meta = jnp.stack([is_end, y, zero, *third]).astype(jnp.int32)
+    plan = [(0, [(2, 7, 5, 3, 0), (3, 0, 3, 0, None)]), (1, [(3, 3, 5, 3, 1)])]
+    total = whole_products(meta, xs, total, [swap_a, in_b, near_b, mid_b], plan, "next_products")
+    last = jnp.concatenate(
+        [strips(fwd_second, last_at, 3), strips(fwd_second, last_at + 4, 3)], 1
     )
-    last = jnp.concatenate(
-        [strips(fwd_second, jnp.where(left, 1, 0), 3), strips(fwd_second, jnp.where(left, 5, 4), 3)], 1
-    )
-    last, total, far_a = together(last, total, far_a)
+    last, far_a = together(last, far_a)
     far_second = line(last, outward)
 
     def exchanged(pieces):

time: 190 us -> 177 us (0.932)
  waiting for transfers between devices: 99 us -> 81.7 us
  Pallas kernels: 43.1 us -> 48.8 us
    ppermute x16, waiting for transfers between devices: 95.7 us -> 76.5 us  [line(): return lax.ppermute(value, 'grid', pairs)]
    pallas_call x1 -> x2, Pallas kernels: 13.9 us -> 19.6 us  [whole_products(): pl.pallas_call(functools.partial(whole_kernel, plan, prev is not None), o...]
    unnamed x26 -> x18, local copies, waits for them, and re-layouts: 4.09 us -> 0.82 us
    concatenate x2 -> x1, other arithmetic: 2.25 us -> 0.07 us  [pairs_in_line(): jnp.concatenate([strips(fwd_second, last_at, 3), strips(fwd_second, last_...]
  transfers between devices with their start and end apart: 21 -> 21, of which waited for: 9 -> 11; matrix products, arithmetic and copies ran while one was open for 7% -> 8% of each run, Pallas kernels for 20% -> 25%
where the time goes in v5:
time: 177 us; the launch traced here: 176 us
  waiting for transfers between devices  81.7 us (46%)
  Pallas kernels  48.8 us (28%)
  starting transfers between devices  30.1 us (17%)
  local copies, waits for them, and re-layouts  10.4 us (6%)
  other arithmetic  4.88 us (3%)
    ppermute x16, waiting for transfers between devices, line(): return lax.ppermute(value, 'grid', pairs)  76.5 us
    ppermute x16, starting transfers between devices, line(): return lax.ppermute(value, 'grid', pairs)  29.4 us
    pallas_call x2, Pallas kernels, whole_products(): pl.pallas_call(functools.partial(whole_kernel, plan, prev is not None), o...  19.6 us
    pallas_call x2, Pallas kernels, masked_half(): pl.pallas_call(mask_kernel, grid_spec=pltpu.PrefetchScalarGridSpec(num_sc...  7.9 us
    pallas_call x1, Pallas kernels, half_products(): pl.pallas_call(half_kernel, out_shape=[jax.ShapeDtypeStruct((rows, n_done...  7.82 us
    pallas_call x1, Pallas kernels, rest_products(): pl.pallas_call(rest_kernel, out_shape=[jax.ShapeDtypeStruct((rows, width)...  5.85 us
    ppermute x2, waiting for transfers between devices, exchanged(): lax.ppermute(pieces[3], ('grid', 'depth'), opposite)  5.19 us
    pallas_call x1, Pallas kernels, b_strips(): pl.pallas_call(strips_kernel, out_shape=[jax.ShapeDtypeStruct(shape, jnp....  3.95 us
  transfers between devices with their start and end apart: 21, of which 11 were waited for; matrix products, arithmetic and copies ran while one was open for 8% of the time, Pallas kernels for 25%

profile of v5, /device:TPU:0, one launch (start us, length us, event | category | flops | bytes accessed | tf_op | source)
XLA Modules:
  0.0 176.2 jit_solution(9726636891577062183)
XLA Ops:
  0.6 3.9 %b_strips.1 = (bf16[512,1024]{1,0:T(8,128)(2,1)}, bf16[512,1024]{1,0:T(8,128)(2,1)}) custom-call(s32[2]{0:T(128)} %pad_add_fusion.1.quarters_ref, bf16[512,4096]{1,0:T(8,128)(2,1)} %w_ref.1), custom_call_target="tpu_custom_call" | custom-call | flops 1000 | bytes 1000 | tf_op jit(solution)/shard_map/b_strips/pallas_call | solution.py:81
  4.6 3.0 %collective-permute-start = (bf16[512,1024]{1,0:T(8,128)(2,1)}, bf16[512,1024]{1,0:T(8,128)(2,1)S(1)}, u32[]{:S(2)}, u32[]{:S(2)}) collective-permute-start(bf16[512,1024]{1,0:T(8,128)(2,1)} %get-tuple-element.36), channel_id=1, source_target_pairs={{0,2},{2,0},{4,6},{6,4},{8,10},{10,8},{12,14},{14,12},{1,3},{3,1},... | collective-permute-start | bytes 3145736 | tf_op jit(solution)/shard_map/ppermute | solution.py:469
  7.6 1.6 collective-permute-start.1
  9.2 1.7 collective-permute-start.2
  11.8 3.9 %masked_half.2.refs_0_ = bf16[256,4096]{1,0:T(8,128)(2,1)} custom-call(s32[1]{0:T(128)} %bitcast.8.half_ref, f32[8,1,4096]{2,1,0:T(1,128)} %reshape.16.mask_ref, bf16[512,4096]{1,0:T(8,128)(2,1)} %x_ref.3), custom_call_target="tpu_custom_call" | custom-call | flops 1000 | bytes 1000 | tf_op jit(solution)/shard_map/masked_half/pallas_call | solution.py:104
  15.7 15.2 %collective-permute-done.refs_5_ = bf16[512,1024]{1,0:T(8,128)(2,1)S(1)} collective-permute-done((bf16[512,1024]{1,0:T(8,128)(2,1)}, bf16[512,1024]{1,0:T(8,128)(2,1)S(1)}, u32[]{:S(2)}, u32[]{:S(2)}) %collective-permute-start) | collective-permute-done | bytes 1048608 | tf_op jit(solution)/shard_map/ppermute | solution.py:469
  31.0 1.5 collective-permute-done.1.refs_8_.refs_5_
  33.7 6.9 %collective-permute-start.6 = (bf16[512,1024]{1,0:T(8,128)(2,1)}, bf16[512,1024]{1,0:T(8,128)(2,1)}, u32[]{:S(2)}, u32[]{:S(2)}) collective-permute-start(bf16[512,1024]{1,0:T(8,128)(2,1)} %copy-done.4), channel_id=1, source_target_pairs={{0,4},{2,6},{12,8},{14,10},{1,5},{3,7},{13,9},{15,11},{16,20},{18,... | collective-permute-start | bytes 3145736 | tf_op jit(solution)/shard_map/ppermute | solution.py:469
  40.6 1.7 collective-permute-start.7
  44.7 1.3 pad_maximum_fusion
  47.4 1.5 collective-permute-start.4
  48.9 11.9 %collective-permute-done.6.refs_6_ = bf16[512,1024]{1,0:T(8,128)(2,1)} collective-permute-done((bf16[512,1024]{1,0:T(8,128)(2,1)}, bf16[512,1024]{1,0:T(8,128)(2,1)}, u32[]{:S(2)}, u32[]{:S(2)}) %collective-permute-start.6) | collective-permute-done | bytes 1048608 | tf_op jit(solution)/shard_map/ppermute | solution.py:469
  61.9 2.1 %constant_dynamic-slice_fusion.2 = (bf16[512,512]{1,0:T(8,128)(2,1)S(1)}, bf16[512,512]{1,0:T(8,128)(2,1)}) fusion(bf16[512,1024]{1,0:T(8,128)(2,1)} %collective-permute-done.6.refs_6_, s32[]{:T(128)S(6)} %select_n.142, s32[]{:T(128)S(6)} %select_n.138), kind=kLoop, calls=%fused_computation.7 | loop fusion | bytes 2097160 | tf_op jit(solution)/shard_map/dynamic_slice | solution.py:472
  65.2 1.7 pad_maximum_fusion.1
  66.8 15.8 %collective-permute-done.3.refs_9_.refs_7_ = bf16[512,1536]{1,0:T(8,128)(2,1)} collective-permute-done((bf16[512,1536]{1,0:T(8,128)(2,1)}, bf16[512,1536]{1,0:T(8,128)(2,1)}, u32[]{:S(2)}, u32[]{:S(2)}) %collective-permute-start.3) | collective-permute-done | bytes 1572896 | tf_op jit(solution)/shard_map/ppermute | solution.py:469
  84.6 1.5 collective-permute-start.10
  87.4 4.0 %masked_half.3.refs_1_ = bf16[256,4096]{1,0:T(8,128)(2,1)} custom-call(s32[1]{0:T(128)} %bitcast.9.half_ref, f32[8,1,4096]{2,1,0:T(1,128)} %reshape.16.mask_ref, bf16[512,4096]{1,0:T(8,128)(2,1)} %x_ref.3), custom_call_target="tpu_custom_call" | custom-call | flops 1000 | bytes 1000 | tf_op jit(solution)/shard_map/masked_half/pallas_call | solution.py:104
  92.1 10.7 %first_products.1.refs_4_ = f32[2,512,1024]{2,1,0:T(8,128)} custom-call(s32[11]{0:T(128)} %stack.127.meta_ref, bf16[256,4096]{1,0:T(8,128)(2,1)} %masked_half.2.refs_0_, bf16[256,4096]{1,0:T(8,128)(2,1)} %masked_half.3.refs_1_, bf16[256,4096]{1,0:T(8,128)(2,1)} %copy-done.2, bf16[256,4096]{1,0:T(8,128)(2,1)} %collective-permute-done.8.refs_3_, ...), custom_call_target="tpu_custom_call" | custom-call | flops 1000 | bytes 1000 | tf_op jit(solution)/shard_map/first_products/pallas_call | solution.py:224
  102.7 8.0 %collective-permute-done.9.refs_8_ = bf16[512,1024]{1,0:T(8,128)(2,1)} collective-permute-done((bf16[512,1024]{1,0:T(8,128)(2,1)}, bf16[512,1024]{1,0:T(8,128)(2,1)}, u32[]{:S(2)}, u32[]{:S(2)}) %collective-permute-start.9) | collective-permute-done | bytes 1048608 | tf_op jit(solution)/shard_map/ppermute | solution.py:469
  112.3 9.3 %collective-permute-done.12.refs_7_ = bf16[512,512]{1,0:T(8,128)(2,1)} collective-permute-done((bf16[512,512]{1,0:T(8,128)(2,1)}, bf16[512,512]{1,0:T(8,128)(2,1)}, u32[]{:S(2)}, u32[]{:S(2)}) %collective-permute-start.12) | collective-permute-done | bytes 524320 | tf_op jit(solution)/shard_map/ppermute | solution.py:469
  124.3 9.0 %next_products.1.refs_4_ = f32[2,512,1024]{2,1,0:T(8,128)} custom-call(s32[7]{0:T(128)} %stack.120.meta_ref, bf16[256,4096]{1,0:T(8,128)(2,1)} %masked_half.2.refs_0_, bf16[256,4096]{1,0:T(8,128)(2,1)} %masked_half.3.refs_1_, bf16[256,4096]{1,0:T(8,128)(2,1)} %copy-done.2, bf16[256,4096]{1,0:T(8,128)(2,1)} %collective-permute-done.8.refs_3_, ...), custom_call_target="tpu_custom_call" | custom-call | flops 1000 | bytes 1000 | tf_op jit(solution)/shard_map/next_products/pallas_call | solution.py:224
  133.3 7.3 %collective-permute-done.13.refs_8_ = bf16[512,512]{1,0:T(8,128)(2,1)S(1)} collective-permute-done((bf16[512,512]{1,0:T(8,128)(2,1)}, bf16[512,512]{1,0:T(8,128)(2,1)S(1)}, u32[]{:S(2)}, u32[]{:S(2)}) %collective-permute-start.13) | collective-permute-done | bytes 524320 | tf_op jit(solution)/shard_map/ppermute | solution.py:469
  141.3 7.8 %half_products.1 = (bf16[256,640]{1,0:T(8,128)(2,1)}, bf16[256,640]{1,0:T(8,128)(2,1)}, bf16[256,640]{1,0:T(8,128)(2,1)}, bf16[256,640]{1,0:T(8,128)(2,1)}, f32[2,512,384]{2,1,0:T(8,128)}) custom-call(s32[9]{0:T(128)} %stack.115.meta_ref, bf16[256,4096]{1,0:T(8,128)(2,1)} %masked_half.2.refs_0_, bf16[256,4096]{1,0:T(8,128)(2,1)} %masked_half.3.refs_1_, ...), custom_call_target="tpu_custom_call" | custom-call | flops 1000 | bytes 1000 | tf_op jit(solution)/shard_map/half_products/pallas_call | solution.py:320
  149.2 1.6 collective-permute-start.19
  151.7 4.5 %collective-permute-done.14.refs_5_ = bf16[512,768]{1,0:T(8,128)(2,1)} collective-permute-done((bf16[512,768]{1,0:T(8,128)(2,1)S(1)}, bf16[512,768]{1,0:T(8,128)(2,1)}, u32[]{:S(2)}, u32[]{:S(2)}) %collective-permute-start.14) | collective-permute-done | bytes 786464 | tf_op jit(solution)/shard_map/ppermute | solution.py:469
  156.2 5.8 %rest_products.1 = (bf16[256,384]{1,0:T(8,128)(2,1)}, bf16[256,384]{1,0:T(8,128)(2,1)}, bf16[256,384]{1,0:T(8,128)(2,1)}, bf16[256,384]{1,0:T(8,128)(2,1)}) custom-call(s32[7]{0:T(128)} %stack.109.meta_ref, bf16[256,4096]{1,0:T(8,128)(2,1)} %masked_half.2.refs_0_, bf16[256,4096]{1,0:T(8,128)(2,1)} %masked_half.3.refs_1_, bf16[256,4096]{1,0:T(8,128)(2,1)} %copy-done.2, ...), custom_call_target="tpu_custom_call" | custom-call | flops 1000 | bytes 1000 | tf_op jit(solution)/shard_map/rest_products/pallas_call | solution.py:382
  162.1 1.6 collective-permute-start.17
  164.3 1.9 %collective-permute-done.20.refs_3_ = bf16[256,640]{1,0:T(8,128)(2,1)S(1)} collective-permute-done((bf16[256,640]{1,0:T(8,128)(2,1)}, bf16[256,640]{1,0:T(8,128)(2,1)S(1)}, u32[]{:S(2)}, u32[]{:S(2)}) %collective-permute-start.20) | collective-permute-done | bytes 327712 | tf_op jit(solution)/shard_map/ppermute | solution.py:536
  166.2 2.0 %assembled.2.refs_4_ = bf16[256,4096]{1,0:T(8,128)(2,1)} custom-call(s32[2]{0:T(128)S(1)} %get-tuple-element.74.place_ref, f32[4,1,4096]{2,1,0:T(1,128)S(1)} %reshape.14.mask_ref, bf16[256,640]{1,0:T(8,128)(2,1)S(1)} %copy-done, bf16[256,640]{1,0:T(8,128)(2,1)S(1)} %collective-permute-done.15.refs_1_, bf16[256,640]{1,0:T(8,128)(2,1)S(1)} %collective-permute-done.19.refs_2_, ...), custom_call_target="tpu_custom_call" | custom-call | flops 1000 | bytes 1000 | tf_op jit(solution)/shard_map/assembled/pallas_call | solution.py:427
  168.2 3.1 %collective-permute-done.17.refs_2_ = bf16[256,384]{1,0:T(8,128)(2,1)S(1)} collective-permute-done((bf16[256,384]{1,0:T(8,128)(2,1)}, bf16[256,384]{1,0:T(8,128)(2,1)S(1)}, u32[]{:S(2)}, u32[]{:S(2)}) %collective-permute-start.17) | collective-permute-done | bytes 196640 | tf_op jit(solution)/shard_map/ppermute | solution.py:469
  171.3 3.3 %collective-permute-done.18.refs_3_ = bf16[256,384]{1,0:T(8,128)(2,1)S(1)} collective-permute-done((bf16[256,384]{1,0:T(8,128)(2,1)}, bf16[256,384]{1,0:T(8,128)(2,1)S(1)}, u32[]{:S(2)}, u32[]{:S(2)}) %collective-permute-start.18) | collective-permute-done | bytes 196640 | tf_op jit(solution)/shard_map/ppermute | solution.py:536
  174.6 1.6 assembled.3
  (59 shorter events, 19.4 us)
Async XLA Ops:
  0.6 10.2 %copy-start.7 = (s32[8,64]{1,0:T(8,128)S(1)}, s32[8,64]{1,0:T(8,128)}, u32[]{:S(2)}) copy-start(s32[8,64]{1,0:T(8,128)} %param.6) | copy-start | bytes 6148
  4.6 26.4 %collective-permute-start = (bf16[512,1024]{1,0:T(8,128)(2,1)}, bf16[512,1024]{1,0:T(8,128)(2,1)S(1)}, u32[]{:S(2)}, u32[]{:S(2)}) collective-permute-start(bf16[512,1024]{1,0:T(8,128)(2,1)} %get-tuple-element.36), channel_id=1, source_target_pairs={{0,2},{2,0},{4,6},{6,4},{8,10},{10,8},{12,14},{14,12},{1,3},{3,1},... | collective-permute-start | bytes 3145736 | tf_op jit(solution)/shard_map/ppermute | solution.py:469
  7.6 24.8 %collective-permute-start.1 = (bf16[512,1024]{1,0:T(8,128)(2,1)}, bf16[512,1024]{1,0:T(8,128)(2,1)S(1)}, u32[]{:S(2)}, u32[]{:S(2)}) collective-permute-start(bf16[512,1024]{1,0:T(8,128)(2,1)} %get-tuple-element.37.refs_4_), channel_id=1, source_target_pairs={{0,4},{2,6},{4,0},{6,2},{8,12},{10,14},{12,8},{14,10},{1,5},{3,7},... | collective-permute-start | bytes 3145736 | tf_op jit(solution)/shard_map/ppermute | solution.py:469
  9.2 23.3 %collective-permute-start.2 = (bf16[512,1024]{1,0:T(8,128)(2,1)}, bf16[512,1024]{1,0:T(8,128)(2,1)}, u32[]{:S(2)}, u32[]{:S(2)}) collective-permute-start(bf16[512,1024]{1,0:T(8,128)(2,1)} %get-tuple-element.37.refs_4_), channel_id=1, source_target_pairs={{4,8},{6,10},{8,4},{10,6},{5,9},{7,11},{9,5},{11,7},{20,24},{22,26... | collective-permute-start | bytes 3145736 | tf_op jit(solution)/shard_map/ppermute | solution.py:469
  31.0 1.5 copy-start.4
  32.4 14.9 %copy-start.3 = (bf16[512,1024]{1,0:T(8,128)(2,1)}, bf16[512,1024]{1,0:T(8,128)(2,1)S(1)}, u32[]{:S(2)}) copy-start(bf16[512,1024]{1,0:T(8,128)(2,1)S(1)} %collective-permute-done.1.refs_8_.refs_5_) | copy-start | bytes 3145732
  32.4 50.2 %collective-permute-start.5 = (bf16[256,4096]{1,0:T(8,128)(2,1)}, bf16[256,4096]{1,0:T(8,128)(2,1)S(1)}, u32[]{:S(2)}, u32[]{:S(2)}) collective-permute-start(bf16[256,4096]{1,0:T(8,128)(2,1)} %masked_half.2.refs_0_), channel_id=1, source_target_pairs={{0,2},{2,0},{4,6},{6,4},{8,10},{10,8},{12,14},{14,12},{1,3},{3,1},... | collective-permute-start | bytes 6291464 | tf_op jit(solution)/shard_map/ppermute | solution.py:469
  33.7 27.1 %collective-permute-start.6 = (bf16[512,1024]{1,0:T(8,128)(2,1)}, bf16[512,1024]{1,0:T(8,128)(2,1)}, u32[]{:S(2)}, u32[]{:S(2)}) collective-permute-start(bf16[512,1024]{1,0:T(8,128)(2,1)} %copy-done.4), channel_id=1, source_target_pairs={{0,4},{2,6},{12,8},{14,10},{1,5},{3,7},{13,9},{15,11},{16,20},{18,... | collective-permute-start | bytes 3145736 | tf_op jit(solution)/shard_map/ppermute | solution.py:469
  40.6 20.2 %collective-permute-start.7 = (bf16[512,1024]{1,0:T(8,128)(2,1)}, bf16[512,1024]{1,0:T(8,128)(2,1)}, u32[]{:S(2)}, u32[]{:S(2)}) collective-permute-start(bf16[512,1024]{1,0:T(8,128)(2,1)} %copy-done.4), channel_id=1, source_target_pairs={{4,8},{6,10},{8,4},{10,6},{5,9},{7,11},{9,5},{11,7},{20,24},{22,26... | collective-permute-start | bytes 3145736 | tf_op jit(solution)/shard_map/ppermute | solution.py:469
  46.0 36.6 %collective-permute-start.3 = (bf16[512,1536]{1,0:T(8,128)(2,1)}, bf16[512,1536]{1,0:T(8,128)(2,1)}, u32[]{:S(2)}, u32[]{:S(2)}) collective-permute-start(bf16[512,1536]{1,0:T(8,128)(2,1)} %pad_maximum_fusion), channel_id=1, source_target_pairs={{4,0},{6,2},{8,12},{10,14},{5,1},{7,3},{9,13},{11,15},{20,16},{22,... | collective-permute-start | bytes 4718600 | tf_op jit(solution)/shard_map/ppermute | solution.py:469
  47.4 19.4 %collective-permute-start.4 = (bf16[512,512]{1,0:T(8,128)(2,1)S(1)}, bf16[512,512]{1,0:T(8,128)(2,1)}, u32[]{:S(2)}, u32[]{:S(2)}) collective-permute-start(bf16[512,512]{1,0:T(8,128)(2,1)S(1)} %get-tuple-element.70), channel_id=1, source_target_pairs={{4,8},{6,10},{8,4},{10,6},{5,9},{7,11},{9,5},{11,7},{20,24},{22,26... | collective-permute-start | bytes 1572872 | tf_op jit(solution)/shard_map/ppermute | solution.py:469
  82.6 8.8 %copy-start.2 = (bf16[256,4096]{1,0:T(8,128)(2,1)}, bf16[256,4096]{1,0:T(8,128)(2,1)S(1)}, u32[]{:S(2)}) copy-start(bf16[256,4096]{1,0:T(8,128)(2,1)S(1)} %collective-permute-done.5.refs_2_) | copy-start | bytes 6291460
  82.6 9.5 %collective-permute-start.8 = (bf16[256,4096]{1,0:T(8,128)(2,1)S(1)}, bf16[256,4096]{1,0:T(8,128)(2,1)}, u32[]{:S(2)}, u32[]{:S(2)}) collective-permute-start(bf16[256,4096]{1,0:T(8,128)(2,1)S(1)} %collective-permute-done.5.refs_2_), channel_id=1, source_target_pairs={{0,1},{1,0},{2,3},{3,2},{4,5},{5,4},{6,7},{7,6},{8,9},{9,8},{10,11... | collective-permute-start | bytes 6291464 | tf_op jit(solution)/shard_map/ppermute | solution.py:501
  82.6 28.2 %collective-permute-start.9 = (bf16[512,1024]{1,0:T(8,128)(2,1)}, bf16[512,1024]{1,0:T(8,128)(2,1)}, u32[]{:S(2)}, u32[]{:S(2)}) collective-permute-start(bf16[512,1024]{1,0:T(8,128)(2,1)} %get-tuple-element.45), channel_id=1, source_target_pairs={{4,0},{6,2},{8,12},{10,14},{5,1},{7,3},{9,13},{11,15},{20,16},{22,... | collective-permute-start | bytes 3145736 | tf_op jit(solution)/shard_map/ppermute | solution.py:469
  83.9 28.2 %collective-permute-start.11 = (bf16[512,1024]{1,0:T(8,128)(2,1)}, bf16[512,1024]{1,0:T(8,128)(2,1)S(1)}, u32[]{:S(2)}, u32[]{:S(2)}) collective-permute-start(bf16[512,1024]{1,0:T(8,128)(2,1)} %get-tuple-element.52), channel_id=1, source_target_pairs={{4,8},{6,10},{8,4},{10,6},{5,9},{7,11},{9,5},{11,7},{20,24},{22,26... | collective-permute-start | bytes 3145736 | tf_op jit(solution)/shard_map/ppermute | solution.py:469
  84.6 18.1 %collective-permute-start.10 = (bf16[512,512]{1,0:T(8,128)(2,1)}, bf16[512,512]{1,0:T(8,128)(2,1)}, u32[]{:S(2)}, u32[]{:S(2)}) collective-permute-start(bf16[512,512]{1,0:T(8,128)(2,1)} %get-tuple-element.46), channel_id=1, source_target_pairs={{4,8},{6,10},{8,4},{10,6},{5,9},{7,11},{9,5},{11,7},{20,24},{22,26... | collective-permute-start | bytes 1572872 | tf_op jit(solution)/shard_map/ppermute | solution.py:469
  86.1 35.5 %collective-permute-start.12 = (bf16[512,512]{1,0:T(8,128)(2,1)}, bf16[512,512]{1,0:T(8,128)(2,1)}, u32[]{:S(2)}, u32[]{:S(2)}) collective-permute-start(bf16[512,512]{1,0:T(8,128)(2,1)} %collective-permute-done.4.refs_5_), channel_id=1, source_target_pairs={{4,0},{6,2},{8,12},{10,14},{5,1},{7,3},{9,13},{11,15},{20,16},{22,... | collective-permute-start | bytes 1572872 | tf_op jit(solution)/shard_map/ppermute | solution.py:469
  110.8 29.8 %collective-permute-start.13 = (bf16[512,512]{1,0:T(8,128)(2,1)}, bf16[512,512]{1,0:T(8,128)(2,1)S(1)}, u32[]{:S(2)}, u32[]{:S(2)}) collective-permute-start(bf16[512,512]{1,0:T(8,128)(2,1)} %collective-permute-done.10.refs_6_), channel_id=1, source_target_pairs={{4,0},{6,2},{8,12},{10,14},{5,1},{7,3},{9,13},{11,15},{20,16},{22,... | collective-permute-start | bytes 1572872 | tf_op jit(solution)/shard_map/ppermute | solution.py:469
  112.1 21.2 %copy-start.5 = (bf16[512,1024]{1,0:T(8,128)(2,1)}, bf16[512,1024]{1,0:T(8,128)(2,1)S(1)}, u32[]{:S(2)}) copy-start(bf16[512,1024]{1,0:T(8,128)(2,1)S(1)} %collective-permute-done.11.refs_9_) | copy-start | bytes 3145732
  121.6 34.6 %collective-permute-start.14 = (bf16[512,768]{1,0:T(8,128)(2,1)S(1)}, bf16[512,768]{1,0:T(8,128)(2,1)}, u32[]{:S(2)}, u32[]{:S(2)}) collective-permute-start(bf16[512,768]{1,0:T(8,128)(2,1)S(1)} %pad_maximum_fusion.3), channel_id=1, source_target_pairs={{4,0},{6,2},{8,12},{10,14},{5,1},{7,3},{9,13},{11,15},{20,16},{22,... | collective-permute-start | bytes 2359304 | tf_op jit(solution)/shard_map/ppermute | solution.py:469
  140.5 0.8 copy-start.6
  149.2 7.0 %collective-permute-start.15 = (bf16[256,640]{1,0:T(8,128)(2,1)}, bf16[256,640]{1,0:T(8,128)(2,1)S(1)}, u32[]{:S(2)}, u32[]{:S(2)}) collective-permute-start(bf16[256,640]{1,0:T(8,128)(2,1)} %get-tuple-element.57), channel_id=1, source_target_pairs={{0,1},{1,0},{2,3},{3,2},{4,5},{5,4},{6,7},{7,6},{8,9},{9,8},{10,11... | collective-permute-start | bytes 983048 | tf_op jit(solution)/shard_map/ppermute | solution.py:534
  149.2 15.1 %collective-permute-start.19 = (bf16[256,640]{1,0:T(8,128)(2,1)}, bf16[256,640]{1,0:T(8,128)(2,1)S(1)}, u32[]{:S(2)}, u32[]{:S(2)}) collective-permute-start(bf16[256,640]{1,0:T(8,128)(2,1)} %get-tuple-element.65), channel_id=1, source_target_pairs={{0,2},{2,0},{4,6},{6,4},{8,10},{10,8},{12,14},{14,12},{1,3},{3,1},... | collective-permute-start | bytes 983048 | tf_op jit(solution)/shard_map/ppermute | solution.py:469
  150.8 15.4 %collective-permute-start.20 = (bf16[256,640]{1,0:T(8,128)(2,1)}, bf16[256,640]{1,0:T(8,128)(2,1)S(1)}, u32[]{:S(2)}, u32[]{:S(2)}) collective-permute-start(bf16[256,640]{1,0:T(8,128)(2,1)} %get-tuple-element.66), channel_id=1, source_target_pairs={{0,3},{1,2},{2,1},{3,0},{4,7},{5,6},{6,5},{7,4},{8,11},{9,10},{10,... | collective-permute-start | bytes 983048 | tf_op jit(solution)/shard_map/ppermute | solution.py:536
  156.2 7.8 %copy-start.8 = (s32[4,64]{1,0:T(4,128)S(1)}, s32[4,64]{1,0:T(4,128)}, u32[]{:S(2)}) copy-start(s32[4,64]{1,0:T(4,128)} %param.7) | copy-start | bytes 3076
  156.2 10.0 %copy-start = (bf16[256,640]{1,0:T(8,128)(2,1)S(1)}, bf16[256,640]{1,0:T(8,128)(2,1)}, u32[]{:S(2)}) copy-start(bf16[256,640]{1,0:T(8,128)(2,1)} %get-tuple-element.63.refs_0_) | copy-start | bytes 983044
  162.0 12.5 %copy-start.1 = (bf16[256,384]{1,0:T(8,128)(2,1)S(1)}, bf16[256,384]{1,0:T(8,128)(2,1)}, u32[]{:S(2)}) copy-start(bf16[256,384]{1,0:T(8,128)(2,1)} %get-tuple-element.59.refs_0_) | copy-start | bytes 589828
  162.0 6.1 %collective-permute-start.16 = (bf16[256,384]{1,0:T(8,128)(2,1)}, bf16[256,384]{1,0:T(8,128)(2,1)S(1)}, u32[]{:S(2)}, u32[]{:S(2)}) collective-permute-start(bf16[256,384]{1,0:T(8,128)(2,1)} %get-tuple-element.60), channel_id=1, source_target_pairs={{0,1},{1,0},{2,3},{3,2},{4,5},{5,4},{6,7},{7,6},{8,9},{9,8},{10,11... | collective-permute-start | bytes 589832 | tf_op jit(solution)/shard_map/ppermute | solution.py:534
  162.1 9.1 %collective-permute-start.17 = (bf16[256,384]{1,0:T(8,128)(2,1)}, bf16[256,384]{1,0:T(8,128)(2,1)S(1)}, u32[]{:S(2)}, u32[]{:S(2)}) collective-permute-start(bf16[256,384]{1,0:T(8,128)(2,1)} %get-tuple-element.61), channel_id=1, source_target_pairs={{0,2},{2,0},{4,6},{6,4},{8,10},{10,8},{12,14},{14,12},{1,3},{3,1},... | collective-permute-start | bytes 589832 | tf_op jit(solution)/shard_map/ppermute | solution.py:469
  163.7 10.9 %collective-permute-start.18 = (bf16[256,384]{1,0:T(8,128)(2,1)}, bf16[256,384]{1,0:T(8,128)(2,1)S(1)}, u32[]{:S(2)}, u32[]{:S(2)}) collective-permute-start(bf16[256,384]{1,0:T(8,128)(2,1)} %get-tuple-element.62), channel_id=1, source_target_pairs={{0,3},{1,2},{2,1},{3,0},{4,7},{5,6},{6,5},{7,4},{8,11},{9,10},{10,... | collective-permute-start | bytes 589832 | tf_op jit(solution)/shard_map/ppermute | solution.py:536

commit v6 on v5

--- a/solution.py
+++ b/solution.py
@@ -93,42 +93,45 @@
     )(jnp.stack(quarters), w_band)
 
 
-def mask_kernel(half_ref, mask_ref, x_ref, out_ref):
+def mask_kernel(first_ref, mask_ref, x_ref, out_ref):
     out_ref[...] = (x_ref[...].astype(jnp.float32) * mask_ref[0]).astype(jnp.bfloat16)
 
 
-def masked_half(x_band, mask_wide, half):
+def masked_rows(x_band, mask_wide, first, count):
     block = x_band.shape[0] // mask_wide.shape[0]
-    per_half = mask_wide.shape[0] // 2
     cols = x_band.shape[1]
     return pl.pallas_call(
         mask_kernel,
         grid_spec=pltpu.PrefetchScalarGridSpec(
             num_scalar_prefetch=1,
-            grid=(per_half,),
+            grid=(count,),
             in_specs=[
-                pl.BlockSpec((1, 1, cols), lambda i, h: (h[0] * per_half + i, 0, 0)),
-                pl.BlockSpec((block, cols), lambda i, h: (h[0] * per_half + i, 0)),
+                pl.BlockSpec((1, 1, cols), lambda i, f: (f[0] + i, 0, 0)),
+                pl.BlockSpec((block, cols), lambda i, f: (f[0] + i, 0)),
             ],
-            out_specs=pl.BlockSpec((block, cols), lambda i, h: (i, 0)),
+            out_specs=pl.BlockSpec((block, cols), lambda i, f: (i, 0)),
         ),
-        out_shape=jax.ShapeDtypeStruct((x_band.shape[0] // 2, cols), jnp.bfloat16),
+        out_shape=jax.ShapeDtypeStruct((count * block, cols), jnp.bfloat16),
         compiler_params=pltpu.CompilerParams(vmem_limit_bytes=58 * MIB),
         cost_estimate=SMALL,
-        name="masked_half",
-    )(half.reshape(1), mask_wide, x_band)
+        name="masked_rows",
+    )(first.reshape(1), mask_wide, x_band)
+
+
+PARTS = 8
 
 
 def x_copies(x_refs, xv, sems, offset_of):
     n_b, _, rows, panel = xv.shape
-    half = rows // 2
+    part = 2 * rows // PARTS
     copies = {}
     for p in range(n_b):
-        for r in range(4):
-            at = pl.multiple_of(offset_of(p, r // 2) * panel, panel)
+        for r in range(PARTS):
+            g, k = divmod(r, PARTS // 2)
+            at = pl.multiple_of(offset_of(p, g) * panel, panel)
             copies[p, r] = pltpu.make_async_copy(
                 x_refs[r].at[:, pl.ds(at, panel)],
-                xv.at[p, r // 2, (r % 2) * half : (r % 2 + 1) * half],
+                xv.at[p, g, k * part : (k + 1) * part],
                 sems.at[p, r],
             )
     return copies
@@ -144,28 +147,26 @@
     lax.fori_loop(0, 2, step, 0)
 
 
-def whole_kernel(plan, has_prev, meta_ref, *refs):
+def whole_kernel(plan, meta_ref, *refs):
     n_b = len(plan)
-    x_refs, refs = refs[:4], refs[4:]
-    prev_ref, refs = (refs[0], refs[1:]) if has_prev else (None, refs)
+    x_refs, refs = refs[:PARTS], refs[PARTS:]
     b_refs, (out_ref, xv, bv, acc, x_sems, b_sems, out_sems) = refs[:-7], refs[-7:]
     quarter = bv.shape[2]
     low = quarter // 2
     is_end = meta_ref[0]
 
     def offset_of(p, g):
-        return meta_ref[3 + 2 * p + g]
+        return meta_ref[2 + 2 * p + g]
 
     def b_middle(p):
-        return [pltpu.make_async_copy(b_refs[plan[p][0]], bv.at[p], b_sems.at[p, 0])]
+        return [pltpu.make_async_copy(b_refs[plan[p][0]].at[:, :quarter], bv.at[p], b_sems.at[p, 0])]
 
     def b_end(p):
         copies = []
         for k, (operand, first, count, at, to) in enumerate(plan[p][1]):
-            at = pl.multiple_of(meta_ref[2] * LANES, LANES) if at is None else at * LANES
             to = meta_ref[1] if to is None else to
             source = b_refs[operand].at[:, first * LANES : (first + count) * LANES]
-            copies.append(pltpu.make_async_copy(source, bv.at[to, :, pl.ds(at, count * LANES)], b_sems.at[p, k]))
+            copies.append(pltpu.make_async_copy(source, bv.at[to, :, at * LANES : (at + count) * LANES], b_sems.at[p, k]))
         return copies
 
     def on_each(p, do):
@@ -179,30 +180,16 @@
             for copy in b_end(p):
                 do(copy)
 
-    prev_copies = [
-        pltpu.make_async_copy(prev_ref.at[g], acc.at[g, :, low : low + quarter], out_sems.at[g])
-        for g in range(2)
-        if has_prev
-    ]
     copies = x_copies(x_refs, xv, x_sems, offset_of)
     for p in range(n_b):
         on_each(p, lambda copy: copy.start())
-        for r in range(4):
+        for r in range(PARTS):
             copies[p, r].start()
-        if p == 0:
-            for copy in prev_copies:
-                copy.start()
-    if has_prev:
-        for copy in prev_copies:
-            copy.wait()
-        for p in range(n_b):
-            on_each(p, lambda copy: copy.wait())
-    else:
-        acc[...] = jnp.zeros_like(acc)
+    acc[...] = jnp.zeros_like(acc)
     for p in range(n_b):
-        if not has_prev:
-            on_each(p, lambda copy: copy.wait())
-        for r in range(4):
+        for k in [p] if p < n_b - 2 else range(n_b - 2, n_b) if p == n_b - 2 else []:
+            on_each(k, lambda copy: copy.wait())
+        for r in range(PARTS):
             copies[p, r].wait()
         add_products(acc, xv, p, bv.at[p], offset_of, 0)
     outs = [
@@ -214,29 +201,28 @@
         out.wait()
 
 
-def whole_products(meta, xs, prev, operands, plan, name):
-    rows = xs[0].shape[0]
+def whole_products(meta, xs, operands, plan):
+    rows = PARTS // 4 * xs[0].shape[0]
     panel, quarter = operands[plan[0][0]].shape
     n_b = len(plan)
     any_spec = pl.BlockSpec(memory_space=pl.ANY)
     x_spec = pl.BlockSpec(memory_space=pltpu.HBM)
-    operands = ([] if prev is None else [prev]) + operands
     return pl.pallas_call(
-        functools.partial(whole_kernel, plan, prev is not None),
+        functools.partial(whole_kernel, plan),
         out_shape=jax.ShapeDtypeStruct((2, 2 * rows, quarter), jnp.float32),
-        in_specs=[pl.BlockSpec(memory_space=pltpu.SMEM)] + [x_spec] * 4 + [any_spec] * len(operands),
+        in_specs=[pl.BlockSpec(memory_space=pltpu.SMEM)] + [x_spec] * PARTS + [any_spec] * len(operands),
         out_specs=any_spec,
         scratch_shapes=[
             pltpu.VMEM((n_b, 2, 2 * rows, panel), jnp.bfloat16),
             pltpu.VMEM((n_b, panel, quarter), jnp.bfloat16),
             pltpu.VMEM((2, 2 * rows, 2 * quarter), jnp.float32),
-            pltpu.SemaphoreType.DMA((n_b, 4)),
-            pltpu.SemaphoreType.DMA((n_b, 2)),
+            pltpu.SemaphoreType.DMA((n_b, PARTS)),
+            pltpu.SemaphoreType.DMA((n_b, 3)),
             pltpu.SemaphoreType.DMA((2,)),
         ],
         compiler_params=pltpu.CompilerParams(vmem_limit_bytes=59 * MIB),
         cost_estimate=SMALL,
-        name=name,
+        name="whole_products",
     )(meta, *xs, *operands)
 
 
@@ -249,7 +235,7 @@
 
 
 def half_kernel(meta_ref, *refs):
-    x_refs, prev_ref, middle_refs, end_refs, second_ref, refs = refs[:4], refs[4], refs[5:7], refs[7:9], refs[9], refs[10:]
+    x_refs, (prev_ref, middle_ref, end_ref, second_ref), refs = refs[:PARTS], refs[PARTS : PARTS + 4], refs[PARTS + 4 :]
     out_refs, rest_ref, xv, bv, acc, x_sems, b_sems, prev_sem, rest_sem = refs[:4], *refs[4:]
     half = bv.shape[2]
     quarter = 2 * half
@@ -261,12 +247,15 @@
         return meta_ref[5 + 2 * p + g]
 
     copies = x_copies(x_refs, xv, x_sems, offset_of)
-    middle = [pltpu.make_async_copy(middle_refs[p], bv.at[p], b_sems.at[p]) for p in range(2)]
-    middle += [
-        pltpu.make_async_copy(second_ref.at[:, p * half : (p + 1) * half], bv.at[2 + p], b_sems.at[2 + p])
-        for p in range(2)
-    ]
-    end = [pltpu.make_async_copy(end_refs[p], bv.at[p], b_sems.at[p]) for p in range(2)]
+
+    def b_copies(ref, first):
+        return [
+            pltpu.make_async_copy(ref.at[:, p * half : (p + 1) * half], bv.at[first + p], b_sems.at[first + p])
+            for p in range(2)
+        ]
+
+    middle = b_copies(middle_ref, 0) + b_copies(second_ref, 2)
+    end = b_copies(end_ref, 0)
     prev = pltpu.make_async_copy(prev_ref, acc.at[:, :, low : low + quarter], prev_sem)
     prev.start()
 
@@ -312,7 +301,7 @@
 
 
 def half_products(meta, xs, prev, middle, end, second, n_done):
-    rows = xs[0].shape[0]
+    rows = PARTS // 4 * xs[0].shape[0]
     panel, quarter = second.shape
     any_spec = pl.BlockSpec(memory_space=pl.ANY)
     x_spec = pl.BlockSpec(memory_space=pltpu.HBM)
@@ -321,13 +310,13 @@
         half_kernel,
         out_shape=[jax.ShapeDtypeStruct((rows, n_done * LANES), jnp.bfloat16)] * 4
         + [jax.ShapeDtypeStruct((2, 2 * rows, n_rest * LANES), jnp.float32)],
-        in_specs=[pl.BlockSpec(memory_space=pltpu.SMEM)] + [x_spec] * 4 + [any_spec] * 6,
+        in_specs=[pl.BlockSpec(memory_space=pltpu.SMEM)] + [x_spec] * PARTS + [any_spec] * 4,
         out_specs=[pl.BlockSpec(memory_space=pltpu.VMEM)] * 4 + [any_spec],
         scratch_shapes=[
             pltpu.VMEM((2, 2, 2 * rows, panel), jnp.bfloat16),
             pltpu.VMEM((4, panel, quarter // 2), jnp.bfloat16),
             pltpu.VMEM((2, 2 * rows, 2 * quarter), jnp.float32),
-            pltpu.SemaphoreType.DMA((2, 4)),
+            pltpu.SemaphoreType.DMA((2, PARTS)),
             pltpu.SemaphoreType.DMA((4,)),
             pltpu.SemaphoreType.DMA,
             pltpu.SemaphoreType.DMA,
@@ -335,12 +324,12 @@
         compiler_params=pltpu.CompilerParams(vmem_limit_bytes=59 * MIB),
         cost_estimate=SMALL,
         name="half_products",
-    )(meta, *xs, prev, *middle, *end, second)
+    )(meta, *xs, prev, middle, end, second)
 
 
 def rest_kernel(meta_ref, *refs):
-    x_refs, rest_ref, b_ref = refs[:4], *refs[4:6]
-    out_refs, xv, bv, acc, x_sems, b_sem, rest_sem = refs[6:10], *refs[10:]
+    x_refs, (rest_ref, b_ref), refs = refs[:PARTS], refs[PARTS : PARTS + 2], refs[PARTS + 2 :]
+    out_refs, xv, bv, acc, x_sems, b_sem, rest_sem = refs[:4], *refs[4:]
     band = acc.shape[2] // (2 * LANES)
     half = bv.shape[1] // 2
     is_end = meta_ref[0]
@@ -374,7 +363,7 @@
 
 
 def rest_products(meta, xs, rest, b, quarter):
-    rows = xs[0].shape[0]
+    rows = PARTS // 4 * xs[0].shape[0]
     panel = b.shape[0]
     width = rest.shape[2]
     any_spec = pl.BlockSpec(memory_space=pl.ANY)
@@ -382,13 +371,13 @@
     return pl.pallas_call(
         rest_kernel,
         out_shape=[jax.ShapeDtypeStruct((rows, width), jnp.bfloat16)] * 4,
-        in_specs=[pl.BlockSpec(memory_space=pltpu.SMEM)] + [x_spec] * 4 + [any_spec] * 2,
+        in_specs=[pl.BlockSpec(memory_space=pltpu.SMEM)] + [x_spec] * PARTS + [any_spec] * 2,
         out_specs=[pl.BlockSpec(memory_space=pltpu.VMEM)] * 4,
         scratch_shapes=[
             pltpu.VMEM((2, 2, 2 * rows, panel), jnp.bfloat16),
             pltpu.VMEM(b.shape, jnp.bfloat16),
             pltpu.VMEM((2, 2 * rows, 2 * quarter), jnp.float32),
-            pltpu.SemaphoreType.DMA((2, 4)),
+            pltpu.SemaphoreType.DMA((2, PARTS)),
             pltpu.SemaphoreType.DMA,
             pltpu.SemaphoreType.DMA,
         ],
@@ -458,7 +447,6 @@
     q = 2 * y + c
 
     swap = [(0, 2), (1, 3), (2, 0), (3, 1), (4, 6), (5, 7), (6, 4), (7, 5)]
-    inward = [(0, 2), (1, 3), (6, 4), (7, 5)]
     outward = [(2, 0), (3, 1), (4, 6), (5, 7)]
     cross = [(2, 4), (3, 5), (4, 2), (5, 3)]
     across = [(i, i ^ 1) for i in range(8)]
@@ -471,7 +459,6 @@
     def strips(value, start, count):
         return lax.dynamic_slice_in_dim(value, start * LANES, count * LANES, 1)
 
-    start_near = jnp.where(left, 0, 1)
     first_out, second_out = jnp.where(left, 0, 4), jnp.where(left, 4, 0)
     first_in, second_in = second_out, first_out
     last_in = jnp.where(left, 1, 4)
@@ -481,28 +468,33 @@
     swap_a = line(own_a, swap)
     cross_a = line(own_a, cross)
     mask_wide = widen(a_mask, block)
-    x_mine = masked_half(x_band, mask_wide, c)
-    own_b, x_mine, swap_a, cross_a = together(own_b, x_mine, swap_a, cross_a)
-    near_b = line(jnp.concatenate([strips(own_b, start_near, 7), cross_a[:, 3 * LANES :]], 1), outward)
-    in_b = line(own_b, inward)
+    rows = a_mask.shape[0]
+    x_mine = [masked_rows(x_band, mask_wide, c * rows // 2 + k * rows // 4, rows // 4) for k in range(2)]
+    own_b, swap_a, cross_a, *x_mine = together(own_b, swap_a, cross_a, *x_mine)
+    swap_b = line(jnp.concatenate([own_b, cross_a[:, 5 * LANES :]], 1), swap)
     cross_b = line(own_b, cross)
-    x_across = line(x_mine, across)
-    x_rest = masked_half(x_band, mask_wide, 1 - c)
-
-    fwd_a = line(strips(swap_a, first_out, 4), cross)
-    in_b, cross_b = together(in_b, cross_b)
+    x_across = [line(part, across) for part in x_mine]
+    x_rest = [masked_rows(x_band, mask_wide, (1 - c) * rows // 2 + k * rows // 4, rows // 4) for k in range(2)]
+
+    cross_a, cross_b = together(cross_a, cross_b)
     mid_b = jnp.concatenate(
-        [jnp.where(y == 0, cross_a[:, : 3 * LANES], cross_b[:, : 3 * LANES]), cross_b[:, 3 * LANES :]], 1
+        [
+            jnp.where(y == 0, cross_a[:, : 3 * LANES], cross_b[:, : 3 * LANES]),
+            cross_a[:, 3 * LANES : 5 * LANES],
+            cross_b[:, 3 * LANES :],
+        ],
+        1,
     )
-    fwd_b = strips(in_b, first_out, 4)
-    fwd_second = jnp.concatenate([strips(v, second_out, 4) for v in (swap_a, in_b)], 1)
-    near_b, fwd_a, x_across, mid_b, fwd_b, fwd_second = together(near_b, fwd_a, x_across, mid_b, fwd_b, fwd_second)
+    fwd_first = jnp.concatenate([strips(v, first_out, 4) for v in (swap_a, swap_b)], 1)
+    fwd_second = jnp.concatenate([strips(v, second_out, 4) for v in (swap_a, swap_b)], 1)
+    mid_b, fwd_first, fwd_second = together(mid_b, fwd_first, fwd_second)
     mid_b = line(mid_b, outward)
-    x_opposite = lax.ppermute(x_across, "depth", layers)
-    xs = [x_mine, x_rest, x_across, x_opposite]
-    fwd_b = line(fwd_b, cross)
+    fwd_first = line(fwd_first, cross)
+    fwd_first, fwd_second, *x_across = together(fwd_first, fwd_second, *x_across)
+    far_first = line(fwd_first, outward)
     fwd_second = line(fwd_second, cross)
-    far_a = line(fwd_a, outward)
+    x_opposite = [lax.ppermute(part, "depth", layers) for part in x_across]
+    xs = x_mine + x_rest + x_across + x_opposite
 
     def offsets(delta):
         tilt = 2 * y - 1
@@ -511,21 +503,21 @@
     zero = jnp.zeros_like(z)
     third = offsets(jnp.where(is_end == 1, 2, -toward))
     fourth = offsets(jnp.where(is_end == 1, -toward, 2))
-    zero = zero.astype(jnp.int32)
-    meta = jnp.stack([is_end, zero, start_near, *offsets(zero), *offsets(toward)]).astype(jnp.int32)
-    whole = lambda operand, p: (operand, [(operand, 0, 8, 0, p)])
-    plan = [whole(0, 0), whole(1, 1), (2, [(4, 0, 8, 0, 2)]), (3, [(5, 0, 7, None, 3)])]
-    total = whole_products(meta, xs, None, [own_a, own_b, cross_a, cross_b, swap_a, near_b], plan, "first_products")
+    meta = jnp.stack([is_end, 4 + y, *offsets(zero), *offsets(toward), *third]).astype(jnp.int32)
+    plan = [
+        (0, [(0, 0, 8, 0, 0)]),
+        (1, [(1, 0, 8, 0, 1)]),
+        (2, [(4, 0, 8, 0, 2)]),
+        (3, [(5, 0, 8, 0, 3)]),
+        (4, [(5, 8, 3, 5, 4), (6, 0, 3, 0, None), (6, 3, 2, 3, 4)]),
+        (5, [(6, 5, 5, 3, 5)]),
+    ]
+    total = whole_products(meta, xs, [own_a, own_b, cross_a, cross_b, swap_a, swap_b, mid_b], plan)
     last_at = jnp.where(left, 1, 0)
-    mid_b, fwd_b, total, last_at = together(mid_b, fwd_b, total, last_at)
-    far_b = line(fwd_b, outward)
-    meta = jnp.stack([is_end, y, zero, *third]).astype(jnp.int32)
-    plan = [(0, [(2, 7, 5, 3, 0), (3, 0, 3, 0, None)]), (1, [(3, 3, 5, 3, 1)])]
-    total = whole_products(meta, xs, total, [swap_a, in_b, near_b, mid_b], plan, "next_products")
+    total, last_at = together(total, last_at)
     last = jnp.concatenate(
         [strips(fwd_second, last_at, 3), strips(fwd_second, last_at + 4, 3)], 1
     )
-    last, far_a = together(last, far_a)
     far_second = line(last, outward)
 
     def exchanged(pieces):
@@ -538,7 +530,7 @@
 
     done_at, rest_at = jnp.where(left, 3, 0), jnp.where(left, 0, 5)
     meta = jnp.stack([is_end, first_in, second_in, done_at, rest_at, *fourth]).astype(jnp.int32)
-    *done, rest = half_products(meta, xs, total, [fwd_a, fwd_b], [far_a, far_b], fwd_second, 5)
+    *done, rest = half_products(meta, xs, total, fwd_first, far_first, fwd_second, 5)
     done = exchanged(done)
     far_second, done[1] = together(far_second, done[1])
     keep_wide = widen(keep_mask, block)

time: 177 us -> 169 us (0.955)
  starting transfers between devices: 30.1 us -> 25.2 us
  Pallas kernels: 48.8 us -> 45.3 us
    ppermute x16 -> x14, starting transfers between devices: 29.4 us -> 24 us  [line(): return lax.ppermute(value, 'grid', pairs)]
    pallas_call x4 -> x5, Pallas kernels: 27.5 us -> 23.5 us  [the longest x1 14.8 us: whole_products(): pl.pallas_call(functools.partial(whole_kernel, plan), out_shape=jax.Shape...]
    concatenate x1 -> x2, other arithmetic: 1.31 us -> 3.56 us  [the longest x1 2.43 us: pairs_in_line(): swap_b = line(jnp.concatenate([own_b, cross_a[:, 5 * LANES:]], 1), swap)]
    unnamed x18 -> x24, local copies, waits for them, and re-layouts: 0.82 us -> 2.91 us
    ppermute x2, waiting for transfers between devices: 5.19 us -> 3.31 us  [exchanged(): lax.ppermute(pieces[3], ('grid', 'depth'), opposite)]
    ppermute x16 -> x14, waiting for transfers between devices: 76.5 us -> 77.1 us  [line(): return lax.ppermute(value, 'grid', pairs)]
    dynamic_slice x4 -> x3, local copies, waits for them, and re-layouts: 3.56 us -> 3.74 us  [strips(): return lax.dynamic_slice_in_dim(value, start * LANES, count * LANES, 1)]
  transfers between devices with their start and end apart: 21 -> 20, of which waited for: 11 -> 9; matrix products, arithmetic and copies ran while one was open for 8% -> 8% of each run, Pallas kernels for 25% -> 24%
where the time goes in v6:
time: 169 us
  waiting for transfers between devices  80.4 us (48%)
  Pallas kernels  45.3 us (27%)
  starting transfers between devices  25.2 us (15%)
  local copies, waits for them, and re-layouts  10.9 us (6%)
  other arithmetic  6.56 us (4%)
    ppermute x14, waiting for transfers between devices, line(): return lax.ppermute(value, 'grid', pairs)  77.1 us
    ppermute x14, starting transfers between devices, line(): return lax.ppermute(value, 'grid', pairs)  24 us
    pallas_call x1, Pallas kernels, whole_products(): pl.pallas_call(functools.partial(whole_kernel, plan), out_shape=jax.Shape...  14.8 us
    pallas_call x4, Pallas kernels, masked_rows(): pl.pallas_call(mask_kernel, grid_spec=pltpu.PrefetchScalarGridSpec(num_sc...  8.76 us
    pallas_call x1, Pallas kernels, half_products(): pl.pallas_call(half_kernel, out_shape=[jax.ShapeDtypeStruct((rows, n_done...  8.11 us
    pallas_call x1, Pallas kernels, rest_products(): pl.pallas_call(rest_kernel, out_shape=[jax.ShapeDtypeStruct((rows, width)...  6.04 us
    pallas_call x1, Pallas kernels, b_strips(): pl.pallas_call(strips_kernel, out_shape=[jax.ShapeDtypeStruct(shape, jnp....  3.94 us
    dynamic_slice x3, local copies, waits for them, and re-layouts, strips(): return lax.dynamic_slice_in_dim(value, start * LANES, count * LANES, 1)  3.74 us
  transfers between devices with their start and end apart: 20, of which 9 were waited for; matrix products, arithmetic and copies ran while one was open for 8% of the time, Pallas kernels for 24%

profile of v6, /device:TPU:0, one launch (start us, length us, event | category | flops | bytes accessed | tf_op | source)
XLA Modules:
  0.0 168.7 jit_solution(17190769361051752732)
XLA Ops:
  0.6 3.9 %b_strips.1 = (bf16[512,1024]{1,0:T(8,128)(2,1)}, bf16[512,1024]{1,0:T(8,128)(2,1)}) custom-call(s32[2]{0:T(128)} %pad_add_fusion.1.quarters_ref, bf16[512,4096]{1,0:T(8,128)(2,1)} %w_ref.1), custom_call_target="tpu_custom_call" | custom-call | flops 1000 | bytes 1000 | tf_op jit(solution)/shard_map/b_strips/pallas_call | solution.py:81
  4.5 3.1 %collective-permute-start.1 = (bf16[512,1024]{1,0:T(8,128)(2,1)}, bf16[512,1024]{1,0:T(8,128)(2,1)}, u32[]{:S(2)}, u32[]{:S(2)}) collective-permute-start(bf16[512,1024]{1,0:T(8,128)(2,1)} %get-tuple-element.35.refs_8_), channel_id=1, source_target_pairs={{0,4},{2,6},{4,0},{6,2},{8,12},{10,14},{12,8},{14,10},{1,5},{3,7},... | collective-permute-start | bytes 3145736 | tf_op jit(solution)/shard_map/ppermute | solution.py:457
  8.3 1.6 collective-permute-start
  10.9 2.2 %masked_rows.5.refs_1_ = bf16[128,4096]{1,0:T(8,128)(2,1)} custom-call(s32[1]{0:T(128)} %bitcast.9.first_ref, f32[8,1,4096]{2,1,0:T(1,128)} %reshape.22.mask_ref, bf16[512,4096]{1,0:T(8,128)(2,1)} %x_ref.7), custom_call_target="tpu_custom_call" | custom-call | flops 1000 | bytes 1000 | tf_op jit(solution)/shard_map/masked_rows/pallas_call | solution.py:103
  13.1 2.2 %masked_rows.4.refs_0_ = bf16[128,4096]{1,0:T(8,128)(2,1)} custom-call(s32[1]{0:T(128)} %bitcast.8.first_ref, f32[8,1,4096]{2,1,0:T(1,128)} %reshape.22.mask_ref, bf16[512,4096]{1,0:T(8,128)(2,1)} %x_ref.7), custom_call_target="tpu_custom_call" | custom-call | flops 1000 | bytes 1000 | tf_op jit(solution)/shard_map/masked_rows/pallas_call | solution.py:103
  15.3 15.8 %collective-permute-done.1.refs_12_ = bf16[512,1024]{1,0:T(8,128)(2,1)} collective-permute-done((bf16[512,1024]{1,0:T(8,128)(2,1)}, bf16[512,1024]{1,0:T(8,128)(2,1)}, u32[]{:S(2)}, u32[]{:S(2)}) %collective-permute-start.1) | collective-permute-done | bytes 1048608 | tf_op jit(solution)/shard_map/ppermute | solution.py:457
  31.1 2.2 %collective-permute-done.refs_9_ = bf16[512,1024]{1,0:T(8,128)(2,1)} collective-permute-done((bf16[512,1024]{1,0:T(8,128)(2,1)}, bf16[512,1024]{1,0:T(8,128)(2,1)}, u32[]{:S(2)}, u32[]{:S(2)}) %collective-permute-start) | collective-permute-done | bytes 1048608 | tf_op jit(solution)/shard_map/ppermute | solution.py:457
  33.4 1.7 collective-permute-start.3
  35.0 2.4 %pad_maximum_fusion = bf16[512,1408]{1,0:T(8,128)(2,1)} fusion(bf16[512,384]{1,0:T(8,128)(2,1)S(1)} %slice.19, bf16[512,1024]{1,0:T(8,128)(2,1)} %collective-permute-done.refs_9_), kind=kLoop, calls=%fused_computation | loop fusion | flops 2883584 | bytes 2883584 | tf_op jit(solution)/shard_map/concatenate | solution.py:474
  37.5 4.6 %collective-permute-start.4 = (bf16[512,1408]{1,0:T(8,128)(2,1)}, bf16[512,1408]{1,0:T(8,128)(2,1)}, u32[]{:S(2)}, u32[]{:S(2)}) collective-permute-start(bf16[512,1408]{1,0:T(8,128)(2,1)} %pad_maximum_fusion), channel_id=1, source_target_pairs={{0,4},{2,6},{4,0},{6,2},{8,12},{10,14},{12,8},{14,10},{1,5},{3,7},... | collective-permute-start | bytes 4325384 | tf_op jit(solution)/shard_map/ppermute | solution.py:457
  42.1 1.6 collective-permute-start.6
  48.9 23.6 %collective-permute-done.4.refs_13_ = bf16[512,1408]{1,0:T(8,128)(2,1)} collective-permute-done((bf16[512,1408]{1,0:T(8,128)(2,1)}, bf16[512,1408]{1,0:T(8,128)(2,1)}, u32[]{:S(2)}, u32[]{:S(2)}) %collective-permute-start.4) | collective-permute-done | bytes 1441824 | tf_op jit(solution)/shard_map/ppermute | solution.py:457
  74.9 1.6 collective-permute-start.5
  76.5 1.3 collective-permute-start.10
  77.8 10.0 %collective-permute-done.7.refs_5_ = bf16[128,4096]{1,0:T(8,128)(2,1)} collective-permute-done((bf16[128,4096]{1,0:T(8,128)(2,1)S(1)}, bf16[128,4096]{1,0:T(8,128)(2,1)}, u32[]{:S(2)}, u32[]{:S(2)}) %collective-permute-start.7) | collective-permute-done | bytes 1048608 | tf_op jit(solution)/shard_map/ppermute | solution.py:457
  88.4 1.6 collective-permute-start.12
  90.0 1.3 collective-permute-start.11
  91.3 2.2 %masked_rows.7.refs_3_ = bf16[128,4096]{1,0:T(8,128)(2,1)} custom-call(s32[1]{0:T(128)} %bitcast.11.first_ref, f32[8,1,4096]{2,1,0:T(1,128)} %reshape.22.mask_ref, bf16[512,4096]{1,0:T(8,128)(2,1)} %x_ref.7), custom_call_target="tpu_custom_call" | custom-call | flops 1000 | bytes 1000 | tf_op jit(solution)/shard_map/masked_rows/pallas_call | solution.py:103
  93.5 2.2 %masked_rows.6.refs_2_ = bf16[128,4096]{1,0:T(8,128)(2,1)} custom-call(s32[1]{0:T(128)} %bitcast.10.first_ref, f32[8,1,4096]{2,1,0:T(1,128)} %reshape.22.mask_ref, bf16[512,4096]{1,0:T(8,128)(2,1)} %x_ref.7), custom_call_target="tpu_custom_call" | custom-call | flops 1000 | bytes 1000 | tf_op jit(solution)/shard_map/masked_rows/pallas_call | solution.py:103
  96.4 11.4 %collective-permute-done.10.refs_14_ = bf16[512,1280]{1,0:T(8,128)(2,1)} collective-permute-done((bf16[512,1280]{1,0:T(8,128)(2,1)}, bf16[512,1280]{1,0:T(8,128)(2,1)}, u32[]{:S(2)}, u32[]{:S(2)}) %collective-permute-start.10) | collective-permute-done | bytes 1310752 | tf_op jit(solution)/shard_map/ppermute | solution.py:457
  109.8 14.8 %whole_products.1.refs_8_ = f32[2,512,1024]{2,1,0:T(8,128)} custom-call(s32[14]{0:T(128)} %stack.118.meta_ref, bf16[128,4096]{1,0:T(8,128)(2,1)} %masked_rows.4.refs_0_, bf16[128,4096]{1,0:T(8,128)(2,1)} %masked_rows.5.refs_1_, bf16[128,4096]{1,0:T(8,128)(2,1)} %masked_rows.6.refs_2_, bf16[128,4096]{1,0:T(8,128)(2,1)} %masked_rows.7.refs_3_, ...), custom_call_target="tpu_custom_call" | custom-call | flops 1000 | bytes 1000 | tf_op jit(solution)/shard_map/whole_products/pallas_call | solution.py:210
  125.9 1.3 collective-permute-start.13
  127.9 2.0 %collective-permute-done.11.refs_10_ = bf16[512,1024]{1,0:T(8,128)(2,1)} collective-permute-done((bf16[512,1024]{1,0:T(8,128)(2,1)}, bf16[512,1024]{1,0:T(8,128)(2,1)}, u32[]{:S(2)}, u32[]{:S(2)}) %collective-permute-start.11) | collective-permute-done | bytes 1048608 | tf_op jit(solution)/shard_map/ppermute | solution.py:457
  129.9 8.1 %half_products.1 = (bf16[256,640]{1,0:T(8,128)(2,1)}, bf16[256,640]{1,0:T(8,128)(2,1)}, bf16[256,640]{1,0:T(8,128)(2,1)}, bf16[256,640]{1,0:T(8,128)(2,1)}, f32[2,512,384]{2,1,0:T(8,128)}) custom-call(s32[9]{0:T(128)} %stack.108.meta_ref, bf16[128,4096]{1,0:T(8,128)(2,1)} %masked_rows.4.refs_0_, bf16[128,4096]{1,0:T(8,128)(2,1)} %masked_rows.5.refs_1_, ...), custom_call_target="tpu_custom_call" | custom-call | flops 1000 | bytes 1000 | tf_op jit(solution)/shard_map/half_products/pallas_call | solution.py:309
  138.1 1.6 collective-permute-start.18
  140.6 8.2 %collective-permute-done.13.refs_9_ = bf16[512,768]{1,0:T(8,128)(2,1)S(1)} collective-permute-done((bf16[512,768]{1,0:T(8,128)(2,1)S(1)}, bf16[512,768]{1,0:T(8,128)(2,1)S(1)}, u32[]{:S(2)}, u32[]{:S(2)}) %collective-permute-start.13) | collective-permute-done | bytes 786464 | tf_op jit(solution)/shard_map/ppermute | solution.py:457
  149.7 6.0 %rest_products.1 = (bf16[256,384]{1,0:T(8,128)(2,1)}, bf16[256,384]{1,0:T(8,128)(2,1)}, bf16[256,384]{1,0:T(8,128)(2,1)}, bf16[256,384]{1,0:T(8,128)(2,1)}) custom-call(s32[7]{0:T(128)} %stack.102.meta_ref, bf16[128,4096]{1,0:T(8,128)(2,1)} %masked_rows.4.refs_0_, bf16[128,4096]{1,0:T(8,128)(2,1)} %masked_rows.5.refs_1_, ...), custom_call_target="tpu_custom_call" | custom-call | flops 1000 | bytes 1000 | tf_op jit(solution)/shard_map/rest_products/pallas_call | solution.py:371
  155.8 1.6 collective-permute-start.16
  158.0 2.0 %assembled.2.refs_4_ = bf16[256,4096]{1,0:T(8,128)(2,1)} custom-call(s32[2]{0:T(128)S(1)} %get-tuple-element.70.place_ref, f32[4,1,4096]{2,1,0:T(1,128)S(1)} %reshape.20.mask_ref, bf16[256,640]{1,0:T(8,128)(2,1)S(1)} %copy-done, bf16[256,640]{1,0:T(8,128)(2,1)S(1)} %collective-permute-done.14.refs_1_, bf16[256,640]{1,0:T(8,128)(2,1)S(1)} %collective-permute-done.18.refs_2_, ...), custom_call_target="tpu_custom_call" | custom-call | flops 1000 | bytes 1000 | tf_op jit(solution)/shard_map/assembled/pallas_call | solution.py:416
  160.0 3.8 %collective-permute-done.16.refs_2_ = bf16[256,384]{1,0:T(8,128)(2,1)S(1)} collective-permute-done((bf16[256,384]{1,0:T(8,128)(2,1)}, bf16[256,384]{1,0:T(8,128)(2,1)S(1)}, u32[]{:S(2)}, u32[]{:S(2)}) %collective-permute-start.16) | collective-permute-done | bytes 196640 | tf_op jit(solution)/shard_map/ppermute | solution.py:457
  163.8 3.3 %collective-permute-done.17.refs_3_ = bf16[256,384]{1,0:T(8,128)(2,1)S(1)} collective-permute-done((bf16[256,384]{1,0:T(8,128)(2,1)}, bf16[256,384]{1,0:T(8,128)(2,1)S(1)}, u32[]{:S(2)}, u32[]{:S(2)}) %collective-permute-start.17) | collective-permute-done | bytes 196640 | tf_op jit(solution)/shard_map/ppermute | solution.py:528
  167.1 1.6 assembled.3
  (65 shorter events, 17.5 us)
Async XLA Ops:
  0.6 9.4 %copy-start.10 = (s32[8,64]{1,0:T(8,128)S(1)}, s32[8,64]{1,0:T(8,128)}, u32[]{:S(2)}) copy-start(s32[8,64]{1,0:T(8,128)} %param.6) | copy-start | bytes 6148
  4.5 26.6 %collective-permute-start.1 = (bf16[512,1024]{1,0:T(8,128)(2,1)}, bf16[512,1024]{1,0:T(8,128)(2,1)}, u32[]{:S(2)}, u32[]{:S(2)}) collective-permute-start(bf16[512,1024]{1,0:T(8,128)(2,1)} %get-tuple-element.35.refs_8_), channel_id=1, source_target_pairs={{0,4},{2,6},{4,0},{6,2},{8,12},{10,14},{12,8},{14,10},{1,5},{3,7},... | collective-permute-start | bytes 3145736 | tf_op jit(solution)/shard_map/ppermute | solution.py:457
  7.6 23.5 %collective-permute-start.2 = (bf16[512,1024]{1,0:T(8,128)(2,1)}, bf16[512,1024]{1,0:T(8,128)(2,1)S(1)}, u32[]{:S(2)}, u32[]{:S(2)}) collective-permute-start(bf16[512,1024]{1,0:T(8,128)(2,1)} %get-tuple-element.35.refs_8_), channel_id=1, source_target_pairs={{4,8},{6,10},{8,4},{10,6},{5,9},{7,11},{9,5},{11,7},{20,24},{22,26... | collective-permute-start | bytes 3145736 | tf_op jit(solution)/shard_map/ppermute | solution.py:457
  8.3 25.0 %collective-permute-start = (bf16[512,1024]{1,0:T(8,128)(2,1)}, bf16[512,1024]{1,0:T(8,128)(2,1)}, u32[]{:S(2)}, u32[]{:S(2)}) collective-permute-start(bf16[512,1024]{1,0:T(8,128)(2,1)} %get-tuple-element.34), channel_id=1, source_target_pairs={{0,2},{2,0},{4,6},{6,4},{8,10},{10,8},{12,14},{14,12},{1,3},{3,1},... | collective-permute-start | bytes 3145736 | tf_op jit(solution)/shard_map/ppermute | solution.py:457
  15.3 26.8 %copy-start.3 = (bf16[128,4096]{1,0:T(8,128)(2,1)S(1)}, bf16[128,4096]{1,0:T(8,128)(2,1)}, u32[]{:S(2)}) copy-start(bf16[128,4096]{1,0:T(8,128)(2,1)} %masked_rows.4.refs_0_) | copy-start | bytes 3145732
  15.3 28.4 %copy-start.2 = (bf16[128,4096]{1,0:T(8,128)(2,1)S(1)}, bf16[128,4096]{1,0:T(8,128)(2,1)}, u32[]{:S(2)}) copy-start(bf16[128,4096]{1,0:T(8,128)(2,1)} %masked_rows.5.refs_1_) | copy-start | bytes 3145732
  31.1 11.0 %copy-start.7 = (bf16[512,1024]{1,0:T(8,128)(2,1)}, bf16[512,1024]{1,0:T(8,128)(2,1)S(1)}, u32[]{:S(2)}) copy-start(bf16[512,1024]{1,0:T(8,128)(2,1)S(1)} %collective-permute-done.2.refs_10_) | copy-start | bytes 3145732
  33.4 12.1 %collective-permute-start.3 = (bf16[512,1024]{1,0:T(8,128)(2,1)}, bf16[512,1024]{1,0:T(8,128)(2,1)}, u32[]{:S(2)}, u32[]{:S(2)}) collective-permute-start(bf16[512,1024]{1,0:T(8,128)(2,1)} %collective-permute-done.refs_9_), channel_id=1, source_target_pairs={{4,8},{6,10},{8,4},{10,6},{5,9},{7,11},{9,5},{11,7},{20,24},{22,26... | collective-permute-start | bytes 3145736 | tf_op jit(solution)/shard_map/ppermute | solution.py:457
  37.5 35.0 %collective-permute-start.4 = (bf16[512,1408]{1,0:T(8,128)(2,1)}, bf16[512,1408]{1,0:T(8,128)(2,1)}, u32[]{:S(2)}, u32[]{:S(2)}) collective-permute-start(bf16[512,1408]{1,0:T(8,128)(2,1)} %pad_maximum_fusion), channel_id=1, source_target_pairs={{0,4},{2,6},{4,0},{6,2},{8,12},{10,14},{12,8},{14,10},{1,5},{3,7},... | collective-permute-start | bytes 4325384 | tf_op jit(solution)/shard_map/ppermute | solution.py:457
  42.1 4.5 %copy-start.8 = (bf16[512,1024]{1,0:T(8,128)(2,1)S(1)}, bf16[512,1024]{1,0:T(8,128)(2,1)}, u32[]{:S(2)}) copy-start(bf16[512,1024]{1,0:T(8,128)(2,1)} %copy-done.7) | copy-start | bytes 3145732
  42.1 5.6 %slice-start = ((bf16[512,1024]{1,0:T(8,128)(2,1)}), bf16[512,256]{1,0:T(8,128)(2,1)S(1)}, s32[]{:S(2)}) async-start(bf16[512,1024]{1,0:T(8,128)(2,1)} %copy-done.7), calls=%async_computation | async-start | bytes 524288 | tf_op jit(solution)/shard_map/slice | solution.py:483
  42.1 35.7 %collective-permute-start.6 = (bf16[128,4096]{1,0:T(8,128)(2,1)S(1)}, bf16[128,4096]{1,0:T(8,128)(2,1)S(1)}, u32[]{:S(2)}, u32[]{:S(2)}) collective-permute-start(bf16[128,4096]{1,0:T(8,128)(2,1)S(1)} %copy-done.3), channel_id=1, source_target_pairs={{0,2},{2,0},{4,6},{6,4},{8,10},{10,8},{12,14},{14,12},{1,3},{3,1},... | collective-permute-start | bytes 3145736 | tf_op jit(solution)/shard_map/ppermute | solution.py:457
  43.7 44.2 %collective-permute-start.7 = (bf16[128,4096]{1,0:T(8,128)(2,1)S(1)}, bf16[128,4096]{1,0:T(8,128)(2,1)}, u32[]{:S(2)}, u32[]{:S(2)}) collective-permute-start(bf16[128,4096]{1,0:T(8,128)(2,1)S(1)} %copy-done.2), channel_id=1, source_target_pairs={{0,2},{2,0},{4,6},{6,4},{8,10},{10,8},{12,14},{14,12},{1,3},{3,1},... | collective-permute-start | bytes 3145736 | tf_op jit(solution)/shard_map/ppermute | solution.py:457
  74.9 13.0 %collective-permute-start.5 = (bf16[512,1024]{1,0:T(8,128)(2,1)S(1)}, bf16[512,1024]{1,0:T(8,128)(2,1)}, u32[]{:S(2)}, u32[]{:S(2)}) collective-permute-start(bf16[512,1024]{1,0:T(8,128)(2,1)S(1)} %get-tuple-element.43), channel_id=1, source_target_pairs={{4,8},{6,10},{8,4},{10,6},{5,9},{7,11},{9,5},{11,7},{20,24},{22,26... | collective-permute-start | bytes 3145736 | tf_op jit(solution)/shard_map/ppermute | solution.py:457
  76.5 31.3 %collective-permute-start.10 = (bf16[512,1280]{1,0:T(8,128)(2,1)}, bf16[512,1280]{1,0:T(8,128)(2,1)}, u32[]{:S(2)}, u32[]{:S(2)}) collective-permute-start(bf16[512,1280]{1,0:T(8,128)(2,1)} %pad_maximum_fusion.1), channel_id=1, source_target_pairs={{4,0},{6,2},{8,12},{10,14},{5,1},{7,3},{9,13},{11,15},{20,16},{22,... | collective-permute-start | bytes 3932168 | tf_op jit(solution)/shard_map/ppermute | solution.py:457
  77.8 15.7 %copy-start.4 = (bf16[128,4096]{1,0:T(8,128)(2,1)}, bf16[128,4096]{1,0:T(8,128)(2,1)S(1)}, u32[]{:S(2)}) copy-start(bf16[128,4096]{1,0:T(8,128)(2,1)S(1)} %collective-permute-done.6.refs_4_) | copy-start | bytes 3145732
  87.9 20.0 %collective-permute-start.8 = (bf16[128,4096]{1,0:T(8,128)(2,1)S(1)}, bf16[128,4096]{1,0:T(8,128)(2,1)S(1)}, u32[]{:S(2)}, u32[]{:S(2)}) collective-permute-start(bf16[128,4096]{1,0:T(8,128)(2,1)S(1)} %collective-permute-done.6.refs_4_), channel_id=1, source_target_pairs={{0,1},{1,0},{2,3},{3,2},{4,5},{5,4},{6,7},{7,6},{8,9},{9,8},{10,11... | collective-permute-start | bytes 3145736 | tf_op jit(solution)/shard_map/ppermute | solution.py:496
  87.9 20.0 %collective-permute-start.9 = (bf16[128,4096]{1,0:T(8,128)(2,1)}, bf16[128,4096]{1,0:T(8,128)(2,1)S(1)}, u32[]{:S(2)}, u32[]{:S(2)}) collective-permute-start(bf16[128,4096]{1,0:T(8,128)(2,1)} %collective-permute-done.7.refs_5_), channel_id=1, source_target_pairs={{0,1},{1,0},{2,3},{3,2},{4,5},{5,4},{6,7},{7,6},{8,9},{9,8},{10,11... | collective-permute-start | bytes 3145736 | tf_op jit(solution)/shard_map/ppermute | solution.py:496
  88.4 36.2 %collective-permute-start.12 = (bf16[512,1024]{1,0:T(8,128)(2,1)}, bf16[512,1024]{1,0:T(8,128)(2,1)}, u32[]{:S(2)}, u32[]{:S(2)}) collective-permute-start(bf16[512,1024]{1,0:T(8,128)(2,1)} %get-tuple-element.50), channel_id=1, source_target_pairs={{4,8},{6,10},{8,4},{10,6},{5,9},{7,11},{9,5},{11,7},{20,24},{22,26... | collective-permute-start | bytes 3145736 | tf_op jit(solution)/shard_map/ppermute | solution.py:457
  90.0 39.8 %collective-permute-start.11 = (bf16[512,1024]{1,0:T(8,128)(2,1)}, bf16[512,1024]{1,0:T(8,128)(2,1)}, u32[]{:S(2)}, u32[]{:S(2)}) collective-permute-start(bf16[512,1024]{1,0:T(8,128)(2,1)} %collective-permute-done.5.refs_9_), channel_id=1, source_target_pairs={{4,0},{6,2},{8,12},{10,14},{5,1},{7,3},{9,13},{11,15},{20,16},{22,... | collective-permute-start | bytes 3145736 | tf_op jit(solution)/shard_map/ppermute | solution.py:457
  107.8 1.0 copy-start.5
  108.9 1.0 copy-start.6
  125.9 22.9 %collective-permute-start.13 = (bf16[512,768]{1,0:T(8,128)(2,1)S(1)}, bf16[512,768]{1,0:T(8,128)(2,1)S(1)}, u32[]{:S(2)}, u32[]{:S(2)}) collective-permute-start(bf16[512,768]{1,0:T(8,128)(2,1)S(1)} %pad_maximum_fusion.4), channel_id=1, source_target_pairs={{4,0},{6,2},{8,12},{10,14},{5,1},{7,3},{9,13},{11,15},{20,16},{22,... | collective-permute-start | bytes 2359304 | tf_op jit(solution)/shard_map/ppermute | solution.py:457
  138.0 2.6 %collective-permute-start.14 = (bf16[256,640]{1,0:T(8,128)(2,1)}, bf16[256,640]{1,0:T(8,128)(2,1)S(1)}, u32[]{:S(2)}, u32[]{:S(2)}) collective-permute-start(bf16[256,640]{1,0:T(8,128)(2,1)} %get-tuple-element.53), channel_id=1, source_target_pairs={{0,1},{1,0},{2,3},{3,2},{4,5},{5,4},{6,7},{7,6},{8,9},{9,8},{10,11... | collective-permute-start | bytes 983048 | tf_op jit(solution)/shard_map/ppermute | solution.py:526
  138.1 19.9 %collective-permute-start.18 = (bf16[256,640]{1,0:T(8,128)(2,1)}, bf16[256,640]{1,0:T(8,128)(2,1)S(1)}, u32[]{:S(2)}, u32[]{:S(2)}) collective-permute-start(bf16[256,640]{1,0:T(8,128)(2,1)} %get-tuple-element.61), channel_id=1, source_target_pairs={{0,2},{2,0},{4,6},{6,4},{8,10},{10,8},{12,14},{14,12},{1,3},{3,1},... | collective-permute-start | bytes 983048 | tf_op jit(solution)/shard_map/ppermute | solution.py:457
  139.6 18.4 %collective-permute-start.19 = (bf16[256,640]{1,0:T(8,128)(2,1)}, bf16[256,640]{1,0:T(8,128)(2,1)S(1)}, u32[]{:S(2)}, u32[]{:S(2)}) collective-permute-start(bf16[256,640]{1,0:T(8,128)(2,1)} %get-tuple-element.62), channel_id=1, source_target_pairs={{0,3},{1,2},{2,1},{3,0},{4,7},{5,6},{6,5},{7,4},{8,11},{9,10},{10,... | collective-permute-start | bytes 983048 | tf_op jit(solution)/shard_map/ppermute | solution.py:528
  149.7 8.0 %copy-start.11 = (s32[4,64]{1,0:T(4,128)S(1)}, s32[4,64]{1,0:T(4,128)}, u32[]{:S(2)}) copy-start(s32[4,64]{1,0:T(4,128)} %param.7) | copy-start | bytes 3076
  149.7 8.3 %copy-start = (bf16[256,640]{1,0:T(8,128)(2,1)S(1)}, bf16[256,640]{1,0:T(8,128)(2,1)}, u32[]{:S(2)}) copy-start(bf16[256,640]{1,0:T(8,128)(2,1)} %get-tuple-element.59.refs_0_) | copy-start | bytes 983044
  155.7 11.4 %copy-start.1 = (bf16[256,384]{1,0:T(8,128)(2,1)S(1)}, bf16[256,384]{1,0:T(8,128)(2,1)}, u32[]{:S(2)}) copy-start(bf16[256,384]{1,0:T(8,128)(2,1)} %get-tuple-element.55.refs_0_) | copy-start | bytes 589828
  155.7 4.3 %collective-permute-start.15 = (bf16[256,384]{1,0:T(8,128)(2,1)}, bf16[256,384]{1,0:T(8,128)(2,1)S(1)}, u32[]{:S(2)}, u32[]{:S(2)}) collective-permute-start(bf16[256,384]{1,0:T(8,128)(2,1)} %get-tuple-element.56), channel_id=1, source_target_pairs={{0,1},{1,0},{2,3},{3,2},{4,5},{5,4},{6,7},{7,6},{8,9},{9,8},{10,11... | collective-permute-start | bytes 589832 | tf_op jit(solution)/shard_map/ppermute | solution.py:526
  155.8 8.0 %collective-permute-start.16 = (bf16[256,384]{1,0:T(8,128)(2,1)}, bf16[256,384]{1,0:T(8,128)(2,1)S(1)}, u32[]{:S(2)}, u32[]{:S(2)}) collective-permute-start(bf16[256,384]{1,0:T(8,128)(2,1)} %get-tuple-element.57), channel_id=1, source_target_pairs={{0,2},{2,0},{4,6},{6,4},{8,10},{10,8},{12,14},{14,12},{1,3},{3,1},... | collective-permute-start | bytes 589832 | tf_op jit(solution)/shard_map/ppermute | solution.py:457
  157.4 9.7 %collective-permute-start.17 = (bf16[256,384]{1,0:T(8,128)(2,1)}, bf16[256,384]{1,0:T(8,128)(2,1)S(1)}, u32[]{:S(2)}, u32[]{:S(2)}) collective-permute-start(bf16[256,384]{1,0:T(8,128)(2,1)} %get-tuple-element.58), channel_id=1, source_target_pairs={{0,3},{1,2},{2,1},{3,0},{4,7},{5,6},{6,5},{7,4},{8,11},{9,10},{10,... | collective-permute-start | bytes 589832 | tf_op jit(solution)/shard_map/ppermute | solution.py:528
  (1 other events, 0.9 us)

commit v7 on v6

--- a/solution.py
+++ b/solution.py
@@ -73,7 +73,7 @@
             b_ref[:, j * LANES : (j + 1) * LANES] = value.astype(jnp.bfloat16)
 
 
-def b_strips(w_band, quarters):
+def b_strips(w_band, quarters, limit):
     panel = w_band.shape[0]
     band = w_band.shape[1] // panel
     n = len(quarters)
@@ -87,7 +87,7 @@
         ],
         out_specs=[pl.BlockSpec(memory_space=pltpu.VMEM)] * n,
         scratch_shapes=[pltpu.VMEM((n, *shape), jnp.bfloat16), pltpu.SemaphoreType.DMA((n, band))],
-        compiler_params=pltpu.CompilerParams(vmem_limit_bytes=56 * MIB),
+        compiler_params=pltpu.CompilerParams(vmem_limit_bytes=limit * MIB),
         cost_estimate=SMALL,
         name="b_strips",
     )(jnp.stack(quarters), w_band)
@@ -217,7 +217,7 @@
             pltpu.VMEM((n_b, panel, quarter), jnp.bfloat16),
             pltpu.VMEM((2, 2 * rows, 2 * quarter), jnp.float32),
             pltpu.SemaphoreType.DMA((n_b, PARTS)),
-            pltpu.SemaphoreType.DMA((n_b, 3)),
+            pltpu.SemaphoreType.DMA((n_b, 2)),
             pltpu.SemaphoreType.DMA((2,)),
         ],
         compiler_params=pltpu.CompilerParams(vmem_limit_bytes=59 * MIB),
@@ -463,15 +463,19 @@
     first_in, second_in = second_out, first_out
     last_in = jnp.where(left, 1, 4)
 
-    sent_b, own_a = b_strips(w_band, [q ^ 2, q])
+    (sent_b,) = b_strips(w_band, [q ^ 2], 58)
     own_b = line(sent_b, across)
+    sent_b, w_band = together(sent_b, w_band)
+    (own_a,) = b_strips(w_band, [q], 48)
     swap_a = line(own_a, swap)
     cross_a = line(own_a, cross)
     mask_wide = widen(a_mask, block)
     rows = a_mask.shape[0]
     x_mine = [masked_rows(x_band, mask_wide, c * rows // 2 + k * rows // 4, rows // 4) for k in range(2)]
-    own_b, swap_a, cross_a, *x_mine = together(own_b, swap_a, cross_a, *x_mine)
-    swap_b = line(jnp.concatenate([own_b, cross_a[:, 5 * LANES :]], 1), swap)
+    own_b, *x_mine = together(own_b, *x_mine)
+    own_b, swap_a = together(own_b, swap_a)
+    own_b, cross_a = together(own_b, cross_a)
+    swap_b = line(own_b, swap)
     cross_b = line(own_b, cross)
     x_across = [line(part, across) for part in x_mine]
     x_rest = [masked_rows(x_band, mask_wide, (1 - c) * rows // 2 + k * rows // 4, rows // 4) for k in range(2)]
@@ -480,13 +484,14 @@
     mid_b = jnp.concatenate(
         [
             jnp.where(y == 0, cross_a[:, : 3 * LANES], cross_b[:, : 3 * LANES]),
-            cross_a[:, 3 * LANES : 5 * LANES],
+            cross_a[:, 3 * LANES :],
             cross_b[:, 3 * LANES :],
         ],
         1,
     )
     fwd_first = jnp.concatenate([strips(v, first_out, 4) for v in (swap_a, swap_b)], 1)
     fwd_second = jnp.concatenate([strips(v, second_out, 4) for v in (swap_a, swap_b)], 1)
+    fwd_first, fwd_second = together(fwd_first, fwd_second)
     mid_b, fwd_first, fwd_second = together(mid_b, fwd_first, fwd_second)
     mid_b = line(mid_b, outward)
     fwd_first = line(fwd_first, cross)
@@ -509,8 +514,8 @@
         (1, [(1, 0, 8, 0, 1)]),
         (2, [(4, 0, 8, 0, 2)]),
         (3, [(5, 0, 8, 0, 3)]),
-        (4, [(5, 8, 3, 5, 4), (6, 0, 3, 0, None), (6, 3, 2, 3, 4)]),
-        (5, [(6, 5, 5, 3, 5)]),
+        (4, [(6, 0, 3, 0, None), (6, 3, 5, 3, 4)]),
+        (5, [(6, 8, 5, 3, 5)]),
     ]
     total = whole_products(meta, xs, [own_a, own_b, cross_a, cross_b, swap_a, swap_b, mid_b], plan)
     last_at = jnp.where(left, 1, 0)

time: 169 us -> 168 us (level)
  other arithmetic: 6.56 us -> 3.82 us
    ppermute x2, waiting for transfers between devices: 3.31 us -> 6.11 us  [exchanged(): lax.ppermute(pieces[3], ('grid', 'depth'), opposite)]
    concatenate x1 -> x0, other arithmetic: 2.43 us -> none  [pairs_in_line(): swap_b = line(jnp.concatenate([own_b, cross_a[:, 5 * LANES:]], 1), swap)]
    pallas_call x1 -> x2, Pallas kernels: 3.94 us -> 3.24 us  [b_strips(): pl.pallas_call(strips_kernel, out_shape=[jax.ShapeDtypeStruct(shape, jnp....]
  transfers between devices with their start and end apart: 20 -> 20, of which waited for: 9 -> 10; matrix products, arithmetic and copies ran while one was open for 8% -> 8% of each run, Pallas kernels for 24% -> 24%
where the time goes in v7:
time: 168 us
  waiting for transfers between devices  81.9 us (49%)
  Pallas kernels  44.6 us (27%)
  starting transfers between devices  26.1 us (16%)
  local copies, waits for them, and re-layouts  10.9 us (6%)
  other arithmetic  3.82 us (2%)
    ppermute x14, waiting for transfers between devices, line(): return lax.ppermute(value, 'grid', pairs)  75.8 us
    ppermute x14, starting transfers between devices, line(): return lax.ppermute(value, 'grid', pairs)  23.7 us
    pallas_call x1, Pallas kernels, whole_products(): pl.pallas_call(functools.partial(whole_kernel, plan), out_shape=jax.Shape...  14.8 us
    pallas_call x4, Pallas kernels, masked_rows(): pl.pallas_call(mask_kernel, grid_spec=pltpu.PrefetchScalarGridSpec(num_sc...  8.81 us
    pallas_call x1, Pallas kernels, half_products(): pl.pallas_call(half_kernel, out_shape=[jax.ShapeDtypeStruct((rows, n_done...  8.17 us
    ppermute x2, waiting for transfers between devices, exchanged(): lax.ppermute(pieces[3], ('grid', 'depth'), opposite)  6.11 us
    pallas_call x1, Pallas kernels, rest_products(): pl.pallas_call(rest_kernel, out_shape=[jax.ShapeDtypeStruct((rows, width)...  6.04 us
    dynamic_slice x3, local copies, waits for them, and re-layouts, strips(): return lax.dynamic_slice_in_dim(value, start * LANES, count * LANES, 1)  3.74 us
  transfers between devices with their start and end apart: 20, of which 10 were waited for; matrix products, arithmetic and copies ran while one was open for 8% of the time, Pallas kernels for 24%

profile of v7, /device:TPU:0, one launch (start us, length us, event | category | flops | bytes accessed | tf_op | source)
XLA Modules:
  0.0 167.7 jit_solution(15457760498263917223)
XLA Ops:
  0.0 2.5 %b_strips.2 = bf16[512,1024]{1,0:T(8,128)(2,1)} custom-call(s32[1]{0:T(128)} %bitcast.7.quarters_ref, bf16[512,4096]{1,0:T(8,128)(2,1)} %w_ref.2), custom_call_target="tpu_custom_call" | custom-call | flops 1000 | bytes 1000 | tf_op jit(solution)/shard_map/b_strips/pallas_call | solution.py:81
  2.5 3.0 %collective-permute-start = (bf16[512,1024]{1,0:T(8,128)(2,1)}, bf16[512,1024]{1,0:T(8,128)(2,1)}, u32[]{:S(2)}, u32[]{:S(2)}) collective-permute-start(bf16[512,1024]{1,0:T(8,128)(2,1)} %b_strips.2), channel_id=1, source_target_pairs={{0,2},{2,0},{4,6},{6,4},{8,10},{10,8},{12,14},{14,12},{1,3},{3,1},... | collective-permute-start | bytes 3145736 | tf_op jit(solution)/shard_map/ppermute | solution.py:457
  6.3 1.6 collective-permute-start.1
  8.0 1.6 collective-permute-start.2
  10.5 2.1 %masked_rows.5.refs_1_ = bf16[128,4096]{1,0:T(8,128)(2,1)} custom-call(s32[1]{0:T(128)} %bitcast.9.first_ref, f32[8,1,4096]{2,1,0:T(1,128)} %reshape.22.mask_ref, bf16[512,4096]{1,0:T(8,128)(2,1)} %x_ref.7), custom_call_target="tpu_custom_call" | custom-call | flops 1000 | bytes 1000 | tf_op jit(solution)/shard_map/masked_rows/pallas_call | solution.py:103
  12.7 2.3 %masked_rows.4.refs_0_ = bf16[128,4096]{1,0:T(8,128)(2,1)} custom-call(s32[1]{0:T(128)} %bitcast.8.first_ref, f32[8,1,4096]{2,1,0:T(1,128)} %reshape.22.mask_ref, bf16[512,4096]{1,0:T(8,128)(2,1)} %x_ref.7), custom_call_target="tpu_custom_call" | custom-call | flops 1000 | bytes 1000 | tf_op jit(solution)/shard_map/masked_rows/pallas_call | solution.py:103
  15.0 14.1 %collective-permute-done.refs_9_ = bf16[512,1024]{1,0:T(8,128)(2,1)} collective-permute-done((bf16[512,1024]{1,0:T(8,128)(2,1)}, bf16[512,1024]{1,0:T(8,128)(2,1)}, u32[]{:S(2)}, u32[]{:S(2)}) %collective-permute-start) | collective-permute-done | bytes 1048608 | tf_op jit(solution)/shard_map/ppermute | solution.py:457
  29.1 2.0 %collective-permute-done.1.refs_12_ = bf16[512,1024]{1,0:T(8,128)(2,1)} collective-permute-done((bf16[512,1024]{1,0:T(8,128)(2,1)S(1)}, bf16[512,1024]{1,0:T(8,128)(2,1)}, u32[]{:S(2)}, u32[]{:S(2)}) %collective-permute-start.1) | collective-permute-done | bytes 1048608 | tf_op jit(solution)/shard_map/ppermute | solution.py:457
  31.1 4.6 %collective-permute-start.4 = (bf16[512,1024]{1,0:T(8,128)(2,1)}, bf16[512,1024]{1,0:T(8,128)(2,1)}, u32[]{:S(2)}, u32[]{:S(2)}) collective-permute-start(bf16[512,1024]{1,0:T(8,128)(2,1)} %collective-permute-done.refs_9_), channel_id=1, source_target_pairs={{0,4},{2,6},{4,0},{6,2},{8,12},{10,14},{12,8},{14,10},{1,5},{3,7},... | collective-permute-start | bytes 3145736 | tf_op jit(solution)/shard_map/ppermute | solution.py:457
  35.7 1.7 collective-permute-start.3
  38.0 1.4 collective-permute-start.7
  40.7 17.3 %collective-permute-done.4.refs_13_ = bf16[512,1024]{1,0:T(8,128)(2,1)} collective-permute-done((bf16[512,1024]{1,0:T(8,128)(2,1)}, bf16[512,1024]{1,0:T(8,128)(2,1)}, u32[]{:S(2)}, u32[]{:S(2)}) %collective-permute-start.4) | collective-permute-done | bytes 1048608 | tf_op jit(solution)/shard_map/ppermute | solution.py:457
  63.9 1.3 pad_maximum_fusion
  65.2 1.6 collective-permute-start.5
  66.9 1.3 collective-permute-start.10
  68.2 15.3 %collective-permute-done.7.refs_5_ = bf16[128,4096]{1,0:T(8,128)(2,1)S(1)} collective-permute-done((bf16[128,4096]{1,0:T(8,128)(2,1)S(1)}, bf16[128,4096]{1,0:T(8,128)(2,1)S(1)}, u32[]{:S(2)}, u32[]{:S(2)}) %collective-permute-start.7) | collective-permute-done | bytes 1048608 | tf_op jit(solution)/shard_map/ppermute | solution.py:457
  84.0 1.6 collective-permute-start.12
  85.6 1.3 collective-permute-start.11
  86.9 2.2 %masked_rows.7.refs_3_ = bf16[128,4096]{1,0:T(8,128)(2,1)} custom-call(s32[1]{0:T(128)} %bitcast.11.first_ref, f32[8,1,4096]{2,1,0:T(1,128)} %reshape.22.mask_ref, bf16[512,4096]{1,0:T(8,128)(2,1)} %x_ref.7), custom_call_target="tpu_custom_call" | custom-call | flops 1000 | bytes 1000 | tf_op jit(solution)/shard_map/masked_rows/pallas_call | solution.py:103
  89.1 2.2 %masked_rows.6.refs_2_ = bf16[128,4096]{1,0:T(8,128)(2,1)} custom-call(s32[1]{0:T(128)} %bitcast.10.first_ref, f32[8,1,4096]{2,1,0:T(1,128)} %reshape.22.mask_ref, bf16[512,4096]{1,0:T(8,128)(2,1)} %x_ref.7), custom_call_target="tpu_custom_call" | custom-call | flops 1000 | bytes 1000 | tf_op jit(solution)/shard_map/masked_rows/pallas_call | solution.py:103
  91.9 18.1 %collective-permute-done.10.refs_14_ = bf16[512,1664]{1,0:T(8,128)(2,1)} collective-permute-done((bf16[512,1664]{1,0:T(8,128)(2,1)}, bf16[512,1664]{1,0:T(8,128)(2,1)}, u32[]{:S(2)}, u32[]{:S(2)}) %collective-permute-start.10) | collective-permute-done | bytes 1703968 | tf_op jit(solution)/shard_map/ppermute | solution.py:457
  111.0 14.8 %whole_products.1.refs_8_ = f32[2,512,1024]{2,1,0:T(8,128)} custom-call(s32[14]{0:T(128)} %stack.114.meta_ref, bf16[128,4096]{1,0:T(8,128)(2,1)} %masked_rows.4.refs_0_, bf16[128,4096]{1,0:T(8,128)(2,1)} %masked_rows.5.refs_1_, bf16[128,4096]{1,0:T(8,128)(2,1)} %masked_rows.6.refs_2_, bf16[128,4096]{1,0:T(8,128)(2,1)} %masked_rows.7.refs_3_, ...), custom_call_target="tpu_custom_call" | custom-call | flops 1000 | bytes 1000 | tf_op jit(solution)/shard_map/whole_products/pallas_call | solution.py:210
  127.0 1.3 collective-permute-start.13
  129.0 3.5 %collective-permute-done.11.refs_10_ = bf16[512,1024]{1,0:T(8,128)(2,1)} collective-permute-done((bf16[512,1024]{1,0:T(8,128)(2,1)}, bf16[512,1024]{1,0:T(8,128)(2,1)}, u32[]{:S(2)}, u32[]{:S(2)}) %collective-permute-start.11) | collective-permute-done | bytes 1048608 | tf_op jit(solution)/shard_map/ppermute | solution.py:457
  132.5 8.2 %half_products.1 = (bf16[256,640]{1,0:T(8,128)(2,1)}, bf16[256,640]{1,0:T(8,128)(2,1)}, bf16[256,640]{1,0:T(8,128)(2,1)}, bf16[256,640]{1,0:T(8,128)(2,1)}, f32[2,512,384]{2,1,0:T(8,128)}) custom-call(s32[9]{0:T(128)} %stack.104.meta_ref, bf16[128,4096]{1,0:T(8,128)(2,1)} %masked_rows.4.refs_0_, bf16[128,4096]{1,0:T(8,128)(2,1)} %masked_rows.5.refs_1_, ...), custom_call_target="tpu_custom_call" | custom-call | flops 1000 | bytes 1000 | tf_op jit(solution)/shard_map/half_products/pallas_call | solution.py:309
  143.3 2.4 %collective-permute-done.13.refs_9_ = bf16[512,768]{1,0:T(8,128)(2,1)S(1)} collective-permute-done((bf16[512,768]{1,0:T(8,128)(2,1)S(1)}, bf16[512,768]{1,0:T(8,128)(2,1)S(1)}, u32[]{:S(2)}, u32[]{:S(2)}) %collective-permute-start.13) | collective-permute-done | bytes 786464 | tf_op jit(solution)/shard_map/ppermute | solution.py:457
  146.5 6.0 %rest_products.1 = (bf16[256,384]{1,0:T(8,128)(2,1)}, bf16[256,384]{1,0:T(8,128)(2,1)}, bf16[256,384]{1,0:T(8,128)(2,1)}, bf16[256,384]{1,0:T(8,128)(2,1)}) custom-call(s32[7]{0:T(128)} %stack.99.meta_ref, bf16[128,4096]{1,0:T(8,128)(2,1)} %masked_rows.4.refs_0_, bf16[128,4096]{1,0:T(8,128)(2,1)} %masked_rows.5.refs_1_, ...), custom_call_target="tpu_custom_call" | custom-call | flops 1000 | bytes 1000 | tf_op jit(solution)/shard_map/rest_products/pallas_call | solution.py:371
  154.8 2.8 %collective-permute-done.19.refs_3_ = bf16[256,640]{1,0:T(8,128)(2,1)S(1)} collective-permute-done((bf16[256,640]{1,0:T(8,128)(2,1)}, bf16[256,640]{1,0:T(8,128)(2,1)S(1)}, u32[]{:S(2)}, u32[]{:S(2)}) %collective-permute-start.19) | collective-permute-done | bytes 327712 | tf_op jit(solution)/shard_map/ppermute | solution.py:533
  157.7 2.0 %assembled.2.refs_4_ = bf16[256,4096]{1,0:T(8,128)(2,1)} custom-call(s32[2]{0:T(128)S(1)} %get-tuple-element.76.place_ref, f32[4,1,4096]{2,1,0:T(1,128)S(1)} %reshape.20.mask_ref, bf16[256,640]{1,0:T(8,128)(2,1)S(1)} %copy-done.2, bf16[256,640]{1,0:T(8,128)(2,1)S(1)} %collective-permute-done.14.refs_1_, ...), custom_call_target="tpu_custom_call" | custom-call | flops 1000 | bytes 1000 | tf_op jit(solution)/shard_map/assembled/pallas_call | solution.py:416
  159.7 3.1 %collective-permute-done.16.refs_2_ = bf16[256,384]{1,0:T(8,128)(2,1)S(1)} collective-permute-done((bf16[256,384]{1,0:T(8,128)(2,1)}, bf16[256,384]{1,0:T(8,128)(2,1)S(1)}, u32[]{:S(2)}, u32[]{:S(2)}) %collective-permute-start.16) | collective-permute-done | bytes 196640 | tf_op jit(solution)/shard_map/ppermute | solution.py:457
  162.8 3.3 %collective-permute-done.17.refs_3_ = bf16[256,384]{1,0:T(8,128)(2,1)S(1)} collective-permute-done((bf16[256,384]{1,0:T(8,128)(2,1)}, bf16[256,384]{1,0:T(8,128)(2,1)S(1)}, u32[]{:S(2)}, u32[]{:S(2)}) %collective-permute-start.17) | collective-permute-done | bytes 196640 | tf_op jit(solution)/shard_map/ppermute | solution.py:533
  166.1 1.6 assembled.3
  (60 shorter events, 19.2 us)
Async XLA Ops:
  0.0 5.6 %copy-start = (bf16[512,4096]{1,0:T(8,128)(2,1)S(1)}, bf16[512,4096]{1,0:T(8,128)(2,1)}, u32[]{:S(2)}) copy-start(bf16[512,4096]{1,0:T(8,128)(2,1)} %w_ref.2) | copy-start | bytes 12582916
  2.5 26.5 %collective-permute-start = (bf16[512,1024]{1,0:T(8,128)(2,1)}, bf16[512,1024]{1,0:T(8,128)(2,1)}, u32[]{:S(2)}, u32[]{:S(2)}) collective-permute-start(bf16[512,1024]{1,0:T(8,128)(2,1)} %b_strips.2), channel_id=1, source_target_pairs={{0,2},{2,0},{4,6},{6,4},{8,10},{10,8},{12,14},{14,12},{1,3},{3,1},... | collective-permute-start | bytes 3145736 | tf_op jit(solution)/shard_map/ppermute | solution.py:457
  5.6 4.0 %copy-start.9 = (s32[8,64]{1,0:T(8,128)S(1)}, s32[8,64]{1,0:T(8,128)}, u32[]{:S(2)}) copy-start(s32[8,64]{1,0:T(8,128)} %param.6) | copy-start | bytes 6148
  6.3 6.4 %copy-start.1 = (bf16[512,1024]{1,0:T(8,128)(2,1)}, bf16[512,1024]{1,0:T(8,128)(2,1)S(1)}, u32[]{:S(2)}) copy-start(bf16[512,1024]{1,0:T(8,128)(2,1)S(1)} %b_strips.3.refs_8_) | copy-start | bytes 3145732
  6.3 24.8 %collective-permute-start.1 = (bf16[512,1024]{1,0:T(8,128)(2,1)S(1)}, bf16[512,1024]{1,0:T(8,128)(2,1)}, u32[]{:S(2)}, u32[]{:S(2)}) collective-permute-start(bf16[512,1024]{1,0:T(8,128)(2,1)S(1)} %b_strips.3.refs_8_), channel_id=1, source_target_pairs={{0,4},{2,6},{4,0},{6,2},{8,12},{10,14},{12,8},{14,10},{1,5},{3,7},... | collective-permute-start | bytes 3145736 | tf_op jit(solution)/shard_map/ppermute | solution.py:457
  8.0 23.1 %collective-permute-start.2 = (bf16[512,1024]{1,0:T(8,128)(2,1)S(1)}, bf16[512,1024]{1,0:T(8,128)(2,1)}, u32[]{:S(2)}, u32[]{:S(2)}) collective-permute-start(bf16[512,1024]{1,0:T(8,128)(2,1)S(1)} %b_strips.3.refs_8_), channel_id=1, source_target_pairs={{4,8},{6,10},{8,4},{10,6},{5,9},{7,11},{9,5},{11,7},{20,24},{22,26... | collective-permute-start | bytes 3145736 | tf_op jit(solution)/shard_map/ppermute | solution.py:457
  12.7 25.3 %copy-start.4 = (bf16[128,4096]{1,0:T(8,128)(2,1)S(1)}, bf16[128,4096]{1,0:T(8,128)(2,1)}, u32[]{:S(2)}) copy-start(bf16[128,4096]{1,0:T(8,128)(2,1)} %masked_rows.5.refs_1_) | copy-start | bytes 3145732
  31.1 26.9 %collective-permute-start.4 = (bf16[512,1024]{1,0:T(8,128)(2,1)}, bf16[512,1024]{1,0:T(8,128)(2,1)}, u32[]{:S(2)}, u32[]{:S(2)}) collective-permute-start(bf16[512,1024]{1,0:T(8,128)(2,1)} %collective-permute-done.refs_9_), channel_id=1, source_target_pairs={{0,4},{2,6},{4,0},{6,2},{8,12},{10,14},{12,8},{14,10},{1,5},{3,7},... | collective-permute-start | bytes 3145736 | tf_op jit(solution)/shard_map/ppermute | solution.py:457
  35.7 24.7 %collective-permute-start.3 = (bf16[512,1024]{1,0:T(8,128)(2,1)}, bf16[512,1024]{1,0:T(8,128)(2,1)}, u32[]{:S(2)}, u32[]{:S(2)}) collective-permute-start(bf16[512,1024]{1,0:T(8,128)(2,1)} %collective-permute-done.refs_9_), channel_id=1, source_target_pairs={{4,8},{6,10},{8,4},{10,6},{5,9},{7,11},{9,5},{11,7},{20,24},{22,26... | collective-permute-start | bytes 3145736 | tf_op jit(solution)/shard_map/ppermute | solution.py:457
  37.4 30.8 %collective-permute-start.6 = (bf16[128,4096]{1,0:T(8,128)(2,1)}, bf16[128,4096]{1,0:T(8,128)(2,1)S(1)}, u32[]{:S(2)}, u32[]{:S(2)}) collective-permute-start(bf16[128,4096]{1,0:T(8,128)(2,1)} %masked_rows.4.refs_0_), channel_id=1, source_target_pairs={{0,2},{2,0},{4,6},{6,4},{8,10},{10,8},{12,14},{14,12},{1,3},{3,1},... | collective-permute-start | bytes 3145736 | tf_op jit(solution)/shard_map/ppermute | solution.py:457
  38.0 45.4 %collective-permute-start.7 = (bf16[128,4096]{1,0:T(8,128)(2,1)S(1)}, bf16[128,4096]{1,0:T(8,128)(2,1)S(1)}, u32[]{:S(2)}, u32[]{:S(2)}) collective-permute-start(bf16[128,4096]{1,0:T(8,128)(2,1)S(1)} %copy-done.4), channel_id=1, source_target_pairs={{0,2},{2,0},{4,6},{6,4},{8,10},{10,8},{12,14},{14,12},{1,3},{3,1},... | collective-permute-start | bytes 3145736 | tf_op jit(solution)/shard_map/ppermute | solution.py:457
  65.2 18.2 %collective-permute-start.5 = (bf16[512,1024]{1,0:T(8,128)(2,1)S(1)}, bf16[512,1024]{1,0:T(8,128)(2,1)}, u32[]{:S(2)}, u32[]{:S(2)}) collective-permute-start(bf16[512,1024]{1,0:T(8,128)(2,1)S(1)} %get-tuple-element.49), channel_id=1, source_target_pairs={{4,8},{6,10},{8,4},{10,6},{5,9},{7,11},{9,5},{11,7},{20,24},{22,26... | collective-permute-start | bytes 3145736 | tf_op jit(solution)/shard_map/ppermute | solution.py:457
  66.9 43.2 %collective-permute-start.10 = (bf16[512,1664]{1,0:T(8,128)(2,1)}, bf16[512,1664]{1,0:T(8,128)(2,1)}, u32[]{:S(2)}, u32[]{:S(2)}) collective-permute-start(bf16[512,1664]{1,0:T(8,128)(2,1)} %pad_maximum_fusion), channel_id=1, source_target_pairs={{4,0},{6,2},{8,12},{10,14},{5,1},{7,3},{9,13},{11,15},{20,16},{22,... | collective-permute-start | bytes 5111816 | tf_op jit(solution)/shard_map/ppermute | solution.py:457
  68.2 20.9 %copy-start.5 = (bf16[128,4096]{1,0:T(8,128)(2,1)}, bf16[128,4096]{1,0:T(8,128)(2,1)S(1)}, u32[]{:S(2)}) copy-start(bf16[128,4096]{1,0:T(8,128)(2,1)S(1)} %collective-permute-done.6.refs_4_) | copy-start | bytes 3145732
  83.5 5.6 %copy-start.6 = (bf16[128,4096]{1,0:T(8,128)(2,1)}, bf16[128,4096]{1,0:T(8,128)(2,1)S(1)}, u32[]{:S(2)}) copy-start(bf16[128,4096]{1,0:T(8,128)(2,1)S(1)} %collective-permute-done.7.refs_5_) | copy-start | bytes 3145732
  83.5 26.6 %collective-permute-start.8 = (bf16[128,4096]{1,0:T(8,128)(2,1)S(1)}, bf16[128,4096]{1,0:T(8,128)(2,1)S(1)}, u32[]{:S(2)}, u32[]{:S(2)}) collective-permute-start(bf16[128,4096]{1,0:T(8,128)(2,1)S(1)} %collective-permute-done.6.refs_4_), channel_id=1, source_target_pairs={{0,1},{1,0},{2,3},{3,2},{4,5},{5,4},{6,7},{7,6},{8,9},{9,8},{10,11... | collective-permute-start | bytes 3145736 | tf_op jit(solution)/shard_map/ppermute | solution.py:501
  83.5 26.6 %collective-permute-start.9 = (bf16[128,4096]{1,0:T(8,128)(2,1)S(1)}, bf16[128,4096]{1,0:T(8,128)(2,1)}, u32[]{:S(2)}, u32[]{:S(2)}) collective-permute-start(bf16[128,4096]{1,0:T(8,128)(2,1)S(1)} %collective-permute-done.7.refs_5_), channel_id=1, source_target_pairs={{0,1},{1,0},{2,3},{3,2},{4,5},{5,4},{6,7},{7,6},{8,9},{9,8},{10,11... | collective-permute-start | bytes 3145736 | tf_op jit(solution)/shard_map/ppermute | solution.py:501
  84.0 41.8 %collective-permute-start.12 = (bf16[512,1024]{1,0:T(8,128)(2,1)}, bf16[512,1024]{1,0:T(8,128)(2,1)}, u32[]{:S(2)}, u32[]{:S(2)}) collective-permute-start(bf16[512,1024]{1,0:T(8,128)(2,1)} %get-tuple-element.56), channel_id=1, source_target_pairs={{4,8},{6,10},{8,4},{10,6},{5,9},{7,11},{9,5},{11,7},{20,24},{22,26... | collective-permute-start | bytes 3145736 | tf_op jit(solution)/shard_map/ppermute | solution.py:457
  85.6 46.9 %collective-permute-start.11 = (bf16[512,1024]{1,0:T(8,128)(2,1)}, bf16[512,1024]{1,0:T(8,128)(2,1)}, u32[]{:S(2)}, u32[]{:S(2)}) collective-permute-start(bf16[512,1024]{1,0:T(8,128)(2,1)} %collective-permute-done.5.refs_9_), channel_id=1, source_target_pairs={{4,0},{6,2},{8,12},{10,14},{5,1},{7,3},{9,13},{11,15},{20,16},{22,... | collective-permute-start | bytes 3145736 | tf_op jit(solution)/shard_map/ppermute | solution.py:457
  110.0 1.0 copy-start.7
  127.0 18.6 %collective-permute-start.13 = (bf16[512,768]{1,0:T(8,128)(2,1)S(1)}, bf16[512,768]{1,0:T(8,128)(2,1)S(1)}, u32[]{:S(2)}, u32[]{:S(2)}) collective-permute-start(bf16[512,768]{1,0:T(8,128)(2,1)S(1)} %pad_maximum_fusion.3), channel_id=1, source_target_pairs={{4,0},{6,2},{8,12},{10,14},{5,1},{7,3},{9,13},{11,15},{20,16},{22,... | collective-permute-start | bytes 2359304 | tf_op jit(solution)/shard_map/ppermute | solution.py:457
  140.7 2.6 %collective-permute-start.14 = (bf16[256,640]{1,0:T(8,128)(2,1)}, bf16[256,640]{1,0:T(8,128)(2,1)S(1)}, u32[]{:S(2)}, u32[]{:S(2)}) collective-permute-start(bf16[256,640]{1,0:T(8,128)(2,1)} %get-tuple-element.59), channel_id=1, source_target_pairs={{0,1},{1,0},{2,3},{3,2},{4,5},{5,4},{6,7},{7,6},{8,9},{9,8},{10,11... | collective-permute-start | bytes 983048 | tf_op jit(solution)/shard_map/ppermute | solution.py:531
  140.7 14.1 %collective-permute-start.18 = (bf16[256,640]{1,0:T(8,128)(2,1)}, bf16[256,640]{1,0:T(8,128)(2,1)S(1)}, u32[]{:S(2)}, u32[]{:S(2)}) collective-permute-start(bf16[256,640]{1,0:T(8,128)(2,1)} %get-tuple-element.67), channel_id=1, source_target_pairs={{0,2},{2,0},{4,6},{6,4},{8,10},{10,8},{12,14},{14,12},{1,3},{3,1},... | collective-permute-start | bytes 983048 | tf_op jit(solution)/shard_map/ppermute | solution.py:457
  141.7 16.0 %collective-permute-start.19 = (bf16[256,640]{1,0:T(8,128)(2,1)}, bf16[256,640]{1,0:T(8,128)(2,1)S(1)}, u32[]{:S(2)}, u32[]{:S(2)}) collective-permute-start(bf16[256,640]{1,0:T(8,128)(2,1)} %get-tuple-element.68), channel_id=1, source_target_pairs={{0,3},{1,2},{2,1},{3,0},{4,7},{5,6},{6,5},{7,4},{8,11},{9,10},{10,... | collective-permute-start | bytes 983048 | tf_op jit(solution)/shard_map/ppermute | solution.py:533
  145.6 0.9 copy-start.8
  146.5 8.0 %copy-start.10 = (s32[4,64]{1,0:T(4,128)S(1)}, s32[4,64]{1,0:T(4,128)}, u32[]{:S(2)}) copy-start(s32[4,64]{1,0:T(4,128)} %param.7) | copy-start | bytes 3076
  146.5 11.1 %copy-start.2 = (bf16[256,640]{1,0:T(8,128)(2,1)S(1)}, bf16[256,640]{1,0:T(8,128)(2,1)}, u32[]{:S(2)}) copy-start(bf16[256,640]{1,0:T(8,128)(2,1)} %get-tuple-element.65.refs_0_) | copy-start | bytes 983044
  152.6 13.5 %copy-start.3 = (bf16[256,384]{1,0:T(8,128)(2,1)S(1)}, bf16[256,384]{1,0:T(8,128)(2,1)}, u32[]{:S(2)}) copy-start(bf16[256,384]{1,0:T(8,128)(2,1)} %get-tuple-element.61.refs_0_) | copy-start | bytes 589828
  152.6 7.1 %collective-permute-start.15 = (bf16[256,384]{1,0:T(8,128)(2,1)}, bf16[256,384]{1,0:T(8,128)(2,1)S(1)}, u32[]{:S(2)}, u32[]{:S(2)}) collective-permute-start(bf16[256,384]{1,0:T(8,128)(2,1)} %get-tuple-element.62), channel_id=1, source_target_pairs={{0,1},{1,0},{2,3},{3,2},{4,5},{5,4},{6,7},{7,6},{8,9},{9,8},{10,11... | collective-permute-start | bytes 589832 | tf_op jit(solution)/shard_map/ppermute | solution.py:531
  152.7 10.1 %collective-permute-start.16 = (bf16[256,384]{1,0:T(8,128)(2,1)}, bf16[256,384]{1,0:T(8,128)(2,1)S(1)}, u32[]{:S(2)}, u32[]{:S(2)}) collective-permute-start(bf16[256,384]{1,0:T(8,128)(2,1)} %get-tuple-element.63), channel_id=1, source_target_pairs={{0,2},{2,0},{4,6},{6,4},{8,10},{10,8},{12,14},{14,12},{1,3},{3,1},... | collective-permute-start | bytes 589832 | tf_op jit(solution)/shard_map/ppermute | solution.py:457
  153.8 12.3 %collective-permute-start.17 = (bf16[256,384]{1,0:T(8,128)(2,1)}, bf16[256,384]{1,0:T(8,128)(2,1)S(1)}, u32[]{:S(2)}, u32[]{:S(2)}) collective-permute-start(bf16[256,384]{1,0:T(8,128)(2,1)} %get-tuple-element.64), channel_id=1, source_target_pairs={{0,3},{1,2},{2,1},{3,0},{4,7},{5,6},{6,5},{7,4},{8,11},{9,10},{10,... | collective-permute-start | bytes 589832 | tf_op jit(solution)/shard_map/ppermute | solution.py:533

commit v8 on v7

--- a/solution.py
+++ b/solution.py
@@ -93,6 +93,41 @@
     )(jnp.stack(quarters), w_band)
 
 
+def pack_kernel(plan, n_in, meta_ref, *refs):
+    sources, outs, sems = refs[:n_in], refs[n_in:-1], refs[-1]
+
+    def on_each(do):
+        for k, (source, start, count, out, to, when) in enumerate(plan):
+            at = start * LANES if isinstance(start, int) else pl.multiple_of(meta_ref[start[0]] * LANES, LANES)
+            copy = pltpu.make_async_copy(
+                sources[source].at[:, pl.ds(at, count * LANES)],
+                outs[out].at[:, to * LANES : (to + count) * LANES],
+                sems.at[k],
+            )
+            if when is None:
+                do(copy)
+            else:
+                pl.when(meta_ref[when[0]] == when[1])(functools.partial(do, copy))
+
+    on_each(lambda copy: copy.start())
+    on_each(lambda copy: copy.wait())
+
+
+def packed(meta, sources, widths, plan):
+    rows = sources[0].shape[0]
+    any_spec = pl.BlockSpec(memory_space=pl.ANY)
+    return pl.pallas_call(
+        functools.partial(pack_kernel, plan, len(sources)),
+        out_shape=[jax.ShapeDtypeStruct((rows, width * LANES), jnp.bfloat16) for width in widths],
+        in_specs=[pl.BlockSpec(memory_space=pltpu.SMEM)] + [any_spec] * len(sources),
+        out_specs=[any_spec] * len(widths),
+        scratch_shapes=[pltpu.SemaphoreType.DMA((len(plan),))],
+        compiler_params=pltpu.CompilerParams(vmem_limit_bytes=59 * MIB),
+        cost_estimate=SMALL,
+        name="packed",
+    )(jnp.stack(meta).astype(jnp.int32), *sources)
+
+
 def mask_kernel(first_ref, mask_ref, x_ref, out_ref):
     out_ref[...] = (x_ref[...].astype(jnp.float32) * mask_ref[0]).astype(jnp.bfloat16)
 
@@ -137,14 +172,9 @@
     return copies
 
 
-def add_products(acc, xv, p, strips, offset_of, start):
-    def step(g, carry):
-        at = (offset_of(p, g) + start) * LANES
-        cols = pl.ds(pl.multiple_of(at, LANES), strips.shape[1])
-        acc[g, :, cols] += jnp.dot(xv[p, g], strips[...], preferred_element_type=jnp.float32)
-        return carry
-
-    lax.fori_loop(0, 2, step, 0)
+def add_product(acc, x, strips, g, first):
+    cols = pl.ds(pl.multiple_of(first * LANES, LANES), strips.shape[1])
+    acc[g, :, cols] += jnp.dot(x, strips, preferred_element_type=jnp.float32)
 
 
 def whole_kernel(plan, meta_ref, *refs):
@@ -191,7 +221,12 @@
             on_each(k, lambda copy: copy.wait())
         for r in range(PARTS):
             copies[p, r].wait()
-        add_products(acc, xv, p, bv.at[p], offset_of, 0)
+
+        def step(g, carry):
+            add_product(acc, xv[p, g], bv[p], g, offset_of(p, g))
+            return carry
+
+        lax.fori_loop(0, 2, step, 0)
     outs = [
         pltpu.make_async_copy(acc.at[g, :, low : low + quarter], out_ref.at[g], out_sems.at[g]) for g in range(2)
     ]
@@ -226,19 +261,39 @@
     )(meta, *xs, *operands)
 
 
-def give_pieces(out_refs, acc, at):
+def finish(acc, wait_for, add, at, out_refs, pieces, sems, also=None):
     half, width = out_refs[0].shape
     cols = pl.ds(pl.multiple_of(at * LANES, LANES), width)
-    for r in range(4):
-        rows = slice((r % 2) * half, (r % 2 + 1) * half)
-        out_refs[r][...] = acc[r // 2, rows, cols].astype(jnp.bfloat16)
+    outs = [pltpu.make_async_copy(pieces.at[r], out_refs[r], sems.at[r]) for r in range(4)]
+    also = also or []
+
+    def step(g, carry):
+        for k in range(2):
+            pl.when(g == k)(functools.partial(wait_for, k))
+        add(g)
+        for k in range(2):
+
+            @pl.when(g == k)
+            def _():
+                for copy in also[k : k + 1]:
+                    copy.start()
+                for r in range(2 * k, 2 * k + 2):
+                    rows = slice((r % 2) * half, (r % 2 + 1) * half)
+                    pieces[r] = acc[k, rows, cols].astype(jnp.bfloat16)
+                    outs[r].start()
+
+        return carry
+
+    lax.fori_loop(0, 2, step, 0)
+    for copy in outs + also:
+        copy.wait()
 
 
 def half_kernel(meta_ref, *refs):
     x_refs, (prev_ref, middle_ref, end_ref, second_ref), refs = refs[:PARTS], refs[PARTS : PARTS + 4], refs[PARTS + 4 :]
-    out_refs, rest_ref, xv, bv, acc, x_sems, b_sems, prev_sem, rest_sem = refs[:4], *refs[4:]
-    half = bv.shape[2]
-    quarter = 2 * half
+    out_refs, rest_ref, xv, bv, acc, pieces, x_sems, b_sems, prev_sems, rest_sems, out_sems = refs[:4], *refs[4:]
+    quarter = bv.shape[2]
+    half = quarter // 2
     low = quarter // 2
     band = quarter // LANES
     is_end = meta_ref[0]
@@ -246,58 +301,55 @@
     def offset_of(p, g):
         return meta_ref[5 + 2 * p + g]
 
-    copies = x_copies(x_refs, xv, x_sems, offset_of)
-
-    def b_copies(ref, first):
-        return [
-            pltpu.make_async_copy(ref.at[:, p * half : (p + 1) * half], bv.at[first + p], b_sems.at[first + p])
-            for p in range(2)
-        ]
-
-    middle = b_copies(middle_ref, 0) + b_copies(second_ref, 2)
-    end = b_copies(end_ref, 0)
-    prev = pltpu.make_async_copy(prev_ref, acc.at[:, :, low : low + quarter], prev_sem)
-    prev.start()
+    x_loads = x_copies(x_refs, xv, x_sems, offset_of)
+    middle = pltpu.make_async_copy(middle_ref, bv.at[0], b_sems.at[0])
+    end = pltpu.make_async_copy(end_ref, bv.at[0], b_sems.at[0])
+    second = pltpu.make_async_copy(second_ref, bv.at[1], b_sems.at[1])
+    prev = [
+        pltpu.make_async_copy(prev_ref.at[g], acc.at[g, :, low : low + quarter], prev_sems.at[g]) for g in range(2)
+    ]
+    at = pl.multiple_of((meta_ref[4] + band // 2) * LANES, LANES)
+    rest = [
+        pltpu.make_async_copy(acc.at[g, :, pl.ds(at, rest_ref.shape[2])], rest_ref.at[g], rest_sems.at[g])
+        for g in range(2)
+    ]
 
     @pl.when(is_end == 0)
     def _():
-        for copy in middle:
+        middle.start()
+        second.start()
+
+    pl.when(is_end != 0)(end.start)
+
+    def rows_loads(g):
+        return [prev[g]] + [copy for (_, r), copy in x_loads.items() if r // (PARTS // 2) == g]
+
+    for g in range(2):
+        for copy in rows_loads(g):
             copy.start()
 
-    @pl.when(is_end != 0)
-    def _():
-        for copy in end:
-            copy.start()
-
-    for copy in copies.values():
-        copy.start()
-
-    @pl.when(is_end == 0)
-    def _():
-        for copy in middle:
+    def wait_for(g):
+        for copy in rows_loads(g):
             copy.wait()
-
-    @pl.when(is_end != 0)
-    def _():
-        for copy in end:
-            copy.wait()
-
-    for copy in copies.values():
-        copy.wait()
-    prev.wait()
-    for p in range(2):
-        add_products(acc, xv, p, bv.at[p], offset_of, meta_ref[1])
-
-    @pl.when(is_end == 0)
-    def _():
+        if g == 0:
+
+            @pl.when(is_end == 0)
+            def _():
+                middle.wait()
+                second.wait()
+
+            pl.when(is_end != 0)(end.wait)
+
+    def add(g):
         for p in range(2):
-            add_products(acc, xv, p, bv.at[2 + p], offset_of, meta_ref[2])
-
-    at = pl.multiple_of((meta_ref[4] + band // 2) * LANES, LANES)
-    rest = pltpu.make_async_copy(acc.at[:, :, pl.ds(at, rest_ref.shape[2])], rest_ref, rest_sem)
-    rest.start()
-    give_pieces(out_refs, acc, meta_ref[3] + band // 2)
-    rest.wait()
+            add_product(acc, xv[p, g], bv[0, :, p * half : (p + 1) * half], g, offset_of(p, g) + meta_ref[1])
+
+        @pl.when(is_end == 0)
+        def _():
+            for p in range(2):
+                add_product(acc, xv[p, g], bv[1, :, p * half : (p + 1) * half], g, offset_of(p, g) + meta_ref[2])
+
+    finish(acc, wait_for, add, meta_ref[3] + band // 2, out_refs, pieces, out_sems, rest)
 
 
 def half_products(meta, xs, prev, middle, end, second, n_done):
@@ -311,15 +363,17 @@
         out_shape=[jax.ShapeDtypeStruct((rows, n_done * LANES), jnp.bfloat16)] * 4
         + [jax.ShapeDtypeStruct((2, 2 * rows, n_rest * LANES), jnp.float32)],
         in_specs=[pl.BlockSpec(memory_space=pltpu.SMEM)] + [x_spec] * PARTS + [any_spec] * 4,
-        out_specs=[pl.BlockSpec(memory_space=pltpu.VMEM)] * 4 + [any_spec],
+        out_specs=[any_spec] * 5,
         scratch_shapes=[
             pltpu.VMEM((2, 2, 2 * rows, panel), jnp.bfloat16),
-            pltpu.VMEM((4, panel, quarter // 2), jnp.bfloat16),
+            pltpu.VMEM((2, panel, quarter), jnp.bfloat16),
             pltpu.VMEM((2, 2 * rows, 2 * quarter), jnp.float32),
+            pltpu.VMEM((4, rows, n_done * LANES), jnp.bfloat16),
             pltpu.SemaphoreType.DMA((2, PARTS)),
+            pltpu.SemaphoreType.DMA((2,)),
+            pltpu.SemaphoreType.DMA((2,)),
+            pltpu.SemaphoreType.DMA((2,)),
             pltpu.SemaphoreType.DMA((4,)),
-            pltpu.SemaphoreType.DMA,
-            pltpu.SemaphoreType.DMA,
         ],
         compiler_params=pltpu.CompilerParams(vmem_limit_bytes=59 * MIB),
         cost_estimate=SMALL,
@@ -329,7 +383,7 @@
 
 def rest_kernel(meta_ref, *refs):
     x_refs, (rest_ref, b_ref), refs = refs[:PARTS], refs[PARTS : PARTS + 2], refs[PARTS + 2 :]
-    out_refs, xv, bv, acc, x_sems, b_sem, rest_sem = refs[:4], *refs[4:]
+    out_refs, xv, bv, acc, pieces, x_sems, b_sem, rest_sems, out_sems = refs[:4], *refs[4:]
     band = acc.shape[2] // (2 * LANES)
     half = bv.shape[1] // 2
     is_end = meta_ref[0]
@@ -338,28 +392,42 @@
         return meta_ref[3 + 2 * p + g]
 
     at = pl.multiple_of((meta_ref[2] + band // 2) * LANES, LANES)
-    rest = pltpu.make_async_copy(rest_ref, acc.at[:, :, pl.ds(at, rest_ref.shape[2])], rest_sem)
-    rest.start()
-    copies = x_copies(x_refs, xv, x_sems, offset_of)
+    rest = [
+        pltpu.make_async_copy(rest_ref.at[g], acc.at[g, :, pl.ds(at, rest_ref.shape[2])], rest_sems.at[g])
+        for g in range(2)
+    ]
+    x_loads = x_copies(x_refs, xv, x_sems, offset_of)
     b_copy = pltpu.make_async_copy(b_ref, bv, b_sem)
 
-    @pl.when(is_end != 0)
-    def _():
-        b_copy.start()
-        for copy in copies.values():
-            copy.start()
-
-    rest.wait()
-
-    @pl.when(is_end != 0)
-    def _():
-        b_copy.wait()
-        for copy in copies.values():
-            copy.wait()
-        for p in range(2):
-            add_products(acc, xv, p, bv.at[:, p * half : (p + 1) * half], offset_of, meta_ref[1])
-
-    give_pieces(out_refs, acc, meta_ref[2] + band // 2)
+    def x_loads_of(g):
+        return [copy for (_, r), copy in x_loads.items() if r // (PARTS // 2) == g]
+
+    pl.when(is_end != 0)(b_copy.start)
+    for g in range(2):
+        rest[g].start()
+
+        @pl.when(is_end != 0)
+        def _():
+            for copy in x_loads_of(g):
+                copy.start()
+
+    def wait_for(g):
+        rest[g].wait()
+
+        @pl.when(is_end != 0)
+        def _():
+            for copy in x_loads_of(g):
+                copy.wait()
+            if g == 0:
+                b_copy.wait()
+
+    def add(g):
+        @pl.when(is_end != 0)
+        def _():
+            for p in range(2):
+                add_product(acc, xv[p, g], bv[:, p * half : (p + 1) * half], g, offset_of(p, g) + meta_ref[1])
+
+    finish(acc, wait_for, add, meta_ref[2] + band // 2, out_refs, pieces, out_sems)
 
 
 def rest_products(meta, xs, rest, b, quarter):
@@ -372,14 +440,16 @@
         rest_kernel,
         out_shape=[jax.ShapeDtypeStruct((rows, width), jnp.bfloat16)] * 4,
         in_specs=[pl.BlockSpec(memory_space=pltpu.SMEM)] + [x_spec] * PARTS + [any_spec] * 2,
-        out_specs=[pl.BlockSpec(memory_space=pltpu.VMEM)] * 4,
+        out_specs=[any_spec] * 4,
         scratch_shapes=[
             pltpu.VMEM((2, 2, 2 * rows, panel), jnp.bfloat16),
             pltpu.VMEM(b.shape, jnp.bfloat16),
             pltpu.VMEM((2, 2 * rows, 2 * quarter), jnp.float32),
+            pltpu.VMEM((4, rows, width), jnp.bfloat16),
             pltpu.SemaphoreType.DMA((2, PARTS)),
             pltpu.SemaphoreType.DMA,
-            pltpu.SemaphoreType.DMA,
+            pltpu.SemaphoreType.DMA((2,)),
+            pltpu.SemaphoreType.DMA((4,)),
         ],
         compiler_params=pltpu.CompilerParams(vmem_limit_bytes=59 * MIB),
         cost_estimate=SMALL,
@@ -456,9 +526,6 @@
     def line(value, pairs):
         return lax.ppermute(value, "grid", pairs)
 
-    def strips(value, start, count):
-        return lax.dynamic_slice_in_dim(value, start * LANES, count * LANES, 1)
-
     first_out, second_out = jnp.where(left, 0, 4), jnp.where(left, 4, 0)
     first_in, second_in = second_out, first_out
     last_in = jnp.where(left, 1, 4)
@@ -474,25 +541,26 @@
     x_mine = [masked_rows(x_band, mask_wide, c * rows // 2 + k * rows // 4, rows // 4) for k in range(2)]
     own_b, *x_mine = together(own_b, *x_mine)
     own_b, swap_a = together(own_b, swap_a)
+    swap_b = line(own_b, swap)
     own_b, cross_a = together(own_b, cross_a)
-    swap_b = line(own_b, swap)
     cross_b = line(own_b, cross)
     x_across = [line(part, across) for part in x_mine]
     x_rest = [masked_rows(x_band, mask_wide, (1 - c) * rows // 2 + k * rows // 4, rows // 4) for k in range(2)]
 
-    cross_a, cross_b = together(cross_a, cross_b)
-    mid_b = jnp.concatenate(
+    mid_b, fwd_first = packed(
+        [y, first_out],
+        [cross_a, cross_b, swap_a, swap_b],
+        [13, 8],
         [
-            jnp.where(y == 0, cross_a[:, : 3 * LANES], cross_b[:, : 3 * LANES]),
-            cross_a[:, 3 * LANES :],
-            cross_b[:, 3 * LANES :],
+            (0, 0, 3, 0, 0, (0, 0)),
+            (1, 0, 3, 0, 0, (0, 1)),
+            (0, 3, 5, 0, 3, None),
+            (1, 3, 5, 0, 8, None),
+            (2, (1,), 4, 1, 0, None),
+            (3, (1,), 4, 1, 4, None),
         ],
-        1,
     )
-    fwd_first = jnp.concatenate([strips(v, first_out, 4) for v in (swap_a, swap_b)], 1)
-    fwd_second = jnp.concatenate([strips(v, second_out, 4) for v in (swap_a, swap_b)], 1)
-    fwd_first, fwd_second = together(fwd_first, fwd_second)
-    mid_b, fwd_first, fwd_second = together(mid_b, fwd_first, fwd_second)
+    (fwd_second,) = packed([second_out], [swap_a, swap_b], [8], [(0, (0,), 4, 0, 0, None), (1, (0,), 4, 0, 4, None)])
     mid_b = line(mid_b, outward)
     fwd_first = line(fwd_first, cross)
     fwd_first, fwd_second, *x_across = together(fwd_first, fwd_second, *x_across)
@@ -520,8 +588,8 @@
     total = whole_products(meta, xs, [own_a, own_b, cross_a, cross_b, swap_a, swap_b, mid_b], plan)
     last_at = jnp.where(left, 1, 0)
     total, last_at = together(total, last_at)
-    last = jnp.concatenate(
-        [strips(fwd_second, last_at, 3), strips(fwd_second, last_at + 4, 3)], 1
+    (last,) = packed(
+        [last_at, last_at + 4], [fwd_second], [6], [(0, (0,), 3, 0, 0, None), (0, (1,), 3, 0, 3, None)]
     )
     far_second = line(last, outward)
 

time: 168 us -> 277 us (1.65)
  Pallas kernels: 44.6 us -> 186 us
  waiting for transfers between devices: 81.9 us -> 61.5 us
  local copies, waits for them, and re-layouts: 10.9 us -> 4.9 us
  starting transfers between devices: 26.1 us -> 23.1 us
    pallas_call x0 -> x3, Pallas kernels: none -> 144 us  [packed(): pl.pallas_call(functools.partial(pack_kernel, plan, len(sources)), out_sh...]
    ppermute x14, waiting for transfers between devices: 75.8 us -> 58.2 us  [line(): return lax.ppermute(value, 'grid', pairs)]
    dynamic_slice x3 -> x0, local copies, waits for them, and re-layouts: 3.74 us -> none  [strips(): return lax.dynamic_slice_in_dim(value, start * LANES, count * LANES, 1)]
    ppermute x14, starting transfers between devices: 23.7 us -> 20.7 us  [line(): return lax.ppermute(value, 'grid', pairs)]
    ppermute x2, waiting for transfers between devices: 6.11 us -> 3.31 us  [exchanged(): lax.ppermute(pieces[3], ('grid', 'depth'), opposite)]
  transfers between devices with their start and end apart: 20 -> 20, of which waited for: 10 -> 7; matrix products, arithmetic and copies ran while one was open for 8% -> 2% of each run, Pallas kernels for 24% -> 66%
where the time goes in v8:
time: 277 us
  Pallas kernels  186 us (67%)
  waiting for transfers between devices  61.5 us (22%)
  starting transfers between devices  23.1 us (8%)
  local copies, waits for them, and re-layouts  4.9 us (2%)
    pallas_call x3, Pallas kernels, packed(): pl.pallas_call(functools.partial(pack_kernel, plan, len(sources)), out_sh...  144 us
    ppermute x14, waiting for transfers between devices, line(): return lax.ppermute(value, 'grid', pairs)  58.2 us
    ppermute x14, starting transfers between devices, line(): return lax.ppermute(value, 'grid', pairs)  20.7 us
    pallas_call x1, Pallas kernels, whole_products(): pl.pallas_call(functools.partial(whole_kernel, plan), out_shape=jax.Shape...  14.7 us
    pallas_call x4, Pallas kernels, masked_rows(): pl.pallas_call(mask_kernel, grid_spec=pltpu.PrefetchScalarGridSpec(num_sc...  8.81 us
    pallas_call x1, Pallas kernels, half_products(): pl.pallas_call(half_kernel, out_shape=[jax.ShapeDtypeStruct((rows, n_done...  6.16 us
  transfers between devices with their start and end apart: 20, of which 7 were waited for; matrix products, arithmetic and copies ran while one was open for 2% of the time, Pallas kernels for 66%

profile of v8, /device:TPU:0, one launch (start us, length us, event | category | flops | bytes accessed | tf_op | source)
XLA Modules:
  0.0 276.9 jit_solution(16960269029306849778)
XLA Ops:
  0.0 2.5 b_strips.2
  2.5 3.0 %collective-permute-start = (bf16[512,1024]{1,0:T(8,128)(2,1)}, bf16[512,1024]{1,0:T(8,128)(2,1)}, u32[]{:S(2)}, u32[]{:S(2)}) collective-permute-start(bf16[512,1024]{1,0:T(8,128)(2,1)} %b_strips.2), channel_id=1, source_target_pairs={{0,2},{2,0},{4,6},{6,4},{8,10},{10,8},{12,14},{14,12},{1,3},{3,1},... | collective-permute-start | bytes 3145736 | tf_op jit(solution)/shard_map/ppermute | solution.py:527
  6.3 1.6 collective-permute-start.1
  8.0 1.6 collective-permute-start.2
  10.6 2.1 masked_rows.5.refs_1_
  12.7 2.3 masked_rows.4.refs_0_
  15.0 14.1 %collective-permute-done.refs_9_ = bf16[512,1024]{1,0:T(8,128)(2,1)} collective-permute-done((bf16[512,1024]{1,0:T(8,128)(2,1)}, bf16[512,1024]{1,0:T(8,128)(2,1)}, u32[]{:S(2)}, u32[]{:S(2)}) %collective-permute-start) | collective-permute-done | bytes 1048608 | tf_op jit(solution)/shard_map/ppermute | solution.py:527
  29.1 2.0 collective-permute-done.1.refs_2_.refs_0_.refs_12_
  31.1 1.6 collective-permute-start.4
  32.7 1.7 collective-permute-start.3
  35.7 1.4 collective-permute-start.7
  37.0 18.1 %collective-permute-done.4.refs_3_.refs_1_.refs_13_ = bf16[512,1024]{1,0:T(8,128)(2,1)} collective-permute-done((bf16[512,1024]{1,0:T(8,128)(2,1)}, bf16[512,1024]{1,0:T(8,128)(2,1)}, u32[]{:S(2)}, u32[]{:S(2)}) %collective-permute-start.4) | collective-permute-done | bytes 1048608 | tf_op jit(solution)/shard_map/ppermute | solution.py:527
  55.1 85.2 %packed.3 = (bf16[512,1664]{1,0:T(8,128)(2,1)}, bf16[512,1024]{1,0:T(8,128)(2,1)}) custom-call(s32[2]{0:T(128)} %pad_add_fusion.1.meta_ref, bf16[512,1024]{1,0:T(8,128)(2,1)} %collective-permute-done.2.refs_0_.refs_10_, bf16[512,1024]{1,0:T(8,128)(2,1)} %collective-permute-done.3.refs_1_.refs_11_, ...), custom_call_target="tpu_custom_call" | custom-call | flops 1000 | bytes 1000 | tf_op jit(solution)/shard_map/packed/pallas_call | solution.py:119
  140.3 1.6 collective-permute-start.5
  142.0 1.3 collective-permute-start.10
  143.3 32.9 %packed.4 = bf16[512,1024]{1,0:T(8,128)(2,1)} custom-call(s32[1]{0:T(128)} %bitcast.14.meta_ref, bf16[512,1024]{1,0:T(8,128)(2,1)} %collective-permute-done.1.refs_2_.refs_0_.refs_12_, bf16[512,1024]{1,0:T(8,128)(2,1)} %collective-permute-done.4.refs_3_.refs_1_.refs_13_), custom_call_target="tpu_custom_call" | custom-call | flops 1000 | bytes 1000 | tf_op jit(solution)/shard_map/packed/pallas_call | solution.py:119
  176.8 1.6 collective-permute-start.12
  178.4 1.3 collective-permute-start.11
  179.7 2.2 masked_rows.7.refs_3_
  181.9 2.2 masked_rows.6.refs_2_
  184.7 1.5 collective-permute-done.10.refs_14_
  187.2 14.7 %whole_products.1.refs_8_ = f32[2,512,1024]{2,1,0:T(8,128)} custom-call(s32[14]{0:T(128)} %stack.133.meta_ref, bf16[128,4096]{1,0:T(8,128)(2,1)} %masked_rows.4.refs_0_, bf16[128,4096]{1,0:T(8,128)(2,1)} %masked_rows.5.refs_1_, bf16[128,4096]{1,0:T(8,128)(2,1)} %masked_rows.6.refs_2_, bf16[128,4096]{1,0:T(8,128)(2,1)} %masked_rows.7.refs_3_, ...), custom_call_target="tpu_custom_call" | custom-call | flops 1000 | bytes 1000 | tf_op jit(solution)/shard_map/whole_products/pallas_call | solution.py:245
  202.6 25.6 %packed.5 = bf16[512,768]{1,0:T(8,128)(2,1)} custom-call(s32[2]{0:T(128)} %pad_add_fusion.2.meta_ref, bf16[512,1024]{1,0:T(8,128)(2,1)} %collective-permute-done.12.refs_11_.refs_0_), custom_call_target="tpu_custom_call" | custom-call | flops 1000 | bytes 1000 | tf_op jit(solution)/shard_map/packed/pallas_call | solution.py:119
  228.2 1.3 collective-permute-start.13
  230.2 6.2 %half_products.1 = (bf16[256,640]{1,0:T(8,128)(2,1)}, bf16[256,640]{1,0:T(8,128)(2,1)}, bf16[256,640]{1,0:T(8,128)(2,1)}, bf16[256,640]{1,0:T(8,128)(2,1)}, f32[2,512,384]{2,1,0:T(8,128)}) custom-call(s32[9]{0:T(128)} %stack.123.meta_ref, bf16[128,4096]{1,0:T(8,128)(2,1)} %masked_rows.4.refs_0_, bf16[128,4096]{1,0:T(8,128)(2,1)} %masked_rows.5.refs_1_, ...), custom_call_target="tpu_custom_call" | custom-call | flops 1000 | bytes 1000 | tf_op jit(solution)/shard_map/half_products/pallas_call | solution.py:361
  236.5 1.1 collective-permute-start.18
  238.9 18.6 %collective-permute-done.13.refs_9_ = bf16[512,768]{1,0:T(8,128)(2,1)S(1)} collective-permute-done((bf16[512,768]{1,0:T(8,128)(2,1)}, bf16[512,768]{1,0:T(8,128)(2,1)S(1)}, u32[]{:S(2)}, u32[]{:S(2)}) %collective-permute-start.13) | collective-permute-done | bytes 786464 | tf_op jit(solution)/shard_map/ppermute | solution.py:527
  258.5 5.4 %rest_products.1 = (bf16[256,384]{1,0:T(8,128)(2,1)}, bf16[256,384]{1,0:T(8,128)(2,1)}, bf16[256,384]{1,0:T(8,128)(2,1)}, bf16[256,384]{1,0:T(8,128)(2,1)}) custom-call(s32[7]{0:T(128)} %stack.116.meta_ref, bf16[128,4096]{1,0:T(8,128)(2,1)} %masked_rows.4.refs_0_, bf16[128,4096]{1,0:T(8,128)(2,1)} %masked_rows.5.refs_1_, ...), custom_call_target="tpu_custom_call" | custom-call | flops 1000 | bytes 1000 | tf_op jit(solution)/shard_map/rest_products/pallas_call | solution.py:439
  266.2 2.0 assembled.2.refs_4_
  268.2 3.8 %collective-permute-done.16.refs_2_ = bf16[256,384]{1,0:T(8,128)(2,1)S(1)} collective-permute-done((bf16[256,384]{1,0:T(8,128)(2,1)}, bf16[256,384]{1,0:T(8,128)(2,1)S(1)}, u32[]{:S(2)}, u32[]{:S(2)}) %collective-permute-start.16) | collective-permute-done | bytes 196640 | tf_op jit(solution)/shard_map/ppermute | solution.py:527
  272.0 3.3 %collective-permute-done.17.refs_3_ = bf16[256,384]{1,0:T(8,128)(2,1)S(1)} collective-permute-done((bf16[256,384]{1,0:T(8,128)(2,1)}, bf16[256,384]{1,0:T(8,128)(2,1)S(1)}, u32[]{:S(2)}, u32[]{:S(2)}) %collective-permute-start.17) | collective-permute-done | bytes 196640 | tf_op jit(solution)/shard_map/ppermute | solution.py:601
  275.3 1.6 assembled.3
  (56 shorter events, 11.0 us)
Async XLA Ops:
  0.0 5.6 %copy-start = (bf16[512,4096]{1,0:T(8,128)(2,1)S(1)}, bf16[512,4096]{1,0:T(8,128)(2,1)}, u32[]{:S(2)}) copy-start(bf16[512,4096]{1,0:T(8,128)(2,1)} %w_ref.2) | copy-start | bytes 12582916
  2.5 26.5 %collective-permute-start = (bf16[512,1024]{1,0:T(8,128)(2,1)}, bf16[512,1024]{1,0:T(8,128)(2,1)}, u32[]{:S(2)}, u32[]{:S(2)}) collective-permute-start(bf16[512,1024]{1,0:T(8,128)(2,1)} %b_strips.2), channel_id=1, source_target_pairs={{0,2},{2,0},{4,6},{6,4},{8,10},{10,8},{12,14},{14,12},{1,3},{3,1},... | collective-permute-start | bytes 3145736 | tf_op jit(solution)/shard_map/ppermute | solution.py:527
  5.6 4.0 %copy-start.9 = (s32[8,64]{1,0:T(8,128)S(1)}, s32[8,64]{1,0:T(8,128)}, u32[]{:S(2)}) copy-start(s32[8,64]{1,0:T(8,128)} %param.6) | copy-start | bytes 6148
  6.3 6.4 %copy-start.1 = (bf16[512,1024]{1,0:T(8,128)(2,1)}, bf16[512,1024]{1,0:T(8,128)(2,1)S(1)}, u32[]{:S(2)}) copy-start(bf16[512,1024]{1,0:T(8,128)(2,1)S(1)} %b_strips.3.refs_8_) | copy-start | bytes 3145732
  6.3 24.8 %collective-permute-start.1 = (bf16[512,1024]{1,0:T(8,128)(2,1)S(1)}, bf16[512,1024]{1,0:T(8,128)(2,1)}, u32[]{:S(2)}, u32[]{:S(2)}) collective-permute-start(bf16[512,1024]{1,0:T(8,128)(2,1)S(1)} %b_strips.3.refs_8_), channel_id=1, source_target_pairs={{0,4},{2,6},{4,0},{6,2},{8,12},{10,14},{12,8},{14,10},{1,5},{3,7},... | collective-permute-start | bytes 3145736 | tf_op jit(solution)/shard_map/ppermute | solution.py:527
  8.0 24.7 %collective-permute-start.2 = (bf16[512,1024]{1,0:T(8,128)(2,1)S(1)}, bf16[512,1024]{1,0:T(8,128)(2,1)}, u32[]{:S(2)}, u32[]{:S(2)}) collective-permute-start(bf16[512,1024]{1,0:T(8,128)(2,1)S(1)} %b_strips.3.refs_8_), channel_id=1, source_target_pairs={{4,8},{6,10},{8,4},{10,6},{5,9},{7,11},{9,5},{11,7},{20,24},{22,26... | collective-permute-start | bytes 3145736 | tf_op jit(solution)/shard_map/ppermute | solution.py:527
  12.7 23.0 %copy-start.4 = (bf16[128,4096]{1,0:T(8,128)(2,1)S(1)}, bf16[128,4096]{1,0:T(8,128)(2,1)}, u32[]{:S(2)}) copy-start(bf16[128,4096]{1,0:T(8,128)(2,1)} %masked_rows.5.refs_1_) | copy-start | bytes 3145732
  31.1 24.0 %collective-permute-start.4 = (bf16[512,1024]{1,0:T(8,128)(2,1)}, bf16[512,1024]{1,0:T(8,128)(2,1)}, u32[]{:S(2)}, u32[]{:S(2)}) collective-permute-start(bf16[512,1024]{1,0:T(8,128)(2,1)} %collective-permute-done.refs_9_), channel_id=1, source_target_pairs={{0,4},{2,6},{4,0},{6,2},{8,12},{10,14},{12,8},{14,10},{1,5},{3,7},... | collective-permute-start | bytes 3145736 | tf_op jit(solution)/shard_map/ppermute | solution.py:527
  32.7 22.4 %collective-permute-start.3 = (bf16[512,1024]{1,0:T(8,128)(2,1)}, bf16[512,1024]{1,0:T(8,128)(2,1)}, u32[]{:S(2)}, u32[]{:S(2)}) collective-permute-start(bf16[512,1024]{1,0:T(8,128)(2,1)} %collective-permute-done.refs_9_), channel_id=1, source_target_pairs={{4,8},{6,10},{8,4},{10,6},{5,9},{7,11},{9,5},{11,7},{20,24},{22,26... | collective-permute-start | bytes 3145736 | tf_op jit(solution)/shard_map/ppermute | solution.py:527
  35.0 141.2 %collective-permute-start.6 = (bf16[128,4096]{1,0:T(8,128)(2,1)}, bf16[128,4096]{1,0:T(8,128)(2,1)S(1)}, u32[]{:S(2)}, u32[]{:S(2)}) collective-permute-start(bf16[128,4096]{1,0:T(8,128)(2,1)} %masked_rows.4.refs_0_), channel_id=1, source_target_pairs={{0,2},{2,0},{4,6},{6,4},{8,10},{10,8},{12,14},{14,12},{1,3},{3,1},... | collective-permute-start | bytes 3145736 | tf_op jit(solution)/shard_map/ppermute | solution.py:527
  35.7 140.5 %collective-permute-start.7 = (bf16[128,4096]{1,0:T(8,128)(2,1)S(1)}, bf16[128,4096]{1,0:T(8,128)(2,1)S(1)}, u32[]{:S(2)}, u32[]{:S(2)}) collective-permute-start(bf16[128,4096]{1,0:T(8,128)(2,1)S(1)} %copy-done.4), channel_id=1, source_target_pairs={{0,2},{2,0},{4,6},{6,4},{8,10},{10,8},{12,14},{14,12},{1,3},{3,1},... | collective-permute-start | bytes 3145736 | tf_op jit(solution)/shard_map/ppermute | solution.py:527
  140.3 35.9 %collective-permute-start.5 = (bf16[512,1024]{1,0:T(8,128)(2,1)}, bf16[512,1024]{1,0:T(8,128)(2,1)}, u32[]{:S(2)}, u32[]{:S(2)}) collective-permute-start(bf16[512,1024]{1,0:T(8,128)(2,1)} %get-tuple-element.40), channel_id=1, source_target_pairs={{4,8},{6,10},{8,4},{10,6},{5,9},{7,11},{9,5},{11,7},{20,24},{22,26... | collective-permute-start | bytes 3145736 | tf_op jit(solution)/shard_map/ppermute | solution.py:527
  142.0 44.3 %collective-permute-start.10 = (bf16[512,1664]{1,0:T(8,128)(2,1)}, bf16[512,1664]{1,0:T(8,128)(2,1)}, u32[]{:S(2)}, u32[]{:S(2)}) collective-permute-start(bf16[512,1664]{1,0:T(8,128)(2,1)} %get-tuple-element.43), channel_id=1, source_target_pairs={{4,0},{6,2},{8,12},{10,14},{5,1},{7,3},{9,13},{11,15},{20,16},{22,... | collective-permute-start | bytes 5111816 | tf_op jit(solution)/shard_map/ppermute | solution.py:527
  176.2 5.7 %copy-start.5 = (bf16[128,4096]{1,0:T(8,128)(2,1)}, bf16[128,4096]{1,0:T(8,128)(2,1)S(1)}, u32[]{:S(2)}) copy-start(bf16[128,4096]{1,0:T(8,128)(2,1)S(1)} %collective-permute-done.6.refs_4_) | copy-start | bytes 3145732
  176.2 5.7 %copy-start.6 = (bf16[128,4096]{1,0:T(8,128)(2,1)}, bf16[128,4096]{1,0:T(8,128)(2,1)S(1)}, u32[]{:S(2)}) copy-start(bf16[128,4096]{1,0:T(8,128)(2,1)S(1)} %collective-permute-done.7.refs_5_) | copy-start | bytes 3145732
  176.2 10.1 %collective-permute-start.8 = (bf16[128,4096]{1,0:T(8,128)(2,1)S(1)}, bf16[128,4096]{1,0:T(8,128)(2,1)S(1)}, u32[]{:S(2)}, u32[]{:S(2)}) collective-permute-start(bf16[128,4096]{1,0:T(8,128)(2,1)S(1)} %collective-permute-done.6.refs_4_), channel_id=1, source_target_pairs={{0,1},{1,0},{2,3},{3,2},{4,5},{5,4},{6,7},{7,6},{8,9},{9,8},{10,11... | collective-permute-start | bytes 3145736 | tf_op jit(solution)/shard_map/ppermute | solution.py:569
  176.3 10.0 %collective-permute-start.9 = (bf16[128,4096]{1,0:T(8,128)(2,1)S(1)}, bf16[128,4096]{1,0:T(8,128)(2,1)}, u32[]{:S(2)}, u32[]{:S(2)}) collective-permute-start(bf16[128,4096]{1,0:T(8,128)(2,1)S(1)} %collective-permute-done.7.refs_5_), channel_id=1, source_target_pairs={{0,1},{1,0},{2,3},{3,2},{4,5},{5,4},{6,7},{7,6},{8,9},{9,8},{10,11... | collective-permute-start | bytes 3145736 | tf_op jit(solution)/shard_map/ppermute | solution.py:569
  176.8 25.8 %collective-permute-start.12 = (bf16[512,1024]{1,0:T(8,128)(2,1)}, bf16[512,1024]{1,0:T(8,128)(2,1)}, u32[]{:S(2)}, u32[]{:S(2)}) collective-permute-start(bf16[512,1024]{1,0:T(8,128)(2,1)} %packed.4), channel_id=1, source_target_pairs={{4,8},{6,10},{8,4},{10,6},{5,9},{7,11},{9,5},{11,7},{20,24},{22,26... | collective-permute-start | bytes 3145736 | tf_op jit(solution)/shard_map/ppermute | solution.py:527
  178.4 51.8 %collective-permute-start.11 = (bf16[512,1024]{1,0:T(8,128)(2,1)}, bf16[512,1024]{1,0:T(8,128)(2,1)}, u32[]{:S(2)}, u32[]{:S(2)}) collective-permute-start(bf16[512,1024]{1,0:T(8,128)(2,1)} %collective-permute-done.5.refs_9_), channel_id=1, source_target_pairs={{4,0},{6,2},{8,12},{10,14},{5,1},{7,3},{9,13},{11,15},{20,16},{22,... | collective-permute-start | bytes 3145736 | tf_op jit(solution)/shard_map/ppermute | solution.py:527
  186.3 1.0 copy-start.7
  228.2 29.3 %collective-permute-start.13 = (bf16[512,768]{1,0:T(8,128)(2,1)}, bf16[512,768]{1,0:T(8,128)(2,1)S(1)}, u32[]{:S(2)}, u32[]{:S(2)}) collective-permute-start(bf16[512,768]{1,0:T(8,128)(2,1)} %packed.5), channel_id=1, source_target_pairs={{4,0},{6,2},{8,12},{10,14},{5,1},{7,3},{9,13},{11,15},{20,16},{22,... | collective-permute-start | bytes 2359304 | tf_op jit(solution)/shard_map/ppermute | solution.py:527
  236.4 2.6 collective-permute-start.14
  236.5 29.7 %collective-permute-start.18 = (bf16[256,640]{1,0:T(8,128)(2,1)}, bf16[256,640]{1,0:T(8,128)(2,1)S(1)}, u32[]{:S(2)}, u32[]{:S(2)}) collective-permute-start(bf16[256,640]{1,0:T(8,128)(2,1)} %get-tuple-element.57), channel_id=1, source_target_pairs={{0,2},{2,0},{4,6},{6,4},{8,10},{10,8},{12,14},{14,12},{1,3},{3,1},... | collective-permute-start | bytes 983048 | tf_op jit(solution)/shard_map/ppermute | solution.py:527
  237.6 28.6 %collective-permute-start.19 = (bf16[256,640]{1,0:T(8,128)(2,1)}, bf16[256,640]{1,0:T(8,128)(2,1)S(1)}, u32[]{:S(2)}, u32[]{:S(2)}) collective-permute-start(bf16[256,640]{1,0:T(8,128)(2,1)} %get-tuple-element.58), channel_id=1, source_target_pairs={{0,3},{1,2},{2,1},{3,0},{4,7},{5,6},{6,5},{7,4},{8,11},{9,10},{10,... | collective-permute-start | bytes 983048 | tf_op jit(solution)/shard_map/ppermute | solution.py:601
  257.6 0.9 copy-start.8
  258.5 7.4 %copy-start.10 = (s32[4,64]{1,0:T(4,128)S(1)}, s32[4,64]{1,0:T(4,128)}, u32[]{:S(2)}) copy-start(s32[4,64]{1,0:T(4,128)} %param.7) | copy-start | bytes 3076
  258.5 7.7 %copy-start.2 = (bf16[256,640]{1,0:T(8,128)(2,1)S(1)}, bf16[256,640]{1,0:T(8,128)(2,1)}, u32[]{:S(2)}) copy-start(bf16[256,640]{1,0:T(8,128)(2,1)} %get-tuple-element.55.refs_0_) | copy-start | bytes 983044
  263.9 11.4 %copy-start.3 = (bf16[256,384]{1,0:T(8,128)(2,1)S(1)}, bf16[256,384]{1,0:T(8,128)(2,1)}, u32[]{:S(2)}) copy-start(bf16[256,384]{1,0:T(8,128)(2,1)} %get-tuple-element.51.refs_0_) | copy-start | bytes 589828
  263.9 4.3 %collective-permute-start.15 = (bf16[256,384]{1,0:T(8,128)(2,1)}, bf16[256,384]{1,0:T(8,128)(2,1)S(1)}, u32[]{:S(2)}, u32[]{:S(2)}) collective-permute-start(bf16[256,384]{1,0:T(8,128)(2,1)} %get-tuple-element.52), channel_id=1, source_target_pairs={{0,1},{1,0},{2,3},{3,2},{4,5},{5,4},{6,7},{7,6},{8,9},{9,8},{10,11... | collective-permute-start | bytes 589832 | tf_op jit(solution)/shard_map/ppermute | solution.py:599
  264.0 8.0 %collective-permute-start.16 = (bf16[256,384]{1,0:T(8,128)(2,1)}, bf16[256,384]{1,0:T(8,128)(2,1)S(1)}, u32[]{:S(2)}, u32[]{:S(2)}) collective-permute-start(bf16[256,384]{1,0:T(8,128)(2,1)} %get-tuple-element.53), channel_id=1, source_target_pairs={{0,2},{2,0},{4,6},{6,4},{8,10},{10,8},{12,14},{14,12},{1,3},{3,1},... | collective-permute-start | bytes 589832 | tf_op jit(solution)/shard_map/ppermute | solution.py:527
  264.9 10.4 %collective-permute-start.17 = (bf16[256,384]{1,0:T(8,128)(2,1)}, bf16[256,384]{1,0:T(8,128)(2,1)S(1)}, u32[]{:S(2)}, u32[]{:S(2)}) collective-permute-start(bf16[256,384]{1,0:T(8,128)(2,1)} %get-tuple-element.54), channel_id=1, source_target_pairs={{0,3},{1,2},{2,1},{3,0},{4,7},{5,6},{6,5},{7,4},{8,11},{9,10},{10,... | collective-permute-start | bytes 589832 | tf_op jit(solution)/shard_map/ppermute | solution.py:601

commit v9 on v8

--- a/solution.py
+++ b/solution.py
@@ -120,9 +120,9 @@
         functools.partial(pack_kernel, plan, len(sources)),
         out_shape=[jax.ShapeDtypeStruct((rows, width * LANES), jnp.bfloat16) for width in widths],
         in_specs=[pl.BlockSpec(memory_space=pltpu.SMEM)] + [any_spec] * len(sources),
-        out_specs=[any_spec] * len(widths),
+        out_specs=[pl.BlockSpec(memory_space=pltpu.VMEM)] * len(widths),
         scratch_shapes=[pltpu.SemaphoreType.DMA((len(plan),))],
-        compiler_params=pltpu.CompilerParams(vmem_limit_bytes=59 * MIB),
+        compiler_params=pltpu.CompilerParams(vmem_limit_bytes=40 * MIB),
         cost_estimate=SMALL,
         name="packed",
     )(jnp.stack(meta).astype(jnp.int32), *sources)

time: 277 us -> 165 us (0.60)
  Pallas kernels: 186 us -> 47 us
  waiting for transfers between devices: 61.5 us -> 90.8 us
    pallas_call x3, Pallas kernels: 144 us -> 4.22 us  [packed(): pl.pallas_call(functools.partial(pack_kernel, plan, len(sources)), out_sh...]
    ppermute x14, waiting for transfers between devices: 58.2 us -> 86.1 us  [line(): return lax.ppermute(value, 'grid', pairs)]
  transfers between devices with their start and end apart: 20 -> 20, of which waited for: 7 -> 10; matrix products, arithmetic and copies ran while one was open for 2% -> 2% of each run, Pallas kernels for 66% -> 26%
where the time goes in v9:
time: 165 us
  waiting for transfers between devices  90.8 us (55%)
  Pallas kernels  47 us (28%)
  starting transfers between devices  21.2 us (13%)
  local copies, waits for them, and re-layouts  5.13 us (3%)
    ppermute x14, waiting for transfers between devices, line(): return lax.ppermute(value, 'grid', pairs)  86.1 us
    ppermute x14, starting transfers between devices, line(): return lax.ppermute(value, 'grid', pairs)  18.9 us
    pallas_call x1, Pallas kernels, whole_products(): pl.pallas_call(functools.partial(whole_kernel, plan), out_shape=jax.Shape...  14.7 us
    pallas_call x4, Pallas kernels, masked_rows(): pl.pallas_call(mask_kernel, grid_spec=pltpu.PrefetchScalarGridSpec(num_sc...  8.7 us
    pallas_call x1, Pallas kernels, half_products(): pl.pallas_call(half_kernel, out_shape=[jax.ShapeDtypeStruct((rows, n_done...  6.16 us
    pallas_call x1, Pallas kernels, rest_products(): pl.pallas_call(rest_kernel, out_shape=[jax.ShapeDtypeStruct((rows, width)...  5.38 us
    ppermute x2, waiting for transfers between devices, exchanged(): lax.ppermute(pieces[3], ('grid', 'depth'), opposite)  4.77 us
    pallas_call x3, Pallas kernels, packed(): pl.pallas_call(functools.partial(pack_kernel, plan, len(sources)), out_sh...  4.22 us
  transfers between devices with their start and end apart: 20, of which 10 were waited for; matrix products, arithmetic and copies ran while one was open for 2% of the time, Pallas kernels for 26%

profile of v9, /device:TPU:0, one launch (start us, length us, event | category | flops | bytes accessed | tf_op | source)
XLA Modules:
  0.0 164.8 jit_solution(14312787888921562078)
XLA Ops:
  0.0 2.5 %b_strips.2 = bf16[512,1024]{1,0:T(8,128)(2,1)} custom-call(s32[1]{0:T(128)} %bitcast.7.quarters_ref, bf16[512,4096]{1,0:T(8,128)(2,1)} %w_ref.2), custom_call_target="tpu_custom_call" | custom-call | flops 1000 | bytes 1000 | tf_op jit(solution)/shard_map/b_strips/pallas_call | solution.py:81
  2.5 3.0 %collective-permute-start = (bf16[512,1024]{1,0:T(8,128)(2,1)}, bf16[512,1024]{1,0:T(8,128)(2,1)}, u32[]{:S(2)}, u32[]{:S(2)}) collective-permute-start(bf16[512,1024]{1,0:T(8,128)(2,1)} %b_strips.2), channel_id=1, source_target_pairs={{0,2},{2,0},{4,6},{6,4},{8,10},{10,8},{12,14},{14,12},{1,3},{3,1},... | collective-permute-start | bytes 3145736 | tf_op jit(solution)/shard_map/ppermute | solution.py:527
  5.6 1.7 %b_strips.3.refs_8_ = bf16[512,1024]{1,0:T(8,128)(2,1)} custom-call(s32[1]{0:T(128)} %bitcast.quarters_ref, bf16[512,4096]{1,0:T(8,128)(2,1)S(1)} %copy-done), custom_call_target="tpu_custom_call" | custom-call | flops 1000 | bytes 1000 | tf_op jit(solution)/shard_map/b_strips/pallas_call | solution.py:81
  7.3 1.6 collective-permute-start.1
  10.7 2.1 %masked_rows.5.refs_1_ = bf16[128,4096]{1,0:T(8,128)(2,1)} custom-call(s32[1]{0:T(128)} %bitcast.9.first_ref, f32[8,1,4096]{2,1,0:T(1,128)} %reshape.22.mask_ref, bf16[512,4096]{1,0:T(8,128)(2,1)} %x_ref.7), custom_call_target="tpu_custom_call" | custom-call | flops 1000 | bytes 1000 | tf_op jit(solution)/shard_map/masked_rows/pallas_call | solution.py:138
  12.8 2.2 %masked_rows.4.refs_0_ = bf16[128,4096]{1,0:T(8,128)(2,1)} custom-call(s32[1]{0:T(128)} %bitcast.8.first_ref, f32[8,1,4096]{2,1,0:T(1,128)} %reshape.22.mask_ref, bf16[512,4096]{1,0:T(8,128)(2,1)} %x_ref.7), custom_call_target="tpu_custom_call" | custom-call | flops 1000 | bytes 1000 | tf_op jit(solution)/shard_map/masked_rows/pallas_call | solution.py:138
  15.0 14.1 %collective-permute-done.refs_9_ = bf16[512,1024]{1,0:T(8,128)(2,1)} collective-permute-done((bf16[512,1024]{1,0:T(8,128)(2,1)}, bf16[512,1024]{1,0:T(8,128)(2,1)}, u32[]{:S(2)}, u32[]{:S(2)}) %collective-permute-start) | collective-permute-done | bytes 1048608 | tf_op jit(solution)/shard_map/ppermute | solution.py:527
  29.1 3.1 %collective-permute-done.1.refs_2_.refs_0_.refs_12_ = bf16[512,1024]{1,0:T(8,128)(2,1)S(1)} collective-permute-done((bf16[512,1024]{1,0:T(8,128)(2,1)}, bf16[512,1024]{1,0:T(8,128)(2,1)S(1)}, u32[]{:S(2)}, u32[]{:S(2)}) %collective-permute-start.1) | collective-permute-done | bytes 1048608 | tf_op jit(solution)/shard_map/ppermute | solution.py:527
  32.2 1.6 collective-permute-start.4
  33.7 1.6 %collective-permute-start.3 = (bf16[512,1024]{1,0:T(8,128)(2,1)}, bf16[512,1024]{1,0:T(8,128)(2,1)}, u32[]{:S(2)}, u32[]{:S(2)}) collective-permute-start(bf16[512,1024]{1,0:T(8,128)(2,1)} %collective-permute-done.refs_9_), channel_id=1, source_target_pairs={{4,8},{6,10},{8,4},{10,6},{5,9},{7,11},{9,5},{11,7},{20,24},{22,26... | collective-permute-start | bytes 3145736 | tf_op jit(solution)/shard_map/ppermute | solution.py:527
  36.1 1.4 collective-permute-start.7
  37.5 18.6 %collective-permute-done.4.refs_3_.refs_1_.refs_13_ = bf16[512,1024]{1,0:T(8,128)(2,1)S(1)} collective-permute-done((bf16[512,1024]{1,0:T(8,128)(2,1)}, bf16[512,1024]{1,0:T(8,128)(2,1)S(1)}, u32[]{:S(2)}, u32[]{:S(2)}) %collective-permute-start.4) | collective-permute-done | bytes 1048608 | tf_op jit(solution)/shard_map/ppermute | solution.py:527
  56.1 3.4 %packed.3 = (bf16[512,1664]{1,0:T(8,128)(2,1)}, bf16[512,1024]{1,0:T(8,128)(2,1)}) custom-call(s32[2]{0:T(128)S(1)} %pad_add_fusion.1.meta_ref, bf16[512,1024]{1,0:T(8,128)(2,1)S(1)} %collective-permute-done.2.refs_0_.refs_10_, bf16[512,1024]{1,0:T(8,128)(2,1)} %collective-permute-done.3.refs_1_.refs_11_, ...), custom_call_target="tpu_custom_call" | custom-call | flops 1000 | bytes 1000 | tf_op jit(solution)/shard_map/packed/pallas_call | solution.py:119
  59.5 1.6 %collective-permute-start.5 = (bf16[512,1024]{1,0:T(8,128)(2,1)}, bf16[512,1024]{1,0:T(8,128)(2,1)}, u32[]{:S(2)}, u32[]{:S(2)}) collective-permute-start(bf16[512,1024]{1,0:T(8,128)(2,1)} %get-tuple-element.40), channel_id=1, source_target_pairs={{4,8},{6,10},{8,4},{10,6},{5,9},{7,11},{9,5},{11,7},{20,24},{22,26... | collective-permute-start | bytes 3145736 | tf_op jit(solution)/shard_map/ppermute | solution.py:527
  61.1 1.3 collective-permute-start.10
  62.6 19.1 %collective-permute-done.7.refs_5_ = bf16[128,4096]{1,0:T(8,128)(2,1)} collective-permute-done((bf16[128,4096]{1,0:T(8,128)(2,1)}, bf16[128,4096]{1,0:T(8,128)(2,1)}, u32[]{:S(2)}, u32[]{:S(2)}) %collective-permute-start.7) | collective-permute-done | bytes 1048608 | tf_op jit(solution)/shard_map/ppermute | solution.py:527
  82.9 1.3 collective-permute-start.11
  84.2 2.2 %masked_rows.7.refs_3_ = bf16[128,4096]{1,0:T(8,128)(2,1)} custom-call(s32[1]{0:T(128)} %bitcast.11.first_ref, f32[8,1,4096]{2,1,0:T(1,128)} %reshape.22.mask_ref, bf16[512,4096]{1,0:T(8,128)(2,1)} %x_ref.7), custom_call_target="tpu_custom_call" | custom-call | flops 1000 | bytes 1000 | tf_op jit(solution)/shard_map/masked_rows/pallas_call | solution.py:138
  86.4 2.2 %masked_rows.6.refs_2_ = bf16[128,4096]{1,0:T(8,128)(2,1)} custom-call(s32[1]{0:T(128)} %bitcast.10.first_ref, f32[8,1,4096]{2,1,0:T(1,128)} %reshape.22.mask_ref, bf16[512,4096]{1,0:T(8,128)(2,1)} %x_ref.7), custom_call_target="tpu_custom_call" | custom-call | flops 1000 | bytes 1000 | tf_op jit(solution)/shard_map/masked_rows/pallas_call | solution.py:138
  89.3 19.8 %collective-permute-done.10.refs_14_ = bf16[512,1664]{1,0:T(8,128)(2,1)} collective-permute-done((bf16[512,1664]{1,0:T(8,128)(2,1)}, bf16[512,1664]{1,0:T(8,128)(2,1)}, u32[]{:S(2)}, u32[]{:S(2)}) %collective-permute-start.10) | collective-permute-done | bytes 1703968 | tf_op jit(solution)/shard_map/ppermute | solution.py:527
  110.1 14.7 %whole_products.1.refs_8_ = f32[2,512,1024]{2,1,0:T(8,128)} custom-call(s32[14]{0:T(128)} %stack.133.meta_ref, bf16[128,4096]{1,0:T(8,128)(2,1)} %masked_rows.4.refs_0_, bf16[128,4096]{1,0:T(8,128)(2,1)} %masked_rows.5.refs_1_, bf16[128,4096]{1,0:T(8,128)(2,1)} %masked_rows.6.refs_2_, bf16[128,4096]{1,0:T(8,128)(2,1)} %masked_rows.7.refs_3_, ...), custom_call_target="tpu_custom_call" | custom-call | flops 1000 | bytes 1000 | tf_op jit(solution)/shard_map/whole_products/pallas_call | solution.py:245
  125.7 1.3 collective-permute-start.13
  127.7 3.9 %collective-permute-done.11.refs_10_ = bf16[512,1024]{1,0:T(8,128)(2,1)} collective-permute-done((bf16[512,1024]{1,0:T(8,128)(2,1)}, bf16[512,1024]{1,0:T(8,128)(2,1)}, u32[]{:S(2)}, u32[]{:S(2)}) %collective-permute-start.11) | collective-permute-done | bytes 1048608 | tf_op jit(solution)/shard_map/ppermute | solution.py:527
  131.6 6.2 %half_products.1 = (bf16[256,640]{1,0:T(8,128)(2,1)}, bf16[256,640]{1,0:T(8,128)(2,1)}, bf16[256,640]{1,0:T(8,128)(2,1)}, bf16[256,640]{1,0:T(8,128)(2,1)}, f32[2,512,384]{2,1,0:T(8,128)}) custom-call(s32[9]{0:T(128)} %stack.123.meta_ref, bf16[128,4096]{1,0:T(8,128)(2,1)} %masked_rows.4.refs_0_, bf16[128,4096]{1,0:T(8,128)(2,1)} %masked_rows.5.refs_1_, ...), custom_call_target="tpu_custom_call" | custom-call | flops 1000 | bytes 1000 | tf_op jit(solution)/shard_map/half_products/pallas_call | solution.py:361
  140.4 4.4 %collective-permute-done.13.refs_9_ = bf16[512,768]{1,0:T(8,128)(2,1)S(1)} collective-permute-done((bf16[512,768]{1,0:T(8,128)(2,1)S(1)}, bf16[512,768]{1,0:T(8,128)(2,1)S(1)}, u32[]{:S(2)}, u32[]{:S(2)}) %collective-permute-start.13) | collective-permute-done | bytes 786464 | tf_op jit(solution)/shard_map/ppermute | solution.py:527
  145.6 5.4 %rest_products.1 = (bf16[256,384]{1,0:T(8,128)(2,1)}, bf16[256,384]{1,0:T(8,128)(2,1)}, bf16[256,384]{1,0:T(8,128)(2,1)}, bf16[256,384]{1,0:T(8,128)(2,1)}) custom-call(s32[7]{0:T(128)} %stack.116.meta_ref, bf16[128,4096]{1,0:T(8,128)(2,1)} %masked_rows.4.refs_0_, bf16[128,4096]{1,0:T(8,128)(2,1)} %masked_rows.5.refs_1_, ...), custom_call_target="tpu_custom_call" | custom-call | flops 1000 | bytes 1000 | tf_op jit(solution)/shard_map/rest_products/pallas_call | solution.py:439
  151.1 1.1 collective-permute-start.16
  153.3 1.5 collective-permute-done.19.refs_3_
  154.8 2.0 %assembled.2.refs_4_ = bf16[256,4096]{1,0:T(8,128)(2,1)} custom-call(s32[2]{0:T(128)S(1)} %get-tuple-element.60.place_ref, f32[4,1,4096]{2,1,0:T(1,128)S(1)} %reshape.20.mask_ref, bf16[256,640]{1,0:T(8,128)(2,1)S(1)} %copy-done.5, bf16[256,640]{1,0:T(8,128)(2,1)S(1)} %collective-permute-done.14.refs_1_, ...), custom_call_target="tpu_custom_call" | custom-call | flops 1000 | bytes 1000 | tf_op jit(solution)/shard_map/assembled/pallas_call | solution.py:486
  156.8 3.1 %collective-permute-done.16.refs_2_ = bf16[256,384]{1,0:T(8,128)(2,1)S(1)} collective-permute-done((bf16[256,384]{1,0:T(8,128)(2,1)}, bf16[256,384]{1,0:T(8,128)(2,1)S(1)}, u32[]{:S(2)}, u32[]{:S(2)}) %collective-permute-start.16) | collective-permute-done | bytes 196640 | tf_op jit(solution)/shard_map/ppermute | solution.py:527
  159.9 3.3 %collective-permute-done.17.refs_3_ = bf16[256,384]{1,0:T(8,128)(2,1)S(1)} collective-permute-done((bf16[256,384]{1,0:T(8,128)(2,1)}, bf16[256,384]{1,0:T(8,128)(2,1)S(1)}, u32[]{:S(2)}, u32[]{:S(2)}) %collective-permute-start.17) | collective-permute-done | bytes 196640 | tf_op jit(solution)/shard_map/ppermute | solution.py:601
  163.2 1.6 assembled.3
  (56 shorter events, 11.6 us)
Async XLA Ops:
  0.0 5.6 %copy-start = (bf16[512,4096]{1,0:T(8,128)(2,1)S(1)}, bf16[512,4096]{1,0:T(8,128)(2,1)}, u32[]{:S(2)}) copy-start(bf16[512,4096]{1,0:T(8,128)(2,1)} %w_ref.2) | copy-start | bytes 12582916
  2.5 26.5 %collective-permute-start = (bf16[512,1024]{1,0:T(8,128)(2,1)}, bf16[512,1024]{1,0:T(8,128)(2,1)}, u32[]{:S(2)}, u32[]{:S(2)}) collective-permute-start(bf16[512,1024]{1,0:T(8,128)(2,1)} %b_strips.2), channel_id=1, source_target_pairs={{0,2},{2,0},{4,6},{6,4},{8,10},{10,8},{12,14},{14,12},{1,3},{3,1},... | collective-permute-start | bytes 3145736 | tf_op jit(solution)/shard_map/ppermute | solution.py:527
  5.6 4.1 %copy-start.9 = (s32[8,64]{1,0:T(8,128)S(1)}, s32[8,64]{1,0:T(8,128)}, u32[]{:S(2)}) copy-start(s32[8,64]{1,0:T(8,128)} %param.6) | copy-start | bytes 6148
  7.3 24.9 %collective-permute-start.1 = (bf16[512,1024]{1,0:T(8,128)(2,1)}, bf16[512,1024]{1,0:T(8,128)(2,1)S(1)}, u32[]{:S(2)}, u32[]{:S(2)}) collective-permute-start(bf16[512,1024]{1,0:T(8,128)(2,1)} %b_strips.3.refs_8_), channel_id=1, source_target_pairs={{0,4},{2,6},{4,0},{6,2},{8,12},{10,14},{12,8},{14,10},{1,5},{3,7},... | collective-permute-start | bytes 3145736 | tf_op jit(solution)/shard_map/ppermute | solution.py:527
  8.9 24.8 %collective-permute-start.2 = (bf16[512,1024]{1,0:T(8,128)(2,1)}, bf16[512,1024]{1,0:T(8,128)(2,1)S(1)}, u32[]{:S(2)}, u32[]{:S(2)}) collective-permute-start(bf16[512,1024]{1,0:T(8,128)(2,1)} %b_strips.3.refs_8_), channel_id=1, source_target_pairs={{4,8},{6,10},{8,4},{10,6},{5,9},{7,11},{9,5},{11,7},{20,24},{22,26... | collective-permute-start | bytes 3145736 | tf_op jit(solution)/shard_map/ppermute | solution.py:527
  32.2 30.3 %copy-start.1 = (bf16[512,1024]{1,0:T(8,128)(2,1)}, bf16[512,1024]{1,0:T(8,128)(2,1)S(1)}, u32[]{:S(2)}) copy-start(bf16[512,1024]{1,0:T(8,128)(2,1)S(1)} %collective-permute-done.1.refs_2_.refs_0_.refs_12_) | copy-start | bytes 3145732
  32.2 23.9 %collective-permute-start.4 = (bf16[512,1024]{1,0:T(8,128)(2,1)}, bf16[512,1024]{1,0:T(8,128)(2,1)S(1)}, u32[]{:S(2)}, u32[]{:S(2)}) collective-permute-start(bf16[512,1024]{1,0:T(8,128)(2,1)} %collective-permute-done.refs_9_), channel_id=1, source_target_pairs={{0,4},{2,6},{4,0},{6,2},{8,12},{10,14},{12,8},{14,10},{1,5},{3,7},... | collective-permute-start | bytes 3145736 | tf_op jit(solution)/shard_map/ppermute | solution.py:527
  33.7 25.7 %copy-start.3 = (bf16[512,1024]{1,0:T(8,128)(2,1)}, bf16[512,1024]{1,0:T(8,128)(2,1)S(1)}, u32[]{:S(2)}) copy-start(bf16[512,1024]{1,0:T(8,128)(2,1)S(1)} %collective-permute-done.2.refs_0_.refs_10_) | copy-start | bytes 3145732
  33.7 22.3 %collective-permute-start.3 = (bf16[512,1024]{1,0:T(8,128)(2,1)}, bf16[512,1024]{1,0:T(8,128)(2,1)}, u32[]{:S(2)}, u32[]{:S(2)}) collective-permute-start(bf16[512,1024]{1,0:T(8,128)(2,1)} %collective-permute-done.refs_9_), channel_id=1, source_target_pairs={{4,8},{6,10},{8,4},{10,6},{5,9},{7,11},{9,5},{11,7},{20,24},{22,26... | collective-permute-start | bytes 3145736 | tf_op jit(solution)/shard_map/ppermute | solution.py:527
  35.5 27.1 %collective-permute-start.6 = (bf16[128,4096]{1,0:T(8,128)(2,1)}, bf16[128,4096]{1,0:T(8,128)(2,1)}, u32[]{:S(2)}, u32[]{:S(2)}) collective-permute-start(bf16[128,4096]{1,0:T(8,128)(2,1)} %masked_rows.4.refs_0_), channel_id=1, source_target_pairs={{0,2},{2,0},{4,6},{6,4},{8,10},{10,8},{12,14},{14,12},{1,3},{3,1},... | collective-permute-start | bytes 3145736 | tf_op jit(solution)/shard_map/ppermute | solution.py:527
  36.1 45.5 %collective-permute-start.7 = (bf16[128,4096]{1,0:T(8,128)(2,1)}, bf16[128,4096]{1,0:T(8,128)(2,1)}, u32[]{:S(2)}, u32[]{:S(2)}) collective-permute-start(bf16[128,4096]{1,0:T(8,128)(2,1)} %masked_rows.5.refs_1_), channel_id=1, source_target_pairs={{0,2},{2,0},{4,6},{6,4},{8,10},{10,8},{12,14},{14,12},{1,3},{3,1},... | collective-permute-start | bytes 3145736 | tf_op jit(solution)/shard_map/ppermute | solution.py:527
  56.1 6.4 %copy-start.2 = (bf16[512,1024]{1,0:T(8,128)(2,1)}, bf16[512,1024]{1,0:T(8,128)(2,1)S(1)}, u32[]{:S(2)}) copy-start(bf16[512,1024]{1,0:T(8,128)(2,1)S(1)} %collective-permute-done.4.refs_3_.refs_1_.refs_13_) | copy-start | bytes 3145732
  59.5 22.2 %collective-permute-start.5 = (bf16[512,1024]{1,0:T(8,128)(2,1)}, bf16[512,1024]{1,0:T(8,128)(2,1)}, u32[]{:S(2)}, u32[]{:S(2)}) collective-permute-start(bf16[512,1024]{1,0:T(8,128)(2,1)} %get-tuple-element.40), channel_id=1, source_target_pairs={{4,8},{6,10},{8,4},{10,6},{5,9},{7,11},{9,5},{11,7},{20,24},{22,26... | collective-permute-start | bytes 3145736 | tf_op jit(solution)/shard_map/ppermute | solution.py:527
  61.1 48.0 %collective-permute-start.10 = (bf16[512,1664]{1,0:T(8,128)(2,1)}, bf16[512,1664]{1,0:T(8,128)(2,1)}, u32[]{:S(2)}, u32[]{:S(2)}) collective-permute-start(bf16[512,1664]{1,0:T(8,128)(2,1)} %get-tuple-element.43), channel_id=1, source_target_pairs={{4,0},{6,2},{8,12},{10,14},{5,1},{7,3},{9,13},{11,15},{20,16},{22,... | collective-permute-start | bytes 5111816 | tf_op jit(solution)/shard_map/ppermute | solution.py:527
  81.7 27.4 %collective-permute-start.8 = (bf16[128,4096]{1,0:T(8,128)(2,1)}, bf16[128,4096]{1,0:T(8,128)(2,1)S(1)}, u32[]{:S(2)}, u32[]{:S(2)}) collective-permute-start(bf16[128,4096]{1,0:T(8,128)(2,1)} %collective-permute-done.6.refs_4_), channel_id=1, source_target_pairs={{0,1},{1,0},{2,3},{3,2},{4,5},{5,4},{6,7},{7,6},{8,9},{9,8},{10,11... | collective-permute-start | bytes 3145736 | tf_op jit(solution)/shard_map/ppermute | solution.py:569
  81.7 27.4 %collective-permute-start.9 = (bf16[128,4096]{1,0:T(8,128)(2,1)}, bf16[128,4096]{1,0:T(8,128)(2,1)}, u32[]{:S(2)}, u32[]{:S(2)}) collective-permute-start(bf16[128,4096]{1,0:T(8,128)(2,1)} %collective-permute-done.7.refs_5_), channel_id=1, source_target_pairs={{0,1},{1,0},{2,3},{3,2},{4,5},{5,4},{6,7},{7,6},{8,9},{9,8},{10,11... | collective-permute-start | bytes 3145736 | tf_op jit(solution)/shard_map/ppermute | solution.py:569
  82.2 42.8 %collective-permute-start.12 = (bf16[512,1024]{1,0:T(8,128)(2,1)S(1)}, bf16[512,1024]{1,0:T(8,128)(2,1)S(1)}, u32[]{:S(2)}, u32[]{:S(2)}) collective-permute-start(bf16[512,1024]{1,0:T(8,128)(2,1)S(1)} %packed.4), channel_id=1, source_target_pairs={{4,8},{6,10},{8,4},{10,6},{5,9},{7,11},{9,5},{11,7},{20,24},{22,26... | collective-permute-start | bytes 3145736 | tf_op jit(solution)/shard_map/ppermute | solution.py:527
  82.9 48.7 %collective-permute-start.11 = (bf16[512,1024]{1,0:T(8,128)(2,1)}, bf16[512,1024]{1,0:T(8,128)(2,1)}, u32[]{:S(2)}, u32[]{:S(2)}) collective-permute-start(bf16[512,1024]{1,0:T(8,128)(2,1)} %collective-permute-done.5.refs_9_), channel_id=1, source_target_pairs={{4,0},{6,2},{8,12},{10,14},{5,1},{7,3},{9,13},{11,15},{20,16},{22,... | collective-permute-start | bytes 3145736 | tf_op jit(solution)/shard_map/ppermute | solution.py:527
  109.1 1.0 copy-start.7
  125.0 6.6 %copy-start.4 = (bf16[512,1024]{1,0:T(8,128)(2,1)}, bf16[512,1024]{1,0:T(8,128)(2,1)S(1)}, u32[]{:S(2)}) copy-start(bf16[512,1024]{1,0:T(8,128)(2,1)S(1)} %collective-permute-done.12.refs_11_.refs_0_) | copy-start | bytes 3145732
  125.7 19.1 %collective-permute-start.13 = (bf16[512,768]{1,0:T(8,128)(2,1)S(1)}, bf16[512,768]{1,0:T(8,128)(2,1)S(1)}, u32[]{:S(2)}, u32[]{:S(2)}) collective-permute-start(bf16[512,768]{1,0:T(8,128)(2,1)S(1)} %packed.5), channel_id=1, source_target_pairs={{4,0},{6,2},{8,12},{10,14},{5,1},{7,3},{9,13},{11,15},{20,16},{22,... | collective-permute-start | bytes 2359304 | tf_op jit(solution)/shard_map/ppermute | solution.py:527
  137.8 2.6 %collective-permute-start.14 = (bf16[256,640]{1,0:T(8,128)(2,1)}, bf16[256,640]{1,0:T(8,128)(2,1)S(1)}, u32[]{:S(2)}, u32[]{:S(2)}) collective-permute-start(bf16[256,640]{1,0:T(8,128)(2,1)} %get-tuple-element.49), channel_id=1, source_target_pairs={{0,1},{1,0},{2,3},{3,2},{4,5},{5,4},{6,7},{7,6},{8,9},{9,8},{10,11... | collective-permute-start | bytes 983048 | tf_op jit(solution)/shard_map/ppermute | solution.py:599
  137.8 15.4 %collective-permute-start.18 = (bf16[256,640]{1,0:T(8,128)(2,1)}, bf16[256,640]{1,0:T(8,128)(2,1)S(1)}, u32[]{:S(2)}, u32[]{:S(2)}) collective-permute-start(bf16[256,640]{1,0:T(8,128)(2,1)} %get-tuple-element.57), channel_id=1, source_target_pairs={{0,2},{2,0},{4,6},{6,4},{8,10},{10,8},{12,14},{14,12},{1,3},{3,1},... | collective-permute-start | bytes 983048 | tf_op jit(solution)/shard_map/ppermute | solution.py:527
  138.8 16.0 %collective-permute-start.19 = (bf16[256,640]{1,0:T(8,128)(2,1)}, bf16[256,640]{1,0:T(8,128)(2,1)S(1)}, u32[]{:S(2)}, u32[]{:S(2)}) collective-permute-start(bf16[256,640]{1,0:T(8,128)(2,1)} %get-tuple-element.58), channel_id=1, source_target_pairs={{0,3},{1,2},{2,1},{3,0},{4,7},{5,6},{6,5},{7,4},{8,11},{9,10},{10,... | collective-permute-start | bytes 983048 | tf_op jit(solution)/shard_map/ppermute | solution.py:601
  144.7 0.9 copy-start.8
  145.6 7.3 %copy-start.10 = (s32[4,64]{1,0:T(4,128)S(1)}, s32[4,64]{1,0:T(4,128)}, u32[]{:S(2)}) copy-start(s32[4,64]{1,0:T(4,128)} %param.7) | copy-start | bytes 3076
  145.6 9.1 %copy-start.5 = (bf16[256,640]{1,0:T(8,128)(2,1)S(1)}, bf16[256,640]{1,0:T(8,128)(2,1)}, u32[]{:S(2)}) copy-start(bf16[256,640]{1,0:T(8,128)(2,1)} %get-tuple-element.55.refs_0_) | copy-start | bytes 983044
  151.0 12.2 %copy-start.6 = (bf16[256,384]{1,0:T(8,128)(2,1)S(1)}, bf16[256,384]{1,0:T(8,128)(2,1)}, u32[]{:S(2)}) copy-start(bf16[256,384]{1,0:T(8,128)(2,1)} %get-tuple-element.51.refs_0_) | copy-start | bytes 589828
  151.0 5.7 %collective-permute-start.15 = (bf16[256,384]{1,0:T(8,128)(2,1)}, bf16[256,384]{1,0:T(8,128)(2,1)S(1)}, u32[]{:S(2)}, u32[]{:S(2)}) collective-permute-start(bf16[256,384]{1,0:T(8,128)(2,1)} %get-tuple-element.52), channel_id=1, source_target_pairs={{0,1},{1,0},{2,3},{3,2},{4,5},{5,4},{6,7},{7,6},{8,9},{9,8},{10,11... | collective-permute-start | bytes 589832 | tf_op jit(solution)/shard_map/ppermute | solution.py:599
  151.1 8.8 %collective-permute-start.16 = (bf16[256,384]{1,0:T(8,128)(2,1)}, bf16[256,384]{1,0:T(8,128)(2,1)S(1)}, u32[]{:S(2)}, u32[]{:S(2)}) collective-permute-start(bf16[256,384]{1,0:T(8,128)(2,1)} %get-tuple-element.53), channel_id=1, source_target_pairs={{0,2},{2,0},{4,6},{6,4},{8,10},{10,8},{12,14},{14,12},{1,3},{3,1},... | collective-permute-start | bytes 589832 | tf_op jit(solution)/shard_map/ppermute | solution.py:527
  152.2 11.0 %collective-permute-start.17 = (bf16[256,384]{1,0:T(8,128)(2,1)}, bf16[256,384]{1,0:T(8,128)(2,1)S(1)}, u32[]{:S(2)}, u32[]{:S(2)}) collective-permute-start(bf16[256,384]{1,0:T(8,128)(2,1)} %get-tuple-element.54), channel_id=1, source_target_pairs={{0,3},{1,2},{2,1},{3,0},{4,7},{5,6},{6,5},{7,4},{8,11},{9,10},{10,... | collective-permute-start | bytes 589832 | tf_op jit(solution)/shard_map/ppermute | solution.py:601

commit v10 on v9

--- a/solution.py
+++ b/solution.py
@@ -252,7 +252,7 @@
             pltpu.VMEM((n_b, panel, quarter), jnp.bfloat16),
             pltpu.VMEM((2, 2 * rows, 2 * quarter), jnp.float32),
             pltpu.SemaphoreType.DMA((n_b, PARTS)),
-            pltpu.SemaphoreType.DMA((n_b, 2)),
+            pltpu.SemaphoreType.DMA((n_b, 3)),
             pltpu.SemaphoreType.DMA((2,)),
         ],
         compiler_params=pltpu.CompilerParams(vmem_limit_bytes=59 * MIB),
@@ -542,25 +542,26 @@
     own_b, *x_mine = together(own_b, *x_mine)
     own_b, swap_a = together(own_b, swap_a)
     swap_b = line(own_b, swap)
-    own_b, cross_a = together(own_b, cross_a)
     cross_b = line(own_b, cross)
     x_across = [line(part, across) for part in x_mine]
     x_rest = [masked_rows(x_band, mask_wide, (1 - c) * rows // 2 + k * rows // 4, rows // 4) for k in range(2)]
 
+    mid_a = line(cross_a[:, 5 * LANES :], outward)
     mid_b, fwd_first = packed(
         [y, first_out],
         [cross_a, cross_b, swap_a, swap_b],
-        [13, 8],
+        [10, 8],
         [
             (0, 0, 3, 0, 0, (0, 0)),
             (1, 0, 3, 0, 0, (0, 1)),
-            (0, 3, 5, 0, 3, None),
-            (1, 3, 5, 0, 8, None),
+            (0, 3, 2, 0, 3, None),
+            (1, 3, 5, 0, 5, None),
             (2, (1,), 4, 1, 0, None),
             (3, (1,), 4, 1, 4, None),
         ],
     )
     (fwd_second,) = packed([second_out], [swap_a, swap_b], [8], [(0, (0,), 4, 0, 0, None), (1, (0,), 4, 0, 4, None)])
+    mid_a, mid_b, fwd_first = together(mid_a, mid_b, fwd_first)
     mid_b = line(mid_b, outward)
     fwd_first = line(fwd_first, cross)
     fwd_first, fwd_second, *x_across = together(fwd_first, fwd_second, *x_across)
@@ -582,10 +583,10 @@
         (1, [(1, 0, 8, 0, 1)]),
         (2, [(4, 0, 8, 0, 2)]),
         (3, [(5, 0, 8, 0, 3)]),
-        (4, [(6, 0, 3, 0, None), (6, 3, 5, 3, 4)]),
-        (5, [(6, 8, 5, 3, 5)]),
+        (4, [(6, 0, 3, 0, None), (6, 3, 2, 3, 4), (7, 0, 3, 5, 4)]),
+        (5, [(6, 5, 5, 3, 5)]),
     ]
-    total = whole_products(meta, xs, [own_a, own_b, cross_a, cross_b, swap_a, swap_b, mid_b], plan)
+    total = whole_products(meta, xs, [own_a, own_b, cross_a, cross_b, swap_a, swap_b, mid_b, mid_a], plan)
     last_at = jnp.where(left, 1, 0)
     total, last_at = together(total, last_at)
     (last,) = packed(

time: 165 us -> 157 us (0.952)
  waiting for transfers between devices: 90.8 us -> 81 us
    ppermute x14 -> x15, waiting for transfers between devices: 86.1 us -> 77.7 us  [line(): return lax.ppermute(value, 'grid', pairs)]
    ppermute x14 -> x15, starting transfers between devices: 18.9 us -> 20.6 us  [line(): return lax.ppermute(value, 'grid', pairs)]
  transfers between devices with their start and end apart: 20 -> 21, of which waited for: 10 -> 10; matrix products, arithmetic and copies ran while one was open for 2% -> 2% of each run, Pallas kernels for 26% -> 27%
where the time goes in v10:
time: 157 us; the launch traced here: 156 us
  waiting for transfers between devices  81 us (52%)
  Pallas kernels  46.8 us (30%)
  starting transfers between devices  22.5 us (14%)
  local copies, waits for them, and re-layouts  4.97 us (3%)
    ppermute x15, waiting for transfers between devices, line(): return lax.ppermute(value, 'grid', pairs)  77.7 us
    ppermute x15, starting transfers between devices, line(): return lax.ppermute(value, 'grid', pairs)  20.6 us
    pallas_call x1, Pallas kernels, whole_products(): pl.pallas_call(functools.partial(whole_kernel, plan), out_shape=jax.Shape...  14.8 us
    pallas_call x4, Pallas kernels, masked_rows(): pl.pallas_call(mask_kernel, grid_spec=pltpu.PrefetchScalarGridSpec(num_sc...  8.59 us
    pallas_call x1, Pallas kernels, half_products(): pl.pallas_call(half_kernel, out_shape=[jax.ShapeDtypeStruct((rows, n_done...  6.17 us
    pallas_call x1, Pallas kernels, rest_products(): pl.pallas_call(rest_kernel, out_shape=[jax.ShapeDtypeStruct((rows, width)...  5.38 us
    pallas_call x2, Pallas kernels, b_strips(): pl.pallas_call(strips_kernel, out_shape=[jax.ShapeDtypeStruct(shape, jnp....  4.24 us
    pallas_call x3, Pallas kernels, packed(): pl.pallas_call(functools.partial(pack_kernel, plan, len(sources)), out_sh...  4.02 us
  transfers between devices with their start and end apart: 21, of which 10 were waited for; matrix products, arithmetic and copies ran while one was open for 2% of the time, Pallas kernels for 27%

profile of v10, /device:TPU:0, one launch (start us, length us, event | category | flops | bytes accessed | tf_op | source)
XLA Modules:
  0.0 155.9 jit_solution(13646126739667095629)
XLA Ops:
  0.0 2.5 %b_strips.2 = bf16[512,1024]{1,0:T(8,128)(2,1)} custom-call(s32[1]{0:T(128)} %bitcast.7.quarters_ref, bf16[512,4096]{1,0:T(8,128)(2,1)} %w_ref.2), custom_call_target="tpu_custom_call" | custom-call | flops 1000 | bytes 1000 | tf_op jit(solution)/shard_map/b_strips/pallas_call | solution.py:81
  2.5 3.0 %collective-permute-start = (bf16[512,1024]{1,0:T(8,128)(2,1)}, bf16[512,1024]{1,0:T(8,128)(2,1)}, u32[]{:S(2)}, u32[]{:S(2)}) collective-permute-start(bf16[512,1024]{1,0:T(8,128)(2,1)} %b_strips.2), channel_id=1, source_target_pairs={{0,2},{2,0},{4,6},{6,4},{8,10},{10,8},{12,14},{14,12},{1,3},{3,1},... | collective-permute-start | bytes 3145736 | tf_op jit(solution)/shard_map/ppermute | solution.py:527
  5.6 1.7 %b_strips.3.refs_8_ = bf16[512,1024]{1,0:T(8,128)(2,1)} custom-call(s32[1]{0:T(128)} %bitcast.quarters_ref, bf16[512,4096]{1,0:T(8,128)(2,1)S(1)} %copy-done), custom_call_target="tpu_custom_call" | custom-call | flops 1000 | bytes 1000 | tf_op jit(solution)/shard_map/b_strips/pallas_call | solution.py:81
  7.3 1.6 %collective-permute-start.3 = (bf16[512,1024]{1,0:T(8,128)(2,1)}, bf16[512,1024]{1,0:T(8,128)(2,1)S(1)}, u32[]{:S(2)}, u32[]{:S(2)}) collective-permute-start(bf16[512,1024]{1,0:T(8,128)(2,1)} %b_strips.3.refs_8_), channel_id=1, source_target_pairs={{0,4},{2,6},{4,0},{6,2},{8,12},{10,14},{12,8},{14,10},{1,5},{3,7},... | collective-permute-start | bytes 3145736 | tf_op jit(solution)/shard_map/ppermute | solution.py:527
  10.7 2.1 %masked_rows.5.refs_1_ = bf16[128,4096]{1,0:T(8,128)(2,1)} custom-call(s32[1]{0:T(128)} %bitcast.9.first_ref, f32[8,1,4096]{2,1,0:T(1,128)} %reshape.22.mask_ref, bf16[512,4096]{1,0:T(8,128)(2,1)} %x_ref.7), custom_call_target="tpu_custom_call" | custom-call | flops 1000 | bytes 1000 | tf_op jit(solution)/shard_map/masked_rows/pallas_call | solution.py:138
  12.8 2.1 %masked_rows.4.refs_0_ = bf16[128,4096]{1,0:T(8,128)(2,1)} custom-call(s32[1]{0:T(128)} %bitcast.8.first_ref, f32[8,1,4096]{2,1,0:T(1,128)} %reshape.22.mask_ref, bf16[512,4096]{1,0:T(8,128)(2,1)} %x_ref.7), custom_call_target="tpu_custom_call" | custom-call | flops 1000 | bytes 1000 | tf_op jit(solution)/shard_map/masked_rows/pallas_call | solution.py:138
  14.9 14.1 %collective-permute-done.refs_9_ = bf16[512,1024]{1,0:T(8,128)(2,1)} collective-permute-done((bf16[512,1024]{1,0:T(8,128)(2,1)}, bf16[512,1024]{1,0:T(8,128)(2,1)}, u32[]{:S(2)}, u32[]{:S(2)}) %collective-permute-start) | collective-permute-done | bytes 1048608 | tf_op jit(solution)/shard_map/ppermute | solution.py:527
  29.1 3.1 %collective-permute-done.3.refs_2_.refs_0_.refs_12_ = bf16[512,1024]{1,0:T(8,128)(2,1)S(1)} collective-permute-done((bf16[512,1024]{1,0:T(8,128)(2,1)}, bf16[512,1024]{1,0:T(8,128)(2,1)S(1)}, u32[]{:S(2)}, u32[]{:S(2)}) %collective-permute-start.3) | collective-permute-done | bytes 1048608 | tf_op jit(solution)/shard_map/ppermute | solution.py:527
  32.2 1.6 %collective-permute-start.5 = (bf16[512,1024]{1,0:T(8,128)(2,1)}, bf16[512,1024]{1,0:T(8,128)(2,1)S(1)}, u32[]{:S(2)}, u32[]{:S(2)}) collective-permute-start(bf16[512,1024]{1,0:T(8,128)(2,1)} %collective-permute-done.refs_9_), channel_id=1, source_target_pairs={{0,4},{2,6},{4,0},{6,2},{8,12},{10,14},{12,8},{14,10},{1,5},{3,7},... | collective-permute-start | bytes 3145736 | tf_op jit(solution)/shard_map/ppermute | solution.py:527
  33.8 1.6 %collective-permute-start.4 = (bf16[512,1024]{1,0:T(8,128)(2,1)}, bf16[512,1024]{1,0:T(8,128)(2,1)}, u32[]{:S(2)}, u32[]{:S(2)}) collective-permute-start(bf16[512,1024]{1,0:T(8,128)(2,1)} %collective-permute-done.refs_9_), channel_id=1, source_target_pairs={{4,8},{6,10},{8,4},{10,6},{5,9},{7,11},{9,5},{11,7},{20,24},{22,26... | collective-permute-start | bytes 3145736 | tf_op jit(solution)/shard_map/ppermute | solution.py:527
  35.4 1.3 collective-permute-start.2
  37.5 1.4 collective-permute-start.8
  38.9 19.6 %collective-permute-done.5.refs_3_.refs_1_.refs_13_ = bf16[512,1024]{1,0:T(8,128)(2,1)S(1)} collective-permute-done((bf16[512,1024]{1,0:T(8,128)(2,1)}, bf16[512,1024]{1,0:T(8,128)(2,1)S(1)}, u32[]{:S(2)}, u32[]{:S(2)}) %collective-permute-start.5) | collective-permute-done | bytes 1048608 | tf_op jit(solution)/shard_map/ppermute | solution.py:527
  58.5 3.2 %packed.3 = (bf16[512,1280]{1,0:T(8,128)(2,1)}, bf16[512,1024]{1,0:T(8,128)(2,1)}) custom-call(s32[2]{0:T(128)S(1)} %pad_add_fusion.1.meta_ref, bf16[512,1024]{1,0:T(8,128)(2,1)S(1)} %collective-permute-done.1.refs_0_.refs_10_, bf16[512,1024]{1,0:T(8,128)(2,1)} %collective-permute-done.4.refs_1_.refs_11_, ...), custom_call_target="tpu_custom_call" | custom-call | flops 1000 | bytes 1000 | tf_op jit(solution)/shard_map/packed/pallas_call | solution.py:119
  61.7 2.9 %collective-permute-done.2.refs_15_ = bf16[512,384]{1,0:T(8,128)(2,1)} collective-permute-done((bf16[512,384]{1,0:T(8,128)(2,1)S(1)}, bf16[512,384]{1,0:T(8,128)(2,1)}, u32[]{:S(2)}, u32[]{:S(2)}) %collective-permute-start.2) | collective-permute-done | bytes 393248 | tf_op jit(solution)/shard_map/ppermute | solution.py:527
  64.6 1.6 %collective-permute-start.6 = (bf16[512,1024]{1,0:T(8,128)(2,1)}, bf16[512,1024]{1,0:T(8,128)(2,1)}, u32[]{:S(2)}, u32[]{:S(2)}) collective-permute-start(bf16[512,1024]{1,0:T(8,128)(2,1)} %get-tuple-element.41), channel_id=1, source_target_pairs={{4,8},{6,10},{8,4},{10,6},{5,9},{7,11},{9,5},{11,7},{20,24},{22,26... | collective-permute-start | bytes 3145736 | tf_op jit(solution)/shard_map/ppermute | solution.py:527
  67.8 15.3 %collective-permute-done.8.refs_5_ = bf16[128,4096]{1,0:T(8,128)(2,1)} collective-permute-done((bf16[128,4096]{1,0:T(8,128)(2,1)}, bf16[128,4096]{1,0:T(8,128)(2,1)}, u32[]{:S(2)}, u32[]{:S(2)}) %collective-permute-start.8) | collective-permute-done | bytes 1048608 | tf_op jit(solution)/shard_map/ppermute | solution.py:527
  84.3 1.3 collective-permute-start.12
  85.6 2.1 %masked_rows.7.refs_3_ = bf16[128,4096]{1,0:T(8,128)(2,1)} custom-call(s32[1]{0:T(128)} %bitcast.11.first_ref, f32[8,1,4096]{2,1,0:T(1,128)} %reshape.22.mask_ref, bf16[512,4096]{1,0:T(8,128)(2,1)} %x_ref.7), custom_call_target="tpu_custom_call" | custom-call | flops 1000 | bytes 1000 | tf_op jit(solution)/shard_map/masked_rows/pallas_call | solution.py:138
  87.7 2.2 %masked_rows.6.refs_2_ = bf16[128,4096]{1,0:T(8,128)(2,1)} custom-call(s32[1]{0:T(128)} %bitcast.10.first_ref, f32[8,1,4096]{2,1,0:T(1,128)} %reshape.22.mask_ref, bf16[512,4096]{1,0:T(8,128)(2,1)} %x_ref.7), custom_call_target="tpu_custom_call" | custom-call | flops 1000 | bytes 1000 | tf_op jit(solution)/shard_map/masked_rows/pallas_call | solution.py:138
  90.6 6.8 %collective-permute-done.11.refs_14_ = bf16[512,1280]{1,0:T(8,128)(2,1)} collective-permute-done((bf16[512,1280]{1,0:T(8,128)(2,1)}, bf16[512,1280]{1,0:T(8,128)(2,1)}, u32[]{:S(2)}, u32[]{:S(2)}) %collective-permute-start.11) | collective-permute-done | bytes 1310752 | tf_op jit(solution)/shard_map/ppermute | solution.py:527
  98.3 14.8 %whole_products.1.refs_8_ = f32[2,512,1024]{2,1,0:T(8,128)} custom-call(s32[14]{0:T(128)} %stack.133.meta_ref, bf16[128,4096]{1,0:T(8,128)(2,1)} %masked_rows.4.refs_0_, bf16[128,4096]{1,0:T(8,128)(2,1)} %masked_rows.5.refs_1_, bf16[128,4096]{1,0:T(8,128)(2,1)} %masked_rows.6.refs_2_, bf16[128,4096]{1,0:T(8,128)(2,1)} %masked_rows.7.refs_3_, ...), custom_call_target="tpu_custom_call" | custom-call | flops 1000 | bytes 1000 | tf_op jit(solution)/shard_map/whole_products/pallas_call | solution.py:245
  113.9 1.3 collective-permute-start.14
  115.8 3.5 %collective-permute-done.12.refs_10_ = bf16[512,1024]{1,0:T(8,128)(2,1)} collective-permute-done((bf16[512,1024]{1,0:T(8,128)(2,1)}, bf16[512,1024]{1,0:T(8,128)(2,1)}, u32[]{:S(2)}, u32[]{:S(2)}) %collective-permute-start.12) | collective-permute-done | bytes 1048608 | tf_op jit(solution)/shard_map/ppermute | solution.py:527
  119.3 6.2 %half_products.1 = (bf16[256,640]{1,0:T(8,128)(2,1)}, bf16[256,640]{1,0:T(8,128)(2,1)}, bf16[256,640]{1,0:T(8,128)(2,1)}, bf16[256,640]{1,0:T(8,128)(2,1)}, f32[2,512,384]{2,1,0:T(8,128)}) custom-call(s32[9]{0:T(128)} %stack.123.meta_ref, bf16[128,4096]{1,0:T(8,128)(2,1)} %masked_rows.4.refs_0_, bf16[128,4096]{1,0:T(8,128)(2,1)} %masked_rows.5.refs_1_, ...), custom_call_target="tpu_custom_call" | custom-call | flops 1000 | bytes 1000 | tf_op jit(solution)/shard_map/half_products/pallas_call | solution.py:361
  125.6 1.4 collective-permute-start.19
  128.1 8.5 %collective-permute-done.14.refs_9_ = bf16[512,768]{1,0:T(8,128)(2,1)S(1)} collective-permute-done((bf16[512,768]{1,0:T(8,128)(2,1)S(1)}, bf16[512,768]{1,0:T(8,128)(2,1)S(1)}, u32[]{:S(2)}, u32[]{:S(2)}) %collective-permute-start.14) | collective-permute-done | bytes 786464 | tf_op jit(solution)/shard_map/ppermute | solution.py:527
  137.5 5.4 %rest_products.1 = (bf16[256,384]{1,0:T(8,128)(2,1)}, bf16[256,384]{1,0:T(8,128)(2,1)}, bf16[256,384]{1,0:T(8,128)(2,1)}, bf16[256,384]{1,0:T(8,128)(2,1)}) custom-call(s32[7]{0:T(128)} %stack.116.meta_ref, bf16[128,4096]{1,0:T(8,128)(2,1)} %masked_rows.4.refs_0_, bf16[128,4096]{1,0:T(8,128)(2,1)} %masked_rows.5.refs_1_, ...), custom_call_target="tpu_custom_call" | custom-call | flops 1000 | bytes 1000 | tf_op jit(solution)/shard_map/rest_products/pallas_call | solution.py:439
  145.1 2.0 %assembled.2.refs_4_ = bf16[256,4096]{1,0:T(8,128)(2,1)} custom-call(s32[2]{0:T(128)S(1)} %get-tuple-element.62.place_ref, f32[4,1,4096]{2,1,0:T(1,128)S(1)} %reshape.20.mask_ref, bf16[256,640]{1,0:T(8,128)(2,1)S(1)} %copy-done.5, bf16[256,640]{1,0:T(8,128)(2,1)S(1)} %collective-permute-done.15.refs_1_, ...), custom_call_target="tpu_custom_call" | custom-call | flops 1000 | bytes 1000 | tf_op jit(solution)/shard_map/assembled/pallas_call | solution.py:486
  147.1 3.8 %collective-permute-done.17.refs_2_ = bf16[256,384]{1,0:T(8,128)(2,1)S(1)} collective-permute-done((bf16[256,384]{1,0:T(8,128)(2,1)}, bf16[256,384]{1,0:T(8,128)(2,1)S(1)}, u32[]{:S(2)}, u32[]{:S(2)}) %collective-permute-start.17) | collective-permute-done | bytes 196640 | tf_op jit(solution)/shard_map/ppermute | solution.py:527
  150.9 3.3 %collective-permute-done.18.refs_3_ = bf16[256,384]{1,0:T(8,128)(2,1)S(1)} collective-permute-done((bf16[256,384]{1,0:T(8,128)(2,1)}, bf16[256,384]{1,0:T(8,128)(2,1)S(1)}, u32[]{:S(2)}, u32[]{:S(2)}) %collective-permute-start.18) | collective-permute-done | bytes 196640 | tf_op jit(solution)/shard_map/ppermute | solution.py:602
  154.2 1.6 %assembled.3 = bf16[256,4096]{1,0:T(8,128)(2,1)} custom-call(s32[2]{0:T(128)S(1)} %get-tuple-element.61.place_ref, f32[4,1,4096]{2,1,0:T(1,128)S(1)} %reshape.20.mask_ref, bf16[256,384]{1,0:T(8,128)(2,1)S(1)} %copy-done.6, bf16[256,384]{1,0:T(8,128)(2,1)S(1)} %collective-permute-done.16.refs_1_, ...), custom_call_target="tpu_custom_call", output_to_operand_aliasing={{}: (6, {})} | custom-call | flops 1000 | bytes 1000 | tf_op jit(solution)/shard_map/assembled/pallas_call | solution.py:486
  (59 shorter events, 12.4 us)
Async XLA Ops:
  0.0 5.6 %copy-start = (bf16[512,4096]{1,0:T(8,128)(2,1)S(1)}, bf16[512,4096]{1,0:T(8,128)(2,1)}, u32[]{:S(2)}) copy-start(bf16[512,4096]{1,0:T(8,128)(2,1)} %w_ref.2) | copy-start | bytes 12582916
  2.5 26.5 %collective-permute-start = (bf16[512,1024]{1,0:T(8,128)(2,1)}, bf16[512,1024]{1,0:T(8,128)(2,1)}, u32[]{:S(2)}, u32[]{:S(2)}) collective-permute-start(bf16[512,1024]{1,0:T(8,128)(2,1)} %b_strips.2), channel_id=1, source_target_pairs={{0,2},{2,0},{4,6},{6,4},{8,10},{10,8},{12,14},{14,12},{1,3},{3,1},... | collective-permute-start | bytes 3145736 | tf_op jit(solution)/shard_map/ppermute | solution.py:527
  5.6 4.1 %copy-start.9 = (s32[8,64]{1,0:T(8,128)S(1)}, s32[8,64]{1,0:T(8,128)}, u32[]{:S(2)}) copy-start(s32[8,64]{1,0:T(8,128)} %param.6) | copy-start | bytes 6148
  7.3 24.9 %collective-permute-start.3 = (bf16[512,1024]{1,0:T(8,128)(2,1)}, bf16[512,1024]{1,0:T(8,128)(2,1)S(1)}, u32[]{:S(2)}, u32[]{:S(2)}) collective-permute-start(bf16[512,1024]{1,0:T(8,128)(2,1)} %b_strips.3.refs_8_), channel_id=1, source_target_pairs={{0,4},{2,6},{4,0},{6,2},{8,12},{10,14},{12,8},{14,10},{1,5},{3,7},... | collective-permute-start | bytes 3145736 | tf_op jit(solution)/shard_map/ppermute | solution.py:527
  8.9 26.4 %collective-permute-start.1 = (bf16[512,1024]{1,0:T(8,128)(2,1)}, bf16[512,1024]{1,0:T(8,128)(2,1)S(1)}, u32[]{:S(2)}, u32[]{:S(2)}) collective-permute-start(bf16[512,1024]{1,0:T(8,128)(2,1)} %b_strips.3.refs_8_), channel_id=1, source_target_pairs={{4,8},{6,10},{8,4},{10,6},{5,9},{7,11},{9,5},{11,7},{20,24},{22,26... | collective-permute-start | bytes 3145736 | tf_op jit(solution)/shard_map/ppermute | solution.py:527
  32.2 35.4 %copy-start.1 = (bf16[512,1024]{1,0:T(8,128)(2,1)}, bf16[512,1024]{1,0:T(8,128)(2,1)S(1)}, u32[]{:S(2)}) copy-start(bf16[512,1024]{1,0:T(8,128)(2,1)S(1)} %collective-permute-done.3.refs_2_.refs_0_.refs_12_) | copy-start | bytes 3145732
  32.2 26.3 %collective-permute-start.5 = (bf16[512,1024]{1,0:T(8,128)(2,1)}, bf16[512,1024]{1,0:T(8,128)(2,1)S(1)}, u32[]{:S(2)}, u32[]{:S(2)}) collective-permute-start(bf16[512,1024]{1,0:T(8,128)(2,1)} %collective-permute-done.refs_9_), channel_id=1, source_target_pairs={{0,4},{2,6},{4,0},{6,2},{8,12},{10,14},{12,8},{14,10},{1,5},{3,7},... | collective-permute-start | bytes 3145736 | tf_op jit(solution)/shard_map/ppermute | solution.py:527
  33.8 24.7 %collective-permute-start.4 = (bf16[512,1024]{1,0:T(8,128)(2,1)}, bf16[512,1024]{1,0:T(8,128)(2,1)}, u32[]{:S(2)}, u32[]{:S(2)}) collective-permute-start(bf16[512,1024]{1,0:T(8,128)(2,1)} %collective-permute-done.refs_9_), channel_id=1, source_target_pairs={{4,8},{6,10},{8,4},{10,6},{5,9},{7,11},{9,5},{11,7},{20,24},{22,26... | collective-permute-start | bytes 3145736 | tf_op jit(solution)/shard_map/ppermute | solution.py:527
  35.4 26.3 %copy-start.3 = (bf16[512,1024]{1,0:T(8,128)(2,1)}, bf16[512,1024]{1,0:T(8,128)(2,1)S(1)}, u32[]{:S(2)}) copy-start(bf16[512,1024]{1,0:T(8,128)(2,1)S(1)} %collective-permute-done.1.refs_0_.refs_10_) | copy-start | bytes 3145732
  35.4 29.2 %collective-permute-start.2 = (bf16[512,384]{1,0:T(8,128)(2,1)S(1)}, bf16[512,384]{1,0:T(8,128)(2,1)}, u32[]{:S(2)}, u32[]{:S(2)}) collective-permute-start(bf16[512,384]{1,0:T(8,128)(2,1)S(1)} %slice.4), channel_id=1, source_target_pairs={{4,0},{6,2},{8,12},{10,14},{5,1},{7,3},{9,13},{11,15},{20,16},{22,... | collective-permute-start | bytes 1179656 | tf_op jit(solution)/shard_map/ppermute | solution.py:527
  36.8 30.9 %collective-permute-start.7 = (bf16[128,4096]{1,0:T(8,128)(2,1)}, bf16[128,4096]{1,0:T(8,128)(2,1)}, u32[]{:S(2)}, u32[]{:S(2)}) collective-permute-start(bf16[128,4096]{1,0:T(8,128)(2,1)} %masked_rows.4.refs_0_), channel_id=1, source_target_pairs={{0,2},{2,0},{4,6},{6,4},{8,10},{10,8},{12,14},{14,12},{1,3},{3,1},... | collective-permute-start | bytes 3145736 | tf_op jit(solution)/shard_map/ppermute | solution.py:527
  37.5 45.5 %collective-permute-start.8 = (bf16[128,4096]{1,0:T(8,128)(2,1)}, bf16[128,4096]{1,0:T(8,128)(2,1)}, u32[]{:S(2)}, u32[]{:S(2)}) collective-permute-start(bf16[128,4096]{1,0:T(8,128)(2,1)} %masked_rows.5.refs_1_), channel_id=1, source_target_pairs={{0,2},{2,0},{4,6},{6,4},{8,10},{10,8},{12,14},{14,12},{1,3},{3,1},... | collective-permute-start | bytes 3145736 | tf_op jit(solution)/shard_map/ppermute | solution.py:527
  58.5 9.1 %copy-start.2 = (bf16[512,1024]{1,0:T(8,128)(2,1)}, bf16[512,1024]{1,0:T(8,128)(2,1)S(1)}, u32[]{:S(2)}) copy-start(bf16[512,1024]{1,0:T(8,128)(2,1)S(1)} %collective-permute-done.5.refs_3_.refs_1_.refs_13_) | copy-start | bytes 3145732
  64.6 18.4 %collective-permute-start.6 = (bf16[512,1024]{1,0:T(8,128)(2,1)}, bf16[512,1024]{1,0:T(8,128)(2,1)}, u32[]{:S(2)}, u32[]{:S(2)}) collective-permute-start(bf16[512,1024]{1,0:T(8,128)(2,1)} %get-tuple-element.41), channel_id=1, source_target_pairs={{4,8},{6,10},{8,4},{10,6},{5,9},{7,11},{9,5},{11,7},{20,24},{22,26... | collective-permute-start | bytes 3145736 | tf_op jit(solution)/shard_map/ppermute | solution.py:527
  66.3 31.1 %collective-permute-start.11 = (bf16[512,1280]{1,0:T(8,128)(2,1)}, bf16[512,1280]{1,0:T(8,128)(2,1)}, u32[]{:S(2)}, u32[]{:S(2)}) collective-permute-start(bf16[512,1280]{1,0:T(8,128)(2,1)} %get-tuple-element.44), channel_id=1, source_target_pairs={{4,0},{6,2},{8,12},{10,14},{5,1},{7,3},{9,13},{11,15},{20,16},{22,... | collective-permute-start | bytes 3932168 | tf_op jit(solution)/shard_map/ppermute | solution.py:527
  83.0 14.3 %collective-permute-start.10 = (bf16[128,4096]{1,0:T(8,128)(2,1)}, bf16[128,4096]{1,0:T(8,128)(2,1)S(1)}, u32[]{:S(2)}, u32[]{:S(2)}) collective-permute-start(bf16[128,4096]{1,0:T(8,128)(2,1)} %collective-permute-done.8.refs_5_), channel_id=1, source_target_pairs={{0,1},{1,0},{2,3},{3,2},{4,5},{5,4},{6,7},{7,6},{8,9},{9,8},{10,11... | collective-permute-start | bytes 3145736 | tf_op jit(solution)/shard_map/ppermute | solution.py:570
  83.0 14.3 %collective-permute-start.9 = (bf16[128,4096]{1,0:T(8,128)(2,1)}, bf16[128,4096]{1,0:T(8,128)(2,1)}, u32[]{:S(2)}, u32[]{:S(2)}) collective-permute-start(bf16[128,4096]{1,0:T(8,128)(2,1)} %collective-permute-done.7.refs_4_), channel_id=1, source_target_pairs={{0,1},{1,0},{2,3},{3,2},{4,5},{5,4},{6,7},{7,6},{8,9},{9,8},{10,11... | collective-permute-start | bytes 3145736 | tf_op jit(solution)/shard_map/ppermute | solution.py:570
  83.6 29.6 %collective-permute-start.13 = (bf16[512,1024]{1,0:T(8,128)(2,1)S(1)}, bf16[512,1024]{1,0:T(8,128)(2,1)S(1)}, u32[]{:S(2)}, u32[]{:S(2)}) collective-permute-start(bf16[512,1024]{1,0:T(8,128)(2,1)S(1)} %packed.4), channel_id=1, source_target_pairs={{4,8},{6,10},{8,4},{10,6},{5,9},{7,11},{9,5},{11,7},{20,24},{22,26... | collective-permute-start | bytes 3145736 | tf_op jit(solution)/shard_map/ppermute | solution.py:527
  84.3 35.1 %collective-permute-start.12 = (bf16[512,1024]{1,0:T(8,128)(2,1)}, bf16[512,1024]{1,0:T(8,128)(2,1)}, u32[]{:S(2)}, u32[]{:S(2)}) collective-permute-start(bf16[512,1024]{1,0:T(8,128)(2,1)} %collective-permute-done.6.refs_9_), channel_id=1, source_target_pairs={{4,0},{6,2},{8,12},{10,14},{5,1},{7,3},{9,13},{11,15},{20,16},{22,... | collective-permute-start | bytes 3145736 | tf_op jit(solution)/shard_map/ppermute | solution.py:527
  97.3 1.0 copy-start.7
  113.2 6.2 %copy-start.4 = (bf16[512,1024]{1,0:T(8,128)(2,1)}, bf16[512,1024]{1,0:T(8,128)(2,1)S(1)}, u32[]{:S(2)}) copy-start(bf16[512,1024]{1,0:T(8,128)(2,1)S(1)} %collective-permute-done.13.refs_11_.refs_0_) | copy-start | bytes 3145732
  113.9 22.7 %collective-permute-start.14 = (bf16[512,768]{1,0:T(8,128)(2,1)S(1)}, bf16[512,768]{1,0:T(8,128)(2,1)S(1)}, u32[]{:S(2)}, u32[]{:S(2)}) collective-permute-start(bf16[512,768]{1,0:T(8,128)(2,1)S(1)} %packed.5), channel_id=1, source_target_pairs={{4,0},{6,2},{8,12},{10,14},{5,1},{7,3},{9,13},{11,15},{20,16},{22,... | collective-permute-start | bytes 2359304 | tf_op jit(solution)/shard_map/ppermute | solution.py:527
  125.5 2.6 %collective-permute-start.15 = (bf16[256,640]{1,0:T(8,128)(2,1)}, bf16[256,640]{1,0:T(8,128)(2,1)S(1)}, u32[]{:S(2)}, u32[]{:S(2)}) collective-permute-start(bf16[256,640]{1,0:T(8,128)(2,1)} %get-tuple-element.51), channel_id=1, source_target_pairs={{0,1},{1,0},{2,3},{3,2},{4,5},{5,4},{6,7},{7,6},{8,9},{9,8},{10,11... | collective-permute-start | bytes 983048 | tf_op jit(solution)/shard_map/ppermute | solution.py:600
  125.6 19.5 %collective-permute-start.19 = (bf16[256,640]{1,0:T(8,128)(2,1)}, bf16[256,640]{1,0:T(8,128)(2,1)S(1)}, u32[]{:S(2)}, u32[]{:S(2)}) collective-permute-start(bf16[256,640]{1,0:T(8,128)(2,1)} %get-tuple-element.59), channel_id=1, source_target_pairs={{0,2},{2,0},{4,6},{6,4},{8,10},{10,8},{12,14},{14,12},{1,3},{3,1},... | collective-permute-start | bytes 983048 | tf_op jit(solution)/shard_map/ppermute | solution.py:527
  127.0 18.1 %collective-permute-start.20 = (bf16[256,640]{1,0:T(8,128)(2,1)}, bf16[256,640]{1,0:T(8,128)(2,1)S(1)}, u32[]{:S(2)}, u32[]{:S(2)}) collective-permute-start(bf16[256,640]{1,0:T(8,128)(2,1)} %get-tuple-element.60), channel_id=1, source_target_pairs={{0,3},{1,2},{2,1},{3,0},{4,7},{5,6},{6,5},{7,4},{8,11},{9,10},{10,... | collective-permute-start | bytes 983048 | tf_op jit(solution)/shard_map/ppermute | solution.py:602
  136.6 0.9 copy-start.8
  137.5 7.3 %copy-start.10 = (s32[4,64]{1,0:T(4,128)S(1)}, s32[4,64]{1,0:T(4,128)}, u32[]{:S(2)}) copy-start(s32[4,64]{1,0:T(4,128)} %param.7) | copy-start | bytes 3076
  137.5 7.7 %copy-start.5 = (bf16[256,640]{1,0:T(8,128)(2,1)S(1)}, bf16[256,640]{1,0:T(8,128)(2,1)}, u32[]{:S(2)}) copy-start(bf16[256,640]{1,0:T(8,128)(2,1)} %get-tuple-element.57.refs_0_) | copy-start | bytes 983044
  142.8 11.4 %copy-start.6 = (bf16[256,384]{1,0:T(8,128)(2,1)S(1)}, bf16[256,384]{1,0:T(8,128)(2,1)}, u32[]{:S(2)}) copy-start(bf16[256,384]{1,0:T(8,128)(2,1)} %get-tuple-element.53.refs_0_) | copy-start | bytes 589828
  142.9 4.3 %collective-permute-start.16 = (bf16[256,384]{1,0:T(8,128)(2,1)}, bf16[256,384]{1,0:T(8,128)(2,1)S(1)}, u32[]{:S(2)}, u32[]{:S(2)}) collective-permute-start(bf16[256,384]{1,0:T(8,128)(2,1)} %get-tuple-element.54), channel_id=1, source_target_pairs={{0,1},{1,0},{2,3},{3,2},{4,5},{5,4},{6,7},{7,6},{8,9},{9,8},{10,11... | collective-permute-start | bytes 589832 | tf_op jit(solution)/shard_map/ppermute | solution.py:600
  142.9 8.0 %collective-permute-start.17 = (bf16[256,384]{1,0:T(8,128)(2,1)}, bf16[256,384]{1,0:T(8,128)(2,1)S(1)}, u32[]{:S(2)}, u32[]{:S(2)}) collective-permute-start(bf16[256,384]{1,0:T(8,128)(2,1)} %get-tuple-element.55), channel_id=1, source_target_pairs={{0,2},{2,0},{4,6},{6,4},{8,10},{10,8},{12,14},{14,12},{1,3},{3,1},... | collective-permute-start | bytes 589832 | tf_op jit(solution)/shard_map/ppermute | solution.py:527
  144.1 10.2 %collective-permute-start.18 = (bf16[256,384]{1,0:T(8,128)(2,1)}, bf16[256,384]{1,0:T(8,128)(2,1)S(1)}, u32[]{:S(2)}, u32[]{:S(2)}) collective-permute-start(bf16[256,384]{1,0:T(8,128)(2,1)} %get-tuple-element.56), channel_id=1, source_target_pairs={{0,3},{1,2},{2,1},{3,0},{4,7},{5,6},{6,5},{7,4},{8,11},{9,10},{10,... | collective-permute-start | bytes 589832 | tf_op jit(solution)/shard_map/ppermute | solution.py:602

commit v11 on v10

--- a/solution.py
+++ b/solution.py
@@ -49,48 +49,58 @@
     return (mine * keep).astype(jnp.bfloat16)
 
 
-def strips_kernel(quarters_ref, w_ref, *refs):
-    *b_refs, held, sems = refs
-    _, panel, width = held.shape
+def strips_kernel(quarter_ref, w_ref, b_ref, held, made, in_sems, out_sems):
+    panel, width = held.shape
+    quarter = quarter_ref[0]
+
+    def strip(j):
+        return slice(j * LANES, (j + 1) * LANES)
+
+    def load(j):
+        at = pl.multiple_of(j * panel + quarter * LANES, LANES)
+        return pltpu.make_async_copy(w_ref.at[:, pl.ds(at, LANES)], held.at[:, strip(j)], in_sems.at[j])
+
+    def give(j):
+        return pltpu.make_async_copy(made.at[:, strip(j)], b_ref.at[:, strip(j)], out_sems.at[j])
+
     band = width // LANES
-
-    def copy(k, j):
-        at = pl.multiple_of(j * panel + quarters_ref[k] * LANES, LANES)
-        to = held.at[k, :, j * LANES : (j + 1) * LANES]
-        return pltpu.make_async_copy(w_ref.at[:, pl.ds(at, LANES)], to, sems.at[k, j])
-
-    for k in range(len(b_refs)):
-        for j in range(band):
-            copy(k, j).start()
-    for k, b_ref in enumerate(b_refs):
-        for j in range(band):
-            copy(k, j).wait()
-            value = -0.5 * held[k, :, j * LANES : (j + 1) * LANES].astype(jnp.float32)
-            if j == band // 2:
-                rows = lax.broadcasted_iota(jnp.int32, value.shape, 0)
-                cols = lax.broadcasted_iota(jnp.int32, value.shape, 1)
-                value = value + jnp.where(rows == cols + quarters_ref[k] * LANES, 1.5, 0.0)
-            b_ref[:, j * LANES : (j + 1) * LANES] = value.astype(jnp.bfloat16)
-
-
-def b_strips(w_band, quarters, limit):
+    for j in range(band):
+        load(j).start()
+    for j in range(band):
+        load(j).wait()
+        value = -0.5 * held[:, strip(j)].astype(jnp.float32)
+        if j == band // 2:
+            rows = lax.broadcasted_iota(jnp.int32, value.shape, 0)
+            cols = lax.broadcasted_iota(jnp.int32, value.shape, 1)
+            value = value + jnp.where(rows == cols + quarter * LANES, 1.5, 0.0)
+        made[:, strip(j)] = value.astype(jnp.bfloat16)
+        give(j).start()
+    for j in range(band):
+        give(j).wait()
+
+
+def b_strips(w_band, quarter, limit):
     panel = w_band.shape[0]
     band = w_band.shape[1] // panel
-    n = len(quarters)
     shape = (panel, band * LANES)
     return pl.pallas_call(
         strips_kernel,
-        out_shape=[jax.ShapeDtypeStruct(shape, jnp.bfloat16)] * n,
+        out_shape=jax.ShapeDtypeStruct(shape, jnp.bfloat16),
         in_specs=[
             pl.BlockSpec(memory_space=pltpu.SMEM),
             pl.BlockSpec(memory_space=pltpu.HBM),
         ],
-        out_specs=[pl.BlockSpec(memory_space=pltpu.VMEM)] * n,
-        scratch_shapes=[pltpu.VMEM((n, *shape), jnp.bfloat16), pltpu.SemaphoreType.DMA((n, band))],
+        out_specs=pl.BlockSpec(memory_space=pl.ANY),
+        scratch_shapes=[
+            pltpu.VMEM(shape, jnp.bfloat16),
+            pltpu.VMEM(shape, jnp.bfloat16),
+            pltpu.SemaphoreType.DMA((band,)),
+            pltpu.SemaphoreType.DMA((band,)),
+        ],
         compiler_params=pltpu.CompilerParams(vmem_limit_bytes=limit * MIB),
         cost_estimate=SMALL,
         name="b_strips",
-    )(jnp.stack(quarters), w_band)
+    )(quarter.reshape(1), w_band)
 
 
 def pack_kernel(plan, n_in, meta_ref, *refs):
@@ -385,7 +395,7 @@
     x_refs, (rest_ref, b_ref), refs = refs[:PARTS], refs[PARTS : PARTS + 2], refs[PARTS + 2 :]
     out_refs, xv, bv, acc, pieces, x_sems, b_sem, rest_sems, out_sems = refs[:4], *refs[4:]
     band = acc.shape[2] // (2 * LANES)
-    half = bv.shape[1] // 2
+    half = (bv.shape[1] - LANES) // 2
     is_end = meta_ref[0]
 
     def offset_of(p, g):
@@ -426,6 +436,8 @@
         def _():
             for p in range(2):
                 add_product(acc, xv[p, g], bv[:, p * half : (p + 1) * half], g, offset_of(p, g) + meta_ref[1])
+            p = meta_ref[8]
+            add_product(acc, xv[p, g], bv[:, 2 * half :], g, offset_of(p, g) + meta_ref[7])
 
     finish(acc, wait_for, add, meta_ref[2] + band // 2, out_refs, pieces, out_sems)
 
@@ -528,12 +540,12 @@
 
     first_out, second_out = jnp.where(left, 0, 4), jnp.where(left, 4, 0)
     first_in, second_in = second_out, first_out
-    last_in = jnp.where(left, 1, 4)
-
-    (sent_b,) = b_strips(w_band, [q ^ 2], 58)
+    last_in = jnp.where(left, 2, 4)
+
+    sent_b = b_strips(w_band, q ^ 2, 58)
     own_b = line(sent_b, across)
     sent_b, w_band = together(sent_b, w_band)
-    (own_a,) = b_strips(w_band, [q], 48)
+    own_a = b_strips(w_band, q, 58)
     swap_a = line(own_a, swap)
     cross_a = line(own_a, cross)
     mask_wide = widen(a_mask, block)
@@ -587,10 +599,15 @@
         (5, [(6, 5, 5, 3, 5)]),
     ]
     total = whole_products(meta, xs, [own_a, own_b, cross_a, cross_b, swap_a, swap_b, mid_b, mid_a], plan)
-    last_at = jnp.where(left, 1, 0)
+    last_at = jnp.where(left, 2, 0)
     total, last_at = together(total, last_at)
+    extra_in, extra_panel = jnp.where(left, 1, 6), jnp.where(left, 1 - y, y)
+    extra_at = jnp.where(left, 1, 2) + 4 * extra_panel
     (last,) = packed(
-        [last_at, last_at + 4], [fwd_second], [6], [(0, (0,), 3, 0, 0, None), (0, (1,), 3, 0, 3, None)]
+        [last_at, last_at + 4, extra_at],
+        [fwd_second],
+        [5],
+        [(0, (0,), 2, 0, 0, None), (0, (1,), 2, 0, 2, None), (0, (2,), 1, 0, 4, None)],
     )
     far_second = line(last, outward)
 
@@ -609,7 +626,7 @@
     far_second, done[1] = together(far_second, done[1])
     keep_wide = widen(keep_mask, block)
     out = assembled(jnp.stack([q, done_at]).astype(jnp.int32), keep_wide, done)
-    meta = jnp.stack([is_end, last_in, rest_at, *fourth]).astype(jnp.int32)
+    meta = jnp.stack([is_end, last_in, rest_at, *fourth, extra_in, extra_panel]).astype(jnp.int32)
     rest = exchanged(rest_products(meta, xs, rest, far_second, own_a.shape[1]))
     return assembled(jnp.stack([q, rest_at]).astype(jnp.int32), keep_wide, rest, out)
 

time: 157 us -> 155 us (0.987)
  waiting for transfers between devices: 81 us -> 77.1 us
    ppermute x15, waiting for transfers between devices: 77.7 us -> 73.3 us  [line(): return lax.ppermute(value, 'grid', pairs)]
  transfers between devices with their start and end apart: 21 -> 21, of which waited for: 10 -> 11; matrix products, arithmetic and copies ran while one was open for 2% -> 2% of each run, Pallas kernels for 27% -> 28%
where the time goes in v11:
time: 155 us; the launch traced here: 153 us
  waiting for transfers between devices  77.1 us (50%)
  Pallas kernels  46.7 us (30%)
  starting transfers between devices  22.5 us (15%)
  local copies, waits for them, and re-layouts  5.98 us (4%)
    ppermute x15, waiting for transfers between devices, line(): return lax.ppermute(value, 'grid', pairs)  73.3 us
    ppermute x15, starting transfers between devices, line(): return lax.ppermute(value, 'grid', pairs)  19.8 us
    pallas_call x1, Pallas kernels, whole_products(): pl.pallas_call(functools.partial(whole_kernel, plan), out_shape=jax.Shape...  14.8 us
    pallas_call x4, Pallas kernels, masked_rows(): pl.pallas_call(mask_kernel, grid_spec=pltpu.PrefetchScalarGridSpec(num_sc...  8.59 us
    pallas_call x1, Pallas kernels, half_products(): pl.pallas_call(half_kernel, out_shape=[jax.ShapeDtypeStruct((rows, n_done...  6.17 us
    pallas_call x1, Pallas kernels, rest_products(): pl.pallas_call(rest_kernel, out_shape=[jax.ShapeDtypeStruct((rows, width)...  5.1 us
    pallas_call x2, Pallas kernels, b_strips(): pl.pallas_call(strips_kernel, out_shape=jax.ShapeDtypeStruct(shape, jnp.b...  4.36 us
    pallas_call x3, Pallas kernels, packed(): pl.pallas_call(functools.partial(pack_kernel, plan, len(sources)), out_sh...  4.04 us
  transfers between devices with their start and end apart: 21, of which 11 were waited for; matrix products, arithmetic and copies ran while one was open for 2% of the time, Pallas kernels for 28%

profile of v11, /device:TPU:0, one launch (start us, length us, event | category | flops | bytes accessed | tf_op | source)
XLA Modules:
  0.0 152.9 jit_solution(2424838949847086004)
XLA Ops:
  0.0 2.2 %b_strips.2 = bf16[512,1024]{1,0:T(8,128)(2,1)} custom-call(s32[1]{0:T(128)} %bitcast.9.quarter_ref, bf16[512,4096]{1,0:T(8,128)(2,1)} %w_ref.2), custom_call_target="tpu_custom_call" | custom-call | flops 1000 | bytes 1000 | tf_op jit(solution)/shard_map/b_strips/pallas_call | solution.py:86
  2.2 3.0 %collective-permute-start = (bf16[512,1024]{1,0:T(8,128)(2,1)}, bf16[512,1024]{1,0:T(8,128)(2,1)S(1)}, u32[]{:S(2)}, u32[]{:S(2)}) collective-permute-start(bf16[512,1024]{1,0:T(8,128)(2,1)} %b_strips.2), channel_id=1, source_target_pairs={{0,2},{2,0},{4,6},{6,4},{8,10},{10,8},{12,14},{14,12},{1,3},{3,1},... | collective-permute-start | bytes 3145736 | tf_op jit(solution)/shard_map/ppermute | solution.py:539
  5.2 2.2 %b_strips.3.refs_8_ = bf16[512,1024]{1,0:T(8,128)(2,1)} custom-call(s32[1]{0:T(128)} %bitcast.quarter_ref, bf16[512,4096]{1,0:T(8,128)(2,1)} %w_ref.2), custom_call_target="tpu_custom_call" | custom-call | flops 1000 | bytes 1000 | tf_op jit(solution)/shard_map/b_strips/pallas_call | solution.py:86
  7.4 1.6 %collective-permute-start.3 = (bf16[512,1024]{1,0:T(8,128)(2,1)}, bf16[512,1024]{1,0:T(8,128)(2,1)S(1)}, u32[]{:S(2)}, u32[]{:S(2)}) collective-permute-start(bf16[512,1024]{1,0:T(8,128)(2,1)} %b_strips.3.refs_8_), channel_id=1, source_target_pairs={{0,4},{2,6},{4,0},{6,2},{8,12},{10,14},{12,8},{14,10},{1,5},{3,7},... | collective-permute-start | bytes 3145736 | tf_op jit(solution)/shard_map/ppermute | solution.py:539
  10.8 2.1 %masked_rows.5.refs_1_ = bf16[128,4096]{1,0:T(8,128)(2,1)} custom-call(s32[1]{0:T(128)} %bitcast.11.first_ref, f32[8,1,4096]{2,1,0:T(1,128)} %reshape.27.mask_ref, bf16[512,4096]{1,0:T(8,128)(2,1)} %x_ref.7), custom_call_target="tpu_custom_call" | custom-call | flops 1000 | bytes 1000 | tf_op jit(solution)/shard_map/masked_rows/pallas_call | solution.py:148
  12.9 2.1 %masked_rows.4.refs_0_ = bf16[128,4096]{1,0:T(8,128)(2,1)} custom-call(s32[1]{0:T(128)} %bitcast.10.first_ref, f32[8,1,4096]{2,1,0:T(1,128)} %reshape.27.mask_ref, bf16[512,4096]{1,0:T(8,128)(2,1)} %x_ref.7), custom_call_target="tpu_custom_call" | custom-call | flops 1000 | bytes 1000 | tf_op jit(solution)/shard_map/masked_rows/pallas_call | solution.py:148
  15.1 13.5 %collective-permute-done.refs_9_ = bf16[512,1024]{1,0:T(8,128)(2,1)S(1)} collective-permute-done((bf16[512,1024]{1,0:T(8,128)(2,1)}, bf16[512,1024]{1,0:T(8,128)(2,1)S(1)}, u32[]{:S(2)}, u32[]{:S(2)}) %collective-permute-start) | collective-permute-done | bytes 1048608 | tf_op jit(solution)/shard_map/ppermute | solution.py:539
  29.6 2.8 %collective-permute-done.3.refs_2_.refs_0_.refs_12_ = bf16[512,1024]{1,0:T(8,128)(2,1)S(1)} collective-permute-done((bf16[512,1024]{1,0:T(8,128)(2,1)}, bf16[512,1024]{1,0:T(8,128)(2,1)S(1)}, u32[]{:S(2)}, u32[]{:S(2)}) %collective-permute-start.3) | collective-permute-done | bytes 1048608 | tf_op jit(solution)/shard_map/ppermute | solution.py:539
  32.3 1.6 %collective-permute-start.5 = (bf16[512,1024]{1,0:T(8,128)(2,1)}, bf16[512,1024]{1,0:T(8,128)(2,1)S(1)}, u32[]{:S(2)}, u32[]{:S(2)}) collective-permute-start(bf16[512,1024]{1,0:T(8,128)(2,1)} %copy-done.7), channel_id=1, source_target_pairs={{0,4},{2,6},{4,0},{6,2},{8,12},{10,14},{12,8},{14,10},{1,5},{3,7},... | collective-permute-start | bytes 3145736 | tf_op jit(solution)/shard_map/ppermute | solution.py:539
  33.9 1.6 %collective-permute-start.4 = (bf16[512,1024]{1,0:T(8,128)(2,1)}, bf16[512,1024]{1,0:T(8,128)(2,1)}, u32[]{:S(2)}, u32[]{:S(2)}) collective-permute-start(bf16[512,1024]{1,0:T(8,128)(2,1)} %copy-done.7), channel_id=1, source_target_pairs={{4,8},{6,10},{8,4},{10,6},{5,9},{7,11},{9,5},{11,7},{20,24},{22,26... | collective-permute-start | bytes 3145736 | tf_op jit(solution)/shard_map/ppermute | solution.py:539
  35.5 1.3 collective-permute-start.2
  37.5 1.5 collective-permute-start.8
  39.0 19.6 %collective-permute-done.5.refs_3_.refs_1_.refs_13_ = bf16[512,1024]{1,0:T(8,128)(2,1)S(1)} collective-permute-done((bf16[512,1024]{1,0:T(8,128)(2,1)}, bf16[512,1024]{1,0:T(8,128)(2,1)S(1)}, u32[]{:S(2)}, u32[]{:S(2)}) %collective-permute-start.5) | collective-permute-done | bytes 1048608 | tf_op jit(solution)/shard_map/ppermute | solution.py:539
  58.6 3.2 %packed.3 = (bf16[512,1280]{1,0:T(8,128)(2,1)}, bf16[512,1024]{1,0:T(8,128)(2,1)}) custom-call(s32[2]{0:T(128)S(1)} %pad_add_fusion.1.meta_ref, bf16[512,1024]{1,0:T(8,128)(2,1)S(1)} %collective-permute-done.1.refs_0_.refs_10_, bf16[512,1024]{1,0:T(8,128)(2,1)} %collective-permute-done.4.refs_1_.refs_11_, ...), custom_call_target="tpu_custom_call" | custom-call | flops 1000 | bytes 1000 | tf_op jit(solution)/shard_map/packed/pallas_call | solution.py:129
  61.8 2.9 %collective-permute-done.2.refs_15_ = bf16[512,384]{1,0:T(8,128)(2,1)} collective-permute-done((bf16[512,384]{1,0:T(8,128)(2,1)S(1)}, bf16[512,384]{1,0:T(8,128)(2,1)}, u32[]{:S(2)}, u32[]{:S(2)}) %collective-permute-start.2) | collective-permute-done | bytes 393248 | tf_op jit(solution)/shard_map/ppermute | solution.py:539
  64.8 1.6 %collective-permute-start.6 = (bf16[512,1024]{1,0:T(8,128)(2,1)}, bf16[512,1024]{1,0:T(8,128)(2,1)}, u32[]{:S(2)}, u32[]{:S(2)}) collective-permute-start(bf16[512,1024]{1,0:T(8,128)(2,1)} %get-tuple-element.41), channel_id=1, source_target_pairs={{4,8},{6,10},{8,4},{10,6},{5,9},{7,11},{9,5},{11,7},{20,24},{22,26... | collective-permute-start | bytes 3145736 | tf_op jit(solution)/shard_map/ppermute | solution.py:539
  66.4 1.3 collective-permute-start.11
  67.9 15.3 %collective-permute-done.8.refs_5_ = bf16[128,4096]{1,0:T(8,128)(2,1)} collective-permute-done((bf16[128,4096]{1,0:T(8,128)(2,1)}, bf16[128,4096]{1,0:T(8,128)(2,1)}, u32[]{:S(2)}, u32[]{:S(2)}) %collective-permute-start.8) | collective-permute-done | bytes 1048608 | tf_op jit(solution)/shard_map/ppermute | solution.py:539
  84.4 1.3 collective-permute-start.12
  85.7 2.1 %masked_rows.7.refs_3_ = bf16[128,4096]{1,0:T(8,128)(2,1)} custom-call(s32[1]{0:T(128)} %bitcast.13.first_ref, f32[8,1,4096]{2,1,0:T(1,128)} %reshape.27.mask_ref, bf16[512,4096]{1,0:T(8,128)(2,1)} %x_ref.7), custom_call_target="tpu_custom_call" | custom-call | flops 1000 | bytes 1000 | tf_op jit(solution)/shard_map/masked_rows/pallas_call | solution.py:148
  87.9 2.2 %masked_rows.6.refs_2_ = bf16[128,4096]{1,0:T(8,128)(2,1)} custom-call(s32[1]{0:T(128)} %bitcast.12.first_ref, f32[8,1,4096]{2,1,0:T(1,128)} %reshape.27.mask_ref, bf16[512,4096]{1,0:T(8,128)(2,1)} %x_ref.7), custom_call_target="tpu_custom_call" | custom-call | flops 1000 | bytes 1000 | tf_op jit(solution)/shard_map/masked_rows/pallas_call | solution.py:148
  90.6 6.8 %collective-permute-done.11.refs_14_ = bf16[512,1280]{1,0:T(8,128)(2,1)} collective-permute-done((bf16[512,1280]{1,0:T(8,128)(2,1)}, bf16[512,1280]{1,0:T(8,128)(2,1)}, u32[]{:S(2)}, u32[]{:S(2)}) %collective-permute-start.11) | collective-permute-done | bytes 1310752 | tf_op jit(solution)/shard_map/ppermute | solution.py:539
  98.5 14.8 %whole_products.1.refs_8_ = f32[2,512,1024]{2,1,0:T(8,128)} custom-call(s32[14]{0:T(128)} %stack.139.meta_ref, bf16[128,4096]{1,0:T(8,128)(2,1)} %masked_rows.4.refs_0_, bf16[128,4096]{1,0:T(8,128)(2,1)} %masked_rows.5.refs_1_, bf16[128,4096]{1,0:T(8,128)(2,1)} %masked_rows.6.refs_2_, bf16[128,4096]{1,0:T(8,128)(2,1)} %masked_rows.7.refs_3_, ...), custom_call_target="tpu_custom_call" | custom-call | flops 1000 | bytes 1000 | tf_op jit(solution)/shard_map/whole_products/pallas_call | solution.py:255
  114.0 1.3 collective-permute-start.14
  116.1 3.4 %collective-permute-done.12.refs_10_ = bf16[512,1024]{1,0:T(8,128)(2,1)} collective-permute-done((bf16[512,1024]{1,0:T(8,128)(2,1)}, bf16[512,1024]{1,0:T(8,128)(2,1)}, u32[]{:S(2)}, u32[]{:S(2)}) %collective-permute-start.12) | collective-permute-done | bytes 1048608 | tf_op jit(solution)/shard_map/ppermute | solution.py:539
  119.5 6.2 %half_products.1 = (bf16[256,640]{1,0:T(8,128)(2,1)}, bf16[256,640]{1,0:T(8,128)(2,1)}, bf16[256,640]{1,0:T(8,128)(2,1)}, bf16[256,640]{1,0:T(8,128)(2,1)}, f32[2,512,384]{2,1,0:T(8,128)}) custom-call(s32[9]{0:T(128)} %stack.129.meta_ref, bf16[128,4096]{1,0:T(8,128)(2,1)} %masked_rows.4.refs_0_, bf16[128,4096]{1,0:T(8,128)(2,1)} %masked_rows.5.refs_1_, ...), custom_call_target="tpu_custom_call" | custom-call | flops 1000 | bytes 1000 | tf_op jit(solution)/shard_map/half_products/pallas_call | solution.py:371
  128.2 5.7 %collective-permute-done.14.refs_9_ = bf16[512,640]{1,0:T(8,128)(2,1)S(1)} collective-permute-done((bf16[512,640]{1,0:T(8,128)(2,1)S(1)}, bf16[512,640]{1,0:T(8,128)(2,1)S(1)}, u32[]{:S(2)}, u32[]{:S(2)}) %collective-permute-start.14) | collective-permute-done | bytes 655392 | tf_op jit(solution)/shard_map/ppermute | solution.py:539
  134.7 5.1 %rest_products.1 = (bf16[256,384]{1,0:T(8,128)(2,1)}, bf16[256,384]{1,0:T(8,128)(2,1)}, bf16[256,384]{1,0:T(8,128)(2,1)}, bf16[256,384]{1,0:T(8,128)(2,1)}) custom-call(s32[9]{0:T(128)} %stack.123.meta_ref, bf16[128,4096]{1,0:T(8,128)(2,1)} %masked_rows.4.refs_0_, bf16[128,4096]{1,0:T(8,128)(2,1)} %masked_rows.5.refs_1_, ...), custom_call_target="tpu_custom_call" | custom-call | flops 1000 | bytes 1000 | tf_op jit(solution)/shard_map/rest_products/pallas_call | solution.py:451
  142.6 2.0 %assembled.2.refs_4_ = bf16[256,4096]{1,0:T(8,128)(2,1)} custom-call(s32[2]{0:T(128)S(1)} %get-tuple-element.62.place_ref, f32[4,1,4096]{2,1,0:T(1,128)S(1)} %reshape.24.mask_ref, bf16[256,640]{1,0:T(8,128)(2,1)S(1)} %copy-done.4, bf16[256,640]{1,0:T(8,128)(2,1)S(1)} %collective-permute-done.15.refs_1_, ...), custom_call_target="tpu_custom_call" | custom-call | flops 1000 | bytes 1000 | tf_op jit(solution)/shard_map/assembled/pallas_call | solution.py:498
  144.6 3.3 %collective-permute-done.17.refs_2_ = bf16[256,384]{1,0:T(8,128)(2,1)S(1)} collective-permute-done((bf16[256,384]{1,0:T(8,128)(2,1)}, bf16[256,384]{1,0:T(8,128)(2,1)S(1)}, u32[]{:S(2)}, u32[]{:S(2)}) %collective-permute-start.17) | collective-permute-done | bytes 196640 | tf_op jit(solution)/shard_map/ppermute | solution.py:539
  147.9 3.3 %collective-permute-done.18.refs_3_ = bf16[256,384]{1,0:T(8,128)(2,1)S(1)} collective-permute-done((bf16[256,384]{1,0:T(8,128)(2,1)}, bf16[256,384]{1,0:T(8,128)(2,1)S(1)}, u32[]{:S(2)}, u32[]{:S(2)}) %collective-permute-start.18) | collective-permute-done | bytes 196640 | tf_op jit(solution)/shard_map/ppermute | solution.py:619
  151.2 1.6 %assembled.3 = bf16[256,4096]{1,0:T(8,128)(2,1)} custom-call(s32[2]{0:T(128)S(1)} %get-tuple-element.61.place_ref, f32[4,1,4096]{2,1,0:T(1,128)S(1)} %reshape.24.mask_ref, bf16[256,384]{1,0:T(8,128)(2,1)S(1)} %copy-done.5, bf16[256,384]{1,0:T(8,128)(2,1)S(1)} %collective-permute-done.16.refs_1_, ...), custom_call_target="tpu_custom_call", output_to_operand_aliasing={{}: (6, {})} | custom-call | flops 1000 | bytes 1000 | tf_op jit(solution)/shard_map/assembled/pallas_call | solution.py:498
  (59 shorter events, 13.9 us)
Async XLA Ops:
  2.2 26.4 %collective-permute-start = (bf16[512,1024]{1,0:T(8,128)(2,1)}, bf16[512,1024]{1,0:T(8,128)(2,1)S(1)}, u32[]{:S(2)}, u32[]{:S(2)}) collective-permute-start(bf16[512,1024]{1,0:T(8,128)(2,1)} %b_strips.2), channel_id=1, source_target_pairs={{0,2},{2,0},{4,6},{6,4},{8,10},{10,8},{12,14},{14,12},{1,3},{3,1},... | collective-permute-start | bytes 3145736 | tf_op jit(solution)/shard_map/ppermute | solution.py:539
  5.2 4.6 %copy-start.9 = (s32[8,64]{1,0:T(8,128)S(1)}, s32[8,64]{1,0:T(8,128)}, u32[]{:S(2)}) copy-start(s32[8,64]{1,0:T(8,128)} %param.6) | copy-start | bytes 6148
  7.4 24.9 %collective-permute-start.3 = (bf16[512,1024]{1,0:T(8,128)(2,1)}, bf16[512,1024]{1,0:T(8,128)(2,1)S(1)}, u32[]{:S(2)}, u32[]{:S(2)}) collective-permute-start(bf16[512,1024]{1,0:T(8,128)(2,1)} %b_strips.3.refs_8_), channel_id=1, source_target_pairs={{0,4},{2,6},{4,0},{6,2},{8,12},{10,14},{12,8},{14,10},{1,5},{3,7},... | collective-permute-start | bytes 3145736 | tf_op jit(solution)/shard_map/ppermute | solution.py:539
  9.1 26.4 %collective-permute-start.1 = (bf16[512,1024]{1,0:T(8,128)(2,1)}, bf16[512,1024]{1,0:T(8,128)(2,1)S(1)}, u32[]{:S(2)}, u32[]{:S(2)}) collective-permute-start(bf16[512,1024]{1,0:T(8,128)(2,1)} %b_strips.3.refs_8_), channel_id=1, source_target_pairs={{4,8},{6,10},{8,4},{10,6},{5,9},{7,11},{9,5},{11,7},{20,24},{22,26... | collective-permute-start | bytes 3145736 | tf_op jit(solution)/shard_map/ppermute | solution.py:539
  28.6 1.0 copy-start.7
  32.3 35.4 %copy-start = (bf16[512,1024]{1,0:T(8,128)(2,1)}, bf16[512,1024]{1,0:T(8,128)(2,1)S(1)}, u32[]{:S(2)}) copy-start(bf16[512,1024]{1,0:T(8,128)(2,1)S(1)} %collective-permute-done.3.refs_2_.refs_0_.refs_12_) | copy-start | bytes 3145732
  32.3 26.3 %collective-permute-start.5 = (bf16[512,1024]{1,0:T(8,128)(2,1)}, bf16[512,1024]{1,0:T(8,128)(2,1)S(1)}, u32[]{:S(2)}, u32[]{:S(2)}) collective-permute-start(bf16[512,1024]{1,0:T(8,128)(2,1)} %copy-done.7), channel_id=1, source_target_pairs={{0,4},{2,6},{4,0},{6,2},{8,12},{10,14},{12,8},{14,10},{1,5},{3,7},... | collective-permute-start | bytes 3145736 | tf_op jit(solution)/shard_map/ppermute | solution.py:539
  33.9 24.7 %collective-permute-start.4 = (bf16[512,1024]{1,0:T(8,128)(2,1)}, bf16[512,1024]{1,0:T(8,128)(2,1)}, u32[]{:S(2)}, u32[]{:S(2)}) collective-permute-start(bf16[512,1024]{1,0:T(8,128)(2,1)} %copy-done.7), channel_id=1, source_target_pairs={{4,8},{6,10},{8,4},{10,6},{5,9},{7,11},{9,5},{11,7},{20,24},{22,26... | collective-permute-start | bytes 3145736 | tf_op jit(solution)/shard_map/ppermute | solution.py:539
  35.5 26.3 %copy-start.2 = (bf16[512,1024]{1,0:T(8,128)(2,1)}, bf16[512,1024]{1,0:T(8,128)(2,1)S(1)}, u32[]{:S(2)}) copy-start(bf16[512,1024]{1,0:T(8,128)(2,1)S(1)} %collective-permute-done.1.refs_0_.refs_10_) | copy-start | bytes 3145732
  35.5 29.2 %collective-permute-start.2 = (bf16[512,384]{1,0:T(8,128)(2,1)S(1)}, bf16[512,384]{1,0:T(8,128)(2,1)}, u32[]{:S(2)}, u32[]{:S(2)}) collective-permute-start(bf16[512,384]{1,0:T(8,128)(2,1)S(1)} %slice.4), channel_id=1, source_target_pairs={{4,0},{6,2},{8,12},{10,14},{5,1},{7,3},{9,13},{11,15},{20,16},{22,... | collective-permute-start | bytes 1179656 | tf_op jit(solution)/shard_map/ppermute | solution.py:539
  36.9 31.0 %collective-permute-start.7 = (bf16[128,4096]{1,0:T(8,128)(2,1)}, bf16[128,4096]{1,0:T(8,128)(2,1)}, u32[]{:S(2)}, u32[]{:S(2)}) collective-permute-start(bf16[128,4096]{1,0:T(8,128)(2,1)} %masked_rows.4.refs_0_), channel_id=1, source_target_pairs={{0,2},{2,0},{4,6},{6,4},{8,10},{10,8},{12,14},{14,12},{1,3},{3,1},... | collective-permute-start | bytes 3145736 | tf_op jit(solution)/shard_map/ppermute | solution.py:539
  37.5 45.7 %collective-permute-start.8 = (bf16[128,4096]{1,0:T(8,128)(2,1)}, bf16[128,4096]{1,0:T(8,128)(2,1)}, u32[]{:S(2)}, u32[]{:S(2)}) collective-permute-start(bf16[128,4096]{1,0:T(8,128)(2,1)} %masked_rows.5.refs_1_), channel_id=1, source_target_pairs={{0,2},{2,0},{4,6},{6,4},{8,10},{10,8},{12,14},{14,12},{1,3},{3,1},... | collective-permute-start | bytes 3145736 | tf_op jit(solution)/shard_map/ppermute | solution.py:539
  58.6 9.1 %copy-start.1 = (bf16[512,1024]{1,0:T(8,128)(2,1)}, bf16[512,1024]{1,0:T(8,128)(2,1)S(1)}, u32[]{:S(2)}) copy-start(bf16[512,1024]{1,0:T(8,128)(2,1)S(1)} %collective-permute-done.5.refs_3_.refs_1_.refs_13_) | copy-start | bytes 3145732
  64.8 18.4 %collective-permute-start.6 = (bf16[512,1024]{1,0:T(8,128)(2,1)}, bf16[512,1024]{1,0:T(8,128)(2,1)}, u32[]{:S(2)}, u32[]{:S(2)}) collective-permute-start(bf16[512,1024]{1,0:T(8,128)(2,1)} %get-tuple-element.41), channel_id=1, source_target_pairs={{4,8},{6,10},{8,4},{10,6},{5,9},{7,11},{9,5},{11,7},{20,24},{22,26... | collective-permute-start | bytes 3145736 | tf_op jit(solution)/shard_map/ppermute | solution.py:539
  66.4 31.1 %collective-permute-start.11 = (bf16[512,1280]{1,0:T(8,128)(2,1)}, bf16[512,1280]{1,0:T(8,128)(2,1)}, u32[]{:S(2)}, u32[]{:S(2)}) collective-permute-start(bf16[512,1280]{1,0:T(8,128)(2,1)} %get-tuple-element.44), channel_id=1, source_target_pairs={{4,0},{6,2},{8,12},{10,14},{5,1},{7,3},{9,13},{11,15},{20,16},{22,... | collective-permute-start | bytes 3932168 | tf_op jit(solution)/shard_map/ppermute | solution.py:539
  83.2 14.3 %collective-permute-start.10 = (bf16[128,4096]{1,0:T(8,128)(2,1)}, bf16[128,4096]{1,0:T(8,128)(2,1)S(1)}, u32[]{:S(2)}, u32[]{:S(2)}) collective-permute-start(bf16[128,4096]{1,0:T(8,128)(2,1)} %collective-permute-done.8.refs_5_), channel_id=1, source_target_pairs={{0,1},{1,0},{2,3},{3,2},{4,5},{5,4},{6,7},{7,6},{8,9},{9,8},{10,11... | collective-permute-start | bytes 3145736 | tf_op jit(solution)/shard_map/ppermute | solution.py:582
  83.2 14.3 %collective-permute-start.9 = (bf16[128,4096]{1,0:T(8,128)(2,1)}, bf16[128,4096]{1,0:T(8,128)(2,1)}, u32[]{:S(2)}, u32[]{:S(2)}) collective-permute-start(bf16[128,4096]{1,0:T(8,128)(2,1)} %collective-permute-done.7.refs_4_), channel_id=1, source_target_pairs={{0,1},{1,0},{2,3},{3,2},{4,5},{5,4},{6,7},{7,6},{8,9},{9,8},{10,11... | collective-permute-start | bytes 3145736 | tf_op jit(solution)/shard_map/ppermute | solution.py:582
  83.7 29.6 %collective-permute-start.13 = (bf16[512,1024]{1,0:T(8,128)(2,1)S(1)}, bf16[512,1024]{1,0:T(8,128)(2,1)S(1)}, u32[]{:S(2)}, u32[]{:S(2)}) collective-permute-start(bf16[512,1024]{1,0:T(8,128)(2,1)S(1)} %packed.4), channel_id=1, source_target_pairs={{4,8},{6,10},{8,4},{10,6},{5,9},{7,11},{9,5},{11,7},{20,24},{22,26... | collective-permute-start | bytes 3145736 | tf_op jit(solution)/shard_map/ppermute | solution.py:539
  84.4 35.1 %collective-permute-start.12 = (bf16[512,1024]{1,0:T(8,128)(2,1)}, bf16[512,1024]{1,0:T(8,128)(2,1)}, u32[]{:S(2)}, u32[]{:S(2)}) collective-permute-start(bf16[512,1024]{1,0:T(8,128)(2,1)} %collective-permute-done.6.refs_9_), channel_id=1, source_target_pairs={{4,0},{6,2},{8,12},{10,14},{5,1},{7,3},{9,13},{11,15},{20,16},{22,... | collective-permute-start | bytes 3145736 | tf_op jit(solution)/shard_map/ppermute | solution.py:539
  97.5 1.0 copy-start.6
  113.3 6.2 %copy-start.3 = (bf16[512,1024]{1,0:T(8,128)(2,1)}, bf16[512,1024]{1,0:T(8,128)(2,1)S(1)}, u32[]{:S(2)}) copy-start(bf16[512,1024]{1,0:T(8,128)(2,1)S(1)} %collective-permute-done.13.refs_11_.refs_0_) | copy-start | bytes 3145732
  114.0 19.9 %collective-permute-start.14 = (bf16[512,640]{1,0:T(8,128)(2,1)S(1)}, bf16[512,640]{1,0:T(8,128)(2,1)S(1)}, u32[]{:S(2)}, u32[]{:S(2)}) collective-permute-start(bf16[512,640]{1,0:T(8,128)(2,1)S(1)} %packed.5), channel_id=1, source_target_pairs={{4,0},{6,2},{8,12},{10,14},{5,1},{7,3},{9,13},{11,15},{20,16},{22,... | collective-permute-start | bytes 1966088 | tf_op jit(solution)/shard_map/ppermute | solution.py:539
  125.7 2.6 %collective-permute-start.15 = (bf16[256,640]{1,0:T(8,128)(2,1)}, bf16[256,640]{1,0:T(8,128)(2,1)S(1)}, u32[]{:S(2)}, u32[]{:S(2)}) collective-permute-start(bf16[256,640]{1,0:T(8,128)(2,1)} %get-tuple-element.51), channel_id=1, source_target_pairs={{0,1},{1,0},{2,3},{3,2},{4,5},{5,4},{6,7},{7,6},{8,9},{9,8},{10,11... | collective-permute-start | bytes 983048 | tf_op jit(solution)/shard_map/ppermute | solution.py:617
  125.7 16.4 %collective-permute-start.19 = (bf16[256,640]{1,0:T(8,128)(2,1)}, bf16[256,640]{1,0:T(8,128)(2,1)S(1)}, u32[]{:S(2)}, u32[]{:S(2)}) collective-permute-start(bf16[256,640]{1,0:T(8,128)(2,1)} %get-tuple-element.59), channel_id=1, source_target_pairs={{0,2},{2,0},{4,6},{6,4},{8,10},{10,8},{12,14},{14,12},{1,3},{3,1},... | collective-permute-start | bytes 983048 | tf_op jit(solution)/shard_map/ppermute | solution.py:539
  126.8 15.9 %collective-permute-start.20 = (bf16[256,640]{1,0:T(8,128)(2,1)}, bf16[256,640]{1,0:T(8,128)(2,1)S(1)}, u32[]{:S(2)}, u32[]{:S(2)}) collective-permute-start(bf16[256,640]{1,0:T(8,128)(2,1)} %get-tuple-element.60), channel_id=1, source_target_pairs={{0,3},{1,2},{2,1},{3,0},{4,7},{5,6},{6,5},{7,4},{8,11},{9,10},{10,... | collective-permute-start | bytes 983048 | tf_op jit(solution)/shard_map/ppermute | solution.py:619
  133.9 0.8 copy-start.8
  134.7 7.1 %copy-start.10 = (s32[4,64]{1,0:T(4,128)S(1)}, s32[4,64]{1,0:T(4,128)}, u32[]{:S(2)}) copy-start(s32[4,64]{1,0:T(4,128)} %param.7) | copy-start | bytes 3076
  134.7 7.9 %copy-start.4 = (bf16[256,640]{1,0:T(8,128)(2,1)S(1)}, bf16[256,640]{1,0:T(8,128)(2,1)}, u32[]{:S(2)}) copy-start(bf16[256,640]{1,0:T(8,128)(2,1)} %get-tuple-element.57.refs_0_) | copy-start | bytes 983044
  139.8 11.4 %copy-start.5 = (bf16[256,384]{1,0:T(8,128)(2,1)S(1)}, bf16[256,384]{1,0:T(8,128)(2,1)}, u32[]{:S(2)}) copy-start(bf16[256,384]{1,0:T(8,128)(2,1)} %get-tuple-element.53.refs_0_) | copy-start | bytes 589828
  139.9 4.8 %collective-permute-start.16 = (bf16[256,384]{1,0:T(8,128)(2,1)}, bf16[256,384]{1,0:T(8,128)(2,1)S(1)}, u32[]{:S(2)}, u32[]{:S(2)}) collective-permute-start(bf16[256,384]{1,0:T(8,128)(2,1)} %get-tuple-element.54), channel_id=1, source_target_pairs={{0,1},{1,0},{2,3},{3,2},{4,5},{5,4},{6,7},{7,6},{8,9},{9,8},{10,11... | collective-permute-start | bytes 589832 | tf_op jit(solution)/shard_map/ppermute | solution.py:617
  139.9 8.0 %collective-permute-start.17 = (bf16[256,384]{1,0:T(8,128)(2,1)}, bf16[256,384]{1,0:T(8,128)(2,1)S(1)}, u32[]{:S(2)}, u32[]{:S(2)}) collective-permute-start(bf16[256,384]{1,0:T(8,128)(2,1)} %get-tuple-element.55), channel_id=1, source_target_pairs={{0,2},{2,0},{4,6},{6,4},{8,10},{10,8},{12,14},{14,12},{1,3},{3,1},... | collective-permute-start | bytes 589832 | tf_op jit(solution)/shard_map/ppermute | solution.py:539
  140.5 10.7 %collective-permute-start.18 = (bf16[256,384]{1,0:T(8,128)(2,1)}, bf16[256,384]{1,0:T(8,128)(2,1)S(1)}, u32[]{:S(2)}, u32[]{:S(2)}) collective-permute-start(bf16[256,384]{1,0:T(8,128)(2,1)} %get-tuple-element.56), channel_id=1, source_target_pairs={{0,3},{1,2},{2,1},{3,0},{4,7},{5,6},{6,5},{7,4},{8,11},{9,10},{10,... | collective-permute-start | bytes 589832 | tf_op jit(solution)/shard_map/ppermute | solution.py:619

commit v12 on v11

--- a/solution.py
+++ b/solution.py
@@ -225,23 +225,48 @@
         on_each(p, lambda copy: copy.start())
         for r in range(PARTS):
             copies[p, r].start()
-    acc[...] = jnp.zeros_like(acc)
-    for p in range(n_b):
+    outs = [
+        pltpu.make_async_copy(acc.at[g, :, low : low + quarter], out_ref.at[g], out_sems.at[g]) for g in range(2)
+    ]
+
+    def wait_for(p):
         for k in [p] if p < n_b - 2 else range(n_b - 2, n_b) if p == n_b - 2 else []:
             on_each(k, lambda copy: copy.wait())
         for r in range(PARTS):
             copies[p, r].wait()
 
-        def step(g, carry):
-            add_product(acc, xv[p, g], bv[p], g, offset_of(p, g))
-            return carry
-
-        lax.fori_loop(0, 2, step, 0)
-    outs = [
-        pltpu.make_async_copy(acc.at[g, :, low : low + quarter], out_ref.at[g], out_sems.at[g]) for g in range(2)
-    ]
-    for out in outs:
-        out.start()
+    middle = quarter // LANES // 2
+
+    def own(g, carry):
+        acc[g, :, low : low + quarter] = jnp.dot(xv[g, g], bv[g], preferred_element_type=jnp.float32)
+        return carry
+
+    def step(i, carry):
+        p = jnp.where(i < 4, i % 2, i // 2)
+        g = jnp.where(i < 4, 1 - i % 2, i % 2)
+        for k in range(2, n_b):
+            pl.when(i == 2 * k)(functools.partial(wait_for, k))
+        pl.when(i == 2 * n_b - 1)(outs[0].start)
+        offset = offset_of(p, g)
+        for k in range(2 * middle):
+            if k == middle:
+                continue
+            first, last = max(0, middle - k), min(2 * middle, 3 * middle - k)
+
+            @pl.when(offset == k)
+            def _():
+                strips = bv[p, :, first * LANES : last * LANES]
+                acc[g, :, (k + first) * LANES : (k + last) * LANES] += jnp.dot(
+                    xv[p, g], strips, preferred_element_type=jnp.float32
+                )
+
+        return carry
+
+    for p in range(2):
+        wait_for(p)
+    lax.fori_loop(0, 2, own, 0)
+    lax.fori_loop(2, 2 * n_b, step, 0)
+    outs[1].start()
     for out in outs:
         out.wait()
 
@@ -266,7 +291,7 @@
             pltpu.SemaphoreType.DMA((2,)),
         ],
         compiler_params=pltpu.CompilerParams(vmem_limit_bytes=59 * MIB),
-        cost_estimate=SMALL,
+        cost_estimate=pl.CostEstimate(flops=6 * 10**9, bytes_accessed=36 * MIB, transcendentals=0),
         name="whole_products",
     )(meta, *xs, *operands)
 
@@ -576,7 +601,7 @@
     mid_a, mid_b, fwd_first = together(mid_a, mid_b, fwd_first)
     mid_b = line(mid_b, outward)
     fwd_first = line(fwd_first, cross)
-    fwd_first, fwd_second, *x_across = together(fwd_first, fwd_second, *x_across)
+    fwd_second, *x_across = together(fwd_second, *x_across)
     far_first = line(fwd_first, outward)
     fwd_second = line(fwd_second, cross)
     x_opposite = [lax.ppermute(part, "depth", layers) for part in x_across]

time: 155 us -> 158 us (1.019)
  the two profiles are of different devices: /device:TPU:0 before, /device:TPU:17 now
where the time goes in v12:
time: 158 us; the launch traced here: 157 us
  waiting for transfers between devices  62.9 us (40%)
  Pallas kernels  47.2 us (30%)
  starting transfers between devices  40.6 us (26%)
  local copies, waits for them, and re-layouts  5.95 us (4%)
    ppermute x15, waiting for transfers between devices, line(): return lax.ppermute(value, 'grid', pairs)  50.9 us
    ppermute x15, starting transfers between devices, line(): return lax.ppermute(value, 'grid', pairs)  26.4 us
    pallas_call x1, Pallas kernels, whole_products(): pl.pallas_call(functools.partial(whole_kernel, plan), out_shape=jax.Shape...  14.4 us
    ppermute x2, waiting for transfers between devices, exchanged(): lax.ppermute(pieces[3], ('grid', 'depth'), opposite)  12 us
    pallas_call x4, Pallas kernels, masked_rows(): pl.pallas_call(mask_kernel, grid_spec=pltpu.PrefetchScalarGridSpec(num_sc...  8.57 us
    pallas_call x1, Pallas kernels, half_products(): pl.pallas_call(half_kernel, out_shape=[jax.ShapeDtypeStruct((rows, n_done...  8.01 us
    ppermute x2, starting transfers between devices, exchanged(): lax.ppermute(pieces[1], 'depth', layers)  7.87 us
    pallas_call x3, Pallas kernels, packed(): pl.pallas_call(functools.partial(pack_kernel, plan, len(sources)), out_sh...  5.03 us
  transfers between devices with their start and end apart: 21, of which 11 were waited for; matrix products, arithmetic and copies ran while one was open for 2% of the time, Pallas kernels for 28%

profile of v12, /device:TPU:17, one launch (start us, length us, event | category | flops | bytes accessed | tf_op | source)
XLA Modules:
  0.0 157.2 jit_solution(1962108354197388525)
XLA Ops:
  0.0 2.2 %b_strips.2 = bf16[512,1024]{1,0:T(8,128)(2,1)} custom-call(s32[1]{0:T(128)} %bitcast.9.quarter_ref, bf16[512,4096]{1,0:T(8,128)(2,1)} %w_ref.2), custom_call_target="tpu_custom_call" | custom-call | flops 1000 | bytes 1000 | tf_op jit(solution)/shard_map/b_strips/pallas_call | solution.py:86
  3.5 2.2 %b_strips.3.refs_8_ = bf16[512,1024]{1,0:T(8,128)(2,1)} custom-call(s32[1]{0:T(128)} %bitcast.quarter_ref, bf16[512,4096]{1,0:T(8,128)(2,1)} %w_ref.2), custom_call_target="tpu_custom_call" | custom-call | flops 1000 | bytes 1000 | tf_op jit(solution)/shard_map/b_strips/pallas_call | solution.py:86
  7.1 1.9 %collective-permute-start.7 = (bf16[512,1024]{1,0:T(8,128)(2,1)}, bf16[512,1024]{1,0:T(8,128)(2,1)S(1)}, u32[]{:S(2)}, u32[]{:S(2)}) collective-permute-start(bf16[512,1024]{1,0:T(8,128)(2,1)} %b_strips.3.refs_8_), channel_id=1, source_target_pairs={{4,8},{6,10},{8,4},{10,6},{5,9},{7,11},{9,5},{11,7},{20,24},{22,26... | collective-permute-start | bytes 3145736 | tf_op jit(solution)/shard_map/ppermute | solution.py:564
  10.0 2.1 %masked_rows.5.refs_1_ = bf16[128,4096]{1,0:T(8,128)(2,1)} custom-call(s32[1]{0:T(128)} %bitcast.11.first_ref, f32[8,1,4096]{2,1,0:T(1,128)} %reshape.27.mask_ref, bf16[512,4096]{1,0:T(8,128)(2,1)} %x_ref.7), custom_call_target="tpu_custom_call" | custom-call | flops 1000 | bytes 1000 | tf_op jit(solution)/shard_map/masked_rows/pallas_call | solution.py:148
  12.1 2.1 %masked_rows.4.refs_0_ = bf16[128,4096]{1,0:T(8,128)(2,1)} custom-call(s32[1]{0:T(128)} %bitcast.10.first_ref, f32[8,1,4096]{2,1,0:T(1,128)} %reshape.27.mask_ref, bf16[512,4096]{1,0:T(8,128)(2,1)} %x_ref.7), custom_call_target="tpu_custom_call" | custom-call | flops 1000 | bytes 1000 | tf_op jit(solution)/shard_map/masked_rows/pallas_call | solution.py:148
  14.2 12.2 %collective-permute-done.refs_9_ = bf16[512,1024]{1,0:T(8,128)(2,1)S(1)} collective-permute-done((bf16[512,1024]{1,0:T(8,128)(2,1)}, bf16[512,1024]{1,0:T(8,128)(2,1)S(1)}, u32[]{:S(2)}, u32[]{:S(2)}) %collective-permute-start) | collective-permute-done | bytes 1048608 | tf_op jit(solution)/shard_map/ppermute | solution.py:564
  27.5 2.2 %collective-permute-done.1.refs_0_.refs_2_.refs_12_ = bf16[512,1024]{1,0:T(8,128)(2,1)S(1)} collective-permute-done((bf16[512,1024]{1,0:T(8,128)(2,1)}, bf16[512,1024]{1,0:T(8,128)(2,1)S(1)}, u32[]{:S(2)}, u32[]{:S(2)}) %collective-permute-start.1) | collective-permute-done | bytes 1048608 | tf_op jit(solution)/shard_map/ppermute | solution.py:564
  31.0 1.9 %collective-permute-start.8 = (bf16[512,1024]{1,0:T(8,128)(2,1)}, bf16[512,1024]{1,0:T(8,128)(2,1)}, u32[]{:S(2)}, u32[]{:S(2)}) collective-permute-start(bf16[512,1024]{1,0:T(8,128)(2,1)} %copy-done.10), channel_id=1, source_target_pairs={{4,8},{6,10},{8,4},{10,6},{5,9},{7,11},{9,5},{11,7},{20,24},{22,26... | collective-permute-start | bytes 3145736 | tf_op jit(solution)/shard_map/ppermute | solution.py:564
  34.5 2.5 %collective-permute-start.9 = (bf16[512,384]{1,0:T(8,128)(2,1)S(1)}, bf16[512,384]{1,0:T(8,128)(2,1)}, u32[]{:S(2)}, u32[]{:S(2)}) collective-permute-start(bf16[512,384]{1,0:T(8,128)(2,1)S(1)} %slice.4), channel_id=1, source_target_pairs={{4,0},{6,2},{8,12},{10,14},{5,1},{7,3},{9,13},{11,15},{20,16},{22,... | collective-permute-start | bytes 1179656 | tf_op jit(solution)/shard_map/ppermute | solution.py:564
  37.0 15.7 %collective-permute-done.2.refs_1_.refs_3_.refs_13_ = bf16[512,1024]{1,0:T(8,128)(2,1)S(1)} collective-permute-done((bf16[512,1024]{1,0:T(8,128)(2,1)}, bf16[512,1024]{1,0:T(8,128)(2,1)S(1)}, u32[]{:S(2)}, u32[]{:S(2)}) %collective-permute-start.2) | collective-permute-done | bytes 1048608 | tf_op jit(solution)/shard_map/ppermute | solution.py:564
  52.8 2.9 %collective-permute-done.8.refs_1_.refs_11_ = bf16[512,1024]{1,0:T(8,128)(2,1)} collective-permute-done((bf16[512,1024]{1,0:T(8,128)(2,1)}, bf16[512,1024]{1,0:T(8,128)(2,1)}, u32[]{:S(2)}, u32[]{:S(2)}) %collective-permute-start.8) | collective-permute-done | bytes 1048608 | tf_op jit(solution)/shard_map/ppermute | solution.py:564
  55.7 3.2 %packed.4 = (bf16[512,1280]{1,0:T(8,128)(2,1)}, bf16[512,1024]{1,0:T(8,128)(2,1)}) custom-call(s32[2]{0:T(128)S(1)} %pad_add_fusion.1.meta_ref, bf16[512,1024]{1,0:T(8,128)(2,1)S(1)} %collective-permute-done.7.refs_0_.refs_10_, bf16[512,1024]{1,0:T(8,128)(2,1)} %collective-permute-done.8.refs_1_.refs_11_, ...), custom_call_target="tpu_custom_call" | custom-call | flops 1000 | bytes 1000 | tf_op jit(solution)/shard_map/packed/pallas_call | solution.py:129
  60.2 5.3 %collective-permute-start.10 = (bf16[512,1280]{1,0:T(8,128)(2,1)}, bf16[512,1280]{1,0:T(8,128)(2,1)}, u32[]{:S(2)}, u32[]{:S(2)}) collective-permute-start(bf16[512,1280]{1,0:T(8,128)(2,1)} %get-tuple-element.42), channel_id=1, source_target_pairs={{4,0},{6,2},{8,12},{10,14},{5,1},{7,3},{9,13},{11,15},{20,16},{22,... | collective-permute-start | bytes 3932168 | tf_op jit(solution)/shard_map/ppermute | solution.py:564
  65.5 1.9 %collective-permute-start.11 = (bf16[512,1024]{1,0:T(8,128)(2,1)}, bf16[512,1024]{1,0:T(8,128)(2,1)}, u32[]{:S(2)}, u32[]{:S(2)}) collective-permute-start(bf16[512,1024]{1,0:T(8,128)(2,1)} %get-tuple-element.45), channel_id=1, source_target_pairs={{4,8},{6,10},{8,4},{10,6},{5,9},{7,11},{9,5},{11,7},{20,24},{22,26... | collective-permute-start | bytes 3145736 | tf_op jit(solution)/shard_map/ppermute | solution.py:564
  68.7 9.6 %collective-permute-done.4.refs_5_ = bf16[128,4096]{1,0:T(8,128)(2,1)} collective-permute-done((bf16[128,4096]{1,0:T(8,128)(2,1)}, bf16[128,4096]{1,0:T(8,128)(2,1)}, u32[]{:S(2)}, u32[]{:S(2)}) %collective-permute-start.4) | collective-permute-done | bytes 1048608 | tf_op jit(solution)/shard_map/ppermute | solution.py:564
  78.2 3.1 %collective-permute-start.5 = (bf16[128,4096]{1,0:T(8,128)(2,1)}, bf16[128,4096]{1,0:T(8,128)(2,1)S(1)}, u32[]{:S(2)}, u32[]{:S(2)}) collective-permute-start(bf16[128,4096]{1,0:T(8,128)(2,1)} %collective-permute-done.3.refs_4_), channel_id=1, source_target_pairs={{0,1},{1,0},{2,3},{3,2},{4,5},{5,4},{6,7},{7,6},{8,9},{9,8},{10,11... | collective-permute-start | bytes 3145736 | tf_op jit(solution)/shard_map/ppermute | solution.py:607
  81.3 3.3 %collective-permute-start.13 = (bf16[512,1024]{1,0:T(8,128)(2,1)}, bf16[512,1024]{1,0:T(8,128)(2,1)S(1)}, u32[]{:S(2)}, u32[]{:S(2)}) collective-permute-start(bf16[512,1024]{1,0:T(8,128)(2,1)} %packed.3), channel_id=1, source_target_pairs={{4,8},{6,10},{8,4},{10,6},{5,9},{7,11},{9,5},{11,7},{20,24},{22,26... | collective-permute-start | bytes 3145736 | tf_op jit(solution)/shard_map/ppermute | solution.py:564
  84.7 4.6 %collective-permute-done.11.refs_9_ = bf16[512,1024]{1,0:T(8,128)(2,1)} collective-permute-done((bf16[512,1024]{1,0:T(8,128)(2,1)}, bf16[512,1024]{1,0:T(8,128)(2,1)}, u32[]{:S(2)}, u32[]{:S(2)}) %collective-permute-start.11) | collective-permute-done | bytes 1048608 | tf_op jit(solution)/shard_map/ppermute | solution.py:564
  89.3 2.3 %collective-permute-start.12 = (bf16[512,1024]{1,0:T(8,128)(2,1)}, bf16[512,1024]{1,0:T(8,128)(2,1)}, u32[]{:S(2)}, u32[]{:S(2)}) collective-permute-start(bf16[512,1024]{1,0:T(8,128)(2,1)} %collective-permute-done.11.refs_9_), channel_id=1, source_target_pairs={{4,0},{6,2},{8,12},{10,14},{5,1},{7,3},{9,13},{11,15},{20,16},{22,... | collective-permute-start | bytes 3145736 | tf_op jit(solution)/shard_map/ppermute | solution.py:564
  91.6 2.1 %masked_rows.7.refs_3_ = bf16[128,4096]{1,0:T(8,128)(2,1)} custom-call(s32[1]{0:T(128)} %bitcast.13.first_ref, f32[8,1,4096]{2,1,0:T(1,128)} %reshape.27.mask_ref, bf16[512,4096]{1,0:T(8,128)(2,1)} %x_ref.7), custom_call_target="tpu_custom_call" | custom-call | flops 1000 | bytes 1000 | tf_op jit(solution)/shard_map/masked_rows/pallas_call | solution.py:148
  93.7 2.2 %masked_rows.6.refs_2_ = bf16[128,4096]{1,0:T(8,128)(2,1)} custom-call(s32[1]{0:T(128)} %bitcast.12.first_ref, f32[8,1,4096]{2,1,0:T(1,128)} %reshape.27.mask_ref, bf16[512,4096]{1,0:T(8,128)(2,1)} %x_ref.7), custom_call_target="tpu_custom_call" | custom-call | flops 1000 | bytes 1000 | tf_op jit(solution)/shard_map/masked_rows/pallas_call | solution.py:148
  97.5 14.4 %whole_products.1.refs_8_ = f32[2,512,1024]{2,1,0:T(8,128)} custom-call(s32[14]{0:T(128)} %stack.137.meta_ref, bf16[128,4096]{1,0:T(8,128)(2,1)} %masked_rows.4.refs_0_, bf16[128,4096]{1,0:T(8,128)(2,1)} %masked_rows.5.refs_1_, bf16[128,4096]{1,0:T(8,128)(2,1)} %masked_rows.6.refs_2_, bf16[128,4096]{1,0:T(8,128)(2,1)} %masked_rows.7.refs_3_, ...), custom_call_target="tpu_custom_call" | custom-call | flops 6000000000 | bytes 37748736 | tf_op jit(solution)/shard_map/whole_products/pallas_call | solution.py:280
  114.8 8.0 %half_products.1 = (bf16[256,640]{1,0:T(8,128)(2,1)}, bf16[256,640]{1,0:T(8,128)(2,1)}, bf16[256,640]{1,0:T(8,128)(2,1)}, bf16[256,640]{1,0:T(8,128)(2,1)}, f32[2,512,384]{2,1,0:T(8,128)}) custom-call(s32[9]{0:T(128)} %stack.127.meta_ref, bf16[128,4096]{1,0:T(8,128)(2,1)} %masked_rows.4.refs_0_, bf16[128,4096]{1,0:T(8,128)(2,1)} %masked_rows.5.refs_1_, ...), custom_call_target="tpu_custom_call" | custom-call | flops 1000 | bytes 1000 | tf_op jit(solution)/shard_map/half_products/pallas_call | solution.py:396
  122.8 7.6 %collective-permute-start.15 = (bf16[256,640]{1,0:T(8,128)(2,1)}, bf16[256,640]{1,0:T(8,128)(2,1)S(1)}, u32[]{:S(2)}, u32[]{:S(2)}) collective-permute-start(bf16[256,640]{1,0:T(8,128)(2,1)} %get-tuple-element.49), channel_id=1, source_target_pairs={{0,1},{1,0},{2,3},{3,2},{4,5},{5,4},{6,7},{7,6},{8,9},{9,8},{10,11... | collective-permute-start | bytes 983048 | tf_op jit(solution)/shard_map/ppermute | solution.py:642
  130.7 1.5 collective-permute-start.20
  133.6 3.2 %rest_products.1 = (bf16[256,384]{1,0:T(8,128)(2,1)}, bf16[256,384]{1,0:T(8,128)(2,1)}, bf16[256,384]{1,0:T(8,128)(2,1)}, bf16[256,384]{1,0:T(8,128)(2,1)}) custom-call(s32[9]{0:T(128)} %stack.123.meta_ref, bf16[128,4096]{1,0:T(8,128)(2,1)} %masked_rows.4.refs_0_, bf16[128,4096]{1,0:T(8,128)(2,1)} %masked_rows.5.refs_1_, ...), custom_call_target="tpu_custom_call" | custom-call | flops 1000 | bytes 1000 | tf_op jit(solution)/shard_map/rest_products/pallas_call | solution.py:476
  137.2 1.8 %collective-permute-start.18 = (bf16[256,384]{1,0:T(8,128)(2,1)}, bf16[256,384]{1,0:T(8,128)(2,1)S(1)}, u32[]{:S(2)}, u32[]{:S(2)}) collective-permute-start(bf16[256,384]{1,0:T(8,128)(2,1)} %get-tuple-element.54), channel_id=1, source_target_pairs={{0,3},{1,2},{2,1},{3,0},{4,7},{5,6},{6,5},{7,4},{8,11},{9,10},{10,... | collective-permute-start | bytes 589832 | tf_op jit(solution)/shard_map/ppermute | solution.py:644
  140.0 7.6 %collective-permute-done.20.refs_3_ = bf16[256,640]{1,0:T(8,128)(2,1)S(1)} collective-permute-done((bf16[256,640]{1,0:T(8,128)(2,1)}, bf16[256,640]{1,0:T(8,128)(2,1)S(1)}, u32[]{:S(2)}, u32[]{:S(2)}) %collective-permute-start.20) | collective-permute-done | bytes 327712 | tf_op jit(solution)/shard_map/ppermute | solution.py:644
  147.6 2.0 %assembled.2.refs_4_ = bf16[256,4096]{1,0:T(8,128)(2,1)} custom-call(s32[2]{0:T(128)S(1)} %get-tuple-element.60.place_ref, f32[4,1,4096]{2,1,0:T(1,128)S(1)} %reshape.24.mask_ref, bf16[256,640]{1,0:T(8,128)(2,1)S(1)} %copy-done.4, bf16[256,640]{1,0:T(8,128)(2,1)S(1)} %collective-permute-done.15.refs_1_, ...), custom_call_target="tpu_custom_call" | custom-call | flops 1000 | bytes 1000 | tf_op jit(solution)/shard_map/assembled/pallas_call | solution.py:523
  149.6 1.6 %collective-permute-done.17.refs_2_ = bf16[256,384]{1,0:T(8,128)(2,1)S(1)} collective-permute-done((bf16[256,384]{1,0:T(8,128)(2,1)}, bf16[256,384]{1,0:T(8,128)(2,1)S(1)}, u32[]{:S(2)}, u32[]{:S(2)}) %collective-permute-start.17) | collective-permute-done | bytes 196640 | tf_op jit(solution)/shard_map/ppermute | solution.py:564
  151.2 4.4 %collective-permute-done.18.refs_3_ = bf16[256,384]{1,0:T(8,128)(2,1)S(1)} collective-permute-done((bf16[256,384]{1,0:T(8,128)(2,1)}, bf16[256,384]{1,0:T(8,128)(2,1)S(1)}, u32[]{:S(2)}, u32[]{:S(2)}) %collective-permute-start.18) | collective-permute-done | bytes 196640 | tf_op jit(solution)/shard_map/ppermute | solution.py:644
  155.6 1.6 %assembled.3 = bf16[256,4096]{1,0:T(8,128)(2,1)} custom-call(s32[2]{0:T(128)S(1)} %get-tuple-element.59.place_ref, f32[4,1,4096]{2,1,0:T(1,128)S(1)} %reshape.24.mask_ref, bf16[256,384]{1,0:T(8,128)(2,1)S(1)} %copy-done.5, bf16[256,384]{1,0:T(8,128)(2,1)S(1)} %collective-permute-done.16.refs_1_, ...), custom_call_target="tpu_custom_call", output_to_operand_aliasing={{}: (6, {})} | custom-call | flops 1000 | bytes 1000 | tf_op jit(solution)/shard_map/assembled/pallas_call | solution.py:523
  (59 shorter events, 17.5 us)
Async XLA Ops:
  2.2 24.3 %collective-permute-start = (bf16[512,1024]{1,0:T(8,128)(2,1)}, bf16[512,1024]{1,0:T(8,128)(2,1)S(1)}, u32[]{:S(2)}, u32[]{:S(2)}) collective-permute-start(bf16[512,1024]{1,0:T(8,128)(2,1)} %b_strips.2), channel_id=1, source_target_pairs={{0,2},{2,0},{4,6},{6,4},{8,10},{10,8},{12,14},{14,12},{1,3},{3,1},... | collective-permute-start | bytes 3145736 | tf_op jit(solution)/shard_map/ppermute | solution.py:564
  3.5 5.5 %copy-start.8 = (s32[8,64]{1,0:T(8,128)S(1)}, s32[8,64]{1,0:T(8,128)}, u32[]{:S(2)}) copy-start(s32[8,64]{1,0:T(8,128)} %param.6) | copy-start | bytes 6148
  5.7 24.0 %collective-permute-start.1 = (bf16[512,1024]{1,0:T(8,128)(2,1)}, bf16[512,1024]{1,0:T(8,128)(2,1)S(1)}, u32[]{:S(2)}, u32[]{:S(2)}) collective-permute-start(bf16[512,1024]{1,0:T(8,128)(2,1)} %b_strips.3.refs_8_), channel_id=1, source_target_pairs={{0,4},{2,6},{4,0},{6,2},{8,12},{10,14},{12,8},{14,10},{1,5},{3,7},... | collective-permute-start | bytes 3145736 | tf_op jit(solution)/shard_map/ppermute | solution.py:564
  7.1 27.4 %collective-permute-start.7 = (bf16[512,1024]{1,0:T(8,128)(2,1)}, bf16[512,1024]{1,0:T(8,128)(2,1)S(1)}, u32[]{:S(2)}, u32[]{:S(2)}) collective-permute-start(bf16[512,1024]{1,0:T(8,128)(2,1)} %b_strips.3.refs_8_), channel_id=1, source_target_pairs={{4,8},{6,10},{8,4},{10,6},{5,9},{7,11},{9,5},{11,7},{20,24},{22,26... | collective-permute-start | bytes 3145736 | tf_op jit(solution)/shard_map/ppermute | solution.py:564
  26.5 1.0 copy-start.10
  29.7 37.8 %copy-start.1 = (bf16[512,1024]{1,0:T(8,128)(2,1)}, bf16[512,1024]{1,0:T(8,128)(2,1)S(1)}, u32[]{:S(2)}) copy-start(bf16[512,1024]{1,0:T(8,128)(2,1)S(1)} %collective-permute-done.1.refs_0_.refs_2_.refs_12_) | copy-start | bytes 3145732
  29.7 23.1 %collective-permute-start.2 = (bf16[512,1024]{1,0:T(8,128)(2,1)}, bf16[512,1024]{1,0:T(8,128)(2,1)S(1)}, u32[]{:S(2)}, u32[]{:S(2)}) collective-permute-start(bf16[512,1024]{1,0:T(8,128)(2,1)} %copy-done.10), channel_id=1, source_target_pairs={{0,4},{2,6},{4,0},{6,2},{8,12},{10,14},{12,8},{14,10},{1,5},{3,7},... | collective-permute-start | bytes 3145736 | tf_op jit(solution)/shard_map/ppermute | solution.py:564
  31.0 24.7 %collective-permute-start.8 = (bf16[512,1024]{1,0:T(8,128)(2,1)}, bf16[512,1024]{1,0:T(8,128)(2,1)}, u32[]{:S(2)}, u32[]{:S(2)}) collective-permute-start(bf16[512,1024]{1,0:T(8,128)(2,1)} %copy-done.10), channel_id=1, source_target_pairs={{4,8},{6,10},{8,4},{10,6},{5,9},{7,11},{9,5},{11,7},{20,24},{22,26... | collective-permute-start | bytes 3145736 | tf_op jit(solution)/shard_map/ppermute | solution.py:564
  32.9 35.8 %collective-permute-start.3 = (bf16[128,4096]{1,0:T(8,128)(2,1)}, bf16[128,4096]{1,0:T(8,128)(2,1)}, u32[]{:S(2)}, u32[]{:S(2)}) collective-permute-start(bf16[128,4096]{1,0:T(8,128)(2,1)} %masked_rows.4.refs_0_), channel_id=1, source_target_pairs={{0,2},{2,0},{4,6},{6,4},{8,10},{10,8},{12,14},{14,12},{1,3},{3,1},... | collective-permute-start | bytes 3145736 | tf_op jit(solution)/shard_map/ppermute | solution.py:564
  33.2 45.1 %collective-permute-start.4 = (bf16[128,4096]{1,0:T(8,128)(2,1)}, bf16[128,4096]{1,0:T(8,128)(2,1)}, u32[]{:S(2)}, u32[]{:S(2)}) collective-permute-start(bf16[128,4096]{1,0:T(8,128)(2,1)} %masked_rows.5.refs_1_), channel_id=1, source_target_pairs={{0,2},{2,0},{4,6},{6,4},{8,10},{10,8},{12,14},{14,12},{1,3},{3,1},... | collective-permute-start | bytes 3145736 | tf_op jit(solution)/shard_map/ppermute | solution.py:564
  34.4 24.4 %copy-start.3 = (bf16[512,1024]{1,0:T(8,128)(2,1)}, bf16[512,1024]{1,0:T(8,128)(2,1)S(1)}, u32[]{:S(2)}) copy-start(bf16[512,1024]{1,0:T(8,128)(2,1)S(1)} %collective-permute-done.7.refs_0_.refs_10_) | copy-start | bytes 3145732
  34.5 25.7 %collective-permute-start.9 = (bf16[512,384]{1,0:T(8,128)(2,1)S(1)}, bf16[512,384]{1,0:T(8,128)(2,1)}, u32[]{:S(2)}, u32[]{:S(2)}) collective-permute-start(bf16[512,384]{1,0:T(8,128)(2,1)S(1)} %slice.4), channel_id=1, source_target_pairs={{4,0},{6,2},{8,12},{10,14},{5,1},{7,3},{9,13},{11,15},{20,16},{22,... | collective-permute-start | bytes 1179656 | tf_op jit(solution)/shard_map/ppermute | solution.py:564
  52.8 14.7 %copy-start.2 = (bf16[512,1024]{1,0:T(8,128)(2,1)}, bf16[512,1024]{1,0:T(8,128)(2,1)S(1)}, u32[]{:S(2)}) copy-start(bf16[512,1024]{1,0:T(8,128)(2,1)S(1)} %collective-permute-done.2.refs_1_.refs_3_.refs_13_) | copy-start | bytes 3145732
  60.2 36.3 %collective-permute-start.10 = (bf16[512,1280]{1,0:T(8,128)(2,1)}, bf16[512,1280]{1,0:T(8,128)(2,1)}, u32[]{:S(2)}, u32[]{:S(2)}) collective-permute-start(bf16[512,1280]{1,0:T(8,128)(2,1)} %get-tuple-element.42), channel_id=1, source_target_pairs={{4,0},{6,2},{8,12},{10,14},{5,1},{7,3},{9,13},{11,15},{20,16},{22,... | collective-permute-start | bytes 3932168 | tf_op jit(solution)/shard_map/ppermute | solution.py:564
  65.5 23.8 %collective-permute-start.11 = (bf16[512,1024]{1,0:T(8,128)(2,1)}, bf16[512,1024]{1,0:T(8,128)(2,1)}, u32[]{:S(2)}, u32[]{:S(2)}) collective-permute-start(bf16[512,1024]{1,0:T(8,128)(2,1)} %get-tuple-element.45), channel_id=1, source_target_pairs={{4,8},{6,10},{8,4},{10,6},{5,9},{7,11},{9,5},{11,7},{20,24},{22,26... | collective-permute-start | bytes 3145736 | tf_op jit(solution)/shard_map/ppermute | solution.py:564
  78.2 18.3 %collective-permute-start.5 = (bf16[128,4096]{1,0:T(8,128)(2,1)}, bf16[128,4096]{1,0:T(8,128)(2,1)S(1)}, u32[]{:S(2)}, u32[]{:S(2)}) collective-permute-start(bf16[128,4096]{1,0:T(8,128)(2,1)} %collective-permute-done.3.refs_4_), channel_id=1, source_target_pairs={{0,1},{1,0},{2,3},{3,2},{4,5},{5,4},{6,7},{7,6},{8,9},{9,8},{10,11... | collective-permute-start | bytes 3145736 | tf_op jit(solution)/shard_map/ppermute | solution.py:607
  81.3 15.2 %collective-permute-start.6 = (bf16[128,4096]{1,0:T(8,128)(2,1)}, bf16[128,4096]{1,0:T(8,128)(2,1)}, u32[]{:S(2)}, u32[]{:S(2)}) collective-permute-start(bf16[128,4096]{1,0:T(8,128)(2,1)} %collective-permute-done.4.refs_5_), channel_id=1, source_target_pairs={{0,1},{1,0},{2,3},{3,2},{4,5},{5,4},{6,7},{7,6},{8,9},{9,8},{10,11... | collective-permute-start | bytes 3145736 | tf_op jit(solution)/shard_map/ppermute | solution.py:607
  81.3 30.7 %collective-permute-start.13 = (bf16[512,1024]{1,0:T(8,128)(2,1)}, bf16[512,1024]{1,0:T(8,128)(2,1)S(1)}, u32[]{:S(2)}, u32[]{:S(2)}) collective-permute-start(bf16[512,1024]{1,0:T(8,128)(2,1)} %packed.3), channel_id=1, source_target_pairs={{4,8},{6,10},{8,4},{10,6},{5,9},{7,11},{9,5},{11,7},{20,24},{22,26... | collective-permute-start | bytes 3145736 | tf_op jit(solution)/shard_map/ppermute | solution.py:564
  89.3 25.5 %collective-permute-start.12 = (bf16[512,1024]{1,0:T(8,128)(2,1)}, bf16[512,1024]{1,0:T(8,128)(2,1)}, u32[]{:S(2)}, u32[]{:S(2)}) collective-permute-start(bf16[512,1024]{1,0:T(8,128)(2,1)} %collective-permute-done.11.refs_9_), channel_id=1, source_target_pairs={{4,0},{6,2},{8,12},{10,14},{5,1},{7,3},{9,13},{11,15},{20,16},{22,... | collective-permute-start | bytes 3145736 | tf_op jit(solution)/shard_map/ppermute | solution.py:564
  96.5 1.0 copy-start.6
  112.0 2.8 %copy-start = (bf16[512,1024]{1,0:T(8,128)(2,1)}, bf16[512,1024]{1,0:T(8,128)(2,1)S(1)}, u32[]{:S(2)}) copy-start(bf16[512,1024]{1,0:T(8,128)(2,1)S(1)} %collective-permute-done.13.refs_11_.refs_0_) | copy-start | bytes 3145732
  112.7 20.0 %collective-permute-start.14 = (bf16[512,640]{1,0:T(8,128)(2,1)S(1)}, bf16[512,640]{1,0:T(8,128)(2,1)S(1)}, u32[]{:S(2)}, u32[]{:S(2)}) collective-permute-start(bf16[512,640]{1,0:T(8,128)(2,1)S(1)} %packed.5), channel_id=1, source_target_pairs={{4,0},{6,2},{8,12},{10,14},{5,1},{7,3},{9,13},{11,15},{20,16},{22,... | collective-permute-start | bytes 1966088 | tf_op jit(solution)/shard_map/ppermute | solution.py:564
  122.8 9.9 %collective-permute-start.15 = (bf16[256,640]{1,0:T(8,128)(2,1)}, bf16[256,640]{1,0:T(8,128)(2,1)S(1)}, u32[]{:S(2)}, u32[]{:S(2)}) collective-permute-start(bf16[256,640]{1,0:T(8,128)(2,1)} %get-tuple-element.49), channel_id=1, source_target_pairs={{0,1},{1,0},{2,3},{3,2},{4,5},{5,4},{6,7},{7,6},{8,9},{9,8},{10,11... | collective-permute-start | bytes 983048 | tf_op jit(solution)/shard_map/ppermute | solution.py:642
  130.5 9.5 %collective-permute-start.19 = (bf16[256,640]{1,0:T(8,128)(2,1)}, bf16[256,640]{1,0:T(8,128)(2,1)S(1)}, u32[]{:S(2)}, u32[]{:S(2)}) collective-permute-start(bf16[256,640]{1,0:T(8,128)(2,1)} %get-tuple-element.57), channel_id=1, source_target_pairs={{0,2},{2,0},{4,6},{6,4},{8,10},{10,8},{12,14},{14,12},{1,3},{3,1},... | collective-permute-start | bytes 983048 | tf_op jit(solution)/shard_map/ppermute | solution.py:564
  130.7 16.9 %collective-permute-start.20 = (bf16[256,640]{1,0:T(8,128)(2,1)}, bf16[256,640]{1,0:T(8,128)(2,1)S(1)}, u32[]{:S(2)}, u32[]{:S(2)}) collective-permute-start(bf16[256,640]{1,0:T(8,128)(2,1)} %get-tuple-element.58), channel_id=1, source_target_pairs={{0,3},{1,2},{2,1},{3,0},{4,7},{5,6},{6,5},{7,4},{8,11},{9,10},{10,... | collective-permute-start | bytes 983048 | tf_op jit(solution)/shard_map/ppermute | solution.py:644
  132.7 0.9 copy-start.7
  133.6 5.4 %copy-start.9 = (s32[4,64]{1,0:T(4,128)S(1)}, s32[4,64]{1,0:T(4,128)}, u32[]{:S(2)}) copy-start(s32[4,64]{1,0:T(4,128)} %param.7) | copy-start | bytes 3076
  133.6 14.0 %copy-start.4 = (bf16[256,640]{1,0:T(8,128)(2,1)S(1)}, bf16[256,640]{1,0:T(8,128)(2,1)}, u32[]{:S(2)}) copy-start(bf16[256,640]{1,0:T(8,128)(2,1)} %get-tuple-element.55.refs_0_) | copy-start | bytes 983044
  136.8 18.8 %copy-start.5 = (bf16[256,384]{1,0:T(8,128)(2,1)S(1)}, bf16[256,384]{1,0:T(8,128)(2,1)}, u32[]{:S(2)}) copy-start(bf16[256,384]{1,0:T(8,128)(2,1)} %get-tuple-element.51.refs_0_) | copy-start | bytes 589828
  136.8 12.8 %collective-permute-start.16 = (bf16[256,384]{1,0:T(8,128)(2,1)}, bf16[256,384]{1,0:T(8,128)(2,1)S(1)}, u32[]{:S(2)}, u32[]{:S(2)}) collective-permute-start(bf16[256,384]{1,0:T(8,128)(2,1)} %get-tuple-element.52), channel_id=1, source_target_pairs={{0,1},{1,0},{2,3},{3,2},{4,5},{5,4},{6,7},{7,6},{8,9},{9,8},{10,11... | collective-permute-start | bytes 589832 | tf_op jit(solution)/shard_map/ppermute | solution.py:642
  137.0 14.2 %collective-permute-start.17 = (bf16[256,384]{1,0:T(8,128)(2,1)}, bf16[256,384]{1,0:T(8,128)(2,1)S(1)}, u32[]{:S(2)}, u32[]{:S(2)}) collective-permute-start(bf16[256,384]{1,0:T(8,128)(2,1)} %get-tuple-element.53), channel_id=1, source_target_pairs={{0,2},{2,0},{4,6},{6,4},{8,10},{10,8},{12,14},{14,12},{1,3},{3,1},... | collective-permute-start | bytes 589832 | tf_op jit(solution)/shard_map/ppermute | solution.py:564
  137.2 18.3 %collective-permute-start.18 = (bf16[256,384]{1,0:T(8,128)(2,1)}, bf16[256,384]{1,0:T(8,128)(2,1)S(1)}, u32[]{:S(2)}, u32[]{:S(2)}) collective-permute-start(bf16[256,384]{1,0:T(8,128)(2,1)} %get-tuple-element.54), channel_id=1, source_target_pairs={{0,3},{1,2},{2,1},{3,0},{4,7},{5,6},{6,5},{7,4},{8,11},{9,10},{10,... | collective-permute-start | bytes 589832 | tf_op jit(solution)/shard_map/ppermute | solution.py:644

commit v13 on v12

--- a/solution.py
+++ b/solution.py
@@ -598,7 +598,7 @@
         ],
     )
     (fwd_second,) = packed([second_out], [swap_a, swap_b], [8], [(0, (0,), 4, 0, 0, None), (1, (0,), 4, 0, 4, None)])
-    mid_a, mid_b, fwd_first = together(mid_a, mid_b, fwd_first)
+    mid_a, mid_b, fwd_first, *x_rest = together(mid_a, mid_b, fwd_first, *x_rest)
     mid_b = line(mid_b, outward)
     fwd_first = line(fwd_first, cross)
     fwd_second, *x_across = together(fwd_second, *x_across)

time: 158 us -> 154 us (0.975)
  the two profiles are of different devices: /device:TPU:17 before, /device:TPU:0 now
where the time goes in v13:
time: 154 us; the launch traced here: 151 us
  waiting for transfers between devices  76.1 us (49%)
  Pallas kernels  47 us (31%)
  starting transfers between devices  22.5 us (15%)
  local copies, waits for them, and re-layouts  4.99 us (3%)
    ppermute x15, waiting for transfers between devices, line(): return lax.ppermute(value, 'grid', pairs)  70.4 us
    ppermute x15, starting transfers between devices, line(): return lax.ppermute(value, 'grid', pairs)  20.7 us
    pallas_call x1, Pallas kernels, whole_products(): pl.pallas_call(functools.partial(whole_kernel, plan), out_shape=jax.Shape...  14.1 us
    pallas_call x4, Pallas kernels, masked_rows(): pl.pallas_call(mask_kernel, grid_spec=pltpu.PrefetchScalarGridSpec(num_sc...  8.52 us
    pallas_call x1, Pallas kernels, half_products(): pl.pallas_call(half_kernel, out_shape=[jax.ShapeDtypeStruct((rows, n_done...  6.16 us
    pallas_call x1, Pallas kernels, rest_products(): pl.pallas_call(rest_kernel, out_shape=[jax.ShapeDtypeStruct((rows, width)...  5.1 us
    pallas_call x3, Pallas kernels, packed(): pl.pallas_call(functools.partial(pack_kernel, plan, len(sources)), out_sh...  5.05 us
    ppermute x2, waiting for transfers between devices, exchanged(): lax.ppermute(pieces[3], ('grid', 'depth'), opposite)  4.46 us
  transfers between devices with their start and end apart: 21, of which 13 were waited for; matrix products, arithmetic and copies ran while one was open for 2% of the time, Pallas kernels for 29%

profile of v13, /device:TPU:0, one launch (start us, length us, event | category | flops | bytes accessed | tf_op | source)
XLA Modules:
  0.0 151.3 jit_solution(10646001671777091822)
XLA Ops:
  0.0 2.2 %b_strips.2 = bf16[512,1024]{1,0:T(8,128)(2,1)} custom-call(s32[1]{0:T(128)} %bitcast.9.quarter_ref, bf16[512,4096]{1,0:T(8,128)(2,1)} %w_ref.2), custom_call_target="tpu_custom_call" | custom-call | flops 1000 | bytes 1000 | tf_op jit(solution)/shard_map/b_strips/pallas_call | solution.py:86
  2.2 3.0 %collective-permute-start = (bf16[512,1024]{1,0:T(8,128)(2,1)}, bf16[512,1024]{1,0:T(8,128)(2,1)S(1)}, u32[]{:S(2)}, u32[]{:S(2)}) collective-permute-start(bf16[512,1024]{1,0:T(8,128)(2,1)} %b_strips.2), channel_id=1, source_target_pairs={{0,2},{2,0},{4,6},{6,4},{8,10},{10,8},{12,14},{14,12},{1,3},{3,1},... | collective-permute-start | bytes 3145736 | tf_op jit(solution)/shard_map/ppermute | solution.py:564
  5.2 2.3 %b_strips.3.refs_8_ = bf16[512,1024]{1,0:T(8,128)(2,1)} custom-call(s32[1]{0:T(128)} %bitcast.quarter_ref, bf16[512,4096]{1,0:T(8,128)(2,1)} %w_ref.2), custom_call_target="tpu_custom_call" | custom-call | flops 1000 | bytes 1000 | tf_op jit(solution)/shard_map/b_strips/pallas_call | solution.py:86
  7.5 1.6 %collective-permute-start.3 = (bf16[512,1024]{1,0:T(8,128)(2,1)}, bf16[512,1024]{1,0:T(8,128)(2,1)S(1)}, u32[]{:S(2)}, u32[]{:S(2)}) collective-permute-start(bf16[512,1024]{1,0:T(8,128)(2,1)} %b_strips.3.refs_8_), channel_id=1, source_target_pairs={{0,4},{2,6},{4,0},{6,2},{8,12},{10,14},{12,8},{14,10},{1,5},{3,7},... | collective-permute-start | bytes 3145736 | tf_op jit(solution)/shard_map/ppermute | solution.py:564
  10.8 2.1 %masked_rows.5.refs_1_ = bf16[128,4096]{1,0:T(8,128)(2,1)} custom-call(s32[1]{0:T(128)} %bitcast.11.first_ref, f32[8,1,4096]{2,1,0:T(1,128)} %reshape.27.mask_ref, bf16[512,4096]{1,0:T(8,128)(2,1)} %x_ref.7), custom_call_target="tpu_custom_call" | custom-call | flops 1000 | bytes 1000 | tf_op jit(solution)/shard_map/masked_rows/pallas_call | solution.py:148
  13.0 2.1 %masked_rows.4.refs_0_ = bf16[128,4096]{1,0:T(8,128)(2,1)} custom-call(s32[1]{0:T(128)} %bitcast.10.first_ref, f32[8,1,4096]{2,1,0:T(1,128)} %reshape.27.mask_ref, bf16[512,4096]{1,0:T(8,128)(2,1)} %x_ref.7), custom_call_target="tpu_custom_call" | custom-call | flops 1000 | bytes 1000 | tf_op jit(solution)/shard_map/masked_rows/pallas_call | solution.py:148
  15.1 13.5 %collective-permute-done.refs_9_ = bf16[512,1024]{1,0:T(8,128)(2,1)S(1)} collective-permute-done((bf16[512,1024]{1,0:T(8,128)(2,1)}, bf16[512,1024]{1,0:T(8,128)(2,1)S(1)}, u32[]{:S(2)}, u32[]{:S(2)}) %collective-permute-start) | collective-permute-done | bytes 1048608 | tf_op jit(solution)/shard_map/ppermute | solution.py:564
  29.6 2.8 %collective-permute-done.3.refs_2_.refs_0_.refs_12_ = bf16[512,1024]{1,0:T(8,128)(2,1)S(1)} collective-permute-done((bf16[512,1024]{1,0:T(8,128)(2,1)}, bf16[512,1024]{1,0:T(8,128)(2,1)S(1)}, u32[]{:S(2)}, u32[]{:S(2)}) %collective-permute-start.3) | collective-permute-done | bytes 1048608 | tf_op jit(solution)/shard_map/ppermute | solution.py:564
  32.4 1.6 %collective-permute-start.5 = (bf16[512,1024]{1,0:T(8,128)(2,1)}, bf16[512,1024]{1,0:T(8,128)(2,1)S(1)}, u32[]{:S(2)}, u32[]{:S(2)}) collective-permute-start(bf16[512,1024]{1,0:T(8,128)(2,1)} %copy-done.10), channel_id=1, source_target_pairs={{0,4},{2,6},{4,0},{6,2},{8,12},{10,14},{12,8},{14,10},{1,5},{3,7},... | collective-permute-start | bytes 3145736 | tf_op jit(solution)/shard_map/ppermute | solution.py:564
  34.0 1.6 %collective-permute-start.4 = (bf16[512,1024]{1,0:T(8,128)(2,1)}, bf16[512,1024]{1,0:T(8,128)(2,1)}, u32[]{:S(2)}, u32[]{:S(2)}) collective-permute-start(bf16[512,1024]{1,0:T(8,128)(2,1)} %copy-done.10), channel_id=1, source_target_pairs={{4,8},{6,10},{8,4},{10,6},{5,9},{7,11},{9,5},{11,7},{20,24},{22,26... | collective-permute-start | bytes 3145736 | tf_op jit(solution)/shard_map/ppermute | solution.py:564
  36.1 1.5 %collective-permute-start.7 = (bf16[128,4096]{1,0:T(8,128)(2,1)}, bf16[128,4096]{1,0:T(8,128)(2,1)}, u32[]{:S(2)}, u32[]{:S(2)}) collective-permute-start(bf16[128,4096]{1,0:T(8,128)(2,1)} %masked_rows.5.refs_1_), channel_id=1, source_target_pairs={{0,2},{2,0},{4,6},{6,4},{8,10},{10,8},{12,14},{14,12},{1,3},{3,1},... | collective-permute-start | bytes 3145736 | tf_op jit(solution)/shard_map/ppermute | solution.py:564
  37.7 1.3 collective-permute-start.2
  39.0 2.1 %masked_rows.7.refs_3_ = bf16[128,4096]{1,0:T(8,128)(2,1)} custom-call(s32[1]{0:T(128)} %bitcast.15.first_ref, f32[8,1,4096]{2,1,0:T(1,128)} %reshape.27.mask_ref, bf16[512,4096]{1,0:T(8,128)(2,1)} %x_ref.7), custom_call_target="tpu_custom_call" | custom-call | flops 1000 | bytes 1000 | tf_op jit(solution)/shard_map/masked_rows/pallas_call | solution.py:148
  41.1 2.1 %masked_rows.6.refs_2_ = bf16[128,4096]{1,0:T(8,128)(2,1)} custom-call(s32[1]{0:T(128)} %bitcast.14.first_ref, f32[8,1,4096]{2,1,0:T(1,128)} %reshape.27.mask_ref, bf16[512,4096]{1,0:T(8,128)(2,1)} %x_ref.7), custom_call_target="tpu_custom_call" | custom-call | flops 1000 | bytes 1000 | tf_op jit(solution)/shard_map/masked_rows/pallas_call | solution.py:148
  43.3 15.4 %collective-permute-done.5.refs_3_.refs_1_.refs_13_ = bf16[512,1024]{1,0:T(8,128)(2,1)S(1)} collective-permute-done((bf16[512,1024]{1,0:T(8,128)(2,1)}, bf16[512,1024]{1,0:T(8,128)(2,1)S(1)}, u32[]{:S(2)}, u32[]{:S(2)}) %collective-permute-start.5) | collective-permute-done | bytes 1048608 | tf_op jit(solution)/shard_map/ppermute | solution.py:564
  58.7 3.2 %packed.3 = (bf16[512,1280]{1,0:T(8,128)(2,1)}, bf16[512,1024]{1,0:T(8,128)(2,1)}) custom-call(s32[2]{0:T(128)S(1)} %pad_add_fusion.1.meta_ref, bf16[512,1024]{1,0:T(8,128)(2,1)S(1)} %collective-permute-done.1.refs_0_.refs_10_, bf16[512,1024]{1,0:T(8,128)(2,1)} %collective-permute-done.4.refs_1_.refs_11_, ...), custom_call_target="tpu_custom_call" | custom-call | flops 1000 | bytes 1000 | tf_op jit(solution)/shard_map/packed/pallas_call | solution.py:129
  61.9 2.9 %collective-permute-done.2.refs_15_ = bf16[512,384]{1,0:T(8,128)(2,1)} collective-permute-done((bf16[512,384]{1,0:T(8,128)(2,1)S(1)}, bf16[512,384]{1,0:T(8,128)(2,1)}, u32[]{:S(2)}, u32[]{:S(2)}) %collective-permute-start.2) | collective-permute-done | bytes 393248 | tf_op jit(solution)/shard_map/ppermute | solution.py:564
  66.1 1.6 %collective-permute-start.11 = (bf16[512,1024]{1,0:T(8,128)(2,1)}, bf16[512,1024]{1,0:T(8,128)(2,1)}, u32[]{:S(2)}, u32[]{:S(2)}) collective-permute-start(bf16[512,1024]{1,0:T(8,128)(2,1)} %get-tuple-element.49), channel_id=1, source_target_pairs={{4,8},{6,10},{8,4},{10,6},{5,9},{7,11},{9,5},{11,7},{20,24},{22,26... | collective-permute-start | bytes 3145736 | tf_op jit(solution)/shard_map/ppermute | solution.py:564
  68.9 12.9 %collective-permute-done.7.refs_5_ = bf16[128,4096]{1,0:T(8,128)(2,1)} collective-permute-done((bf16[128,4096]{1,0:T(8,128)(2,1)}, bf16[128,4096]{1,0:T(8,128)(2,1)}, u32[]{:S(2)}, u32[]{:S(2)}) %collective-permute-start.7) | collective-permute-done | bytes 1048608 | tf_op jit(solution)/shard_map/ppermute | solution.py:564
  83.1 1.3 collective-permute-start.12
  86.3 9.7 %collective-permute-done.10.refs_14_ = bf16[512,1280]{1,0:T(8,128)(2,1)} collective-permute-done((bf16[512,1280]{1,0:T(8,128)(2,1)}, bf16[512,1280]{1,0:T(8,128)(2,1)}, u32[]{:S(2)}, u32[]{:S(2)}) %collective-permute-start.10) | collective-permute-done | bytes 1310752 | tf_op jit(solution)/shard_map/ppermute | solution.py:564
  96.0 14.1 %whole_products.1.refs_8_ = f32[2,512,1024]{2,1,0:T(8,128)} custom-call(s32[14]{0:T(128)} %stack.139.meta_ref, bf16[128,4096]{1,0:T(8,128)(2,1)} %masked_rows.4.refs_0_, bf16[128,4096]{1,0:T(8,128)(2,1)} %masked_rows.5.refs_1_, bf16[128,4096]{1,0:T(8,128)(2,1)} %masked_rows.6.refs_2_, bf16[128,4096]{1,0:T(8,128)(2,1)} %masked_rows.7.refs_3_, ...), custom_call_target="tpu_custom_call" | custom-call | flops 6000000000 | bytes 37748736 | tf_op jit(solution)/shard_map/whole_products/pallas_call | solution.py:280
  110.9 1.3 collective-permute-start.14
  113.0 5.1 %collective-permute-done.12.refs_10_ = bf16[512,1024]{1,0:T(8,128)(2,1)} collective-permute-done((bf16[512,1024]{1,0:T(8,128)(2,1)}, bf16[512,1024]{1,0:T(8,128)(2,1)}, u32[]{:S(2)}, u32[]{:S(2)}) %collective-permute-start.12) | collective-permute-done | bytes 1048608 | tf_op jit(solution)/shard_map/ppermute | solution.py:564
  118.1 6.2 %half_products.1 = (bf16[256,640]{1,0:T(8,128)(2,1)}, bf16[256,640]{1,0:T(8,128)(2,1)}, bf16[256,640]{1,0:T(8,128)(2,1)}, bf16[256,640]{1,0:T(8,128)(2,1)}, f32[2,512,384]{2,1,0:T(8,128)}) custom-call(s32[9]{0:T(128)} %stack.129.meta_ref, bf16[128,4096]{1,0:T(8,128)(2,1)} %masked_rows.4.refs_0_, bf16[128,4096]{1,0:T(8,128)(2,1)} %masked_rows.5.refs_1_, ...), custom_call_target="tpu_custom_call" | custom-call | flops 1000 | bytes 1000 | tf_op jit(solution)/shard_map/half_products/pallas_call | solution.py:396
  124.3 1.5 %collective-permute-start.19 = (bf16[256,640]{1,0:T(8,128)(2,1)}, bf16[256,640]{1,0:T(8,128)(2,1)S(1)}, u32[]{:S(2)}, u32[]{:S(2)}) collective-permute-start(bf16[256,640]{1,0:T(8,128)(2,1)} %get-tuple-element.61), channel_id=1, source_target_pairs={{0,2},{2,0},{4,6},{6,4},{8,10},{10,8},{12,14},{14,12},{1,3},{3,1},... | collective-permute-start | bytes 983048 | tf_op jit(solution)/shard_map/ppermute | solution.py:564
  126.8 5.1 %collective-permute-done.14.refs_9_ = bf16[512,640]{1,0:T(8,128)(2,1)S(1)} collective-permute-done((bf16[512,640]{1,0:T(8,128)(2,1)S(1)}, bf16[512,640]{1,0:T(8,128)(2,1)S(1)}, u32[]{:S(2)}, u32[]{:S(2)}) %collective-permute-start.14) | collective-permute-done | bytes 655392 | tf_op jit(solution)/shard_map/ppermute | solution.py:564
  132.7 5.1 %rest_products.1 = (bf16[256,384]{1,0:T(8,128)(2,1)}, bf16[256,384]{1,0:T(8,128)(2,1)}, bf16[256,384]{1,0:T(8,128)(2,1)}, bf16[256,384]{1,0:T(8,128)(2,1)}) custom-call(s32[9]{0:T(128)} %stack.123.meta_ref, bf16[128,4096]{1,0:T(8,128)(2,1)} %masked_rows.4.refs_0_, bf16[128,4096]{1,0:T(8,128)(2,1)} %masked_rows.5.refs_1_, ...), custom_call_target="tpu_custom_call" | custom-call | flops 1000 | bytes 1000 | tf_op jit(solution)/shard_map/rest_products/pallas_call | solution.py:476
  141.2 2.0 %assembled.2.refs_4_ = bf16[256,4096]{1,0:T(8,128)(2,1)} custom-call(s32[2]{0:T(128)S(1)} %get-tuple-element.64.place_ref, f32[4,1,4096]{2,1,0:T(1,128)S(1)} %reshape.24.mask_ref, bf16[256,640]{1,0:T(8,128)(2,1)S(1)} %copy-done.4, bf16[256,640]{1,0:T(8,128)(2,1)S(1)} %collective-permute-done.15.refs_1_, ...), custom_call_target="tpu_custom_call" | custom-call | flops 1000 | bytes 1000 | tf_op jit(solution)/shard_map/assembled/pallas_call | solution.py:523
  143.2 3.1 %collective-permute-done.17.refs_2_ = bf16[256,384]{1,0:T(8,128)(2,1)S(1)} collective-permute-done((bf16[256,384]{1,0:T(8,128)(2,1)}, bf16[256,384]{1,0:T(8,128)(2,1)S(1)}, u32[]{:S(2)}, u32[]{:S(2)}) %collective-permute-start.17) | collective-permute-done | bytes 196640 | tf_op jit(solution)/shard_map/ppermute | solution.py:564
  146.4 3.3 %collective-permute-done.18.refs_3_ = bf16[256,384]{1,0:T(8,128)(2,1)S(1)} collective-permute-done((bf16[256,384]{1,0:T(8,128)(2,1)}, bf16[256,384]{1,0:T(8,128)(2,1)S(1)}, u32[]{:S(2)}, u32[]{:S(2)}) %collective-permute-start.18) | collective-permute-done | bytes 196640 | tf_op jit(solution)/shard_map/ppermute | solution.py:644
  149.7 1.6 %assembled.3 = bf16[256,4096]{1,0:T(8,128)(2,1)} custom-call(s32[2]{0:T(128)S(1)} %get-tuple-element.63.place_ref, f32[4,1,4096]{2,1,0:T(1,128)S(1)} %reshape.24.mask_ref, bf16[256,384]{1,0:T(8,128)(2,1)S(1)} %copy-done.5, bf16[256,384]{1,0:T(8,128)(2,1)S(1)} %collective-permute-done.16.refs_1_, ...), custom_call_target="tpu_custom_call", output_to_operand_aliasing={{}: (6, {})} | custom-call | flops 1000 | bytes 1000 | tf_op jit(solution)/shard_map/assembled/pallas_call | solution.py:523
  (59 shorter events, 15.5 us)
Async XLA Ops:
  2.2 26.4 %collective-permute-start = (bf16[512,1024]{1,0:T(8,128)(2,1)}, bf16[512,1024]{1,0:T(8,128)(2,1)S(1)}, u32[]{:S(2)}, u32[]{:S(2)}) collective-permute-start(bf16[512,1024]{1,0:T(8,128)(2,1)} %b_strips.2), channel_id=1, source_target_pairs={{0,2},{2,0},{4,6},{6,4},{8,10},{10,8},{12,14},{14,12},{1,3},{3,1},... | collective-permute-start | bytes 3145736 | tf_op jit(solution)/shard_map/ppermute | solution.py:564
  5.2 4.7 %copy-start.8 = (s32[8,64]{1,0:T(8,128)S(1)}, s32[8,64]{1,0:T(8,128)}, u32[]{:S(2)}) copy-start(s32[8,64]{1,0:T(8,128)} %param.6) | copy-start | bytes 6148
  7.5 24.9 %collective-permute-start.3 = (bf16[512,1024]{1,0:T(8,128)(2,1)}, bf16[512,1024]{1,0:T(8,128)(2,1)S(1)}, u32[]{:S(2)}, u32[]{:S(2)}) collective-permute-start(bf16[512,1024]{1,0:T(8,128)(2,1)} %b_strips.3.refs_8_), channel_id=1, source_target_pairs={{0,4},{2,6},{4,0},{6,2},{8,12},{10,14},{12,8},{14,10},{1,5},{3,7},... | collective-permute-start | bytes 3145736 | tf_op jit(solution)/shard_map/ppermute | solution.py:564
  9.1 28.5 %collective-permute-start.1 = (bf16[512,1024]{1,0:T(8,128)(2,1)}, bf16[512,1024]{1,0:T(8,128)(2,1)S(1)}, u32[]{:S(2)}, u32[]{:S(2)}) collective-permute-start(bf16[512,1024]{1,0:T(8,128)(2,1)} %b_strips.3.refs_8_), channel_id=1, source_target_pairs={{4,8},{6,10},{8,4},{10,6},{5,9},{7,11},{9,5},{11,7},{20,24},{22,26... | collective-permute-start | bytes 3145736 | tf_op jit(solution)/shard_map/ppermute | solution.py:564
  28.6 1.0 copy-start.10
  32.4 35.4 %copy-start.1 = (bf16[512,1024]{1,0:T(8,128)(2,1)}, bf16[512,1024]{1,0:T(8,128)(2,1)S(1)}, u32[]{:S(2)}) copy-start(bf16[512,1024]{1,0:T(8,128)(2,1)S(1)} %collective-permute-done.3.refs_2_.refs_0_.refs_12_) | copy-start | bytes 3145732
  32.4 26.3 %collective-permute-start.5 = (bf16[512,1024]{1,0:T(8,128)(2,1)}, bf16[512,1024]{1,0:T(8,128)(2,1)S(1)}, u32[]{:S(2)}, u32[]{:S(2)}) collective-permute-start(bf16[512,1024]{1,0:T(8,128)(2,1)} %copy-done.10), channel_id=1, source_target_pairs={{0,4},{2,6},{4,0},{6,2},{8,12},{10,14},{12,8},{14,10},{1,5},{3,7},... | collective-permute-start | bytes 3145736 | tf_op jit(solution)/shard_map/ppermute | solution.py:564
  34.0 24.7 %collective-permute-start.4 = (bf16[512,1024]{1,0:T(8,128)(2,1)}, bf16[512,1024]{1,0:T(8,128)(2,1)}, u32[]{:S(2)}, u32[]{:S(2)}) collective-permute-start(bf16[512,1024]{1,0:T(8,128)(2,1)} %copy-done.10), channel_id=1, source_target_pairs={{4,8},{6,10},{8,4},{10,6},{5,9},{7,11},{9,5},{11,7},{20,24},{22,26... | collective-permute-start | bytes 3145736 | tf_op jit(solution)/shard_map/ppermute | solution.py:564
  35.6 33.3 %collective-permute-start.6 = (bf16[128,4096]{1,0:T(8,128)(2,1)}, bf16[128,4096]{1,0:T(8,128)(2,1)}, u32[]{:S(2)}, u32[]{:S(2)}) collective-permute-start(bf16[128,4096]{1,0:T(8,128)(2,1)} %masked_rows.4.refs_0_), channel_id=1, source_target_pairs={{0,2},{2,0},{4,6},{6,4},{8,10},{10,8},{12,14},{14,12},{1,3},{3,1},... | collective-permute-start | bytes 3145736 | tf_op jit(solution)/shard_map/ppermute | solution.py:564
  36.1 45.7 %collective-permute-start.7 = (bf16[128,4096]{1,0:T(8,128)(2,1)}, bf16[128,4096]{1,0:T(8,128)(2,1)}, u32[]{:S(2)}, u32[]{:S(2)}) collective-permute-start(bf16[128,4096]{1,0:T(8,128)(2,1)} %masked_rows.5.refs_1_), channel_id=1, source_target_pairs={{0,2},{2,0},{4,6},{6,4},{8,10},{10,8},{12,14},{14,12},{1,3},{3,1},... | collective-permute-start | bytes 3145736 | tf_op jit(solution)/shard_map/ppermute | solution.py:564
  37.6 21.1 %copy-start.3 = (bf16[512,1024]{1,0:T(8,128)(2,1)}, bf16[512,1024]{1,0:T(8,128)(2,1)S(1)}, u32[]{:S(2)}) copy-start(bf16[512,1024]{1,0:T(8,128)(2,1)S(1)} %collective-permute-done.1.refs_0_.refs_10_) | copy-start | bytes 3145732
  37.7 27.2 %collective-permute-start.2 = (bf16[512,384]{1,0:T(8,128)(2,1)S(1)}, bf16[512,384]{1,0:T(8,128)(2,1)}, u32[]{:S(2)}, u32[]{:S(2)}) collective-permute-start(bf16[512,384]{1,0:T(8,128)(2,1)S(1)} %slice.4), channel_id=1, source_target_pairs={{4,0},{6,2},{8,12},{10,14},{5,1},{7,3},{9,13},{11,15},{20,16},{22,... | collective-permute-start | bytes 1179656 | tf_op jit(solution)/shard_map/ppermute | solution.py:564
  58.7 9.1 %copy-start.2 = (bf16[512,1024]{1,0:T(8,128)(2,1)}, bf16[512,1024]{1,0:T(8,128)(2,1)S(1)}, u32[]{:S(2)}) copy-start(bf16[512,1024]{1,0:T(8,128)(2,1)S(1)} %collective-permute-done.5.refs_3_.refs_1_.refs_13_) | copy-start | bytes 3145732
  64.8 31.2 %collective-permute-start.10 = (bf16[512,1280]{1,0:T(8,128)(2,1)}, bf16[512,1280]{1,0:T(8,128)(2,1)}, u32[]{:S(2)}, u32[]{:S(2)}) collective-permute-start(bf16[512,1280]{1,0:T(8,128)(2,1)} %get-tuple-element.46), channel_id=1, source_target_pairs={{4,0},{6,2},{8,12},{10,14},{5,1},{7,3},{9,13},{11,15},{20,16},{22,... | collective-permute-start | bytes 3932168 | tf_op jit(solution)/shard_map/ppermute | solution.py:564
  66.1 16.9 %collective-permute-start.11 = (bf16[512,1024]{1,0:T(8,128)(2,1)}, bf16[512,1024]{1,0:T(8,128)(2,1)}, u32[]{:S(2)}, u32[]{:S(2)}) collective-permute-start(bf16[512,1024]{1,0:T(8,128)(2,1)} %get-tuple-element.49), channel_id=1, source_target_pairs={{4,8},{6,10},{8,4},{10,6},{5,9},{7,11},{9,5},{11,7},{20,24},{22,26... | collective-permute-start | bytes 3145736 | tf_op jit(solution)/shard_map/ppermute | solution.py:564
  81.8 4.3 %collective-permute-start.8 = (bf16[128,4096]{1,0:T(8,128)(2,1)}, bf16[128,4096]{1,0:T(8,128)(2,1)S(1)}, u32[]{:S(2)}, u32[]{:S(2)}) collective-permute-start(bf16[128,4096]{1,0:T(8,128)(2,1)} %collective-permute-done.6.refs_4_), channel_id=1, source_target_pairs={{0,1},{1,0},{2,3},{3,2},{4,5},{5,4},{6,7},{7,6},{8,9},{9,8},{10,11... | collective-permute-start | bytes 3145736 | tf_op jit(solution)/shard_map/ppermute | solution.py:607
  81.8 4.5 %collective-permute-start.9 = (bf16[128,4096]{1,0:T(8,128)(2,1)}, bf16[128,4096]{1,0:T(8,128)(2,1)}, u32[]{:S(2)}, u32[]{:S(2)}) collective-permute-start(bf16[128,4096]{1,0:T(8,128)(2,1)} %collective-permute-done.7.refs_5_), channel_id=1, source_target_pairs={{0,1},{1,0},{2,3},{3,2},{4,5},{5,4},{6,7},{7,6},{8,9},{9,8},{10,11... | collective-permute-start | bytes 3145736 | tf_op jit(solution)/shard_map/ppermute | solution.py:607
  82.3 27.9 %collective-permute-start.13 = (bf16[512,1024]{1,0:T(8,128)(2,1)}, bf16[512,1024]{1,0:T(8,128)(2,1)S(1)}, u32[]{:S(2)}, u32[]{:S(2)}) collective-permute-start(bf16[512,1024]{1,0:T(8,128)(2,1)} %packed.4), channel_id=1, source_target_pairs={{4,8},{6,10},{8,4},{10,6},{5,9},{7,11},{9,5},{11,7},{20,24},{22,26... | collective-permute-start | bytes 3145736 | tf_op jit(solution)/shard_map/ppermute | solution.py:564
  83.1 35.0 %collective-permute-start.12 = (bf16[512,1024]{1,0:T(8,128)(2,1)}, bf16[512,1024]{1,0:T(8,128)(2,1)}, u32[]{:S(2)}, u32[]{:S(2)}) collective-permute-start(bf16[512,1024]{1,0:T(8,128)(2,1)} %collective-permute-done.11.refs_9_), channel_id=1, source_target_pairs={{4,0},{6,2},{8,12},{10,14},{5,1},{7,3},{9,13},{11,15},{20,16},{22,... | collective-permute-start | bytes 3145736 | tf_op jit(solution)/shard_map/ppermute | solution.py:564
  86.1 9.9 %copy-start.6 = (bf16[128,4096]{1,0:T(8,128)(2,1)}, bf16[128,4096]{1,0:T(8,128)(2,1)S(1)}, u32[]{:S(2)}) copy-start(bf16[128,4096]{1,0:T(8,128)(2,1)S(1)} %collective-permute-done.8.refs_6_) | copy-start | bytes 3145732
  110.2 7.9 %copy-start = (bf16[512,1024]{1,0:T(8,128)(2,1)}, bf16[512,1024]{1,0:T(8,128)(2,1)S(1)}, u32[]{:S(2)}) copy-start(bf16[512,1024]{1,0:T(8,128)(2,1)S(1)} %collective-permute-done.13.refs_11_.refs_0_) | copy-start | bytes 3145732
  110.9 20.9 %collective-permute-start.14 = (bf16[512,640]{1,0:T(8,128)(2,1)S(1)}, bf16[512,640]{1,0:T(8,128)(2,1)S(1)}, u32[]{:S(2)}, u32[]{:S(2)}) collective-permute-start(bf16[512,640]{1,0:T(8,128)(2,1)S(1)} %packed.5), channel_id=1, source_target_pairs={{4,0},{6,2},{8,12},{10,14},{5,1},{7,3},{9,13},{11,15},{20,16},{22,... | collective-permute-start | bytes 1966088 | tf_op jit(solution)/shard_map/ppermute | solution.py:564
  124.3 7.6 %collective-permute-start.15 = (bf16[256,640]{1,0:T(8,128)(2,1)}, bf16[256,640]{1,0:T(8,128)(2,1)S(1)}, u32[]{:S(2)}, u32[]{:S(2)}) collective-permute-start(bf16[256,640]{1,0:T(8,128)(2,1)} %get-tuple-element.53), channel_id=1, source_target_pairs={{0,1},{1,0},{2,3},{3,2},{4,5},{5,4},{6,7},{7,6},{8,9},{9,8},{10,11... | collective-permute-start | bytes 983048 | tf_op jit(solution)/shard_map/ppermute | solution.py:642
  124.3 15.7 %collective-permute-start.19 = (bf16[256,640]{1,0:T(8,128)(2,1)}, bf16[256,640]{1,0:T(8,128)(2,1)S(1)}, u32[]{:S(2)}, u32[]{:S(2)}) collective-permute-start(bf16[256,640]{1,0:T(8,128)(2,1)} %get-tuple-element.61), channel_id=1, source_target_pairs={{0,2},{2,0},{4,6},{6,4},{8,10},{10,8},{12,14},{14,12},{1,3},{3,1},... | collective-permute-start | bytes 983048 | tf_op jit(solution)/shard_map/ppermute | solution.py:564
  125.8 15.4 %collective-permute-start.20 = (bf16[256,640]{1,0:T(8,128)(2,1)}, bf16[256,640]{1,0:T(8,128)(2,1)S(1)}, u32[]{:S(2)}, u32[]{:S(2)}) collective-permute-start(bf16[256,640]{1,0:T(8,128)(2,1)} %get-tuple-element.62), channel_id=1, source_target_pairs={{0,3},{1,2},{2,1},{3,0},{4,7},{5,6},{6,5},{7,4},{8,11},{9,10},{10,... | collective-permute-start | bytes 983048 | tf_op jit(solution)/shard_map/ppermute | solution.py:644
  131.8 0.8 copy-start.7
  132.7 7.1 %copy-start.9 = (s32[4,64]{1,0:T(4,128)S(1)}, s32[4,64]{1,0:T(4,128)}, u32[]{:S(2)}) copy-start(s32[4,64]{1,0:T(4,128)} %param.7) | copy-start | bytes 3076
  132.7 8.5 %copy-start.4 = (bf16[256,640]{1,0:T(8,128)(2,1)S(1)}, bf16[256,640]{1,0:T(8,128)(2,1)}, u32[]{:S(2)}) copy-start(bf16[256,640]{1,0:T(8,128)(2,1)} %get-tuple-element.59.refs_0_) | copy-start | bytes 983044
  137.8 11.9 %copy-start.5 = (bf16[256,384]{1,0:T(8,128)(2,1)S(1)}, bf16[256,384]{1,0:T(8,128)(2,1)}, u32[]{:S(2)}) copy-start(bf16[256,384]{1,0:T(8,128)(2,1)} %get-tuple-element.55.refs_0_) | copy-start | bytes 589828
  137.8 5.4 %collective-permute-start.16 = (bf16[256,384]{1,0:T(8,128)(2,1)}, bf16[256,384]{1,0:T(8,128)(2,1)S(1)}, u32[]{:S(2)}, u32[]{:S(2)}) collective-permute-start(bf16[256,384]{1,0:T(8,128)(2,1)} %get-tuple-element.56), channel_id=1, source_target_pairs={{0,1},{1,0},{2,3},{3,2},{4,5},{5,4},{6,7},{7,6},{8,9},{9,8},{10,11... | collective-permute-start | bytes 589832 | tf_op jit(solution)/shard_map/ppermute | solution.py:642
  137.9 8.5 %collective-permute-start.17 = (bf16[256,384]{1,0:T(8,128)(2,1)}, bf16[256,384]{1,0:T(8,128)(2,1)S(1)}, u32[]{:S(2)}, u32[]{:S(2)}) collective-permute-start(bf16[256,384]{1,0:T(8,128)(2,1)} %get-tuple-element.57), channel_id=1, source_target_pairs={{0,2},{2,0},{4,6},{6,4},{8,10},{10,8},{12,14},{14,12},{1,3},{3,1},... | collective-permute-start | bytes 589832 | tf_op jit(solution)/shard_map/ppermute | solution.py:564
  138.9 10.7 %collective-permute-start.18 = (bf16[256,384]{1,0:T(8,128)(2,1)}, bf16[256,384]{1,0:T(8,128)(2,1)S(1)}, u32[]{:S(2)}, u32[]{:S(2)}) collective-permute-start(bf16[256,384]{1,0:T(8,128)(2,1)} %get-tuple-element.58), channel_id=1, source_target_pairs={{0,3},{1,2},{2,1},{3,0},{4,7},{5,6},{6,5},{7,4},{8,11},{9,10},{10,... | collective-permute-start | bytes 589832 | tf_op jit(solution)/shard_map/ppermute | solution.py:644

commit v14 on v12

--- a/solution.py
+++ b/solution.py
@@ -142,8 +142,9 @@
     out_ref[...] = (x_ref[...].astype(jnp.float32) * mask_ref[0]).astype(jnp.bfloat16)
 
 
-def masked_rows(x_band, mask_wide, first, count):
-    block = x_band.shape[0] // mask_wide.shape[0]
+def masked_x(x_band, mask_wide, first):
+    count = mask_wide.shape[0]
+    block = x_band.shape[0] // count
     cols = x_band.shape[1]
     return pl.pallas_call(
         mask_kernel,
@@ -151,34 +152,30 @@
             num_scalar_prefetch=1,
             grid=(count,),
             in_specs=[
-                pl.BlockSpec((1, 1, cols), lambda i, f: (f[0] + i, 0, 0)),
-                pl.BlockSpec((block, cols), lambda i, f: (f[0] + i, 0)),
+                pl.BlockSpec((1, 1, cols), lambda i, f: (lax.rem(f[0] + i, count), 0, 0)),
+                pl.BlockSpec((block, cols), lambda i, f: (lax.rem(f[0] + i, count), 0)),
             ],
             out_specs=pl.BlockSpec((block, cols), lambda i, f: (i, 0)),
         ),
-        out_shape=jax.ShapeDtypeStruct((count * block, cols), jnp.bfloat16),
+        out_shape=jax.ShapeDtypeStruct(x_band.shape, jnp.bfloat16),
         compiler_params=pltpu.CompilerParams(vmem_limit_bytes=58 * MIB),
         cost_estimate=SMALL,
-        name="masked_rows",
+        name="masked_x",
     )(first.reshape(1), mask_wide, x_band)
 
 
-PARTS = 8
+PARTS = 5
 
 
 def x_copies(x_refs, xv, sems, offset_of):
     n_b, _, rows, panel = xv.shape
-    part = 2 * rows // PARTS
     copies = {}
     for p in range(n_b):
         for r in range(PARTS):
-            g, k = divmod(r, PARTS // 2)
+            g = min(r, 1)
             at = pl.multiple_of(offset_of(p, g) * panel, panel)
-            copies[p, r] = pltpu.make_async_copy(
-                x_refs[r].at[:, pl.ds(at, panel)],
-                xv.at[p, g, k * part : (k + 1) * part],
-                sems.at[p, r],
-            )
+            to = xv.at[p, 0] if r == 0 else xv.at[p, 1, (r - 1) * rows // 4 : r * rows // 4]
+            copies[p, r] = pltpu.make_async_copy(x_refs[r].at[:, pl.ds(at, panel)], to, sems.at[p, r])
     return copies
 
 
@@ -272,7 +269,7 @@
 
 
 def whole_products(meta, xs, operands, plan):
-    rows = PARTS // 4 * xs[0].shape[0]
+    rows = xs[0].shape[0] // 2
     panel, quarter = operands[plan[0][0]].shape
     n_b = len(plan)
     any_spec = pl.BlockSpec(memory_space=pl.ANY)
@@ -357,7 +354,7 @@
     pl.when(is_end != 0)(end.start)
 
     def rows_loads(g):
-        return [prev[g]] + [copy for (_, r), copy in x_loads.items() if r // (PARTS // 2) == g]
+        return [prev[g]] + [copy for (_, r), copy in x_loads.items() if min(r, 1) == g]
 
     for g in range(2):
         for copy in rows_loads(g):
@@ -388,7 +385,7 @@
 
 
 def half_products(meta, xs, prev, middle, end, second, n_done):
-    rows = PARTS // 4 * xs[0].shape[0]
+    rows = xs[0].shape[0] // 2
     panel, quarter = second.shape
     any_spec = pl.BlockSpec(memory_space=pl.ANY)
     x_spec = pl.BlockSpec(memory_space=pltpu.HBM)
@@ -435,7 +432,7 @@
     b_copy = pltpu.make_async_copy(b_ref, bv, b_sem)
 
     def x_loads_of(g):
-        return [copy for (_, r), copy in x_loads.items() if r // (PARTS // 2) == g]
+        return [copy for (_, r), copy in x_loads.items() if min(r, 1) == g]
 
     pl.when(is_end != 0)(b_copy.start)
     for g in range(2):
@@ -468,7 +465,7 @@
 
 
 def rest_products(meta, xs, rest, b, quarter):
-    rows = PARTS // 4 * xs[0].shape[0]
+    rows = xs[0].shape[0] // 2
     panel = b.shape[0]
     width = rest.shape[2]
     any_spec = pl.BlockSpec(memory_space=pl.ANY)
@@ -575,13 +572,13 @@
     cross_a = line(own_a, cross)
     mask_wide = widen(a_mask, block)
     rows = a_mask.shape[0]
-    x_mine = [masked_rows(x_band, mask_wide, c * rows // 2 + k * rows // 4, rows // 4) for k in range(2)]
+    x_own = masked_x(x_band, mask_wide, c * rows // 2)
+    x_mine = [x_own[k * panel // 4 : (k + 1) * panel // 4] for k in range(2)]
     own_b, *x_mine = together(own_b, *x_mine)
     own_b, swap_a = together(own_b, swap_a)
     swap_b = line(own_b, swap)
     cross_b = line(own_b, cross)
     x_across = [line(part, across) for part in x_mine]
-    x_rest = [masked_rows(x_band, mask_wide, (1 - c) * rows // 2 + k * rows // 4, rows // 4) for k in range(2)]
 
     mid_a = line(cross_a[:, 5 * LANES :], outward)
     mid_b, fwd_first = packed(
@@ -605,7 +602,7 @@
     far_first = line(fwd_first, outward)
     fwd_second = line(fwd_second, cross)
     x_opposite = [lax.ppermute(part, "depth", layers) for part in x_across]
-    xs = x_mine + x_rest + x_across + x_opposite
+    xs = [x_own] + x_across + x_opposite
 
     def offsets(delta):
         tilt = 2 * y - 1

time: 158 us -> 155 us (0.981)
  the two profiles are of different devices: /device:TPU:17 before, /device:TPU:0 now
where the time goes in v14:
time: 155 us; the launch traced here: 152 us
  waiting for transfers between devices  76.3 us (49%)
  Pallas kernels  44.5 us (29%)
  starting transfers between devices  22.5 us (15%)
  local copies, waits for them, and re-layouts  7.97 us (5%)
    ppermute x15, waiting for transfers between devices, line(): return lax.ppermute(value, 'grid', pairs)  70.6 us
    ppermute x15, starting transfers between devices, line(): return lax.ppermute(value, 'grid', pairs)  20.7 us
    pallas_call x1, Pallas kernels, whole_products(): pl.pallas_call(functools.partial(whole_kernel, plan), out_shape=jax.Shape...  13.6 us
    pallas_call x1, Pallas kernels, masked_x(): pl.pallas_call(mask_kernel, grid_spec=pltpu.PrefetchScalarGridSpec(num_sc...  6.87 us
    pallas_call x1, Pallas kernels, half_products(): pl.pallas_call(half_kernel, out_shape=[jax.ShapeDtypeStruct((rows, n_done...  6.01 us
    pallas_call x3, Pallas kernels, packed(): pl.pallas_call(functools.partial(pack_kernel, plan, len(sources)), out_sh...  5.09 us
    pallas_call x1, Pallas kernels, rest_products(): pl.pallas_call(rest_kernel, out_shape=[jax.ShapeDtypeStruct((rows, width)...  4.95 us
    ppermute x2, waiting for transfers between devices, exchanged(): lax.ppermute(pieces[3], ('grid', 'depth'), opposite)  4.5 us
  transfers between devices with their start and end apart: 21, of which 12 were waited for; matrix products, arithmetic and copies ran while one was open for 4% of the time, Pallas kernels for 27%

profile of v14, /device:TPU:0, one launch (start us, length us, event | category | flops | bytes accessed | tf_op | source)
XLA Modules:
  0.0 152.0 jit_solution(5815905933231485764)
XLA Ops:
  0.0 2.2 %b_strips.2 = bf16[512,1024]{1,0:T(8,128)(2,1)} custom-call(s32[1]{0:T(128)} %bitcast.11.quarter_ref, bf16[512,4096]{1,0:T(8,128)(2,1)} %w_ref.2), custom_call_target="tpu_custom_call" | custom-call | flops 1000 | bytes 1000 | tf_op jit(solution)/shard_map/b_strips/pallas_call | solution.py:86
  2.2 3.0 %collective-permute-start = (bf16[512,1024]{1,0:T(8,128)(2,1)}, bf16[512,1024]{1,0:T(8,128)(2,1)}, u32[]{:S(2)}, u32[]{:S(2)}) collective-permute-start(bf16[512,1024]{1,0:T(8,128)(2,1)} %b_strips.2), channel_id=1, source_target_pairs={{0,2},{2,0},{4,6},{6,4},{8,10},{10,8},{12,14},{14,12},{1,3},{3,1},... | collective-permute-start | bytes 3145736 | tf_op jit(solution)/shard_map/ppermute | solution.py:561
  5.2 2.2 %b_strips.3.refs_5_ = bf16[512,1024]{1,0:T(8,128)(2,1)} custom-call(s32[1]{0:T(128)} %bitcast.quarter_ref, bf16[512,4096]{1,0:T(8,128)(2,1)} %w_ref.2), custom_call_target="tpu_custom_call" | custom-call | flops 1000 | bytes 1000 | tf_op jit(solution)/shard_map/b_strips/pallas_call | solution.py:86
  7.4 1.6 %collective-permute-start.1 = (bf16[512,1024]{1,0:T(8,128)(2,1)}, bf16[512,1024]{1,0:T(8,128)(2,1)S(1)}, u32[]{:S(2)}, u32[]{:S(2)}) collective-permute-start(bf16[512,1024]{1,0:T(8,128)(2,1)} %b_strips.3.refs_5_), channel_id=1, source_target_pairs={{0,4},{2,6},{4,0},{6,2},{8,12},{10,14},{12,8},{14,10},{1,5},{3,7},... | collective-permute-start | bytes 3145736 | tf_op jit(solution)/shard_map/ppermute | solution.py:561
  10.8 6.9 %masked_x.1.refs_0_ = bf16[512,4096]{1,0:T(8,128)(2,1)} custom-call(s32[1]{0:T(128)} %bitcast.9.first_ref, f32[8,1,4096]{2,1,0:T(1,128)} %reshape.17.mask_ref, bf16[512,4096]{1,0:T(8,128)(2,1)} %x_ref.1), custom_call_target="tpu_custom_call" | custom-call | flops 1000 | bytes 1000 | tf_op jit(solution)/shard_map/masked_x/pallas_call | solution.py:149
  17.7 3.2 %fusion = (bf16[128,4096]{1,0:T(8,128)(2,1)}, bf16[128,4096]{1,0:T(8,128)(2,1)}) fusion(bf16[512,4096]{1,0:T(8,128)(2,1)} %masked_x.1.refs_0_), kind=kLoop, calls=%fused_computation.4 | loop fusion | bytes 4194304 | tf_op jit(solution)/shard_map/slice | solution.py:576
  20.8 7.8 %collective-permute-done.refs_6_ = bf16[512,1024]{1,0:T(8,128)(2,1)} collective-permute-done((bf16[512,1024]{1,0:T(8,128)(2,1)}, bf16[512,1024]{1,0:T(8,128)(2,1)}, u32[]{:S(2)}, u32[]{:S(2)}) %collective-permute-start) | collective-permute-done | bytes 1048608 | tf_op jit(solution)/shard_map/ppermute | solution.py:561
  28.7 3.6 %collective-permute-done.1.refs_0_.refs_2_.refs_9_ = bf16[512,1024]{1,0:T(8,128)(2,1)S(1)} collective-permute-done((bf16[512,1024]{1,0:T(8,128)(2,1)}, bf16[512,1024]{1,0:T(8,128)(2,1)S(1)}, u32[]{:S(2)}, u32[]{:S(2)}) %collective-permute-start.1) | collective-permute-done | bytes 1048608 | tf_op jit(solution)/shard_map/ppermute | solution.py:561
  32.3 1.6 %collective-permute-start.2 = (bf16[512,1024]{1,0:T(8,128)(2,1)}, bf16[512,1024]{1,0:T(8,128)(2,1)S(1)}, u32[]{:S(2)}, u32[]{:S(2)}) collective-permute-start(bf16[512,1024]{1,0:T(8,128)(2,1)} %collective-permute-done.refs_6_), channel_id=1, source_target_pairs={{0,4},{2,6},{4,0},{6,2},{8,12},{10,14},{12,8},{14,10},{1,5},{3,7},... | collective-permute-start | bytes 3145736 | tf_op jit(solution)/shard_map/ppermute | solution.py:561
  33.9 1.7 %collective-permute-start.8 = (bf16[512,1024]{1,0:T(8,128)(2,1)}, bf16[512,1024]{1,0:T(8,128)(2,1)}, u32[]{:S(2)}, u32[]{:S(2)}) collective-permute-start(bf16[512,1024]{1,0:T(8,128)(2,1)} %collective-permute-done.refs_6_), channel_id=1, source_target_pairs={{4,8},{6,10},{8,4},{10,6},{5,9},{7,11},{9,5},{11,7},{20,24},{22,26... | collective-permute-start | bytes 3145736 | tf_op jit(solution)/shard_map/ppermute | solution.py:561
  36.0 1.5 collective-permute-start.4
  37.6 1.3 collective-permute-start.9
  39.0 19.6 %collective-permute-done.2.refs_1_.refs_3_.refs_10_ = bf16[512,1024]{1,0:T(8,128)(2,1)S(1)} collective-permute-done((bf16[512,1024]{1,0:T(8,128)(2,1)}, bf16[512,1024]{1,0:T(8,128)(2,1)S(1)}, u32[]{:S(2)}, u32[]{:S(2)}) %collective-permute-start.2) | collective-permute-done | bytes 1048608 | tf_op jit(solution)/shard_map/ppermute | solution.py:561
  58.6 3.3 %packed.4 = (bf16[512,1280]{1,0:T(8,128)(2,1)}, bf16[512,1024]{1,0:T(8,128)(2,1)}) custom-call(s32[2]{0:T(128)S(1)} %pad_add_fusion.1.meta_ref, bf16[512,1024]{1,0:T(8,128)(2,1)S(1)} %collective-permute-done.7.refs_0_.refs_7_, bf16[512,1024]{1,0:T(8,128)(2,1)} %collective-permute-done.8.refs_1_.refs_8_, ...), custom_call_target="tpu_custom_call" | custom-call | flops 1000 | bytes 1000 | tf_op jit(solution)/shard_map/packed/pallas_call | solution.py:129
  61.9 2.9 %collective-permute-done.9.refs_12_ = bf16[512,384]{1,0:T(8,128)(2,1)} collective-permute-done((bf16[512,384]{1,0:T(8,128)(2,1)S(1)}, bf16[512,384]{1,0:T(8,128)(2,1)}, u32[]{:S(2)}, u32[]{:S(2)}) %collective-permute-start.9) | collective-permute-done | bytes 393248 | tf_op jit(solution)/shard_map/ppermute | solution.py:561
  64.8 1.3 collective-permute-start.10
  66.1 1.6 %collective-permute-start.11 = (bf16[512,1024]{1,0:T(8,128)(2,1)}, bf16[512,1024]{1,0:T(8,128)(2,1)}, u32[]{:S(2)}, u32[]{:S(2)}) collective-permute-start(bf16[512,1024]{1,0:T(8,128)(2,1)} %get-tuple-element.45), channel_id=1, source_target_pairs={{4,8},{6,10},{8,4},{10,6},{5,9},{7,11},{9,5},{11,7},{20,24},{22,26... | collective-permute-start | bytes 3145736 | tf_op jit(solution)/shard_map/ppermute | solution.py:561
  68.9 12.9 %collective-permute-done.4.refs_2_ = bf16[128,4096]{1,0:T(8,128)(2,1)} collective-permute-done((bf16[128,4096]{1,0:T(8,128)(2,1)}, bf16[128,4096]{1,0:T(8,128)(2,1)}, u32[]{:S(2)}, u32[]{:S(2)}) %collective-permute-start.4) | collective-permute-done | bytes 1048608 | tf_op jit(solution)/shard_map/ppermute | solution.py:561
  83.0 1.3 collective-permute-start.12
  86.3 9.7 %collective-permute-done.10.refs_11_ = bf16[512,1280]{1,0:T(8,128)(2,1)} collective-permute-done((bf16[512,1280]{1,0:T(8,128)(2,1)}, bf16[512,1280]{1,0:T(8,128)(2,1)}, u32[]{:S(2)}, u32[]{:S(2)}) %collective-permute-start.10) | collective-permute-done | bytes 1310752 | tf_op jit(solution)/shard_map/ppermute | solution.py:561
  96.0 13.6 %whole_products.1.refs_5_ = f32[2,512,1024]{2,1,0:T(8,128)} custom-call(s32[14]{0:T(128)} %stack.137.meta_ref, bf16[512,4096]{1,0:T(8,128)(2,1)} %masked_x.1.refs_0_, bf16[128,4096]{1,0:T(8,128)(2,1)} %collective-permute-done.3.refs_1_, bf16[128,4096]{1,0:T(8,128)(2,1)} %collective-permute-done.4.refs_2_, bf16[128,4096]{1,0:T(8,128)(2,1)} %collective-permute-done.5.refs_3_, ...), custom_call_target="tpu_custom_call" | custom-call | flops 6000000000 | bytes 37748736 | tf_op jit(solution)/shard_map/whole_products/pallas_call | solution.py:277
  110.4 1.3 collective-permute-start.14
  112.3 5.7 %collective-permute-done.12.refs_7_ = bf16[512,1024]{1,0:T(8,128)(2,1)} collective-permute-done((bf16[512,1024]{1,0:T(8,128)(2,1)}, bf16[512,1024]{1,0:T(8,128)(2,1)}, u32[]{:S(2)}, u32[]{:S(2)}) %collective-permute-start.12) | collective-permute-done | bytes 1048608 | tf_op jit(solution)/shard_map/ppermute | solution.py:561
  118.0 6.0 %half_products.1 = (bf16[256,640]{1,0:T(8,128)(2,1)}, bf16[256,640]{1,0:T(8,128)(2,1)}, bf16[256,640]{1,0:T(8,128)(2,1)}, bf16[256,640]{1,0:T(8,128)(2,1)}, f32[2,512,384]{2,1,0:T(8,128)}) custom-call(s32[9]{0:T(128)} %stack.127.meta_ref, bf16[512,4096]{1,0:T(8,128)(2,1)} %masked_x.1.refs_0_, bf16[128,4096]{1,0:T(8,128)(2,1)} %collective-permute-done.3.refs_1_, ...), custom_call_target="tpu_custom_call" | custom-call | flops 1000 | bytes 1000 | tf_op jit(solution)/shard_map/half_products/pallas_call | solution.py:393
  124.1 1.5 collective-permute-start.19
  126.6 5.2 %collective-permute-done.14.refs_6_ = bf16[512,640]{1,0:T(8,128)(2,1)S(1)} collective-permute-done((bf16[512,640]{1,0:T(8,128)(2,1)S(1)}, bf16[512,640]{1,0:T(8,128)(2,1)S(1)}, u32[]{:S(2)}, u32[]{:S(2)}) %collective-permute-start.14) | collective-permute-done | bytes 655392 | tf_op jit(solution)/shard_map/ppermute | solution.py:561
  132.6 5.0 %rest_products.1 = (bf16[256,384]{1,0:T(8,128)(2,1)}, bf16[256,384]{1,0:T(8,128)(2,1)}, bf16[256,384]{1,0:T(8,128)(2,1)}, bf16[256,384]{1,0:T(8,128)(2,1)}) custom-call(s32[9]{0:T(128)} %stack.123.meta_ref, bf16[512,4096]{1,0:T(8,128)(2,1)} %masked_x.1.refs_0_, bf16[128,4096]{1,0:T(8,128)(2,1)} %collective-permute-done.3.refs_1_, ...), custom_call_target="tpu_custom_call" | custom-call | flops 1000 | bytes 1000 | tf_op jit(solution)/shard_map/rest_products/pallas_call | solution.py:473
  139.9 1.2 collective-permute-done.20.refs_3_
  141.0 2.0 %assembled.2.refs_4_ = bf16[256,4096]{1,0:T(8,128)(2,1)} custom-call(s32[2]{0:T(128)S(1)} %get-tuple-element.62.place_ref, f32[4,1,4096]{2,1,0:T(1,128)S(1)} %reshape.15.mask_ref, bf16[256,640]{1,0:T(8,128)(2,1)S(1)} %copy-done.4, bf16[256,640]{1,0:T(8,128)(2,1)S(1)} %collective-permute-done.15.refs_1_, ...), custom_call_target="tpu_custom_call" | custom-call | flops 1000 | bytes 1000 | tf_op jit(solution)/shard_map/assembled/pallas_call | solution.py:520
  143.0 3.1 %collective-permute-done.17.refs_2_ = bf16[256,384]{1,0:T(8,128)(2,1)S(1)} collective-permute-done((bf16[256,384]{1,0:T(8,128)(2,1)}, bf16[256,384]{1,0:T(8,128)(2,1)S(1)}, u32[]{:S(2)}, u32[]{:S(2)}) %collective-permute-start.17) | collective-permute-done | bytes 196640 | tf_op jit(solution)/shard_map/ppermute | solution.py:561
  146.2 3.3 %collective-permute-done.18.refs_3_ = bf16[256,384]{1,0:T(8,128)(2,1)S(1)} collective-permute-done((bf16[256,384]{1,0:T(8,128)(2,1)}, bf16[256,384]{1,0:T(8,128)(2,1)S(1)}, u32[]{:S(2)}, u32[]{:S(2)}) %collective-permute-start.18) | collective-permute-done | bytes 196640 | tf_op jit(solution)/shard_map/ppermute | solution.py:641
  150.4 1.6 %assembled.3 = bf16[256,4096]{1,0:T(8,128)(2,1)} custom-call(s32[2]{0:T(128)S(1)} %get-tuple-element.61.place_ref, f32[4,1,4096]{2,1,0:T(1,128)S(1)} %reshape.15.mask_ref, bf16[256,384]{1,0:T(8,128)(2,1)S(1)} %copy-done.5, bf16[256,384]{1,0:T(8,128)(2,1)S(1)} %collective-permute-done.16.refs_1_, ...), custom_call_target="tpu_custom_call", output_to_operand_aliasing={{}: (6, {})} | custom-call | flops 1000 | bytes 1000 | tf_op jit(solution)/shard_map/assembled/pallas_call | solution.py:520
  (53 shorter events, 12.9 us)
Async XLA Ops:
  0.0 9.8 %copy-start.7 = (s32[8,64]{1,0:T(8,128)S(1)}, s32[8,64]{1,0:T(8,128)}, u32[]{:S(2)}) copy-start(s32[8,64]{1,0:T(8,128)} %param.6) | copy-start | bytes 6148
  2.2 26.5 %collective-permute-start = (bf16[512,1024]{1,0:T(8,128)(2,1)}, bf16[512,1024]{1,0:T(8,128)(2,1)}, u32[]{:S(2)}, u32[]{:S(2)}) collective-permute-start(bf16[512,1024]{1,0:T(8,128)(2,1)} %b_strips.2), channel_id=1, source_target_pairs={{0,2},{2,0},{4,6},{6,4},{8,10},{10,8},{12,14},{14,12},{1,3},{3,1},... | collective-permute-start | bytes 3145736 | tf_op jit(solution)/shard_map/ppermute | solution.py:561
  7.4 24.9 %collective-permute-start.1 = (bf16[512,1024]{1,0:T(8,128)(2,1)}, bf16[512,1024]{1,0:T(8,128)(2,1)S(1)}, u32[]{:S(2)}, u32[]{:S(2)}) collective-permute-start(bf16[512,1024]{1,0:T(8,128)(2,1)} %b_strips.3.refs_5_), channel_id=1, source_target_pairs={{0,4},{2,6},{4,0},{6,2},{8,12},{10,14},{12,8},{14,10},{1,5},{3,7},... | collective-permute-start | bytes 3145736 | tf_op jit(solution)/shard_map/ppermute | solution.py:561
  9.1 28.5 %collective-permute-start.7 = (bf16[512,1024]{1,0:T(8,128)(2,1)}, bf16[512,1024]{1,0:T(8,128)(2,1)S(1)}, u32[]{:S(2)}, u32[]{:S(2)}) collective-permute-start(bf16[512,1024]{1,0:T(8,128)(2,1)} %b_strips.3.refs_5_), channel_id=1, source_target_pairs={{4,8},{6,10},{8,4},{10,6},{5,9},{7,11},{9,5},{11,7},{20,24},{22,26... | collective-permute-start | bytes 3145736 | tf_op jit(solution)/shard_map/ppermute | solution.py:561
  32.3 52.1 %copy-start.1 = (bf16[512,1024]{1,0:T(8,128)(2,1)}, bf16[512,1024]{1,0:T(8,128)(2,1)S(1)}, u32[]{:S(2)}) copy-start(bf16[512,1024]{1,0:T(8,128)(2,1)S(1)} %collective-permute-done.1.refs_0_.refs_2_.refs_9_) | copy-start | bytes 3145732
  32.3 26.3 %collective-permute-start.2 = (bf16[512,1024]{1,0:T(8,128)(2,1)}, bf16[512,1024]{1,0:T(8,128)(2,1)S(1)}, u32[]{:S(2)}, u32[]{:S(2)}) collective-permute-start(bf16[512,1024]{1,0:T(8,128)(2,1)} %collective-permute-done.refs_6_), channel_id=1, source_target_pairs={{0,4},{2,6},{4,0},{6,2},{8,12},{10,14},{12,8},{14,10},{1,5},{3,7},... | collective-permute-start | bytes 3145736 | tf_op jit(solution)/shard_map/ppermute | solution.py:561
  33.9 24.7 %collective-permute-start.8 = (bf16[512,1024]{1,0:T(8,128)(2,1)}, bf16[512,1024]{1,0:T(8,128)(2,1)}, u32[]{:S(2)}, u32[]{:S(2)}) collective-permute-start(bf16[512,1024]{1,0:T(8,128)(2,1)} %collective-permute-done.refs_6_), channel_id=1, source_target_pairs={{4,8},{6,10},{8,4},{10,6},{5,9},{7,11},{9,5},{11,7},{20,24},{22,26... | collective-permute-start | bytes 3145736 | tf_op jit(solution)/shard_map/ppermute | solution.py:561
  35.5 33.3 %collective-permute-start.3 = (bf16[128,4096]{1,0:T(8,128)(2,1)}, bf16[128,4096]{1,0:T(8,128)(2,1)}, u32[]{:S(2)}, u32[]{:S(2)}) collective-permute-start(bf16[128,4096]{1,0:T(8,128)(2,1)} %get-tuple-element.36), channel_id=1, source_target_pairs={{0,2},{2,0},{4,6},{6,4},{8,10},{10,8},{12,14},{14,12},{1,3},{3,1},... | collective-permute-start | bytes 3145736 | tf_op jit(solution)/shard_map/ppermute | solution.py:561
  36.0 45.7 %collective-permute-start.4 = (bf16[128,4096]{1,0:T(8,128)(2,1)}, bf16[128,4096]{1,0:T(8,128)(2,1)}, u32[]{:S(2)}, u32[]{:S(2)}) collective-permute-start(bf16[128,4096]{1,0:T(8,128)(2,1)} %get-tuple-element.37), channel_id=1, source_target_pairs={{0,2},{2,0},{4,6},{6,4},{8,10},{10,8},{12,14},{14,12},{1,3},{3,1},... | collective-permute-start | bytes 3145736 | tf_op jit(solution)/shard_map/ppermute | solution.py:561
  37.6 44.2 %copy-start.3 = (bf16[512,1024]{1,0:T(8,128)(2,1)}, bf16[512,1024]{1,0:T(8,128)(2,1)S(1)}, u32[]{:S(2)}) copy-start(bf16[512,1024]{1,0:T(8,128)(2,1)S(1)} %collective-permute-done.7.refs_0_.refs_7_) | copy-start | bytes 3145732
  37.6 27.2 %collective-permute-start.9 = (bf16[512,384]{1,0:T(8,128)(2,1)S(1)}, bf16[512,384]{1,0:T(8,128)(2,1)}, u32[]{:S(2)}, u32[]{:S(2)}) collective-permute-start(bf16[512,384]{1,0:T(8,128)(2,1)S(1)} %slice.14), channel_id=1, source_target_pairs={{4,0},{6,2},{8,12},{10,14},{5,1},{7,3},{9,13},{11,15},{20,16},{22,... | collective-permute-start | bytes 1179656 | tf_op jit(solution)/shard_map/ppermute | solution.py:561
  58.6 37.4 %copy-start.2 = (bf16[512,1024]{1,0:T(8,128)(2,1)}, bf16[512,1024]{1,0:T(8,128)(2,1)S(1)}, u32[]{:S(2)}) copy-start(bf16[512,1024]{1,0:T(8,128)(2,1)S(1)} %collective-permute-done.2.refs_1_.refs_3_.refs_10_) | copy-start | bytes 3145732
  64.8 31.2 %collective-permute-start.10 = (bf16[512,1280]{1,0:T(8,128)(2,1)}, bf16[512,1280]{1,0:T(8,128)(2,1)}, u32[]{:S(2)}, u32[]{:S(2)}) collective-permute-start(bf16[512,1280]{1,0:T(8,128)(2,1)} %get-tuple-element.42), channel_id=1, source_target_pairs={{4,0},{6,2},{8,12},{10,14},{5,1},{7,3},{9,13},{11,15},{20,16},{22,... | collective-permute-start | bytes 3932168 | tf_op jit(solution)/shard_map/ppermute | solution.py:561
  66.1 16.9 %collective-permute-start.11 = (bf16[512,1024]{1,0:T(8,128)(2,1)}, bf16[512,1024]{1,0:T(8,128)(2,1)}, u32[]{:S(2)}, u32[]{:S(2)}) collective-permute-start(bf16[512,1024]{1,0:T(8,128)(2,1)} %get-tuple-element.45), channel_id=1, source_target_pairs={{4,8},{6,10},{8,4},{10,6},{5,9},{7,11},{9,5},{11,7},{20,24},{22,26... | collective-permute-start | bytes 3145736 | tf_op jit(solution)/shard_map/ppermute | solution.py:561
  81.8 3.3 %collective-permute-start.5 = (bf16[128,4096]{1,0:T(8,128)(2,1)}, bf16[128,4096]{1,0:T(8,128)(2,1)}, u32[]{:S(2)}, u32[]{:S(2)}) collective-permute-start(bf16[128,4096]{1,0:T(8,128)(2,1)} %collective-permute-done.3.refs_1_), channel_id=1, source_target_pairs={{0,1},{1,0},{2,3},{3,2},{4,5},{5,4},{6,7},{7,6},{8,9},{9,8},{10,11... | collective-permute-start | bytes 3145736 | tf_op jit(solution)/shard_map/ppermute | solution.py:604
  81.8 4.5 %collective-permute-start.6 = (bf16[128,4096]{1,0:T(8,128)(2,1)}, bf16[128,4096]{1,0:T(8,128)(2,1)}, u32[]{:S(2)}, u32[]{:S(2)}) collective-permute-start(bf16[128,4096]{1,0:T(8,128)(2,1)} %collective-permute-done.4.refs_2_), channel_id=1, source_target_pairs={{0,1},{1,0},{2,3},{3,2},{4,5},{5,4},{6,7},{7,6},{8,9},{9,8},{10,11... | collective-permute-start | bytes 3145736 | tf_op jit(solution)/shard_map/ppermute | solution.py:604
  82.3 27.4 %collective-permute-start.13 = (bf16[512,1024]{1,0:T(8,128)(2,1)}, bf16[512,1024]{1,0:T(8,128)(2,1)S(1)}, u32[]{:S(2)}, u32[]{:S(2)}) collective-permute-start(bf16[512,1024]{1,0:T(8,128)(2,1)} %packed.3), channel_id=1, source_target_pairs={{4,8},{6,10},{8,4},{10,6},{5,9},{7,11},{9,5},{11,7},{20,24},{22,26... | collective-permute-start | bytes 3145736 | tf_op jit(solution)/shard_map/ppermute | solution.py:561
  83.0 35.0 %collective-permute-start.12 = (bf16[512,1024]{1,0:T(8,128)(2,1)}, bf16[512,1024]{1,0:T(8,128)(2,1)}, u32[]{:S(2)}, u32[]{:S(2)}) collective-permute-start(bf16[512,1024]{1,0:T(8,128)(2,1)} %collective-permute-done.11.refs_6_), channel_id=1, source_target_pairs={{4,0},{6,2},{8,12},{10,14},{5,1},{7,3},{9,13},{11,15},{20,16},{22,... | collective-permute-start | bytes 3145736 | tf_op jit(solution)/shard_map/ppermute | solution.py:561
  109.7 8.4 %copy-start = (bf16[512,1024]{1,0:T(8,128)(2,1)}, bf16[512,1024]{1,0:T(8,128)(2,1)S(1)}, u32[]{:S(2)}) copy-start(bf16[512,1024]{1,0:T(8,128)(2,1)S(1)} %collective-permute-done.13.refs_8_.refs_0_) | copy-start | bytes 3145732
  110.4 21.4 %collective-permute-start.14 = (bf16[512,640]{1,0:T(8,128)(2,1)S(1)}, bf16[512,640]{1,0:T(8,128)(2,1)S(1)}, u32[]{:S(2)}, u32[]{:S(2)}) collective-permute-start(bf16[512,640]{1,0:T(8,128)(2,1)S(1)} %packed.5), channel_id=1, source_target_pairs={{4,0},{6,2},{8,12},{10,14},{5,1},{7,3},{9,13},{11,15},{20,16},{22,... | collective-permute-start | bytes 1966088 | tf_op jit(solution)/shard_map/ppermute | solution.py:561
  124.1 7.7 %collective-permute-start.15 = (bf16[256,640]{1,0:T(8,128)(2,1)}, bf16[256,640]{1,0:T(8,128)(2,1)S(1)}, u32[]{:S(2)}, u32[]{:S(2)}) collective-permute-start(bf16[256,640]{1,0:T(8,128)(2,1)} %get-tuple-element.49), channel_id=1, source_target_pairs={{0,1},{1,0},{2,3},{3,2},{4,5},{5,4},{6,7},{7,6},{8,9},{9,8},{10,11... | collective-permute-start | bytes 983048 | tf_op jit(solution)/shard_map/ppermute | solution.py:639
  124.1 15.7 %collective-permute-start.19 = (bf16[256,640]{1,0:T(8,128)(2,1)}, bf16[256,640]{1,0:T(8,128)(2,1)S(1)}, u32[]{:S(2)}, u32[]{:S(2)}) collective-permute-start(bf16[256,640]{1,0:T(8,128)(2,1)} %get-tuple-element.57), channel_id=1, source_target_pairs={{0,2},{2,0},{4,6},{6,4},{8,10},{10,8},{12,14},{14,12},{1,3},{3,1},... | collective-permute-start | bytes 983048 | tf_op jit(solution)/shard_map/ppermute | solution.py:561
  125.7 15.4 %collective-permute-start.20 = (bf16[256,640]{1,0:T(8,128)(2,1)}, bf16[256,640]{1,0:T(8,128)(2,1)S(1)}, u32[]{:S(2)}, u32[]{:S(2)}) collective-permute-start(bf16[256,640]{1,0:T(8,128)(2,1)} %get-tuple-element.58), channel_id=1, source_target_pairs={{0,3},{1,2},{2,1},{3,0},{4,7},{5,6},{6,5},{7,4},{8,11},{9,10},{10,... | collective-permute-start | bytes 983048 | tf_op jit(solution)/shard_map/ppermute | solution.py:641
  131.8 0.8 copy-start.6
  132.6 6.9 %copy-start.8 = (s32[4,64]{1,0:T(4,128)S(1)}, s32[4,64]{1,0:T(4,128)}, u32[]{:S(2)}) copy-start(s32[4,64]{1,0:T(4,128)} %param.7) | copy-start | bytes 3076
  132.6 8.4 %copy-start.4 = (bf16[256,640]{1,0:T(8,128)(2,1)S(1)}, bf16[256,640]{1,0:T(8,128)(2,1)}, u32[]{:S(2)}) copy-start(bf16[256,640]{1,0:T(8,128)(2,1)} %get-tuple-element.55.refs_0_) | copy-start | bytes 983044
  137.6 5.5 %collective-permute-start.16 = (bf16[256,384]{1,0:T(8,128)(2,1)}, bf16[256,384]{1,0:T(8,128)(2,1)S(1)}, u32[]{:S(2)}, u32[]{:S(2)}) collective-permute-start(bf16[256,384]{1,0:T(8,128)(2,1)} %get-tuple-element.52), channel_id=1, source_target_pairs={{0,1},{1,0},{2,3},{3,2},{4,5},{5,4},{6,7},{7,6},{8,9},{9,8},{10,11... | collective-permute-start | bytes 589832 | tf_op jit(solution)/shard_map/ppermute | solution.py:639
  137.7 8.5 %collective-permute-start.17 = (bf16[256,384]{1,0:T(8,128)(2,1)}, bf16[256,384]{1,0:T(8,128)(2,1)S(1)}, u32[]{:S(2)}, u32[]{:S(2)}) collective-permute-start(bf16[256,384]{1,0:T(8,128)(2,1)} %get-tuple-element.53), channel_id=1, source_target_pairs={{0,2},{2,0},{4,6},{6,4},{8,10},{10,8},{12,14},{14,12},{1,3},{3,1},... | collective-permute-start | bytes 589832 | tf_op jit(solution)/shard_map/ppermute | solution.py:561
  138.7 10.8 %collective-permute-start.18 = (bf16[256,384]{1,0:T(8,128)(2,1)}, bf16[256,384]{1,0:T(8,128)(2,1)S(1)}, u32[]{:S(2)}, u32[]{:S(2)}) collective-permute-start(bf16[256,384]{1,0:T(8,128)(2,1)} %get-tuple-element.54), channel_id=1, source_target_pairs={{0,3},{1,2},{2,1},{3,0},{4,7},{5,6},{6,5},{7,4},{8,11},{9,10},{10,... | collective-permute-start | bytes 589832 | tf_op jit(solution)/shard_map/ppermute | solution.py:641
  149.5 0.9 copy-start.5

commit v15 on v14

--- a/solution.py
+++ b/solution.py
@@ -580,16 +580,16 @@
     cross_b = line(own_b, cross)
     x_across = [line(part, across) for part in x_mine]
 
-    mid_a = line(cross_a[:, 5 * LANES :], outward)
+    mid_a = line(cross_a[:, 6 * LANES :], outward)
     mid_b, fwd_first = packed(
         [y, first_out],
         [cross_a, cross_b, swap_a, swap_b],
-        [10, 8],
+        [11, 8],
         [
             (0, 0, 3, 0, 0, (0, 0)),
             (1, 0, 3, 0, 0, (0, 1)),
-            (0, 3, 2, 0, 3, None),
-            (1, 3, 5, 0, 5, None),
+            (0, 3, 3, 0, 3, None),
+            (1, 3, 5, 0, 6, None),
             (2, (1,), 4, 1, 0, None),
             (3, (1,), 4, 1, 4, None),
         ],
@@ -617,8 +617,8 @@
         (1, [(1, 0, 8, 0, 1)]),
         (2, [(4, 0, 8, 0, 2)]),
         (3, [(5, 0, 8, 0, 3)]),
-        (4, [(6, 0, 3, 0, None), (6, 3, 2, 3, 4), (7, 0, 3, 5, 4)]),
-        (5, [(6, 5, 5, 3, 5)]),
+        (4, [(6, 0, 3, 0, None), (6, 3, 3, 3, 4), (7, 0, 2, 6, 4)]),
+        (5, [(6, 6, 5, 3, 5)]),
     ]
     total = whole_products(meta, xs, [own_a, own_b, cross_a, cross_b, swap_a, swap_b, mid_b, mid_a], plan)
     last_at = jnp.where(left, 2, 0)

time: 155 us -> 156 us (level)
  waiting for transfers between devices: 76.3 us -> 78.1 us
    ppermute x2, waiting for transfers between devices: 4.5 us -> 6.34 us  [exchanged(): lax.ppermute(pieces[3], ('grid', 'depth'), opposite)]
  transfers between devices with their start and end apart: 21 -> 21, of which waited for: 12 -> 11; matrix products, arithmetic and copies ran while one was open for 4% -> 4% of each run, Pallas kernels for 27% -> 26%
where the time goes in v15:
time: 156 us; the launch traced here: 154 us
  waiting for transfers between devices  78.1 us (50%)
  Pallas kernels  44.5 us (29%)
  starting transfers between devices  22.5 us (14%)
  local copies, waits for them, and re-layouts  8.05 us (5%)
    ppermute x15, waiting for transfers between devices, line(): return lax.ppermute(value, 'grid', pairs)  70.5 us
    ppermute x15, starting transfers between devices, line(): return lax.ppermute(value, 'grid', pairs)  20.7 us
    pallas_call x1, Pallas kernels, whole_products(): pl.pallas_call(functools.partial(whole_kernel, plan), out_shape=jax.Shape...  13.6 us
    pallas_call x1, Pallas kernels, masked_x(): pl.pallas_call(mask_kernel, grid_spec=pltpu.PrefetchScalarGridSpec(num_sc...  6.87 us
    ppermute x2, waiting for transfers between devices, exchanged(): lax.ppermute(pieces[3], ('grid', 'depth'), opposite)  6.34 us
    pallas_call x1, Pallas kernels, half_products(): pl.pallas_call(half_kernel, out_shape=[jax.ShapeDtypeStruct((rows, n_done...  5.98 us
    pallas_call x3, Pallas kernels, packed(): pl.pallas_call(functools.partial(pack_kernel, plan, len(sources)), out_sh...  5.15 us
    pallas_call x1, Pallas kernels, rest_products(): pl.pallas_call(rest_kernel, out_shape=[jax.ShapeDtypeStruct((rows, width)...  4.92 us
  transfers between devices with their start and end apart: 21, of which 11 were waited for; matrix products, arithmetic and copies ran while one was open for 4% of the time, Pallas kernels for 26%

profile of v15, /device:TPU:0, one launch (start us, length us, event | category | flops | bytes accessed | tf_op | source)
XLA Modules:
  0.0 153.9 jit_solution(11130045753460435484)
XLA Ops:
  0.0 2.2 %b_strips.2 = bf16[512,1024]{1,0:T(8,128)(2,1)} custom-call(s32[1]{0:T(128)} %bitcast.11.quarter_ref, bf16[512,4096]{1,0:T(8,128)(2,1)} %w_ref.2), custom_call_target="tpu_custom_call" | custom-call | flops 1000 | bytes 1000 | tf_op jit(solution)/shard_map/b_strips/pallas_call | solution.py:86
  2.2 3.0 %collective-permute-start = (bf16[512,1024]{1,0:T(8,128)(2,1)}, bf16[512,1024]{1,0:T(8,128)(2,1)}, u32[]{:S(2)}, u32[]{:S(2)}) collective-permute-start(bf16[512,1024]{1,0:T(8,128)(2,1)} %b_strips.2), channel_id=1, source_target_pairs={{0,2},{2,0},{4,6},{6,4},{8,10},{10,8},{12,14},{14,12},{1,3},{3,1},... | collective-permute-start | bytes 3145736 | tf_op jit(solution)/shard_map/ppermute | solution.py:561
  5.2 2.2 %b_strips.3.refs_5_ = bf16[512,1024]{1,0:T(8,128)(2,1)} custom-call(s32[1]{0:T(128)} %bitcast.quarter_ref, bf16[512,4096]{1,0:T(8,128)(2,1)} %w_ref.2), custom_call_target="tpu_custom_call" | custom-call | flops 1000 | bytes 1000 | tf_op jit(solution)/shard_map/b_strips/pallas_call | solution.py:86
  7.4 1.6 %collective-permute-start.1 = (bf16[512,1024]{1,0:T(8,128)(2,1)}, bf16[512,1024]{1,0:T(8,128)(2,1)S(1)}, u32[]{:S(2)}, u32[]{:S(2)}) collective-permute-start(bf16[512,1024]{1,0:T(8,128)(2,1)} %b_strips.3.refs_5_), channel_id=1, source_target_pairs={{0,4},{2,6},{4,0},{6,2},{8,12},{10,14},{12,8},{14,10},{1,5},{3,7},... | collective-permute-start | bytes 3145736 | tf_op jit(solution)/shard_map/ppermute | solution.py:561
  10.8 6.9 %masked_x.1.refs_0_ = bf16[512,4096]{1,0:T(8,128)(2,1)} custom-call(s32[1]{0:T(128)} %bitcast.9.first_ref, f32[8,1,4096]{2,1,0:T(1,128)} %reshape.17.mask_ref, bf16[512,4096]{1,0:T(8,128)(2,1)} %x_ref.1), custom_call_target="tpu_custom_call" | custom-call | flops 1000 | bytes 1000 | tf_op jit(solution)/shard_map/masked_x/pallas_call | solution.py:149
  17.6 3.2 %fusion = (bf16[128,4096]{1,0:T(8,128)(2,1)}, bf16[128,4096]{1,0:T(8,128)(2,1)}) fusion(bf16[512,4096]{1,0:T(8,128)(2,1)} %masked_x.1.refs_0_), kind=kLoop, calls=%fused_computation.4 | loop fusion | bytes 4194304 | tf_op jit(solution)/shard_map/slice | solution.py:576
  20.8 7.9 %collective-permute-done.refs_6_ = bf16[512,1024]{1,0:T(8,128)(2,1)} collective-permute-done((bf16[512,1024]{1,0:T(8,128)(2,1)}, bf16[512,1024]{1,0:T(8,128)(2,1)}, u32[]{:S(2)}, u32[]{:S(2)}) %collective-permute-start) | collective-permute-done | bytes 1048608 | tf_op jit(solution)/shard_map/ppermute | solution.py:561
  28.7 3.6 %collective-permute-done.1.refs_0_.refs_2_.refs_9_ = bf16[512,1024]{1,0:T(8,128)(2,1)S(1)} collective-permute-done((bf16[512,1024]{1,0:T(8,128)(2,1)}, bf16[512,1024]{1,0:T(8,128)(2,1)S(1)}, u32[]{:S(2)}, u32[]{:S(2)}) %collective-permute-start.1) | collective-permute-done | bytes 1048608 | tf_op jit(solution)/shard_map/ppermute | solution.py:561
  32.3 1.6 %collective-permute-start.2 = (bf16[512,1024]{1,0:T(8,128)(2,1)}, bf16[512,1024]{1,0:T(8,128)(2,1)S(1)}, u32[]{:S(2)}, u32[]{:S(2)}) collective-permute-start(bf16[512,1024]{1,0:T(8,128)(2,1)} %collective-permute-done.refs_6_), channel_id=1, source_target_pairs={{0,4},{2,6},{4,0},{6,2},{8,12},{10,14},{12,8},{14,10},{1,5},{3,7},... | collective-permute-start | bytes 3145736 | tf_op jit(solution)/shard_map/ppermute | solution.py:561
  33.9 1.6 %collective-permute-start.8 = (bf16[512,1024]{1,0:T(8,128)(2,1)}, bf16[512,1024]{1,0:T(8,128)(2,1)}, u32[]{:S(2)}, u32[]{:S(2)}) collective-permute-start(bf16[512,1024]{1,0:T(8,128)(2,1)} %collective-permute-done.refs_6_), channel_id=1, source_target_pairs={{4,8},{6,10},{8,4},{10,6},{5,9},{7,11},{9,5},{11,7},{20,24},{22,26... | collective-permute-start | bytes 3145736 | tf_op jit(solution)/shard_map/ppermute | solution.py:561
  36.0 1.5 collective-permute-start.4
  37.6 1.3 collective-permute-start.9
  39.0 19.6 %collective-permute-done.2.refs_1_.refs_3_.refs_10_ = bf16[512,1024]{1,0:T(8,128)(2,1)S(1)} collective-permute-done((bf16[512,1024]{1,0:T(8,128)(2,1)}, bf16[512,1024]{1,0:T(8,128)(2,1)S(1)}, u32[]{:S(2)}, u32[]{:S(2)}) %collective-permute-start.2) | collective-permute-done | bytes 1048608 | tf_op jit(solution)/shard_map/ppermute | solution.py:561
  58.6 3.3 %packed.4 = (bf16[512,1408]{1,0:T(8,128)(2,1)}, bf16[512,1024]{1,0:T(8,128)(2,1)}) custom-call(s32[2]{0:T(128)S(1)} %pad_add_fusion.1.meta_ref, bf16[512,1024]{1,0:T(8,128)(2,1)S(1)} %collective-permute-done.7.refs_0_.refs_7_, bf16[512,1024]{1,0:T(8,128)(2,1)} %collective-permute-done.8.refs_1_.refs_8_, ...), custom_call_target="tpu_custom_call" | custom-call | flops 1000 | bytes 1000 | tf_op jit(solution)/shard_map/packed/pallas_call | solution.py:129
  61.9 1.3 collective-permute-start.10
  63.2 1.6 %collective-permute-start.11 = (bf16[512,1024]{1,0:T(8,128)(2,1)}, bf16[512,1024]{1,0:T(8,128)(2,1)}, u32[]{:S(2)}, u32[]{:S(2)}) collective-permute-start(bf16[512,1024]{1,0:T(8,128)(2,1)} %get-tuple-element.45), channel_id=1, source_target_pairs={{4,8},{6,10},{8,4},{10,6},{5,9},{7,11},{9,5},{11,7},{20,24},{22,26... | collective-permute-start | bytes 3145736 | tf_op jit(solution)/shard_map/ppermute | solution.py:561
  66.0 15.7 %collective-permute-done.4.refs_2_ = bf16[128,4096]{1,0:T(8,128)(2,1)} collective-permute-done((bf16[128,4096]{1,0:T(8,128)(2,1)}, bf16[128,4096]{1,0:T(8,128)(2,1)}, u32[]{:S(2)}, u32[]{:S(2)}) %collective-permute-start.4) | collective-permute-done | bytes 1048608 | tf_op jit(solution)/shard_map/ppermute | solution.py:561
  83.0 1.3 collective-permute-start.12
  85.0 1.2 collective-permute-done.6.refs_4_
  86.2 12.4 %collective-permute-done.10.refs_11_ = bf16[512,1408]{1,0:T(8,128)(2,1)} collective-permute-done((bf16[512,1408]{1,0:T(8,128)(2,1)}, bf16[512,1408]{1,0:T(8,128)(2,1)}, u32[]{:S(2)}, u32[]{:S(2)}) %collective-permute-start.10) | collective-permute-done | bytes 1441824 | tf_op jit(solution)/shard_map/ppermute | solution.py:561
  98.7 13.6 %whole_products.1.refs_5_ = f32[2,512,1024]{2,1,0:T(8,128)} custom-call(s32[14]{0:T(128)} %stack.137.meta_ref, bf16[512,4096]{1,0:T(8,128)(2,1)} %masked_x.1.refs_0_, bf16[128,4096]{1,0:T(8,128)(2,1)} %collective-permute-done.3.refs_1_, bf16[128,4096]{1,0:T(8,128)(2,1)} %collective-permute-done.4.refs_2_, bf16[128,4096]{1,0:T(8,128)(2,1)} %collective-permute-done.5.refs_3_, ...), custom_call_target="tpu_custom_call" | custom-call | flops 6000000000 | bytes 37748736 | tf_op jit(solution)/shard_map/whole_products/pallas_call | solution.py:277
  113.1 1.3 collective-permute-start.14
  115.1 4.8 %collective-permute-done.12.refs_7_ = bf16[512,1024]{1,0:T(8,128)(2,1)} collective-permute-done((bf16[512,1024]{1,0:T(8,128)(2,1)}, bf16[512,1024]{1,0:T(8,128)(2,1)}, u32[]{:S(2)}, u32[]{:S(2)}) %collective-permute-start.12) | collective-permute-done | bytes 1048608 | tf_op jit(solution)/shard_map/ppermute | solution.py:561
  119.9 6.0 %half_products.1 = (bf16[256,640]{1,0:T(8,128)(2,1)}, bf16[256,640]{1,0:T(8,128)(2,1)}, bf16[256,640]{1,0:T(8,128)(2,1)}, bf16[256,640]{1,0:T(8,128)(2,1)}, f32[2,512,384]{2,1,0:T(8,128)}) custom-call(s32[9]{0:T(128)} %stack.127.meta_ref, bf16[512,4096]{1,0:T(8,128)(2,1)} %masked_x.1.refs_0_, bf16[128,4096]{1,0:T(8,128)(2,1)} %collective-permute-done.3.refs_1_, ...), custom_call_target="tpu_custom_call" | custom-call | flops 1000 | bytes 1000 | tf_op jit(solution)/shard_map/half_products/pallas_call | solution.py:393
  125.9 1.5 collective-permute-start.19
  128.4 3.4 %collective-permute-done.14.refs_6_ = bf16[512,640]{1,0:T(8,128)(2,1)S(1)} collective-permute-done((bf16[512,640]{1,0:T(8,128)(2,1)S(1)}, bf16[512,640]{1,0:T(8,128)(2,1)S(1)}, u32[]{:S(2)}, u32[]{:S(2)}) %collective-permute-start.14) | collective-permute-done | bytes 655392 | tf_op jit(solution)/shard_map/ppermute | solution.py:561
  132.6 4.9 %rest_products.1 = (bf16[256,384]{1,0:T(8,128)(2,1)}, bf16[256,384]{1,0:T(8,128)(2,1)}, bf16[256,384]{1,0:T(8,128)(2,1)}, bf16[256,384]{1,0:T(8,128)(2,1)}) custom-call(s32[9]{0:T(128)} %stack.123.meta_ref, bf16[512,4096]{1,0:T(8,128)(2,1)} %masked_x.1.refs_0_, bf16[128,4096]{1,0:T(8,128)(2,1)} %collective-permute-done.3.refs_1_, ...), custom_call_target="tpu_custom_call" | custom-call | flops 1000 | bytes 1000 | tf_op jit(solution)/shard_map/rest_products/pallas_call | solution.py:473
  139.8 3.0 %collective-permute-done.20.refs_3_ = bf16[256,640]{1,0:T(8,128)(2,1)S(1)} collective-permute-done((bf16[256,640]{1,0:T(8,128)(2,1)}, bf16[256,640]{1,0:T(8,128)(2,1)S(1)}, u32[]{:S(2)}, u32[]{:S(2)}) %collective-permute-start.20) | collective-permute-done | bytes 327712 | tf_op jit(solution)/shard_map/ppermute | solution.py:641
  142.9 2.0 %assembled.2.refs_4_ = bf16[256,4096]{1,0:T(8,128)(2,1)} custom-call(s32[2]{0:T(128)S(1)} %get-tuple-element.62.place_ref, f32[4,1,4096]{2,1,0:T(1,128)S(1)} %reshape.15.mask_ref, bf16[256,640]{1,0:T(8,128)(2,1)S(1)} %copy-done.4, bf16[256,640]{1,0:T(8,128)(2,1)S(1)} %collective-permute-done.15.refs_1_, ...), custom_call_target="tpu_custom_call" | custom-call | flops 1000 | bytes 1000 | tf_op jit(solution)/shard_map/assembled/pallas_call | solution.py:520
  144.9 3.1 %collective-permute-done.17.refs_2_ = bf16[256,384]{1,0:T(8,128)(2,1)S(1)} collective-permute-done((bf16[256,384]{1,0:T(8,128)(2,1)}, bf16[256,384]{1,0:T(8,128)(2,1)S(1)}, u32[]{:S(2)}, u32[]{:S(2)}) %collective-permute-start.17) | collective-permute-done | bytes 196640 | tf_op jit(solution)/shard_map/ppermute | solution.py:561
  148.0 3.3 %collective-permute-done.18.refs_3_ = bf16[256,384]{1,0:T(8,128)(2,1)S(1)} collective-permute-done((bf16[256,384]{1,0:T(8,128)(2,1)}, bf16[256,384]{1,0:T(8,128)(2,1)S(1)}, u32[]{:S(2)}, u32[]{:S(2)}) %collective-permute-start.18) | collective-permute-done | bytes 196640 | tf_op jit(solution)/shard_map/ppermute | solution.py:641
  152.2 1.6 %assembled.3 = bf16[256,4096]{1,0:T(8,128)(2,1)} custom-call(s32[2]{0:T(128)S(1)} %get-tuple-element.61.place_ref, f32[4,1,4096]{2,1,0:T(1,128)S(1)} %reshape.15.mask_ref, bf16[256,384]{1,0:T(8,128)(2,1)S(1)} %copy-done.5, bf16[256,384]{1,0:T(8,128)(2,1)S(1)} %collective-permute-done.16.refs_1_, ...), custom_call_target="tpu_custom_call", output_to_operand_aliasing={{}: (6, {})} | custom-call | flops 1000 | bytes 1000 | tf_op jit(solution)/shard_map/assembled/pallas_call | solution.py:520
  (53 shorter events, 11.8 us)
Async XLA Ops:
  0.0 9.8 %copy-start.7 = (s32[8,64]{1,0:T(8,128)S(1)}, s32[8,64]{1,0:T(8,128)}, u32[]{:S(2)}) copy-start(s32[8,64]{1,0:T(8,128)} %param.6) | copy-start | bytes 6148
  2.2 26.5 %collective-permute-start = (bf16[512,1024]{1,0:T(8,128)(2,1)}, bf16[512,1024]{1,0:T(8,128)(2,1)}, u32[]{:S(2)}, u32[]{:S(2)}) collective-permute-start(bf16[512,1024]{1,0:T(8,128)(2,1)} %b_strips.2), channel_id=1, source_target_pairs={{0,2},{2,0},{4,6},{6,4},{8,10},{10,8},{12,14},{14,12},{1,3},{3,1},... | collective-permute-start | bytes 3145736 | tf_op jit(solution)/shard_map/ppermute | solution.py:561
  7.4 24.9 %collective-permute-start.1 = (bf16[512,1024]{1,0:T(8,128)(2,1)}, bf16[512,1024]{1,0:T(8,128)(2,1)S(1)}, u32[]{:S(2)}, u32[]{:S(2)}) collective-permute-start(bf16[512,1024]{1,0:T(8,128)(2,1)} %b_strips.3.refs_5_), channel_id=1, source_target_pairs={{0,4},{2,6},{4,0},{6,2},{8,12},{10,14},{12,8},{14,10},{1,5},{3,7},... | collective-permute-start | bytes 3145736 | tf_op jit(solution)/shard_map/ppermute | solution.py:561
  9.0 28.5 %collective-permute-start.7 = (bf16[512,1024]{1,0:T(8,128)(2,1)}, bf16[512,1024]{1,0:T(8,128)(2,1)S(1)}, u32[]{:S(2)}, u32[]{:S(2)}) collective-permute-start(bf16[512,1024]{1,0:T(8,128)(2,1)} %b_strips.3.refs_5_), channel_id=1, source_target_pairs={{4,8},{6,10},{8,4},{10,6},{5,9},{7,11},{9,5},{11,7},{20,24},{22,26... | collective-permute-start | bytes 3145736 | tf_op jit(solution)/shard_map/ppermute | solution.py:561
  32.3 66.4 %copy-start.1 = (bf16[512,1024]{1,0:T(8,128)(2,1)}, bf16[512,1024]{1,0:T(8,128)(2,1)S(1)}, u32[]{:S(2)}) copy-start(bf16[512,1024]{1,0:T(8,128)(2,1)S(1)} %collective-permute-done.1.refs_0_.refs_2_.refs_9_) | copy-start | bytes 3145732
  32.3 26.3 %collective-permute-start.2 = (bf16[512,1024]{1,0:T(8,128)(2,1)}, bf16[512,1024]{1,0:T(8,128)(2,1)S(1)}, u32[]{:S(2)}, u32[]{:S(2)}) collective-permute-start(bf16[512,1024]{1,0:T(8,128)(2,1)} %collective-permute-done.refs_6_), channel_id=1, source_target_pairs={{0,4},{2,6},{4,0},{6,2},{8,12},{10,14},{12,8},{14,10},{1,5},{3,7},... | collective-permute-start | bytes 3145736 | tf_op jit(solution)/shard_map/ppermute | solution.py:561
  33.9 24.7 %collective-permute-start.8 = (bf16[512,1024]{1,0:T(8,128)(2,1)}, bf16[512,1024]{1,0:T(8,128)(2,1)}, u32[]{:S(2)}, u32[]{:S(2)}) collective-permute-start(bf16[512,1024]{1,0:T(8,128)(2,1)} %collective-permute-done.refs_6_), channel_id=1, source_target_pairs={{4,8},{6,10},{8,4},{10,6},{5,9},{7,11},{9,5},{11,7},{20,24},{22,26... | collective-permute-start | bytes 3145736 | tf_op jit(solution)/shard_map/ppermute | solution.py:561
  35.5 30.5 %collective-permute-start.3 = (bf16[128,4096]{1,0:T(8,128)(2,1)}, bf16[128,4096]{1,0:T(8,128)(2,1)}, u32[]{:S(2)}, u32[]{:S(2)}) collective-permute-start(bf16[128,4096]{1,0:T(8,128)(2,1)} %get-tuple-element.36), channel_id=1, source_target_pairs={{0,2},{2,0},{4,6},{6,4},{8,10},{10,8},{12,14},{14,12},{1,3},{3,1},... | collective-permute-start | bytes 3145736 | tf_op jit(solution)/shard_map/ppermute | solution.py:561
  36.0 45.7 %collective-permute-start.4 = (bf16[128,4096]{1,0:T(8,128)(2,1)}, bf16[128,4096]{1,0:T(8,128)(2,1)}, u32[]{:S(2)}, u32[]{:S(2)}) collective-permute-start(bf16[128,4096]{1,0:T(8,128)(2,1)} %get-tuple-element.37), channel_id=1, source_target_pairs={{0,2},{2,0},{4,6},{6,4},{8,10},{10,8},{12,14},{14,12},{1,3},{3,1},... | collective-permute-start | bytes 3145736 | tf_op jit(solution)/shard_map/ppermute | solution.py:561
  37.5 44.2 %copy-start.3 = (bf16[512,1024]{1,0:T(8,128)(2,1)}, bf16[512,1024]{1,0:T(8,128)(2,1)S(1)}, u32[]{:S(2)}) copy-start(bf16[512,1024]{1,0:T(8,128)(2,1)S(1)} %collective-permute-done.7.refs_0_.refs_7_) | copy-start | bytes 3145732
  37.6 24.4 %collective-permute-start.9 = (bf16[512,256]{1,0:T(8,128)(2,1)S(1)}, bf16[512,256]{1,0:T(8,128)(2,1)}, u32[]{:S(2)}, u32[]{:S(2)}) collective-permute-start(bf16[512,256]{1,0:T(8,128)(2,1)S(1)} %slice.14), channel_id=1, source_target_pairs={{4,0},{6,2},{8,12},{10,14},{5,1},{7,3},{9,13},{11,15},{20,16},{22,... | collective-permute-start | bytes 786440 | tf_op jit(solution)/shard_map/ppermute | solution.py:561
  58.6 40.1 %copy-start.2 = (bf16[512,1024]{1,0:T(8,128)(2,1)}, bf16[512,1024]{1,0:T(8,128)(2,1)S(1)}, u32[]{:S(2)}) copy-start(bf16[512,1024]{1,0:T(8,128)(2,1)S(1)} %collective-permute-done.2.refs_1_.refs_3_.refs_10_) | copy-start | bytes 3145732
  61.9 36.7 %collective-permute-start.10 = (bf16[512,1408]{1,0:T(8,128)(2,1)}, bf16[512,1408]{1,0:T(8,128)(2,1)}, u32[]{:S(2)}, u32[]{:S(2)}) collective-permute-start(bf16[512,1408]{1,0:T(8,128)(2,1)} %get-tuple-element.42), channel_id=1, source_target_pairs={{4,0},{6,2},{8,12},{10,14},{5,1},{7,3},{9,13},{11,15},{20,16},{22,... | collective-permute-start | bytes 4325384 | tf_op jit(solution)/shard_map/ppermute | solution.py:561
  63.2 19.7 %collective-permute-start.11 = (bf16[512,1024]{1,0:T(8,128)(2,1)}, bf16[512,1024]{1,0:T(8,128)(2,1)}, u32[]{:S(2)}, u32[]{:S(2)}) collective-permute-start(bf16[512,1024]{1,0:T(8,128)(2,1)} %get-tuple-element.45), channel_id=1, source_target_pairs={{4,8},{6,10},{8,4},{10,6},{5,9},{7,11},{9,5},{11,7},{20,24},{22,26... | collective-permute-start | bytes 3145736 | tf_op jit(solution)/shard_map/ppermute | solution.py:561
  81.7 3.3 %collective-permute-start.5 = (bf16[128,4096]{1,0:T(8,128)(2,1)}, bf16[128,4096]{1,0:T(8,128)(2,1)}, u32[]{:S(2)}, u32[]{:S(2)}) collective-permute-start(bf16[128,4096]{1,0:T(8,128)(2,1)} %collective-permute-done.3.refs_1_), channel_id=1, source_target_pairs={{0,1},{1,0},{2,3},{3,2},{4,5},{5,4},{6,7},{7,6},{8,9},{9,8},{10,11... | collective-permute-start | bytes 3145736 | tf_op jit(solution)/shard_map/ppermute | solution.py:604
  81.7 4.5 %collective-permute-start.6 = (bf16[128,4096]{1,0:T(8,128)(2,1)}, bf16[128,4096]{1,0:T(8,128)(2,1)}, u32[]{:S(2)}, u32[]{:S(2)}) collective-permute-start(bf16[128,4096]{1,0:T(8,128)(2,1)} %collective-permute-done.4.refs_2_), channel_id=1, source_target_pairs={{0,1},{1,0},{2,3},{3,2},{4,5},{5,4},{6,7},{7,6},{8,9},{9,8},{10,11... | collective-permute-start | bytes 3145736 | tf_op jit(solution)/shard_map/ppermute | solution.py:604
  82.2 30.1 %collective-permute-start.13 = (bf16[512,1024]{1,0:T(8,128)(2,1)}, bf16[512,1024]{1,0:T(8,128)(2,1)S(1)}, u32[]{:S(2)}, u32[]{:S(2)}) collective-permute-start(bf16[512,1024]{1,0:T(8,128)(2,1)} %packed.3), channel_id=1, source_target_pairs={{4,8},{6,10},{8,4},{10,6},{5,9},{7,11},{9,5},{11,7},{20,24},{22,26... | collective-permute-start | bytes 3145736 | tf_op jit(solution)/shard_map/ppermute | solution.py:561
  83.0 36.9 %collective-permute-start.12 = (bf16[512,1024]{1,0:T(8,128)(2,1)}, bf16[512,1024]{1,0:T(8,128)(2,1)}, u32[]{:S(2)}, u32[]{:S(2)}) collective-permute-start(bf16[512,1024]{1,0:T(8,128)(2,1)} %collective-permute-done.11.refs_6_), channel_id=1, source_target_pairs={{4,0},{6,2},{8,12},{10,14},{5,1},{7,3},{9,13},{11,15},{20,16},{22,... | collective-permute-start | bytes 3145736 | tf_op jit(solution)/shard_map/ppermute | solution.py:561
  112.4 7.5 %copy-start = (bf16[512,1024]{1,0:T(8,128)(2,1)}, bf16[512,1024]{1,0:T(8,128)(2,1)S(1)}, u32[]{:S(2)}) copy-start(bf16[512,1024]{1,0:T(8,128)(2,1)S(1)} %collective-permute-done.13.refs_8_.refs_0_) | copy-start | bytes 3145732
  113.1 18.7 %collective-permute-start.14 = (bf16[512,640]{1,0:T(8,128)(2,1)S(1)}, bf16[512,640]{1,0:T(8,128)(2,1)S(1)}, u32[]{:S(2)}, u32[]{:S(2)}) collective-permute-start(bf16[512,640]{1,0:T(8,128)(2,1)S(1)} %packed.5), channel_id=1, source_target_pairs={{4,0},{6,2},{8,12},{10,14},{5,1},{7,3},{9,13},{11,15},{20,16},{22,... | collective-permute-start | bytes 1966088 | tf_op jit(solution)/shard_map/ppermute | solution.py:561
  125.9 5.9 %collective-permute-start.15 = (bf16[256,640]{1,0:T(8,128)(2,1)}, bf16[256,640]{1,0:T(8,128)(2,1)S(1)}, u32[]{:S(2)}, u32[]{:S(2)}) collective-permute-start(bf16[256,640]{1,0:T(8,128)(2,1)} %get-tuple-element.49), channel_id=1, source_target_pairs={{0,1},{1,0},{2,3},{3,2},{4,5},{5,4},{6,7},{7,6},{8,9},{9,8},{10,11... | collective-permute-start | bytes 983048 | tf_op jit(solution)/shard_map/ppermute | solution.py:639
  125.9 13.9 %collective-permute-start.19 = (bf16[256,640]{1,0:T(8,128)(2,1)}, bf16[256,640]{1,0:T(8,128)(2,1)S(1)}, u32[]{:S(2)}, u32[]{:S(2)}) collective-permute-start(bf16[256,640]{1,0:T(8,128)(2,1)} %get-tuple-element.57), channel_id=1, source_target_pairs={{0,2},{2,0},{4,6},{6,4},{8,10},{10,8},{12,14},{14,12},{1,3},{3,1},... | collective-permute-start | bytes 983048 | tf_op jit(solution)/shard_map/ppermute | solution.py:561
  127.5 15.4 %collective-permute-start.20 = (bf16[256,640]{1,0:T(8,128)(2,1)}, bf16[256,640]{1,0:T(8,128)(2,1)S(1)}, u32[]{:S(2)}, u32[]{:S(2)}) collective-permute-start(bf16[256,640]{1,0:T(8,128)(2,1)} %get-tuple-element.58), channel_id=1, source_target_pairs={{0,3},{1,2},{2,1},{3,0},{4,7},{5,6},{6,5},{7,4},{8,11},{9,10},{10,... | collective-permute-start | bytes 983048 | tf_op jit(solution)/shard_map/ppermute | solution.py:641
  131.8 0.8 copy-start.6
  132.6 6.9 %copy-start.8 = (s32[4,64]{1,0:T(4,128)S(1)}, s32[4,64]{1,0:T(4,128)}, u32[]{:S(2)}) copy-start(s32[4,64]{1,0:T(4,128)} %param.7) | copy-start | bytes 3076
  132.6 10.2 %copy-start.4 = (bf16[256,640]{1,0:T(8,128)(2,1)S(1)}, bf16[256,640]{1,0:T(8,128)(2,1)}, u32[]{:S(2)}) copy-start(bf16[256,640]{1,0:T(8,128)(2,1)} %get-tuple-element.55.refs_0_) | copy-start | bytes 983044
  137.5 7.3 %collective-permute-start.16 = (bf16[256,384]{1,0:T(8,128)(2,1)}, bf16[256,384]{1,0:T(8,128)(2,1)S(1)}, u32[]{:S(2)}, u32[]{:S(2)}) collective-permute-start(bf16[256,384]{1,0:T(8,128)(2,1)} %get-tuple-element.52), channel_id=1, source_target_pairs={{0,1},{1,0},{2,3},{3,2},{4,5},{5,4},{6,7},{7,6},{8,9},{9,8},{10,11... | collective-permute-start | bytes 589832 | tf_op jit(solution)/shard_map/ppermute | solution.py:639
  137.6 10.3 %collective-permute-start.17 = (bf16[256,384]{1,0:T(8,128)(2,1)}, bf16[256,384]{1,0:T(8,128)(2,1)S(1)}, u32[]{:S(2)}, u32[]{:S(2)}) collective-permute-start(bf16[256,384]{1,0:T(8,128)(2,1)} %get-tuple-element.53), channel_id=1, source_target_pairs={{0,2},{2,0},{4,6},{6,4},{8,10},{10,8},{12,14},{14,12},{1,3},{3,1},... | collective-permute-start | bytes 589832 | tf_op jit(solution)/shard_map/ppermute | solution.py:561
  138.7 12.6 %collective-permute-start.18 = (bf16[256,384]{1,0:T(8,128)(2,1)}, bf16[256,384]{1,0:T(8,128)(2,1)S(1)}, u32[]{:S(2)}, u32[]{:S(2)}) collective-permute-start(bf16[256,384]{1,0:T(8,128)(2,1)} %get-tuple-element.54), channel_id=1, source_target_pairs={{0,3},{1,2},{2,1},{3,0},{4,7},{5,6},{6,5},{7,4},{8,11},{9,10},{10,... | collective-permute-start | bytes 589832 | tf_op jit(solution)/shard_map/ppermute | solution.py:641
  151.3 0.9 copy-start.5

commit v16 on v14

--- a/solution.py
+++ b/solution.py
@@ -179,9 +179,14 @@
     return copies
 
 
-def add_product(acc, x, strips, g, first):
-    cols = pl.ds(pl.multiple_of(first * LANES, LANES), strips.shape[1])
-    acc[g, :, cols] += jnp.dot(x, strips, preferred_element_type=jnp.float32)
+def add_product(acc, x, strips, g, first, start=False):
+    width = strips.shape[1]
+    for n in range(0, width, 2 * LANES):
+        block = min(2 * LANES, width - n)
+        at = first * LANES + n
+        cols = slice(at, at + block) if isinstance(at, int) else pl.ds(pl.multiple_of(at, LANES), block)
+        value = jnp.dot(x[...], strips[:, n : n + block], preferred_element_type=jnp.float32)
+        acc[g, :, cols] = value if start else acc[g, :, cols] + value
 
 
 def whole_kernel(plan, meta_ref, *refs):
@@ -235,7 +240,7 @@
     middle = quarter // LANES // 2
 
     def own(g, carry):
-        acc[g, :, low : low + quarter] = jnp.dot(xv[g, g], bv[g], preferred_element_type=jnp.float32)
+        add_product(acc, xv.at[g, g], bv.at[g], g, low // LANES, True)
         return carry
 
     def step(i, carry):
@@ -252,10 +257,7 @@
 
             @pl.when(offset == k)
             def _():
-                strips = bv[p, :, first * LANES : last * LANES]
-                acc[g, :, (k + first) * LANES : (k + last) * LANES] += jnp.dot(
-                    xv[p, g], strips, preferred_element_type=jnp.float32
-                )
+                add_product(acc, xv.at[p, g], bv.at[p, :, first * LANES : last * LANES], g, k + first)
 
         return carry
 
@@ -374,12 +376,12 @@
 
     def add(g):
         for p in range(2):
-            add_product(acc, xv[p, g], bv[0, :, p * half : (p + 1) * half], g, offset_of(p, g) + meta_ref[1])
+            add_product(acc, xv.at[p, g], bv.at[0, :, p * half : (p + 1) * half], g, offset_of(p, g) + meta_ref[1])
 
         @pl.when(is_end == 0)
         def _():
             for p in range(2):
-                add_product(acc, xv[p, g], bv[1, :, p * half : (p + 1) * half], g, offset_of(p, g) + meta_ref[2])
+                add_product(acc, xv.at[p, g], bv.at[1, :, p * half : (p + 1) * half], g, offset_of(p, g) + meta_ref[2])
 
     finish(acc, wait_for, add, meta_ref[3] + band // 2, out_refs, pieces, out_sems, rest)
 
@@ -457,9 +459,9 @@
         @pl.when(is_end != 0)
         def _():
             for p in range(2):
-                add_product(acc, xv[p, g], bv[:, p * half : (p + 1) * half], g, offset_of(p, g) + meta_ref[1])
+                add_product(acc, xv.at[p, g], bv.at[:, p * half : (p + 1) * half], g, offset_of(p, g) + meta_ref[1])
             p = meta_ref[8]
-            add_product(acc, xv[p, g], bv[:, 2 * half :], g, offset_of(p, g) + meta_ref[7])
+            add_product(acc, xv.at[p, g], bv.at[:, 2 * half :], g, offset_of(p, g) + meta_ref[7])
 
     finish(acc, wait_for, add, meta_ref[2] + band // 2, out_refs, pieces, out_sems)
 

time: 155 us -> 155 us (level)
  no operation moved by 1% of the time
where the time goes in v16:
time: 155 us; the launch traced here: 152 us
  waiting for transfers between devices  76.3 us (49%)
  Pallas kernels  44.7 us (29%)
  starting transfers between devices  22.5 us (15%)
  local copies, waits for them, and re-layouts  7.97 us (5%)
    ppermute x15, waiting for transfers between devices, line(): return lax.ppermute(value, 'grid', pairs)  70.4 us
    ppermute x15, starting transfers between devices, line(): return lax.ppermute(value, 'grid', pairs)  20.7 us
    pallas_call x1, Pallas kernels, whole_products(): pl.pallas_call(functools.partial(whole_kernel, plan), out_shape=jax.Shape...  13.6 us
    pallas_call x1, Pallas kernels, masked_x(): pl.pallas_call(mask_kernel, grid_spec=pltpu.PrefetchScalarGridSpec(num_sc...  6.87 us
    pallas_call x1, Pallas kernels, half_products(): pl.pallas_call(half_kernel, out_shape=[jax.ShapeDtypeStruct((rows, n_done...  6.23 us
    pallas_call x3, Pallas kernels, packed(): pl.pallas_call(functools.partial(pack_kernel, plan, len(sources)), out_sh...  5.09 us
    pallas_call x1, Pallas kernels, rest_products(): pl.pallas_call(rest_kernel, out_shape=[jax.ShapeDtypeStruct((rows, width)...  4.95 us
    ppermute x2, waiting for transfers between devices, exchanged(): lax.ppermute(pieces[3], ('grid', 'depth'), opposite)  4.72 us
  transfers between devices with their start and end apart: 21, of which 12 were waited for; matrix products, arithmetic and copies ran while one was open for 4% of the time, Pallas kernels for 27%

profile of v16, /device:TPU:0, one launch (start us, length us, event | category | flops | bytes accessed | tf_op | source)
XLA Modules:
  0.0 152.3 jit_solution(9719171511930511099)
XLA Ops:
  0.0 2.2 %b_strips.2 = bf16[512,1024]{1,0:T(8,128)(2,1)} custom-call(s32[1]{0:T(128)} %bitcast.11.quarter_ref, bf16[512,4096]{1,0:T(8,128)(2,1)} %w_ref.2), custom_call_target="tpu_custom_call" | custom-call | flops 1000 | bytes 1000 | tf_op jit(solution)/shard_map/b_strips/pallas_call | solution.py:86
  2.2 3.0 %collective-permute-start = (bf16[512,1024]{1,0:T(8,128)(2,1)}, bf16[512,1024]{1,0:T(8,128)(2,1)}, u32[]{:S(2)}, u32[]{:S(2)}) collective-permute-start(bf16[512,1024]{1,0:T(8,128)(2,1)} %b_strips.2), channel_id=1, source_target_pairs={{0,2},{2,0},{4,6},{6,4},{8,10},{10,8},{12,14},{14,12},{1,3},{3,1},... | collective-permute-start | bytes 3145736 | tf_op jit(solution)/shard_map/ppermute | solution.py:563
  5.2 2.2 %b_strips.3.refs_5_ = bf16[512,1024]{1,0:T(8,128)(2,1)} custom-call(s32[1]{0:T(128)} %bitcast.quarter_ref, bf16[512,4096]{1,0:T(8,128)(2,1)} %w_ref.2), custom_call_target="tpu_custom_call" | custom-call | flops 1000 | bytes 1000 | tf_op jit(solution)/shard_map/b_strips/pallas_call | solution.py:86
  7.4 1.6 %collective-permute-start.1 = (bf16[512,1024]{1,0:T(8,128)(2,1)}, bf16[512,1024]{1,0:T(8,128)(2,1)S(1)}, u32[]{:S(2)}, u32[]{:S(2)}) collective-permute-start(bf16[512,1024]{1,0:T(8,128)(2,1)} %b_strips.3.refs_5_), channel_id=1, source_target_pairs={{0,4},{2,6},{4,0},{6,2},{8,12},{10,14},{12,8},{14,10},{1,5},{3,7},... | collective-permute-start | bytes 3145736 | tf_op jit(solution)/shard_map/ppermute | solution.py:563
  10.8 6.9 %masked_x.1.refs_0_ = bf16[512,4096]{1,0:T(8,128)(2,1)} custom-call(s32[1]{0:T(128)} %bitcast.9.first_ref, f32[8,1,4096]{2,1,0:T(1,128)} %reshape.17.mask_ref, bf16[512,4096]{1,0:T(8,128)(2,1)} %x_ref.1), custom_call_target="tpu_custom_call" | custom-call | flops 1000 | bytes 1000 | tf_op jit(solution)/shard_map/masked_x/pallas_call | solution.py:149
  17.7 3.2 %fusion = (bf16[128,4096]{1,0:T(8,128)(2,1)}, bf16[128,4096]{1,0:T(8,128)(2,1)}) fusion(bf16[512,4096]{1,0:T(8,128)(2,1)} %masked_x.1.refs_0_), kind=kLoop, calls=%fused_computation.4 | loop fusion | bytes 4194304 | tf_op jit(solution)/shard_map/slice | solution.py:578
  20.8 7.8 %collective-permute-done.refs_6_ = bf16[512,1024]{1,0:T(8,128)(2,1)} collective-permute-done((bf16[512,1024]{1,0:T(8,128)(2,1)}, bf16[512,1024]{1,0:T(8,128)(2,1)}, u32[]{:S(2)}, u32[]{:S(2)}) %collective-permute-start) | collective-permute-done | bytes 1048608 | tf_op jit(solution)/shard_map/ppermute | solution.py:563
  28.7 3.6 %collective-permute-done.1.refs_0_.refs_2_.refs_9_ = bf16[512,1024]{1,0:T(8,128)(2,1)S(1)} collective-permute-done((bf16[512,1024]{1,0:T(8,128)(2,1)}, bf16[512,1024]{1,0:T(8,128)(2,1)S(1)}, u32[]{:S(2)}, u32[]{:S(2)}) %collective-permute-start.1) | collective-permute-done | bytes 1048608 | tf_op jit(solution)/shard_map/ppermute | solution.py:563
  32.3 1.6 %collective-permute-start.2 = (bf16[512,1024]{1,0:T(8,128)(2,1)}, bf16[512,1024]{1,0:T(8,128)(2,1)S(1)}, u32[]{:S(2)}, u32[]{:S(2)}) collective-permute-start(bf16[512,1024]{1,0:T(8,128)(2,1)} %collective-permute-done.refs_6_), channel_id=1, source_target_pairs={{0,4},{2,6},{4,0},{6,2},{8,12},{10,14},{12,8},{14,10},{1,5},{3,7},... | collective-permute-start | bytes 3145736 | tf_op jit(solution)/shard_map/ppermute | solution.py:563
  33.9 1.7 %collective-permute-start.8 = (bf16[512,1024]{1,0:T(8,128)(2,1)}, bf16[512,1024]{1,0:T(8,128)(2,1)}, u32[]{:S(2)}, u32[]{:S(2)}) collective-permute-start(bf16[512,1024]{1,0:T(8,128)(2,1)} %collective-permute-done.refs_6_), channel_id=1, source_target_pairs={{4,8},{6,10},{8,4},{10,6},{5,9},{7,11},{9,5},{11,7},{20,24},{22,26... | collective-permute-start | bytes 3145736 | tf_op jit(solution)/shard_map/ppermute | solution.py:563
  36.0 1.5 collective-permute-start.4
  37.6 1.3 collective-permute-start.9
  39.0 19.6 %collective-permute-done.2.refs_1_.refs_3_.refs_10_ = bf16[512,1024]{1,0:T(8,128)(2,1)S(1)} collective-permute-done((bf16[512,1024]{1,0:T(8,128)(2,1)}, bf16[512,1024]{1,0:T(8,128)(2,1)S(1)}, u32[]{:S(2)}, u32[]{:S(2)}) %collective-permute-start.2) | collective-permute-done | bytes 1048608 | tf_op jit(solution)/shard_map/ppermute | solution.py:563
  58.6 3.3 %packed.4 = (bf16[512,1280]{1,0:T(8,128)(2,1)}, bf16[512,1024]{1,0:T(8,128)(2,1)}) custom-call(s32[2]{0:T(128)S(1)} %pad_add_fusion.1.meta_ref, bf16[512,1024]{1,0:T(8,128)(2,1)S(1)} %collective-permute-done.7.refs_0_.refs_7_, bf16[512,1024]{1,0:T(8,128)(2,1)} %collective-permute-done.8.refs_1_.refs_8_, ...), custom_call_target="tpu_custom_call" | custom-call | flops 1000 | bytes 1000 | tf_op jit(solution)/shard_map/packed/pallas_call | solution.py:129
  61.9 2.9 %collective-permute-done.9.refs_12_ = bf16[512,384]{1,0:T(8,128)(2,1)} collective-permute-done((bf16[512,384]{1,0:T(8,128)(2,1)S(1)}, bf16[512,384]{1,0:T(8,128)(2,1)}, u32[]{:S(2)}, u32[]{:S(2)}) %collective-permute-start.9) | collective-permute-done | bytes 393248 | tf_op jit(solution)/shard_map/ppermute | solution.py:563
  64.8 1.3 collective-permute-start.10
  66.1 1.6 %collective-permute-start.11 = (bf16[512,1024]{1,0:T(8,128)(2,1)}, bf16[512,1024]{1,0:T(8,128)(2,1)}, u32[]{:S(2)}, u32[]{:S(2)}) collective-permute-start(bf16[512,1024]{1,0:T(8,128)(2,1)} %get-tuple-element.45), channel_id=1, source_target_pairs={{4,8},{6,10},{8,4},{10,6},{5,9},{7,11},{9,5},{11,7},{20,24},{22,26... | collective-permute-start | bytes 3145736 | tf_op jit(solution)/shard_map/ppermute | solution.py:563
  68.9 12.9 %collective-permute-done.4.refs_2_ = bf16[128,4096]{1,0:T(8,128)(2,1)} collective-permute-done((bf16[128,4096]{1,0:T(8,128)(2,1)}, bf16[128,4096]{1,0:T(8,128)(2,1)}, u32[]{:S(2)}, u32[]{:S(2)}) %collective-permute-start.4) | collective-permute-done | bytes 1048608 | tf_op jit(solution)/shard_map/ppermute | solution.py:563
  83.0 1.3 collective-permute-start.12
  86.3 9.7 %collective-permute-done.10.refs_11_ = bf16[512,1280]{1,0:T(8,128)(2,1)} collective-permute-done((bf16[512,1280]{1,0:T(8,128)(2,1)}, bf16[512,1280]{1,0:T(8,128)(2,1)}, u32[]{:S(2)}, u32[]{:S(2)}) %collective-permute-start.10) | collective-permute-done | bytes 1310752 | tf_op jit(solution)/shard_map/ppermute | solution.py:563
  96.0 13.6 %whole_products.1.refs_5_ = f32[2,512,1024]{2,1,0:T(8,128)} custom-call(s32[14]{0:T(128)} %stack.137.meta_ref, bf16[512,4096]{1,0:T(8,128)(2,1)} %masked_x.1.refs_0_, bf16[128,4096]{1,0:T(8,128)(2,1)} %collective-permute-done.3.refs_1_, bf16[128,4096]{1,0:T(8,128)(2,1)} %collective-permute-done.4.refs_2_, bf16[128,4096]{1,0:T(8,128)(2,1)} %collective-permute-done.5.refs_3_, ...), custom_call_target="tpu_custom_call" | custom-call | flops 6000000000 | bytes 37748736 | tf_op jit(solution)/shard_map/whole_products/pallas_call | solution.py:279
  110.4 1.3 collective-permute-start.14
  112.3 5.7 %collective-permute-done.12.refs_7_ = bf16[512,1024]{1,0:T(8,128)(2,1)} collective-permute-done((bf16[512,1024]{1,0:T(8,128)(2,1)}, bf16[512,1024]{1,0:T(8,128)(2,1)}, u32[]{:S(2)}, u32[]{:S(2)}) %collective-permute-start.12) | collective-permute-done | bytes 1048608 | tf_op jit(solution)/shard_map/ppermute | solution.py:563
  118.0 6.2 %half_products.1 = (bf16[256,640]{1,0:T(8,128)(2,1)}, bf16[256,640]{1,0:T(8,128)(2,1)}, bf16[256,640]{1,0:T(8,128)(2,1)}, bf16[256,640]{1,0:T(8,128)(2,1)}, f32[2,512,384]{2,1,0:T(8,128)}) custom-call(s32[9]{0:T(128)} %stack.127.meta_ref, bf16[512,4096]{1,0:T(8,128)(2,1)} %masked_x.1.refs_0_, bf16[128,4096]{1,0:T(8,128)(2,1)} %collective-permute-done.3.refs_1_, ...), custom_call_target="tpu_custom_call" | custom-call | flops 1000 | bytes 1000 | tf_op jit(solution)/shard_map/half_products/pallas_call | solution.py:395
  124.4 1.5 collective-permute-start.19
  126.8 5.0 %collective-permute-done.14.refs_6_ = bf16[512,640]{1,0:T(8,128)(2,1)S(1)} collective-permute-done((bf16[512,640]{1,0:T(8,128)(2,1)S(1)}, bf16[512,640]{1,0:T(8,128)(2,1)S(1)}, u32[]{:S(2)}, u32[]{:S(2)}) %collective-permute-start.14) | collective-permute-done | bytes 655392 | tf_op jit(solution)/shard_map/ppermute | solution.py:563
  132.6 5.0 %rest_products.1 = (bf16[256,384]{1,0:T(8,128)(2,1)}, bf16[256,384]{1,0:T(8,128)(2,1)}, bf16[256,384]{1,0:T(8,128)(2,1)}, bf16[256,384]{1,0:T(8,128)(2,1)}) custom-call(s32[9]{0:T(128)} %stack.123.meta_ref, bf16[512,4096]{1,0:T(8,128)(2,1)} %masked_x.1.refs_0_, bf16[128,4096]{1,0:T(8,128)(2,1)} %collective-permute-done.3.refs_1_, ...), custom_call_target="tpu_custom_call" | custom-call | flops 1000 | bytes 1000 | tf_op jit(solution)/shard_map/rest_products/pallas_call | solution.py:475
  139.9 1.4 collective-permute-done.20.refs_3_
  141.3 2.0 %assembled.2.refs_4_ = bf16[256,4096]{1,0:T(8,128)(2,1)} custom-call(s32[2]{0:T(128)S(1)} %get-tuple-element.62.place_ref, f32[4,1,4096]{2,1,0:T(1,128)S(1)} %reshape.15.mask_ref, bf16[256,640]{1,0:T(8,128)(2,1)S(1)} %copy-done.4, bf16[256,640]{1,0:T(8,128)(2,1)S(1)} %collective-permute-done.15.refs_1_, ...), custom_call_target="tpu_custom_call" | custom-call | flops 1000 | bytes 1000 | tf_op jit(solution)/shard_map/assembled/pallas_call | solution.py:522
  143.3 3.1 %collective-permute-done.17.refs_2_ = bf16[256,384]{1,0:T(8,128)(2,1)S(1)} collective-permute-done((bf16[256,384]{1,0:T(8,128)(2,1)}, bf16[256,384]{1,0:T(8,128)(2,1)S(1)}, u32[]{:S(2)}, u32[]{:S(2)}) %collective-permute-start.17) | collective-permute-done | bytes 196640 | tf_op jit(solution)/shard_map/ppermute | solution.py:563
  146.4 3.3 %collective-permute-done.18.refs_3_ = bf16[256,384]{1,0:T(8,128)(2,1)S(1)} collective-permute-done((bf16[256,384]{1,0:T(8,128)(2,1)}, bf16[256,384]{1,0:T(8,128)(2,1)S(1)}, u32[]{:S(2)}, u32[]{:S(2)}) %collective-permute-start.18) | collective-permute-done | bytes 196640 | tf_op jit(solution)/shard_map/ppermute | solution.py:643
  150.6 1.6 %assembled.3 = bf16[256,4096]{1,0:T(8,128)(2,1)} custom-call(s32[2]{0:T(128)S(1)} %get-tuple-element.61.place_ref, f32[4,1,4096]{2,1,0:T(1,128)S(1)} %reshape.15.mask_ref, bf16[256,384]{1,0:T(8,128)(2,1)S(1)} %copy-done.5, bf16[256,384]{1,0:T(8,128)(2,1)S(1)} %collective-permute-done.16.refs_1_, ...), custom_call_target="tpu_custom_call", output_to_operand_aliasing={{}: (6, {})} | custom-call | flops 1000 | bytes 1000 | tf_op jit(solution)/shard_map/assembled/pallas_call | solution.py:522
  (53 shorter events, 12.9 us)
Async XLA Ops:
  0.0 9.8 %copy-start.7 = (s32[8,64]{1,0:T(8,128)S(1)}, s32[8,64]{1,0:T(8,128)}, u32[]{:S(2)}) copy-start(s32[8,64]{1,0:T(8,128)} %param.6) | copy-start | bytes 6148
  2.2 26.5 %collective-permute-start = (bf16[512,1024]{1,0:T(8,128)(2,1)}, bf16[512,1024]{1,0:T(8,128)(2,1)}, u32[]{:S(2)}, u32[]{:S(2)}) collective-permute-start(bf16[512,1024]{1,0:T(8,128)(2,1)} %b_strips.2), channel_id=1, source_target_pairs={{0,2},{2,0},{4,6},{6,4},{8,10},{10,8},{12,14},{14,12},{1,3},{3,1},... | collective-permute-start | bytes 3145736 | tf_op jit(solution)/shard_map/ppermute | solution.py:563
  7.4 24.9 %collective-permute-start.1 = (bf16[512,1024]{1,0:T(8,128)(2,1)}, bf16[512,1024]{1,0:T(8,128)(2,1)S(1)}, u32[]{:S(2)}, u32[]{:S(2)}) collective-permute-start(bf16[512,1024]{1,0:T(8,128)(2,1)} %b_strips.3.refs_5_), channel_id=1, source_target_pairs={{0,4},{2,6},{4,0},{6,2},{8,12},{10,14},{12,8},{14,10},{1,5},{3,7},... | collective-permute-start | bytes 3145736 | tf_op jit(solution)/shard_map/ppermute | solution.py:563
  9.1 28.5 %collective-permute-start.7 = (bf16[512,1024]{1,0:T(8,128)(2,1)}, bf16[512,1024]{1,0:T(8,128)(2,1)S(1)}, u32[]{:S(2)}, u32[]{:S(2)}) collective-permute-start(bf16[512,1024]{1,0:T(8,128)(2,1)} %b_strips.3.refs_5_), channel_id=1, source_target_pairs={{4,8},{6,10},{8,4},{10,6},{5,9},{7,11},{9,5},{11,7},{20,24},{22,26... | collective-permute-start | bytes 3145736 | tf_op jit(solution)/shard_map/ppermute | solution.py:563
  32.3 52.1 %copy-start.1 = (bf16[512,1024]{1,0:T(8,128)(2,1)}, bf16[512,1024]{1,0:T(8,128)(2,1)S(1)}, u32[]{:S(2)}) copy-start(bf16[512,1024]{1,0:T(8,128)(2,1)S(1)} %collective-permute-done.1.refs_0_.refs_2_.refs_9_) | copy-start | bytes 3145732
  32.3 26.3 %collective-permute-start.2 = (bf16[512,1024]{1,0:T(8,128)(2,1)}, bf16[512,1024]{1,0:T(8,128)(2,1)S(1)}, u32[]{:S(2)}, u32[]{:S(2)}) collective-permute-start(bf16[512,1024]{1,0:T(8,128)(2,1)} %collective-permute-done.refs_6_), channel_id=1, source_target_pairs={{0,4},{2,6},{4,0},{6,2},{8,12},{10,14},{12,8},{14,10},{1,5},{3,7},... | collective-permute-start | bytes 3145736 | tf_op jit(solution)/shard_map/ppermute | solution.py:563
  33.9 24.7 %collective-permute-start.8 = (bf16[512,1024]{1,0:T(8,128)(2,1)}, bf16[512,1024]{1,0:T(8,128)(2,1)}, u32[]{:S(2)}, u32[]{:S(2)}) collective-permute-start(bf16[512,1024]{1,0:T(8,128)(2,1)} %collective-permute-done.refs_6_), channel_id=1, source_target_pairs={{4,8},{6,10},{8,4},{10,6},{5,9},{7,11},{9,5},{11,7},{20,24},{22,26... | collective-permute-start | bytes 3145736 | tf_op jit(solution)/shard_map/ppermute | solution.py:563
  35.5 33.3 %collective-permute-start.3 = (bf16[128,4096]{1,0:T(8,128)(2,1)}, bf16[128,4096]{1,0:T(8,128)(2,1)}, u32[]{:S(2)}, u32[]{:S(2)}) collective-permute-start(bf16[128,4096]{1,0:T(8,128)(2,1)} %get-tuple-element.36), channel_id=1, source_target_pairs={{0,2},{2,0},{4,6},{6,4},{8,10},{10,8},{12,14},{14,12},{1,3},{3,1},... | collective-permute-start | bytes 3145736 | tf_op jit(solution)/shard_map/ppermute | solution.py:563
  36.0 45.7 %collective-permute-start.4 = (bf16[128,4096]{1,0:T(8,128)(2,1)}, bf16[128,4096]{1,0:T(8,128)(2,1)}, u32[]{:S(2)}, u32[]{:S(2)}) collective-permute-start(bf16[128,4096]{1,0:T(8,128)(2,1)} %get-tuple-element.37), channel_id=1, source_target_pairs={{0,2},{2,0},{4,6},{6,4},{8,10},{10,8},{12,14},{14,12},{1,3},{3,1},... | collective-permute-start | bytes 3145736 | tf_op jit(solution)/shard_map/ppermute | solution.py:563
  37.6 44.2 %copy-start.3 = (bf16[512,1024]{1,0:T(8,128)(2,1)}, bf16[512,1024]{1,0:T(8,128)(2,1)S(1)}, u32[]{:S(2)}) copy-start(bf16[512,1024]{1,0:T(8,128)(2,1)S(1)} %collective-permute-done.7.refs_0_.refs_7_) | copy-start | bytes 3145732
  37.6 27.2 %collective-permute-start.9 = (bf16[512,384]{1,0:T(8,128)(2,1)S(1)}, bf16[512,384]{1,0:T(8,128)(2,1)}, u32[]{:S(2)}, u32[]{:S(2)}) collective-permute-start(bf16[512,384]{1,0:T(8,128)(2,1)S(1)} %slice.14), channel_id=1, source_target_pairs={{4,0},{6,2},{8,12},{10,14},{5,1},{7,3},{9,13},{11,15},{20,16},{22,... | collective-permute-start | bytes 1179656 | tf_op jit(solution)/shard_map/ppermute | solution.py:563
  58.6 37.4 %copy-start.2 = (bf16[512,1024]{1,0:T(8,128)(2,1)}, bf16[512,1024]{1,0:T(8,128)(2,1)S(1)}, u32[]{:S(2)}) copy-start(bf16[512,1024]{1,0:T(8,128)(2,1)S(1)} %collective-permute-done.2.refs_1_.refs_3_.refs_10_) | copy-start | bytes 3145732
  64.8 31.2 %collective-permute-start.10 = (bf16[512,1280]{1,0:T(8,128)(2,1)}, bf16[512,1280]{1,0:T(8,128)(2,1)}, u32[]{:S(2)}, u32[]{:S(2)}) collective-permute-start(bf16[512,1280]{1,0:T(8,128)(2,1)} %get-tuple-element.42), channel_id=1, source_target_pairs={{4,0},{6,2},{8,12},{10,14},{5,1},{7,3},{9,13},{11,15},{20,16},{22,... | collective-permute-start | bytes 3932168 | tf_op jit(solution)/shard_map/ppermute | solution.py:563
  66.1 16.9 %collective-permute-start.11 = (bf16[512,1024]{1,0:T(8,128)(2,1)}, bf16[512,1024]{1,0:T(8,128)(2,1)}, u32[]{:S(2)}, u32[]{:S(2)}) collective-permute-start(bf16[512,1024]{1,0:T(8,128)(2,1)} %get-tuple-element.45), channel_id=1, source_target_pairs={{4,8},{6,10},{8,4},{10,6},{5,9},{7,11},{9,5},{11,7},{20,24},{22,26... | collective-permute-start | bytes 3145736 | tf_op jit(solution)/shard_map/ppermute | solution.py:563
  81.8 3.3 %collective-permute-start.5 = (bf16[128,4096]{1,0:T(8,128)(2,1)}, bf16[128,4096]{1,0:T(8,128)(2,1)}, u32[]{:S(2)}, u32[]{:S(2)}) collective-permute-start(bf16[128,4096]{1,0:T(8,128)(2,1)} %collective-permute-done.3.refs_1_), channel_id=1, source_target_pairs={{0,1},{1,0},{2,3},{3,2},{4,5},{5,4},{6,7},{7,6},{8,9},{9,8},{10,11... | collective-permute-start | bytes 3145736 | tf_op jit(solution)/shard_map/ppermute | solution.py:606
  81.8 4.5 %collective-permute-start.6 = (bf16[128,4096]{1,0:T(8,128)(2,1)}, bf16[128,4096]{1,0:T(8,128)(2,1)}, u32[]{:S(2)}, u32[]{:S(2)}) collective-permute-start(bf16[128,4096]{1,0:T(8,128)(2,1)} %collective-permute-done.4.refs_2_), channel_id=1, source_target_pairs={{0,1},{1,0},{2,3},{3,2},{4,5},{5,4},{6,7},{7,6},{8,9},{9,8},{10,11... | collective-permute-start | bytes 3145736 | tf_op jit(solution)/shard_map/ppermute | solution.py:606
  82.3 27.4 %collective-permute-start.13 = (bf16[512,1024]{1,0:T(8,128)(2,1)}, bf16[512,1024]{1,0:T(8,128)(2,1)S(1)}, u32[]{:S(2)}, u32[]{:S(2)}) collective-permute-start(bf16[512,1024]{1,0:T(8,128)(2,1)} %packed.3), channel_id=1, source_target_pairs={{4,8},{6,10},{8,4},{10,6},{5,9},{7,11},{9,5},{11,7},{20,24},{22,26... | collective-permute-start | bytes 3145736 | tf_op jit(solution)/shard_map/ppermute | solution.py:563
  83.0 35.0 %collective-permute-start.12 = (bf16[512,1024]{1,0:T(8,128)(2,1)}, bf16[512,1024]{1,0:T(8,128)(2,1)}, u32[]{:S(2)}, u32[]{:S(2)}) collective-permute-start(bf16[512,1024]{1,0:T(8,128)(2,1)} %collective-permute-done.11.refs_6_), channel_id=1, source_target_pairs={{4,0},{6,2},{8,12},{10,14},{5,1},{7,3},{9,13},{11,15},{20,16},{22,... | collective-permute-start | bytes 3145736 | tf_op jit(solution)/shard_map/ppermute | solution.py:563
  109.7 8.4 %copy-start = (bf16[512,1024]{1,0:T(8,128)(2,1)}, bf16[512,1024]{1,0:T(8,128)(2,1)S(1)}, u32[]{:S(2)}) copy-start(bf16[512,1024]{1,0:T(8,128)(2,1)S(1)} %collective-permute-done.13.refs_8_.refs_0_) | copy-start | bytes 3145732
  110.4 21.4 %collective-permute-start.14 = (bf16[512,640]{1,0:T(8,128)(2,1)S(1)}, bf16[512,640]{1,0:T(8,128)(2,1)S(1)}, u32[]{:S(2)}, u32[]{:S(2)}) collective-permute-start(bf16[512,640]{1,0:T(8,128)(2,1)S(1)} %packed.5), channel_id=1, source_target_pairs={{4,0},{6,2},{8,12},{10,14},{5,1},{7,3},{9,13},{11,15},{20,16},{22,... | collective-permute-start | bytes 1966088 | tf_op jit(solution)/shard_map/ppermute | solution.py:563
  124.3 7.5 %collective-permute-start.15 = (bf16[256,640]{1,0:T(8,128)(2,1)}, bf16[256,640]{1,0:T(8,128)(2,1)S(1)}, u32[]{:S(2)}, u32[]{:S(2)}) collective-permute-start(bf16[256,640]{1,0:T(8,128)(2,1)} %get-tuple-element.49), channel_id=1, source_target_pairs={{0,1},{1,0},{2,3},{3,2},{4,5},{5,4},{6,7},{7,6},{8,9},{9,8},{10,11... | collective-permute-start | bytes 983048 | tf_op jit(solution)/shard_map/ppermute | solution.py:641
  124.4 15.5 %collective-permute-start.19 = (bf16[256,640]{1,0:T(8,128)(2,1)}, bf16[256,640]{1,0:T(8,128)(2,1)S(1)}, u32[]{:S(2)}, u32[]{:S(2)}) collective-permute-start(bf16[256,640]{1,0:T(8,128)(2,1)} %get-tuple-element.57), channel_id=1, source_target_pairs={{0,2},{2,0},{4,6},{6,4},{8,10},{10,8},{12,14},{14,12},{1,3},{3,1},... | collective-permute-start | bytes 983048 | tf_op jit(solution)/shard_map/ppermute | solution.py:563
  125.9 15.4 %collective-permute-start.20 = (bf16[256,640]{1,0:T(8,128)(2,1)}, bf16[256,640]{1,0:T(8,128)(2,1)S(1)}, u32[]{:S(2)}, u32[]{:S(2)}) collective-permute-start(bf16[256,640]{1,0:T(8,128)(2,1)} %get-tuple-element.58), channel_id=1, source_target_pairs={{0,3},{1,2},{2,1},{3,0},{4,7},{5,6},{6,5},{7,4},{8,11},{9,10},{10,... | collective-permute-start | bytes 983048 | tf_op jit(solution)/shard_map/ppermute | solution.py:643
  131.8 0.8 copy-start.6
  132.6 6.9 %copy-start.8 = (s32[4,64]{1,0:T(4,128)S(1)}, s32[4,64]{1,0:T(4,128)}, u32[]{:S(2)}) copy-start(s32[4,64]{1,0:T(4,128)} %param.7) | copy-start | bytes 3076
  132.6 8.6 %copy-start.4 = (bf16[256,640]{1,0:T(8,128)(2,1)S(1)}, bf16[256,640]{1,0:T(8,128)(2,1)}, u32[]{:S(2)}) copy-start(bf16[256,640]{1,0:T(8,128)(2,1)} %get-tuple-element.55.refs_0_) | copy-start | bytes 983044
  137.6 5.7 %collective-permute-start.16 = (bf16[256,384]{1,0:T(8,128)(2,1)}, bf16[256,384]{1,0:T(8,128)(2,1)S(1)}, u32[]{:S(2)}, u32[]{:S(2)}) collective-permute-start(bf16[256,384]{1,0:T(8,128)(2,1)} %get-tuple-element.52), channel_id=1, source_target_pairs={{0,1},{1,0},{2,3},{3,2},{4,5},{5,4},{6,7},{7,6},{8,9},{9,8},{10,11... | collective-permute-start | bytes 589832 | tf_op jit(solution)/shard_map/ppermute | solution.py:641
  137.7 8.7 %collective-permute-start.17 = (bf16[256,384]{1,0:T(8,128)(2,1)}, bf16[256,384]{1,0:T(8,128)(2,1)S(1)}, u32[]{:S(2)}, u32[]{:S(2)}) collective-permute-start(bf16[256,384]{1,0:T(8,128)(2,1)} %get-tuple-element.53), channel_id=1, source_target_pairs={{0,2},{2,0},{4,6},{6,4},{8,10},{10,8},{12,14},{14,12},{1,3},{3,1},... | collective-permute-start | bytes 589832 | tf_op jit(solution)/shard_map/ppermute | solution.py:563
  138.7 11.0 %collective-permute-start.18 = (bf16[256,384]{1,0:T(8,128)(2,1)}, bf16[256,384]{1,0:T(8,128)(2,1)S(1)}, u32[]{:S(2)}, u32[]{:S(2)}) collective-permute-start(bf16[256,384]{1,0:T(8,128)(2,1)} %get-tuple-element.54), channel_id=1, source_target_pairs={{0,3},{1,2},{2,1},{3,0},{4,7},{5,6},{6,5},{7,4},{8,11},{9,10},{10,... | collective-permute-start | bytes 589832 | tf_op jit(solution)/shard_map/ppermute | solution.py:643
  149.7 0.9 copy-start.5

commit v17 on v14

--- a/solution.py
+++ b/solution.py
@@ -293,11 +293,10 @@
     )(meta, *xs, *operands)
 
 
-def finish(acc, wait_for, add, at, out_refs, pieces, sems, also=None):
+def finish(acc, wait_for, add, at, out_refs, pieces, sems):
     half, width = out_refs[0].shape
     cols = pl.ds(pl.multiple_of(at * LANES, LANES), width)
     outs = [pltpu.make_async_copy(pieces.at[r], out_refs[r], sems.at[r]) for r in range(4)]
-    also = also or []
 
     def step(g, carry):
         for k in range(2):
@@ -307,8 +306,6 @@
 
             @pl.when(g == k)
             def _():
-                for copy in also[k : k + 1]:
-                    copy.start()
                 for r in range(2 * k, 2 * k + 2):
                     rows = slice((r % 2) * half, (r % 2 + 1) * half)
                     pieces[r] = acc[k, rows, cols].astype(jnp.bfloat16)
@@ -317,45 +314,58 @@
         return carry
 
     lax.fori_loop(0, 2, step, 0)
-    for copy in outs + also:
+    for copy in outs:
         copy.wait()
 
 
-def half_kernel(meta_ref, *refs):
+def last_kernel(has_b, meta_ref, *refs):
     x_refs, (prev_ref, middle_ref, end_ref, second_ref), refs = refs[:PARTS], refs[PARTS : PARTS + 4], refs[PARTS + 4 :]
-    out_refs, rest_ref, xv, bv, acc, pieces, x_sems, b_sems, prev_sems, rest_sems, out_sems = refs[:4], *refs[4:]
+    b_ref, refs = (refs[0], refs[1:]) if has_b else (None, refs)
+    out_refs, xv, bv, acc, pieces, x_sems, b_sems, prev_sems, out_sems = refs[:4], *refs[4:]
     quarter = bv.shape[2]
     half = quarter // 2
-    low = quarter // 2
     band = quarter // LANES
+    width = out_refs[0].shape[1]
     is_end = meta_ref[0]
 
     def offset_of(p, g):
-        return meta_ref[5 + 2 * p + g]
+        return meta_ref[4 + 2 * p + g]
+
+    def strips(first):
+        return pl.ds(pl.multiple_of(first * LANES, LANES), width)
 
     x_loads = x_copies(x_refs, xv, x_sems, offset_of)
-    middle = pltpu.make_async_copy(middle_ref, bv.at[0], b_sems.at[0])
-    end = pltpu.make_async_copy(end_ref, bv.at[0], b_sems.at[0])
-    second = pltpu.make_async_copy(second_ref, bv.at[1], b_sems.at[1])
+    middle = [
+        pltpu.make_async_copy(middle_ref, bv.at[0], b_sems.at[0]),
+        pltpu.make_async_copy(second_ref, bv.at[1], b_sems.at[1]),
+    ]
+    end = [pltpu.make_async_copy(end_ref, bv.at[0], b_sems.at[0])]
+    if has_b:
+        n_b = b_ref.shape[1]
+        few = (n_b - LANES) // 2
+        end.append(pltpu.make_async_copy(b_ref, bv.at[1, :, :n_b], b_sems.at[1]))
     prev = [
-        pltpu.make_async_copy(prev_ref.at[g], acc.at[g, :, low : low + quarter], prev_sems.at[g]) for g in range(2)
-    ]
-    at = pl.multiple_of((meta_ref[4] + band // 2) * LANES, LANES)
-    rest = [
-        pltpu.make_async_copy(acc.at[g, :, pl.ds(at, rest_ref.shape[2])], rest_ref.at[g], rest_sems.at[g])
+        pltpu.make_async_copy(
+            prev_ref.at[g, :, strips(meta_ref[3])], acc.at[g, :, strips(meta_ref[3] + band // 2)], prev_sems.at[g]
+        )
         for g in range(2)
     ]
 
-    @pl.when(is_end == 0)
-    def _():
-        middle.start()
-        second.start()
-
-    pl.when(is_end != 0)(end.start)
+    def on_b(do):
+        @pl.when(is_end == 0)
+        def _():
+            for copy in middle:
+                do(copy)
+
+        @pl.when(is_end != 0)
+        def _():
+            for copy in end:
+                do(copy)
 
     def rows_loads(g):
         return [prev[g]] + [copy for (_, r), copy in x_loads.items() if min(r, 1) == g]
 
+    on_b(lambda copy: copy.start())
     for g in range(2):
         for copy in rows_loads(g):
             copy.start()
@@ -364,13 +374,7 @@
         for copy in rows_loads(g):
             copy.wait()
         if g == 0:
-
-            @pl.when(is_end == 0)
-            def _():
-                middle.wait()
-                second.wait()
-
-            pl.when(is_end != 0)(end.wait)
+            on_b(lambda copy: copy.wait())
 
     def add(g):
         for p in range(2):
@@ -381,114 +385,44 @@
             for p in range(2):
                 add_product(acc, xv[p, g], bv[1, :, p * half : (p + 1) * half], g, offset_of(p, g) + meta_ref[2])
 
-    finish(acc, wait_for, add, meta_ref[3] + band // 2, out_refs, pieces, out_sems, rest)
-
-
-def half_products(meta, xs, prev, middle, end, second, n_done):
+        if has_b:
+
+            @pl.when(is_end != 0)
+            def _():
+                for p in range(2):
+                    add_product(acc, xv[p, g], bv[1, :, p * few : (p + 1) * few], g, offset_of(p, g) + meta_ref[8])
+                p = meta_ref[10]
+                add_product(acc, xv[p, g], bv[1, :, 2 * few : n_b], g, offset_of(p, g) + meta_ref[9])
+
+    finish(acc, wait_for, add, meta_ref[3] + band // 2, out_refs, pieces, out_sems)
+
+
+def last_products(meta, xs, prev, middle, end, second, b, count, name):
     rows = xs[0].shape[0] // 2
     panel, quarter = second.shape
     any_spec = pl.BlockSpec(memory_space=pl.ANY)
     x_spec = pl.BlockSpec(memory_space=pltpu.HBM)
-    n_rest = quarter // LANES - n_done
+    operands = [prev, middle, end, second] + ([] if b is None else [b])
+    width = count * LANES
     return pl.pallas_call(
-        half_kernel,
-        out_shape=[jax.ShapeDtypeStruct((rows, n_done * LANES), jnp.bfloat16)] * 4
-        + [jax.ShapeDtypeStruct((2, 2 * rows, n_rest * LANES), jnp.float32)],
-        in_specs=[pl.BlockSpec(memory_space=pltpu.SMEM)] + [x_spec] * PARTS + [any_spec] * 4,
-        out_specs=[any_spec] * 5,
+        functools.partial(last_kernel, b is not None),
+        out_shape=[jax.ShapeDtypeStruct((rows, width), jnp.bfloat16)] * 4,
+        in_specs=[pl.BlockSpec(memory_space=pltpu.SMEM)] + [x_spec] * PARTS + [any_spec] * len(operands),
+        out_specs=[any_spec] * 4,
         scratch_shapes=[
             pltpu.VMEM((2, 2, 2 * rows, panel), jnp.bfloat16),
             pltpu.VMEM((2, panel, quarter), jnp.bfloat16),
             pltpu.VMEM((2, 2 * rows, 2 * quarter), jnp.float32),
-            pltpu.VMEM((4, rows, n_done * LANES), jnp.bfloat16),
+            pltpu.VMEM((4, rows, width), jnp.bfloat16),
             pltpu.SemaphoreType.DMA((2, PARTS)),
-            pltpu.SemaphoreType.DMA((2,)),
             pltpu.SemaphoreType.DMA((2,)),
             pltpu.SemaphoreType.DMA((2,)),
             pltpu.SemaphoreType.DMA((4,)),
         ],
         compiler_params=pltpu.CompilerParams(vmem_limit_bytes=59 * MIB),
         cost_estimate=SMALL,
-        name="half_products",
-    )(meta, *xs, prev, middle, end, second)
-
-
-def rest_kernel(meta_ref, *refs):
-    x_refs, (rest_ref, b_ref), refs = refs[:PARTS], refs[PARTS : PARTS + 2], refs[PARTS + 2 :]
-    out_refs, xv, bv, acc, pieces, x_sems, b_sem, rest_sems, out_sems = refs[:4], *refs[4:]
-    band = acc.shape[2] // (2 * LANES)
-    half = (bv.shape[1] - LANES) // 2
-    is_end = meta_ref[0]
-
-    def offset_of(p, g):
-        return meta_ref[3 + 2 * p + g]
-
-    at = pl.multiple_of((meta_ref[2] + band // 2) * LANES, LANES)
-    rest = [
-        pltpu.make_async_copy(rest_ref.at[g], acc.at[g, :, pl.ds(at, rest_ref.shape[2])], rest_sems.at[g])
-        for g in range(2)
-    ]
-    x_loads = x_copies(x_refs, xv, x_sems, offset_of)
-    b_copy = pltpu.make_async_copy(b_ref, bv, b_sem)
-
-    def x_loads_of(g):
-        return [copy for (_, r), copy in x_loads.items() if min(r, 1) == g]
-
-    pl.when(is_end != 0)(b_copy.start)
-    for g in range(2):
-        rest[g].start()
-
-        @pl.when(is_end != 0)
-        def _():
-            for copy in x_loads_of(g):
-                copy.start()
-
-    def wait_for(g):
-        rest[g].wait()
-
-        @pl.when(is_end != 0)
-        def _():
-            for copy in x_loads_of(g):
-                copy.wait()
-            if g == 0:
-                b_copy.wait()
-
-    def add(g):
-        @pl.when(is_end != 0)
-        def _():
-            for p in range(2):
-                add_product(acc, xv[p, g], bv[:, p * half : (p + 1) * half], g, offset_of(p, g) + meta_ref[1])
-            p = meta_ref[8]
-            add_product(acc, xv[p, g], bv[:, 2 * half :], g, offset_of(p, g) + meta_ref[7])
-
-    finish(acc, wait_for, add, meta_ref[2] + band // 2, out_refs, pieces, out_sems)
-
-
-def rest_products(meta, xs, rest, b, quarter):
-    rows = xs[0].shape[0] // 2
-    panel = b.shape[0]
-    width = rest.shape[2]
-    any_spec = pl.BlockSpec(memory_space=pl.ANY)
-    x_spec = pl.BlockSpec(memory_space=pltpu.HBM)
-    return pl.pallas_call(
-        rest_kernel,
-        out_shape=[jax.ShapeDtypeStruct((rows, width), jnp.bfloat16)] * 4,
-        in_specs=[pl.BlockSpec(memory_space=pltpu.SMEM)] + [x_spec] * PARTS + [any_spec] * 2,
-        out_specs=[any_spec] * 4,
-        scratch_shapes=[
-            pltpu.VMEM((2, 2, 2 * rows, panel), jnp.bfloat16),
-            pltpu.VMEM(b.shape, jnp.bfloat16),
-            pltpu.VMEM((2, 2 * rows, 2 * quarter), jnp.float32),
-            pltpu.VMEM((4, rows, width), jnp.bfloat16),
-            pltpu.SemaphoreType.DMA((2, PARTS)),
-            pltpu.SemaphoreType.DMA,
-            pltpu.SemaphoreType.DMA((2,)),
-            pltpu.SemaphoreType.DMA((4,)),
-        ],
-        compiler_params=pltpu.CompilerParams(vmem_limit_bytes=59 * MIB),
-        cost_estimate=SMALL,
-        name="rest_products",
-    )(meta, *xs, rest, b)
+        name=name,
+    )(meta, *xs, *operands)
 
 
 def assemble_kernel(place_ref, mask_ref, *refs):
@@ -642,14 +576,15 @@
         ]
 
     done_at, rest_at = jnp.where(left, 3, 0), jnp.where(left, 0, 5)
-    meta = jnp.stack([is_end, first_in, second_in, done_at, rest_at, *fourth]).astype(jnp.int32)
-    *done, rest = half_products(meta, xs, total, fwd_first, far_first, fwd_second, 5)
-    done = exchanged(done)
+    halves = [total, fwd_first, far_first, fwd_second]
+    meta = jnp.stack([is_end, first_in, second_in, done_at, *fourth]).astype(jnp.int32)
+    done = exchanged(last_products(meta, xs, *halves, None, 5, "half_products"))
     far_second, done[1] = together(far_second, done[1])
     keep_wide = widen(keep_mask, block)
     out = assembled(jnp.stack([q, done_at]).astype(jnp.int32), keep_wide, done)
-    meta = jnp.stack([is_end, last_in, rest_at, *fourth, extra_in, extra_panel]).astype(jnp.int32)
-    rest = exchanged(rest_products(meta, xs, rest, far_second, own_a.shape[1]))
+    meta = [is_end, first_in, second_in, rest_at, *fourth, last_in, extra_in, extra_panel]
+    meta = jnp.stack(meta).astype(jnp.int32)
+    rest = exchanged(last_products(meta, xs, *halves, far_second, 3, "rest_products"))
     return assembled(jnp.stack([q, rest_at]).astype(jnp.int32), keep_wide, rest, out)
 
 

time: 155 us -> 154 us (level); the launches traced: 152 us -> 153 us
  transfers between devices with their start and end apart: 21 -> 21, of which waited for: 12 -> 11; matrix products, arithmetic and copies ran while one was open for 4% -> 4% of each run, Pallas kernels for 27% -> 27%
where the time goes in v17:
time: 154 us; the launch traced here: 153 us
  waiting for transfers between devices  76.2 us (49%)
  Pallas kernels  45.7 us (30%)
  starting transfers between devices  22.6 us (15%)
  local copies, waits for them, and re-layouts  8.09 us (5%)
    ppermute x15, waiting for transfers between devices, line(): return lax.ppermute(value, 'grid', pairs)  71.7 us
    ppermute x15, starting transfers between devices, line(): return lax.ppermute(value, 'grid', pairs)  20.8 us
    pallas_call x1, Pallas kernels, whole_products(): pl.pallas_call(functools.partial(whole_kernel, plan), out_shape=jax.Shape...  13.6 us
    pallas_call x2, Pallas kernels, last_products(): pl.pallas_call(functools.partial(last_kernel, b is not None), out_shape=[...  12.2 us
    pallas_call x1, Pallas kernels, masked_x(): pl.pallas_call(mask_kernel, grid_spec=pltpu.PrefetchScalarGridSpec(num_sc...  6.87 us
    pallas_call x3, Pallas kernels, packed(): pl.pallas_call(functools.partial(pack_kernel, plan, len(sources)), out_sh...  5.07 us
    pallas_call x2, Pallas kernels, b_strips(): pl.pallas_call(strips_kernel, out_shape=jax.ShapeDtypeStruct(shape, jnp.b...  4.39 us
    pallas_call x2, Pallas kernels, assembled(): pl.pallas_call(assemble_kernel, out_shape=jax.ShapeDtypeStruct((rows, col...  3.63 us
  transfers between devices with their start and end apart: 21, of which 11 were waited for; matrix products, arithmetic and copies ran while one was open for 4% of the time, Pallas kernels for 27%

profile of v17, /device:TPU:0, one launch (start us, length us, event | category | flops | bytes accessed | tf_op | source)
XLA Modules:
  0.0 153.3 jit_solution(16409688349210190415)
XLA Ops:
  0.0 2.2 %b_strips.2 = bf16[512,1024]{1,0:T(8,128)(2,1)} custom-call(s32[1]{0:T(128)} %bitcast.12.quarter_ref, bf16[512,4096]{1,0:T(8,128)(2,1)} %w_ref.2), custom_call_target="tpu_custom_call" | custom-call | flops 1000 | bytes 1000 | tf_op jit(solution)/shard_map/b_strips/pallas_call | solution.py:86
  2.2 3.0 %collective-permute-start = (bf16[512,1024]{1,0:T(8,128)(2,1)}, bf16[512,1024]{1,0:T(8,128)(2,1)}, u32[]{:S(2)}, u32[]{:S(2)}) collective-permute-start(bf16[512,1024]{1,0:T(8,128)(2,1)} %b_strips.2), channel_id=1, source_target_pairs={{0,2},{2,0},{4,6},{6,4},{8,10},{10,8},{12,14},{14,12},{1,3},{3,1},... | collective-permute-start | bytes 3145736 | tf_op jit(solution)/shard_map/ppermute | solution.py:495
  5.2 2.2 %b_strips.3.refs_5_ = bf16[512,1024]{1,0:T(8,128)(2,1)} custom-call(s32[1]{0:T(128)} %bitcast.quarter_ref, bf16[512,4096]{1,0:T(8,128)(2,1)} %w_ref.2), custom_call_target="tpu_custom_call" | custom-call | flops 1000 | bytes 1000 | tf_op jit(solution)/shard_map/b_strips/pallas_call | solution.py:86
  7.4 1.6 %collective-permute-start.1 = (bf16[512,1024]{1,0:T(8,128)(2,1)}, bf16[512,1024]{1,0:T(8,128)(2,1)S(1)}, u32[]{:S(2)}, u32[]{:S(2)}) collective-permute-start(bf16[512,1024]{1,0:T(8,128)(2,1)} %b_strips.3.refs_5_), channel_id=1, source_target_pairs={{0,4},{2,6},{4,0},{6,2},{8,12},{10,14},{12,8},{14,10},{1,5},{3,7},... | collective-permute-start | bytes 3145736 | tf_op jit(solution)/shard_map/ppermute | solution.py:495
  10.8 6.9 %masked_x.1.refs_0_ = bf16[512,4096]{1,0:T(8,128)(2,1)} custom-call(s32[1]{0:T(128)} %bitcast.11.first_ref, f32[8,1,4096]{2,1,0:T(1,128)} %reshape.17.mask_ref, bf16[512,4096]{1,0:T(8,128)(2,1)} %x_ref.1), custom_call_target="tpu_custom_call" | custom-call | flops 1000 | bytes 1000 | tf_op jit(solution)/shard_map/masked_x/pallas_call | solution.py:149
  17.7 3.1 %fusion = (bf16[128,4096]{1,0:T(8,128)(2,1)}, bf16[128,4096]{1,0:T(8,128)(2,1)}) fusion(bf16[512,4096]{1,0:T(8,128)(2,1)} %masked_x.1.refs_0_), kind=kLoop, calls=%fused_computation.4 | loop fusion | bytes 4194304 | tf_op jit(solution)/shard_map/slice | solution.py:510
  20.7 8.0 %collective-permute-done.refs_6_ = bf16[512,1024]{1,0:T(8,128)(2,1)} collective-permute-done((bf16[512,1024]{1,0:T(8,128)(2,1)}, bf16[512,1024]{1,0:T(8,128)(2,1)}, u32[]{:S(2)}, u32[]{:S(2)}) %collective-permute-start) | collective-permute-done | bytes 1048608 | tf_op jit(solution)/shard_map/ppermute | solution.py:495
  28.7 3.6 %collective-permute-done.1.refs_0_.refs_2_.refs_9_ = bf16[512,1024]{1,0:T(8,128)(2,1)S(1)} collective-permute-done((bf16[512,1024]{1,0:T(8,128)(2,1)}, bf16[512,1024]{1,0:T(8,128)(2,1)S(1)}, u32[]{:S(2)}, u32[]{:S(2)}) %collective-permute-start.1) | collective-permute-done | bytes 1048608 | tf_op jit(solution)/shard_map/ppermute | solution.py:495
  32.3 1.6 %collective-permute-start.2 = (bf16[512,1024]{1,0:T(8,128)(2,1)}, bf16[512,1024]{1,0:T(8,128)(2,1)S(1)}, u32[]{:S(2)}, u32[]{:S(2)}) collective-permute-start(bf16[512,1024]{1,0:T(8,128)(2,1)} %collective-permute-done.refs_6_), channel_id=1, source_target_pairs={{0,4},{2,6},{4,0},{6,2},{8,12},{10,14},{12,8},{14,10},{1,5},{3,7},... | collective-permute-start | bytes 3145736 | tf_op jit(solution)/shard_map/ppermute | solution.py:495
  33.9 1.7 %collective-permute-start.8 = (bf16[512,1024]{1,0:T(8,128)(2,1)}, bf16[512,1024]{1,0:T(8,128)(2,1)}, u32[]{:S(2)}, u32[]{:S(2)}) collective-permute-start(bf16[512,1024]{1,0:T(8,128)(2,1)} %collective-permute-done.refs_6_), channel_id=1, source_target_pairs={{4,8},{6,10},{8,4},{10,6},{5,9},{7,11},{9,5},{11,7},{20,24},{22,26... | collective-permute-start | bytes 3145736 | tf_op jit(solution)/shard_map/ppermute | solution.py:495
  36.1 1.5 collective-permute-start.4
  37.6 1.3 collective-permute-start.9
  39.0 19.6 %collective-permute-done.2.refs_1_.refs_3_.refs_10_ = bf16[512,1024]{1,0:T(8,128)(2,1)S(1)} collective-permute-done((bf16[512,1024]{1,0:T(8,128)(2,1)}, bf16[512,1024]{1,0:T(8,128)(2,1)S(1)}, u32[]{:S(2)}, u32[]{:S(2)}) %collective-permute-start.2) | collective-permute-done | bytes 1048608 | tf_op jit(solution)/shard_map/ppermute | solution.py:495
  58.6 3.2 %packed.4 = (bf16[512,1280]{1,0:T(8,128)(2,1)}, bf16[512,1024]{1,0:T(8,128)(2,1)}) custom-call(s32[2]{0:T(128)S(1)} %pad_add_fusion.1.meta_ref, bf16[512,1024]{1,0:T(8,128)(2,1)S(1)} %collective-permute-done.7.refs_0_.refs_7_, bf16[512,1024]{1,0:T(8,128)(2,1)} %collective-permute-done.8.refs_1_.refs_8_, ...), custom_call_target="tpu_custom_call" | custom-call | flops 1000 | bytes 1000 | tf_op jit(solution)/shard_map/packed/pallas_call | solution.py:129
  61.9 2.9 %collective-permute-done.9.refs_12_ = bf16[512,384]{1,0:T(8,128)(2,1)} collective-permute-done((bf16[512,384]{1,0:T(8,128)(2,1)S(1)}, bf16[512,384]{1,0:T(8,128)(2,1)}, u32[]{:S(2)}, u32[]{:S(2)}) %collective-permute-start.9) | collective-permute-done | bytes 393248 | tf_op jit(solution)/shard_map/ppermute | solution.py:495
  64.8 1.3 collective-permute-start.10
  66.1 1.7 %collective-permute-start.11 = (bf16[512,1024]{1,0:T(8,128)(2,1)}, bf16[512,1024]{1,0:T(8,128)(2,1)}, u32[]{:S(2)}, u32[]{:S(2)}) collective-permute-start(bf16[512,1024]{1,0:T(8,128)(2,1)} %get-tuple-element.44), channel_id=1, source_target_pairs={{4,8},{6,10},{8,4},{10,6},{5,9},{7,11},{9,5},{11,7},{20,24},{22,26... | collective-permute-start | bytes 3145736 | tf_op jit(solution)/shard_map/ppermute | solution.py:495
  69.0 12.8 %collective-permute-done.4.refs_2_ = bf16[128,4096]{1,0:T(8,128)(2,1)} collective-permute-done((bf16[128,4096]{1,0:T(8,128)(2,1)}, bf16[128,4096]{1,0:T(8,128)(2,1)}, u32[]{:S(2)}, u32[]{:S(2)}) %collective-permute-start.4) | collective-permute-done | bytes 1048608 | tf_op jit(solution)/shard_map/ppermute | solution.py:495
  83.0 1.3 collective-permute-start.12
  85.1 1.2 collective-permute-done.6.refs_4_
  86.3 9.7 %collective-permute-done.10.refs_11_ = bf16[512,1280]{1,0:T(8,128)(2,1)} collective-permute-done((bf16[512,1280]{1,0:T(8,128)(2,1)}, bf16[512,1280]{1,0:T(8,128)(2,1)}, u32[]{:S(2)}, u32[]{:S(2)}) %collective-permute-start.10) | collective-permute-done | bytes 1310752 | tf_op jit(solution)/shard_map/ppermute | solution.py:495
  96.0 13.6 %whole_products.1.refs_5_ = f32[2,512,1024]{2,1,0:T(8,128)} custom-call(s32[14]{0:T(128)} %stack.136.meta_ref, bf16[512,4096]{1,0:T(8,128)(2,1)} %masked_x.1.refs_0_, bf16[128,4096]{1,0:T(8,128)(2,1)} %collective-permute-done.3.refs_1_, bf16[128,4096]{1,0:T(8,128)(2,1)} %collective-permute-done.4.refs_2_, bf16[128,4096]{1,0:T(8,128)(2,1)} %collective-permute-done.5.refs_3_, ...), custom_call_target="tpu_custom_call" | custom-call | flops 6000000000 | bytes 37748736 | tf_op jit(solution)/shard_map/whole_products/pallas_call | solution.py:277
  110.4 1.3 collective-permute-start.14
  112.4 5.7 %collective-permute-done.12.refs_7_ = bf16[512,1024]{1,0:T(8,128)(2,1)} collective-permute-done((bf16[512,1024]{1,0:T(8,128)(2,1)}, bf16[512,1024]{1,0:T(8,128)(2,1)}, u32[]{:S(2)}, u32[]{:S(2)}) %collective-permute-start.12) | collective-permute-done | bytes 1048608 | tf_op jit(solution)/shard_map/ppermute | solution.py:495
  118.1 5.5 %half_products.1 = (bf16[256,640]{1,0:T(8,128)(2,1)}, bf16[256,640]{1,0:T(8,128)(2,1)}, bf16[256,640]{1,0:T(8,128)(2,1)}, bf16[256,640]{1,0:T(8,128)(2,1)}) custom-call(s32[8]{0:T(128)} %stack.144.meta_ref, bf16[512,4096]{1,0:T(8,128)(2,1)} %masked_x.1.refs_0_, bf16[128,4096]{1,0:T(8,128)(2,1)} %collective-permute-done.3.refs_1_, ...), custom_call_target="tpu_custom_call" | custom-call | flops 1000 | bytes 1000 | tf_op jit(solution)/shard_map/half_products/pallas_call | solution.py:407
  123.6 1.5 collective-permute-start.19
  126.2 5.6 %collective-permute-done.14.refs_9_ = bf16[512,640]{1,0:T(8,128)(2,1)S(1)} collective-permute-done((bf16[512,640]{1,0:T(8,128)(2,1)S(1)}, bf16[512,640]{1,0:T(8,128)(2,1)S(1)}, u32[]{:S(2)}, u32[]{:S(2)}) %collective-permute-start.14) | collective-permute-done | bytes 655392 | tf_op jit(solution)/shard_map/ppermute | solution.py:495
  132.7 6.7 %rest_products.1 = (bf16[256,384]{1,0:T(8,128)(2,1)}, bf16[256,384]{1,0:T(8,128)(2,1)}, bf16[256,384]{1,0:T(8,128)(2,1)}, bf16[256,384]{1,0:T(8,128)(2,1)}) custom-call(s32[11]{0:T(128)} %stack.126.meta_ref, bf16[512,4096]{1,0:T(8,128)(2,1)} %masked_x.1.refs_0_, bf16[128,4096]{1,0:T(8,128)(2,1)} %collective-permute-done.3.refs_1_, ...), custom_call_target="tpu_custom_call" | custom-call | flops 1000 | bytes 1000 | tf_op jit(solution)/shard_map/rest_products/pallas_call | solution.py:407
  141.7 2.0 %assembled.2.refs_4_ = bf16[256,4096]{1,0:T(8,128)(2,1)} custom-call(s32[2]{0:T(128)S(1)} %get-tuple-element.60.place_ref, f32[4,1,4096]{2,1,0:T(1,128)S(1)} %reshape.15.mask_ref, bf16[256,640]{1,0:T(8,128)(2,1)S(1)} %copy-done.4, bf16[256,640]{1,0:T(8,128)(2,1)S(1)} %collective-permute-done.15.refs_1_, ...), custom_call_target="tpu_custom_call" | custom-call | flops 1000 | bytes 1000 | tf_op jit(solution)/shard_map/assembled/pallas_call | solution.py:454
  143.7 3.8 %collective-permute-done.17.refs_2_ = bf16[256,384]{1,0:T(8,128)(2,1)S(1)} collective-permute-done((bf16[256,384]{1,0:T(8,128)(2,1)}, bf16[256,384]{1,0:T(8,128)(2,1)S(1)}, u32[]{:S(2)}, u32[]{:S(2)}) %collective-permute-start.17) | collective-permute-done | bytes 196640 | tf_op jit(solution)/shard_map/ppermute | solution.py:495
  147.4 3.3 %collective-permute-done.18.refs_3_ = bf16[256,384]{1,0:T(8,128)(2,1)S(1)} collective-permute-done((bf16[256,384]{1,0:T(8,128)(2,1)}, bf16[256,384]{1,0:T(8,128)(2,1)S(1)}, u32[]{:S(2)}, u32[]{:S(2)}) %collective-permute-start.18) | collective-permute-done | bytes 196640 | tf_op jit(solution)/shard_map/ppermute | solution.py:575
  151.7 1.6 %assembled.3 = bf16[256,4096]{1,0:T(8,128)(2,1)} custom-call(s32[2]{0:T(128)S(1)} %get-tuple-element.59.place_ref, f32[4,1,4096]{2,1,0:T(1,128)S(1)} %reshape.15.mask_ref, bf16[256,384]{1,0:T(8,128)(2,1)S(1)} %copy-done.5, bf16[256,384]{1,0:T(8,128)(2,1)S(1)} %collective-permute-done.16.refs_1_, ...), custom_call_target="tpu_custom_call", output_to_operand_aliasing={{}: (6, {})} | custom-call | flops 1000 | bytes 1000 | tf_op jit(solution)/shard_map/assembled/pallas_call | solution.py:454
  (53 shorter events, 11.9 us)
Async XLA Ops:
  0.0 9.8 %copy-start.7 = (s32[8,64]{1,0:T(8,128)S(1)}, s32[8,64]{1,0:T(8,128)}, u32[]{:S(2)}) copy-start(s32[8,64]{1,0:T(8,128)} %param.6) | copy-start | bytes 6148
  2.2 26.5 %collective-permute-start = (bf16[512,1024]{1,0:T(8,128)(2,1)}, bf16[512,1024]{1,0:T(8,128)(2,1)}, u32[]{:S(2)}, u32[]{:S(2)}) collective-permute-start(bf16[512,1024]{1,0:T(8,128)(2,1)} %b_strips.2), channel_id=1, source_target_pairs={{0,2},{2,0},{4,6},{6,4},{8,10},{10,8},{12,14},{14,12},{1,3},{3,1},... | collective-permute-start | bytes 3145736 | tf_op jit(solution)/shard_map/ppermute | solution.py:495
  7.4 24.9 %collective-permute-start.1 = (bf16[512,1024]{1,0:T(8,128)(2,1)}, bf16[512,1024]{1,0:T(8,128)(2,1)S(1)}, u32[]{:S(2)}, u32[]{:S(2)}) collective-permute-start(bf16[512,1024]{1,0:T(8,128)(2,1)} %b_strips.3.refs_5_), channel_id=1, source_target_pairs={{0,4},{2,6},{4,0},{6,2},{8,12},{10,14},{12,8},{14,10},{1,5},{3,7},... | collective-permute-start | bytes 3145736 | tf_op jit(solution)/shard_map/ppermute | solution.py:495
  9.1 28.5 %collective-permute-start.7 = (bf16[512,1024]{1,0:T(8,128)(2,1)}, bf16[512,1024]{1,0:T(8,128)(2,1)S(1)}, u32[]{:S(2)}, u32[]{:S(2)}) collective-permute-start(bf16[512,1024]{1,0:T(8,128)(2,1)} %b_strips.3.refs_5_), channel_id=1, source_target_pairs={{4,8},{6,10},{8,4},{10,6},{5,9},{7,11},{9,5},{11,7},{20,24},{22,26... | collective-permute-start | bytes 3145736 | tf_op jit(solution)/shard_map/ppermute | solution.py:495
  32.3 52.1 %copy-start.1 = (bf16[512,1024]{1,0:T(8,128)(2,1)}, bf16[512,1024]{1,0:T(8,128)(2,1)S(1)}, u32[]{:S(2)}) copy-start(bf16[512,1024]{1,0:T(8,128)(2,1)S(1)} %collective-permute-done.1.refs_0_.refs_2_.refs_9_) | copy-start | bytes 3145732
  32.3 26.3 %collective-permute-start.2 = (bf16[512,1024]{1,0:T(8,128)(2,1)}, bf16[512,1024]{1,0:T(8,128)(2,1)S(1)}, u32[]{:S(2)}, u32[]{:S(2)}) collective-permute-start(bf16[512,1024]{1,0:T(8,128)(2,1)} %collective-permute-done.refs_6_), channel_id=1, source_target_pairs={{0,4},{2,6},{4,0},{6,2},{8,12},{10,14},{12,8},{14,10},{1,5},{3,7},... | collective-permute-start | bytes 3145736 | tf_op jit(solution)/shard_map/ppermute | solution.py:495
  33.9 24.7 %collective-permute-start.8 = (bf16[512,1024]{1,0:T(8,128)(2,1)}, bf16[512,1024]{1,0:T(8,128)(2,1)}, u32[]{:S(2)}, u32[]{:S(2)}) collective-permute-start(bf16[512,1024]{1,0:T(8,128)(2,1)} %collective-permute-done.refs_6_), channel_id=1, source_target_pairs={{4,8},{6,10},{8,4},{10,6},{5,9},{7,11},{9,5},{11,7},{20,24},{22,26... | collective-permute-start | bytes 3145736 | tf_op jit(solution)/shard_map/ppermute | solution.py:495
  35.6 33.4 %collective-permute-start.3 = (bf16[128,4096]{1,0:T(8,128)(2,1)}, bf16[128,4096]{1,0:T(8,128)(2,1)}, u32[]{:S(2)}, u32[]{:S(2)}) collective-permute-start(bf16[128,4096]{1,0:T(8,128)(2,1)} %get-tuple-element.35), channel_id=1, source_target_pairs={{0,2},{2,0},{4,6},{6,4},{8,10},{10,8},{12,14},{14,12},{1,3},{3,1},... | collective-permute-start | bytes 3145736 | tf_op jit(solution)/shard_map/ppermute | solution.py:495
  36.1 45.7 %collective-permute-start.4 = (bf16[128,4096]{1,0:T(8,128)(2,1)}, bf16[128,4096]{1,0:T(8,128)(2,1)}, u32[]{:S(2)}, u32[]{:S(2)}) collective-permute-start(bf16[128,4096]{1,0:T(8,128)(2,1)} %get-tuple-element.36), channel_id=1, source_target_pairs={{0,2},{2,0},{4,6},{6,4},{8,10},{10,8},{12,14},{14,12},{1,3},{3,1},... | collective-permute-start | bytes 3145736 | tf_op jit(solution)/shard_map/ppermute | solution.py:495
  37.6 44.2 %copy-start.3 = (bf16[512,1024]{1,0:T(8,128)(2,1)}, bf16[512,1024]{1,0:T(8,128)(2,1)S(1)}, u32[]{:S(2)}) copy-start(bf16[512,1024]{1,0:T(8,128)(2,1)S(1)} %collective-permute-done.7.refs_0_.refs_7_) | copy-start | bytes 3145732
  37.6 27.2 %collective-permute-start.9 = (bf16[512,384]{1,0:T(8,128)(2,1)S(1)}, bf16[512,384]{1,0:T(8,128)(2,1)}, u32[]{:S(2)}, u32[]{:S(2)}) collective-permute-start(bf16[512,384]{1,0:T(8,128)(2,1)S(1)} %slice.14), channel_id=1, source_target_pairs={{4,0},{6,2},{8,12},{10,14},{5,1},{7,3},{9,13},{11,15},{20,16},{22,... | collective-permute-start | bytes 1179656 | tf_op jit(solution)/shard_map/ppermute | solution.py:495
  58.6 37.4 %copy-start.2 = (bf16[512,1024]{1,0:T(8,128)(2,1)}, bf16[512,1024]{1,0:T(8,128)(2,1)S(1)}, u32[]{:S(2)}) copy-start(bf16[512,1024]{1,0:T(8,128)(2,1)S(1)} %collective-permute-done.2.refs_1_.refs_3_.refs_10_) | copy-start | bytes 3145732
  64.8 31.2 %collective-permute-start.10 = (bf16[512,1280]{1,0:T(8,128)(2,1)}, bf16[512,1280]{1,0:T(8,128)(2,1)}, u32[]{:S(2)}, u32[]{:S(2)}) collective-permute-start(bf16[512,1280]{1,0:T(8,128)(2,1)} %get-tuple-element.41), channel_id=1, source_target_pairs={{4,0},{6,2},{8,12},{10,14},{5,1},{7,3},{9,13},{11,15},{20,16},{22,... | collective-permute-start | bytes 3932168 | tf_op jit(solution)/shard_map/ppermute | solution.py:495
  66.1 16.9 %collective-permute-start.11 = (bf16[512,1024]{1,0:T(8,128)(2,1)}, bf16[512,1024]{1,0:T(8,128)(2,1)}, u32[]{:S(2)}, u32[]{:S(2)}) collective-permute-start(bf16[512,1024]{1,0:T(8,128)(2,1)} %get-tuple-element.44), channel_id=1, source_target_pairs={{4,8},{6,10},{8,4},{10,6},{5,9},{7,11},{9,5},{11,7},{20,24},{22,26... | collective-permute-start | bytes 3145736 | tf_op jit(solution)/shard_map/ppermute | solution.py:495
  81.8 3.3 %collective-permute-start.5 = (bf16[128,4096]{1,0:T(8,128)(2,1)}, bf16[128,4096]{1,0:T(8,128)(2,1)}, u32[]{:S(2)}, u32[]{:S(2)}) collective-permute-start(bf16[128,4096]{1,0:T(8,128)(2,1)} %collective-permute-done.3.refs_1_), channel_id=1, source_target_pairs={{0,1},{1,0},{2,3},{3,2},{4,5},{5,4},{6,7},{7,6},{8,9},{9,8},{10,11... | collective-permute-start | bytes 3145736 | tf_op jit(solution)/shard_map/ppermute | solution.py:538
  81.8 4.5 %collective-permute-start.6 = (bf16[128,4096]{1,0:T(8,128)(2,1)}, bf16[128,4096]{1,0:T(8,128)(2,1)}, u32[]{:S(2)}, u32[]{:S(2)}) collective-permute-start(bf16[128,4096]{1,0:T(8,128)(2,1)} %collective-permute-done.4.refs_2_), channel_id=1, source_target_pairs={{0,1},{1,0},{2,3},{3,2},{4,5},{5,4},{6,7},{7,6},{8,9},{9,8},{10,11... | collective-permute-start | bytes 3145736 | tf_op jit(solution)/shard_map/ppermute | solution.py:538
  82.3 27.4 %collective-permute-start.13 = (bf16[512,1024]{1,0:T(8,128)(2,1)}, bf16[512,1024]{1,0:T(8,128)(2,1)S(1)}, u32[]{:S(2)}, u32[]{:S(2)}) collective-permute-start(bf16[512,1024]{1,0:T(8,128)(2,1)} %packed.3), channel_id=1, source_target_pairs={{4,8},{6,10},{8,4},{10,6},{5,9},{7,11},{9,5},{11,7},{20,24},{22,26... | collective-permute-start | bytes 3145736 | tf_op jit(solution)/shard_map/ppermute | solution.py:495
  83.0 35.0 %collective-permute-start.12 = (bf16[512,1024]{1,0:T(8,128)(2,1)}, bf16[512,1024]{1,0:T(8,128)(2,1)}, u32[]{:S(2)}, u32[]{:S(2)}) collective-permute-start(bf16[512,1024]{1,0:T(8,128)(2,1)} %collective-permute-done.11.refs_6_), channel_id=1, source_target_pairs={{4,0},{6,2},{8,12},{10,14},{5,1},{7,3},{9,13},{11,15},{20,16},{22,... | collective-permute-start | bytes 3145736 | tf_op jit(solution)/shard_map/ppermute | solution.py:495
  109.7 8.4 %copy-start = (bf16[512,1024]{1,0:T(8,128)(2,1)}, bf16[512,1024]{1,0:T(8,128)(2,1)S(1)}, u32[]{:S(2)}) copy-start(bf16[512,1024]{1,0:T(8,128)(2,1)S(1)} %collective-permute-done.13.refs_0_.refs_8_) | copy-start | bytes 3145732
  110.4 21.4 %collective-permute-start.14 = (bf16[512,640]{1,0:T(8,128)(2,1)S(1)}, bf16[512,640]{1,0:T(8,128)(2,1)S(1)}, u32[]{:S(2)}, u32[]{:S(2)}) collective-permute-start(bf16[512,640]{1,0:T(8,128)(2,1)S(1)} %packed.5), channel_id=1, source_target_pairs={{4,0},{6,2},{8,12},{10,14},{5,1},{7,3},{9,13},{11,15},{20,16},{22,... | collective-permute-start | bytes 1966088 | tf_op jit(solution)/shard_map/ppermute | solution.py:495
  123.6 8.2 %collective-permute-start.15 = (bf16[256,640]{1,0:T(8,128)(2,1)}, bf16[256,640]{1,0:T(8,128)(2,1)S(1)}, u32[]{:S(2)}, u32[]{:S(2)}) collective-permute-start(bf16[256,640]{1,0:T(8,128)(2,1)} %get-tuple-element.47), channel_id=1, source_target_pairs={{0,1},{1,0},{2,3},{3,2},{4,5},{5,4},{6,7},{7,6},{8,9},{9,8},{10,11... | collective-permute-start | bytes 983048 | tf_op jit(solution)/shard_map/ppermute | solution.py:573
  123.6 18.0 %collective-permute-start.19 = (bf16[256,640]{1,0:T(8,128)(2,1)}, bf16[256,640]{1,0:T(8,128)(2,1)S(1)}, u32[]{:S(2)}, u32[]{:S(2)}) collective-permute-start(bf16[256,640]{1,0:T(8,128)(2,1)} %get-tuple-element.55), channel_id=1, source_target_pairs={{0,2},{2,0},{4,6},{6,4},{8,10},{10,8},{12,14},{14,12},{1,3},{3,1},... | collective-permute-start | bytes 983048 | tf_op jit(solution)/shard_map/ppermute | solution.py:495
  125.2 16.5 %collective-permute-start.20 = (bf16[256,640]{1,0:T(8,128)(2,1)}, bf16[256,640]{1,0:T(8,128)(2,1)S(1)}, u32[]{:S(2)}, u32[]{:S(2)}) collective-permute-start(bf16[256,640]{1,0:T(8,128)(2,1)} %get-tuple-element.56), channel_id=1, source_target_pairs={{0,3},{1,2},{2,1},{3,0},{4,7},{5,6},{6,5},{7,4},{8,11},{9,10},{10,... | collective-permute-start | bytes 983048 | tf_op jit(solution)/shard_map/ppermute | solution.py:575
  126.2 15.1 %copy-start.8 = (s32[4,64]{1,0:T(4,128)S(1)}, s32[4,64]{1,0:T(4,128)}, u32[]{:S(2)}) copy-start(s32[4,64]{1,0:T(4,128)} %param.7) | copy-start | bytes 3076
  126.2 15.4 %copy-start.4 = (bf16[256,640]{1,0:T(8,128)(2,1)S(1)}, bf16[256,640]{1,0:T(8,128)(2,1)}, u32[]{:S(2)}) copy-start(bf16[256,640]{1,0:T(8,128)(2,1)} %get-tuple-element.53.refs_0_) | copy-start | bytes 983044
  131.8 0.9 copy-start.6
  139.4 4.3 %collective-permute-start.16 = (bf16[256,384]{1,0:T(8,128)(2,1)}, bf16[256,384]{1,0:T(8,128)(2,1)S(1)}, u32[]{:S(2)}, u32[]{:S(2)}) collective-permute-start(bf16[256,384]{1,0:T(8,128)(2,1)} %get-tuple-element.50), channel_id=1, source_target_pairs={{0,1},{1,0},{2,3},{3,2},{4,5},{5,4},{6,7},{7,6},{8,9},{9,8},{10,11... | collective-permute-start | bytes 589832 | tf_op jit(solution)/shard_map/ppermute | solution.py:573
  139.5 8.0 %collective-permute-start.17 = (bf16[256,384]{1,0:T(8,128)(2,1)}, bf16[256,384]{1,0:T(8,128)(2,1)S(1)}, u32[]{:S(2)}, u32[]{:S(2)}) collective-permute-start(bf16[256,384]{1,0:T(8,128)(2,1)} %get-tuple-element.51), channel_id=1, source_target_pairs={{0,2},{2,0},{4,6},{6,4},{8,10},{10,8},{12,14},{14,12},{1,3},{3,1},... | collective-permute-start | bytes 589832 | tf_op jit(solution)/shard_map/ppermute | solution.py:495
  140.5 10.3 %collective-permute-start.18 = (bf16[256,384]{1,0:T(8,128)(2,1)}, bf16[256,384]{1,0:T(8,128)(2,1)S(1)}, u32[]{:S(2)}, u32[]{:S(2)}) collective-permute-start(bf16[256,384]{1,0:T(8,128)(2,1)} %get-tuple-element.52), channel_id=1, source_target_pairs={{0,3},{1,2},{2,1},{3,0},{4,7},{5,6},{6,5},{7,4},{8,11},{9,10},{10,... | collective-permute-start | bytes 589832 | tf_op jit(solution)/shard_map/ppermute | solution.py:575
  150.7 0.9 copy-start.5

commit v18 on v17

--- a/solution.py
+++ b/solution.py
@@ -585,6 +585,8 @@
     meta = [is_end, first_in, second_in, rest_at, *fourth, last_in, extra_in, extra_panel]
     meta = jnp.stack(meta).astype(jnp.int32)
     rest = exchanged(last_products(meta, xs, *halves, far_second, 3, "rest_products"))
+    rest[2], rest[3] = together(rest[2], rest[3])
+    rest[0], rest[1], rest[2] = together(rest[0], rest[1], rest[2])
     return assembled(jnp.stack([q, rest_at]).astype(jnp.int32), keep_wide, rest, out)
 
 

time: 154 us -> 154 us (level); the launches traced: 153 us -> 151 us
  waiting for transfers between devices: 76.2 us -> 73.7 us
    ppermute x2, waiting for transfers between devices: 3.31 us -> 1.38 us  [exchanged(): lax.ppermute(pieces[3], ('grid', 'depth'), opposite)]
  transfers between devices with their start and end apart: 21 -> 21, of which waited for: 11 -> 11; matrix products, arithmetic and copies ran while one was open for 4% -> 4% of each run, Pallas kernels for 27% -> 28%
where the time goes in v18:
time: 154 us; the launch traced here: 151 us
  waiting for transfers between devices  73.7 us (48%)
  Pallas kernels  45.7 us (30%)
  starting transfers between devices  22.9 us (15%)
  local copies, waits for them, and re-layouts  8.09 us (5%)
    ppermute x15, waiting for transfers between devices, line(): return lax.ppermute(value, 'grid', pairs)  71.2 us
    ppermute x15, starting transfers between devices, line(): return lax.ppermute(value, 'grid', pairs)  20.8 us
    pallas_call x1, Pallas kernels, whole_products(): pl.pallas_call(functools.partial(whole_kernel, plan), out_shape=jax.Shape...  13.6 us
    pallas_call x2, Pallas kernels, last_products(): pl.pallas_call(functools.partial(last_kernel, b is not None), out_shape=[...  12.2 us
    pallas_call x1, Pallas kernels, masked_x(): pl.pallas_call(mask_kernel, grid_spec=pltpu.PrefetchScalarGridSpec(num_sc...  6.87 us
    pallas_call x3, Pallas kernels, packed(): pl.pallas_call(functools.partial(pack_kernel, plan, len(sources)), out_sh...  5.07 us
    pallas_call x2, Pallas kernels, b_strips(): pl.pallas_call(strips_kernel, out_shape=jax.ShapeDtypeStruct(shape, jnp.b...  4.39 us
    pallas_call x2, Pallas kernels, assembled(): pl.pallas_call(assemble_kernel, out_shape=jax.ShapeDtypeStruct((rows, col...  3.63 us
  transfers between devices with their start and end apart: 21, of which 11 were waited for; matrix products, arithmetic and copies ran while one was open for 4% of the time, Pallas kernels for 28%

profile of v18, /device:TPU:0, one launch (start us, length us, event | category | flops | bytes accessed | tf_op | source)
XLA Modules:
  0.0 151.1 jit_solution(8237826175154242570)
XLA Ops:
  0.0 2.2 %b_strips.2 = bf16[512,1024]{1,0:T(8,128)(2,1)} custom-call(s32[1]{0:T(128)} %bitcast.12.quarter_ref, bf16[512,4096]{1,0:T(8,128)(2,1)} %w_ref.2), custom_call_target="tpu_custom_call" | custom-call | flops 1000 | bytes 1000 | tf_op jit(solution)/shard_map/b_strips/pallas_call | solution.py:86
  2.2 3.0 %collective-permute-start = (bf16[512,1024]{1,0:T(8,128)(2,1)}, bf16[512,1024]{1,0:T(8,128)(2,1)}, u32[]{:S(2)}, u32[]{:S(2)}) collective-permute-start(bf16[512,1024]{1,0:T(8,128)(2,1)} %b_strips.2), channel_id=1, source_target_pairs={{0,2},{2,0},{4,6},{6,4},{8,10},{10,8},{12,14},{14,12},{1,3},{3,1},... | collective-permute-start | bytes 3145736 | tf_op jit(solution)/shard_map/ppermute | solution.py:495
  5.2 2.2 %b_strips.3.refs_5_ = bf16[512,1024]{1,0:T(8,128)(2,1)} custom-call(s32[1]{0:T(128)} %bitcast.quarter_ref, bf16[512,4096]{1,0:T(8,128)(2,1)} %w_ref.2), custom_call_target="tpu_custom_call" | custom-call | flops 1000 | bytes 1000 | tf_op jit(solution)/shard_map/b_strips/pallas_call | solution.py:86
  7.4 1.6 %collective-permute-start.1 = (bf16[512,1024]{1,0:T(8,128)(2,1)}, bf16[512,1024]{1,0:T(8,128)(2,1)S(1)}, u32[]{:S(2)}, u32[]{:S(2)}) collective-permute-start(bf16[512,1024]{1,0:T(8,128)(2,1)} %b_strips.3.refs_5_), channel_id=1, source_target_pairs={{0,4},{2,6},{4,0},{6,2},{8,12},{10,14},{12,8},{14,10},{1,5},{3,7},... | collective-permute-start | bytes 3145736 | tf_op jit(solution)/shard_map/ppermute | solution.py:495
  10.8 6.9 %masked_x.1.refs_0_ = bf16[512,4096]{1,0:T(8,128)(2,1)} custom-call(s32[1]{0:T(128)} %bitcast.11.first_ref, f32[8,1,4096]{2,1,0:T(1,128)} %reshape.17.mask_ref, bf16[512,4096]{1,0:T(8,128)(2,1)} %x_ref.1), custom_call_target="tpu_custom_call" | custom-call | flops 1000 | bytes 1000 | tf_op jit(solution)/shard_map/masked_x/pallas_call | solution.py:149
  17.7 3.1 %fusion = (bf16[128,4096]{1,0:T(8,128)(2,1)}, bf16[128,4096]{1,0:T(8,128)(2,1)}) fusion(bf16[512,4096]{1,0:T(8,128)(2,1)} %masked_x.1.refs_0_), kind=kLoop, calls=%fused_computation.4 | loop fusion | bytes 4194304 | tf_op jit(solution)/shard_map/slice | solution.py:510
  20.7 8.0 %collective-permute-done.refs_6_ = bf16[512,1024]{1,0:T(8,128)(2,1)} collective-permute-done((bf16[512,1024]{1,0:T(8,128)(2,1)}, bf16[512,1024]{1,0:T(8,128)(2,1)}, u32[]{:S(2)}, u32[]{:S(2)}) %collective-permute-start) | collective-permute-done | bytes 1048608 | tf_op jit(solution)/shard_map/ppermute | solution.py:495
  28.7 3.6 %collective-permute-done.1.refs_0_.refs_2_.refs_9_ = bf16[512,1024]{1,0:T(8,128)(2,1)S(1)} collective-permute-done((bf16[512,1024]{1,0:T(8,128)(2,1)}, bf16[512,1024]{1,0:T(8,128)(2,1)S(1)}, u32[]{:S(2)}, u32[]{:S(2)}) %collective-permute-start.1) | collective-permute-done | bytes 1048608 | tf_op jit(solution)/shard_map/ppermute | solution.py:495
  32.3 1.6 %collective-permute-start.2 = (bf16[512,1024]{1,0:T(8,128)(2,1)}, bf16[512,1024]{1,0:T(8,128)(2,1)S(1)}, u32[]{:S(2)}, u32[]{:S(2)}) collective-permute-start(bf16[512,1024]{1,0:T(8,128)(2,1)} %collective-permute-done.refs_6_), channel_id=1, source_target_pairs={{0,4},{2,6},{4,0},{6,2},{8,12},{10,14},{12,8},{14,10},{1,5},{3,7},... | collective-permute-start | bytes 3145736 | tf_op jit(solution)/shard_map/ppermute | solution.py:495
  33.9 1.7 %collective-permute-start.8 = (bf16[512,1024]{1,0:T(8,128)(2,1)}, bf16[512,1024]{1,0:T(8,128)(2,1)}, u32[]{:S(2)}, u32[]{:S(2)}) collective-permute-start(bf16[512,1024]{1,0:T(8,128)(2,1)} %collective-permute-done.refs_6_), channel_id=1, source_target_pairs={{4,8},{6,10},{8,4},{10,6},{5,9},{7,11},{9,5},{11,7},{20,24},{22,26... | collective-permute-start | bytes 3145736 | tf_op jit(solution)/shard_map/ppermute | solution.py:495
  36.1 1.5 %collective-permute-start.4 = (bf16[128,4096]{1,0:T(8,128)(2,1)}, bf16[128,4096]{1,0:T(8,128)(2,1)}, u32[]{:S(2)}, u32[]{:S(2)}) collective-permute-start(bf16[128,4096]{1,0:T(8,128)(2,1)} %get-tuple-element.41), channel_id=1, source_target_pairs={{0,2},{2,0},{4,6},{6,4},{8,10},{10,8},{12,14},{14,12},{1,3},{3,1},... | collective-permute-start | bytes 3145736 | tf_op jit(solution)/shard_map/ppermute | solution.py:495
  37.6 1.3 collective-permute-start.9
  39.0 19.6 %collective-permute-done.2.refs_1_.refs_3_.refs_10_ = bf16[512,1024]{1,0:T(8,128)(2,1)S(1)} collective-permute-done((bf16[512,1024]{1,0:T(8,128)(2,1)}, bf16[512,1024]{1,0:T(8,128)(2,1)S(1)}, u32[]{:S(2)}, u32[]{:S(2)}) %collective-permute-start.2) | collective-permute-done | bytes 1048608 | tf_op jit(solution)/shard_map/ppermute | solution.py:495
  58.6 3.2 %packed.4 = (bf16[512,1280]{1,0:T(8,128)(2,1)}, bf16[512,1024]{1,0:T(8,128)(2,1)}) custom-call(s32[2]{0:T(128)S(1)} %pad_add_fusion.1.meta_ref, bf16[512,1024]{1,0:T(8,128)(2,1)S(1)} %collective-permute-done.7.refs_0_.refs_7_, bf16[512,1024]{1,0:T(8,128)(2,1)} %collective-permute-done.8.refs_1_.refs_8_, ...), custom_call_target="tpu_custom_call" | custom-call | flops 1000 | bytes 1000 | tf_op jit(solution)/shard_map/packed/pallas_call | solution.py:129
  61.9 2.9 %collective-permute-done.9.refs_12_ = bf16[512,384]{1,0:T(8,128)(2,1)} collective-permute-done((bf16[512,384]{1,0:T(8,128)(2,1)S(1)}, bf16[512,384]{1,0:T(8,128)(2,1)}, u32[]{:S(2)}, u32[]{:S(2)}) %collective-permute-start.9) | collective-permute-done | bytes 393248 | tf_op jit(solution)/shard_map/ppermute | solution.py:495
  64.8 1.3 collective-permute-start.10
  66.1 1.7 %collective-permute-start.11 = (bf16[512,1024]{1,0:T(8,128)(2,1)}, bf16[512,1024]{1,0:T(8,128)(2,1)}, u32[]{:S(2)}, u32[]{:S(2)}) collective-permute-start(bf16[512,1024]{1,0:T(8,128)(2,1)} %get-tuple-element.49), channel_id=1, source_target_pairs={{4,8},{6,10},{8,4},{10,6},{5,9},{7,11},{9,5},{11,7},{20,24},{22,26... | collective-permute-start | bytes 3145736 | tf_op jit(solution)/shard_map/ppermute | solution.py:495
  69.0 12.8 %collective-permute-done.4.refs_2_ = bf16[128,4096]{1,0:T(8,128)(2,1)} collective-permute-done((bf16[128,4096]{1,0:T(8,128)(2,1)}, bf16[128,4096]{1,0:T(8,128)(2,1)}, u32[]{:S(2)}, u32[]{:S(2)}) %collective-permute-start.4) | collective-permute-done | bytes 1048608 | tf_op jit(solution)/shard_map/ppermute | solution.py:495
  83.0 1.3 collective-permute-start.12
  86.3 9.7 %collective-permute-done.10.refs_11_ = bf16[512,1280]{1,0:T(8,128)(2,1)} collective-permute-done((bf16[512,1280]{1,0:T(8,128)(2,1)}, bf16[512,1280]{1,0:T(8,128)(2,1)}, u32[]{:S(2)}, u32[]{:S(2)}) %collective-permute-start.10) | collective-permute-done | bytes 1310752 | tf_op jit(solution)/shard_map/ppermute | solution.py:495
  96.0 13.6 %whole_products.1.refs_5_ = f32[2,512,1024]{2,1,0:T(8,128)} custom-call(s32[14]{0:T(128)} %stack.136.meta_ref, bf16[512,4096]{1,0:T(8,128)(2,1)} %masked_x.1.refs_0_, bf16[128,4096]{1,0:T(8,128)(2,1)} %collective-permute-done.3.refs_1_, bf16[128,4096]{1,0:T(8,128)(2,1)} %collective-permute-done.4.refs_2_, bf16[128,4096]{1,0:T(8,128)(2,1)} %collective-permute-done.5.refs_3_, ...), custom_call_target="tpu_custom_call" | custom-call | flops 6000000000 | bytes 37748736 | tf_op jit(solution)/shard_map/whole_products/pallas_call | solution.py:277
  110.4 1.3 collective-permute-start.14
  112.4 5.7 %collective-permute-done.12.refs_7_ = bf16[512,1024]{1,0:T(8,128)(2,1)} collective-permute-done((bf16[512,1024]{1,0:T(8,128)(2,1)}, bf16[512,1024]{1,0:T(8,128)(2,1)}, u32[]{:S(2)}, u32[]{:S(2)}) %collective-permute-start.12) | collective-permute-done | bytes 1048608 | tf_op jit(solution)/shard_map/ppermute | solution.py:495
  118.1 5.5 %half_products.1 = (bf16[256,640]{1,0:T(8,128)(2,1)}, bf16[256,640]{1,0:T(8,128)(2,1)}, bf16[256,640]{1,0:T(8,128)(2,1)}, bf16[256,640]{1,0:T(8,128)(2,1)}) custom-call(s32[8]{0:T(128)} %stack.144.meta_ref, bf16[512,4096]{1,0:T(8,128)(2,1)} %masked_x.1.refs_0_, bf16[128,4096]{1,0:T(8,128)(2,1)} %collective-permute-done.3.refs_1_, ...), custom_call_target="tpu_custom_call" | custom-call | flops 1000 | bytes 1000 | tf_op jit(solution)/shard_map/half_products/pallas_call | solution.py:407
  123.6 1.5 %collective-permute-start.19 = (bf16[256,640]{1,0:T(8,128)(2,1)}, bf16[256,640]{1,0:T(8,128)(2,1)S(1)}, u32[]{:S(2)}, u32[]{:S(2)}) collective-permute-start(bf16[256,640]{1,0:T(8,128)(2,1)} %get-tuple-element.65), channel_id=1, source_target_pairs={{0,2},{2,0},{4,6},{6,4},{8,10},{10,8},{12,14},{14,12},{1,3},{3,1},... | collective-permute-start | bytes 983048 | tf_op jit(solution)/shard_map/ppermute | solution.py:495
  126.2 5.6 %collective-permute-done.14.refs_9_ = bf16[512,640]{1,0:T(8,128)(2,1)S(1)} collective-permute-done((bf16[512,640]{1,0:T(8,128)(2,1)S(1)}, bf16[512,640]{1,0:T(8,128)(2,1)S(1)}, u32[]{:S(2)}, u32[]{:S(2)}) %collective-permute-start.14) | collective-permute-done | bytes 655392 | tf_op jit(solution)/shard_map/ppermute | solution.py:495
  132.7 6.7 %rest_products.1 = (bf16[256,384]{1,0:T(8,128)(2,1)}, bf16[256,384]{1,0:T(8,128)(2,1)}, bf16[256,384]{1,0:T(8,128)(2,1)}, bf16[256,384]{1,0:T(8,128)(2,1)}) custom-call(s32[11]{0:T(128)} %stack.126.meta_ref, bf16[512,4096]{1,0:T(8,128)(2,1)} %masked_x.1.refs_0_, bf16[128,4096]{1,0:T(8,128)(2,1)} %collective-permute-done.3.refs_1_, ...), custom_call_target="tpu_custom_call" | custom-call | flops 1000 | bytes 1000 | tf_op jit(solution)/shard_map/rest_products/pallas_call | solution.py:407
  140.4 1.2 collective-permute-start.16
  141.9 2.0 %assembled.2.refs_4_ = bf16[256,4096]{1,0:T(8,128)(2,1)} custom-call(s32[2]{0:T(128)S(1)} %get-tuple-element.70.place_ref, f32[4,1,4096]{2,1,0:T(1,128)S(1)} %reshape.15.mask_ref, bf16[256,640]{1,0:T(8,128)(2,1)S(1)} %copy-done.4, bf16[256,640]{1,0:T(8,128)(2,1)S(1)} %collective-permute-done.15.refs_1_, ...), custom_call_target="tpu_custom_call" | custom-call | flops 1000 | bytes 1000 | tf_op jit(solution)/shard_map/assembled/pallas_call | solution.py:454
  143.9 3.2 %collective-permute-done.17.refs_2_ = bf16[256,384]{1,0:T(8,128)(2,1)S(1)} collective-permute-done((bf16[256,384]{1,0:T(8,128)(2,1)}, bf16[256,384]{1,0:T(8,128)(2,1)S(1)}, u32[]{:S(2)}, u32[]{:S(2)}) %collective-permute-start.17) | collective-permute-done | bytes 196640 | tf_op jit(solution)/shard_map/ppermute | solution.py:495
  147.1 1.4 collective-permute-done.18.refs_3_
  149.4 1.6 %assembled.3 = bf16[256,4096]{1,0:T(8,128)(2,1)} custom-call(s32[2]{0:T(128)S(1)} %get-tuple-element.69.place_ref, f32[4,1,4096]{2,1,0:T(1,128)S(1)} %reshape.15.mask_ref, bf16[256,384]{1,0:T(8,128)(2,1)S(1)} %copy-done.5, bf16[256,384]{1,0:T(8,128)(2,1)S(1)} %collective-permute-done.16.refs_1_, ...), custom_call_target="tpu_custom_call", output_to_operand_aliasing={{}: (6, {})} | custom-call | flops 1000 | bytes 1000 | tf_op jit(solution)/shard_map/assembled/pallas_call | solution.py:454
  (53 shorter events, 12.2 us)
Async XLA Ops:
  0.0 9.8 %copy-start.7 = (s32[8,64]{1,0:T(8,128)S(1)}, s32[8,64]{1,0:T(8,128)}, u32[]{:S(2)}) copy-start(s32[8,64]{1,0:T(8,128)} %param.6) | copy-start | bytes 6148
  2.2 26.5 %collective-permute-start = (bf16[512,1024]{1,0:T(8,128)(2,1)}, bf16[512,1024]{1,0:T(8,128)(2,1)}, u32[]{:S(2)}, u32[]{:S(2)}) collective-permute-start(bf16[512,1024]{1,0:T(8,128)(2,1)} %b_strips.2), channel_id=1, source_target_pairs={{0,2},{2,0},{4,6},{6,4},{8,10},{10,8},{12,14},{14,12},{1,3},{3,1},... | collective-permute-start | bytes 3145736 | tf_op jit(solution)/shard_map/ppermute | solution.py:495
  7.4 24.9 %collective-permute-start.1 = (bf16[512,1024]{1,0:T(8,128)(2,1)}, bf16[512,1024]{1,0:T(8,128)(2,1)S(1)}, u32[]{:S(2)}, u32[]{:S(2)}) collective-permute-start(bf16[512,1024]{1,0:T(8,128)(2,1)} %b_strips.3.refs_5_), channel_id=1, source_target_pairs={{0,4},{2,6},{4,0},{6,2},{8,12},{10,14},{12,8},{14,10},{1,5},{3,7},... | collective-permute-start | bytes 3145736 | tf_op jit(solution)/shard_map/ppermute | solution.py:495
  9.1 28.5 %collective-permute-start.7 = (bf16[512,1024]{1,0:T(8,128)(2,1)}, bf16[512,1024]{1,0:T(8,128)(2,1)S(1)}, u32[]{:S(2)}, u32[]{:S(2)}) collective-permute-start(bf16[512,1024]{1,0:T(8,128)(2,1)} %b_strips.3.refs_5_), channel_id=1, source_target_pairs={{4,8},{6,10},{8,4},{10,6},{5,9},{7,11},{9,5},{11,7},{20,24},{22,26... | collective-permute-start | bytes 3145736 | tf_op jit(solution)/shard_map/ppermute | solution.py:495
  32.3 52.1 %copy-start.1 = (bf16[512,1024]{1,0:T(8,128)(2,1)}, bf16[512,1024]{1,0:T(8,128)(2,1)S(1)}, u32[]{:S(2)}) copy-start(bf16[512,1024]{1,0:T(8,128)(2,1)S(1)} %collective-permute-done.1.refs_0_.refs_2_.refs_9_) | copy-start | bytes 3145732
  32.3 26.3 %collective-permute-start.2 = (bf16[512,1024]{1,0:T(8,128)(2,1)}, bf16[512,1024]{1,0:T(8,128)(2,1)S(1)}, u32[]{:S(2)}, u32[]{:S(2)}) collective-permute-start(bf16[512,1024]{1,0:T(8,128)(2,1)} %collective-permute-done.refs_6_), channel_id=1, source_target_pairs={{0,4},{2,6},{4,0},{6,2},{8,12},{10,14},{12,8},{14,10},{1,5},{3,7},... | collective-permute-start | bytes 3145736 | tf_op jit(solution)/shard_map/ppermute | solution.py:495
  33.9 24.7 %collective-permute-start.8 = (bf16[512,1024]{1,0:T(8,128)(2,1)}, bf16[512,1024]{1,0:T(8,128)(2,1)}, u32[]{:S(2)}, u32[]{:S(2)}) collective-permute-start(bf16[512,1024]{1,0:T(8,128)(2,1)} %collective-permute-done.refs_6_), channel_id=1, source_target_pairs={{4,8},{6,10},{8,4},{10,6},{5,9},{7,11},{9,5},{11,7},{20,24},{22,26... | collective-permute-start | bytes 3145736 | tf_op jit(solution)/shard_map/ppermute | solution.py:495
  35.6 33.4 %collective-permute-start.3 = (bf16[128,4096]{1,0:T(8,128)(2,1)}, bf16[128,4096]{1,0:T(8,128)(2,1)}, u32[]{:S(2)}, u32[]{:S(2)}) collective-permute-start(bf16[128,4096]{1,0:T(8,128)(2,1)} %get-tuple-element.40), channel_id=1, source_target_pairs={{0,2},{2,0},{4,6},{6,4},{8,10},{10,8},{12,14},{14,12},{1,3},{3,1},... | collective-permute-start | bytes 3145736 | tf_op jit(solution)/shard_map/ppermute | solution.py:495
  36.1 45.7 %collective-permute-start.4 = (bf16[128,4096]{1,0:T(8,128)(2,1)}, bf16[128,4096]{1,0:T(8,128)(2,1)}, u32[]{:S(2)}, u32[]{:S(2)}) collective-permute-start(bf16[128,4096]{1,0:T(8,128)(2,1)} %get-tuple-element.41), channel_id=1, source_target_pairs={{0,2},{2,0},{4,6},{6,4},{8,10},{10,8},{12,14},{14,12},{1,3},{3,1},... | collective-permute-start | bytes 3145736 | tf_op jit(solution)/shard_map/ppermute | solution.py:495
  37.6 44.2 %copy-start.3 = (bf16[512,1024]{1,0:T(8,128)(2,1)}, bf16[512,1024]{1,0:T(8,128)(2,1)S(1)}, u32[]{:S(2)}) copy-start(bf16[512,1024]{1,0:T(8,128)(2,1)S(1)} %collective-permute-done.7.refs_0_.refs_7_) | copy-start | bytes 3145732
  37.6 27.2 %collective-permute-start.9 = (bf16[512,384]{1,0:T(8,128)(2,1)S(1)}, bf16[512,384]{1,0:T(8,128)(2,1)}, u32[]{:S(2)}, u32[]{:S(2)}) collective-permute-start(bf16[512,384]{1,0:T(8,128)(2,1)S(1)} %slice.14), channel_id=1, source_target_pairs={{4,0},{6,2},{8,12},{10,14},{5,1},{7,3},{9,13},{11,15},{20,16},{22,... | collective-permute-start | bytes 1179656 | tf_op jit(solution)/shard_map/ppermute | solution.py:495
  58.6 37.4 %copy-start.2 = (bf16[512,1024]{1,0:T(8,128)(2,1)}, bf16[512,1024]{1,0:T(8,128)(2,1)S(1)}, u32[]{:S(2)}) copy-start(bf16[512,1024]{1,0:T(8,128)(2,1)S(1)} %collective-permute-done.2.refs_1_.refs_3_.refs_10_) | copy-start | bytes 3145732
  64.8 31.2 %collective-permute-start.10 = (bf16[512,1280]{1,0:T(8,128)(2,1)}, bf16[512,1280]{1,0:T(8,128)(2,1)}, u32[]{:S(2)}, u32[]{:S(2)}) collective-permute-start(bf16[512,1280]{1,0:T(8,128)(2,1)} %get-tuple-element.46), channel_id=1, source_target_pairs={{4,0},{6,2},{8,12},{10,14},{5,1},{7,3},{9,13},{11,15},{20,16},{22,... | collective-permute-start | bytes 3932168 | tf_op jit(solution)/shard_map/ppermute | solution.py:495
  66.1 16.9 %collective-permute-start.11 = (bf16[512,1024]{1,0:T(8,128)(2,1)}, bf16[512,1024]{1,0:T(8,128)(2,1)}, u32[]{:S(2)}, u32[]{:S(2)}) collective-permute-start(bf16[512,1024]{1,0:T(8,128)(2,1)} %get-tuple-element.49), channel_id=1, source_target_pairs={{4,8},{6,10},{8,4},{10,6},{5,9},{7,11},{9,5},{11,7},{20,24},{22,26... | collective-permute-start | bytes 3145736 | tf_op jit(solution)/shard_map/ppermute | solution.py:495
  81.8 3.3 %collective-permute-start.5 = (bf16[128,4096]{1,0:T(8,128)(2,1)}, bf16[128,4096]{1,0:T(8,128)(2,1)}, u32[]{:S(2)}, u32[]{:S(2)}) collective-permute-start(bf16[128,4096]{1,0:T(8,128)(2,1)} %collective-permute-done.3.refs_1_), channel_id=1, source_target_pairs={{0,1},{1,0},{2,3},{3,2},{4,5},{5,4},{6,7},{7,6},{8,9},{9,8},{10,11... | collective-permute-start | bytes 3145736 | tf_op jit(solution)/shard_map/ppermute | solution.py:538
  81.8 4.5 %collective-permute-start.6 = (bf16[128,4096]{1,0:T(8,128)(2,1)}, bf16[128,4096]{1,0:T(8,128)(2,1)}, u32[]{:S(2)}, u32[]{:S(2)}) collective-permute-start(bf16[128,4096]{1,0:T(8,128)(2,1)} %collective-permute-done.4.refs_2_), channel_id=1, source_target_pairs={{0,1},{1,0},{2,3},{3,2},{4,5},{5,4},{6,7},{7,6},{8,9},{9,8},{10,11... | collective-permute-start | bytes 3145736 | tf_op jit(solution)/shard_map/ppermute | solution.py:538
  82.3 27.4 %collective-permute-start.13 = (bf16[512,1024]{1,0:T(8,128)(2,1)}, bf16[512,1024]{1,0:T(8,128)(2,1)S(1)}, u32[]{:S(2)}, u32[]{:S(2)}) collective-permute-start(bf16[512,1024]{1,0:T(8,128)(2,1)} %packed.3), channel_id=1, source_target_pairs={{4,8},{6,10},{8,4},{10,6},{5,9},{7,11},{9,5},{11,7},{20,24},{22,26... | collective-permute-start | bytes 3145736 | tf_op jit(solution)/shard_map/ppermute | solution.py:495
  83.0 35.0 %collective-permute-start.12 = (bf16[512,1024]{1,0:T(8,128)(2,1)}, bf16[512,1024]{1,0:T(8,128)(2,1)}, u32[]{:S(2)}, u32[]{:S(2)}) collective-permute-start(bf16[512,1024]{1,0:T(8,128)(2,1)} %collective-permute-done.11.refs_6_), channel_id=1, source_target_pairs={{4,0},{6,2},{8,12},{10,14},{5,1},{7,3},{9,13},{11,15},{20,16},{22,... | collective-permute-start | bytes 3145736 | tf_op jit(solution)/shard_map/ppermute | solution.py:495
  109.7 8.4 %copy-start = (bf16[512,1024]{1,0:T(8,128)(2,1)}, bf16[512,1024]{1,0:T(8,128)(2,1)S(1)}, u32[]{:S(2)}) copy-start(bf16[512,1024]{1,0:T(8,128)(2,1)S(1)} %collective-permute-done.13.refs_0_.refs_8_) | copy-start | bytes 3145732
  110.4 21.4 %collective-permute-start.14 = (bf16[512,640]{1,0:T(8,128)(2,1)S(1)}, bf16[512,640]{1,0:T(8,128)(2,1)S(1)}, u32[]{:S(2)}, u32[]{:S(2)}) collective-permute-start(bf16[512,640]{1,0:T(8,128)(2,1)S(1)} %packed.5), channel_id=1, source_target_pairs={{4,0},{6,2},{8,12},{10,14},{5,1},{7,3},{9,13},{11,15},{20,16},{22,... | collective-permute-start | bytes 1966088 | tf_op jit(solution)/shard_map/ppermute | solution.py:495
  123.6 8.2 %collective-permute-start.15 = (bf16[256,640]{1,0:T(8,128)(2,1)}, bf16[256,640]{1,0:T(8,128)(2,1)S(1)}, u32[]{:S(2)}, u32[]{:S(2)}) collective-permute-start(bf16[256,640]{1,0:T(8,128)(2,1)} %get-tuple-element.52), channel_id=1, source_target_pairs={{0,1},{1,0},{2,3},{3,2},{4,5},{5,4},{6,7},{7,6},{8,9},{9,8},{10,11... | collective-permute-start | bytes 983048 | tf_op jit(solution)/shard_map/ppermute | solution.py:573
  123.6 18.3 %collective-permute-start.19 = (bf16[256,640]{1,0:T(8,128)(2,1)}, bf16[256,640]{1,0:T(8,128)(2,1)S(1)}, u32[]{:S(2)}, u32[]{:S(2)}) collective-permute-start(bf16[256,640]{1,0:T(8,128)(2,1)} %get-tuple-element.65), channel_id=1, source_target_pairs={{0,2},{2,0},{4,6},{6,4},{8,10},{10,8},{12,14},{14,12},{1,3},{3,1},... | collective-permute-start | bytes 983048 | tf_op jit(solution)/shard_map/ppermute | solution.py:495
  125.2 16.8 %collective-permute-start.20 = (bf16[256,640]{1,0:T(8,128)(2,1)}, bf16[256,640]{1,0:T(8,128)(2,1)S(1)}, u32[]{:S(2)}, u32[]{:S(2)}) collective-permute-start(bf16[256,640]{1,0:T(8,128)(2,1)} %get-tuple-element.66), channel_id=1, source_target_pairs={{0,3},{1,2},{2,1},{3,0},{4,7},{5,6},{6,5},{7,4},{8,11},{9,10},{10,... | collective-permute-start | bytes 983048 | tf_op jit(solution)/shard_map/ppermute | solution.py:575
  126.2 15.4 %copy-start.8 = (s32[4,64]{1,0:T(4,128)S(1)}, s32[4,64]{1,0:T(4,128)}, u32[]{:S(2)}) copy-start(s32[4,64]{1,0:T(4,128)} %param.7) | copy-start | bytes 3076
  126.2 15.7 %copy-start.4 = (bf16[256,640]{1,0:T(8,128)(2,1)S(1)}, bf16[256,640]{1,0:T(8,128)(2,1)}, u32[]{:S(2)}) copy-start(bf16[256,640]{1,0:T(8,128)(2,1)} %get-tuple-element.63.refs_0_) | copy-start | bytes 983044
  131.8 0.9 copy-start.6
  139.4 7.8 %collective-permute-start.17 = (bf16[256,384]{1,0:T(8,128)(2,1)}, bf16[256,384]{1,0:T(8,128)(2,1)S(1)}, u32[]{:S(2)}, u32[]{:S(2)}) collective-permute-start(bf16[256,384]{1,0:T(8,128)(2,1)} %get-tuple-element.56), channel_id=1, source_target_pairs={{0,2},{2,0},{4,6},{6,4},{8,10},{10,8},{12,14},{14,12},{1,3},{3,1},... | collective-permute-start | bytes 589832 | tf_op jit(solution)/shard_map/ppermute | solution.py:495
  140.4 8.1 %collective-permute-start.18 = (bf16[256,384]{1,0:T(8,128)(2,1)}, bf16[256,384]{1,0:T(8,128)(2,1)S(1)}, u32[]{:S(2)}, u32[]{:S(2)}) collective-permute-start(bf16[256,384]{1,0:T(8,128)(2,1)} %get-tuple-element.57), channel_id=1, source_target_pairs={{0,3},{1,2},{2,1},{3,0},{4,7},{5,6},{6,5},{7,4},{8,11},{9,10},{10,... | collective-permute-start | bytes 589832 | tf_op jit(solution)/shard_map/ppermute | solution.py:575
  140.4 8.1 %collective-permute-start.16 = (bf16[256,384]{1,0:T(8,128)(2,1)}, bf16[256,384]{1,0:T(8,128)(2,1)S(1)}, u32[]{:S(2)}, u32[]{:S(2)}) collective-permute-start(bf16[256,384]{1,0:T(8,128)(2,1)} %get-tuple-element.55), channel_id=1, source_target_pairs={{0,1},{1,0},{2,3},{3,2},{4,5},{5,4},{6,7},{7,6},{8,9},{9,8},{10,11... | collective-permute-start | bytes 589832 | tf_op jit(solution)/shard_map/ppermute | solution.py:573
  148.5 0.9 copy-start.5

commit v19 on v17

--- a/solution.py
+++ b/solution.py
@@ -142,9 +142,8 @@
     out_ref[...] = (x_ref[...].astype(jnp.float32) * mask_ref[0]).astype(jnp.bfloat16)
 
 
-def masked_x(x_band, mask_wide, first):
-    count = mask_wide.shape[0]
-    block = x_band.shape[0] // count
+def masked_rows(x_band, mask_wide, first, count):
+    block = x_band.shape[0] // mask_wide.shape[0]
     cols = x_band.shape[1]
     return pl.pallas_call(
         mask_kernel,
@@ -152,30 +151,34 @@
             num_scalar_prefetch=1,
             grid=(count,),
             in_specs=[
-                pl.BlockSpec((1, 1, cols), lambda i, f: (lax.rem(f[0] + i, count), 0, 0)),
-                pl.BlockSpec((block, cols), lambda i, f: (lax.rem(f[0] + i, count), 0)),
+                pl.BlockSpec((1, 1, cols), lambda i, f: (f[0] + i, 0, 0)),
+                pl.BlockSpec((block, cols), lambda i, f: (f[0] + i, 0)),
             ],
             out_specs=pl.BlockSpec((block, cols), lambda i, f: (i, 0)),
         ),
-        out_shape=jax.ShapeDtypeStruct(x_band.shape, jnp.bfloat16),
+        out_shape=jax.ShapeDtypeStruct((count * block, cols), jnp.bfloat16),
         compiler_params=pltpu.CompilerParams(vmem_limit_bytes=58 * MIB),
         cost_estimate=SMALL,
-        name="masked_x",
+        name="masked_rows",
     )(first.reshape(1), mask_wide, x_band)
 
 
-PARTS = 5
+PARTS = 8
 
 
 def x_copies(x_refs, xv, sems, offset_of):
     n_b, _, rows, panel = xv.shape
+    part = 2 * rows // PARTS
     copies = {}
     for p in range(n_b):
         for r in range(PARTS):
-            g = min(r, 1)
+            g, k = divmod(r, PARTS // 2)
             at = pl.multiple_of(offset_of(p, g) * panel, panel)
-            to = xv.at[p, 0] if r == 0 else xv.at[p, 1, (r - 1) * rows // 4 : r * rows // 4]
-            copies[p, r] = pltpu.make_async_copy(x_refs[r].at[:, pl.ds(at, panel)], to, sems.at[p, r])
+            copies[p, r] = pltpu.make_async_copy(
+                x_refs[r].at[:, pl.ds(at, panel)],
+                xv.at[p, g, k * part : (k + 1) * part],
+                sems.at[p, r],
+            )
     return copies
 
 
@@ -269,7 +272,7 @@
 
 
 def whole_products(meta, xs, operands, plan):
-    rows = xs[0].shape[0] // 2
+    rows = PARTS // 4 * xs[0].shape[0]
     panel, quarter = operands[plan[0][0]].shape
     n_b = len(plan)
     any_spec = pl.BlockSpec(memory_space=pl.ANY)
@@ -363,7 +366,7 @@
                 do(copy)
 
     def rows_loads(g):
-        return [prev[g]] + [copy for (_, r), copy in x_loads.items() if min(r, 1) == g]
+        return [prev[g]] + [copy for (_, r), copy in x_loads.items() if r // (PARTS // 2) == g]
 
     on_b(lambda copy: copy.start())
     for g in range(2):
@@ -398,7 +401,7 @@
 
 
 def last_products(meta, xs, prev, middle, end, second, b, count, name):
-    rows = xs[0].shape[0] // 2
+    rows = PARTS // 4 * xs[0].shape[0]
     panel, quarter = second.shape
     any_spec = pl.BlockSpec(memory_space=pl.ANY)
     x_spec = pl.BlockSpec(memory_space=pltpu.HBM)
@@ -506,13 +509,13 @@
     cross_a = line(own_a, cross)
     mask_wide = widen(a_mask, block)
     rows = a_mask.shape[0]
-    x_own = masked_x(x_band, mask_wide, c * rows // 2)
-    x_mine = [x_own[k * panel // 4 : (k + 1) * panel // 4] for k in range(2)]
+    x_mine = [masked_rows(x_band, mask_wide, c * rows // 2 + k * rows // 4, rows // 4) for k in range(2)]
     own_b, *x_mine = together(own_b, *x_mine)
     own_b, swap_a = together(own_b, swap_a)
     swap_b = line(own_b, swap)
     cross_b = line(own_b, cross)
     x_across = [line(part, across) for part in x_mine]
+    x_rest = [masked_rows(x_band, mask_wide, (1 - c) * rows // 2 + k * rows // 4, rows // 4) for k in range(2)]
 
     mid_a = line(cross_a[:, 5 * LANES :], outward)
     mid_b, fwd_first = packed(
@@ -529,14 +532,14 @@
         ],
     )
     (fwd_second,) = packed([second_out], [swap_a, swap_b], [8], [(0, (0,), 4, 0, 0, None), (1, (0,), 4, 0, 4, None)])
-    mid_a, mid_b, fwd_first = together(mid_a, mid_b, fwd_first)
+    mid_a, mid_b, fwd_first, *x_rest = together(mid_a, mid_b, fwd_first, *x_rest)
     mid_b = line(mid_b, outward)
     fwd_first = line(fwd_first, cross)
     fwd_second, *x_across = together(fwd_second, *x_across)
     far_first = line(fwd_first, outward)
     fwd_second = line(fwd_second, cross)
     x_opposite = [lax.ppermute(part, "depth", layers) for part in x_across]
-    xs = [x_own] + x_across + x_opposite
+    xs = x_mine + x_rest + x_across + x_opposite
 
     def offsets(delta):
         tilt = 2 * y - 1

time: 154 us -> 154 us (level)
  local copies, waits for them, and re-layouts: 8.09 us -> 4.96 us
  Pallas kernels: 45.7 us -> 48.1 us
    slice x1 -> x0, local copies, waits for them, and re-layouts: 3.06 us -> none  [pairs_in_line(): x_mine = [x_own[k * panel // 4:(k + 1) * panel // 4] for k in range(2)]]
    pallas_call x1 -> x4, Pallas kernels: 6.87 us -> 8.52 us  [masked_rows(): pl.pallas_call(mask_kernel, grid_spec=pltpu.PrefetchScalarGridSpec(num_sc...]
  transfers between devices with their start and end apart: 21 -> 21, of which waited for: 11 -> 12; matrix products, arithmetic and copies ran while one was open for 4% -> 2% of each run, Pallas kernels for 27% -> 29%
where the time goes in v19:
time: 154 us; the launch traced here: 153 us
  waiting for transfers between devices  75.9 us (49%)
  Pallas kernels  48.1 us (31%)
  starting transfers between devices  22.8 us (15%)
  local copies, waits for them, and re-layouts  4.96 us (3%)
    ppermute x15, waiting for transfers between devices, line(): return lax.ppermute(value, 'grid', pairs)  71.4 us
    ppermute x15, starting transfers between devices, line(): return lax.ppermute(value, 'grid', pairs)  21 us
    pallas_call x1, Pallas kernels, whole_products(): pl.pallas_call(functools.partial(whole_kernel, plan), out_shape=jax.Shape...  14.1 us
    pallas_call x2, Pallas kernels, last_products(): pl.pallas_call(functools.partial(last_kernel, b is not None), out_shape=[...  12.4 us
    pallas_call x4, Pallas kernels, masked_rows(): pl.pallas_call(mask_kernel, grid_spec=pltpu.PrefetchScalarGridSpec(num_sc...  8.52 us
    pallas_call x3, Pallas kernels, packed(): pl.pallas_call(functools.partial(pack_kernel, plan, len(sources)), out_sh...  5.02 us
    pallas_call x2, Pallas kernels, b_strips(): pl.pallas_call(strips_kernel, out_shape=jax.ShapeDtypeStruct(shape, jnp.b...  4.36 us
    pallas_call x2, Pallas kernels, assembled(): pl.pallas_call(assemble_kernel, out_shape=jax.ShapeDtypeStruct((rows, col...  3.63 us
  transfers between devices with their start and end apart: 21, of which 12 were waited for; matrix products, arithmetic and copies ran while one was open for 2% of the time, Pallas kernels for 29%

profile of v19, /device:TPU:0, one launch (start us, length us, event | category | flops | bytes accessed | tf_op | source)
XLA Modules:
  0.0 152.6 jit_solution(13479047720198280419)
XLA Ops:
  0.0 2.2 %b_strips.2 = bf16[512,1024]{1,0:T(8,128)(2,1)} custom-call(s32[1]{0:T(128)} %bitcast.11.quarter_ref, bf16[512,4096]{1,0:T(8,128)(2,1)} %w_ref.2), custom_call_target="tpu_custom_call" | custom-call | flops 1000 | bytes 1000 | tf_op jit(solution)/shard_map/b_strips/pallas_call | solution.py:86
  2.2 3.0 %collective-permute-start = (bf16[512,1024]{1,0:T(8,128)(2,1)}, bf16[512,1024]{1,0:T(8,128)(2,1)S(1)}, u32[]{:S(2)}, u32[]{:S(2)}) collective-permute-start(bf16[512,1024]{1,0:T(8,128)(2,1)} %b_strips.2), channel_id=1, source_target_pairs={{0,2},{2,0},{4,6},{6,4},{8,10},{10,8},{12,14},{14,12},{1,3},{3,1},... | collective-permute-start | bytes 3145736 | tf_op jit(solution)/shard_map/ppermute | solution.py:498
  5.2 2.2 %b_strips.3.refs_8_ = bf16[512,1024]{1,0:T(8,128)(2,1)} custom-call(s32[1]{0:T(128)} %bitcast.quarter_ref, bf16[512,4096]{1,0:T(8,128)(2,1)} %w_ref.2), custom_call_target="tpu_custom_call" | custom-call | flops 1000 | bytes 1000 | tf_op jit(solution)/shard_map/b_strips/pallas_call | solution.py:86
  7.4 1.6 %collective-permute-start.3 = (bf16[512,1024]{1,0:T(8,128)(2,1)}, bf16[512,1024]{1,0:T(8,128)(2,1)S(1)}, u32[]{:S(2)}, u32[]{:S(2)}) collective-permute-start(bf16[512,1024]{1,0:T(8,128)(2,1)} %b_strips.3.refs_8_), channel_id=1, source_target_pairs={{0,4},{2,6},{4,0},{6,2},{8,12},{10,14},{12,8},{14,10},{1,5},{3,7},... | collective-permute-start | bytes 3145736 | tf_op jit(solution)/shard_map/ppermute | solution.py:498
  10.8 2.1 %masked_rows.5.refs_1_ = bf16[128,4096]{1,0:T(8,128)(2,1)} custom-call(s32[1]{0:T(128)} %bitcast.13.first_ref, f32[8,1,4096]{2,1,0:T(1,128)} %reshape.27.mask_ref, bf16[512,4096]{1,0:T(8,128)(2,1)} %x_ref.7), custom_call_target="tpu_custom_call" | custom-call | flops 1000 | bytes 1000 | tf_op jit(solution)/shard_map/masked_rows/pallas_call | solution.py:148
  12.9 2.1 %masked_rows.4.refs_0_ = bf16[128,4096]{1,0:T(8,128)(2,1)} custom-call(s32[1]{0:T(128)} %bitcast.12.first_ref, f32[8,1,4096]{2,1,0:T(1,128)} %reshape.27.mask_ref, bf16[512,4096]{1,0:T(8,128)(2,1)} %x_ref.7), custom_call_target="tpu_custom_call" | custom-call | flops 1000 | bytes 1000 | tf_op jit(solution)/shard_map/masked_rows/pallas_call | solution.py:148
  15.1 13.5 %collective-permute-done.refs_9_ = bf16[512,1024]{1,0:T(8,128)(2,1)S(1)} collective-permute-done((bf16[512,1024]{1,0:T(8,128)(2,1)}, bf16[512,1024]{1,0:T(8,128)(2,1)S(1)}, u32[]{:S(2)}, u32[]{:S(2)}) %collective-permute-start) | collective-permute-done | bytes 1048608 | tf_op jit(solution)/shard_map/ppermute | solution.py:498
  29.6 2.8 %collective-permute-done.3.refs_2_.refs_0_.refs_12_ = bf16[512,1024]{1,0:T(8,128)(2,1)S(1)} collective-permute-done((bf16[512,1024]{1,0:T(8,128)(2,1)}, bf16[512,1024]{1,0:T(8,128)(2,1)S(1)}, u32[]{:S(2)}, u32[]{:S(2)}) %collective-permute-start.3) | collective-permute-done | bytes 1048608 | tf_op jit(solution)/shard_map/ppermute | solution.py:498
  32.3 1.6 %collective-permute-start.5 = (bf16[512,1024]{1,0:T(8,128)(2,1)}, bf16[512,1024]{1,0:T(8,128)(2,1)S(1)}, u32[]{:S(2)}, u32[]{:S(2)}) collective-permute-start(bf16[512,1024]{1,0:T(8,128)(2,1)} %copy-done.10), channel_id=1, source_target_pairs={{0,4},{2,6},{4,0},{6,2},{8,12},{10,14},{12,8},{14,10},{1,5},{3,7},... | collective-permute-start | bytes 3145736 | tf_op jit(solution)/shard_map/ppermute | solution.py:498
  33.9 1.6 %collective-permute-start.4 = (bf16[512,1024]{1,0:T(8,128)(2,1)}, bf16[512,1024]{1,0:T(8,128)(2,1)}, u32[]{:S(2)}, u32[]{:S(2)}) collective-permute-start(bf16[512,1024]{1,0:T(8,128)(2,1)} %copy-done.10), channel_id=1, source_target_pairs={{4,8},{6,10},{8,4},{10,6},{5,9},{7,11},{9,5},{11,7},{20,24},{22,26... | collective-permute-start | bytes 3145736 | tf_op jit(solution)/shard_map/ppermute | solution.py:498
  36.0 1.5 collective-permute-start.7
  37.6 1.3 collective-permute-start.2
  38.9 2.1 %masked_rows.7.refs_3_ = bf16[128,4096]{1,0:T(8,128)(2,1)} custom-call(s32[1]{0:T(128)} %bitcast.16.first_ref, f32[8,1,4096]{2,1,0:T(1,128)} %reshape.27.mask_ref, bf16[512,4096]{1,0:T(8,128)(2,1)} %x_ref.7), custom_call_target="tpu_custom_call" | custom-call | flops 1000 | bytes 1000 | tf_op jit(solution)/shard_map/masked_rows/pallas_call | solution.py:148
  41.1 2.1 %masked_rows.6.refs_2_ = bf16[128,4096]{1,0:T(8,128)(2,1)} custom-call(s32[1]{0:T(128)} %bitcast.15.first_ref, f32[8,1,4096]{2,1,0:T(1,128)} %reshape.27.mask_ref, bf16[512,4096]{1,0:T(8,128)(2,1)} %x_ref.7), custom_call_target="tpu_custom_call" | custom-call | flops 1000 | bytes 1000 | tf_op jit(solution)/shard_map/masked_rows/pallas_call | solution.py:148
  43.3 15.4 %collective-permute-done.5.refs_3_.refs_1_.refs_13_ = bf16[512,1024]{1,0:T(8,128)(2,1)S(1)} collective-permute-done((bf16[512,1024]{1,0:T(8,128)(2,1)}, bf16[512,1024]{1,0:T(8,128)(2,1)S(1)}, u32[]{:S(2)}, u32[]{:S(2)}) %collective-permute-start.5) | collective-permute-done | bytes 1048608 | tf_op jit(solution)/shard_map/ppermute | solution.py:498
  58.6 3.2 %packed.3 = (bf16[512,1280]{1,0:T(8,128)(2,1)}, bf16[512,1024]{1,0:T(8,128)(2,1)}) custom-call(s32[2]{0:T(128)S(1)} %pad_add_fusion.1.meta_ref, bf16[512,1024]{1,0:T(8,128)(2,1)S(1)} %collective-permute-done.1.refs_0_.refs_10_, bf16[512,1024]{1,0:T(8,128)(2,1)} %collective-permute-done.4.refs_1_.refs_11_, ...), custom_call_target="tpu_custom_call" | custom-call | flops 1000 | bytes 1000 | tf_op jit(solution)/shard_map/packed/pallas_call | solution.py:129
  61.8 2.9 %collective-permute-done.2.refs_15_ = bf16[512,384]{1,0:T(8,128)(2,1)} collective-permute-done((bf16[512,384]{1,0:T(8,128)(2,1)S(1)}, bf16[512,384]{1,0:T(8,128)(2,1)}, u32[]{:S(2)}, u32[]{:S(2)}) %collective-permute-start.2) | collective-permute-done | bytes 393248 | tf_op jit(solution)/shard_map/ppermute | solution.py:498
  66.1 1.7 %collective-permute-start.11 = (bf16[512,1024]{1,0:T(8,128)(2,1)}, bf16[512,1024]{1,0:T(8,128)(2,1)}, u32[]{:S(2)}, u32[]{:S(2)}) collective-permute-start(bf16[512,1024]{1,0:T(8,128)(2,1)} %get-tuple-element.48), channel_id=1, source_target_pairs={{4,8},{6,10},{8,4},{10,6},{5,9},{7,11},{9,5},{11,7},{20,24},{22,26... | collective-permute-start | bytes 3145736 | tf_op jit(solution)/shard_map/ppermute | solution.py:498
  68.9 12.8 %collective-permute-done.7.refs_5_ = bf16[128,4096]{1,0:T(8,128)(2,1)} collective-permute-done((bf16[128,4096]{1,0:T(8,128)(2,1)}, bf16[128,4096]{1,0:T(8,128)(2,1)}, u32[]{:S(2)}, u32[]{:S(2)}) %collective-permute-start.7) | collective-permute-done | bytes 1048608 | tf_op jit(solution)/shard_map/ppermute | solution.py:498
  83.0 1.3 collective-permute-start.12
  86.3 9.7 %collective-permute-done.10.refs_14_ = bf16[512,1280]{1,0:T(8,128)(2,1)} collective-permute-done((bf16[512,1280]{1,0:T(8,128)(2,1)}, bf16[512,1280]{1,0:T(8,128)(2,1)}, u32[]{:S(2)}, u32[]{:S(2)}) %collective-permute-start.10) | collective-permute-done | bytes 1310752 | tf_op jit(solution)/shard_map/ppermute | solution.py:498
  95.9 14.1 %whole_products.1.refs_8_ = f32[2,512,1024]{2,1,0:T(8,128)} custom-call(s32[14]{0:T(128)} %stack.138.meta_ref, bf16[128,4096]{1,0:T(8,128)(2,1)} %masked_rows.4.refs_0_, bf16[128,4096]{1,0:T(8,128)(2,1)} %masked_rows.5.refs_1_, bf16[128,4096]{1,0:T(8,128)(2,1)} %masked_rows.6.refs_2_, bf16[128,4096]{1,0:T(8,128)(2,1)} %masked_rows.7.refs_3_, ...), custom_call_target="tpu_custom_call" | custom-call | flops 6000000000 | bytes 37748736 | tf_op jit(solution)/shard_map/whole_products/pallas_call | solution.py:280
  110.9 1.5 collective-permute-start.14
  113.0 5.0 %collective-permute-done.12.refs_10_ = bf16[512,1024]{1,0:T(8,128)(2,1)} collective-permute-done((bf16[512,1024]{1,0:T(8,128)(2,1)}, bf16[512,1024]{1,0:T(8,128)(2,1)}, u32[]{:S(2)}, u32[]{:S(2)}) %collective-permute-start.12) | collective-permute-done | bytes 1048608 | tf_op jit(solution)/shard_map/ppermute | solution.py:498
  118.0 5.7 %half_products.1 = (bf16[256,640]{1,0:T(8,128)(2,1)}, bf16[256,640]{1,0:T(8,128)(2,1)}, bf16[256,640]{1,0:T(8,128)(2,1)}, bf16[256,640]{1,0:T(8,128)(2,1)}) custom-call(s32[8]{0:T(128)} %stack.144.meta_ref, bf16[128,4096]{1,0:T(8,128)(2,1)} %masked_rows.4.refs_0_, bf16[128,4096]{1,0:T(8,128)(2,1)} %masked_rows.5.refs_1_, ...), custom_call_target="tpu_custom_call" | custom-call | flops 1000 | bytes 1000 | tf_op jit(solution)/shard_map/half_products/pallas_call | solution.py:410
  123.8 1.5 collective-permute-start.19
  126.2 5.6 %collective-permute-done.14.refs_12_ = bf16[512,640]{1,0:T(8,128)(2,1)S(1)} collective-permute-done((bf16[512,640]{1,0:T(8,128)(2,1)S(1)}, bf16[512,640]{1,0:T(8,128)(2,1)S(1)}, u32[]{:S(2)}, u32[]{:S(2)}) %collective-permute-start.14) | collective-permute-done | bytes 655392 | tf_op jit(solution)/shard_map/ppermute | solution.py:498
  132.6 6.8 %rest_products.1 = (bf16[256,384]{1,0:T(8,128)(2,1)}, bf16[256,384]{1,0:T(8,128)(2,1)}, bf16[256,384]{1,0:T(8,128)(2,1)}, bf16[256,384]{1,0:T(8,128)(2,1)}) custom-call(s32[11]{0:T(128)} %stack.126.meta_ref, bf16[128,4096]{1,0:T(8,128)(2,1)} %masked_rows.4.refs_0_, bf16[128,4096]{1,0:T(8,128)(2,1)} %masked_rows.5.refs_1_, ...), custom_call_target="tpu_custom_call" | custom-call | flops 1000 | bytes 1000 | tf_op jit(solution)/shard_map/rest_products/pallas_call | solution.py:410
  141.7 2.0 %assembled.2.refs_4_ = bf16[256,4096]{1,0:T(8,128)(2,1)} custom-call(s32[2]{0:T(128)S(1)} %get-tuple-element.62.place_ref, f32[4,1,4096]{2,1,0:T(1,128)S(1)} %reshape.24.mask_ref, bf16[256,640]{1,0:T(8,128)(2,1)S(1)} %copy-done.4, bf16[256,640]{1,0:T(8,128)(2,1)S(1)} %collective-permute-done.15.refs_1_, ...), custom_call_target="tpu_custom_call" | custom-call | flops 1000 | bytes 1000 | tf_op jit(solution)/shard_map/assembled/pallas_call | solution.py:457
  143.7 3.8 %collective-permute-done.17.refs_2_ = bf16[256,384]{1,0:T(8,128)(2,1)S(1)} collective-permute-done((bf16[256,384]{1,0:T(8,128)(2,1)}, bf16[256,384]{1,0:T(8,128)(2,1)S(1)}, u32[]{:S(2)}, u32[]{:S(2)}) %collective-permute-start.17) | collective-permute-done | bytes 196640 | tf_op jit(solution)/shard_map/ppermute | solution.py:498
  147.5 3.3 %collective-permute-done.18.refs_3_ = bf16[256,384]{1,0:T(8,128)(2,1)S(1)} collective-permute-done((bf16[256,384]{1,0:T(8,128)(2,1)}, bf16[256,384]{1,0:T(8,128)(2,1)S(1)}, u32[]{:S(2)}, u32[]{:S(2)}) %collective-permute-start.18) | collective-permute-done | bytes 196640 | tf_op jit(solution)/shard_map/ppermute | solution.py:578
  150.8 1.6 %assembled.3 = bf16[256,4096]{1,0:T(8,128)(2,1)} custom-call(s32[2]{0:T(128)S(1)} %get-tuple-element.61.place_ref, f32[4,1,4096]{2,1,0:T(1,128)S(1)} %reshape.24.mask_ref, bf16[256,384]{1,0:T(8,128)(2,1)S(1)} %copy-done.5, bf16[256,384]{1,0:T(8,128)(2,1)S(1)} %collective-permute-done.16.refs_1_, ...), custom_call_target="tpu_custom_call", output_to_operand_aliasing={{}: (6, {})} | custom-call | flops 1000 | bytes 1000 | tf_op jit(solution)/shard_map/assembled/pallas_call | solution.py:457
  (59 shorter events, 14.3 us)
Async XLA Ops:
  2.2 26.4 %collective-permute-start = (bf16[512,1024]{1,0:T(8,128)(2,1)}, bf16[512,1024]{1,0:T(8,128)(2,1)S(1)}, u32[]{:S(2)}, u32[]{:S(2)}) collective-permute-start(bf16[512,1024]{1,0:T(8,128)(2,1)} %b_strips.2), channel_id=1, source_target_pairs={{0,2},{2,0},{4,6},{6,4},{8,10},{10,8},{12,14},{14,12},{1,3},{3,1},... | collective-permute-start | bytes 3145736 | tf_op jit(solution)/shard_map/ppermute | solution.py:498
  5.2 4.6 %copy-start.8 = (s32[8,64]{1,0:T(8,128)S(1)}, s32[8,64]{1,0:T(8,128)}, u32[]{:S(2)}) copy-start(s32[8,64]{1,0:T(8,128)} %param.6) | copy-start | bytes 6148
  7.4 24.9 %collective-permute-start.3 = (bf16[512,1024]{1,0:T(8,128)(2,1)}, bf16[512,1024]{1,0:T(8,128)(2,1)S(1)}, u32[]{:S(2)}, u32[]{:S(2)}) collective-permute-start(bf16[512,1024]{1,0:T(8,128)(2,1)} %b_strips.3.refs_8_), channel_id=1, source_target_pairs={{0,4},{2,6},{4,0},{6,2},{8,12},{10,14},{12,8},{14,10},{1,5},{3,7},... | collective-permute-start | bytes 3145736 | tf_op jit(solution)/shard_map/ppermute | solution.py:498
  9.1 28.5 %collective-permute-start.1 = (bf16[512,1024]{1,0:T(8,128)(2,1)}, bf16[512,1024]{1,0:T(8,128)(2,1)S(1)}, u32[]{:S(2)}, u32[]{:S(2)}) collective-permute-start(bf16[512,1024]{1,0:T(8,128)(2,1)} %b_strips.3.refs_8_), channel_id=1, source_target_pairs={{4,8},{6,10},{8,4},{10,6},{5,9},{7,11},{9,5},{11,7},{20,24},{22,26... | collective-permute-start | bytes 3145736 | tf_op jit(solution)/shard_map/ppermute | solution.py:498
  28.6 1.0 copy-start.10
  32.3 35.5 %copy-start.1 = (bf16[512,1024]{1,0:T(8,128)(2,1)}, bf16[512,1024]{1,0:T(8,128)(2,1)S(1)}, u32[]{:S(2)}) copy-start(bf16[512,1024]{1,0:T(8,128)(2,1)S(1)} %collective-permute-done.3.refs_2_.refs_0_.refs_12_) | copy-start | bytes 3145732
  32.3 26.3 %collective-permute-start.5 = (bf16[512,1024]{1,0:T(8,128)(2,1)}, bf16[512,1024]{1,0:T(8,128)(2,1)S(1)}, u32[]{:S(2)}, u32[]{:S(2)}) collective-permute-start(bf16[512,1024]{1,0:T(8,128)(2,1)} %copy-done.10), channel_id=1, source_target_pairs={{0,4},{2,6},{4,0},{6,2},{8,12},{10,14},{12,8},{14,10},{1,5},{3,7},... | collective-permute-start | bytes 3145736 | tf_op jit(solution)/shard_map/ppermute | solution.py:498
  33.9 24.7 %collective-permute-start.4 = (bf16[512,1024]{1,0:T(8,128)(2,1)}, bf16[512,1024]{1,0:T(8,128)(2,1)}, u32[]{:S(2)}, u32[]{:S(2)}) collective-permute-start(bf16[512,1024]{1,0:T(8,128)(2,1)} %copy-done.10), channel_id=1, source_target_pairs={{4,8},{6,10},{8,4},{10,6},{5,9},{7,11},{9,5},{11,7},{20,24},{22,26... | collective-permute-start | bytes 3145736 | tf_op jit(solution)/shard_map/ppermute | solution.py:498
  35.5 33.4 %collective-permute-start.6 = (bf16[128,4096]{1,0:T(8,128)(2,1)}, bf16[128,4096]{1,0:T(8,128)(2,1)}, u32[]{:S(2)}, u32[]{:S(2)}) collective-permute-start(bf16[128,4096]{1,0:T(8,128)(2,1)} %masked_rows.4.refs_0_), channel_id=1, source_target_pairs={{0,2},{2,0},{4,6},{6,4},{8,10},{10,8},{12,14},{14,12},{1,3},{3,1},... | collective-permute-start | bytes 3145736 | tf_op jit(solution)/shard_map/ppermute | solution.py:498
  36.0 45.7 %collective-permute-start.7 = (bf16[128,4096]{1,0:T(8,128)(2,1)}, bf16[128,4096]{1,0:T(8,128)(2,1)}, u32[]{:S(2)}, u32[]{:S(2)}) collective-permute-start(bf16[128,4096]{1,0:T(8,128)(2,1)} %masked_rows.5.refs_1_), channel_id=1, source_target_pairs={{0,2},{2,0},{4,6},{6,4},{8,10},{10,8},{12,14},{14,12},{1,3},{3,1},... | collective-permute-start | bytes 3145736 | tf_op jit(solution)/shard_map/ppermute | solution.py:498
  37.6 21.1 %copy-start.3 = (bf16[512,1024]{1,0:T(8,128)(2,1)}, bf16[512,1024]{1,0:T(8,128)(2,1)S(1)}, u32[]{:S(2)}) copy-start(bf16[512,1024]{1,0:T(8,128)(2,1)S(1)} %collective-permute-done.1.refs_0_.refs_10_) | copy-start | bytes 3145732
  37.6 27.2 %collective-permute-start.2 = (bf16[512,384]{1,0:T(8,128)(2,1)S(1)}, bf16[512,384]{1,0:T(8,128)(2,1)}, u32[]{:S(2)}, u32[]{:S(2)}) collective-permute-start(bf16[512,384]{1,0:T(8,128)(2,1)S(1)} %slice.4), channel_id=1, source_target_pairs={{4,0},{6,2},{8,12},{10,14},{5,1},{7,3},{9,13},{11,15},{20,16},{22,... | collective-permute-start | bytes 1179656 | tf_op jit(solution)/shard_map/ppermute | solution.py:498
  58.6 9.1 %copy-start.2 = (bf16[512,1024]{1,0:T(8,128)(2,1)}, bf16[512,1024]{1,0:T(8,128)(2,1)S(1)}, u32[]{:S(2)}) copy-start(bf16[512,1024]{1,0:T(8,128)(2,1)S(1)} %collective-permute-done.5.refs_3_.refs_1_.refs_13_) | copy-start | bytes 3145732
  64.8 31.2 %collective-permute-start.10 = (bf16[512,1280]{1,0:T(8,128)(2,1)}, bf16[512,1280]{1,0:T(8,128)(2,1)}, u32[]{:S(2)}, u32[]{:S(2)}) collective-permute-start(bf16[512,1280]{1,0:T(8,128)(2,1)} %get-tuple-element.45), channel_id=1, source_target_pairs={{4,0},{6,2},{8,12},{10,14},{5,1},{7,3},{9,13},{11,15},{20,16},{22,... | collective-permute-start | bytes 3932168 | tf_op jit(solution)/shard_map/ppermute | solution.py:498
  66.1 16.9 %collective-permute-start.11 = (bf16[512,1024]{1,0:T(8,128)(2,1)}, bf16[512,1024]{1,0:T(8,128)(2,1)}, u32[]{:S(2)}, u32[]{:S(2)}) collective-permute-start(bf16[512,1024]{1,0:T(8,128)(2,1)} %get-tuple-element.48), channel_id=1, source_target_pairs={{4,8},{6,10},{8,4},{10,6},{5,9},{7,11},{9,5},{11,7},{20,24},{22,26... | collective-permute-start | bytes 3145736 | tf_op jit(solution)/shard_map/ppermute | solution.py:498
  81.8 4.3 %collective-permute-start.8 = (bf16[128,4096]{1,0:T(8,128)(2,1)}, bf16[128,4096]{1,0:T(8,128)(2,1)S(1)}, u32[]{:S(2)}, u32[]{:S(2)}) collective-permute-start(bf16[128,4096]{1,0:T(8,128)(2,1)} %collective-permute-done.6.refs_4_), channel_id=1, source_target_pairs={{0,1},{1,0},{2,3},{3,2},{4,5},{5,4},{6,7},{7,6},{8,9},{9,8},{10,11... | collective-permute-start | bytes 3145736 | tf_op jit(solution)/shard_map/ppermute | solution.py:541
  81.8 4.5 %collective-permute-start.9 = (bf16[128,4096]{1,0:T(8,128)(2,1)}, bf16[128,4096]{1,0:T(8,128)(2,1)}, u32[]{:S(2)}, u32[]{:S(2)}) collective-permute-start(bf16[128,4096]{1,0:T(8,128)(2,1)} %collective-permute-done.7.refs_5_), channel_id=1, source_target_pairs={{0,1},{1,0},{2,3},{3,2},{4,5},{5,4},{6,7},{7,6},{8,9},{9,8},{10,11... | collective-permute-start | bytes 3145736 | tf_op jit(solution)/shard_map/ppermute | solution.py:541
  82.3 27.9 %collective-permute-start.13 = (bf16[512,1024]{1,0:T(8,128)(2,1)}, bf16[512,1024]{1,0:T(8,128)(2,1)S(1)}, u32[]{:S(2)}, u32[]{:S(2)}) collective-permute-start(bf16[512,1024]{1,0:T(8,128)(2,1)} %packed.4), channel_id=1, source_target_pairs={{4,8},{6,10},{8,4},{10,6},{5,9},{7,11},{9,5},{11,7},{20,24},{22,26... | collective-permute-start | bytes 3145736 | tf_op jit(solution)/shard_map/ppermute | solution.py:498
  83.0 35.0 %collective-permute-start.12 = (bf16[512,1024]{1,0:T(8,128)(2,1)}, bf16[512,1024]{1,0:T(8,128)(2,1)}, u32[]{:S(2)}, u32[]{:S(2)}) collective-permute-start(bf16[512,1024]{1,0:T(8,128)(2,1)} %collective-permute-done.11.refs_9_), channel_id=1, source_target_pairs={{4,0},{6,2},{8,12},{10,14},{5,1},{7,3},{9,13},{11,15},{20,16},{22,... | collective-permute-start | bytes 3145736 | tf_op jit(solution)/shard_map/ppermute | solution.py:498
  86.1 9.9 %copy-start.6 = (bf16[128,4096]{1,0:T(8,128)(2,1)}, bf16[128,4096]{1,0:T(8,128)(2,1)S(1)}, u32[]{:S(2)}) copy-start(bf16[128,4096]{1,0:T(8,128)(2,1)S(1)} %collective-permute-done.8.refs_6_) | copy-start | bytes 3145732
  110.2 7.9 %copy-start = (bf16[512,1024]{1,0:T(8,128)(2,1)}, bf16[512,1024]{1,0:T(8,128)(2,1)S(1)}, u32[]{:S(2)}) copy-start(bf16[512,1024]{1,0:T(8,128)(2,1)S(1)} %collective-permute-done.13.refs_0_.refs_11_) | copy-start | bytes 3145732
  110.9 20.9 %collective-permute-start.14 = (bf16[512,640]{1,0:T(8,128)(2,1)S(1)}, bf16[512,640]{1,0:T(8,128)(2,1)S(1)}, u32[]{:S(2)}, u32[]{:S(2)}) collective-permute-start(bf16[512,640]{1,0:T(8,128)(2,1)S(1)} %packed.5), channel_id=1, source_target_pairs={{4,0},{6,2},{8,12},{10,14},{5,1},{7,3},{9,13},{11,15},{20,16},{22,... | collective-permute-start | bytes 1966088 | tf_op jit(solution)/shard_map/ppermute | solution.py:498
  123.7 8.1 %collective-permute-start.15 = (bf16[256,640]{1,0:T(8,128)(2,1)}, bf16[256,640]{1,0:T(8,128)(2,1)S(1)}, u32[]{:S(2)}, u32[]{:S(2)}) collective-permute-start(bf16[256,640]{1,0:T(8,128)(2,1)} %get-tuple-element.51), channel_id=1, source_target_pairs={{0,1},{1,0},{2,3},{3,2},{4,5},{5,4},{6,7},{7,6},{8,9},{9,8},{10,11... | collective-permute-start | bytes 983048 | tf_op jit(solution)/shard_map/ppermute | solution.py:576
  123.8 17.9 %collective-permute-start.19 = (bf16[256,640]{1,0:T(8,128)(2,1)}, bf16[256,640]{1,0:T(8,128)(2,1)S(1)}, u32[]{:S(2)}, u32[]{:S(2)}) collective-permute-start(bf16[256,640]{1,0:T(8,128)(2,1)} %get-tuple-element.59), channel_id=1, source_target_pairs={{0,2},{2,0},{4,6},{6,4},{8,10},{10,8},{12,14},{14,12},{1,3},{3,1},... | collective-permute-start | bytes 983048 | tf_op jit(solution)/shard_map/ppermute | solution.py:498
  125.3 16.4 %collective-permute-start.20 = (bf16[256,640]{1,0:T(8,128)(2,1)}, bf16[256,640]{1,0:T(8,128)(2,1)S(1)}, u32[]{:S(2)}, u32[]{:S(2)}) collective-permute-start(bf16[256,640]{1,0:T(8,128)(2,1)} %get-tuple-element.60), channel_id=1, source_target_pairs={{0,3},{1,2},{2,1},{3,0},{4,7},{5,6},{6,5},{7,4},{8,11},{9,10},{10,... | collective-permute-start | bytes 983048 | tf_op jit(solution)/shard_map/ppermute | solution.py:578
  126.2 15.1 %copy-start.9 = (s32[4,64]{1,0:T(4,128)S(1)}, s32[4,64]{1,0:T(4,128)}, u32[]{:S(2)}) copy-start(s32[4,64]{1,0:T(4,128)} %param.7) | copy-start | bytes 3076
  126.2 15.5 %copy-start.4 = (bf16[256,640]{1,0:T(8,128)(2,1)S(1)}, bf16[256,640]{1,0:T(8,128)(2,1)}, u32[]{:S(2)}) copy-start(bf16[256,640]{1,0:T(8,128)(2,1)} %get-tuple-element.57.refs_0_) | copy-start | bytes 983044
  131.8 0.9 copy-start.7
  139.4 11.4 %copy-start.5 = (bf16[256,384]{1,0:T(8,128)(2,1)S(1)}, bf16[256,384]{1,0:T(8,128)(2,1)}, u32[]{:S(2)}) copy-start(bf16[256,384]{1,0:T(8,128)(2,1)} %get-tuple-element.53.refs_0_) | copy-start | bytes 589828
  139.4 4.3 %collective-permute-start.16 = (bf16[256,384]{1,0:T(8,128)(2,1)}, bf16[256,384]{1,0:T(8,128)(2,1)S(1)}, u32[]{:S(2)}, u32[]{:S(2)}) collective-permute-start(bf16[256,384]{1,0:T(8,128)(2,1)} %get-tuple-element.54), channel_id=1, source_target_pairs={{0,1},{1,0},{2,3},{3,2},{4,5},{5,4},{6,7},{7,6},{8,9},{9,8},{10,11... | collective-permute-start | bytes 589832 | tf_op jit(solution)/shard_map/ppermute | solution.py:576
  139.5 8.0 %collective-permute-start.17 = (bf16[256,384]{1,0:T(8,128)(2,1)}, bf16[256,384]{1,0:T(8,128)(2,1)S(1)}, u32[]{:S(2)}, u32[]{:S(2)}) collective-permute-start(bf16[256,384]{1,0:T(8,128)(2,1)} %get-tuple-element.55), channel_id=1, source_target_pairs={{0,2},{2,0},{4,6},{6,4},{8,10},{10,8},{12,14},{14,12},{1,3},{3,1},... | collective-permute-start | bytes 589832 | tf_op jit(solution)/shard_map/ppermute | solution.py:498
  140.5 10.2 %collective-permute-start.18 = (bf16[256,384]{1,0:T(8,128)(2,1)}, bf16[256,384]{1,0:T(8,128)(2,1)S(1)}, u32[]{:S(2)}, u32[]{:S(2)}) collective-permute-start(bf16[256,384]{1,0:T(8,128)(2,1)} %get-tuple-element.56), channel_id=1, source_target_pairs={{0,3},{1,2},{2,1},{3,0},{4,7},{5,6},{6,5},{7,4},{8,11},{9,10},{10,... | collective-permute-start | bytes 589832 | tf_op jit(solution)/shard_map/ppermute | solution.py:578

commit v20 on v19

--- a/solution.py
+++ b/solution.py
@@ -196,10 +196,14 @@
     is_end = meta_ref[0]
 
     def offset_of(p, g):
-        return meta_ref[2 + 2 * p + g]
+        return meta_ref[3 + 2 * p + g]
 
     def b_middle(p):
-        return [pltpu.make_async_copy(b_refs[plan[p][0]].at[:, :quarter], bv.at[p], b_sems.at[p, 0])]
+        if p < 2:
+            return [pltpu.make_async_copy(b_refs[p], bv.at[p], b_sems.at[p, 0])]
+        first = meta_ref[2] if p < 4 else 1 - meta_ref[2]
+        cols = pl.ds(pl.multiple_of(first * LANES, LANES), quarter - LANES)
+        return [pltpu.make_async_copy(b_refs[plan[p][0]].at[:, cols], bv.at[p, :, cols], b_sems.at[p, 0])]
 
     def b_end(p):
         copies = []
@@ -548,7 +552,7 @@
     zero = jnp.zeros_like(z)
     third = offsets(jnp.where(is_end == 1, 2, -toward))
     fourth = offsets(jnp.where(is_end == 1, -toward, 2))
-    meta = jnp.stack([is_end, 4 + y, *offsets(zero), *offsets(toward), *third]).astype(jnp.int32)
+    meta = jnp.stack([is_end, 4 + y, jnp.where(left, 0, 1), *offsets(zero), *offsets(toward), *third]).astype(jnp.int32)
     plan = [
         (0, [(0, 0, 8, 0, 0)]),
         (1, [(1, 0, 8, 0, 1)]),

time: 154 us -> 154 us (level)
  no operation moved by 1% of the time
where the time goes in v20:
time: 154 us; the launch traced here: 153 us
  waiting for transfers between devices  75.9 us (49%)
  Pallas kernels  48.1 us (31%)
  starting transfers between devices  22.8 us (15%)
  local copies, waits for them, and re-layouts  4.96 us (3%)
    ppermute x15, waiting for transfers between devices, line(): return lax.ppermute(value, 'grid', pairs)  71.4 us
    ppermute x15, starting transfers between devices, line(): return lax.ppermute(value, 'grid', pairs)  21 us
    pallas_call x1, Pallas kernels, whole_products(): pl.pallas_call(functools.partial(whole_kernel, plan), out_shape=jax.Shape...  14.1 us
    pallas_call x2, Pallas kernels, last_products(): pl.pallas_call(functools.partial(last_kernel, b is not None), out_shape=[...  12.4 us
    pallas_call x4, Pallas kernels, masked_rows(): pl.pallas_call(mask_kernel, grid_spec=pltpu.PrefetchScalarGridSpec(num_sc...  8.52 us
    pallas_call x3, Pallas kernels, packed(): pl.pallas_call(functools.partial(pack_kernel, plan, len(sources)), out_sh...  5.02 us
    pallas_call x2, Pallas kernels, b_strips(): pl.pallas_call(strips_kernel, out_shape=jax.ShapeDtypeStruct(shape, jnp.b...  4.36 us
    pallas_call x2, Pallas kernels, assembled(): pl.pallas_call(assemble_kernel, out_shape=jax.ShapeDtypeStruct((rows, col...  3.63 us
  transfers between devices with their start and end apart: 21, of which 12 were waited for; matrix products, arithmetic and copies ran while one was open for 2% of the time, Pallas kernels for 29%

profile of v20, /device:TPU:0, one launch (start us, length us, event | category | flops | bytes accessed | tf_op | source)
XLA Modules:
  0.0 152.6 jit_solution(15386859025348091365)
XLA Ops:
  0.0 2.2 %b_strips.2 = bf16[512,1024]{1,0:T(8,128)(2,1)} custom-call(s32[1]{0:T(128)} %bitcast.11.quarter_ref, bf16[512,4096]{1,0:T(8,128)(2,1)} %w_ref.2), custom_call_target="tpu_custom_call" | custom-call | flops 1000 | bytes 1000 | tf_op jit(solution)/shard_map/b_strips/pallas_call | solution.py:86
  2.2 3.0 %collective-permute-start = (bf16[512,1024]{1,0:T(8,128)(2,1)}, bf16[512,1024]{1,0:T(8,128)(2,1)S(1)}, u32[]{:S(2)}, u32[]{:S(2)}) collective-permute-start(bf16[512,1024]{1,0:T(8,128)(2,1)} %b_strips.2), channel_id=1, source_target_pairs={{0,2},{2,0},{4,6},{6,4},{8,10},{10,8},{12,14},{14,12},{1,3},{3,1},... | collective-permute-start | bytes 3145736 | tf_op jit(solution)/shard_map/ppermute | solution.py:502
  5.2 2.2 %b_strips.3.refs_8_ = bf16[512,1024]{1,0:T(8,128)(2,1)} custom-call(s32[1]{0:T(128)} %bitcast.quarter_ref, bf16[512,4096]{1,0:T(8,128)(2,1)} %w_ref.2), custom_call_target="tpu_custom_call" | custom-call | flops 1000 | bytes 1000 | tf_op jit(solution)/shard_map/b_strips/pallas_call | solution.py:86
  7.4 1.6 %collective-permute-start.3 = (bf16[512,1024]{1,0:T(8,128)(2,1)}, bf16[512,1024]{1,0:T(8,128)(2,1)S(1)}, u32[]{:S(2)}, u32[]{:S(2)}) collective-permute-start(bf16[512,1024]{1,0:T(8,128)(2,1)} %b_strips.3.refs_8_), channel_id=1, source_target_pairs={{0,4},{2,6},{4,0},{6,2},{8,12},{10,14},{12,8},{14,10},{1,5},{3,7},... | collective-permute-start | bytes 3145736 | tf_op jit(solution)/shard_map/ppermute | solution.py:502
  10.8 2.1 %masked_rows.5.refs_1_ = bf16[128,4096]{1,0:T(8,128)(2,1)} custom-call(s32[1]{0:T(128)} %bitcast.13.first_ref, f32[8,1,4096]{2,1,0:T(1,128)} %reshape.27.mask_ref, bf16[512,4096]{1,0:T(8,128)(2,1)} %x_ref.7), custom_call_target="tpu_custom_call" | custom-call | flops 1000 | bytes 1000 | tf_op jit(solution)/shard_map/masked_rows/pallas_call | solution.py:148
  12.9 2.1 %masked_rows.4.refs_0_ = bf16[128,4096]{1,0:T(8,128)(2,1)} custom-call(s32[1]{0:T(128)} %bitcast.12.first_ref, f32[8,1,4096]{2,1,0:T(1,128)} %reshape.27.mask_ref, bf16[512,4096]{1,0:T(8,128)(2,1)} %x_ref.7), custom_call_target="tpu_custom_call" | custom-call | flops 1000 | bytes 1000 | tf_op jit(solution)/shard_map/masked_rows/pallas_call | solution.py:148
  15.1 13.5 %collective-permute-done.refs_9_ = bf16[512,1024]{1,0:T(8,128)(2,1)S(1)} collective-permute-done((bf16[512,1024]{1,0:T(8,128)(2,1)}, bf16[512,1024]{1,0:T(8,128)(2,1)S(1)}, u32[]{:S(2)}, u32[]{:S(2)}) %collective-permute-start) | collective-permute-done | bytes 1048608 | tf_op jit(solution)/shard_map/ppermute | solution.py:502
  29.6 2.8 %collective-permute-done.3.refs_2_.refs_0_.refs_12_ = bf16[512,1024]{1,0:T(8,128)(2,1)S(1)} collective-permute-done((bf16[512,1024]{1,0:T(8,128)(2,1)}, bf16[512,1024]{1,0:T(8,128)(2,1)S(1)}, u32[]{:S(2)}, u32[]{:S(2)}) %collective-permute-start.3) | collective-permute-done | bytes 1048608 | tf_op jit(solution)/shard_map/ppermute | solution.py:502
  32.3 1.6 %collective-permute-start.5 = (bf16[512,1024]{1,0:T(8,128)(2,1)}, bf16[512,1024]{1,0:T(8,128)(2,1)S(1)}, u32[]{:S(2)}, u32[]{:S(2)}) collective-permute-start(bf16[512,1024]{1,0:T(8,128)(2,1)} %copy-done.10), channel_id=1, source_target_pairs={{0,4},{2,6},{4,0},{6,2},{8,12},{10,14},{12,8},{14,10},{1,5},{3,7},... | collective-permute-start | bytes 3145736 | tf_op jit(solution)/shard_map/ppermute | solution.py:502
  33.9 1.6 %collective-permute-start.4 = (bf16[512,1024]{1,0:T(8,128)(2,1)}, bf16[512,1024]{1,0:T(8,128)(2,1)}, u32[]{:S(2)}, u32[]{:S(2)}) collective-permute-start(bf16[512,1024]{1,0:T(8,128)(2,1)} %copy-done.10), channel_id=1, source_target_pairs={{4,8},{6,10},{8,4},{10,6},{5,9},{7,11},{9,5},{11,7},{20,24},{22,26... | collective-permute-start | bytes 3145736 | tf_op jit(solution)/shard_map/ppermute | solution.py:502
  36.0 1.5 collective-permute-start.7
  37.6 1.3 collective-permute-start.2
  38.9 2.1 %masked_rows.7.refs_3_ = bf16[128,4096]{1,0:T(8,128)(2,1)} custom-call(s32[1]{0:T(128)} %bitcast.16.first_ref, f32[8,1,4096]{2,1,0:T(1,128)} %reshape.27.mask_ref, bf16[512,4096]{1,0:T(8,128)(2,1)} %x_ref.7), custom_call_target="tpu_custom_call" | custom-call | flops 1000 | bytes 1000 | tf_op jit(solution)/shard_map/masked_rows/pallas_call | solution.py:148
  41.1 2.1 %masked_rows.6.refs_2_ = bf16[128,4096]{1,0:T(8,128)(2,1)} custom-call(s32[1]{0:T(128)} %bitcast.15.first_ref, f32[8,1,4096]{2,1,0:T(1,128)} %reshape.27.mask_ref, bf16[512,4096]{1,0:T(8,128)(2,1)} %x_ref.7), custom_call_target="tpu_custom_call" | custom-call | flops 1000 | bytes 1000 | tf_op jit(solution)/shard_map/masked_rows/pallas_call | solution.py:148
  43.3 15.4 %collective-permute-done.5.refs_3_.refs_1_.refs_13_ = bf16[512,1024]{1,0:T(8,128)(2,1)S(1)} collective-permute-done((bf16[512,1024]{1,0:T(8,128)(2,1)}, bf16[512,1024]{1,0:T(8,128)(2,1)S(1)}, u32[]{:S(2)}, u32[]{:S(2)}) %collective-permute-start.5) | collective-permute-done | bytes 1048608 | tf_op jit(solution)/shard_map/ppermute | solution.py:502
  58.6 3.2 %packed.3 = (bf16[512,1280]{1,0:T(8,128)(2,1)}, bf16[512,1024]{1,0:T(8,128)(2,1)}) custom-call(s32[2]{0:T(128)S(1)} %pad_add_fusion.1.meta_ref, bf16[512,1024]{1,0:T(8,128)(2,1)S(1)} %collective-permute-done.1.refs_0_.refs_10_, bf16[512,1024]{1,0:T(8,128)(2,1)} %collective-permute-done.4.refs_1_.refs_11_, ...), custom_call_target="tpu_custom_call" | custom-call | flops 1000 | bytes 1000 | tf_op jit(solution)/shard_map/packed/pallas_call | solution.py:129
  61.8 2.9 %collective-permute-done.2.refs_15_ = bf16[512,384]{1,0:T(8,128)(2,1)} collective-permute-done((bf16[512,384]{1,0:T(8,128)(2,1)S(1)}, bf16[512,384]{1,0:T(8,128)(2,1)}, u32[]{:S(2)}, u32[]{:S(2)}) %collective-permute-start.2) | collective-permute-done | bytes 393248 | tf_op jit(solution)/shard_map/ppermute | solution.py:502
  66.1 1.7 %collective-permute-start.11 = (bf16[512,1024]{1,0:T(8,128)(2,1)}, bf16[512,1024]{1,0:T(8,128)(2,1)}, u32[]{:S(2)}, u32[]{:S(2)}) collective-permute-start(bf16[512,1024]{1,0:T(8,128)(2,1)} %get-tuple-element.48), channel_id=1, source_target_pairs={{4,8},{6,10},{8,4},{10,6},{5,9},{7,11},{9,5},{11,7},{20,24},{22,26... | collective-permute-start | bytes 3145736 | tf_op jit(solution)/shard_map/ppermute | solution.py:502
  68.9 12.8 %collective-permute-done.7.refs_5_ = bf16[128,4096]{1,0:T(8,128)(2,1)} collective-permute-done((bf16[128,4096]{1,0:T(8,128)(2,1)}, bf16[128,4096]{1,0:T(8,128)(2,1)}, u32[]{:S(2)}, u32[]{:S(2)}) %collective-permute-start.7) | collective-permute-done | bytes 1048608 | tf_op jit(solution)/shard_map/ppermute | solution.py:502
  83.0 1.3 collective-permute-start.12
  86.3 9.7 %collective-permute-done.10.refs_14_ = bf16[512,1280]{1,0:T(8,128)(2,1)} collective-permute-done((bf16[512,1280]{1,0:T(8,128)(2,1)}, bf16[512,1280]{1,0:T(8,128)(2,1)}, u32[]{:S(2)}, u32[]{:S(2)}) %collective-permute-start.10) | collective-permute-done | bytes 1310752 | tf_op jit(solution)/shard_map/ppermute | solution.py:502
  95.9 14.1 %whole_products.1.refs_8_ = f32[2,512,1024]{2,1,0:T(8,128)} custom-call(s32[15]{0:T(128)} %stack.142.meta_ref, bf16[128,4096]{1,0:T(8,128)(2,1)} %masked_rows.4.refs_0_, bf16[128,4096]{1,0:T(8,128)(2,1)} %masked_rows.5.refs_1_, bf16[128,4096]{1,0:T(8,128)(2,1)} %masked_rows.6.refs_2_, bf16[128,4096]{1,0:T(8,128)(2,1)} %masked_rows.7.refs_3_, ...), custom_call_target="tpu_custom_call" | custom-call | flops 6000000000 | bytes 37748736 | tf_op jit(solution)/shard_map/whole_products/pallas_call | solution.py:284
  110.9 1.5 collective-permute-start.14
  113.0 5.0 %collective-permute-done.12.refs_10_ = bf16[512,1024]{1,0:T(8,128)(2,1)} collective-permute-done((bf16[512,1024]{1,0:T(8,128)(2,1)}, bf16[512,1024]{1,0:T(8,128)(2,1)}, u32[]{:S(2)}, u32[]{:S(2)}) %collective-permute-start.12) | collective-permute-done | bytes 1048608 | tf_op jit(solution)/shard_map/ppermute | solution.py:502
  118.0 5.7 %half_products.1 = (bf16[256,640]{1,0:T(8,128)(2,1)}, bf16[256,640]{1,0:T(8,128)(2,1)}, bf16[256,640]{1,0:T(8,128)(2,1)}, bf16[256,640]{1,0:T(8,128)(2,1)}) custom-call(s32[8]{0:T(128)} %stack.148.meta_ref, bf16[128,4096]{1,0:T(8,128)(2,1)} %masked_rows.4.refs_0_, bf16[128,4096]{1,0:T(8,128)(2,1)} %masked_rows.5.refs_1_, ...), custom_call_target="tpu_custom_call" | custom-call | flops 1000 | bytes 1000 | tf_op jit(solution)/shard_map/half_products/pallas_call | solution.py:414
  123.8 1.5 collective-permute-start.19
  126.2 5.6 %collective-permute-done.14.refs_12_ = bf16[512,640]{1,0:T(8,128)(2,1)S(1)} collective-permute-done((bf16[512,640]{1,0:T(8,128)(2,1)S(1)}, bf16[512,640]{1,0:T(8,128)(2,1)S(1)}, u32[]{:S(2)}, u32[]{:S(2)}) %collective-permute-start.14) | collective-permute-done | bytes 655392 | tf_op jit(solution)/shard_map/ppermute | solution.py:502
  132.6 6.8 %rest_products.1 = (bf16[256,384]{1,0:T(8,128)(2,1)}, bf16[256,384]{1,0:T(8,128)(2,1)}, bf16[256,384]{1,0:T(8,128)(2,1)}, bf16[256,384]{1,0:T(8,128)(2,1)}) custom-call(s32[11]{0:T(128)} %stack.129.meta_ref, bf16[128,4096]{1,0:T(8,128)(2,1)} %masked_rows.4.refs_0_, bf16[128,4096]{1,0:T(8,128)(2,1)} %masked_rows.5.refs_1_, ...), custom_call_target="tpu_custom_call" | custom-call | flops 1000 | bytes 1000 | tf_op jit(solution)/shard_map/rest_products/pallas_call | solution.py:414
  141.7 2.0 %assembled.2.refs_4_ = bf16[256,4096]{1,0:T(8,128)(2,1)} custom-call(s32[2]{0:T(128)S(1)} %get-tuple-element.62.place_ref, f32[4,1,4096]{2,1,0:T(1,128)S(1)} %reshape.24.mask_ref, bf16[256,640]{1,0:T(8,128)(2,1)S(1)} %copy-done.4, bf16[256,640]{1,0:T(8,128)(2,1)S(1)} %collective-permute-done.15.refs_1_, ...), custom_call_target="tpu_custom_call" | custom-call | flops 1000 | bytes 1000 | tf_op jit(solution)/shard_map/assembled/pallas_call | solution.py:461
  143.7 3.8 %collective-permute-done.17.refs_2_ = bf16[256,384]{1,0:T(8,128)(2,1)S(1)} collective-permute-done((bf16[256,384]{1,0:T(8,128)(2,1)}, bf16[256,384]{1,0:T(8,128)(2,1)S(1)}, u32[]{:S(2)}, u32[]{:S(2)}) %collective-permute-start.17) | collective-permute-done | bytes 196640 | tf_op jit(solution)/shard_map/ppermute | solution.py:502
  147.5 3.3 %collective-permute-done.18.refs_3_ = bf16[256,384]{1,0:T(8,128)(2,1)S(1)} collective-permute-done((bf16[256,384]{1,0:T(8,128)(2,1)}, bf16[256,384]{1,0:T(8,128)(2,1)S(1)}, u32[]{:S(2)}, u32[]{:S(2)}) %collective-permute-start.18) | collective-permute-done | bytes 196640 | tf_op jit(solution)/shard_map/ppermute | solution.py:582
  150.8 1.6 %assembled.3 = bf16[256,4096]{1,0:T(8,128)(2,1)} custom-call(s32[2]{0:T(128)S(1)} %get-tuple-element.61.place_ref, f32[4,1,4096]{2,1,0:T(1,128)S(1)} %reshape.24.mask_ref, bf16[256,384]{1,0:T(8,128)(2,1)S(1)} %copy-done.5, bf16[256,384]{1,0:T(8,128)(2,1)S(1)} %collective-permute-done.16.refs_1_, ...), custom_call_target="tpu_custom_call", output_to_operand_aliasing={{}: (6, {})} | custom-call | flops 1000 | bytes 1000 | tf_op jit(solution)/shard_map/assembled/pallas_call | solution.py:461
  (59 shorter events, 14.3 us)
Async XLA Ops:
  2.2 26.4 %collective-permute-start = (bf16[512,1024]{1,0:T(8,128)(2,1)}, bf16[512,1024]{1,0:T(8,128)(2,1)S(1)}, u32[]{:S(2)}, u32[]{:S(2)}) collective-permute-start(bf16[512,1024]{1,0:T(8,128)(2,1)} %b_strips.2), channel_id=1, source_target_pairs={{0,2},{2,0},{4,6},{6,4},{8,10},{10,8},{12,14},{14,12},{1,3},{3,1},... | collective-permute-start | bytes 3145736 | tf_op jit(solution)/shard_map/ppermute | solution.py:502
  5.2 4.6 %copy-start.8 = (s32[8,64]{1,0:T(8,128)S(1)}, s32[8,64]{1,0:T(8,128)}, u32[]{:S(2)}) copy-start(s32[8,64]{1,0:T(8,128)} %param.6) | copy-start | bytes 6148
  7.4 24.9 %collective-permute-start.3 = (bf16[512,1024]{1,0:T(8,128)(2,1)}, bf16[512,1024]{1,0:T(8,128)(2,1)S(1)}, u32[]{:S(2)}, u32[]{:S(2)}) collective-permute-start(bf16[512,1024]{1,0:T(8,128)(2,1)} %b_strips.3.refs_8_), channel_id=1, source_target_pairs={{0,4},{2,6},{4,0},{6,2},{8,12},{10,14},{12,8},{14,10},{1,5},{3,7},... | collective-permute-start | bytes 3145736 | tf_op jit(solution)/shard_map/ppermute | solution.py:502
  9.1 28.5 %collective-permute-start.1 = (bf16[512,1024]{1,0:T(8,128)(2,1)}, bf16[512,1024]{1,0:T(8,128)(2,1)S(1)}, u32[]{:S(2)}, u32[]{:S(2)}) collective-permute-start(bf16[512,1024]{1,0:T(8,128)(2,1)} %b_strips.3.refs_8_), channel_id=1, source_target_pairs={{4,8},{6,10},{8,4},{10,6},{5,9},{7,11},{9,5},{11,7},{20,24},{22,26... | collective-permute-start | bytes 3145736 | tf_op jit(solution)/shard_map/ppermute | solution.py:502
  28.6 1.0 copy-start.10
  32.3 35.5 %copy-start.1 = (bf16[512,1024]{1,0:T(8,128)(2,1)}, bf16[512,1024]{1,0:T(8,128)(2,1)S(1)}, u32[]{:S(2)}) copy-start(bf16[512,1024]{1,0:T(8,128)(2,1)S(1)} %collective-permute-done.3.refs_2_.refs_0_.refs_12_) | copy-start | bytes 3145732
  32.3 26.3 %collective-permute-start.5 = (bf16[512,1024]{1,0:T(8,128)(2,1)}, bf16[512,1024]{1,0:T(8,128)(2,1)S(1)}, u32[]{:S(2)}, u32[]{:S(2)}) collective-permute-start(bf16[512,1024]{1,0:T(8,128)(2,1)} %copy-done.10), channel_id=1, source_target_pairs={{0,4},{2,6},{4,0},{6,2},{8,12},{10,14},{12,8},{14,10},{1,5},{3,7},... | collective-permute-start | bytes 3145736 | tf_op jit(solution)/shard_map/ppermute | solution.py:502
  33.9 24.7 %collective-permute-start.4 = (bf16[512,1024]{1,0:T(8,128)(2,1)}, bf16[512,1024]{1,0:T(8,128)(2,1)}, u32[]{:S(2)}, u32[]{:S(2)}) collective-permute-start(bf16[512,1024]{1,0:T(8,128)(2,1)} %copy-done.10), channel_id=1, source_target_pairs={{4,8},{6,10},{8,4},{10,6},{5,9},{7,11},{9,5},{11,7},{20,24},{22,26... | collective-permute-start | bytes 3145736 | tf_op jit(solution)/shard_map/ppermute | solution.py:502
  35.5 33.4 %collective-permute-start.6 = (bf16[128,4096]{1,0:T(8,128)(2,1)}, bf16[128,4096]{1,0:T(8,128)(2,1)}, u32[]{:S(2)}, u32[]{:S(2)}) collective-permute-start(bf16[128,4096]{1,0:T(8,128)(2,1)} %masked_rows.4.refs_0_), channel_id=1, source_target_pairs={{0,2},{2,0},{4,6},{6,4},{8,10},{10,8},{12,14},{14,12},{1,3},{3,1},... | collective-permute-start | bytes 3145736 | tf_op jit(solution)/shard_map/ppermute | solution.py:502
  36.0 45.7 %collective-permute-start.7 = (bf16[128,4096]{1,0:T(8,128)(2,1)}, bf16[128,4096]{1,0:T(8,128)(2,1)}, u32[]{:S(2)}, u32[]{:S(2)}) collective-permute-start(bf16[128,4096]{1,0:T(8,128)(2,1)} %masked_rows.5.refs_1_), channel_id=1, source_target_pairs={{0,2},{2,0},{4,6},{6,4},{8,10},{10,8},{12,14},{14,12},{1,3},{3,1},... | collective-permute-start | bytes 3145736 | tf_op jit(solution)/shard_map/ppermute | solution.py:502
  37.6 21.1 %copy-start.3 = (bf16[512,1024]{1,0:T(8,128)(2,1)}, bf16[512,1024]{1,0:T(8,128)(2,1)S(1)}, u32[]{:S(2)}) copy-start(bf16[512,1024]{1,0:T(8,128)(2,1)S(1)} %collective-permute-done.1.refs_0_.refs_10_) | copy-start | bytes 3145732
  37.6 27.2 %collective-permute-start.2 = (bf16[512,384]{1,0:T(8,128)(2,1)S(1)}, bf16[512,384]{1,0:T(8,128)(2,1)}, u32[]{:S(2)}, u32[]{:S(2)}) collective-permute-start(bf16[512,384]{1,0:T(8,128)(2,1)S(1)} %slice.4), channel_id=1, source_target_pairs={{4,0},{6,2},{8,12},{10,14},{5,1},{7,3},{9,13},{11,15},{20,16},{22,... | collective-permute-start | bytes 1179656 | tf_op jit(solution)/shard_map/ppermute | solution.py:502
  58.6 9.1 %copy-start.2 = (bf16[512,1024]{1,0:T(8,128)(2,1)}, bf16[512,1024]{1,0:T(8,128)(2,1)S(1)}, u32[]{:S(2)}) copy-start(bf16[512,1024]{1,0:T(8,128)(2,1)S(1)} %collective-permute-done.5.refs_3_.refs_1_.refs_13_) | copy-start | bytes 3145732
  64.8 31.2 %collective-permute-start.10 = (bf16[512,1280]{1,0:T(8,128)(2,1)}, bf16[512,1280]{1,0:T(8,128)(2,1)}, u32[]{:S(2)}, u32[]{:S(2)}) collective-permute-start(bf16[512,1280]{1,0:T(8,128)(2,1)} %get-tuple-element.45), channel_id=1, source_target_pairs={{4,0},{6,2},{8,12},{10,14},{5,1},{7,3},{9,13},{11,15},{20,16},{22,... | collective-permute-start | bytes 3932168 | tf_op jit(solution)/shard_map/ppermute | solution.py:502
  66.1 16.9 %collective-permute-start.11 = (bf16[512,1024]{1,0:T(8,128)(2,1)}, bf16[512,1024]{1,0:T(8,128)(2,1)}, u32[]{:S(2)}, u32[]{:S(2)}) collective-permute-start(bf16[512,1024]{1,0:T(8,128)(2,1)} %get-tuple-element.48), channel_id=1, source_target_pairs={{4,8},{6,10},{8,4},{10,6},{5,9},{7,11},{9,5},{11,7},{20,24},{22,26... | collective-permute-start | bytes 3145736 | tf_op jit(solution)/shard_map/ppermute | solution.py:502
  81.8 4.3 %collective-permute-start.8 = (bf16[128,4096]{1,0:T(8,128)(2,1)}, bf16[128,4096]{1,0:T(8,128)(2,1)S(1)}, u32[]{:S(2)}, u32[]{:S(2)}) collective-permute-start(bf16[128,4096]{1,0:T(8,128)(2,1)} %collective-permute-done.6.refs_4_), channel_id=1, source_target_pairs={{0,1},{1,0},{2,3},{3,2},{4,5},{5,4},{6,7},{7,6},{8,9},{9,8},{10,11... | collective-permute-start | bytes 3145736 | tf_op jit(solution)/shard_map/ppermute | solution.py:545
  81.8 4.5 %collective-permute-start.9 = (bf16[128,4096]{1,0:T(8,128)(2,1)}, bf16[128,4096]{1,0:T(8,128)(2,1)}, u32[]{:S(2)}, u32[]{:S(2)}) collective-permute-start(bf16[128,4096]{1,0:T(8,128)(2,1)} %collective-permute-done.7.refs_5_), channel_id=1, source_target_pairs={{0,1},{1,0},{2,3},{3,2},{4,5},{5,4},{6,7},{7,6},{8,9},{9,8},{10,11... | collective-permute-start | bytes 3145736 | tf_op jit(solution)/shard_map/ppermute | solution.py:545
  82.3 27.9 %collective-permute-start.13 = (bf16[512,1024]{1,0:T(8,128)(2,1)}, bf16[512,1024]{1,0:T(8,128)(2,1)S(1)}, u32[]{:S(2)}, u32[]{:S(2)}) collective-permute-start(bf16[512,1024]{1,0:T(8,128)(2,1)} %packed.4), channel_id=1, source_target_pairs={{4,8},{6,10},{8,4},{10,6},{5,9},{7,11},{9,5},{11,7},{20,24},{22,26... | collective-permute-start | bytes 3145736 | tf_op jit(solution)/shard_map/ppermute | solution.py:502
  83.0 35.0 %collective-permute-start.12 = (bf16[512,1024]{1,0:T(8,128)(2,1)}, bf16[512,1024]{1,0:T(8,128)(2,1)}, u32[]{:S(2)}, u32[]{:S(2)}) collective-permute-start(bf16[512,1024]{1,0:T(8,128)(2,1)} %collective-permute-done.11.refs_9_), channel_id=1, source_target_pairs={{4,0},{6,2},{8,12},{10,14},{5,1},{7,3},{9,13},{11,15},{20,16},{22,... | collective-permute-start | bytes 3145736 | tf_op jit(solution)/shard_map/ppermute | solution.py:502
  86.1 9.9 %copy-start.6 = (bf16[128,4096]{1,0:T(8,128)(2,1)}, bf16[128,4096]{1,0:T(8,128)(2,1)S(1)}, u32[]{:S(2)}) copy-start(bf16[128,4096]{1,0:T(8,128)(2,1)S(1)} %collective-permute-done.8.refs_6_) | copy-start | bytes 3145732
  110.2 7.9 %copy-start = (bf16[512,1024]{1,0:T(8,128)(2,1)}, bf16[512,1024]{1,0:T(8,128)(2,1)S(1)}, u32[]{:S(2)}) copy-start(bf16[512,1024]{1,0:T(8,128)(2,1)S(1)} %collective-permute-done.13.refs_0_.refs_11_) | copy-start | bytes 3145732
  110.9 20.9 %collective-permute-start.14 = (bf16[512,640]{1,0:T(8,128)(2,1)S(1)}, bf16[512,640]{1,0:T(8,128)(2,1)S(1)}, u32[]{:S(2)}, u32[]{:S(2)}) collective-permute-start(bf16[512,640]{1,0:T(8,128)(2,1)S(1)} %packed.5), channel_id=1, source_target_pairs={{4,0},{6,2},{8,12},{10,14},{5,1},{7,3},{9,13},{11,15},{20,16},{22,... | collective-permute-start | bytes 1966088 | tf_op jit(solution)/shard_map/ppermute | solution.py:502
  123.7 8.1 %collective-permute-start.15 = (bf16[256,640]{1,0:T(8,128)(2,1)}, bf16[256,640]{1,0:T(8,128)(2,1)S(1)}, u32[]{:S(2)}, u32[]{:S(2)}) collective-permute-start(bf16[256,640]{1,0:T(8,128)(2,1)} %get-tuple-element.51), channel_id=1, source_target_pairs={{0,1},{1,0},{2,3},{3,2},{4,5},{5,4},{6,7},{7,6},{8,9},{9,8},{10,11... | collective-permute-start | bytes 983048 | tf_op jit(solution)/shard_map/ppermute | solution.py:580
  123.8 17.9 %collective-permute-start.19 = (bf16[256,640]{1,0:T(8,128)(2,1)}, bf16[256,640]{1,0:T(8,128)(2,1)S(1)}, u32[]{:S(2)}, u32[]{:S(2)}) collective-permute-start(bf16[256,640]{1,0:T(8,128)(2,1)} %get-tuple-element.59), channel_id=1, source_target_pairs={{0,2},{2,0},{4,6},{6,4},{8,10},{10,8},{12,14},{14,12},{1,3},{3,1},... | collective-permute-start | bytes 983048 | tf_op jit(solution)/shard_map/ppermute | solution.py:502
  125.3 16.4 %collective-permute-start.20 = (bf16[256,640]{1,0:T(8,128)(2,1)}, bf16[256,640]{1,0:T(8,128)(2,1)S(1)}, u32[]{:S(2)}, u32[]{:S(2)}) collective-permute-start(bf16[256,640]{1,0:T(8,128)(2,1)} %get-tuple-element.60), channel_id=1, source_target_pairs={{0,3},{1,2},{2,1},{3,0},{4,7},{5,6},{6,5},{7,4},{8,11},{9,10},{10,... | collective-permute-start | bytes 983048 | tf_op jit(solution)/shard_map/ppermute | solution.py:582
  126.2 15.1 %copy-start.9 = (s32[4,64]{1,0:T(4,128)S(1)}, s32[4,64]{1,0:T(4,128)}, u32[]{:S(2)}) copy-start(s32[4,64]{1,0:T(4,128)} %param.7) | copy-start | bytes 3076
  126.2 15.5 %copy-start.4 = (bf16[256,640]{1,0:T(8,128)(2,1)S(1)}, bf16[256,640]{1,0:T(8,128)(2,1)}, u32[]{:S(2)}) copy-start(bf16[256,640]{1,0:T(8,128)(2,1)} %get-tuple-element.57.refs_0_) | copy-start | bytes 983044
  131.8 0.9 copy-start.7
  139.4 11.4 %copy-start.5 = (bf16[256,384]{1,0:T(8,128)(2,1)S(1)}, bf16[256,384]{1,0:T(8,128)(2,1)}, u32[]{:S(2)}) copy-start(bf16[256,384]{1,0:T(8,128)(2,1)} %get-tuple-element.53.refs_0_) | copy-start | bytes 589828
  139.4 4.3 %collective-permute-start.16 = (bf16[256,384]{1,0:T(8,128)(2,1)}, bf16[256,384]{1,0:T(8,128)(2,1)S(1)}, u32[]{:S(2)}, u32[]{:S(2)}) collective-permute-start(bf16[256,384]{1,0:T(8,128)(2,1)} %get-tuple-element.54), channel_id=1, source_target_pairs={{0,1},{1,0},{2,3},{3,2},{4,5},{5,4},{6,7},{7,6},{8,9},{9,8},{10,11... | collective-permute-start | bytes 589832 | tf_op jit(solution)/shard_map/ppermute | solution.py:580
  139.5 8.0 %collective-permute-start.17 = (bf16[256,384]{1,0:T(8,128)(2,1)}, bf16[256,384]{1,0:T(8,128)(2,1)S(1)}, u32[]{:S(2)}, u32[]{:S(2)}) collective-permute-start(bf16[256,384]{1,0:T(8,128)(2,1)} %get-tuple-element.55), channel_id=1, source_target_pairs={{0,2},{2,0},{4,6},{6,4},{8,10},{10,8},{12,14},{14,12},{1,3},{3,1},... | collective-permute-start | bytes 589832 | tf_op jit(solution)/shard_map/ppermute | solution.py:502
  140.5 10.2 %collective-permute-start.18 = (bf16[256,384]{1,0:T(8,128)(2,1)}, bf16[256,384]{1,0:T(8,128)(2,1)S(1)}, u32[]{:S(2)}, u32[]{:S(2)}) collective-permute-start(bf16[256,384]{1,0:T(8,128)(2,1)} %get-tuple-element.56), channel_id=1, source_target_pairs={{0,3},{1,2},{2,1},{3,0},{4,7},{5,6},{6,5},{7,4},{8,11},{9,10},{10,... | collective-permute-start | bytes 589832 | tf_op jit(solution)/shard_map/ppermute | solution.py:582
